TPU v7x, 32 devices: a whole 2x2x4 slice. The times are simulated.
32 devices in a mesh: row: 4 (over x, core), col: 8 (over z, y).
Axes of the slice: x: 2, y: 2, z: 4, core: 2. Of those that a mesh axis runs over, the one named last changes fastest.
Arguments:
- imu: bfloat16 [16384, 128], P(('row', 'col')), may hold values from -30 to 30
- camera: bfloat16 [8, 2048, 128], P('col', 'row'), may hold values from -30 to 30
- imu_mass: float32 [16384], P('row'), may hold values from 0.3 to 3
- cam_mass: float32 [16384], P('col'), may hold values from 0.3 to 3
Outputs:
- grad_imu: float32 [16384, 128], P(('row', 'col'))
- grad_camera: float32 [8, 2048, 128], P('col', 'row')
All inputs are finite; a program needn't handle non-finite values.
Results may differ from a plain program's by a relative error of at most 0.0028.
Values may be sent and summed in bfloat16 or wider, within the bound.
No kernel may reach another device: no remote copies, remote signals or barrier semaphores. Data moves between devices by JAX's collectives and lax.ppermute only.
A program may use at most 128 MiB of HBM per device.

v0:
```python
import math

import jax
import jax.numpy as jnp
from jax import lax
from jax.sharding import PartitionSpec as P

D = 128
ITERS = 3


def cost_block(rows, rows_sq, cols, cols_sq):
    cross = jnp.dot(rows, cols.T, preferred_element_type=jnp.float32)
    return rows_sq[:, None] + cols_sq[None, :] - 2.0 * cross


def squares(values):
    return jnp.sum(jnp.square(values.astype(jnp.float32)), axis=1)


def local(imu, camera, imu_mass, cam_mass):
    epsilon = D / 20.0
    imu_rows = lax.all_gather(imu, "col", axis=0, tiled=True)
    cam_rows = lax.all_gather(camera, "row", axis=1, tiled=True)[0]
    rows = imu_rows.shape[0]
    cols = cam_rows.shape[0]
    block = math.gcd(rows, 512)
    count = rows // block
    rows_sq = squares(imu_rows)
    cols_sq = squares(cam_rows)
    log_a = jnp.log(imu_mass)
    log_b = jnp.log(cam_mass)
    stored = cost_block(imu_rows, rows_sq, cam_rows, cols_sq)

    def tile(k):
        return lax.dynamic_slice_in_dim(stored, k * block, block, 0)

    blocks = jnp.arange(count, dtype=jnp.int32)

    def row_lse(g):

        def single(k):
            scores = (g[None, :] - tile(k)) / epsilon
            peak = jnp.max(scores, axis=1)
            return (peak, jnp.sum(jnp.exp(scores - peak[:, None]), axis=1))

        peak, total = lax.map(single, blocks)
        peak = peak.reshape(rows)
        total = total.reshape(rows)
        top = lax.pmax(peak, "col")
        total = lax.psum(total * jnp.exp(peak - top), "col")
        peak = top
        return peak + jnp.log(total)

    def col_lse(f):

        def advance(k, carry):
            peak, total = carry
            f_blk = lax.dynamic_slice_in_dim(f, k * block, block, 0)
            scores = (f_blk[:, None] - tile(k)) / epsilon
            new_peak = jnp.maximum(peak, jnp.max(scores, axis=0))
            total = total * jnp.exp(peak - new_peak) + jnp.sum(
                jnp.exp(scores - new_peak[None, :]), axis=0
            )
            return (new_peak, total)

        start = (jnp.full((cols,), -1e30, jnp.float32), jnp.zeros((cols,), jnp.float32))
        peak, total = lax.fori_loop(0, count, advance, start)
        top = lax.pmax(peak, "row")
        total = lax.psum(total * jnp.exp(peak - top), "row")
        peak = top
        return peak + jnp.log(total)

    g = jnp.zeros((cols,), jnp.float32)
    f = jnp.zeros((rows,), jnp.float32)
    for step in range(ITERS):
        f = epsilon * log_a - epsilon * row_lse(g)
        g = epsilon * log_b - epsilon * col_lse(f)

    def plan_rows(k):
        f_blk = lax.dynamic_slice_in_dim(f, k * block, block, 0)
        return jnp.exp((f_blk[:, None] + g[None, :] - tile(k)) / epsilon).astype(jnp.bfloat16)

    plan = lax.map(plan_rows, blocks).reshape(rows, cols)
    row_total = jnp.sum(plan, axis=1, dtype=jnp.float32)
    col_total = jnp.sum(plan, axis=0, dtype=jnp.float32)
    imu_share = rows // lax.axis_size("col")
    cam_share = cols // lax.axis_size("row")
    plan_part = plan
    own = imu_rows.astype(jnp.float32)
    weight = row_total
    pulled = jnp.dot(plan_part, cam_rows, preferred_element_type=jnp.float32)
    whole_imu = lax.psum(2.0 * (weight[:, None] * own - pulled), "col")
    grad_imu = lax.dynamic_slice_in_dim(whole_imu, lax.axis_index("col") * imu_share, imu_share, 0)
    plan_part = plan
    own = cam_rows.astype(jnp.float32)
    weight = col_total
    pulled = lax.dot_general(
        plan_part, imu_rows, (((0,), (0,)), ((), ())), preferred_element_type=jnp.float32
    )
    whole_cam = lax.psum(2.0 * (weight[:, None] * own - pulled), "row")
    grad_cam = lax.dynamic_slice_in_dim(whole_cam, lax.axis_index("row") * cam_share, cam_share, 0)
    return (grad_imu, grad_cam[None])


def solution(mesh):
    in_specs = (P(("row", "col"), None), P("col", "row", None), P("row"), P("col"))
    out_specs = (P(("row", "col"), None), P("col", "row", None))
    return jax.shard_map(local, mesh=mesh, in_specs=in_specs, out_specs=out_specs, check_vma=False)
```

profile of v0, /device:TPU:0, one launch (start us, length us, event | category | flops | bytes accessed | tf_op | source)
XLA Modules:
  0.0 829.4 jit_solution(4209700109592127624)
XLA Ops:
  8.0 8.8 %all_gather.7 = bf16[1,2048,128]{2,1,0:T(8,128)(2,1)S(1)} all-gather(bf16[1,512,128]{2,1,0:T(8,128)(2,1)} %param.19), channel_id=1, replica_groups=mesh['row'=4,'col'=8] {'row'}, dimensions={1}, use_global_device_ids=true | all-gather | bytes 655360 | tf_op jit(solution)/shard_map/all_gather | solution.py:24
  17.2 35.8 %all-gather.2.cloned.1.call-done = bf16[4096,128]{1,0:T(8,128)(2,1)} async-done(((bf16[512,128]{1,0:T(8,128)(2,1)}), bf16[4096,128]{1,0:T(8,128)(2,1)}) %all-gather.2.cloned.1.call-update) | async-done | bytes 1048592 | tf_op jit(solution)/shard_map/all_gather | solution.py:23
  54.8 14.3 %multiply_subtract_fusion = f32[4096,2048]{1,0:T(8,128)} fusion(f32[2048]{0:T(1024)S(1)} %fusion.14, f32[4096]{0:T(1024)S(1)} %fusion.13, bf16[4096,128]{1,0:T(8,128)(2,1)} %all-gather.2.cloned.1.call-done, bf16[1,2048,128]{2,1,0:T(8,128)(2,1)S(1)} %all_gather.7), kind=kOutput, calls=%fused_computation.32 | convolution fusion | flops 2172649472 | bytes 35151872 | tf_op jit(solution)/shard_map/dot_general | solution.py:13
  69.2 56.4 %while.94 = (s32[]{:T(128)}, f32[8,512]{1,0:T(8,128)S(1)}, f32[8,512]{1,0:T(8,128)S(1)}, s32[8]{0:T(128)S(1)}, f32[4096,2048]{1,0:T(8,128)}, /*index=5*/s32[]{:T(128)}, s32[1]{0:T(128)}, s32[]{:T(128)}, s32[]{:T(128)}) while((s32[]{:T(128)}, f32[8,512]{1,0:T(8,128)S(1)}, f32[8,512]{1,0:T(8,128)S(1)}, s32[8]{0:T(128)S(1)}, ...), condition=%wide.region_5.6_spmd, body=%wide.region_2.5_spmd.sunk | while | flops 7339014 | bytes 8403111 | solution.py:47
  125.6 34.9 %pmax.42 = f32[4096]{0:T(1024)S(1)} all-reduce(f32[4096]{0:T(1024)S(1)} %bitcast.72), channel_id=1, replica_groups=mesh['row'=4,'col'=8] {'col'}, use_global_device_ids=true, to_apply=%region_6.7 | all-reduce | flops 4096 | bytes 32768 | tf_op jit(solution)/shard_map/pmax | solution.py:50
  160.6 33.0 %psum.56 = f32[4096]{0:T(1024)S(1)} all-reduce(f32[4096]{0:T(1024)S(1)} %exponential_multiply_fusion.2), channel_id=1, replica_groups=mesh['row'=4,'col'=8] {'col'}, use_global_device_ids=true, to_apply=%region_7.8 | all-reduce | flops 4096 | bytes 32768 | tf_op jit(solution)/shard_map/psum | solution.py:51
  193.6 47.5 %while.98 = (s32[]{:T(128)}, f32[2048]{0:T(1024)S(1)}, f32[2048]{0:T(1024)S(1)}, f32[4096]{0:T(1024)S(1)}, f32[4096,2048]{1,0:T(8,128)}, /*index=5*/s32[]{:T(128)}, s32[]{:T(128)}, s32[]{:T(128)}, s32[]{:T(128)}) while((s32[]{:T(128)}, f32[2048]{0:T(1024)S(1)}, f32[2048]{0:T(1024)S(1)}, f32[4096]{0:T(1024)S(1)}, ...), condition=%wide.region_11.12_spmd.clone, body=%wide.region_8.11_spmd.clone.sunk | while | flops 7350279 | bytes 8503458 | solution.py:68
  241.1 5.8 pmax.43
  246.9 6.7 psum.57
  253.6 57.8 %while.95 = (s32[]{:T(128)}, f32[8,512]{1,0:T(8,128)S(1)}, f32[8,512]{1,0:T(8,128)S(1)}, f32[2048]{0:T(1024)S(1)}, s32[8]{0:T(128)S(1)}, /*index=5*/f32[4096,204...) while((s32[]{:T(128)}, f32[8,512]{1,0:T(8,128)S(1)}, f32[8,512]{1,0:T(8,128)S(1)}, ...), condition=%wide.region_17.18_spmd, body=%wide.region_14.17_spmd.sunk | while | flops 7339014 | bytes 8419503 | solution.py:47
  257.6 3.1 exponential_reduce_fusion.13
  264.8 3.1 exponential_reduce_fusion.13
  272.0 3.1 exponential_reduce_fusion.13
  279.2 3.1 exponential_reduce_fusion.13
  286.4 3.1 exponential_reduce_fusion.13
  293.6 3.1 exponential_reduce_fusion.13
  308.1 3.1 exponential_reduce_fusion.13
  311.4 33.0 %pmax.44 = f32[4096]{0:T(1024)S(1)} all-reduce(f32[4096]{0:T(1024)S(1)} %bitcast.74), channel_id=1, replica_groups=mesh['row'=4,'col'=8] {'col'}, use_global_device_ids=true, to_apply=%region_18.19 | all-reduce | flops 4096 | bytes 32768 | tf_op jit(solution)/shard_map/pmax | solution.py:50
  344.4 33.0 %psum.58 = f32[4096]{0:T(1024)S(1)} all-reduce(f32[4096]{0:T(1024)S(1)} %exponential_multiply_fusion.1), channel_id=1, replica_groups=mesh['row'=4,'col'=8] {'col'}, use_global_device_ids=true, to_apply=%region_19.20 | all-reduce | flops 4096 | bytes 32768 | tf_op jit(solution)/shard_map/psum | solution.py:51
  377.4 47.5 %while.99 = (s32[]{:T(128)}, f32[2048]{0:T(1024)S(1)}, f32[2048]{0:T(1024)S(1)}, f32[4096]{0:T(1024)S(1)}, f32[4096,2048]{1,0:T(8,128)}, /*index=5*/s32[]{:T(128)}, s32[]{:T(128)}, s32[]{:T(128)}, s32[]{:T(128)}) while((s32[]{:T(128)}, f32[2048]{0:T(1024)S(1)}, f32[2048]{0:T(1024)S(1)}, f32[4096]{0:T(1024)S(1)}, ...), condition=%wide.region_23.24_spmd.clone, body=%wide.region_20.23_spmd.clone.sunk | while | flops 7350279 | bytes 8503458 | solution.py:68
  424.9 5.8 pmax.45
  430.7 6.7 psum.59
  437.4 56.9 %while.96 = (s32[]{:T(128)}, f32[8,512]{1,0:T(8,128)S(1)}, f32[8,512]{1,0:T(8,128)S(1)}, f32[2048]{0:T(1024)S(1)}, s32[8]{0:T(128)S(1)}, /*index=5*/f32[4096,204...) while((s32[]{:T(128)}, f32[8,512]{1,0:T(8,128)S(1)}, f32[8,512]{1,0:T(8,128)S(1)}, ...), condition=%wide.region_29.30_spmd, body=%wide.region_26.29_spmd.sunk | while | flops 7339014 | bytes 8419503 | solution.py:47
  455.5 3.1 exponential_reduce_fusion.14
  462.6 3.1 exponential_reduce_fusion.14
  469.7 3.1 exponential_reduce_fusion.14
  476.8 3.1 exponential_reduce_fusion.14
  483.9 3.1 exponential_reduce_fusion.14
  491.0 3.1 exponential_reduce_fusion.14
  494.3 33.0 %pmax.46 = f32[4096]{0:T(1024)S(1)} all-reduce(f32[4096]{0:T(1024)S(1)} %bitcast.76), channel_id=1, replica_groups=mesh['row'=4,'col'=8] {'col'}, use_global_device_ids=true, to_apply=%region_30.31 | all-reduce | flops 4096 | bytes 32768 | tf_op jit(solution)/shard_map/pmax | solution.py:50
  527.3 33.0 %psum.60 = f32[4096]{0:T(1024)S(1)} all-reduce(f32[4096]{0:T(1024)S(1)} %exponential_multiply_fusion), channel_id=1, replica_groups=mesh['row'=4,'col'=8] {'col'}, use_global_device_ids=true, to_apply=%region_31.32 | all-reduce | flops 4096 | bytes 32768 | tf_op jit(solution)/shard_map/psum | solution.py:51
  560.3 47.5 %while.100 = (s32[]{:T(128)}, f32[2048]{0:T(1024)S(1)}, f32[2048]{0:T(1024)S(1)}, f32[4096]{0:T(1024)S(1)}, f32[4096,2048]{1,0:T(8,128)}, /*index=5*/s32[]{:T(128)}, s32[]{:T(128)}, s32[]{:T(128)}, s32[]{:T(128)}) while((s32[]{:T(128)}, f32[2048]{0:T(1024)S(1)}, f32[2048]{0:T(1024)S(1)}, f32[4096]{0:T(1024)S(1)}, ...), condition=%wide.region_35.36_spmd.clone, body=%wide.region_32.35_spmd.clone.sunk | while | flops 7350279 | bytes 8503458 | solution.py:68
  607.8 5.8 pmax.47
  613.6 6.7 psum.61
  620.3 45.2 %while.97 = (s32[]{:T(128)}, bf16[8,512,2048]{2,1,0:T(8,128)(2,1)}, s32[8]{0:T(128)S(1)}, f32[4096]{0:T(1024)S(1)}, f32[2048]{0:T(1024)S(1)}, /*index=5*/f32[409...) while((s32[]{:T(128)}, bf16[8,512,2048]{2,1,0:T(8,128)(2,1)}, s32[8]{0:T(128)S(1)}, ...), condition=%wide.region_39.40_spmd, body=%wide.region_38.39_spmd.sunk | while | flops 4194310 | bytes 6306471 | solution.py:84
  621.7 4.3 fusion.34
  627.3 4.4 fusion.34
  633.0 4.3 fusion.34
  638.6 4.3 fusion.34
  644.2 4.4 fusion.34
  649.9 4.3 fusion.34
  655.5 4.4 fusion.34
  661.2 4.3 fusion.34
  665.5 8.5 %convert_reduce_fusion = (f32[2048]{0:T(1024)S(1)}, f32[8,512]{1,0:T(8,128)S(1)}) fusion(bf16[8,512,2048]{2,1,0:T(8,128)(2,1)} %get-tuple-element.425), kind=kLoop, calls=%fused_computation.30 | loop fusion | flops 25159680 | bytes 16801792 | tf_op jit(solution)/shard_map/reduce_sum | solution.py:86
  676.2 5.8 fusion.12
  682.3 11.9 %fusion.11 = f32[4096,128]{1,0:T(8,128)} fusion(bf16[4096,2048]{1,0:T(8,128)(2,1)} %bitcast.64, bf16[4096,128]{1,0:T(8,128)(2,1)S(1)} %copy-done.1, f32[4096]{0:T(1024)S(1)} %bitcast.88, bf16[1,2048,128]{2,1,0:T(8,128)(2,1)S(1)} %all_gather.7), kind=kOutput, calls=%fused_computation.34 | convolution fusion | flops 2149580800 | bytes 20463616 | tf_op jit(solution)/shard_map/dot_general | solution.py:92
  694.2 20.6 %all-reduce.5.cloned.1.call-done = f32[2048,128]{1,0:T(8,128)} async-done(((f32[2048,128]{1,0:T(8,128)}), f32[2048,128]{1,0:T(8,128)}) %all-reduce.5.cloned.1.call-update) | async-done | bytes 1048592 | tf_op jit(solution)/shard_map/psum | solution.py:101
  716.5 104.7 %all-reduce.3.cloned.1.call-done = f32[4096,128]{1,0:T(8,128)} async-done(((f32[4096,128]{1,0:T(8,128)}), f32[4096,128]{1,0:T(8,128)}) %all-reduce.3.cloned.1.call-update) | async-done | bytes 2097168 | tf_op jit(solution)/shard_map/psum | solution.py:93
  (321 shorter events, 270.5 us)
Async XLA Ops:
  7.2 45.8 %all-gather.2.cloned.1.call-start = ((), (), s32[]{:S(2)}) async-start(), calls=%async_computation | async-start | bytes 1179648 | tf_op jit(solution)/shard_map/all_gather | solution.py:23
  7.9 706.9 %all-reduce.5.cloned.1.call-start = ((), (), s32[]{:S(2)}) async-start(), calls=%async_computation.2 | async-start | bytes 2097152 | tf_op jit(solution)/shard_map/psum | solution.py:101
  69.2 124.4 %copy-start.2 = (f32[4096]{0:T(1024)S(1)}, f32[4096]{0:T(1024)}, u32[]{:S(2)}) copy-start(f32[4096]{0:T(1024)} %param.20) | copy-start | bytes 49156
  193.6 60.0 %copy-start.3 = (f32[2048]{0:T(1024)S(1)}, f32[2048]{0:T(1024)}, u32[]{:S(2)}) copy-start(f32[2048]{0:T(1024)} %param.21) | copy-start | bytes 24580
  620.3 53.7 %copy-start.1 = (bf16[4096,128]{1,0:T(8,128)(2,1)S(1)}, bf16[4096,128]{1,0:T(8,128)(2,1)}, u32[]{:S(2)}) copy-start(bf16[4096,128]{1,0:T(8,128)(2,1)} %all-gather.2.cloned.1.call-done) | copy-start | bytes 3145732
  665.5 10.7 %copy-start = (bf16[8,512,2048]{2,1,0:T(8,128)(2,1)S(1)}, bf16[8,512,2048]{2,1,0:T(8,128)(2,1)}, u32[]{:S(2)}) copy-start(bf16[8,512,2048]{2,1,0:T(8,128)(2,1)} %get-tuple-element.425) | copy-start | bytes 50331652
  682.0 139.2 %all-reduce.3.cloned.1.call-start = ((), (), s32[]{:S(2)}) async-start(), calls=%async_computation.1 | async-start | bytes 4194304 | tf_op jit(solution)/shard_map/psum | solution.py:93
Sparse Core Ops, SparseCore 0:
  10.1 42.8 all-gather.1
  682.1 32.6 all-reduce.4
  718.9 102.2 all-reduce.2
where the time goes:
time: 834 us; the launch traced here: 829 us
  other arithmetic  324 us (39%)
  blocking collectives  246 us (29%)
  waiting for transfers between devices  162 us (19%)
  matrix products  32 us (4%)
  local copies, waits for them, and re-layouts  29.5 us (4%)
  loops' own time  21.8 us (3%)
  between operations  14.1 us (2%)
    psum x1, waiting for transfers between devices, local(): whole_imu = lax.psum(2.0 * (weight[:, None] * own - pulled), 'col')  105 us
    pmax x3, blocking collectives, row_lse(): top = lax.pmax(peak, 'col')  101 us
    psum x3, blocking collectives, row_lse(): total = lax.psum(total * jnp.exp(peak - top), 'col')  99 us
    reduce_sum x24, other arithmetic, single(): return (peak, jnp.sum(jnp.exp(scores - peak[:, None]), axis=1))  75 us
    reduce_sum x24, other arithmetic, advance(): jnp.sum(jnp.exp(scores - new_peak[None, :]), axis=0)  74.4 us
    reduce_max x24, other arithmetic, single(): peak = jnp.max(scores, axis=1)  64.4 us
    reduce_max x24, other arithmetic, advance(): new_peak = jnp.maximum(peak, jnp.max(scores, axis=0))  64.1 us
    all_gather x1, waiting for transfers between devices, local(): imu_rows = lax.all_gather(imu, 'col', axis=0, tiled=True)  35.8 us
  transfers between devices with their start and end apart: 3, of which 3 were waited for; matrix products, arithmetic and copies ran while one was open for 2% of the time, Pallas kernels for 0%

commit v1 on v0

v1 whole, which is shorter than its diff:
```python
import functools
import math

import jax
import jax.numpy as jnp
from jax import lax
from jax.experimental import pallas as pl
from jax.experimental.pallas import tpu as pltpu
from jax.sharding import PartitionSpec as P

D = 128
ITERS = 3
EPSILON = D / 20.0
LOG2E = math.log2(math.e)
CROSS = 2.0 * LOG2E / EPSILON
NT = (((1,), (1,)), ((), ()))
VMEM = pl.BlockSpec(memory_space=pltpu.VMEM)


def spread(s_ref, sb_ref):
    chunks = s_ref.shape[0]
    turned = jnp.transpose(s_ref[...])
    for k in range(chunks):
        sb_ref[k * 128:(k + 1) * 128, :] = jnp.broadcast_to(turned[:, k:k + 1], (128, 128))


def first_kernel(chunk, width, a_ref, b_ref, s_ref, o_ref, sb_ref):
    depth, lanes = a_ref.shape[0], b_ref.shape[0]
    tiles = width // 128
    spread(s_ref, sb_ref)

    def column(n, _):
        start = pl.multiple_of(n * width, width)
        b = b_ref[pl.ds(start, width), :]

        def step(m, carry):
            peak, total = carry
            at = pl.multiple_of(m * chunk, chunk)
            d = lax.dot_general(a_ref[pl.ds(at, chunk), :], b, NT, preferred_element_type=jnp.float32)
            s = sb_ref[pl.ds(at, chunk), :]
            peaks, totals = [], []
            for q in range(tiles):
                t = (d[:, q * 128:(q + 1) * 128] * CROSS + s).reshape(chunk // 8, 8, 128)
                old = peak[:, q * 128:(q + 1) * 128]
                new = jnp.maximum(old, jnp.max(t, axis=0))
                part = jnp.sum(jnp.exp2(t - new[None]), axis=0)
                peaks.append(new)
                totals.append(total[:, q * 128:(q + 1) * 128] * jnp.exp2(old - new) + part)
            return jnp.concatenate(peaks, axis=1), jnp.concatenate(totals, axis=1)

        init = (jnp.full((8, width), -1e30, jnp.float32), jnp.zeros((8, width), jnp.float32))
        peak, total = lax.fori_loop(0, depth // chunk, step, init, unroll=True)
        top = jnp.max(peak, axis=0, keepdims=True)
        whole = jnp.sum(total * jnp.exp2(peak - top), axis=0, keepdims=True)
        o_ref[:, pl.ds(start, width)] = top + jnp.log2(whole)
        return 0

    lax.fori_loop(0, lanes // width, column, 0)


def sum_kernel(chunk, width, a_ref, b_ref, s_ref, l_ref, o_ref, sb_ref):
    depth, lanes = a_ref.shape[0], b_ref.shape[0]
    tiles = width // 128
    spread(s_ref, sb_ref)

    def column(n, _):
        start = pl.multiple_of(n * width, width)
        b = b_ref[pl.ds(start, width), :]
        l = l_ref[:, pl.ds(start, width)]
        total = [jnp.zeros((8, 128), jnp.float32) for q in range(tiles)]
        for m in range(depth // chunk):
            d = lax.dot_general(a_ref[m * chunk:(m + 1) * chunk, :], b, NT, preferred_element_type=jnp.float32)
            s = sb_ref[m * chunk:(m + 1) * chunk, :]
            for q in range(tiles):
                t = d[:, q * 128:(q + 1) * 128] * CROSS + s + l[:, q * 128:(q + 1) * 128]
                total[q] = total[q] + jnp.sum(jnp.exp2(t).reshape(chunk // 8, 8, 128), axis=0)
        o_ref[:, pl.ds(start, width)] = jnp.sum(jnp.concatenate(total, axis=1), axis=0, keepdims=True)
        return 0

    lax.fori_loop(0, lanes // width, column, 0)


def pass_cost(a, b):
    size = a.shape[0] * b.shape[0]
    return pl.CostEstimate(flops=2 * size * D, bytes_accessed=2 * (a.size + b.size), transcendentals=size)


def first_pass(a, b, s, chunk=512, width=256):
    depth, lanes = a.shape[0], b.shape[0]
    out = pl.pallas_call(
        functools.partial(first_kernel, chunk, width),
        out_shape=jax.ShapeDtypeStruct((1, lanes), jnp.float32),
        in_specs=[VMEM] * 3,
        out_specs=VMEM,
        scratch_shapes=[pltpu.VMEM((depth, 128), jnp.float32)],
        compiler_params=pltpu.CompilerParams(vmem_limit_bytes=32 << 20),
        cost_estimate=pass_cost(a, b),
        name="first_pass",
    )(a, b, s.reshape(depth // 128, 128))
    return out.reshape(lanes)


def sum_pass(a, b, s, l, chunk=512, width=256):
    depth, lanes = a.shape[0], b.shape[0]
    out = pl.pallas_call(
        functools.partial(sum_kernel, chunk, width),
        out_shape=jax.ShapeDtypeStruct((1, lanes), jnp.float32),
        in_specs=[VMEM] * 4,
        out_specs=VMEM,
        scratch_shapes=[pltpu.VMEM((depth, 128), jnp.float32)],
        compiler_params=pltpu.CompilerParams(vmem_limit_bytes=32 << 20),
        cost_estimate=pass_cost(a, b),
        name="sum_pass",
    )(a, b, s.reshape(depth // 128, 128), l.reshape(1, lanes))
    return out.reshape(lanes)


def final_kernel(chunk, x_ref, xt_ref, y_ref, u_ref, v_ref, gi_ref, gc_ref, ub_ref, acc_ref):
    rows, cols = x_ref.shape[0], y_ref.shape[0]
    spread(u_ref, ub_ref)
    acc_ref[...] = jnp.zeros_like(acc_ref)
    y = y_ref[...]
    v = v_ref[...]
    y_one = jnp.concatenate([y, jnp.ones((cols, 128), jnp.bfloat16)], axis=1)

    def block(k, _):
        at = pl.multiple_of(k * chunk, chunk)
        x = x_ref[pl.ds(at, chunk), :]
        d = lax.dot_general(x, y, NT, preferred_element_type=jnp.float32)
        u = ub_ref[pl.ds(at, chunk), :]
        parts = []
        for q in range(cols // 128):
            t = d[:, q * 128:(q + 1) * 128] * CROSS + u + v[:, q * 128:(q + 1) * 128]
            parts.append(jnp.exp2(t).astype(jnp.bfloat16))
        plan = jnp.concatenate(parts, axis=1)
        pulled = jnp.dot(plan, y_one, preferred_element_type=jnp.float32)
        gi_ref[pl.ds(at, chunk), :] = 2.0 * (pulled[:, 128:] * x.astype(jnp.float32) - pulled[:, :128])
        acc_ref[...] += jnp.dot(xt_ref[:, pl.ds(at, chunk)], plan, preferred_element_type=jnp.float32)
        return 0

    lax.fori_loop(0, rows // chunk, block, 0)
    yf = y.astype(jnp.float32)
    for q in range(cols // 128):
        pulled = jnp.transpose(acc_ref[0:128, q * 128:(q + 1) * 128])
        count = jnp.transpose(jnp.broadcast_to(acc_ref[128:129, q * 128:(q + 1) * 128], (128, 128)))
        gc_ref[q * 128:(q + 1) * 128, :] = 2.0 * (count * yf[q * 128:(q + 1) * 128, :] - pulled)


def final_pass(x, y, u, v, chunk=256):
    rows, cols = x.shape[0], y.shape[0]
    size = rows * cols
    xt = jnp.concatenate([x.T, jnp.ones((16, rows), jnp.bfloat16)], axis=0)
    return pl.pallas_call(
        functools.partial(final_kernel, chunk),
        out_shape=(
            jax.ShapeDtypeStruct((rows, D), jnp.float32),
            jax.ShapeDtypeStruct((cols, D), jnp.float32),
        ),
        in_specs=[VMEM] * 5,
        out_specs=(VMEM, VMEM),
        scratch_shapes=[
            pltpu.VMEM((rows, 128), jnp.float32),
            pltpu.VMEM((144, cols), jnp.float32),
        ],
        compiler_params=pltpu.CompilerParams(vmem_limit_bytes=48 << 20),
        cost_estimate=pl.CostEstimate(flops=6 * size * D, bytes_accessed=4 * D * (rows + cols), transcendentals=size),
        name="final_pass",
    )(x, xt, y, u.reshape(rows // 128, 128), v.reshape(1, cols))


def shifted(value, axis, count, shift):
    return lax.ppermute(value, axis, [(i, (i + shift) % count) for i in range(count)])


def everyone(value, axis, count):
    return [value] + [shifted(value, axis, count, s) for s in range(1, count)]


def gathered(value, axis, count):
    parts = everyone(value, axis, count)
    me = lax.axis_index(axis)
    size = value.shape[0]
    out = jnp.zeros((count * size,) + value.shape[1:], value.dtype)
    for s, part in enumerate(parts):
        place = lax.rem(me + count - s, count) * size
        out = lax.dynamic_update_slice_in_dim(out, part, place, 0)
    return out


def lse2(parts):
    top = functools.reduce(jnp.maximum, parts)
    return top + jnp.log2(sum(jnp.exp2(part - top) for part in parts))


def doubled(value, axis, count):
    step = 1
    while step < count:
        value = value + lax.ppermute(value, axis, [(i, i ^ step) for i in range(count)])
        step *= 2
    return value


def scattered(value, axis, count):
    me = lax.axis_index(axis)
    size = value.shape[0] // count

    def share(owner):
        return lax.dynamic_slice_in_dim(value, owner * size, size, 0)

    total = share(me)
    for s in range(1, count):
        part = share(lax.rem(me + s, count)).astype(jnp.bfloat16)
        total = total + shifted(part, axis, count, s).astype(jnp.float32)
    return total


def local(imu, camera, imu_mass, cam_mass):
    nrow, ncol = lax.axis_size("row"), lax.axis_size("col")
    y = gathered(camera[0], "row", nrow)
    x = gathered(imu, "col", ncol)
    log_a = jnp.log2(imu_mass)
    log_b = jnp.log2(cam_mass)
    v = jnp.sum(jnp.square(y.astype(jnp.float32)), axis=1) * (-LOG2E / EPSILON)
    u = log_a - lse2(everyone(first_pass(y, x, v), "col", ncol))
    v = log_b - lse2(everyone(first_pass(x, y, u), "row", nrow))
    u = u + log_a - jnp.log2(doubled(sum_pass(y, x, v, u), "col", ncol))
    v = v + log_b - jnp.log2(doubled(sum_pass(x, y, u, v), "row", nrow))
    u = u + log_a - jnp.log2(jnp.sum(lax.all_gather(sum_pass(y, x, v, u, 2048), "col"), axis=0))
    v = v + log_b - jnp.log2(jnp.sum(lax.all_gather(sum_pass(x, y, u, v, 1024, 512), "row"), axis=0))
    grad_imu, grad_cam = final_pass(x, y, u, v)
    return scattered(grad_imu, "col", ncol), scattered(grad_cam, "row", nrow)[None]


def solution(mesh):
    in_specs = (P(("row", "col"), None), P("col", "row", None), P("row"), P("col"))
    out_specs = (P(("row", "col"), None), P("col", "row", None))
    return jax.shard_map(local, mesh=mesh, in_specs=in_specs, out_specs=out_specs, check_vma=False)
```

time: 834 us -> 218 us (0.26)
  other arithmetic: 324 us -> 4.11 us
  blocking collectives: 246 us -> 36 us
  waiting for transfers between devices: 162 us -> 62.3 us
  Pallas kernels: 0 us -> 73.5 us
  starting transfers between devices: 0.34 us -> 36.5 us
  matrix products: 32 us -> 0 us
  local copies, waits for them, and re-layouts: 29.5 us -> 3.32 us
  loops' own time: 21.8 us -> 0 us
  between operations: 14.1 us -> 1.1 us
    reduce_sum x51 -> x3, other arithmetic: 160 us -> 0.48 us  [the longest x1 0.34 us: local(): v = jnp.sum(jnp.square(y.astype(jnp.float32)), axis=1) * (-LOG2E / EPSILON)]
    reduce_max x48 -> x0, other arithmetic: 129 us -> none  [the longest x24 64.4 us: single(): peak = jnp.max(scores, axis=1)]
    psum x2 -> x0, waiting for transfers between devices: 125 us -> none  [the longest x1 105 us: local(): whole_imu = lax.psum(2.0 * (weight[:, None] * own - pulled), 'col')]
    psum x6 -> x0, blocking collectives: 119 us -> none  [the longest x3 99 us: row_lse(): total = lax.psum(total * jnp.exp(peak - top), 'col')]
    pmax x6 -> x0, blocking collectives: 118 us -> none  [the longest x3 101 us: row_lse(): top = lax.pmax(peak, 'col')]
    pallas_call x0 -> x7, Pallas kernels: none -> 73.5 us  [the longest x4 33.4 us: sum_pass(): pl.pallas_call(functools.partial(sum_kernel, chunk, width), out_shape=jax...]
    ppermute x0 -> x35, waiting for transfers between devices: none -> 62.3 us  [the longest x30 47.7 us: shifted(): lax.ppermute(value, axis, [(i, (i + shift) % count) for i in range(count)])]
    ppermute x0 -> x35, starting transfers between devices: none -> 36.5 us  [the longest x30 34 us: shifted(): lax.ppermute(value, axis, [(i, (i + shift) % count) for i in range(count)])]
  transfers between devices with their start and end apart: 3 -> 35, of which waited for: 3 -> 20; matrix products, arithmetic and copies ran while one was open for 2% -> 2% of each run, Pallas kernels for 0% -> 0%
where the time goes in v1:
time: 218 us; the launch traced here: 217 us
  Pallas kernels  73.5 us (34%)
  waiting for transfers between devices  62.3 us (29%)
  starting transfers between devices  36.5 us (17%)
  blocking collectives  36 us (17%)
  other arithmetic  4.11 us (2%)
  local copies, waits for them, and re-layouts  3.32 us (2%)
    ppermute x30, waiting for transfers between devices, shifted(): lax.ppermute(value, axis, [(i, (i + shift) % count) for i in range(count)])  47.7 us
    ppermute x30, starting transfers between devices, shifted(): lax.ppermute(value, axis, [(i, (i + shift) % count) for i in range(count)])  34 us
    pallas_call x4, Pallas kernels, sum_pass(): pl.pallas_call(functools.partial(sum_kernel, chunk, width), out_shape=jax...  33.4 us
    all_gather x1, blocking collectives, local(): lax.all_gather(sum_pass(y, x, v, u, 2048), 'col')  30.6 us
    pallas_call x2, Pallas kernels, first_pass(): pl.pallas_call(functools.partial(first_kernel, chunk, width), out_shape=j...  23.4 us
    pallas_call x1, Pallas kernels, final_pass(): pl.pallas_call(functools.partial(final_kernel, chunk), out_shape=(jax.Sha...  16.6 us
    ppermute x5, waiting for transfers between devices, doubled(): lax.ppermute(value, axis, [(i, i ^ step) for i in range(count)])  14.6 us
    all_gather x1, blocking collectives, local(): lax.all_gather(sum_pass(x, y, u, v, 1024, 512), 'row')  5.37 us
  transfers between devices with their start and end apart: 35, of which 20 were waited for; matrix products, arithmetic and copies ran while one was open for 2% of the time, Pallas kernels for 0%

profile of v1, /device:TPU:0, one launch (start us, length us, event | category | flops | bytes accessed | tf_op | source)
XLA Modules:
  0.0 216.8 jit_solution(3390383911691206102)
XLA Ops:
  0.6 1.0 copy.21
  1.7 6.1 %collective-permute-start.6 = (bf16[512,128]{0,1:T(8,128)(2,1)S(1)}, bf16[512,128]{0,1:T(8,128)(2,1)S(1)}, u32[]{:S(2)}, u32[]{:S(2)}) collective-permute-start(bf16[512,128]{0,1:T(8,128)(2,1)S(1)} %copy.21), channel_id=1, source_target_pairs={{0,7},{1,0},{2,1},{3,2},{4,3},{5,4},{6,5},{7,6},{8,15},{9,8},{10,9... | collective-permute-start | bytes 393224 | tf_op jit(solution)/shard_map/ppermute | solution.py:172
  8.2 1.5 collective-permute-start.8
  9.8 0.9 constant_dynamic-update-slice_fusion.3
  10.9 3.9 %collective-permute-done.7 = bf16[512,128]{1,0:T(8,128)(2,1)S(1)} collective-permute-done((bf16[512,128]{1,0:T(8,128)(2,1)}, bf16[512,128]{1,0:T(8,128)(2,1)S(1)}, u32[]{:S(2)}, u32[]{:S(2)}) %collective-permute-start.7) | collective-permute-done | bytes 131104 | tf_op jit(solution)/shard_map/ppermute | solution.py:172
  14.8 1.6 collective-permute-start.1
  16.5 0.8 collective-permute-done.9
  17.3 1.9 collective-permute-start
  19.6 6.7 %collective-permute-done = bf16[512,128]{0,1:T(8,128)(2,1)S(1)} collective-permute-done((bf16[512,128]{0,1:T(8,128)(2,1)S(1)}, bf16[512,128]{0,1:T(8,128)(2,1)S(1)}, u32[]{:S(2)}, u32[]{:S(2)}) %collective-permute-start) | collective-permute-done | bytes 131104 | tf_op jit(solution)/shard_map/ppermute | solution.py:172
  26.4 1.3 collective-permute-start.3
  27.7 11.0 %collective-permute-done.2 = bf16[512,128]{0,1:T(8,128)(2,1)S(1)} collective-permute-done((bf16[512,128]{0,1:T(8,128)(2,1)S(1)}, bf16[512,128]{0,1:T(8,128)(2,1)S(1)}, u32[]{:S(2)}, u32[]{:S(2)}) %collective-permute-start.2) | collective-permute-done | bytes 131104 | tf_op jit(solution)/shard_map/ppermute | solution.py:172
  38.8 0.7 copy.35.b_ref.a_ref.x_ref
  39.5 12.5 %first_pass.2 = f32[1,4096]{1,0:T(1,128)S(1)} custom-call(bf16[2048,128]{1,0:T(8,128)(2,1)S(1)} %constant_dynamic-update-slice_fusion.a_ref.b_ref.y_ref, bf16[4096,128]{1,0:T(8,128)(2,1)S(1)} %copy.35.b_ref.a_ref.x_ref, f32[16,128]{1,0:T(8,128)S(1)} %multiply_bitcast_fusion.s_ref), custom_call_target="tpu_custom_call" | custom-call | flops 2147483648 | bytes 1572864 | tf_op jit(solution)/shard_map/first_pass/pallas_call | solution.py:90
  52.0 4.1 %collective-permute-start.16 = (f32[4096]{0:T(1024)S(1)}, f32[4096]{0:T(1024)S(1)}, u32[]{:S(2)}, u32[]{:S(2)}) collective-permute-start(f32[4096]{0:T(1024)S(1)} %bitcast.32), channel_id=1, source_target_pairs={{0,7},{1,0},{2,1},{3,2},{4,3},{5,4},{6,5},{7,6},{8,15},{9,8},{10,9... | collective-permute-start | bytes 49160 | tf_op jit(solution)/shard_map/ppermute | solution.py:172
  56.0 3.0 %collective-permute-start.13 = (f32[4096]{0:T(1024)S(1)}, f32[4096]{0:T(1024)S(1)}, u32[]{:S(2)}, u32[]{:S(2)}) collective-permute-start(f32[4096]{0:T(1024)S(1)} %bitcast.35), channel_id=1, source_target_pairs={{0,4},{1,5},{2,6},{3,7},{4,0},{5,1},{6,2},{7,3},{8,12},{9,13},{10,... | collective-permute-start | bytes 49160 | tf_op jit(solution)/shard_map/ppermute | solution.py:172
  59.0 2.1 collective-permute-start.12
  61.2 1.3 collective-permute-start.10
  62.5 2.1 collective-permute-done.12
  64.6 2.1 collective-permute-done.11
  66.7 1.0 collective-permute-done.10
  67.7 11.0 %first_pass.3 = f32[1,2048]{1,0:T(1,128)S(1)} custom-call(bf16[4096,128]{1,0:T(8,128)(2,1)S(1)} %copy.35.b_ref.a_ref.x_ref, bf16[2048,128]{1,0:T(8,128)(2,1)S(1)} %constant_dynamic-update-slice_fusion.a_ref.b_ref.y_ref, f32[32,128]{1,0:T(8,128)S(1)} %bitcast.24), custom_call_target="tpu_custom_call" | custom-call | flops 2147483648 | bytes 1572864 | tf_op jit(solution)/shard_map/first_pass/pallas_call | solution.py:90
  78.8 1.4 collective-permute-start.18
  80.4 2.1 collective-permute-done.18
  82.5 0.8 collective-permute-done.17
  83.3 8.8 %sum_pass.4 = f32[1,4096]{1,0:T(1,128)S(1)} custom-call(bf16[2048,128]{1,0:T(8,128)(2,1)S(1)} %constant_dynamic-update-slice_fusion.a_ref.b_ref.y_ref, bf16[4096,128]{1,0:T(8,128)(2,1)S(1)} %copy.35.b_ref.a_ref.x_ref, f32[16,128]{1,0:T(8,128)S(1)} %bitcast.28, f32[1,4096]{1,0:T(1,128)S(1)} %bitcast.25), custom_call_target="tpu_custom_call" | custom-call | flops 2147483648 | bytes 1572864 | tf_op jit(solution)/shard_map/sum_pass/pallas_call | solution.py:105
  92.2 3.7 %collective-permute-done.20 = f32[4096]{0:T(1024)S(1)} collective-permute-done((f32[4096]{0:T(1024)S(1)}, f32[4096]{0:T(1024)S(1)}, u32[]{:S(2)}, u32[]{:S(2)}) %collective-permute-start.20) | collective-permute-done | bytes 16416 | tf_op jit(solution)/shard_map/ppermute | solution.py:198
  96.0 3.9 %collective-permute-done.21 = f32[4096]{0:T(1024)S(1)} collective-permute-done((f32[4096]{0:T(1024)S(1)}, f32[4096]{0:T(1024)S(1)}, u32[]{:S(2)}, u32[]{:S(2)}) %collective-permute-start.21) | collective-permute-done | bytes 16416 | tf_op jit(solution)/shard_map/ppermute | solution.py:198
  99.9 1.8 collective-permute-start.22
  101.7 2.8 %collective-permute-done.22 = f32[4096]{0:T(1024)S(1)} collective-permute-done((f32[4096]{0:T(1024)S(1)}, f32[4096]{0:T(1024)S(1)}, u32[]{:S(2)}, u32[]{:S(2)}) %collective-permute-start.22) | collective-permute-done | bytes 16416 | tf_op jit(solution)/shard_map/ppermute | solution.py:198
  104.5 7.7 %sum_pass.5 = f32[1,2048]{1,0:T(1,128)S(1)} custom-call(bf16[4096,128]{1,0:T(8,128)(2,1)S(1)} %copy.35.b_ref.a_ref.x_ref, bf16[2048,128]{1,0:T(8,128)(2,1)S(1)} %constant_dynamic-update-slice_fusion.a_ref.b_ref.y_ref, f32[32,128]{1,0:T(8,128)S(1)} %bitcast.26, f32[1,2048]{1,0:T(1,128)S(1)} %bitcast.29), custom_call_target="tpu_custom_call" | custom-call | flops 2147483648 | bytes 1572864 | tf_op jit(solution)/shard_map/sum_pass/pallas_call | solution.py:105
  112.4 1.2 collective-permute-done.23
  114.1 3.0 %collective-permute-done.24 = f32[2048]{0:T(1024)S(1)} collective-permute-done((f32[2048]{0:T(1024)S(1)}, f32[2048]{0:T(1024)S(1)}, u32[]{:S(2)}, u32[]{:S(2)}) %collective-permute-start.24) | collective-permute-done | bytes 8224 | tf_op jit(solution)/shard_map/ppermute | solution.py:198
  117.2 9.9 %sum_pass.6 = f32[1,4096]{1,0:T(1,128)S(1)} custom-call(bf16[2048,128]{1,0:T(8,128)(2,1)S(1)} %constant_dynamic-update-slice_fusion.a_ref.b_ref.y_ref, bf16[4096,128]{1,0:T(8,128)(2,1)S(1)} %copy.35.b_ref.a_ref.x_ref, f32[16,128]{1,0:T(8,128)S(1)} %bitcast.30, f32[1,4096]{1,0:T(1,128)S(1)} %bitcast.27), custom_call_target="tpu_custom_call" | custom-call | flops 2147483648 | bytes 1572864 | tf_op jit(solution)/shard_map/sum_pass/pallas_call | solution.py:105
  127.1 30.6 %all-gather = f32[8,1,4096]{2,1,0:T(1,128)S(1)} all-gather(f32[1,1,4096]{2,1,0:T(1,128)S(1)} %bitcast.42), channel_id=1, replica_groups=mesh['row'=4,'col'=8] {'col'}, dimensions={0}, use_global_device_ids=true | all-gather | bytes 147456 | tf_op jit(solution)/shard_map/all_gather | solution.py:228
  157.8 6.9 %sum_pass.7 = f32[1,2048]{1,0:T(1,128)S(1)} custom-call(bf16[4096,128]{1,0:T(8,128)(2,1)S(1)} %copy.35.b_ref.a_ref.x_ref, bf16[2048,128]{1,0:T(8,128)(2,1)S(1)} %constant_dynamic-update-slice_fusion.a_ref.b_ref.y_ref, f32[32,128]{1,0:T(8,128)S(1)} %subtract_bitcast_fusion.s_ref.u_ref, f32[1,2048]{1,0:T(1,128)S(1)} %bitcast.31), custom_call_target="tpu_custom_call" | custom-call | flops 2147483648 | bytes 1572864 | tf_op jit(solution)/shard_map/sum_pass/pallas_call | solution.py:105
  164.8 5.4 %all-gather.1 = f32[4,1,2048]{2,1,0:T(1,128)S(1)} all-gather(f32[1,1,2048]{2,1,0:T(1,128)S(1)} %bitcast.45), channel_id=1, replica_groups=mesh['row'=4,'col'=8] {'row'}, dimensions={0}, use_global_device_ids=true | all-gather | bytes 40960 | tf_op jit(solution)/shard_map/all_gather | solution.py:229
  170.2 16.6 %final_pass.1 = (f32[4096,128]{1,0:T(8,128)S(1)}, f32[2048,128]{1,0:T(8,128)S(1)}) custom-call(bf16[4096,128]{1,0:T(8,128)(2,1)S(1)} %copy.35.b_ref.a_ref.x_ref, bf16[144,4096]{1,0:T(8,128)(2,1)S(1)} %concatenate.3.xt_ref, bf16[2048,128]{1,0:T(8,128)(2,1)S(1)} %constant_dynamic-update-slice_fusion.a_ref.b_ref.y_ref, ...), custom_call_target="tpu_custom_call" | custom-call | flops 6442450944 | bytes 3145728 | tf_op jit(solution)/shard_map/final_pass/pallas_call | solution.py:153
  187.3 1.4 collective-permute-start.34
  189.4 4.7 %collective-permute-start.31 = (bf16[512,128]{1,0:T(8,128)(2,1)S(1)}, bf16[512,128]{1,0:T(8,128)(2,1)S(1)}, u32[]{:S(2)}, u32[]{:S(2)}) collective-permute-start(bf16[512,128]{1,0:T(8,128)(2,1)S(1)} %get-tuple-element.7), channel_id=1, source_target_pairs={{0,7},{1,0},{2,1},{3,2},{4,3},{5,4},{6,5},{7,6},{8,15},{9,8},{10,9... | collective-permute-start | bytes 393224 | tf_op jit(solution)/shard_map/ppermute | solution.py:172
  194.1 1.5 collective-permute-done.33
  195.6 1.4 collective-permute-start.28
  197.0 1.4 collective-permute-done.25
  198.5 0.6 collective-permute-start.26
  199.1 1.7 add_bitcast_fusion
  200.9 2.8 %collective-permute-done.29 = bf16[512,128]{1,0:T(8,128)(2,1)S(1)} collective-permute-done((bf16[512,128]{1,0:T(8,128)(2,1)S(1)}, bf16[512,128]{1,0:T(8,128)(2,1)S(1)}, u32[]{:S(2)}, u32[]{:S(2)}) %collective-permute-start.29) | collective-permute-done | bytes 131104 | tf_op jit(solution)/shard_map/ppermute | solution.py:172
  203.7 9.9 %collective-permute-done.28 = bf16[512,128]{1,0:T(8,128)(2,1)S(1)} collective-permute-done((bf16[512,128]{1,0:T(8,128)(2,1)S(1)}, bf16[512,128]{1,0:T(8,128)(2,1)S(1)}, u32[]{:S(2)}, u32[]{:S(2)}) %collective-permute-start.28) | collective-permute-done | bytes 131104 | tf_op jit(solution)/shard_map/ppermute | solution.py:172
  213.6 1.4 collective-permute-done.27
  215.0 1.8 convert_add_fusion
  (79 shorter events, 3.6 us)
Async XLA Ops:
  0.6 14.2 %copy-start.5 = (bf16[1,512,128]{2,1,0:T(8,128)(2,1)S(1)}, bf16[1,512,128]{2,1,0:T(8,128)(2,1)}, u32[]{:S(2)}) copy-start(bf16[1,512,128]{2,1,0:T(8,128)(2,1)} %param.5) | copy-start | bytes 393220
  1.7 37.1 %collective-permute-start.6 = (bf16[512,128]{0,1:T(8,128)(2,1)S(1)}, bf16[512,128]{0,1:T(8,128)(2,1)S(1)}, u32[]{:S(2)}, u32[]{:S(2)}) collective-permute-start(bf16[512,128]{0,1:T(8,128)(2,1)S(1)} %copy.21), channel_id=1, source_target_pairs={{0,7},{1,0},{2,1},{3,2},{4,3},{5,4},{6,5},{7,6},{8,15},{9,8},{10,9... | collective-permute-start | bytes 393224 | tf_op jit(solution)/shard_map/ppermute | solution.py:172
  7.7 31.0 %collective-permute-start.5 = (bf16[512,128]{0,1:T(8,128)(2,1)S(1)}, bf16[512,128]{0,1:T(8,128)(2,1)S(1)}, u32[]{:S(2)}, u32[]{:S(2)}) collective-permute-start(bf16[512,128]{0,1:T(8,128)(2,1)S(1)} %copy.21), channel_id=1, source_target_pairs={{0,6},{1,7},{2,0},{3,1},{4,2},{5,3},{6,4},{7,5},{8,14},{9,15},{10,... | collective-permute-start | bytes 393224 | tf_op jit(solution)/shard_map/ppermute | solution.py:172
  8.2 30.5 %collective-permute-start.4 = (bf16[512,128]{0,1:T(8,128)(2,1)S(1)}, bf16[512,128]{0,1:T(8,128)(2,1)S(1)}, u32[]{:S(2)}, u32[]{:S(2)}) collective-permute-start(bf16[512,128]{0,1:T(8,128)(2,1)S(1)} %copy.21), channel_id=1, source_target_pairs={{0,5},{1,6},{2,7},{3,0},{4,1},{5,2},{6,3},{7,4},{8,13},{9,14},{10,... | collective-permute-start | bytes 393224 | tf_op jit(solution)/shard_map/ppermute | solution.py:172
  8.2 6.6 %collective-permute-start.8 = (bf16[512,128]{1,0:T(8,128)(2,1)}, bf16[512,128]{1,0:T(8,128)(2,1)S(1)}, u32[]{:S(2)}, u32[]{:S(2)}) collective-permute-start(bf16[512,128]{1,0:T(8,128)(2,1)} %bitcast.52), channel_id=1, source_target_pairs={{0,16},{8,24},{16,0},{24,8},{1,17},{9,25},{17,1},{25,9},{2,18},{10... | collective-permute-start | bytes 393224 | tf_op jit(solution)/shard_map/ppermute | solution.py:172
  9.7 5.1 %collective-permute-start.7 = (bf16[512,128]{1,0:T(8,128)(2,1)}, bf16[512,128]{1,0:T(8,128)(2,1)S(1)}, u32[]{:S(2)}, u32[]{:S(2)}) collective-permute-start(bf16[512,128]{1,0:T(8,128)(2,1)} %bitcast.53), channel_id=1, source_target_pairs={{0,8},{8,16},{16,24},{24,0},{1,9},{9,17},{17,25},{25,1},{2,10},{10... | collective-permute-start | bytes 393224 | tf_op jit(solution)/shard_map/ppermute | solution.py:172
  14.8 2.5 %collective-permute-start.9 = (bf16[512,128]{1,0:T(8,128)(2,1)S(1)}, bf16[512,128]{1,0:T(8,128)(2,1)S(1)}, u32[]{:S(2)}, u32[]{:S(2)}) collective-permute-start(bf16[512,128]{1,0:T(8,128)(2,1)S(1)} %bitcast.54), channel_id=1, source_target_pairs={{0,24},{8,0},{16,8},{24,16},{1,25},{9,1},{17,9},{25,17},{2,26},{10... | collective-permute-start | bytes 393224 | tf_op jit(solution)/shard_map/ppermute | solution.py:172
  14.8 11.5 %collective-permute-start.1 = (bf16[512,128]{0,1:T(8,128)(2,1)S(1)}, bf16[512,128]{0,1:T(8,128)(2,1)S(1)}, u32[]{:S(2)}, u32[]{:S(2)}) collective-permute-start(bf16[512,128]{0,1:T(8,128)(2,1)S(1)} %copy.21), channel_id=1, source_target_pairs={{0,2},{1,3},{2,4},{3,5},{4,6},{5,7},{6,0},{7,1},{8,10},{9,11},{10,... | collective-permute-start | bytes 393224 | tf_op jit(solution)/shard_map/ppermute | solution.py:172
  17.3 9.0 %collective-permute-start = (bf16[512,128]{0,1:T(8,128)(2,1)S(1)}, bf16[512,128]{0,1:T(8,128)(2,1)S(1)}, u32[]{:S(2)}, u32[]{:S(2)}) collective-permute-start(bf16[512,128]{0,1:T(8,128)(2,1)S(1)} %copy.21), channel_id=1, source_target_pairs={{0,1},{1,2},{2,3},{3,4},{4,5},{5,6},{6,7},{7,0},{8,9},{9,10},{10,1... | collective-permute-start | bytes 393224 | tf_op jit(solution)/shard_map/ppermute | solution.py:172
  26.3 12.3 %collective-permute-start.2 = (bf16[512,128]{0,1:T(8,128)(2,1)S(1)}, bf16[512,128]{0,1:T(8,128)(2,1)S(1)}, u32[]{:S(2)}, u32[]{:S(2)}) collective-permute-start(bf16[512,128]{0,1:T(8,128)(2,1)S(1)} %copy.21), channel_id=1, source_target_pairs={{0,3},{1,4},{2,5},{3,6},{4,7},{5,0},{6,1},{7,2},{8,11},{9,12},{10,... | collective-permute-start | bytes 393224 | tf_op jit(solution)/shard_map/ppermute | solution.py:172
  26.4 12.3 %collective-permute-start.3 = (bf16[512,128]{0,1:T(8,128)(2,1)S(1)}, bf16[512,128]{0,1:T(8,128)(2,1)S(1)}, u32[]{:S(2)}, u32[]{:S(2)}) collective-permute-start(bf16[512,128]{0,1:T(8,128)(2,1)S(1)} %copy.21), channel_id=1, source_target_pairs={{0,4},{1,5},{2,6},{3,7},{4,0},{5,1},{6,2},{7,3},{8,12},{9,13},{10,... | collective-permute-start | bytes 393224 | tf_op jit(solution)/shard_map/ppermute | solution.py:172
  38.8 13.1 %copy-start.2 = (bf16[4096,128]{0,1:T(8,128)(2,1)}, bf16[4096,128]{0,1:T(8,128)(2,1)S(1)}, u32[]{:S(2)}) copy-start(bf16[4096,128]{0,1:T(8,128)(2,1)S(1)} %constant_dynamic-update-slice_fusion.4) | copy-start | bytes 3145732
  39.5 28.2 %copy-start.4 = (f32[4096]{0:T(1024)S(1)}, f32[4096]{0:T(1024)}, u32[]{:S(2)}) copy-start(f32[4096]{0:T(1024)} %param.6) | copy-start | bytes 49156
  52.0 9.2 %collective-permute-start.16 = (f32[4096]{0:T(1024)S(1)}, f32[4096]{0:T(1024)S(1)}, u32[]{:S(2)}, u32[]{:S(2)}) collective-permute-start(f32[4096]{0:T(1024)S(1)} %bitcast.32), channel_id=1, source_target_pairs={{0,7},{1,0},{2,1},{3,2},{4,3},{5,4},{6,5},{7,6},{8,15},{9,8},{10,9... | collective-permute-start | bytes 49160 | tf_op jit(solution)/shard_map/ppermute | solution.py:172
  56.0 5.1 %collective-permute-start.15 = (f32[4096]{0:T(1024)S(1)}, f32[4096]{0:T(1024)S(1)}, u32[]{:S(2)}, u32[]{:S(2)}) collective-permute-start(f32[4096]{0:T(1024)S(1)} %bitcast.33), channel_id=1, source_target_pairs={{0,6},{1,7},{2,0},{3,1},{4,2},{5,3},{6,4},{7,5},{8,14},{9,15},{10,... | collective-permute-start | bytes 49160 | tf_op jit(solution)/shard_map/ppermute | solution.py:172
  56.0 6.4 %collective-permute-start.14 = (f32[4096]{0:T(1024)S(1)}, f32[4096]{0:T(1024)S(1)}, u32[]{:S(2)}, u32[]{:S(2)}) collective-permute-start(f32[4096]{0:T(1024)S(1)} %bitcast.34), channel_id=1, source_target_pairs={{0,5},{1,6},{2,7},{3,0},{4,1},{5,2},{6,3},{7,4},{8,13},{9,14},{10,... | collective-permute-start | bytes 49160 | tf_op jit(solution)/shard_map/ppermute | solution.py:172
  56.0 6.4 %collective-permute-start.13 = (f32[4096]{0:T(1024)S(1)}, f32[4096]{0:T(1024)S(1)}, u32[]{:S(2)}, u32[]{:S(2)}) collective-permute-start(f32[4096]{0:T(1024)S(1)} %bitcast.35), channel_id=1, source_target_pairs={{0,4},{1,5},{2,6},{3,7},{4,0},{5,1},{6,2},{7,3},{8,12},{9,13},{10,... | collective-permute-start | bytes 49160 | tf_op jit(solution)/shard_map/ppermute | solution.py:172
  59.0 5.5 %collective-permute-start.12 = (f32[4096]{0:T(1024)S(1)}, f32[4096]{0:T(1024)S(1)}, u32[]{:S(2)}, u32[]{:S(2)}) collective-permute-start(f32[4096]{0:T(1024)S(1)} %bitcast.36), channel_id=1, source_target_pairs={{0,3},{1,4},{2,5},{3,6},{4,7},{5,0},{6,1},{7,2},{8,11},{9,12},{10,... | collective-permute-start | bytes 49160 | tf_op jit(solution)/shard_map/ppermute | solution.py:172
  61.1 5.5 %collective-permute-start.11 = (f32[4096]{0:T(1024)S(1)}, f32[4096]{0:T(1024)S(1)}, u32[]{:S(2)}, u32[]{:S(2)}) collective-permute-start(f32[4096]{0:T(1024)S(1)} %bitcast.37), channel_id=1, source_target_pairs={{0,2},{1,3},{2,4},{3,5},{4,6},{5,7},{6,0},{7,1},{8,10},{9,11},{10,... | collective-permute-start | bytes 49160 | tf_op jit(solution)/shard_map/ppermute | solution.py:172
  61.2 6.5 %collective-permute-start.10 = (f32[4096]{0:T(1024)S(1)}, f32[4096]{0:T(1024)S(1)}, u32[]{:S(2)}, u32[]{:S(2)}) collective-permute-start(f32[4096]{0:T(1024)S(1)} %bitcast.38), channel_id=1, source_target_pairs={{0,1},{1,2},{2,3},{3,4},{4,5},{5,6},{6,7},{7,0},{8,9},{9,10},{10,1... | collective-permute-start | bytes 49160 | tf_op jit(solution)/shard_map/ppermute | solution.py:172
  67.7 15.6 %copy-start.6 = (f32[2048]{0:T(1024)S(1)}, f32[2048]{0:T(1024)}, u32[]{:S(2)}) copy-start(f32[2048]{0:T(1024)} %param.7) | copy-start | bytes 24580
  78.7 1.7 collective-permute-start.19
  78.8 3.7 %collective-permute-start.18 = (f32[2048]{0:T(1024)S(1)}, f32[2048]{0:T(1024)S(1)}, u32[]{:S(2)}, u32[]{:S(2)}) collective-permute-start(f32[2048]{0:T(1024)S(1)} %bitcast.47), channel_id=1, source_target_pairs={{0,16},{8,24},{16,0},{24,8},{1,17},{9,25},{17,1},{25,9},{2,18},{10... | collective-permute-start | bytes 24584 | tf_op jit(solution)/shard_map/ppermute | solution.py:172
  80.2 3.1 %collective-permute-start.17 = (f32[2048]{0:T(1024)S(1)}, f32[2048]{0:T(1024)S(1)}, u32[]{:S(2)}, u32[]{:S(2)}) collective-permute-start(f32[2048]{0:T(1024)S(1)} %bitcast.48), channel_id=1, source_target_pairs={{0,8},{8,16},{16,24},{24,0},{1,9},{9,17},{17,25},{25,1},{2,10},{10... | collective-permute-start | bytes 24584 | tf_op jit(solution)/shard_map/ppermute | solution.py:172
  92.2 3.8 %collective-permute-start.20 = (f32[4096]{0:T(1024)S(1)}, f32[4096]{0:T(1024)S(1)}, u32[]{:S(2)}, u32[]{:S(2)}) collective-permute-start(f32[4096]{0:T(1024)S(1)} %bitcast.40), channel_id=1, source_target_pairs={{0,1},{1,0},{2,3},{3,2},{4,5},{5,4},{6,7},{7,6},{8,9},{9,8},{10,11... | collective-permute-start | bytes 49160 | tf_op jit(solution)/shard_map/ppermute | solution.py:198
  96.0 3.9 %collective-permute-start.21 = (f32[4096]{0:T(1024)S(1)}, f32[4096]{0:T(1024)S(1)}, u32[]{:S(2)}, u32[]{:S(2)}) collective-permute-start(f32[4096]{0:T(1024)S(1)} %add.230), channel_id=1, source_target_pairs={{0,2},{1,3},{2,0},{3,1},{4,6},{5,7},{6,4},{7,5},{8,10},{9,11},{10,... | collective-permute-start | bytes 49160 | tf_op jit(solution)/shard_map/ppermute | solution.py:198
  99.9 4.6 %collective-permute-start.22 = (f32[4096]{0:T(1024)S(1)}, f32[4096]{0:T(1024)S(1)}, u32[]{:S(2)}, u32[]{:S(2)}) collective-permute-start(f32[4096]{0:T(1024)S(1)} %add.231), channel_id=1, source_target_pairs={{0,4},{1,5},{2,6},{3,7},{4,0},{5,1},{6,2},{7,3},{8,12},{9,13},{10,... | collective-permute-start | bytes 49160 | tf_op jit(solution)/shard_map/ppermute | solution.py:198
  104.5 9.5 %copy-start.3 = (bf16[4096,128]{0,1:T(8,128)(2,1)S(1)}, bf16[4096,128]{0,1:T(8,128)(2,1)}, u32[]{:S(2)}) copy-start(bf16[4096,128]{0,1:T(8,128)(2,1)} %copy-done.2) | copy-start | bytes 3145732
  112.3 1.2 collective-permute-start.23
  113.5 3.7 %collective-permute-start.24 = (f32[2048]{0:T(1024)S(1)}, f32[2048]{0:T(1024)S(1)}, u32[]{:S(2)}, u32[]{:S(2)}) collective-permute-start(f32[2048]{0:T(1024)S(1)} %add.235), channel_id=1, source_target_pairs={{0,16},{8,24},{16,0},{24,8},{1,17},{9,25},{17,1},{25,9},{2,18},{10... | collective-permute-start | bytes 24584 | tf_op jit(solution)/shard_map/ppermute | solution.py:198
  186.9 2.3 %copy-start = (f32[4096,128]{1,0:T(8,128)}, f32[4096,128]{1,0:T(8,128)S(1)}, u32[]{:S(2)}) copy-start(f32[4096,128]{1,0:T(8,128)S(1)} %get-tuple-element.4) | copy-start | bytes 6291460
  186.9 2.4 %copy-start.1 = (f32[2048,128]{1,0:T(8,128)}, f32[2048,128]{1,0:T(8,128)S(1)}, u32[]{:S(2)}) copy-start(f32[2048,128]{1,0:T(8,128)S(1)} %get-tuple-element.5) | copy-start | bytes 3145732
  187.0 7.1 %collective-permute-start.32 = (bf16[512,128]{1,0:T(8,128)(2,1)S(1)}, bf16[512,128]{1,0:T(8,128)(2,1)S(1)}, u32[]{:S(2)}, u32[]{:S(2)}) collective-permute-start(bf16[512,128]{1,0:T(8,128)(2,1)S(1)} %get-tuple-element.13), channel_id=1, source_target_pairs={{0,8},{8,16},{16,24},{24,0},{1,9},{9,17},{17,25},{25,1},{2,10},{10... | collective-permute-start | bytes 393224 | tf_op jit(solution)/shard_map/ppermute | solution.py:172
  187.3 6.8 %collective-permute-start.34 = (bf16[512,128]{1,0:T(8,128)(2,1)S(1)}, bf16[512,128]{1,0:T(8,128)(2,1)S(1)}, u32[]{:S(2)}, u32[]{:S(2)}) collective-permute-start(bf16[512,128]{1,0:T(8,128)(2,1)S(1)} %get-tuple-element.14), channel_id=1, source_target_pairs={{0,24},{8,0},{16,8},{24,16},{1,25},{9,1},{17,9},{25,17},{2,26},{10... | collective-permute-start | bytes 393224 | tf_op jit(solution)/shard_map/ppermute | solution.py:172
  188.8 6.9 %collective-permute-start.33 = (bf16[512,128]{1,0:T(8,128)(2,1)S(1)}, bf16[512,128]{1,0:T(8,128)(2,1)S(1)}, u32[]{:S(2)}, u32[]{:S(2)}) collective-permute-start(bf16[512,128]{1,0:T(8,128)(2,1)S(1)} %get-tuple-element.15), channel_id=1, source_target_pairs={{0,16},{8,24},{16,0},{24,8},{1,17},{9,25},{17,1},{25,9},{2,18},{10... | collective-permute-start | bytes 393224 | tf_op jit(solution)/shard_map/ppermute | solution.py:172
  189.3 9.2 %collective-permute-start.25 = (bf16[512,128]{1,0:T(8,128)(2,1)S(1)}, bf16[512,128]{1,0:T(8,128)(2,1)S(1)}, u32[]{:S(2)}, u32[]{:S(2)}) collective-permute-start(bf16[512,128]{1,0:T(8,128)(2,1)S(1)} %get-tuple-element.6), channel_id=1, source_target_pairs={{0,1},{1,2},{2,3},{3,4},{4,5},{5,6},{6,7},{7,0},{8,9},{9,10},{10,1... | collective-permute-start | bytes 393224 | tf_op jit(solution)/shard_map/ppermute | solution.py:172
  189.4 9.1 %collective-permute-start.31 = (bf16[512,128]{1,0:T(8,128)(2,1)S(1)}, bf16[512,128]{1,0:T(8,128)(2,1)S(1)}, u32[]{:S(2)}, u32[]{:S(2)}) collective-permute-start(bf16[512,128]{1,0:T(8,128)(2,1)S(1)} %get-tuple-element.7), channel_id=1, source_target_pairs={{0,7},{1,0},{2,1},{3,2},{4,3},{5,4},{6,5},{7,6},{8,15},{9,8},{10,9... | collective-permute-start | bytes 393224 | tf_op jit(solution)/shard_map/ppermute | solution.py:172
  194.1 6.8 %collective-permute-start.30 = (bf16[512,128]{1,0:T(8,128)(2,1)S(1)}, bf16[512,128]{1,0:T(8,128)(2,1)S(1)}, u32[]{:S(2)}, u32[]{:S(2)}) collective-permute-start(bf16[512,128]{1,0:T(8,128)(2,1)S(1)} %get-tuple-element.8), channel_id=1, source_target_pairs={{0,6},{1,7},{2,0},{3,1},{4,2},{5,3},{6,4},{7,5},{8,14},{9,15},{10,... | collective-permute-start | bytes 393224 | tf_op jit(solution)/shard_map/ppermute | solution.py:172
  194.1 9.6 %collective-permute-start.29 = (bf16[512,128]{1,0:T(8,128)(2,1)S(1)}, bf16[512,128]{1,0:T(8,128)(2,1)S(1)}, u32[]{:S(2)}, u32[]{:S(2)}) collective-permute-start(bf16[512,128]{1,0:T(8,128)(2,1)S(1)} %get-tuple-element.9), channel_id=1, source_target_pairs={{0,5},{1,6},{2,7},{3,0},{4,1},{5,2},{6,3},{7,4},{8,13},{9,14},{10,... | collective-permute-start | bytes 393224 | tf_op jit(solution)/shard_map/ppermute | solution.py:172
  195.6 18.0 %collective-permute-start.28 = (bf16[512,128]{1,0:T(8,128)(2,1)S(1)}, bf16[512,128]{1,0:T(8,128)(2,1)S(1)}, u32[]{:S(2)}, u32[]{:S(2)}) collective-permute-start(bf16[512,128]{1,0:T(8,128)(2,1)S(1)} %get-tuple-element.10), channel_id=1, source_target_pairs={{0,4},{1,5},{2,6},{3,7},{4,0},{5,1},{6,2},{7,3},{8,12},{9,13},{10,... | collective-permute-start | bytes 393224 | tf_op jit(solution)/shard_map/ppermute | solution.py:172
  198.4 16.6 %collective-permute-start.27 = (bf16[512,128]{1,0:T(8,128)(2,1)S(1)}, bf16[512,128]{1,0:T(8,128)(2,1)S(1)}, u32[]{:S(2)}, u32[]{:S(2)}) collective-permute-start(bf16[512,128]{1,0:T(8,128)(2,1)S(1)} %get-tuple-element.11), channel_id=1, source_target_pairs={{0,3},{1,4},{2,5},{3,6},{4,7},{5,0},{6,1},{7,2},{8,11},{9,12},{10,... | collective-permute-start | bytes 393224 | tf_op jit(solution)/shard_map/ppermute | solution.py:172
  198.5 16.6 %collective-permute-start.26 = (bf16[512,128]{1,0:T(8,128)(2,1)S(1)}, bf16[512,128]{1,0:T(8,128)(2,1)S(1)}, u32[]{:S(2)}, u32[]{:S(2)}) collective-permute-start(bf16[512,128]{1,0:T(8,128)(2,1)S(1)} %get-tuple-element.12), channel_id=1, source_target_pairs={{0,2},{1,3},{2,4},{3,5},{4,6},{5,7},{6,0},{7,1},{8,10},{9,11},{10,... | collective-permute-start | bytes 393224 | tf_op jit(solution)/shard_map/ppermute | solution.py:172

commit v2 on v1

v2 whole, which is shorter than its diff:
```python
import functools
import math

import jax
import jax.numpy as jnp
from jax import lax
from jax.experimental import pallas as pl
from jax.experimental.pallas import tpu as pltpu
from jax.sharding import PartitionSpec as P

D = 128
ITERS = 3
EPSILON = D / 20.0
LOG2E = math.log2(math.e)
CROSS = 2.0 * LOG2E / EPSILON
NT = (((1,), (1,)), ((), ()))
VMEM = pl.BlockSpec(memory_space=pltpu.VMEM)


def spread(s_ref, sb_ref):
    chunks = s_ref.shape[0]
    turned = jnp.transpose(s_ref[...])
    for k in range(chunks):
        sb_ref[k * 128:(k + 1) * 128, :] = jnp.broadcast_to(turned[:, k:k + 1], (128, 128))


def norms(a_ref, sb_ref, chunk):
    def block(k, _):
        at = pl.multiple_of(k * chunk, chunk)
        a = a_ref[pl.ds(at, chunk), :].astype(jnp.float32)
        total = jnp.sum(a * a, axis=1, keepdims=True) * (-LOG2E / EPSILON)
        sb_ref[pl.ds(at, chunk), :] = jnp.broadcast_to(total, (chunk, 128))
        return 0

    lax.fori_loop(0, a_ref.shape[0] // chunk, block, 0)


def first_kernel(chunk, width, from_norms, a_ref, b_ref, s_ref, mass_ref, o_ref, sb_ref):
    depth, lanes = a_ref.shape[0], b_ref.shape[0]
    tiles = width // 128
    if from_norms:
        norms(a_ref, sb_ref, chunk)
    else:
        spread(s_ref, sb_ref)
    o_ref[:, lanes:] = jnp.log2(mass_ref[...])

    def column(n, _):
        start = pl.multiple_of(n * width, width)
        b = b_ref[pl.ds(start, width), :]

        def step(m, carry):
            peak, total = carry
            at = pl.multiple_of(m * chunk, chunk)
            d = lax.dot_general(a_ref[pl.ds(at, chunk), :], b, NT, preferred_element_type=jnp.float32)
            s = sb_ref[pl.ds(at, chunk), :]
            peaks, totals = [], []
            for q in range(tiles):
                t = (d[:, q * 128:(q + 1) * 128] * CROSS + s).reshape(chunk // 8, 8, 128)
                old = peak[:, q * 128:(q + 1) * 128]
                new = jnp.maximum(old, jnp.max(t, axis=0))
                part = jnp.sum(jnp.exp2(t - new[None]), axis=0)
                peaks.append(new)
                totals.append(total[:, q * 128:(q + 1) * 128] * jnp.exp2(old - new) + part)
            return jnp.concatenate(peaks, axis=1), jnp.concatenate(totals, axis=1)

        init = (jnp.full((8, width), -1e30, jnp.float32), jnp.zeros((8, width), jnp.float32))
        peak, total = lax.fori_loop(0, depth // chunk, step, init, unroll=True)
        top = jnp.max(peak, axis=0, keepdims=True)
        whole = jnp.sum(total * jnp.exp2(peak - top), axis=0, keepdims=True)
        o_ref[:, pl.ds(start, width)] = top + jnp.log2(whole)
        return 0

    lax.fori_loop(0, lanes // width, column, 0)


def sum_kernel(chunk, width, a_ref, b_ref, s_ref, l_ref, o_ref, sb_ref):
    depth, lanes = a_ref.shape[0], b_ref.shape[0]
    tiles = width // 128
    spread(s_ref, sb_ref)

    def column(n, _):
        start = pl.multiple_of(n * width, width)
        b = b_ref[pl.ds(start, width), :]
        l = l_ref[:, pl.ds(start, width)]
        total = [jnp.zeros((8, 128), jnp.float32) for q in range(tiles)]
        for m in range(depth // chunk):
            d = lax.dot_general(a_ref[m * chunk:(m + 1) * chunk, :], b, NT, preferred_element_type=jnp.float32)
            s = sb_ref[m * chunk:(m + 1) * chunk, :]
            for q in range(tiles):
                t = d[:, q * 128:(q + 1) * 128] * CROSS + s + l[:, q * 128:(q + 1) * 128]
                total[q] = total[q] + jnp.sum(jnp.exp2(t).reshape(chunk // 8, 8, 128), axis=0)
        o_ref[:, pl.ds(start, width)] = jnp.sum(jnp.concatenate(total, axis=1), axis=0, keepdims=True)
        return 0

    lax.fori_loop(0, lanes // width, column, 0)


def pass_cost(a, b):
    size = a.shape[0] * b.shape[0]
    return pl.CostEstimate(flops=2 * size * D, bytes_accessed=2 * (a.size + b.size), transcendentals=size)


def first_pass(a, b, s, mass, chunk=512, width=256):
    depth, lanes, extra = a.shape[0], b.shape[0], mass.shape[0]
    from_norms = s is None
    s = jnp.zeros((8, 128), jnp.float32) if from_norms else s.reshape(depth // 128, 128)
    out = pl.pallas_call(
        functools.partial(first_kernel, chunk, width, from_norms),
        out_shape=jax.ShapeDtypeStruct((1, lanes + extra), jnp.float32),
        in_specs=[VMEM] * 4,
        out_specs=VMEM,
        scratch_shapes=[pltpu.VMEM((depth, 128), jnp.float32)],
        compiler_params=pltpu.CompilerParams(vmem_limit_bytes=32 << 20),
        cost_estimate=pass_cost(a, b),
        name="first_pass",
    )(a, b, s, mass.reshape(1, extra))
    return out.reshape(lanes + extra)


def sum_pass(a, b, s, l, chunk=512, width=256):
    depth, lanes = a.shape[0], b.shape[0]
    out = pl.pallas_call(
        functools.partial(sum_kernel, chunk, width),
        out_shape=jax.ShapeDtypeStruct((1, lanes), jnp.float32),
        in_specs=[VMEM] * 4,
        out_specs=VMEM,
        scratch_shapes=[pltpu.VMEM((depth, 128), jnp.float32)],
        compiler_params=pltpu.CompilerParams(vmem_limit_bytes=32 << 20),
        cost_estimate=pass_cost(a, b),
        name="sum_pass",
    )(a, b, s.reshape(depth // 128, 128), l.reshape(1, lanes))
    return out.reshape(lanes)


def final_kernel(chunk, own_x, own_y, x_ref, y_ref, u_ref, v_ref, gi_ref, gis_ref, gc_ref, gcs_ref, ub_ref, acc_ref):
    rows, cols = x_ref.shape[0], y_ref.shape[0]
    spread(u_ref, ub_ref)
    acc_ref[...] = jnp.zeros_like(acc_ref)
    y_one = jnp.concatenate([y_ref[...], jnp.ones((cols, 128), jnp.bfloat16)], axis=1)

    def block(at):
        x = x_ref[pl.ds(at, chunk), :]
        d = lax.dot_general(x, y_ref[...], NT, preferred_element_type=jnp.float32)
        u = ub_ref[pl.ds(at, chunk), :]
        parts = []
        for q in range(cols // 128):
            t = d[:, q * 128:(q + 1) * 128] * CROSS + u + v_ref[:, q * 128:(q + 1) * 128]
            parts.append(jnp.exp2(t).astype(jnp.bfloat16))
        plan = jnp.concatenate(parts, axis=1)
        pulled = jnp.dot(plan, y_one, preferred_element_type=jnp.float32)
        xf = x.astype(jnp.float32)
        xt = jnp.concatenate([jnp.transpose(xf).astype(jnp.bfloat16), jnp.ones((16, chunk), jnp.bfloat16)], axis=0)
        acc_ref[...] += jnp.dot(xt, plan, preferred_element_type=jnp.float32)
        return 2.0 * (pulled[:, 128:] * xf - pulled[:, :128])

    def own_block(k, _):
        at = pl.multiple_of(k * chunk, chunk)
        gi_ref[pl.ds(at, chunk), :] = block(at)
        return 0

    def sent_block(k, _):
        at = pl.multiple_of(k * chunk, chunk)
        gis_ref[pl.ds(pl.multiple_of(at - own_x, chunk), chunk), :] = block(at).astype(jnp.bfloat16)
        return 0

    lax.fori_loop(0, own_x // chunk, own_block, 0)
    lax.fori_loop(own_x // chunk, rows // chunk, sent_block, 0)
    for q in range(cols // 128):
        at = q * 128
        pulled = jnp.transpose(acc_ref[0:128, at:at + 128])
        count = jnp.transpose(jnp.broadcast_to(acc_ref[128:129, at:at + 128], (128, 128)))
        grad = 2.0 * (count * y_ref[at:at + 128, :].astype(jnp.float32) - pulled)
        if at < own_y:
            gc_ref[at:at + 128, :] = grad
        else:
            gcs_ref[at - own_y:at - own_y + 128, :] = grad


def final_pass(x, y, u, v, own_x, own_y, chunk=256):
    rows, cols = x.shape[0], y.shape[0]
    size = rows * cols
    return pl.pallas_call(
        functools.partial(final_kernel, chunk, own_x, own_y),
        out_shape=(
            jax.ShapeDtypeStruct((own_x, D), jnp.float32),
            jax.ShapeDtypeStruct((rows - own_x, D), jnp.bfloat16),
            jax.ShapeDtypeStruct((own_y, D), jnp.float32),
            jax.ShapeDtypeStruct((cols - own_y, D), jnp.float32),
        ),
        in_specs=[VMEM] * 4,
        out_specs=(VMEM,) * 4,
        scratch_shapes=[
            pltpu.VMEM((rows, 128), jnp.float32),
            pltpu.VMEM((144, cols), jnp.float32),
        ],
        compiler_params=pltpu.CompilerParams(vmem_limit_bytes=48 << 20),
        cost_estimate=pl.CostEstimate(flops=6 * size * D, bytes_accessed=4 * D * (rows + cols), transcendentals=size),
        name="final_pass",
    )(x, y, u.reshape(rows // 128, 128), v.reshape(1, cols))


class Groups:
    def __init__(self, nrow, ncol):
        self.count = nrow * ncol
        self.across = [(a << 1) * ncol + b for a in range(nrow // 2) for b in range(2)]
        self.along = [z << 1 for z in range(ncol // 2)]
        self.core = ncol

    def swap(self, value, mask):
        if mask == 0:
            return value
        return lax.ppermute(value, ("row", "col"), [(i, i ^ mask) for i in range(self.count)])


def reordered(value, shift, parts):
    if shift == 0:
        return value
    blocks = value.reshape(parts, -1)
    return jnp.concatenate([blocks[s ^ shift] for s in range(parts)])


def lse2(parts):
    top = functools.reduce(jnp.maximum, parts)
    return top + jnp.log2(sum(jnp.exp2(part - top) for part in parts))


def local(imu, camera, imu_mass, cam_mass):
    nrow, ncol = lax.axis_size("row"), lax.axis_size("col")
    row, col = lax.axis_index("row"), lax.axis_index("col")
    groups = Groups(nrow, ncol)
    swap, across, along, core = groups.swap, groups.across, groups.along, groups.core
    na, nz = len(across), len(along)
    share_x, share_y = imu.shape[0], camera.shape[1]

    x = jnp.concatenate([swap(imu, mask) for mask in across])
    near = [swap(camera[0], mask) for mask in along]
    y = jnp.concatenate(near + [swap(part, core) for part in near])

    def pair(mass, place, share):
        return jnp.concatenate([lax.dynamic_slice_in_dim(mass, (place ^ k) * share, share, 0) for k in range(2)])

    def row_exchange(local_value):
        return [reordered(swap(local_value, mask), s, na) for s, mask in enumerate(across)]

    def halves(value):
        return jnp.concatenate([value[value.shape[0] // 2:], value[:value.shape[0] // 2]])

    sent = first_pass(y, x, None, pair(imu_mass, col, share_x))
    got = [swap(sent, mask) for mask in across]
    size = na * share_x
    log_a = jnp.concatenate([got[2 * a][size:] for a in range(na // 2)])
    u = log_a - lse2([reordered(got[s][:size], s, na) for s in range(na)])

    sent = first_pass(x, y, u, pair(cam_mass, row, share_y))
    size = 2 * nz * share_y
    lse, mass = sent[:size], sent[size:]
    lse = lse2([lse, halves(swap(lse, core))])
    sent = jnp.concatenate([lse, mass])
    got = [swap(sent, mask) for mask in along]

    def turned(value, z):
        half = value.shape[0] // 2
        return jnp.concatenate([reordered(value[:half], z, nz), reordered(value[half:], z, nz)])

    masses = [part[size:].reshape(2, share_y) for part in got]
    log_b = jnp.concatenate([part[0] for part in masses] + [part[1] for part in masses])
    v = log_b - lse2([turned(got[z][:size], z) for z in range(nz)])

    for step in range(1, ITERS):
        total = sum(row_exchange(sum_pass(y, x, v, u, 1024, 512)))
        u = u + log_a - jnp.log2(total)
        part = sum_pass(x, y, u, v, 1024, 512)
        part = part + halves(swap(part, core))
        v = v + log_b - jnp.log2(sum(turned(swap(part, mask), z) for z, mask in enumerate(along)))

    gi, gi_send, gc, gc_send = final_pass(x, y, u, v, share_x, nz * share_y)
    gc = gc + swap(gc_send, core)
    for s in range(1, na):
        gi = gi + swap(gi_send[(s - 1) * share_x:s * share_x], across[s]).astype(jnp.float32)
    grad_cam = gc[:share_y]
    for z in range(1, nz):
        part = gc[z * share_y:(z + 1) * share_y].astype(jnp.bfloat16)
        grad_cam = grad_cam + swap(part, along[z]).astype(jnp.float32)
    return gi, grad_cam[None]


def solution(mesh):
    in_specs = (P(("row", "col"), None), P("col", "row", None), P("row"), P("col"))
    out_specs = (P(("row", "col"), None), P("col", "row", None))
    return jax.shard_map(local, mesh=mesh, in_specs=in_specs, out_specs=out_specs, check_vma=False)
```

time: 218 us -> 159 us (0.73)
  blocking collectives: 36 us -> 0 us
  waiting for transfers between devices: 62.3 us -> 38 us
  starting transfers between devices: 36.5 us -> 44.3 us
  Pallas kernels: 73.5 us -> 67.6 us
    all_gather x2 -> x0, blocking collectives: 36 us -> none  [the longest x1 30.6 us: local(): lax.all_gather(sum_pass(y, x, v, u, 2048), 'col')]
    ppermute x35 -> x38, waiting for transfers between devices: 62.3 us -> 38 us  [swap(): lax.ppermute(value, ('row', 'col'), [(i, i ^ mask) for i in range(self.co...]
    ppermute x35 -> x38, starting transfers between devices: 36.5 us -> 44.3 us  [swap(): lax.ppermute(value, ('row', 'col'), [(i, i ^ mask) for i in range(self.co...]
    pallas_call x4, Pallas kernels: 33.4 us -> 29.1 us  [sum_pass(): pl.pallas_call(functools.partial(sum_kernel, chunk, width), out_shape=jax...]
  transfers between devices with their start and end apart: 35 -> 38, of which waited for: 20 -> 22; matrix products, arithmetic and copies ran while one was open for 2% -> 3% of each run, Pallas kernels for 0% -> 0%
where the time goes in v2:
time: 159 us
  Pallas kernels  67.6 us (43%)
  starting transfers between devices  44.3 us (28%)
  waiting for transfers between devices  38 us (24%)
  local copies, waits for them, and re-layouts  5.23 us (3%)
  other arithmetic  2.64 us (2%)
    ppermute x38, starting transfers between devices, swap(): lax.ppermute(value, ('row', 'col'), [(i, i ^ mask) for i in range(self.co...  44.3 us
    ppermute x38, waiting for transfers between devices, swap(): lax.ppermute(value, ('row', 'col'), [(i, i ^ mask) for i in range(self.co...  38 us
    pallas_call x4, Pallas kernels, sum_pass(): pl.pallas_call(functools.partial(sum_kernel, chunk, width), out_shape=jax...  29.1 us
    pallas_call x2, Pallas kernels, first_pass(): pl.pallas_call(functools.partial(first_kernel, chunk, width, from_norms),...  24 us
    pallas_call x1, Pallas kernels, final_pass(): pl.pallas_call(functools.partial(final_kernel, chunk, own_x, own_y), out_...  14.5 us
  transfers between devices with their start and end apart: 38, of which 22 were waited for; matrix products, arithmetic and copies ran while one was open for 3% of the time, Pallas kernels for 0%

profile of v2, /device:TPU:0, one launch (start us, length us, event | category | flops | bytes accessed | tf_op | source)
XLA Modules:
  0.0 159.0 jit_solution(11386904053587788519)
XLA Ops:
  1.1 4.7 %collective-permute-start.5 = (bf16[512,128]{1,0:T(8,128)(2,1)}, bf16[512,128]{1,0:T(8,128)(2,1)S(1)}, u32[]{:S(2)}, u32[]{:S(2)}) collective-permute-start(bf16[512,128]{1,0:T(8,128)(2,1)} %bitcast.342), channel_id=1, source_target_pairs={{0,6},{1,7},{2,4},{3,5},{4,2},{5,3},{6,0},{7,1},{8,14},{9,15},{10,... | collective-permute-start | bytes 393224 | tf_op jit(solution)/shard_map/ppermute | solution.py:212
  6.5 1.6 %collective-permute-start.1 = (bf16[512,128]{1,0:T(8,128)(2,1)}, bf16[512,128]{1,0:T(8,128)(2,1)S(1)}, u32[]{:S(2)}, u32[]{:S(2)}) collective-permute-start(bf16[512,128]{1,0:T(8,128)(2,1)} %param.4), channel_id=1, source_target_pairs={{0,16},{1,17},{2,18},{3,19},{4,20},{5,21},{6,22},{7,23},{8,24},{9,... | collective-permute-start | bytes 393224 | tf_op jit(solution)/shard_map/ppermute | solution.py:212
  8.1 1.0 constant_dynamic-update-slice_fusion.3
  9.1 0.8 fusion.45
  10.8 4.4 %collective-permute-done.3 = bf16[512,128]{1,0:T(8,128)(2,1)S(1)} collective-permute-done((bf16[512,128]{1,0:T(8,128)(2,1)}, bf16[512,128]{1,0:T(8,128)(2,1)S(1)}, u32[]{:S(2)}, u32[]{:S(2)}) %collective-permute-start.3) | collective-permute-done | bytes 131104 | tf_op jit(solution)/shard_map/ppermute | solution.py:212
  15.2 1.5 collective-permute-start
  16.8 1.5 collective-permute-start.2
  18.3 4.8 %collective-permute-done = bf16[512,128]{1,0:T(8,128)(2,1)S(1)} collective-permute-done((bf16[512,128]{1,0:T(8,128)(2,1)S(1)}, bf16[512,128]{1,0:T(8,128)(2,1)S(1)}, u32[]{:S(2)}, u32[]{:S(2)}) %collective-permute-start) | collective-permute-done | bytes 131104 | tf_op jit(solution)/shard_map/ppermute | solution.py:212
  23.8 0.9 collective-permute-done.7
  24.8 11.6 %first_pass.2 = f32[1,3072]{1,0:T(1,128)S(1)} custom-call(bf16[4096,128]{1,0:T(8,128)(2,1)S(1)} %constant_dynamic-update-slice_fusion.4.a_ref.b_ref.y_ref, bf16[2048,128]{1,0:T(8,128)(2,1)S(1)} %constant_dynamic-update-slice_fusion.b_ref.a_ref.x_ref, f32[8,128]{1,0:T(8,128)S(1)} %broadcast_in_dim.6.s_ref, f32[1,1024]{1,0:T(1,128)S(1)} %bitcast.333), custom_call_target="tpu_custom_call" | custom-call | flops 2147483648 | bytes 1572864 | tf_op jit(solution)/shard_map/first_pass/pallas_call | solution.py:107
  36.4 2.5 %collective-permute-start.12 = (f32[3072]{0:T(1024)S(1)}, f32[3072]{0:T(1024)S(1)}, u32[]{:S(2)}, u32[]{:S(2)}) collective-permute-start(f32[3072]{0:T(1024)S(1)} %bitcast.326), channel_id=1, source_target_pairs={{0,17},{1,16},{2,19},{3,18},{4,21},{5,20},{6,23},{7,22},{8,25},{9,... | collective-permute-start | bytes 36872 | tf_op jit(solution)/shard_map/ppermute | solution.py:212
  40.0 1.0 collective-permute-done.12
  41.1 2.1 %collective-permute-done.10 = f32[3072]{0:T(1024)S(1)} collective-permute-done((f32[3072]{0:T(1024)S(1)}, f32[3072]{0:T(1024)S(1)}, u32[]{:S(2)}, u32[]{:S(2)}) %collective-permute-start.10) | collective-permute-done | bytes 12320 | tf_op jit(solution)/shard_map/ppermute | solution.py:212
  43.3 12.5 %first_pass.3 = f32[1,5120]{1,0:T(1,128)S(1)} custom-call(bf16[2048,128]{1,0:T(8,128)(2,1)S(1)} %constant_dynamic-update-slice_fusion.b_ref.a_ref.x_ref, bf16[4096,128]{1,0:T(8,128)(2,1)S(1)} %constant_dynamic-update-slice_fusion.4.a_ref.b_ref.y_ref, f32[16,128]{1,0:T(8,128)S(1)} %add_subtract_fusion.3.s_ref, f32[1,1024]{1,0:T(1,128)S(1)} %bitcast.334), custom_call_target="tpu_custom_call" | custom-call | flops 2147483648 | bytes 1572864 | tf_op jit(solution)/shard_map/first_pass/pallas_call | solution.py:107
  57.8 2.4 %collective-permute-start.14 = (f32[5120]{0:T(1024)S(1)}, f32[5120]{0:T(1024)S(1)}, u32[]{:S(2)}, u32[]{:S(2)}) collective-permute-start(f32[5120]{0:T(1024)S(1)} %pad_maximum_fusion), channel_id=1, source_target_pairs={{0,2},{1,3},{2,0},{3,1},{4,6},{5,7},{6,4},{7,5},{8,10},{9,11},{10,... | collective-permute-start | bytes 61448 | tf_op jit(solution)/shard_map/ppermute | solution.py:212
  60.4 1.9 %collective-permute-start.15 = (f32[5120]{0:T(1024)S(1)}, f32[5120]{0:T(1024)S(1)}, u32[]{:S(2)}, u32[]{:S(2)}) collective-permute-start(f32[5120]{0:T(1024)S(1)} %pad_maximum_fusion), channel_id=1, source_target_pairs={{0,4},{1,5},{2,6},{3,7},{4,0},{5,1},{6,2},{7,3},{8,12},{9,13},{10,... | collective-permute-start | bytes 61448 | tf_op jit(solution)/shard_map/ppermute | solution.py:212
  62.4 2.7 %collective-permute-done.15 = f32[5120]{0:T(1024)S(1)} collective-permute-done((f32[5120]{0:T(1024)S(1)}, f32[5120]{0:T(1024)S(1)}, u32[]{:S(2)}, u32[]{:S(2)}) %collective-permute-start.15) | collective-permute-done | bytes 20512 | tf_op jit(solution)/shard_map/ppermute | solution.py:212
  66.2 7.0 %sum_pass.4 = f32[1,2048]{1,0:T(1,128)S(1)} custom-call(bf16[4096,128]{1,0:T(8,128)(2,1)S(1)} %constant_dynamic-update-slice_fusion.4.a_ref.b_ref.y_ref, bf16[2048,128]{1,0:T(8,128)(2,1)S(1)} %constant_dynamic-update-slice_fusion.b_ref.a_ref.x_ref, f32[32,128]{1,0:T(8,128)S(1)} %add_subtract_fusion.1.s_ref, f32[1,2048]{1,0:T(1,128)S(1)} %get-tuple-element.160.l_ref), custom_call_target="tpu_custom_call" | custom-call | flops 2147483648 | bytes 1572864 | tf_op jit(solution)/shard_map/sum_pass/pallas_call | solution.py:122
  73.2 1.5 collective-permute-start.19
  74.8 1.5 collective-permute-start.18
  78.4 1.5 collective-permute-done.17
  79.9 7.4 %sum_pass.5 = f32[1,4096]{1,0:T(1,128)S(1)} custom-call(bf16[2048,128]{1,0:T(8,128)(2,1)S(1)} %constant_dynamic-update-slice_fusion.b_ref.a_ref.x_ref, bf16[4096,128]{1,0:T(8,128)(2,1)S(1)} %constant_dynamic-update-slice_fusion.4.a_ref.b_ref.y_ref, f32[16,128]{1,0:T(8,128)S(1)} %fusion.23.s_ref, f32[1,4096]{1,0:T(1,128)S(1)} %get-tuple-element.12.l_ref), custom_call_target="tpu_custom_call" | custom-call | flops 2147483648 | bytes 1572864 | tf_op jit(solution)/shard_map/sum_pass/pallas_call | solution.py:122
  87.4 1.2 collective-permute-done.20
  88.6 3.0 %collective-permute-start.23 = (f32[4096]{0:T(1024)S(1)}, f32[4096]{0:T(1024)S(1)}, u32[]{:S(2)}, u32[]{:S(2)}) collective-permute-start(f32[4096]{0:T(1024)S(1)} %maximum_add_fusion.1), channel_id=1, source_target_pairs={{0,6},{1,7},{2,4},{3,5},{4,2},{5,3},{6,0},{7,1},{8,14},{9,15},{10,... | collective-permute-start | bytes 49160 | tf_op jit(solution)/shard_map/ppermute | solution.py:212
  91.7 1.4 collective-permute-start.21
  93.2 1.0 collective-permute-done.23
  94.2 2.2 %collective-permute-done.22 = f32[4096]{0:T(1024)S(1)} collective-permute-done((f32[4096]{0:T(1024)S(1)}, f32[4096]{0:T(1024)S(1)}, u32[]{:S(2)}, u32[]{:S(2)}) %collective-permute-start.22) | collective-permute-done | bytes 16416 | tf_op jit(solution)/shard_map/ppermute | solution.py:212
  96.7 7.0 %sum_pass.6 = f32[1,2048]{1,0:T(1,128)S(1)} custom-call(bf16[4096,128]{1,0:T(8,128)(2,1)S(1)} %constant_dynamic-update-slice_fusion.4.a_ref.b_ref.y_ref, bf16[2048,128]{1,0:T(8,128)(2,1)S(1)} %constant_dynamic-update-slice_fusion.b_ref.a_ref.x_ref, f32[32,128]{1,0:T(8,128)S(1)} %fusion.9.s_ref, f32[1,2048]{1,0:T(1,128)S(1)} %multiply_subtract_fusion.1.l_ref), custom_call_target="tpu_custom_call" | custom-call | flops 2147483648 | bytes 1572864 | tf_op jit(solution)/shard_map/sum_pass/pallas_call | solution.py:122
  104.2 1.5 collective-permute-start.25
  105.7 1.5 collective-permute-start.24
  107.6 0.7 collective-permute-done.26
  108.3 1.1 collective-permute-done.24
  109.4 7.6 %sum_pass.7 = f32[1,4096]{1,0:T(1,128)S(1)} custom-call(bf16[2048,128]{1,0:T(8,128)(2,1)S(1)} %constant_dynamic-update-slice_fusion.b_ref.a_ref.x_ref, bf16[4096,128]{1,0:T(8,128)(2,1)S(1)} %constant_dynamic-update-slice_fusion.4.a_ref.b_ref.y_ref, f32[16,128]{1,0:T(8,128)S(1)} %fusion.30.s_ref.u_ref, f32[1,4096]{1,0:T(1,128)S(1)} %fusion.3.l_ref), custom_call_target="tpu_custom_call" | custom-call | flops 2147483648 | bytes 1572864 | tf_op jit(solution)/shard_map/sum_pass/pallas_call | solution.py:122
  117.1 1.2 collective-permute-done.27
  118.3 1.3 collective-permute-start.30
  120.2 2.5 %collective-permute-start.28 = (f32[4096]{0:T(1024)S(1)}, f32[4096]{0:T(1024)S(1)}, u32[]{:S(2)}, u32[]{:S(2)}) collective-permute-start(f32[4096]{0:T(1024)S(1)} %maximum_add_fusion.4), channel_id=1, source_target_pairs={{0,2},{1,3},{2,0},{3,1},{4,6},{5,7},{6,4},{7,5},{8,10},{9,11},{10,... | collective-permute-start | bytes 49160 | tf_op jit(solution)/shard_map/ppermute | solution.py:212
  122.7 1.2 collective-permute-done.30
  124.7 14.5 %final_pass.1 = (f32[512,128]{1,0:T(8,128)S(1)}, bf16[1536,128]{1,0:T(8,128)(2,1)S(1)}, f32[2048,128]{1,0:T(8,128)S(1)}, f32[2048,128]{1,0:T(8,128)S(1)}) custom-call(bf16[2048,128]{1,0:T(8,128)(2,1)S(1)} %constant_dynamic-update-slice_fusion.b_ref.a_ref.x_ref, bf16[4096,128]{1,0:T(8,128)(2,1)S(1)} %constant_dynamic-update-slice_fusion.4.a_ref.b_ref.y_ref, ...), custom_call_target="tpu_custom_call" | custom-call | flops 6442450944 | bytes 3145728 | tf_op jit(solution)/shard_map/final_pass/pallas_call | solution.py:182
  139.3 1.6 collective-permute-start.31
  141.4 1.5 collective-permute-start.32
  143.2 2.1 %collective-permute-start.35 = (bf16[512,128]{1,0:T(8,128)(2,1)S(1)}, bf16[512,128]{1,0:T(8,128)(2,1)S(1)}, u32[]{:S(2)}, u32[]{:S(2)}) collective-permute-start(bf16[512,128]{1,0:T(8,128)(2,1)S(1)} %get-tuple-element.14), channel_id=1, source_target_pairs={{0,2},{1,3},{2,0},{3,1},{4,6},{5,7},{6,4},{7,5},{8,10},{9,11},{10,... | collective-permute-start | bytes 393224 | tf_op jit(solution)/shard_map/ppermute | solution.py:212
  145.3 1.3 collective-permute-start.37
  146.6 1.4 collective-permute-done.31
  148.0 1.9 %collective-permute-start.36 = (bf16[512,128]{1,0:T(8,128)(2,1)S(1)}, bf16[512,128]{1,0:T(8,128)(2,1)S(1)}, u32[]{:S(2)}, u32[]{:S(2)}) collective-permute-start(bf16[512,128]{1,0:T(8,128)(2,1)S(1)} %get-tuple-element.16), channel_id=1, source_target_pairs={{0,4},{1,5},{2,6},{3,7},{4,0},{5,1},{6,2},{7,3},{8,12},{9,13},{10,... | collective-permute-start | bytes 393224 | tf_op jit(solution)/shard_map/ppermute | solution.py:212
  149.9 0.8 convert_add_fusion
  150.6 1.9 %collective-permute-done.37 = bf16[512,128]{1,0:T(8,128)(2,1)S(1)} collective-permute-done((bf16[512,128]{1,0:T(8,128)(2,1)S(1)}, bf16[512,128]{1,0:T(8,128)(2,1)S(1)}, u32[]{:S(2)}, u32[]{:S(2)}) %collective-permute-start.37) | collective-permute-done | bytes 131104 | tf_op jit(solution)/shard_map/ppermute | solution.py:212
  152.5 5.8 %collective-permute-done.36 = bf16[512,128]{1,0:T(8,128)(2,1)S(1)} collective-permute-done((bf16[512,128]{1,0:T(8,128)(2,1)S(1)}, bf16[512,128]{1,0:T(8,128)(2,1)S(1)}, u32[]{:S(2)}, u32[]{:S(2)}) %collective-permute-start.36) | collective-permute-done | bytes 131104 | tf_op jit(solution)/shard_map/ppermute | solution.py:212
  158.3 0.8 fusion.2
  (181 shorter events, 13.2 us)
Async XLA Ops:
  0.6 23.1 %collective-permute-start.6 = (bf16[512,128]{1,0:T(8,128)(2,1)}, bf16[512,128]{1,0:T(8,128)(2,1)S(1)}, u32[]{:S(2)}, u32[]{:S(2)}) collective-permute-start(bf16[512,128]{1,0:T(8,128)(2,1)} %bitcast.341), channel_id=1, source_target_pairs={{0,8},{1,9},{2,10},{3,11},{4,12},{5,13},{6,14},{7,15},{8,0},{9,1},... | collective-permute-start | bytes 393224 | tf_op jit(solution)/shard_map/ppermute | solution.py:212
  1.1 15.6 %collective-permute-start.5 = (bf16[512,128]{1,0:T(8,128)(2,1)}, bf16[512,128]{1,0:T(8,128)(2,1)S(1)}, u32[]{:S(2)}, u32[]{:S(2)}) collective-permute-start(bf16[512,128]{1,0:T(8,128)(2,1)} %bitcast.342), channel_id=1, source_target_pairs={{0,6},{1,7},{2,4},{3,5},{4,2},{5,3},{6,0},{7,1},{8,14},{9,15},{10,... | collective-permute-start | bytes 393224 | tf_op jit(solution)/shard_map/ppermute | solution.py:212
  5.8 12.4 %collective-permute-start.4 = (bf16[512,128]{1,0:T(8,128)(2,1)}, bf16[512,128]{1,0:T(8,128)(2,1)S(1)}, u32[]{:S(2)}, u32[]{:S(2)}) collective-permute-start(bf16[512,128]{1,0:T(8,128)(2,1)} %bitcast.343), channel_id=1, source_target_pairs={{0,4},{1,5},{2,6},{3,7},{4,0},{5,1},{6,2},{7,3},{8,12},{9,13},{10,... | collective-permute-start | bytes 393224 | tf_op jit(solution)/shard_map/ppermute | solution.py:212
  5.8 9.4 %collective-permute-start.3 = (bf16[512,128]{1,0:T(8,128)(2,1)}, bf16[512,128]{1,0:T(8,128)(2,1)S(1)}, u32[]{:S(2)}, u32[]{:S(2)}) collective-permute-start(bf16[512,128]{1,0:T(8,128)(2,1)} %bitcast.344), channel_id=1, source_target_pairs={{0,2},{1,3},{2,0},{3,1},{4,6},{5,7},{6,4},{7,5},{8,10},{9,11},{10,... | collective-permute-start | bytes 393224 | tf_op jit(solution)/shard_map/ppermute | solution.py:212
  6.5 16.6 %collective-permute-start.1 = (bf16[512,128]{1,0:T(8,128)(2,1)}, bf16[512,128]{1,0:T(8,128)(2,1)S(1)}, u32[]{:S(2)}, u32[]{:S(2)}) collective-permute-start(bf16[512,128]{1,0:T(8,128)(2,1)} %param.4), channel_id=1, source_target_pairs={{0,16},{1,17},{2,18},{3,19},{4,20},{5,21},{6,22},{7,23},{8,24},{9,... | collective-permute-start | bytes 393224 | tf_op jit(solution)/shard_map/ppermute | solution.py:212
  8.1 1.0 copy-start.3
  9.1 6.1 %copy-start.2 = (bf16[512,128]{1,0:T(8,128)(2,1)S(1)}, bf16[512,128]{1,0:T(8,128)(2,1)}, u32[]{:S(2)}) copy-start(bf16[512,128]{1,0:T(8,128)(2,1)} %param.4) | copy-start | bytes 393220
  10.0 0.7 copy-start.4
  15.2 7.9 %collective-permute-start = (bf16[512,128]{1,0:T(8,128)(2,1)S(1)}, bf16[512,128]{1,0:T(8,128)(2,1)S(1)}, u32[]{:S(2)}, u32[]{:S(2)}) collective-permute-start(bf16[512,128]{1,0:T(8,128)(2,1)S(1)} %copy-done.2), channel_id=1, source_target_pairs={{0,1},{1,0},{2,3},{3,2},{4,5},{5,4},{6,7},{7,6},{8,9},{9,8},{10,11... | collective-permute-start | bytes 393224 | tf_op jit(solution)/shard_map/ppermute | solution.py:212
  16.8 7.0 %collective-permute-start.2 = (bf16[512,128]{1,0:T(8,128)(2,1)S(1)}, bf16[512,128]{1,0:T(8,128)(2,1)S(1)}, u32[]{:S(2)}, u32[]{:S(2)}) collective-permute-start(bf16[512,128]{1,0:T(8,128)(2,1)S(1)} %copy-done.2), channel_id=1, source_target_pairs={{0,17},{1,16},{2,19},{3,18},{4,21},{5,20},{6,23},{7,22},{8,25},{9,... | collective-permute-start | bytes 393224 | tf_op jit(solution)/shard_map/ppermute | solution.py:212
  18.3 6.5 %collective-permute-start.9 = (bf16[512,128]{1,0:T(8,128)(2,1)S(1)}, bf16[512,128]{1,0:T(8,128)(2,1)S(1)}, u32[]{:S(2)}, u32[]{:S(2)}) collective-permute-start(bf16[512,128]{1,0:T(8,128)(2,1)S(1)} %collective-permute-done.5), channel_id=1, source_target_pairs={{0,8},{1,9},{2,10},{3,11},{4,12},{5,13},{6,14},{7,15},{8,0},{9,1},... | collective-permute-start | bytes 393224 | tf_op jit(solution)/shard_map/ppermute | solution.py:212
  23.1 1.6 %collective-permute-start.8 = (bf16[512,128]{1,0:T(8,128)(2,1)S(1)}, bf16[512,128]{1,0:T(8,128)(2,1)S(1)}, u32[]{:S(2)}, u32[]{:S(2)}) collective-permute-start(bf16[512,128]{1,0:T(8,128)(2,1)S(1)} %collective-permute-done.4), channel_id=1, source_target_pairs={{0,8},{1,9},{2,10},{3,11},{4,12},{5,13},{6,14},{7,15},{8,0},{9,1},... | collective-permute-start | bytes 393224 | tf_op jit(solution)/shard_map/ppermute | solution.py:212
  23.1 1.6 collective-permute-start.7
  36.4 4.7 %collective-permute-start.12 = (f32[3072]{0:T(1024)S(1)}, f32[3072]{0:T(1024)S(1)}, u32[]{:S(2)}, u32[]{:S(2)}) collective-permute-start(f32[3072]{0:T(1024)S(1)} %bitcast.326), channel_id=1, source_target_pairs={{0,17},{1,16},{2,19},{3,18},{4,21},{5,20},{6,23},{7,22},{8,25},{9,... | collective-permute-start | bytes 36872 | tf_op jit(solution)/shard_map/ppermute | solution.py:212
  38.9 4.3 %collective-permute-start.11 = (f32[3072]{0:T(1024)S(1)}, f32[3072]{0:T(1024)S(1)}, u32[]{:S(2)}, u32[]{:S(2)}) collective-permute-start(f32[3072]{0:T(1024)S(1)} %bitcast.327), channel_id=1, source_target_pairs={{0,1},{1,0},{2,3},{3,2},{4,5},{5,4},{6,7},{7,6},{8,9},{9,8},{10,11... | collective-permute-start | bytes 36872 | tf_op jit(solution)/shard_map/ppermute | solution.py:212
  39.5 3.7 %collective-permute-start.10 = (f32[3072]{0:T(1024)S(1)}, f32[3072]{0:T(1024)S(1)}, u32[]{:S(2)}, u32[]{:S(2)}) collective-permute-start(f32[3072]{0:T(1024)S(1)} %bitcast.328), channel_id=1, source_target_pairs={{0,16},{1,17},{2,18},{3,19},{4,20},{5,21},{6,22},{7,23},{8,24},{9,... | collective-permute-start | bytes 36872 | tf_op jit(solution)/shard_map/ppermute | solution.py:212
  55.8 0.6 copy-start
  55.8 1.2 collective-permute-start.13
  57.1 0.7 slice-start
  57.8 2.4 %copy-start.1 = (f32[1,5120]{1,0:T(1,128)S(1)}, f32[1,5120]{1,0:T(1,128)}, u32[]{:S(2)}) copy-start(f32[1,5120]{1,0:T(1,128)} %copy-done) | copy-start | bytes 61444
  57.8 4.6 %collective-permute-start.14 = (f32[5120]{0:T(1024)S(1)}, f32[5120]{0:T(1024)S(1)}, u32[]{:S(2)}, u32[]{:S(2)}) collective-permute-start(f32[5120]{0:T(1024)S(1)} %pad_maximum_fusion), channel_id=1, source_target_pairs={{0,2},{1,3},{2,0},{3,1},{4,6},{5,7},{6,4},{7,5},{8,10},{9,11},{10,... | collective-permute-start | bytes 61448 | tf_op jit(solution)/shard_map/ppermute | solution.py:212
  60.2 5.6 %collective-permute-start.16 = (f32[5120]{0:T(1024)S(1)}, f32[5120]{0:T(1024)S(1)}, u32[]{:S(2)}, u32[]{:S(2)}) collective-permute-start(f32[5120]{0:T(1024)S(1)} %pad_maximum_fusion), channel_id=1, source_target_pairs={{0,6},{1,7},{2,4},{3,5},{4,2},{5,3},{6,0},{7,1},{8,14},{9,15},{10,... | collective-permute-start | bytes 61448 | tf_op jit(solution)/shard_map/ppermute | solution.py:212
  60.4 4.7 %collective-permute-start.15 = (f32[5120]{0:T(1024)S(1)}, f32[5120]{0:T(1024)S(1)}, u32[]{:S(2)}, u32[]{:S(2)}) collective-permute-start(f32[5120]{0:T(1024)S(1)} %pad_maximum_fusion), channel_id=1, source_target_pairs={{0,4},{1,5},{2,6},{3,7},{4,0},{5,1},{6,2},{7,3},{8,12},{9,13},{10,... | collective-permute-start | bytes 61448 | tf_op jit(solution)/shard_map/ppermute | solution.py:212
  73.2 4.6 %collective-permute-start.19 = (f32[2048]{0:T(1024)S(1)}, f32[2048]{0:T(1024)S(1)}, u32[]{:S(2)}, u32[]{:S(2)}) collective-permute-start(f32[2048]{0:T(1024)S(1)} %bitcast.322), channel_id=1, source_target_pairs={{0,17},{1,16},{2,19},{3,18},{4,21},{5,20},{6,23},{7,22},{8,25},{9,... | collective-permute-start | bytes 24584 | tf_op jit(solution)/shard_map/ppermute | solution.py:212
  74.8 3.7 %collective-permute-start.18 = (f32[2048]{0:T(1024)S(1)}, f32[2048]{0:T(1024)S(1)}, u32[]{:S(2)}, u32[]{:S(2)}) collective-permute-start(f32[2048]{0:T(1024)S(1)} %bitcast.323), channel_id=1, source_target_pairs={{0,16},{1,17},{2,18},{3,19},{4,20},{5,21},{6,22},{7,23},{8,24},{9,... | collective-permute-start | bytes 24584 | tf_op jit(solution)/shard_map/ppermute | solution.py:212
  76.2 3.7 %collective-permute-start.17 = (f32[2048]{0:T(1024)S(1)}, f32[2048]{0:T(1024)S(1)}, u32[]{:S(2)}, u32[]{:S(2)}) collective-permute-start(f32[2048]{0:T(1024)S(1)} %bitcast.324), channel_id=1, source_target_pairs={{0,1},{1,0},{2,3},{3,2},{4,5},{5,4},{6,7},{7,6},{8,9},{9,8},{10,11... | collective-permute-start | bytes 24584 | tf_op jit(solution)/shard_map/ppermute | solution.py:212
  87.3 1.2 collective-permute-start.20
  88.6 5.6 %collective-permute-start.23 = (f32[4096]{0:T(1024)S(1)}, f32[4096]{0:T(1024)S(1)}, u32[]{:S(2)}, u32[]{:S(2)}) collective-permute-start(f32[4096]{0:T(1024)S(1)} %maximum_add_fusion.1), channel_id=1, source_target_pairs={{0,6},{1,7},{2,4},{3,5},{4,2},{5,3},{6,0},{7,1},{8,14},{9,15},{10,... | collective-permute-start | bytes 49160 | tf_op jit(solution)/shard_map/ppermute | solution.py:212
  91.7 4.7 %collective-permute-start.22 = (f32[4096]{0:T(1024)S(1)}, f32[4096]{0:T(1024)S(1)}, u32[]{:S(2)}, u32[]{:S(2)}) collective-permute-start(f32[4096]{0:T(1024)S(1)} %maximum_add_fusion.1), channel_id=1, source_target_pairs={{0,4},{1,5},{2,6},{3,7},{4,0},{5,1},{6,2},{7,3},{8,12},{9,13},{10,... | collective-permute-start | bytes 49160 | tf_op jit(solution)/shard_map/ppermute | solution.py:212
  91.7 4.8 %collective-permute-start.21 = (f32[4096]{0:T(1024)S(1)}, f32[4096]{0:T(1024)S(1)}, u32[]{:S(2)}, u32[]{:S(2)}) collective-permute-start(f32[4096]{0:T(1024)S(1)} %maximum_add_fusion.1), channel_id=1, source_target_pairs={{0,2},{1,3},{2,0},{3,1},{4,6},{5,7},{6,4},{7,5},{8,10},{9,11},{10,... | collective-permute-start | bytes 49160 | tf_op jit(solution)/shard_map/ppermute | solution.py:212
  103.7 4.6 %collective-permute-start.26 = (f32[2048]{0:T(1024)S(1)}, f32[2048]{0:T(1024)S(1)}, u32[]{:S(2)}, u32[]{:S(2)}) collective-permute-start(f32[2048]{0:T(1024)S(1)} %bitcast.329), channel_id=1, source_target_pairs={{0,17},{1,16},{2,19},{3,18},{4,21},{5,20},{6,23},{7,22},{8,25},{9,... | collective-permute-start | bytes 24584 | tf_op jit(solution)/shard_map/ppermute | solution.py:212
  104.2 4.1 %collective-permute-start.25 = (f32[2048]{0:T(1024)S(1)}, f32[2048]{0:T(1024)S(1)}, u32[]{:S(2)}, u32[]{:S(2)}) collective-permute-start(f32[2048]{0:T(1024)S(1)} %bitcast.330), channel_id=1, source_target_pairs={{0,16},{1,17},{2,18},{3,19},{4,20},{5,21},{6,22},{7,23},{8,24},{9,... | collective-permute-start | bytes 24584 | tf_op jit(solution)/shard_map/ppermute | solution.py:212
  105.7 3.7 %collective-permute-start.24 = (f32[2048]{0:T(1024)S(1)}, f32[2048]{0:T(1024)S(1)}, u32[]{:S(2)}, u32[]{:S(2)}) collective-permute-start(f32[2048]{0:T(1024)S(1)} %bitcast.331), channel_id=1, source_target_pairs={{0,1},{1,0},{2,3},{3,2},{4,5},{5,4},{6,7},{7,6},{8,9},{9,8},{10,11... | collective-permute-start | bytes 24584 | tf_op jit(solution)/shard_map/ppermute | solution.py:212
  117.0 1.2 collective-permute-start.27
  118.3 5.6 %collective-permute-start.30 = (f32[4096]{0:T(1024)S(1)}, f32[4096]{0:T(1024)S(1)}, u32[]{:S(2)}, u32[]{:S(2)}) collective-permute-start(f32[4096]{0:T(1024)S(1)} %maximum_add_fusion.4), channel_id=1, source_target_pairs={{0,6},{1,7},{2,4},{3,5},{4,2},{5,3},{6,0},{7,1},{8,14},{9,15},{10,... | collective-permute-start | bytes 49160 | tf_op jit(solution)/shard_map/ppermute | solution.py:212
  119.6 5.0 %collective-permute-start.29 = (f32[4096]{0:T(1024)S(1)}, f32[4096]{0:T(1024)S(1)}, u32[]{:S(2)}, u32[]{:S(2)}) collective-permute-start(f32[4096]{0:T(1024)S(1)} %maximum_add_fusion.4), channel_id=1, source_target_pairs={{0,4},{1,5},{2,6},{3,7},{4,0},{5,1},{6,2},{7,3},{8,12},{9,13},{10,... | collective-permute-start | bytes 49160 | tf_op jit(solution)/shard_map/ppermute | solution.py:212
  120.2 4.2 %collective-permute-start.28 = (f32[4096]{0:T(1024)S(1)}, f32[4096]{0:T(1024)S(1)}, u32[]{:S(2)}, u32[]{:S(2)}) collective-permute-start(f32[4096]{0:T(1024)S(1)} %maximum_add_fusion.4), channel_id=1, source_target_pairs={{0,2},{1,3},{2,0},{3,1},{4,6},{5,7},{6,4},{7,5},{8,10},{9,11},{10,... | collective-permute-start | bytes 49160 | tf_op jit(solution)/shard_map/ppermute | solution.py:212
  139.2 3.7 %collective-permute-start.34 = (f32[2048,128]{1,0:T(8,128)S(1)}, f32[2048,128]{1,0:T(8,128)S(1)}, u32[]{:S(2)}, u32[]{:S(2)}) collective-permute-start(f32[2048,128]{1,0:T(8,128)S(1)} %get-tuple-element.9), channel_id=1, source_target_pairs={{0,8},{1,9},{2,10},{3,11},{4,12},{5,13},{6,14},{7,15},{8,0},{9,1},... | collective-permute-start | bytes 3145736 | tf_op jit(solution)/shard_map/ppermute | solution.py:212
  139.3 8.7 %collective-permute-start.31 = (bf16[512,128]{1,0:T(8,128)(2,1)S(1)}, bf16[512,128]{1,0:T(8,128)(2,1)S(1)}, u32[]{:S(2)}, u32[]{:S(2)}) collective-permute-start(bf16[512,128]{1,0:T(8,128)(2,1)S(1)} %get-tuple-element.17), channel_id=1, source_target_pairs={{0,1},{1,0},{2,3},{3,2},{4,5},{5,4},{6,7},{7,6},{8,9},{9,8},{10,11... | collective-permute-start | bytes 393224 | tf_op jit(solution)/shard_map/ppermute | solution.py:212
  140.9 9.0 %collective-permute-start.33 = (bf16[512,128]{1,0:T(8,128)(2,1)S(1)}, bf16[512,128]{1,0:T(8,128)(2,1)S(1)}, u32[]{:S(2)}, u32[]{:S(2)}) collective-permute-start(bf16[512,128]{1,0:T(8,128)(2,1)S(1)} %get-tuple-element.18), channel_id=1, source_target_pairs={{0,17},{1,16},{2,19},{3,18},{4,21},{5,20},{6,23},{7,22},{8,25},{9,... | collective-permute-start | bytes 393224 | tf_op jit(solution)/shard_map/ppermute | solution.py:212
  141.4 8.5 %collective-permute-start.32 = (bf16[512,128]{1,0:T(8,128)(2,1)S(1)}, bf16[512,128]{1,0:T(8,128)(2,1)S(1)}, u32[]{:S(2)}, u32[]{:S(2)}) collective-permute-start(bf16[512,128]{1,0:T(8,128)(2,1)S(1)} %get-tuple-element.19), channel_id=1, source_target_pairs={{0,16},{1,17},{2,18},{3,19},{4,20},{5,21},{6,22},{7,23},{8,24},{9,... | collective-permute-start | bytes 393224 | tf_op jit(solution)/shard_map/ppermute | solution.py:212
  143.2 7.4 %collective-permute-start.35 = (bf16[512,128]{1,0:T(8,128)(2,1)S(1)}, bf16[512,128]{1,0:T(8,128)(2,1)S(1)}, u32[]{:S(2)}, u32[]{:S(2)}) collective-permute-start(bf16[512,128]{1,0:T(8,128)(2,1)S(1)} %get-tuple-element.14), channel_id=1, source_target_pairs={{0,2},{1,3},{2,0},{3,1},{4,6},{5,7},{6,4},{7,5},{8,10},{9,11},{10,... | collective-permute-start | bytes 393224 | tf_op jit(solution)/shard_map/ppermute | solution.py:212
  145.3 7.2 %collective-permute-start.37 = (bf16[512,128]{1,0:T(8,128)(2,1)S(1)}, bf16[512,128]{1,0:T(8,128)(2,1)S(1)}, u32[]{:S(2)}, u32[]{:S(2)}) collective-permute-start(bf16[512,128]{1,0:T(8,128)(2,1)S(1)} %get-tuple-element.15), channel_id=1, source_target_pairs={{0,6},{1,7},{2,4},{3,5},{4,2},{5,3},{6,0},{7,1},{8,14},{9,15},{10,... | collective-permute-start | bytes 393224 | tf_op jit(solution)/shard_map/ppermute | solution.py:212
  148.0 10.3 %collective-permute-start.36 = (bf16[512,128]{1,0:T(8,128)(2,1)S(1)}, bf16[512,128]{1,0:T(8,128)(2,1)S(1)}, u32[]{:S(2)}, u32[]{:S(2)}) collective-permute-start(bf16[512,128]{1,0:T(8,128)(2,1)S(1)} %get-tuple-element.16), channel_id=1, source_target_pairs={{0,4},{1,5},{2,6},{3,7},{4,0},{5,1},{6,2},{7,3},{8,12},{9,13},{10,... | collective-permute-start | bytes 393224 | tf_op jit(solution)/shard_map/ppermute | solution.py:212

commit v3 on v2

--- a/solution.py
+++ b/solution.py
@@ -35,64 +35,120 @@
     lax.fori_loop(0, a_ref.shape[0] // chunk, block, 0)
 
 
-def first_kernel(chunk, width, from_norms, a_ref, b_ref, s_ref, mass_ref, o_ref, sb_ref):
+def scores(d, s, l, q):
+    return d * CROSS + s + l[:, q * 128:(q + 1) * 128]
+
+
+def fold(t):
+    return jnp.sum(t.reshape(t.shape[0] // 8, 8, 128), axis=0)
+
+
+def pipelined(chunk, width, a_ref, b_ref, sb_ref, d_ref, head, tile, finish):
     depth, lanes = a_ref.shape[0], b_ref.shape[0]
+    steps, last = depth // chunk, lanes // width - 1
+    tiles = width // 128
+
+    def product(n, m):
+        b = b_ref[pl.ds(pl.multiple_of(n * width, width), width), :]
+        a = a_ref[m * chunk:(m + 1) * chunk, :]
+        d_ref[m % 2] = lax.dot_general(a, b, NT, preferred_element_type=jnp.float32)
+
+    product(0, 0)
+
+    def column(n, _):
+        start = pl.multiple_of(n * width, width)
+        state = head(start)
+        for m in range(steps):
+            if m + 1 < steps:
+                product(n, m + 1)
+            else:
+                product(jnp.minimum(n + 1, last), 0)
+            s = sb_ref[m * chunk:(m + 1) * chunk, :]
+            state = tile(m, lambda q: d_ref[m % 2, :, q * 128:(q + 1) * 128], s, state)
+        finish(start, state)
+        return 0
+
+    lax.fori_loop(0, last + 1, column, 0)
+
+
+def running_max(chunk, width, a_ref, b_ref, sb_ref, o_ref):
+    depth, lanes = a_ref.shape[0], b_ref.shape[0]
+
+    def column(n, _):
+        start = pl.multiple_of(n * width, width)
+        b = b_ref[pl.ds(start, width), :]
+
+        def step(m, carry):
+            peak, total = carry
+            at = pl.multiple_of(m * chunk, chunk)
+            d = lax.dot_general(a_ref[pl.ds(at, chunk), :], b, NT, preferred_element_type=jnp.float32)
+            s = sb_ref[pl.ds(at, chunk), :]
+            peaks, totals = [], []
+            for q in range(width // 128):
+                t = d[:, q * 128:(q + 1) * 128] * CROSS + s
+                old = peak[:, q * 128:(q + 1) * 128]
+                new = jnp.maximum(old, jnp.max(t, axis=0, keepdims=True))
+                part = jnp.sum(jnp.exp2(t - new), axis=0, keepdims=True)
+                peaks.append(new)
+                totals.append(total[:, q * 128:(q + 1) * 128] * jnp.exp2(old - new) + part)
+            return jnp.concatenate(peaks, axis=1), jnp.concatenate(totals, axis=1)
+
+        init = (jnp.full((1, width), -1e30, jnp.float32), jnp.zeros((1, width), jnp.float32))
+        peak, total = lax.fori_loop(0, depth // chunk, step, init)
+        o_ref[:, pl.ds(start, width)] = peak + jnp.log2(total)
+        return 0
+
+    lax.fori_loop(0, lanes // width, column, 0)
+
+
+def first_kernel(chunk, width, from_norms, a_ref, b_ref, s_ref, mass_ref, o_ref, sb_ref, d_ref, top_ref):
+    lanes = b_ref.shape[0]
     tiles = width // 128
     if from_norms:
         norms(a_ref, sb_ref, chunk)
     else:
         spread(s_ref, sb_ref)
     o_ref[:, lanes:] = jnp.log2(mass_ref[...])
-
-    def column(n, _):
-        start = pl.multiple_of(n * width, width)
-        b = b_ref[pl.ds(start, width), :]
-
-        def step(m, carry):
-            peak, total = carry
-            at = pl.multiple_of(m * chunk, chunk)
-            d = lax.dot_general(a_ref[pl.ds(at, chunk), :], b, NT, preferred_element_type=jnp.float32)
-            s = sb_ref[pl.ds(at, chunk), :]
-            peaks, totals = [], []
+    top_ref[...] = jnp.zeros_like(top_ref)
+
+    def tile(m, piece, s, state):
+        if m == 0:
+            state = []
             for q in range(tiles):
-                t = (d[:, q * 128:(q + 1) * 128] * CROSS + s).reshape(chunk // 8, 8, 128)
-                old = peak[:, q * 128:(q + 1) * 128]
-                new = jnp.maximum(old, jnp.max(t, axis=0))
-                part = jnp.sum(jnp.exp2(t - new[None]), axis=0)
-                peaks.append(new)
-                totals.append(total[:, q * 128:(q + 1) * 128] * jnp.exp2(old - new) + part)
-            return jnp.concatenate(peaks, axis=1), jnp.concatenate(totals, axis=1)
-
-        init = (jnp.full((8, width), -1e30, jnp.float32), jnp.zeros((8, width), jnp.float32))
-        peak, total = lax.fori_loop(0, depth // chunk, step, init, unroll=True)
-        top = jnp.max(peak, axis=0, keepdims=True)
-        whole = jnp.sum(total * jnp.exp2(peak - top), axis=0, keepdims=True)
-        o_ref[:, pl.ds(start, width)] = top + jnp.log2(whole)
-        return 0
-
-    lax.fori_loop(0, lanes // width, column, 0)
-
-
-def sum_kernel(chunk, width, a_ref, b_ref, s_ref, l_ref, o_ref, sb_ref):
-    depth, lanes = a_ref.shape[0], b_ref.shape[0]
+                t = piece(q) * CROSS + s
+                peak = jnp.max(t, axis=0, keepdims=True)
+                state.append((peak, fold(jnp.exp2(t - peak))))
+            return state
+        return [(peak, total + fold(jnp.exp2(piece(q) * CROSS + s - peak))) for q, (peak, total) in enumerate(state)]
+
+    def finish(start, state):
+        for q, (peak, total) in enumerate(state):
+            top_ref[...] = jnp.maximum(top_ref[...], total)
+            whole = jnp.sum(total, axis=0, keepdims=True)
+            o_ref[:, pl.ds(pl.multiple_of(start + q * 128, 128), 128)] = peak + jnp.log2(whole)
+
+    pipelined(chunk, width, a_ref, b_ref, sb_ref, d_ref, lambda start: None, tile, finish)
+
+    @pl.when(jnp.logical_not(jnp.max(top_ref[...]) < 2.0 ** 100))
+    def _():
+        running_max(min(chunk, 256), min(width, 256), a_ref, b_ref, sb_ref, o_ref)
+
+
+def sum_kernel(chunk, width, a_ref, b_ref, s_ref, l_ref, o_ref, sb_ref, d_ref):
     tiles = width // 128
     spread(s_ref, sb_ref)
 
-    def column(n, _):
-        start = pl.multiple_of(n * width, width)
-        b = b_ref[pl.ds(start, width), :]
-        l = l_ref[:, pl.ds(start, width)]
-        total = [jnp.zeros((8, 128), jnp.float32) for q in range(tiles)]
-        for m in range(depth // chunk):
-            d = lax.dot_general(a_ref[m * chunk:(m + 1) * chunk, :], b, NT, preferred_element_type=jnp.float32)
-            s = sb_ref[m * chunk:(m + 1) * chunk, :]
-            for q in range(tiles):
-                t = d[:, q * 128:(q + 1) * 128] * CROSS + s + l[:, q * 128:(q + 1) * 128]
-                total[q] = total[q] + jnp.sum(jnp.exp2(t).reshape(chunk // 8, 8, 128), axis=0)
-        o_ref[:, pl.ds(start, width)] = jnp.sum(jnp.concatenate(total, axis=1), axis=0, keepdims=True)
-        return 0
-
-    lax.fori_loop(0, lanes // width, column, 0)
+    def head(start):
+        return l_ref[:, pl.ds(start, width)], [jnp.zeros((8, 128), jnp.float32)] * tiles
+
+    def tile(m, piece, s, state):
+        l, total = state
+        return l, [total[q] + fold(jnp.exp2(scores(piece(q), s, l, q))) for q in range(tiles)]
+
+    def finish(start, state):
+        o_ref[:, pl.ds(start, width)] = jnp.sum(jnp.concatenate(state[1], axis=1), axis=0, keepdims=True)
+
+    pipelined(chunk, width, a_ref, b_ref, sb_ref, d_ref, head, tile, finish)
 
 
 def pass_cost(a, b):
@@ -100,7 +156,7 @@
     return pl.CostEstimate(flops=2 * size * D, bytes_accessed=2 * (a.size + b.size), transcendentals=size)
 
 
-def first_pass(a, b, s, mass, chunk=512, width=256):
+def first_pass(a, b, s, mass, chunk=512, width=512):
     depth, lanes, extra = a.shape[0], b.shape[0], mass.shape[0]
     from_norms = s is None
     s = jnp.zeros((8, 128), jnp.float32) if from_norms else s.reshape(depth // 128, 128)
@@ -109,7 +165,11 @@
         out_shape=jax.ShapeDtypeStruct((1, lanes + extra), jnp.float32),
         in_specs=[VMEM] * 4,
         out_specs=VMEM,
-        scratch_shapes=[pltpu.VMEM((depth, 128), jnp.float32)],
+        scratch_shapes=[
+            pltpu.VMEM((depth, 128), jnp.float32),
+            pltpu.VMEM((2, chunk, width), jnp.float32),
+            pltpu.VMEM((8, 128), jnp.float32),
+        ],
         compiler_params=pltpu.CompilerParams(vmem_limit_bytes=32 << 20),
         cost_estimate=pass_cost(a, b),
         name="first_pass",
@@ -124,7 +184,10 @@
         out_shape=jax.ShapeDtypeStruct((1, lanes), jnp.float32),
         in_specs=[VMEM] * 4,
         out_specs=VMEM,
-        scratch_shapes=[pltpu.VMEM((depth, 128), jnp.float32)],
+        scratch_shapes=[
+            pltpu.VMEM((depth, 128), jnp.float32),
+            pltpu.VMEM((2, chunk, width), jnp.float32),
+        ],
         compiler_params=pltpu.CompilerParams(vmem_limit_bytes=32 << 20),
         cost_estimate=pass_cost(a, b),
         name="sum_pass",
@@ -132,37 +195,62 @@
     return out.reshape(lanes)
 
 
-def final_kernel(chunk, own_x, own_y, x_ref, y_ref, u_ref, v_ref, gi_ref, gis_ref, gc_ref, gcs_ref, ub_ref, acc_ref):
+def final_kernel(chunk, width, own_x, own_y, x_ref, y_ref, u_ref, v_ref, gi_ref, gis_ref, gc_ref, gcs_ref,
+                 ub_ref, d_ref, p_ref, y1_ref, xt_ref, acc_ref, pull_ref):
     rows, cols = x_ref.shape[0], y_ref.shape[0]
+    steps, last = cols // width, rows // chunk - 1
     spread(u_ref, ub_ref)
     acc_ref[...] = jnp.zeros_like(acc_ref)
-    y_one = jnp.concatenate([y_ref[...], jnp.ones((cols, 128), jnp.bfloat16)], axis=1)
-
-    def block(at):
-        x = x_ref[pl.ds(at, chunk), :]
-        d = lax.dot_general(x, y_ref[...], NT, preferred_element_type=jnp.float32)
+    y1_ref[:, :128] = y_ref[...]
+    y1_ref[:, 128:] = jnp.ones((cols, 128), jnp.bfloat16)
+    for k in range(rows // 128):
+        at = k * 128
+        xt_ref[:128, at:at + 128] = jnp.transpose(x_ref[at:at + 128, :].astype(jnp.float32)).astype(jnp.bfloat16)
+    xt_ref[128:, :] = jnp.ones((16, rows), jnp.bfloat16)
+
+    def product(k, j):
+        x = x_ref[pl.ds(pl.multiple_of(k * chunk, chunk), chunk), :]
+        y = y_ref[j * width:(j + 1) * width, :]
+        d_ref[j % 2] = lax.dot_general(x, y, NT, preferred_element_type=jnp.float32)
+
+    def plan(at, j):
         u = ub_ref[pl.ds(at, chunk), :]
-        parts = []
-        for q in range(cols // 128):
-            t = d[:, q * 128:(q + 1) * 128] * CROSS + u + v_ref[:, q * 128:(q + 1) * 128]
-            parts.append(jnp.exp2(t).astype(jnp.bfloat16))
-        plan = jnp.concatenate(parts, axis=1)
-        pulled = jnp.dot(plan, y_one, preferred_element_type=jnp.float32)
-        xf = x.astype(jnp.float32)
-        xt = jnp.concatenate([jnp.transpose(xf).astype(jnp.bfloat16), jnp.ones((16, chunk), jnp.bfloat16)], axis=0)
-        acc_ref[...] += jnp.dot(xt, plan, preferred_element_type=jnp.float32)
-        return 2.0 * (pulled[:, 128:] * xf - pulled[:, :128])
+        for q in range(width // 128):
+            t = scores(d_ref[j % 2, :, q * 128:(q + 1) * 128], u, v_ref[:, j * width:(j + 1) * width], q)
+            p_ref[j % 2, :, q * 128:(q + 1) * 128] = jnp.exp2(t).astype(jnp.bfloat16)
+
+    def pull(at, j):
+        p = p_ref[j % 2]
+        part = jnp.dot(p, y1_ref[j * width:(j + 1) * width, :], preferred_element_type=jnp.float32)
+        pull_ref[...] = part if j == 0 else pull_ref[...] + part
+        xt = xt_ref[:, pl.ds(at, chunk)]
+        acc_ref[:, j * width:(j + 1) * width] += jnp.dot(xt, p, preferred_element_type=jnp.float32)
+
+    def block(k):
+        at = pl.multiple_of(k * chunk, chunk)
+        for j in range(steps):
+            if j + 1 < steps:
+                product(k, j + 1)
+            else:
+                product(jnp.minimum(k + 1, last), 0)
+            if j > 0:
+                pull(at, j - 1)
+            plan(at, j)
+        pull(at, steps - 1)
+        x = x_ref[pl.ds(at, chunk), :].astype(jnp.float32)
+        return at, 2.0 * (pull_ref[:, 128:] * x - pull_ref[:, :128])
 
     def own_block(k, _):
-        at = pl.multiple_of(k * chunk, chunk)
-        gi_ref[pl.ds(at, chunk), :] = block(at)
+        at, grad = block(k)
+        gi_ref[pl.ds(at, chunk), :] = grad
         return 0
 
     def sent_block(k, _):
-        at = pl.multiple_of(k * chunk, chunk)
-        gis_ref[pl.ds(pl.multiple_of(at - own_x, chunk), chunk), :] = block(at).astype(jnp.bfloat16)
-        return 0
-
+        at, grad = block(k)
+        gis_ref[pl.ds(pl.multiple_of(at - own_x, chunk), chunk), :] = grad.astype(jnp.bfloat16)
+        return 0
+
+    product(0, 0)
     lax.fori_loop(0, own_x // chunk, own_block, 0)
     lax.fori_loop(own_x // chunk, rows // chunk, sent_block, 0)
     for q in range(cols // 128):
@@ -176,11 +264,12 @@
             gcs_ref[at - own_y:at - own_y + 128, :] = grad
 
 
-def final_pass(x, y, u, v, own_x, own_y, chunk=256):
+def final_pass(x, y, u, v, own_x, own_y, width=1024):
     rows, cols = x.shape[0], y.shape[0]
+    chunk = math.gcd(own_x, 512)
     size = rows * cols
     return pl.pallas_call(
-        functools.partial(final_kernel, chunk, own_x, own_y),
+        functools.partial(final_kernel, chunk, width, own_x, own_y),
         out_shape=(
             jax.ShapeDtypeStruct((own_x, D), jnp.float32),
             jax.ShapeDtypeStruct((rows - own_x, D), jnp.bfloat16),
@@ -191,7 +280,12 @@
         out_specs=(VMEM,) * 4,
         scratch_shapes=[
             pltpu.VMEM((rows, 128), jnp.float32),
+            pltpu.VMEM((2, chunk, width), jnp.float32),
+            pltpu.VMEM((2, chunk, width), jnp.bfloat16),
+            pltpu.VMEM((cols, 256), jnp.bfloat16),
+            pltpu.VMEM((144, rows), jnp.bfloat16),
             pltpu.VMEM((144, cols), jnp.float32),
+            pltpu.VMEM((chunk, 256), jnp.float32),
         ],
         compiler_params=pltpu.CompilerParams(vmem_limit_bytes=48 << 20),
         cost_estimate=pl.CostEstimate(flops=6 * size * D, bytes_accessed=4 * D * (rows + cols), transcendentals=size),
@@ -267,9 +361,10 @@
     v = log_b - lse2([turned(got[z][:size], z) for z in range(nz)])
 
     for step in range(1, ITERS):
-        total = sum(row_exchange(sum_pass(y, x, v, u, 1024, 512)))
+        chunk = 512 if step == 1 else 256
+        total = sum(row_exchange(sum_pass(y, x, v, u, chunk, 512)))
         u = u + log_a - jnp.log2(total)
-        part = sum_pass(x, y, u, v, 1024, 512)
+        part = sum_pass(x, y, u, v, chunk, 512)
         part = part + halves(swap(part, core))
         v = v + log_b - jnp.log2(sum(turned(swap(part, mask), z) for z, mask in enumerate(along)))
 

time: 159 us -> 219 us (1.38)
  Pallas kernels: 67.6 us -> 129 us
    pallas_call x2, Pallas kernels: 24 us -> 85.1 us  [first_pass(): pl.pallas_call(functools.partial(first_kernel, chunk, width, from_norms),...]
  transfers between devices with their start and end apart: 38 -> 38, of which waited for: 22 -> 22; matrix products, arithmetic and copies ran while one was open for 3% -> 2% of each run, Pallas kernels for 0% -> 0%
where the time goes in v3:
time: 219 us
  Pallas kernels  129 us (59%)
  starting transfers between devices  43.6 us (20%)
  waiting for transfers between devices  36.2 us (17%)
  local copies, waits for them, and re-layouts  5.94 us (3%)
  other arithmetic  2.64 us (1%)
    pallas_call x2, Pallas kernels, first_pass(): pl.pallas_call(functools.partial(first_kernel, chunk, width, from_norms),...  85.1 us
    ppermute x38, starting transfers between devices, swap(): lax.ppermute(value, ('row', 'col'), [(i, i ^ mask) for i in range(self.co...  43.6 us
    ppermute x38, waiting for transfers between devices, swap(): lax.ppermute(value, ('row', 'col'), [(i, i ^ mask) for i in range(self.co...  36.2 us
    pallas_call x4, Pallas kernels, sum_pass(): pl.pallas_call(functools.partial(sum_kernel, chunk, width), out_shape=jax...  29.8 us
    pallas_call x1, Pallas kernels, final_pass(): pl.pallas_call(functools.partial(final_kernel, chunk, width, own_x, own_y...  14.6 us
  transfers between devices with their start and end apart: 38, of which 22 were waited for; matrix products, arithmetic and copies ran while one was open for 2% of the time, Pallas kernels for 0%

profile of v3, /device:TPU:0, one launch (start us, length us, event | category | flops | bytes accessed | tf_op | source)
XLA Modules:
  0.0 219.1 jit_solution(7959682193119236625)
XLA Ops:
  1.1 4.7 %collective-permute-start.5 = (bf16[512,128]{1,0:T(8,128)(2,1)}, bf16[512,128]{1,0:T(8,128)(2,1)S(1)}, u32[]{:S(2)}, u32[]{:S(2)}) collective-permute-start(bf16[512,128]{1,0:T(8,128)(2,1)} %bitcast.342), channel_id=1, source_target_pairs={{0,6},{1,7},{2,4},{3,5},{4,2},{5,3},{6,0},{7,1},{8,14},{9,15},{10,... | collective-permute-start | bytes 393224 | tf_op jit(solution)/shard_map/ppermute | solution.py:306
  6.5 1.6 collective-permute-start.1
  8.1 1.0 constant_dynamic-update-slice_fusion.3
  9.1 0.8 fusion.45
  10.0 0.7 copy-done.4
  10.8 4.4 %collective-permute-done.3 = bf16[512,128]{1,0:T(8,128)(2,1)S(1)} collective-permute-done((bf16[512,128]{1,0:T(8,128)(2,1)}, bf16[512,128]{1,0:T(8,128)(2,1)S(1)}, u32[]{:S(2)}, u32[]{:S(2)}) %collective-permute-start.3) | collective-permute-done | bytes 131104 | tf_op jit(solution)/shard_map/ppermute | solution.py:306
  15.2 1.5 collective-permute-start
  16.8 1.5 collective-permute-start.2
  18.3 4.8 %collective-permute-done = bf16[512,128]{1,0:T(8,128)(2,1)S(1)} collective-permute-done((bf16[512,128]{1,0:T(8,128)(2,1)S(1)}, bf16[512,128]{1,0:T(8,128)(2,1)S(1)}, u32[]{:S(2)}, u32[]{:S(2)}) %collective-permute-start) | collective-permute-done | bytes 131104 | tf_op jit(solution)/shard_map/ppermute | solution.py:306
  23.8 0.9 collective-permute-done.7
  24.8 42.6 %first_pass.2 = f32[1,3072]{1,0:T(1,128)S(1)} custom-call(bf16[4096,128]{1,0:T(8,128)(2,1)S(1)} %constant_dynamic-update-slice_fusion.4.a_ref.b_ref.y_ref, bf16[2048,128]{1,0:T(8,128)(2,1)S(1)} %constant_dynamic-update-slice_fusion.b_ref.a_ref.x_ref, f32[8,128]{1,0:T(8,128)S(1)} %broadcast_in_dim.6.s_ref, f32[1,1024]{1,0:T(1,128)S(1)} %bitcast.333), custom_call_target="tpu_custom_call" | custom-call | flops 2147483648 | bytes 1572864 | tf_op jit(solution)/shard_map/first_pass/pallas_call | solution.py:163
  67.6 3.4 %collective-permute-start.10 = (f32[3072]{0:T(1024)S(1)}, f32[3072]{0:T(1024)S(1)}, u32[]{:S(2)}, u32[]{:S(2)}) collective-permute-start(f32[3072]{0:T(1024)S(1)} %bitcast.328), channel_id=1, source_target_pairs={{0,16},{1,17},{2,18},{3,19},{4,20},{5,21},{6,22},{7,23},{8,24},{9,... | collective-permute-start | bytes 36872 | tf_op jit(solution)/shard_map/ppermute | solution.py:306
  71.0 1.0 collective-permute-done.12
  72.8 42.5 %first_pass.3 = f32[1,5120]{1,0:T(1,128)S(1)} custom-call(bf16[2048,128]{1,0:T(8,128)(2,1)S(1)} %constant_dynamic-update-slice_fusion.b_ref.a_ref.x_ref, bf16[4096,128]{1,0:T(8,128)(2,1)S(1)} %constant_dynamic-update-slice_fusion.4.a_ref.b_ref.y_ref, f32[16,128]{1,0:T(8,128)S(1)} %add_subtract_fusion.3.s_ref, f32[1,1024]{1,0:T(1,128)S(1)} %bitcast.334), custom_call_target="tpu_custom_call" | custom-call | flops 2147483648 | bytes 1572864 | tf_op jit(solution)/shard_map/first_pass/pallas_call | solution.py:163
  116.0 0.7 collective-permute-done.13
  116.7 0.7 slice-done
  117.4 0.7 copy-done.1
  118.7 2.2 collective-permute-start.15
  121.2 2.2 %collective-permute-done.15 = f32[5120]{0:T(1024)S(1)} collective-permute-done((f32[5120]{0:T(1024)S(1)}, f32[5120]{0:T(1024)S(1)}, u32[]{:S(2)}, u32[]{:S(2)}) %collective-permute-start.15) | collective-permute-done | bytes 20512 | tf_op jit(solution)/shard_map/ppermute | solution.py:306
  124.1 7.2 %sum_pass.4 = f32[1,2048]{1,0:T(1,128)S(1)} custom-call(bf16[4096,128]{1,0:T(8,128)(2,1)S(1)} %constant_dynamic-update-slice_fusion.4.a_ref.b_ref.y_ref, bf16[2048,128]{1,0:T(8,128)(2,1)S(1)} %constant_dynamic-update-slice_fusion.b_ref.a_ref.x_ref, f32[32,128]{1,0:T(8,128)S(1)} %add_subtract_fusion.1.s_ref, f32[1,2048]{1,0:T(1,128)S(1)} %get-tuple-element.160.l_ref), custom_call_target="tpu_custom_call" | custom-call | flops 2147483648 | bytes 1572864 | tf_op jit(solution)/shard_map/sum_pass/pallas_call | solution.py:182
  131.3 3.5 %collective-permute-start.19 = (f32[2048]{0:T(1024)S(1)}, f32[2048]{0:T(1024)S(1)}, u32[]{:S(2)}, u32[]{:S(2)}) collective-permute-start(f32[2048]{0:T(1024)S(1)} %bitcast.322), channel_id=1, source_target_pairs={{0,17},{1,16},{2,19},{3,18},{4,21},{5,20},{6,23},{7,22},{8,25},{9,... | collective-permute-start | bytes 24584 | tf_op jit(solution)/shard_map/ppermute | solution.py:306
  136.5 1.9 collective-permute-done.18
  139.1 7.7 %sum_pass.5 = f32[1,4096]{1,0:T(1,128)S(1)} custom-call(bf16[2048,128]{1,0:T(8,128)(2,1)S(1)} %constant_dynamic-update-slice_fusion.b_ref.a_ref.x_ref, bf16[4096,128]{1,0:T(8,128)(2,1)S(1)} %constant_dynamic-update-slice_fusion.4.a_ref.b_ref.y_ref, f32[16,128]{1,0:T(8,128)S(1)} %fusion.23.s_ref, f32[1,4096]{1,0:T(1,128)S(1)} %get-tuple-element.12.l_ref), custom_call_target="tpu_custom_call" | custom-call | flops 2147483648 | bytes 1572864 | tf_op jit(solution)/shard_map/sum_pass/pallas_call | solution.py:182
  146.9 1.2 collective-permute-done.20
  148.1 2.2 %collective-permute-start.23 = (f32[4096]{0:T(1024)S(1)}, f32[4096]{0:T(1024)S(1)}, u32[]{:S(2)}, u32[]{:S(2)}) collective-permute-start(f32[4096]{0:T(1024)S(1)} %maximum_add_fusion.1), channel_id=1, source_target_pairs={{0,6},{1,7},{2,4},{3,5},{4,2},{5,3},{6,0},{7,1},{8,14},{9,15},{10,... | collective-permute-start | bytes 49160 | tf_op jit(solution)/shard_map/ppermute | solution.py:306
  150.4 2.2 %collective-permute-start.21 = (f32[4096]{0:T(1024)S(1)}, f32[4096]{0:T(1024)S(1)}, u32[]{:S(2)}, u32[]{:S(2)}) collective-permute-start(f32[4096]{0:T(1024)S(1)} %maximum_add_fusion.1), channel_id=1, source_target_pairs={{0,2},{1,3},{2,0},{3,1},{4,6},{5,7},{6,4},{7,5},{8,10},{9,11},{10,... | collective-permute-start | bytes 49160 | tf_op jit(solution)/shard_map/ppermute | solution.py:306
  152.7 1.0 collective-permute-done.23
  153.7 1.3 collective-permute-done.22
  155.3 7.2 %sum_pass.6 = f32[1,2048]{1,0:T(1,128)S(1)} custom-call(bf16[4096,128]{1,0:T(8,128)(2,1)S(1)} %constant_dynamic-update-slice_fusion.4.a_ref.b_ref.y_ref, bf16[2048,128]{1,0:T(8,128)(2,1)S(1)} %constant_dynamic-update-slice_fusion.b_ref.a_ref.x_ref, f32[32,128]{1,0:T(8,128)S(1)} %fusion.9.s_ref, f32[1,2048]{1,0:T(1,128)S(1)} %multiply_subtract_fusion.1.l_ref), custom_call_target="tpu_custom_call" | custom-call | flops 2147483648 | bytes 1572864 | tf_op jit(solution)/shard_map/sum_pass/pallas_call | solution.py:182
  162.5 2.9 %collective-permute-start.26 = (f32[2048]{0:T(1024)S(1)}, f32[2048]{0:T(1024)S(1)}, u32[]{:S(2)}, u32[]{:S(2)}) collective-permute-start(f32[2048]{0:T(1024)S(1)} %bitcast.329), channel_id=1, source_target_pairs={{0,17},{1,16},{2,19},{3,18},{4,21},{5,20},{6,23},{7,22},{8,25},{9,... | collective-permute-start | bytes 24584 | tf_op jit(solution)/shard_map/ppermute | solution.py:306
  166.5 0.7 collective-permute-done.26
  167.2 1.9 collective-permute-done.25
  169.1 7.7 %sum_pass.7 = f32[1,4096]{1,0:T(1,128)S(1)} custom-call(bf16[2048,128]{1,0:T(8,128)(2,1)S(1)} %constant_dynamic-update-slice_fusion.b_ref.a_ref.x_ref, bf16[4096,128]{1,0:T(8,128)(2,1)S(1)} %constant_dynamic-update-slice_fusion.4.a_ref.b_ref.y_ref, f32[16,128]{1,0:T(8,128)S(1)} %fusion.30.s_ref.u_ref, f32[1,4096]{1,0:T(1,128)S(1)} %fusion.3.l_ref), custom_call_target="tpu_custom_call" | custom-call | flops 2147483648 | bytes 1572864 | tf_op jit(solution)/shard_map/sum_pass/pallas_call | solution.py:182
  176.9 1.2 collective-permute-done.27
  178.1 1.3 collective-permute-start.30
  180.0 2.5 %collective-permute-start.28 = (f32[4096]{0:T(1024)S(1)}, f32[4096]{0:T(1024)S(1)}, u32[]{:S(2)}, u32[]{:S(2)}) collective-permute-start(f32[4096]{0:T(1024)S(1)} %maximum_add_fusion.4), channel_id=1, source_target_pairs={{0,2},{1,3},{2,0},{3,1},{4,6},{5,7},{6,4},{7,5},{8,10},{9,11},{10,... | collective-permute-start | bytes 49160 | tf_op jit(solution)/shard_map/ppermute | solution.py:306
  182.5 1.2 collective-permute-done.30
  184.5 14.6 %final_pass.1 = (f32[512,128]{1,0:T(8,128)S(1)}, bf16[1536,128]{1,0:T(8,128)(2,1)S(1)}, f32[2048,128]{1,0:T(8,128)S(1)}, f32[2048,128]{1,0:T(8,128)S(1)}) custom-call(bf16[2048,128]{1,0:T(8,128)(2,1)S(1)} %constant_dynamic-update-slice_fusion.b_ref.a_ref.x_ref, bf16[4096,128]{1,0:T(8,128)(2,1)S(1)} %constant_dynamic-update-slice_fusion.4.a_ref.b_ref.y_ref, ...), custom_call_target="tpu_custom_call" | custom-call | flops 6442450944 | bytes 3145728 | tf_op jit(solution)/shard_map/final_pass/pallas_call | solution.py:271
  199.2 1.1 collective-permute-start.31
  200.3 2.4 %collective-permute-start.33 = (bf16[512,128]{1,0:T(8,128)(2,1)S(1)}, bf16[512,128]{1,0:T(8,128)(2,1)S(1)}, u32[]{:S(2)}, u32[]{:S(2)}) collective-permute-start(bf16[512,128]{1,0:T(8,128)(2,1)S(1)} %get-tuple-element.18), channel_id=1, source_target_pairs={{0,17},{1,16},{2,19},{3,18},{4,21},{5,20},{6,23},{7,22},{8,25},{9,... | collective-permute-start | bytes 393224 | tf_op jit(solution)/shard_map/ppermute | solution.py:306
  203.0 2.1 collective-permute-start.35
  205.1 1.3 collective-permute-start.37
  206.4 1.5 collective-permute-done.31
  207.9 1.9 collective-permute-start.36
  209.8 0.8 convert_add_fusion
  210.6 2.1 collective-permute-done.37
  212.6 5.8 %collective-permute-done.36 = bf16[512,128]{1,0:T(8,128)(2,1)S(1)} collective-permute-done((bf16[512,128]{1,0:T(8,128)(2,1)S(1)}, bf16[512,128]{1,0:T(8,128)(2,1)S(1)}, u32[]{:S(2)}, u32[]{:S(2)}) %collective-permute-start.36) | collective-permute-done | bytes 131104 | tf_op jit(solution)/shard_map/ppermute | solution.py:306
  218.4 0.8 fusion.2
  (181 shorter events, 10.9 us)
Async XLA Ops:
  0.6 23.1 %collective-permute-start.6 = (bf16[512,128]{1,0:T(8,128)(2,1)}, bf16[512,128]{1,0:T(8,128)(2,1)S(1)}, u32[]{:S(2)}, u32[]{:S(2)}) collective-permute-start(bf16[512,128]{1,0:T(8,128)(2,1)} %bitcast.341), channel_id=1, source_target_pairs={{0,8},{1,9},{2,10},{3,11},{4,12},{5,13},{6,14},{7,15},{8,0},{9,1},... | collective-permute-start | bytes 393224 | tf_op jit(solution)/shard_map/ppermute | solution.py:306
  1.1 15.6 %collective-permute-start.5 = (bf16[512,128]{1,0:T(8,128)(2,1)}, bf16[512,128]{1,0:T(8,128)(2,1)S(1)}, u32[]{:S(2)}, u32[]{:S(2)}) collective-permute-start(bf16[512,128]{1,0:T(8,128)(2,1)} %bitcast.342), channel_id=1, source_target_pairs={{0,6},{1,7},{2,4},{3,5},{4,2},{5,3},{6,0},{7,1},{8,14},{9,15},{10,... | collective-permute-start | bytes 393224 | tf_op jit(solution)/shard_map/ppermute | solution.py:306
  5.8 12.4 %collective-permute-start.4 = (bf16[512,128]{1,0:T(8,128)(2,1)}, bf16[512,128]{1,0:T(8,128)(2,1)S(1)}, u32[]{:S(2)}, u32[]{:S(2)}) collective-permute-start(bf16[512,128]{1,0:T(8,128)(2,1)} %bitcast.343), channel_id=1, source_target_pairs={{0,4},{1,5},{2,6},{3,7},{4,0},{5,1},{6,2},{7,3},{8,12},{9,13},{10,... | collective-permute-start | bytes 393224 | tf_op jit(solution)/shard_map/ppermute | solution.py:306
  5.8 9.4 %collective-permute-start.3 = (bf16[512,128]{1,0:T(8,128)(2,1)}, bf16[512,128]{1,0:T(8,128)(2,1)S(1)}, u32[]{:S(2)}, u32[]{:S(2)}) collective-permute-start(bf16[512,128]{1,0:T(8,128)(2,1)} %bitcast.344), channel_id=1, source_target_pairs={{0,2},{1,3},{2,0},{3,1},{4,6},{5,7},{6,4},{7,5},{8,10},{9,11},{10,... | collective-permute-start | bytes 393224 | tf_op jit(solution)/shard_map/ppermute | solution.py:306
  6.5 16.6 %collective-permute-start.1 = (bf16[512,128]{1,0:T(8,128)(2,1)}, bf16[512,128]{1,0:T(8,128)(2,1)S(1)}, u32[]{:S(2)}, u32[]{:S(2)}) collective-permute-start(bf16[512,128]{1,0:T(8,128)(2,1)} %param.4), channel_id=1, source_target_pairs={{0,16},{1,17},{2,18},{3,19},{4,20},{5,21},{6,22},{7,23},{8,24},{9,... | collective-permute-start | bytes 393224 | tf_op jit(solution)/shard_map/ppermute | solution.py:306
  8.1 1.0 copy-start.3
  9.1 6.1 %copy-start.2 = (bf16[512,128]{1,0:T(8,128)(2,1)S(1)}, bf16[512,128]{1,0:T(8,128)(2,1)}, u32[]{:S(2)}) copy-start(bf16[512,128]{1,0:T(8,128)(2,1)} %param.4) | copy-start | bytes 393220
  10.0 0.7 copy-start.4
  15.2 7.9 %collective-permute-start = (bf16[512,128]{1,0:T(8,128)(2,1)S(1)}, bf16[512,128]{1,0:T(8,128)(2,1)S(1)}, u32[]{:S(2)}, u32[]{:S(2)}) collective-permute-start(bf16[512,128]{1,0:T(8,128)(2,1)S(1)} %copy-done.2), channel_id=1, source_target_pairs={{0,1},{1,0},{2,3},{3,2},{4,5},{5,4},{6,7},{7,6},{8,9},{9,8},{10,11... | collective-permute-start | bytes 393224 | tf_op jit(solution)/shard_map/ppermute | solution.py:306
  16.8 7.0 %collective-permute-start.2 = (bf16[512,128]{1,0:T(8,128)(2,1)S(1)}, bf16[512,128]{1,0:T(8,128)(2,1)S(1)}, u32[]{:S(2)}, u32[]{:S(2)}) collective-permute-start(bf16[512,128]{1,0:T(8,128)(2,1)S(1)} %copy-done.2), channel_id=1, source_target_pairs={{0,17},{1,16},{2,19},{3,18},{4,21},{5,20},{6,23},{7,22},{8,25},{9,... | collective-permute-start | bytes 393224 | tf_op jit(solution)/shard_map/ppermute | solution.py:306
  18.3 6.5 %collective-permute-start.9 = (bf16[512,128]{1,0:T(8,128)(2,1)S(1)}, bf16[512,128]{1,0:T(8,128)(2,1)S(1)}, u32[]{:S(2)}, u32[]{:S(2)}) collective-permute-start(bf16[512,128]{1,0:T(8,128)(2,1)S(1)} %collective-permute-done.5), channel_id=1, source_target_pairs={{0,8},{1,9},{2,10},{3,11},{4,12},{5,13},{6,14},{7,15},{8,0},{9,1},... | collective-permute-start | bytes 393224 | tf_op jit(solution)/shard_map/ppermute | solution.py:306
  23.1 1.6 collective-permute-start.8
  23.1 1.6 collective-permute-start.7
  67.4 4.7 %collective-permute-start.12 = (f32[3072]{0:T(1024)S(1)}, f32[3072]{0:T(1024)S(1)}, u32[]{:S(2)}, u32[]{:S(2)}) collective-permute-start(f32[3072]{0:T(1024)S(1)} %bitcast.326), channel_id=1, source_target_pairs={{0,17},{1,16},{2,19},{3,18},{4,21},{5,20},{6,23},{7,22},{8,25},{9,... | collective-permute-start | bytes 36872 | tf_op jit(solution)/shard_map/ppermute | solution.py:306
  67.5 5.2 %collective-permute-start.11 = (f32[3072]{0:T(1024)S(1)}, f32[3072]{0:T(1024)S(1)}, u32[]{:S(2)}, u32[]{:S(2)}) collective-permute-start(f32[3072]{0:T(1024)S(1)} %bitcast.327), channel_id=1, source_target_pairs={{0,1},{1,0},{2,3},{3,2},{4,5},{5,4},{6,7},{7,6},{8,9},{9,8},{10,11... | collective-permute-start | bytes 36872 | tf_op jit(solution)/shard_map/ppermute | solution.py:306
  67.6 5.1 %collective-permute-start.10 = (f32[3072]{0:T(1024)S(1)}, f32[3072]{0:T(1024)S(1)}, u32[]{:S(2)}, u32[]{:S(2)}) collective-permute-start(f32[3072]{0:T(1024)S(1)} %bitcast.328), channel_id=1, source_target_pairs={{0,16},{1,17},{2,18},{3,19},{4,20},{5,21},{6,22},{7,23},{8,24},{9,... | collective-permute-start | bytes 36872 | tf_op jit(solution)/shard_map/ppermute | solution.py:306
  115.4 0.6 copy-start
  115.4 1.2 collective-permute-start.13
  116.7 0.7 slice-start
  117.4 0.7 copy-start.1
  117.4 3.8 %collective-permute-start.14 = (f32[5120]{0:T(1024)S(1)}, f32[5120]{0:T(1024)S(1)}, u32[]{:S(2)}, u32[]{:S(2)}) collective-permute-start(f32[5120]{0:T(1024)S(1)} %pad_maximum_fusion), channel_id=1, source_target_pairs={{0,2},{1,3},{2,0},{3,1},{4,6},{5,7},{6,4},{7,5},{8,10},{9,11},{10,... | collective-permute-start | bytes 61448 | tf_op jit(solution)/shard_map/ppermute | solution.py:306
  118.1 5.6 %collective-permute-start.16 = (f32[5120]{0:T(1024)S(1)}, f32[5120]{0:T(1024)S(1)}, u32[]{:S(2)}, u32[]{:S(2)}) collective-permute-start(f32[5120]{0:T(1024)S(1)} %pad_maximum_fusion), channel_id=1, source_target_pairs={{0,6},{1,7},{2,4},{3,5},{4,2},{5,3},{6,0},{7,1},{8,14},{9,15},{10,... | collective-permute-start | bytes 61448 | tf_op jit(solution)/shard_map/ppermute | solution.py:306
  118.7 4.7 %collective-permute-start.15 = (f32[5120]{0:T(1024)S(1)}, f32[5120]{0:T(1024)S(1)}, u32[]{:S(2)}, u32[]{:S(2)}) collective-permute-start(f32[5120]{0:T(1024)S(1)} %pad_maximum_fusion), channel_id=1, source_target_pairs={{0,4},{1,5},{2,6},{3,7},{4,0},{5,1},{6,2},{7,3},{8,12},{9,13},{10,... | collective-permute-start | bytes 61448 | tf_op jit(solution)/shard_map/ppermute | solution.py:306
  131.3 5.2 %collective-permute-start.19 = (f32[2048]{0:T(1024)S(1)}, f32[2048]{0:T(1024)S(1)}, u32[]{:S(2)}, u32[]{:S(2)}) collective-permute-start(f32[2048]{0:T(1024)S(1)} %bitcast.322), channel_id=1, source_target_pairs={{0,17},{1,16},{2,19},{3,18},{4,21},{5,20},{6,23},{7,22},{8,25},{9,... | collective-permute-start | bytes 24584 | tf_op jit(solution)/shard_map/ppermute | solution.py:306
  134.8 3.7 %collective-permute-start.18 = (f32[2048]{0:T(1024)S(1)}, f32[2048]{0:T(1024)S(1)}, u32[]{:S(2)}, u32[]{:S(2)}) collective-permute-start(f32[2048]{0:T(1024)S(1)} %bitcast.323), channel_id=1, source_target_pairs={{0,16},{1,17},{2,18},{3,19},{4,20},{5,21},{6,22},{7,23},{8,24},{9,... | collective-permute-start | bytes 24584 | tf_op jit(solution)/shard_map/ppermute | solution.py:306
  135.5 3.7 %collective-permute-start.17 = (f32[2048]{0:T(1024)S(1)}, f32[2048]{0:T(1024)S(1)}, u32[]{:S(2)}, u32[]{:S(2)}) collective-permute-start(f32[2048]{0:T(1024)S(1)} %bitcast.324), channel_id=1, source_target_pairs={{0,1},{1,0},{2,3},{3,2},{4,5},{5,4},{6,7},{7,6},{8,9},{9,8},{10,11... | collective-permute-start | bytes 24584 | tf_op jit(solution)/shard_map/ppermute | solution.py:306
  146.9 1.2 collective-permute-start.20
  148.1 5.6 %collective-permute-start.23 = (f32[4096]{0:T(1024)S(1)}, f32[4096]{0:T(1024)S(1)}, u32[]{:S(2)}, u32[]{:S(2)}) collective-permute-start(f32[4096]{0:T(1024)S(1)} %maximum_add_fusion.1), channel_id=1, source_target_pairs={{0,6},{1,7},{2,4},{3,5},{4,2},{5,3},{6,0},{7,1},{8,14},{9,15},{10,... | collective-permute-start | bytes 49160 | tf_op jit(solution)/shard_map/ppermute | solution.py:306
  150.4 4.7 %collective-permute-start.22 = (f32[4096]{0:T(1024)S(1)}, f32[4096]{0:T(1024)S(1)}, u32[]{:S(2)}, u32[]{:S(2)}) collective-permute-start(f32[4096]{0:T(1024)S(1)} %maximum_add_fusion.1), channel_id=1, source_target_pairs={{0,4},{1,5},{2,6},{3,7},{4,0},{5,1},{6,2},{7,3},{8,12},{9,13},{10,... | collective-permute-start | bytes 49160 | tf_op jit(solution)/shard_map/ppermute | solution.py:306
  150.4 4.8 %collective-permute-start.21 = (f32[4096]{0:T(1024)S(1)}, f32[4096]{0:T(1024)S(1)}, u32[]{:S(2)}, u32[]{:S(2)}) collective-permute-start(f32[4096]{0:T(1024)S(1)} %maximum_add_fusion.1), channel_id=1, source_target_pairs={{0,2},{1,3},{2,0},{3,1},{4,6},{5,7},{6,4},{7,5},{8,10},{9,11},{10,... | collective-permute-start | bytes 49160 | tf_op jit(solution)/shard_map/ppermute | solution.py:306
  162.5 4.6 %collective-permute-start.26 = (f32[2048]{0:T(1024)S(1)}, f32[2048]{0:T(1024)S(1)}, u32[]{:S(2)}, u32[]{:S(2)}) collective-permute-start(f32[2048]{0:T(1024)S(1)} %bitcast.329), channel_id=1, source_target_pairs={{0,17},{1,16},{2,19},{3,18},{4,21},{5,20},{6,23},{7,22},{8,25},{9,... | collective-permute-start | bytes 24584 | tf_op jit(solution)/shard_map/ppermute | solution.py:306
  165.4 3.7 %collective-permute-start.25 = (f32[2048]{0:T(1024)S(1)}, f32[2048]{0:T(1024)S(1)}, u32[]{:S(2)}, u32[]{:S(2)}) collective-permute-start(f32[2048]{0:T(1024)S(1)} %bitcast.330), channel_id=1, source_target_pairs={{0,16},{1,17},{2,18},{3,19},{4,20},{5,21},{6,22},{7,23},{8,24},{9,... | collective-permute-start | bytes 24584 | tf_op jit(solution)/shard_map/ppermute | solution.py:306
  165.5 3.7 %collective-permute-start.24 = (f32[2048]{0:T(1024)S(1)}, f32[2048]{0:T(1024)S(1)}, u32[]{:S(2)}, u32[]{:S(2)}) collective-permute-start(f32[2048]{0:T(1024)S(1)} %bitcast.331), channel_id=1, source_target_pairs={{0,1},{1,0},{2,3},{3,2},{4,5},{5,4},{6,7},{7,6},{8,9},{9,8},{10,11... | collective-permute-start | bytes 24584 | tf_op jit(solution)/shard_map/ppermute | solution.py:306
  176.8 1.2 collective-permute-start.27
  178.1 5.6 %collective-permute-start.30 = (f32[4096]{0:T(1024)S(1)}, f32[4096]{0:T(1024)S(1)}, u32[]{:S(2)}, u32[]{:S(2)}) collective-permute-start(f32[4096]{0:T(1024)S(1)} %maximum_add_fusion.4), channel_id=1, source_target_pairs={{0,6},{1,7},{2,4},{3,5},{4,2},{5,3},{6,0},{7,1},{8,14},{9,15},{10,... | collective-permute-start | bytes 49160 | tf_op jit(solution)/shard_map/ppermute | solution.py:306
  179.4 5.0 %collective-permute-start.29 = (f32[4096]{0:T(1024)S(1)}, f32[4096]{0:T(1024)S(1)}, u32[]{:S(2)}, u32[]{:S(2)}) collective-permute-start(f32[4096]{0:T(1024)S(1)} %maximum_add_fusion.4), channel_id=1, source_target_pairs={{0,4},{1,5},{2,6},{3,7},{4,0},{5,1},{6,2},{7,3},{8,12},{9,13},{10,... | collective-permute-start | bytes 49160 | tf_op jit(solution)/shard_map/ppermute | solution.py:306
  180.0 4.2 %collective-permute-start.28 = (f32[4096]{0:T(1024)S(1)}, f32[4096]{0:T(1024)S(1)}, u32[]{:S(2)}, u32[]{:S(2)}) collective-permute-start(f32[4096]{0:T(1024)S(1)} %maximum_add_fusion.4), channel_id=1, source_target_pairs={{0,2},{1,3},{2,0},{3,1},{4,6},{5,7},{6,4},{7,5},{8,10},{9,11},{10,... | collective-permute-start | bytes 49160 | tf_op jit(solution)/shard_map/ppermute | solution.py:306
  199.1 3.7 %collective-permute-start.34 = (f32[2048,128]{1,0:T(8,128)S(1)}, f32[2048,128]{1,0:T(8,128)S(1)}, u32[]{:S(2)}, u32[]{:S(2)}) collective-permute-start(f32[2048,128]{1,0:T(8,128)S(1)} %get-tuple-element.9), channel_id=1, source_target_pairs={{0,8},{1,9},{2,10},{3,11},{4,12},{5,13},{6,14},{7,15},{8,0},{9,1},... | collective-permute-start | bytes 3145736 | tf_op jit(solution)/shard_map/ppermute | solution.py:306
  199.2 8.8 %collective-permute-start.31 = (bf16[512,128]{1,0:T(8,128)(2,1)S(1)}, bf16[512,128]{1,0:T(8,128)(2,1)S(1)}, u32[]{:S(2)}, u32[]{:S(2)}) collective-permute-start(bf16[512,128]{1,0:T(8,128)(2,1)S(1)} %get-tuple-element.17), channel_id=1, source_target_pairs={{0,1},{1,0},{2,3},{3,2},{4,5},{5,4},{6,7},{7,6},{8,9},{9,8},{10,11... | collective-permute-start | bytes 393224 | tf_op jit(solution)/shard_map/ppermute | solution.py:306
  200.3 9.5 %collective-permute-start.33 = (bf16[512,128]{1,0:T(8,128)(2,1)S(1)}, bf16[512,128]{1,0:T(8,128)(2,1)S(1)}, u32[]{:S(2)}, u32[]{:S(2)}) collective-permute-start(bf16[512,128]{1,0:T(8,128)(2,1)S(1)} %get-tuple-element.18), channel_id=1, source_target_pairs={{0,17},{1,16},{2,19},{3,18},{4,21},{5,20},{6,23},{7,22},{8,25},{9,... | collective-permute-start | bytes 393224 | tf_op jit(solution)/shard_map/ppermute | solution.py:306
  202.7 7.1 %collective-permute-start.32 = (bf16[512,128]{1,0:T(8,128)(2,1)S(1)}, bf16[512,128]{1,0:T(8,128)(2,1)S(1)}, u32[]{:S(2)}, u32[]{:S(2)}) collective-permute-start(bf16[512,128]{1,0:T(8,128)(2,1)S(1)} %get-tuple-element.19), channel_id=1, source_target_pairs={{0,16},{1,17},{2,18},{3,19},{4,20},{5,21},{6,22},{7,23},{8,24},{9,... | collective-permute-start | bytes 393224 | tf_op jit(solution)/shard_map/ppermute | solution.py:306
  203.0 7.5 %collective-permute-start.35 = (bf16[512,128]{1,0:T(8,128)(2,1)S(1)}, bf16[512,128]{1,0:T(8,128)(2,1)S(1)}, u32[]{:S(2)}, u32[]{:S(2)}) collective-permute-start(bf16[512,128]{1,0:T(8,128)(2,1)S(1)} %get-tuple-element.14), channel_id=1, source_target_pairs={{0,2},{1,3},{2,0},{3,1},{4,6},{5,7},{6,4},{7,5},{8,10},{9,11},{10,... | collective-permute-start | bytes 393224 | tf_op jit(solution)/shard_map/ppermute | solution.py:306
  205.1 7.5 %collective-permute-start.37 = (bf16[512,128]{1,0:T(8,128)(2,1)S(1)}, bf16[512,128]{1,0:T(8,128)(2,1)S(1)}, u32[]{:S(2)}, u32[]{:S(2)}) collective-permute-start(bf16[512,128]{1,0:T(8,128)(2,1)S(1)} %get-tuple-element.15), channel_id=1, source_target_pairs={{0,6},{1,7},{2,4},{3,5},{4,2},{5,3},{6,0},{7,1},{8,14},{9,15},{10,... | collective-permute-start | bytes 393224 | tf_op jit(solution)/shard_map/ppermute | solution.py:306
  207.9 10.4 %collective-permute-start.36 = (bf16[512,128]{1,0:T(8,128)(2,1)S(1)}, bf16[512,128]{1,0:T(8,128)(2,1)S(1)}, u32[]{:S(2)}, u32[]{:S(2)}) collective-permute-start(bf16[512,128]{1,0:T(8,128)(2,1)S(1)} %get-tuple-element.16), channel_id=1, source_target_pairs={{0,4},{1,5},{2,6},{3,7},{4,0},{5,1},{6,2},{7,3},{8,12},{9,13},{10,... | collective-permute-start | bytes 393224 | tf_op jit(solution)/shard_map/ppermute | solution.py:306

commit v4 on v3

v4 whole, which is shorter than its diff:
```python
import functools
import math

import jax
import jax.numpy as jnp
from jax import lax
from jax.experimental import pallas as pl
from jax.experimental.pallas import tpu as pltpu
from jax.sharding import PartitionSpec as P

D = 128
ITERS = 3
EPSILON = D / 20.0
LOG2E = math.log2(math.e)
CROSS = 2.0 * LOG2E / EPSILON
NT = (((1,), (1,)), ((), ()))
VMEM = pl.BlockSpec(memory_space=pltpu.VMEM)


def spread(s_ref, sb_ref):
    chunks = s_ref.shape[0]
    turned = jnp.transpose(s_ref[...])
    for k in range(chunks):
        sb_ref[k * 128:(k + 1) * 128, :] = jnp.broadcast_to(turned[:, k:k + 1], (128, 128))


def norms(a_ref, sb_ref, chunk):
    def block(k, _):
        at = pl.multiple_of(k * chunk, chunk)
        a = a_ref[pl.ds(at, chunk), :].astype(jnp.float32)
        total = jnp.sum(a * a, axis=1, keepdims=True) * (-LOG2E / EPSILON)
        sb_ref[pl.ds(at, chunk), :] = jnp.broadcast_to(total, (chunk, 128))
        return 0

    lax.fori_loop(0, a_ref.shape[0] // chunk, block, 0)


def fold(t):
    return jnp.sum(t.reshape(t.shape[0] // 8, 8, 128), axis=0)


def pipelined(chunk, width, a_ref, b_ref, sb_ref, d_ref, head, tile, finish):
    depth, lanes = a_ref.shape[0], b_ref.shape[0]
    steps, last = depth // chunk, lanes // width - 1
    tiles = width // 128

    def product(n, m):
        b = b_ref[pl.ds(pl.multiple_of(n * width, width), width), :]
        a = a_ref[m * chunk:(m + 1) * chunk, :]
        d_ref[m % 2] = lax.dot_general(a, b, NT, preferred_element_type=jnp.float32)

    product(0, 0)

    def column(n, _):
        start = pl.multiple_of(n * width, width)
        state = head(start)
        for m in range(steps):
            if m + 1 < steps:
                product(n, m + 1)
            else:
                product(jnp.minimum(n + 1, last), 0)
            s = sb_ref[m * chunk:(m + 1) * chunk, :]
            state = tile(m, lambda q: d_ref[m % 2, :, q * 128:(q + 1) * 128], s, state)
        finish(start, state)
        return 0

    lax.fori_loop(0, last + 1, column, 0)


def running_max(chunk, width, a_ref, b_ref, sb_ref, o_ref, e_ref, shift_ref):
    depth, lanes = a_ref.shape[0], b_ref.shape[0]

    def column(n, _):
        start = pl.multiple_of(n * width, width)
        b = b_ref[pl.ds(start, width), :]

        def exponents(m):
            at = pl.multiple_of(m * chunk, chunk)
            d = lax.dot_general(a_ref[pl.ds(at, chunk), :], b, NT, preferred_element_type=jnp.float32)
            s = sb_ref[pl.ds(at, chunk), :]
            return at, [d[:, q * 128:(q + 1) * 128] * CROSS + s for q in range(width // 128)]

        def step(m, carry):
            peak, total = carry
            peaks, totals = [], []
            for q, t in enumerate(exponents(m)[1]):
                old = peak[:, q * 128:(q + 1) * 128]
                new = jnp.maximum(old, jnp.max(t, axis=0, keepdims=True))
                part = jnp.sum(jnp.exp2(t - new), axis=0, keepdims=True)
                peaks.append(new)
                totals.append(total[:, q * 128:(q + 1) * 128] * jnp.exp2(old - new) + part)
            return jnp.concatenate(peaks, axis=1), jnp.concatenate(totals, axis=1)

        def store(m, _):
            at, ts = exponents(m)
            for q, t in enumerate(ts):
                place = pl.ds(pl.multiple_of(start + q * 128, 128), 128)
                e_ref[pl.ds(at, chunk), place] = jnp.exp2(t - shift_ref[:, place]).astype(jnp.bfloat16)
            return 0

        init = (jnp.full((1, width), -1e30, jnp.float32), jnp.zeros((1, width), jnp.float32))
        peak, total = lax.fori_loop(0, depth // chunk, step, init)
        o_ref[:, pl.ds(start, width)] = peak + jnp.log2(total)
        if e_ref is not None:
            shift_ref[:, pl.ds(start, width)] = peak
            lax.fori_loop(0, depth // chunk, store, 0)
        return 0

    lax.fori_loop(0, lanes // width, column, 0)


def first_kernel(chunk, width, is_row, a_ref, b_ref, s_ref, mass_ref, o_ref, *rest):
    e_ref, shift_ref = (None, None) if is_row else rest[:2]
    sb_ref, d_ref, top_ref = rest[-3:]
    lanes = b_ref.shape[0]
    tiles = width // 128
    if is_row:
        norms(a_ref, sb_ref, chunk)
    else:
        spread(s_ref, sb_ref)
    o_ref[:, lanes:] = mass_ref[...]
    top_ref[...] = jnp.zeros_like(top_ref)

    def exponential(m, start, q, t):
        e = jnp.exp2(t)
        if e_ref is not None:
            place = pl.ds(pl.multiple_of(start + q * 128, 128), 128)
            e_ref[m * chunk:(m + 1) * chunk, place] = e.astype(jnp.bfloat16)
        return fold(e)

    def tile(m, piece, s, state):
        start, sums = state
        if m == 0:
            sums = []
            for q in range(tiles):
                t = piece(q) * CROSS + s
                peak = jnp.max(t, axis=0, keepdims=True)
                sums.append((peak, exponential(m, start, q, t - peak)))
            return start, sums
        return start, [
            (peak, total + exponential(m, start, q, piece(q) * CROSS + s - peak))
            for q, (peak, total) in enumerate(sums)
        ]

    def finish(start, state):
        for q, (peak, total) in enumerate(state[1]):
            top_ref[...] = jnp.maximum(top_ref[...], total)
            whole = jnp.sum(total, axis=0, keepdims=True)
            place = pl.ds(pl.multiple_of(start + q * 128, 128), 128)
            o_ref[:, place] = peak + jnp.log2(whole)
            if e_ref is not None:
                shift_ref[:, place] = peak

    pipelined(chunk, width, a_ref, b_ref, sb_ref, d_ref, lambda start: (start, None), tile, finish)

    @pl.when(jnp.logical_not(jnp.max(top_ref[...]) < 2.0 ** 60))
    def _():
        running_max(min(chunk, 256), min(width, 256), a_ref, b_ref, sb_ref, o_ref, e_ref, shift_ref)


def split3(value):
    high = value.astype(jnp.bfloat16)
    rest = value - high.astype(jnp.float32)
    mid = rest.astype(jnp.bfloat16)
    return high, mid, (rest - mid.astype(jnp.float32)).astype(jnp.bfloat16)


def stacked(w_ref):
    high, mid, low = [part.astype(jnp.float32) for part in split3(w_ref[...])]
    shape = (16, w_ref.shape[1])
    place = lax.broadcasted_iota(jnp.int32, shape, 0)
    parts = jnp.where(place == 0, high, jnp.where(place == 1, mid, jnp.where(place == 2, low, 0.0)))
    return parts.astype(jnp.bfloat16)


def row_kernel(width, e_ref, w_ref, o_ref, w16_ref):
    w16_ref[...] = stacked(w_ref)

    def block(k, _):
        at = pl.multiple_of(k * width, width)
        got = lax.dot_general(w16_ref[...], e_ref[pl.ds(at, width), :], NT, preferred_element_type=jnp.float32)
        o_ref[:, pl.ds(at, width)] = jnp.sum(got, axis=0, keepdims=True)
        return 0

    lax.fori_loop(0, e_ref.shape[0] // width, block, 0)


def row_turned_kernel(width, e_ref, w_ref, o_ref, w16_ref):
    w16_ref[...] = stacked(w_ref)

    def block(k, _):
        at = pl.multiple_of(k * width, width)
        got = lax.dot_general(e_ref[pl.ds(at, width), :], w16_ref[...], NT, preferred_element_type=jnp.float32)
        o_ref[:, pl.ds(at, width)] = jnp.sum(jnp.transpose(got), axis=0, keepdims=True)
        return 0

    lax.fori_loop(0, e_ref.shape[0] // width, block, 0)


def col_kernel(width, e_ref, w_ref, o_ref, w16_ref):
    w16_ref[...] = stacked(w_ref)

    def block(k, _):
        at = pl.multiple_of(k * width, width)
        got = jnp.dot(w16_ref[...], e_ref[:, pl.ds(at, width)], preferred_element_type=jnp.float32)
        o_ref[:, pl.ds(at, width)] = jnp.sum(got, axis=0, keepdims=True)
        return 0

    lax.fori_loop(0, e_ref.shape[1] // width, block, 0)


def weighted(kernel, e, w, lanes, width=512):
    out = pl.pallas_call(
        functools.partial(kernel, width),
        out_shape=jax.ShapeDtypeStruct((1, lanes), jnp.float32),
        in_specs=[VMEM] * 2,
        out_specs=VMEM,
        scratch_shapes=[pltpu.VMEM((16, w.shape[0]), jnp.bfloat16)],
        compiler_params=pltpu.CompilerParams(vmem_limit_bytes=16 << 20),
        cost_estimate=pl.CostEstimate(flops=2 * e.size, bytes_accessed=2 * e.size, transcendentals=0),
        name="weighted_sum",
    )(e, w.reshape(1, w.shape[0]))
    return out.reshape(lanes)


def pass_cost(a, b):
    size = a.shape[0] * b.shape[0]
    return pl.CostEstimate(flops=2 * size * D, bytes_accessed=2 * (a.size + b.size), transcendentals=size)


def first_pass(a, b, s, mass, chunk=512, width=512):
    depth, lanes, extra = a.shape[0], b.shape[0], mass.shape[0]
    is_row = s is None
    s = jnp.zeros((8, 128), jnp.float32) if is_row else s.reshape(depth // 128, 128)
    out_shape = [jax.ShapeDtypeStruct((1, lanes + extra), jnp.float32)]
    if not is_row:
        out_shape += [jax.ShapeDtypeStruct((depth, lanes), jnp.bfloat16), jax.ShapeDtypeStruct((1, lanes), jnp.float32)]
    out = pl.pallas_call(
        functools.partial(first_kernel, chunk, width, is_row),
        out_shape=out_shape,
        in_specs=[VMEM] * 4,
        out_specs=[VMEM] * len(out_shape),
        scratch_shapes=[
            pltpu.VMEM((depth, 128), jnp.float32),
            pltpu.VMEM((2, chunk, width), jnp.float32),
            pltpu.VMEM((8, 128), jnp.float32),
        ],
        compiler_params=pltpu.CompilerParams(vmem_limit_bytes=16 << 20),
        cost_estimate=pass_cost(a, b),
        name="first_pass",
    )(a, b, s, mass.reshape(1, extra))
    sent = out[0].reshape(lanes + extra)
    return sent if is_row else (sent, out[1], out[2].reshape(lanes))


def final_kernel(chunk, width, own_x, own_y, x_ref, y_ref, e_ref, alpha_ref, arow_ref, beta_ref, brow_ref,
                 gi_ref, gis_ref, gc_ref, gcs_ref, ab_ref, bb_ref, yb_ref, xa_ref, b16_ref, sums_ref, rb_ref, acc_ref):
    rows, cols = x_ref.shape[0], y_ref.shape[0]
    spread(alpha_ref, ab_ref)
    spread(beta_ref, bb_ref)
    b16_ref[...] = stacked(brow_ref)

    def high_low(value):
        high = value.astype(jnp.bfloat16)
        return high, (value - high.astype(jnp.float32)).astype(jnp.bfloat16)

    for k in range(cols // 512):
        at = k * 512
        yb_ref[at:at + 512, :128], yb_ref[at:at + 512, 128:] = high_low(
            y_ref[at:at + 512, :].astype(jnp.float32) * bb_ref[at:at + 512, :])
    for k in range(rows // 128):
        at = k * 128
        xa = jnp.transpose(x_ref[at:at + 128, :].astype(jnp.float32)) * arow_ref[:, at:at + 128]
        xa_ref[:128, at:at + 128], xa_ref[128:256, at:at + 128] = high_low(xa)
    xa_ref[256:, :] = stacked(arow_ref)

    for k in range(rows // 512):
        got = lax.dot_general(b16_ref[...], e_ref[k * 512:(k + 1) * 512, :], NT, preferred_element_type=jnp.float32)
        got = jnp.sum(got, axis=0, keepdims=True)
        for q in range(4):
            sums_ref[k * 4 + q:k * 4 + q + 1, :] = got[:, q * 128:(q + 1) * 128]
    spread(sums_ref, rb_ref)

    def block(at):
        pulled = jnp.dot(e_ref[pl.ds(at, chunk), :], yb_ref[...], preferred_element_type=jnp.float32)
        scale = 2.0 * ab_ref[pl.ds(at, chunk), :]
        x = x_ref[pl.ds(at, chunk), :].astype(jnp.float32)
        return scale * (rb_ref[pl.ds(at, chunk), :] * x - (pulled[:, :128] + pulled[:, 128:]))

    def own_block(k, _):
        at = pl.multiple_of(k * chunk, chunk)
        gi_ref[pl.ds(at, chunk), :] = block(at)
        return 0

    def sent_block(k, _):
        at = pl.multiple_of(k * chunk, chunk)
        gis_ref[pl.ds(pl.multiple_of(at - own_x, chunk), chunk), :] = block(at).astype(jnp.bfloat16)
        return 0

    lax.fori_loop(0, own_x // chunk, own_block, 0)
    lax.fori_loop(own_x // chunk, rows // chunk, sent_block, 0)

    for k in range(cols // width):
        got = jnp.dot(xa_ref[...], e_ref[:, k * width:(k + 1) * width], preferred_element_type=jnp.float32)
        acc_ref[:, k * width:(k + 1) * width] = got[:128] + got[128:256]
        count = jnp.sum(got[256:], axis=0, keepdims=True)
        for q in range(width // 128):
            at = k * width + q * 128
            whole = jnp.transpose(jnp.broadcast_to(count[:, q * 128:(q + 1) * 128], (128, 128)))
            pulled = jnp.transpose(acc_ref[:, at:at + 128])
            grad = 2.0 * bb_ref[at:at + 128, :] * (whole * y_ref[at:at + 128, :].astype(jnp.float32) - pulled)
            if at < own_y:
                gc_ref[at:at + 128, :] = grad
            else:
                gcs_ref[at - own_y:at - own_y + 128, :] = grad


def final_pass(x, y, e, alpha, beta, own_x, own_y, width=512):
    rows, cols = x.shape[0], y.shape[0]
    size = rows * cols
    chunk = math.gcd(own_x, 512)
    return pl.pallas_call(
        functools.partial(final_kernel, chunk, width, own_x, own_y),
        out_shape=(
            jax.ShapeDtypeStruct((own_x, D), jnp.float32),
            jax.ShapeDtypeStruct((rows - own_x, D), jnp.bfloat16),
            jax.ShapeDtypeStruct((own_y, D), jnp.float32),
            jax.ShapeDtypeStruct((cols - own_y, D), jnp.float32),
        ),
        in_specs=[VMEM] * 7,
        out_specs=(VMEM,) * 4,
        scratch_shapes=[
            pltpu.VMEM((rows, 128), jnp.float32),
            pltpu.VMEM((cols, 128), jnp.float32),
            pltpu.VMEM((cols, 256), jnp.bfloat16),
            pltpu.VMEM((272, rows), jnp.bfloat16),
            pltpu.VMEM((16, cols), jnp.bfloat16),
            pltpu.VMEM((rows // 128, 128), jnp.float32),
            pltpu.VMEM((rows, 128), jnp.float32),
            pltpu.VMEM((128, cols), jnp.float32),
        ],
        compiler_params=pltpu.CompilerParams(vmem_limit_bytes=28 << 20),
        cost_estimate=pl.CostEstimate(flops=8 * size * D, bytes_accessed=2 * size, transcendentals=0),
        name="final_pass",
    )(x, y, e, alpha.reshape(rows // 128, 128), alpha.reshape(1, rows), beta.reshape(cols // 128, 128),
      beta.reshape(1, cols))


class Groups:
    def __init__(self, nrow, ncol):
        self.count = nrow * ncol
        self.across = [(a << 1) * ncol + b for a in range(nrow // 2) for b in range(2)]
        self.along = [z << 1 for z in range(ncol // 2)]
        self.core = ncol

    def swap(self, value, mask):
        if mask == 0:
            return value
        return lax.ppermute(value, ("row", "col"), [(i, i ^ mask) for i in range(self.count)])


def reordered(value, shift, parts):
    if shift == 0:
        return value
    blocks = value.reshape(parts, -1)
    return jnp.concatenate([blocks[s ^ shift] for s in range(parts)])


def lse2(parts):
    top = functools.reduce(jnp.maximum, parts)
    return top + jnp.log2(sum(jnp.exp2(part - top) for part in parts))


def local(imu, camera, imu_mass, cam_mass):
    nrow, ncol = lax.axis_size("row"), lax.axis_size("col")
    row, col = lax.axis_index("row"), lax.axis_index("col")
    groups = Groups(nrow, ncol)
    swap, across, along, core = groups.swap, groups.across, groups.along, groups.core
    na, nz = len(across), len(along)
    share_x, share_y = imu.shape[0], camera.shape[1]

    x = jnp.concatenate([swap(imu, mask) for mask in across])
    near = [swap(camera[0], mask) for mask in along]
    y = jnp.concatenate(near + [swap(part, core) for part in near])

    def pair(mass, place, share):
        return jnp.concatenate([lax.dynamic_slice_in_dim(mass, (place ^ k) * share, share, 0) for k in range(2)])

    def row_exchange(local_value):
        return [reordered(swap(local_value, mask), s, na) for s, mask in enumerate(across)]

    def halves(value):
        return jnp.concatenate([value[value.shape[0] // 2:], value[:value.shape[0] // 2]])

    sent = first_pass(y, x, None, pair(imu_mass, col, share_x))
    got = [swap(sent, mask) for mask in across]
    size = na * share_x
    mass_a = jnp.concatenate([got[2 * a][size:] for a in range(na // 2)])
    u = jnp.log2(mass_a) - lse2([reordered(got[s][:size], s, na) for s in range(na)])

    sent, e, shift = first_pass(x, y, u, pair(cam_mass, row, share_y))
    size = 2 * nz * share_y
    lse, mass = sent[:size], sent[size:]
    lse = lse2([lse, halves(swap(lse, core))])
    sent = jnp.concatenate([lse, mass])
    got = [swap(sent, mask) for mask in along]

    def turned(value, z):
        half = value.shape[0] // 2
        return jnp.concatenate([reordered(value[:half], z, nz), reordered(value[half:], z, nz)])

    masses = [part[size:].reshape(2, share_y) for part in got]
    mass_b = jnp.concatenate([part[0] for part in masses] + [part[1] for part in masses])
    v = jnp.log2(mass_b) - lse2([turned(got[z][:size], z) for z in range(nz)])

    first_beta = beta = jnp.exp2(v + shift)
    for step in range(1, ITERS):
        kernel = row_kernel if step == 1 else row_turned_kernel
        alpha = mass_a / sum(row_exchange(weighted(kernel, e, beta, x.shape[0])))
        part = first_beta * weighted(col_kernel, e, alpha, y.shape[0])
        part = part + halves(swap(part, core))
        beta = first_beta * (mass_b / sum(turned(swap(part, mask), z) for z, mask in enumerate(along)))

    gi, gi_send, gc, gc_send = final_pass(x, y, e, alpha, beta, share_x, nz * share_y)
    gc = gc + swap(gc_send, core)
    for s in range(1, na):
        gi = gi + swap(gi_send[(s - 1) * share_x:s * share_x], across[s]).astype(jnp.float32)
    grad_cam = gc[:share_y]
    for z in range(1, nz):
        part = gc[z * share_y:(z + 1) * share_y].astype(jnp.bfloat16)
        grad_cam = grad_cam + swap(part, along[z]).astype(jnp.float32)
    return gi, grad_cam[None]


def solution(mesh):
    in_specs = (P(("row", "col"), None), P("col", "row", None), P("row"), P("col"))
    out_specs = (P(("row", "col"), None), P("col", "row", None))
    return jax.shard_map(local, mesh=mesh, in_specs=in_specs, out_specs=out_specs, check_vma=False)
```

time: 219 us -> 247 us (1.13)
  Pallas kernels: 129 us -> 149 us
  local copies, waits for them, and re-layouts: 5.94 us -> 10.9 us
    pallas_call x6, Pallas kernels: 115 us -> 135 us  [the longest x2 118 us: first_pass(): pl.pallas_call(functools.partial(first_kernel, chunk, width, is_row), out...]
    unnamed x76 -> x82, local copies, waits for them, and re-layouts: 3.51 us -> 8.32 us
  transfers between devices with their start and end apart: 38 -> 38, of which waited for: 22 -> 24; matrix products, arithmetic and copies ran while one was open for 2% -> 2% of each run, Pallas kernels for 0% -> 0%
where the time goes in v4:
time: 247 us; the launch traced here: 246 us
  Pallas kernels  149 us (60%)
  starting transfers between devices  45.9 us (19%)
  waiting for transfers between devices  36.6 us (15%)
  local copies, waits for them, and re-layouts  10.9 us (4%)
  other arithmetic  2.55 us (1%)
    pallas_call x2, Pallas kernels, first_pass(): pl.pallas_call(functools.partial(first_kernel, chunk, width, is_row), out...  118 us
    ppermute x38, starting transfers between devices, swap(): lax.ppermute(value, ('row', 'col'), [(i, i ^ mask) for i in range(self.co...  45.9 us
    ppermute x38, waiting for transfers between devices, swap(): lax.ppermute(value, ('row', 'col'), [(i, i ^ mask) for i in range(self.co...  36.6 us
    pallas_call x4, Pallas kernels, weighted(): pl.pallas_call(functools.partial(kernel, width), out_shape=jax.ShapeDtype...  16.6 us
    pallas_call x1, Pallas kernels, final_pass(): pl.pallas_call(functools.partial(final_kernel, chunk, width, own_x, own_y...  14.6 us
    unnamed x82, local copies, waits for them, and re-layouts  8.32 us
  transfers between devices with their start and end apart: 38, of which 24 were waited for; matrix products, arithmetic and copies ran while one was open for 2% of the time, Pallas kernels for 0%

profile of v4, /device:TPU:0, one launch (start us, length us, event | category | flops | bytes accessed | tf_op | source)
XLA Modules:
  0.0 246.4 jit_solution(10925083067707883939)
XLA Ops:
  1.1 4.7 %collective-permute-start.5 = (bf16[512,128]{1,0:T(8,128)(2,1)}, bf16[512,128]{1,0:T(8,128)(2,1)S(1)}, u32[]{:S(2)}, u32[]{:S(2)}) collective-permute-start(bf16[512,128]{1,0:T(8,128)(2,1)} %bitcast.324), channel_id=1, source_target_pairs={{0,6},{1,7},{2,4},{3,5},{4,2},{5,3},{6,0},{7,1},{8,14},{9,15},{10,... | collective-permute-start | bytes 393224 | tf_op jit(solution)/shard_map/ppermute | solution.py:359
  6.5 1.6 collective-permute-start.1
  8.1 0.9 constant_dynamic-update-slice_fusion.3
  9.1 0.9 constant_dynamic-update-slice_fusion.11
  11.7 3.5 %collective-permute-done.3 = bf16[512,128]{1,0:T(8,128)(2,1)S(1)} collective-permute-done((bf16[512,128]{1,0:T(8,128)(2,1)}, bf16[512,128]{1,0:T(8,128)(2,1)S(1)}, u32[]{:S(2)}, u32[]{:S(2)}) %collective-permute-start.3) | collective-permute-done | bytes 131104 | tf_op jit(solution)/shard_map/ppermute | solution.py:359
  15.2 1.5 collective-permute-start
  16.8 1.5 collective-permute-start.2
  18.3 5.0 %collective-permute-done = bf16[512,128]{1,0:T(8,128)(2,1)S(1)} collective-permute-done((bf16[512,128]{1,0:T(8,128)(2,1)}, bf16[512,128]{1,0:T(8,128)(2,1)S(1)}, u32[]{:S(2)}, u32[]{:S(2)}) %collective-permute-start) | collective-permute-done | bytes 131104 | tf_op jit(solution)/shard_map/ppermute | solution.py:359
  24.0 0.9 collective-permute-done.7
  25.0 42.3 %first_pass.2 = f32[1,3072]{1,0:T(1,128)S(1)} custom-call(bf16[4096,128]{1,0:T(8,128)(2,1)S(1)} %constant_dynamic-update-slice_fusion.4.a_ref.b_ref.y_ref, bf16[2048,128]{1,0:T(8,128)(2,1)S(1)} %constant_dynamic-update-slice_fusion.b_ref.a_ref.x_ref, f32[8,128]{1,0:T(8,128)S(1)} %broadcast_in_dim.6.s_ref, f32[1,1024]{1,0:T(1,128)S(1)} %bitcast.318), custom_call_target="tpu_custom_call" | custom-call | flops 2147483648 | bytes 1572864 | tf_op jit(solution)/shard_map/first_pass/pallas_call | solution.py:238
  67.5 3.5 %collective-permute-start.10 = (f32[3072]{0:T(1024)S(1)}, f32[3072]{0:T(1024)S(1)}, u32[]{:S(2)}, u32[]{:S(2)}) collective-permute-start(f32[3072]{0:T(1024)S(1)} %bitcast.317), channel_id=1, source_target_pairs={{0,16},{1,17},{2,18},{3,19},{4,20},{5,21},{6,22},{7,23},{8,24},{9,... | collective-permute-start | bytes 36872 | tf_op jit(solution)/shard_map/ppermute | solution.py:359
  71.0 1.0 collective-permute-done.12
  72.7 75.6 %first_pass.3 = (f32[1,5120]{1,0:T(1,128)S(1)}, bf16[2048,4096]{1,0:T(8,128)(2,1)S(1)}, f32[1,4096]{1,0:T(1,128)S(1)}) custom-call(bf16[2048,128]{1,0:T(8,128)(2,1)S(1)} %constant_dynamic-update-slice_fusion.b_ref.a_ref.x_ref, bf16[4096,128]{1,0:T(8,128)(2,1)S(1)} %constant_dynamic-update-slice_fusion.4.a_ref.b_ref.y_ref, ...), custom_call_target="tpu_custom_call" | custom-call | flops 2147483648 | bytes 1572864 | tf_op jit(solution)/shard_map/first_pass/pallas_call | solution.py:238
  148.5 1.1 collective-permute-done.13
  149.7 3.9 %collective-permute-start.14 = (f32[5120]{0:T(1024)S(1)}, f32[5120]{0:T(1024)S(1)}, u32[]{:S(2)}, u32[]{:S(2)}) collective-permute-start(f32[5120]{0:T(1024)S(1)} %pad_maximum_fusion), channel_id=1, source_target_pairs={{0,2},{1,3},{2,0},{3,1},{4,6},{5,7},{6,4},{7,5},{8,10},{9,11},{10,... | collective-permute-start | bytes 61448 | tf_op jit(solution)/shard_map/ppermute | solution.py:359
  153.6 1.5 collective-permute-start.15
  155.3 3.2 %collective-permute-done.15 = f32[5120]{0:T(1024)S(1)} collective-permute-done((f32[5120]{0:T(1024)S(1)}, f32[5120]{0:T(1024)S(1)}, u32[]{:S(2)}, u32[]{:S(2)}) %collective-permute-start.15) | collective-permute-done | bytes 20512 | tf_op jit(solution)/shard_map/ppermute | solution.py:359
  159.8 4.9 %weighted_sum.4 = f32[1,2048]{1,0:T(1,128)S(1)} custom-call(bf16[2048,4096]{1,0:T(8,128)(2,1)S(1)} %get-tuple-element.9.e_ref, f32[1,4096]{1,0:T(1,128)S(1)} %get-tuple-element.22.w_ref), custom_call_target="tpu_custom_call" | custom-call | flops 16777216 | bytes 16777216 | tf_op jit(solution)/shard_map/weighted_sum/pallas_call | solution.py:213
  164.8 1.0 collective-permute-start.19
  165.7 0.9 collective-permute-start.18
  166.6 1.7 collective-permute-start.17
  168.5 0.9 collective-permute-done.19
  169.4 0.9 collective-permute-done.17
  170.3 3.3 %weighted_sum.5 = f32[1,4096]{1,0:T(1,128)S(1)} custom-call(bf16[2048,4096]{1,0:T(8,128)(2,1)S(1)} %get-tuple-element.9.e_ref, f32[1,2048]{1,0:T(1,128)S(1)} %fusion.25.w_ref), custom_call_target="tpu_custom_call" | custom-call | flops 16777216 | bytes 16777216 | tf_op jit(solution)/shard_map/weighted_sum/pallas_call | solution.py:213
  173.7 1.2 collective-permute-done.20
  174.9 2.7 %collective-permute-start.23 = (f32[4096]{0:T(1024)S(1)}, f32[4096]{0:T(1024)S(1)}, u32[]{:S(2)}, u32[]{:S(2)}) collective-permute-start(f32[4096]{0:T(1024)S(1)} %maximum_add_fusion.1), channel_id=1, source_target_pairs={{0,6},{1,7},{2,4},{3,5},{4,2},{5,3},{6,0},{7,1},{8,14},{9,15},{10,... | collective-permute-start | bytes 49160 | tf_op jit(solution)/shard_map/ppermute | solution.py:359
  177.6 1.7 collective-permute-start.21
  179.3 1.2 collective-permute-done.23
  180.5 0.9 collective-permute-done.21
  182.5 5.2 %weighted_sum.6 = f32[1,2048]{1,0:T(1,128)S(1)} custom-call(bf16[2048,4096]{1,0:T(8,128)(2,1)S(1)} %get-tuple-element.9.e_ref, f32[1,4096]{1,0:T(1,128)S(1)} %get-tuple-element.18.w_ref), custom_call_target="tpu_custom_call" | custom-call | flops 16777216 | bytes 16777216 | tf_op jit(solution)/shard_map/weighted_sum/pallas_call | solution.py:213
  187.6 1.5 collective-permute-start.26
  189.1 2.0 collective-permute-start.25
  191.2 1.1 collective-permute-done.26
  192.8 1.9 collective-permute-done.24
  194.8 3.3 %weighted_sum.7 = f32[1,4096]{1,0:T(1,128)S(1)} custom-call(bf16[2048,4096]{1,0:T(8,128)(2,1)S(1)} %get-tuple-element.9.e_ref, f32[1,2048]{1,0:T(1,128)S(1)} %fusion.24.w_ref.arow_ref), custom_call_target="tpu_custom_call" | custom-call | flops 16777216 | bytes 16777216 | tf_op jit(solution)/shard_map/weighted_sum/pallas_call | solution.py:213
  199.4 1.7 collective-permute-start.30
  201.7 2.2 collective-permute-start.28
  203.9 1.1 collective-permute-done.30
  206.2 5.8 %copy-done.1 = bf16[2048,4096]{1,0:T(8,128)(2,1)S(1)} copy-done((bf16[2048,4096]{1,0:T(8,128)(2,1)S(1)}, bf16[2048,4096]{1,0:T(8,128)(2,1)}, u32[]{:S(2)}) %copy-start.1) | copy-done | bytes 16777240
  212.0 14.6 %final_pass.1 = (f32[512,128]{1,0:T(8,128)S(1)}, bf16[1536,128]{1,0:T(8,128)(2,1)S(1)}, f32[2048,128]{1,0:T(8,128)S(1)}, f32[2048,128]{1,0:T(8,128)S(1)}) custom-call(bf16[2048,128]{1,0:T(8,128)(2,1)S(1)} %constant_dynamic-update-slice_fusion.b_ref.a_ref.x_ref, bf16[4096,128]{1,0:T(8,128)(2,1)S(1)} %constant_dynamic-update-slice_fusion.4.a_ref.b_ref.y_ref, ...), custom_call_target="tpu_custom_call" | custom-call | flops 8589934592 | bytes 16777216 | tf_op jit(solution)/shard_map/final_pass/pallas_call | solution.py:322
  226.9 1.3 collective-permute-start.33
  228.3 2.0 collective-permute-start.32
  230.4 2.1 collective-permute-start.35
  232.5 1.6 collective-permute-start.37
  234.2 1.3 collective-permute-done.31
  235.5 2.2 collective-permute-start.36
  238.5 1.6 collective-permute-done.37
  240.0 5.6 %collective-permute-done.36 = bf16[512,128]{1,0:T(8,128)(2,1)S(1)} collective-permute-done((bf16[512,128]{1,0:T(8,128)(2,1)S(1)}, bf16[512,128]{1,0:T(8,128)(2,1)S(1)}, u32[]{:S(2)}, u32[]{:S(2)}) %collective-permute-start.36) | collective-permute-done | bytes 131104 | tf_op jit(solution)/shard_map/ppermute | solution.py:359
  (193 shorter events, 13.3 us)
Async XLA Ops:
  0.6 23.3 %collective-permute-start.6 = (bf16[512,128]{1,0:T(8,128)(2,1)}, bf16[512,128]{1,0:T(8,128)(2,1)S(1)}, u32[]{:S(2)}, u32[]{:S(2)}) collective-permute-start(bf16[512,128]{1,0:T(8,128)(2,1)} %bitcast.323), channel_id=1, source_target_pairs={{0,8},{1,9},{2,10},{3,11},{4,12},{5,13},{6,14},{7,15},{8,0},{9,1},... | collective-permute-start | bytes 393224 | tf_op jit(solution)/shard_map/ppermute | solution.py:359
  1.1 15.6 %collective-permute-start.5 = (bf16[512,128]{1,0:T(8,128)(2,1)}, bf16[512,128]{1,0:T(8,128)(2,1)S(1)}, u32[]{:S(2)}, u32[]{:S(2)}) collective-permute-start(bf16[512,128]{1,0:T(8,128)(2,1)} %bitcast.324), channel_id=1, source_target_pairs={{0,6},{1,7},{2,4},{3,5},{4,2},{5,3},{6,0},{7,1},{8,14},{9,15},{10,... | collective-permute-start | bytes 393224 | tf_op jit(solution)/shard_map/ppermute | solution.py:359
  5.8 12.4 %collective-permute-start.4 = (bf16[512,128]{1,0:T(8,128)(2,1)}, bf16[512,128]{1,0:T(8,128)(2,1)S(1)}, u32[]{:S(2)}, u32[]{:S(2)}) collective-permute-start(bf16[512,128]{1,0:T(8,128)(2,1)} %bitcast.325), channel_id=1, source_target_pairs={{0,4},{1,5},{2,6},{3,7},{4,0},{5,1},{6,2},{7,3},{8,12},{9,13},{10,... | collective-permute-start | bytes 393224 | tf_op jit(solution)/shard_map/ppermute | solution.py:359
  5.8 9.4 %collective-permute-start.3 = (bf16[512,128]{1,0:T(8,128)(2,1)}, bf16[512,128]{1,0:T(8,128)(2,1)S(1)}, u32[]{:S(2)}, u32[]{:S(2)}) collective-permute-start(bf16[512,128]{1,0:T(8,128)(2,1)} %bitcast.326), channel_id=1, source_target_pairs={{0,2},{1,3},{2,0},{3,1},{4,6},{5,7},{6,4},{7,5},{8,10},{9,11},{10,... | collective-permute-start | bytes 393224 | tf_op jit(solution)/shard_map/ppermute | solution.py:359
  6.5 16.9 %collective-permute-start.1 = (bf16[512,128]{1,0:T(8,128)(2,1)}, bf16[512,128]{1,0:T(8,128)(2,1)S(1)}, u32[]{:S(2)}, u32[]{:S(2)}) collective-permute-start(bf16[512,128]{1,0:T(8,128)(2,1)} %param.4), channel_id=1, source_target_pairs={{0,16},{1,17},{2,18},{3,19},{4,20},{5,21},{6,22},{7,23},{8,24},{9,... | collective-permute-start | bytes 393224 | tf_op jit(solution)/shard_map/ppermute | solution.py:359
  15.2 8.1 %collective-permute-start = (bf16[512,128]{1,0:T(8,128)(2,1)}, bf16[512,128]{1,0:T(8,128)(2,1)S(1)}, u32[]{:S(2)}, u32[]{:S(2)}) collective-permute-start(bf16[512,128]{1,0:T(8,128)(2,1)} %param.4), channel_id=1, source_target_pairs={{0,1},{1,0},{2,3},{3,2},{4,5},{5,4},{6,7},{7,6},{8,9},{9,8},{10,11... | collective-permute-start | bytes 393224 | tf_op jit(solution)/shard_map/ppermute | solution.py:359
  16.8 7.2 %collective-permute-start.2 = (bf16[512,128]{1,0:T(8,128)(2,1)}, bf16[512,128]{1,0:T(8,128)(2,1)S(1)}, u32[]{:S(2)}, u32[]{:S(2)}) collective-permute-start(bf16[512,128]{1,0:T(8,128)(2,1)} %param.4), channel_id=1, source_target_pairs={{0,17},{1,16},{2,19},{3,18},{4,21},{5,20},{6,23},{7,22},{8,25},{9,... | collective-permute-start | bytes 393224 | tf_op jit(solution)/shard_map/ppermute | solution.py:359
  18.3 6.7 %collective-permute-start.9 = (bf16[512,128]{1,0:T(8,128)(2,1)S(1)}, bf16[512,128]{1,0:T(8,128)(2,1)S(1)}, u32[]{:S(2)}, u32[]{:S(2)}) collective-permute-start(bf16[512,128]{1,0:T(8,128)(2,1)S(1)} %collective-permute-done.5), channel_id=1, source_target_pairs={{0,8},{1,9},{2,10},{3,11},{4,12},{5,13},{6,14},{7,15},{8,0},{9,1},... | collective-permute-start | bytes 393224 | tf_op jit(solution)/shard_map/ppermute | solution.py:359
  23.3 1.6 collective-permute-start.8
  23.3 1.6 collective-permute-start.7
  67.3 4.7 %collective-permute-start.12 = (f32[3072]{0:T(1024)S(1)}, f32[3072]{0:T(1024)S(1)}, u32[]{:S(2)}, u32[]{:S(2)}) collective-permute-start(f32[3072]{0:T(1024)S(1)} %bitcast.315), channel_id=1, source_target_pairs={{0,17},{1,16},{2,19},{3,18},{4,21},{5,20},{6,23},{7,22},{8,25},{9,... | collective-permute-start | bytes 36872 | tf_op jit(solution)/shard_map/ppermute | solution.py:359
  67.5 5.2 %collective-permute-start.11 = (f32[3072]{0:T(1024)S(1)}, f32[3072]{0:T(1024)S(1)}, u32[]{:S(2)}, u32[]{:S(2)}) collective-permute-start(f32[3072]{0:T(1024)S(1)} %bitcast.316), channel_id=1, source_target_pairs={{0,1},{1,0},{2,3},{3,2},{4,5},{5,4},{6,7},{7,6},{8,9},{9,8},{10,11... | collective-permute-start | bytes 36872 | tf_op jit(solution)/shard_map/ppermute | solution.py:359
  67.5 5.1 %collective-permute-start.10 = (f32[3072]{0:T(1024)S(1)}, f32[3072]{0:T(1024)S(1)}, u32[]{:S(2)}, u32[]{:S(2)}) collective-permute-start(f32[3072]{0:T(1024)S(1)} %bitcast.317), channel_id=1, source_target_pairs={{0,16},{1,17},{2,18},{3,19},{4,20},{5,21},{6,22},{7,23},{8,24},{9,... | collective-permute-start | bytes 36872 | tf_op jit(solution)/shard_map/ppermute | solution.py:359
  148.3 46.5 %copy-start = (bf16[2048,4096]{1,0:T(8,128)(2,1)}, bf16[2048,4096]{1,0:T(8,128)(2,1)S(1)}, u32[]{:S(2)}) copy-start(bf16[2048,4096]{1,0:T(8,128)(2,1)S(1)} %get-tuple-element.9.e_ref) | copy-start | bytes 50331652
  148.4 1.2 collective-permute-start.13
  149.7 5.7 %collective-permute-start.14 = (f32[5120]{0:T(1024)S(1)}, f32[5120]{0:T(1024)S(1)}, u32[]{:S(2)}, u32[]{:S(2)}) collective-permute-start(f32[5120]{0:T(1024)S(1)} %pad_maximum_fusion), channel_id=1, source_target_pairs={{0,2},{1,3},{2,0},{3,1},{4,6},{5,7},{6,4},{7,5},{8,10},{9,11},{10,... | collective-permute-start | bytes 61448 | tf_op jit(solution)/shard_map/ppermute | solution.py:359
  153.6 5.6 %collective-permute-start.16 = (f32[5120]{0:T(1024)S(1)}, f32[5120]{0:T(1024)S(1)}, u32[]{:S(2)}, u32[]{:S(2)}) collective-permute-start(f32[5120]{0:T(1024)S(1)} %pad_maximum_fusion), channel_id=1, source_target_pairs={{0,6},{1,7},{2,4},{3,5},{4,2},{5,3},{6,0},{7,1},{8,14},{9,15},{10,... | collective-permute-start | bytes 61448 | tf_op jit(solution)/shard_map/ppermute | solution.py:359
  153.6 4.9 %collective-permute-start.15 = (f32[5120]{0:T(1024)S(1)}, f32[5120]{0:T(1024)S(1)}, u32[]{:S(2)}, u32[]{:S(2)}) collective-permute-start(f32[5120]{0:T(1024)S(1)} %pad_maximum_fusion), channel_id=1, source_target_pairs={{0,4},{1,5},{2,6},{3,7},{4,0},{5,1},{6,2},{7,3},{8,12},{9,13},{10,... | collective-permute-start | bytes 61448 | tf_op jit(solution)/shard_map/ppermute | solution.py:359
  164.8 4.6 %collective-permute-start.19 = (f32[2048]{0:T(1024)S(1)}, f32[2048]{0:T(1024)S(1)}, u32[]{:S(2)}, u32[]{:S(2)}) collective-permute-start(f32[2048]{0:T(1024)S(1)} %bitcast.312), channel_id=1, source_target_pairs={{0,17},{1,16},{2,19},{3,18},{4,21},{5,20},{6,23},{7,22},{8,25},{9,... | collective-permute-start | bytes 24584 | tf_op jit(solution)/shard_map/ppermute | solution.py:359
  165.7 3.7 %collective-permute-start.18 = (f32[2048]{0:T(1024)S(1)}, f32[2048]{0:T(1024)S(1)}, u32[]{:S(2)}, u32[]{:S(2)}) collective-permute-start(f32[2048]{0:T(1024)S(1)} %bitcast.313), channel_id=1, source_target_pairs={{0,16},{1,17},{2,18},{3,19},{4,20},{5,21},{6,22},{7,23},{8,24},{9,... | collective-permute-start | bytes 24584 | tf_op jit(solution)/shard_map/ppermute | solution.py:359
  166.6 3.7 %collective-permute-start.17 = (f32[2048]{0:T(1024)S(1)}, f32[2048]{0:T(1024)S(1)}, u32[]{:S(2)}, u32[]{:S(2)}) collective-permute-start(f32[2048]{0:T(1024)S(1)} %bitcast.314), channel_id=1, source_target_pairs={{0,1},{1,0},{2,3},{3,2},{4,5},{5,4},{6,7},{7,6},{8,9},{9,8},{10,11... | collective-permute-start | bytes 24584 | tf_op jit(solution)/shard_map/ppermute | solution.py:359
  173.6 1.2 collective-permute-start.20
  174.9 5.5 %collective-permute-start.23 = (f32[4096]{0:T(1024)S(1)}, f32[4096]{0:T(1024)S(1)}, u32[]{:S(2)}, u32[]{:S(2)}) collective-permute-start(f32[4096]{0:T(1024)S(1)} %maximum_add_fusion.1), channel_id=1, source_target_pairs={{0,6},{1,7},{2,4},{3,5},{4,2},{5,3},{6,0},{7,1},{8,14},{9,15},{10,... | collective-permute-start | bytes 49160 | tf_op jit(solution)/shard_map/ppermute | solution.py:359
  177.6 4.6 %collective-permute-start.22 = (f32[4096]{0:T(1024)S(1)}, f32[4096]{0:T(1024)S(1)}, u32[]{:S(2)}, u32[]{:S(2)}) collective-permute-start(f32[4096]{0:T(1024)S(1)} %maximum_add_fusion.1), channel_id=1, source_target_pairs={{0,4},{1,5},{2,6},{3,7},{4,0},{5,1},{6,2},{7,3},{8,12},{9,13},{10,... | collective-permute-start | bytes 49160 | tf_op jit(solution)/shard_map/ppermute | solution.py:359
  177.6 3.7 %collective-permute-start.21 = (f32[4096]{0:T(1024)S(1)}, f32[4096]{0:T(1024)S(1)}, u32[]{:S(2)}, u32[]{:S(2)}) collective-permute-start(f32[4096]{0:T(1024)S(1)} %maximum_add_fusion.1), channel_id=1, source_target_pairs={{0,2},{1,3},{2,0},{3,1},{4,6},{5,7},{6,4},{7,5},{8,10},{9,11},{10,... | collective-permute-start | bytes 49160 | tf_op jit(solution)/shard_map/ppermute | solution.py:359
  187.6 4.6 %collective-permute-start.26 = (f32[2048]{0:T(1024)S(1)}, f32[2048]{0:T(1024)S(1)}, u32[]{:S(2)}, u32[]{:S(2)}) collective-permute-start(f32[2048]{0:T(1024)S(1)} %bitcast.308), channel_id=1, source_target_pairs={{0,17},{1,16},{2,19},{3,18},{4,21},{5,20},{6,23},{7,22},{8,25},{9,... | collective-permute-start | bytes 24584 | tf_op jit(solution)/shard_map/ppermute | solution.py:359
  189.1 3.7 %collective-permute-start.25 = (f32[2048]{0:T(1024)S(1)}, f32[2048]{0:T(1024)S(1)}, u32[]{:S(2)}, u32[]{:S(2)}) collective-permute-start(f32[2048]{0:T(1024)S(1)} %bitcast.309), channel_id=1, source_target_pairs={{0,16},{1,17},{2,18},{3,19},{4,20},{5,21},{6,22},{7,23},{8,24},{9,... | collective-permute-start | bytes 24584 | tf_op jit(solution)/shard_map/ppermute | solution.py:359
  191.1 3.7 %collective-permute-start.24 = (f32[2048]{0:T(1024)S(1)}, f32[2048]{0:T(1024)S(1)}, u32[]{:S(2)}, u32[]{:S(2)}) collective-permute-start(f32[2048]{0:T(1024)S(1)} %bitcast.310), channel_id=1, source_target_pairs={{0,1},{1,0},{2,3},{3,2},{4,5},{5,4},{6,7},{7,6},{8,9},{9,8},{10,11... | collective-permute-start | bytes 24584 | tf_op jit(solution)/shard_map/ppermute | solution.py:359
  198.1 1.2 collective-permute-start.27
  199.4 5.6 %collective-permute-start.30 = (f32[4096]{0:T(1024)S(1)}, f32[4096]{0:T(1024)S(1)}, u32[]{:S(2)}, u32[]{:S(2)}) collective-permute-start(f32[4096]{0:T(1024)S(1)} %maximum_add_fusion.3), channel_id=1, source_target_pairs={{0,6},{1,7},{2,4},{3,5},{4,2},{5,3},{6,0},{7,1},{8,14},{9,15},{10,... | collective-permute-start | bytes 49160 | tf_op jit(solution)/shard_map/ppermute | solution.py:359
  201.1 4.8 %collective-permute-start.29 = (f32[4096]{0:T(1024)S(1)}, f32[4096]{0:T(1024)S(1)}, u32[]{:S(2)}, u32[]{:S(2)}) collective-permute-start(f32[4096]{0:T(1024)S(1)} %maximum_add_fusion.3), channel_id=1, source_target_pairs={{0,4},{1,5},{2,6},{3,7},{4,0},{5,1},{6,2},{7,3},{8,12},{9,13},{10,... | collective-permute-start | bytes 49160 | tf_op jit(solution)/shard_map/ppermute | solution.py:359
  201.7 3.9 %collective-permute-start.28 = (f32[4096]{0:T(1024)S(1)}, f32[4096]{0:T(1024)S(1)}, u32[]{:S(2)}, u32[]{:S(2)}) collective-permute-start(f32[4096]{0:T(1024)S(1)} %maximum_add_fusion.3), channel_id=1, source_target_pairs={{0,2},{1,3},{2,0},{3,1},{4,6},{5,7},{6,4},{7,5},{8,10},{9,11},{10,... | collective-permute-start | bytes 49160 | tf_op jit(solution)/shard_map/ppermute | solution.py:359
  206.2 5.8 %copy-start.1 = (bf16[2048,4096]{1,0:T(8,128)(2,1)S(1)}, bf16[2048,4096]{1,0:T(8,128)(2,1)}, u32[]{:S(2)}) copy-start(bf16[2048,4096]{1,0:T(8,128)(2,1)} %copy-done) | copy-start | bytes 50331652
  226.6 3.7 %collective-permute-start.34 = (f32[2048,128]{1,0:T(8,128)S(1)}, f32[2048,128]{1,0:T(8,128)S(1)}, u32[]{:S(2)}, u32[]{:S(2)}) collective-permute-start(f32[2048,128]{1,0:T(8,128)S(1)} %get-tuple-element.15), channel_id=1, source_target_pairs={{0,8},{1,9},{2,10},{3,11},{4,12},{5,13},{6,14},{7,15},{8,0},{9,1},... | collective-permute-start | bytes 3145736 | tf_op jit(solution)/shard_map/ppermute | solution.py:359
  226.7 8.8 %collective-permute-start.31 = (bf16[512,128]{1,0:T(8,128)(2,1)S(1)}, bf16[512,128]{1,0:T(8,128)(2,1)S(1)}, u32[]{:S(2)}, u32[]{:S(2)}) collective-permute-start(bf16[512,128]{1,0:T(8,128)(2,1)S(1)} %get-tuple-element.27), channel_id=1, source_target_pairs={{0,1},{1,0},{2,3},{3,2},{4,5},{5,4},{6,7},{7,6},{8,9},{9,8},{10,11... | collective-permute-start | bytes 393224 | tf_op jit(solution)/shard_map/ppermute | solution.py:359
  226.9 10.7 %collective-permute-start.33 = (bf16[512,128]{1,0:T(8,128)(2,1)S(1)}, bf16[512,128]{1,0:T(8,128)(2,1)S(1)}, u32[]{:S(2)}, u32[]{:S(2)}) collective-permute-start(bf16[512,128]{1,0:T(8,128)(2,1)S(1)} %get-tuple-element.28), channel_id=1, source_target_pairs={{0,17},{1,16},{2,19},{3,18},{4,21},{5,20},{6,23},{7,22},{8,25},{9,... | collective-permute-start | bytes 393224 | tf_op jit(solution)/shard_map/ppermute | solution.py:359
  228.3 9.4 %collective-permute-start.32 = (bf16[512,128]{1,0:T(8,128)(2,1)S(1)}, bf16[512,128]{1,0:T(8,128)(2,1)S(1)}, u32[]{:S(2)}, u32[]{:S(2)}) collective-permute-start(bf16[512,128]{1,0:T(8,128)(2,1)S(1)} %get-tuple-element.29), channel_id=1, source_target_pairs={{0,16},{1,17},{2,18},{3,19},{4,20},{5,21},{6,22},{7,23},{8,24},{9,... | collective-permute-start | bytes 393224 | tf_op jit(solution)/shard_map/ppermute | solution.py:359
  230.4 8.0 %collective-permute-start.35 = (bf16[512,128]{1,0:T(8,128)(2,1)S(1)}, bf16[512,128]{1,0:T(8,128)(2,1)S(1)}, u32[]{:S(2)}, u32[]{:S(2)}) collective-permute-start(bf16[512,128]{1,0:T(8,128)(2,1)S(1)} %get-tuple-element.24), channel_id=1, source_target_pairs={{0,2},{1,3},{2,0},{3,1},{4,6},{5,7},{6,4},{7,5},{8,10},{9,11},{10,... | collective-permute-start | bytes 393224 | tf_op jit(solution)/shard_map/ppermute | solution.py:359
  232.5 7.5 %collective-permute-start.37 = (bf16[512,128]{1,0:T(8,128)(2,1)S(1)}, bf16[512,128]{1,0:T(8,128)(2,1)S(1)}, u32[]{:S(2)}, u32[]{:S(2)}) collective-permute-start(bf16[512,128]{1,0:T(8,128)(2,1)S(1)} %get-tuple-element.25), channel_id=1, source_target_pairs={{0,6},{1,7},{2,4},{3,5},{4,2},{5,3},{6,0},{7,1},{8,14},{9,15},{10,... | collective-permute-start | bytes 393224 | tf_op jit(solution)/shard_map/ppermute | solution.py:359
  235.5 10.2 %collective-permute-start.36 = (bf16[512,128]{1,0:T(8,128)(2,1)S(1)}, bf16[512,128]{1,0:T(8,128)(2,1)S(1)}, u32[]{:S(2)}, u32[]{:S(2)}) collective-permute-start(bf16[512,128]{1,0:T(8,128)(2,1)S(1)} %get-tuple-element.26), channel_id=1, source_target_pairs={{0,4},{1,5},{2,6},{3,7},{4,0},{5,1},{6,2},{7,3},{8,12},{9,13},{10,... | collective-permute-start | bytes 393224 | tf_op jit(solution)/shard_map/ppermute | solution.py:359

commit v5 on v4

--- a/solution.py
+++ b/solution.py
@@ -15,6 +15,7 @@
 CROSS = 2.0 * LOG2E / EPSILON
 NT = (((1,), (1,)), ((), ()))
 VMEM = pl.BlockSpec(memory_space=pltpu.VMEM)
+GROUP = 32
 
 
 def spread(s_ref, sb_ref):
@@ -35,14 +36,9 @@
     lax.fori_loop(0, a_ref.shape[0] // chunk, block, 0)
 
 
-def fold(t):
-    return jnp.sum(t.reshape(t.shape[0] // 8, 8, 128), axis=0)
-
-
-def pipelined(chunk, width, a_ref, b_ref, sb_ref, d_ref, head, tile, finish):
+def pipelined(chunk, width, a_ref, b_ref, d_ref, head, tile, finish):
     depth, lanes = a_ref.shape[0], b_ref.shape[0]
     steps, last = depth // chunk, lanes // width - 1
-    tiles = width // 128
 
     def product(n, m):
         b = b_ref[pl.ds(pl.multiple_of(n * width, width), width), :]
@@ -59,8 +55,7 @@
                 product(n, m + 1)
             else:
                 product(jnp.minimum(n + 1, last), 0)
-            s = sb_ref[m * chunk:(m + 1) * chunk, :]
-            state = tile(m, lambda q: d_ref[m % 2, :, q * 128:(q + 1) * 128], s, state)
+            state = tile(m, start, state)
         finish(start, state)
         return 0
 
@@ -121,37 +116,37 @@
     o_ref[:, lanes:] = mass_ref[...]
     top_ref[...] = jnp.zeros_like(top_ref)
 
-    def exponential(m, start, q, t):
-        e = jnp.exp2(t)
-        if e_ref is not None:
-            place = pl.ds(pl.multiple_of(start + q * 128, 128), 128)
-            e_ref[m * chunk:(m + 1) * chunk, place] = e.astype(jnp.bfloat16)
-        return fold(e)
-
-    def tile(m, piece, s, state):
-        start, sums = state
+    def lanes_of(start, q):
+        return pl.ds(pl.multiple_of(start + q * 128, 128), 128)
+
+    def tile(m, start, state):
+        def exponents(g, q):
+            at = g * GROUP
+            s = sb_ref[m * chunk + at:m * chunk + at + GROUP, :]
+            return d_ref[m % 2, at:at + GROUP, q * 128:(q + 1) * 128] * CROSS + s
+
         if m == 0:
-            sums = []
-            for q in range(tiles):
-                t = piece(q) * CROSS + s
-                peak = jnp.max(t, axis=0, keepdims=True)
-                sums.append((peak, exponential(m, start, q, t - peak)))
-            return start, sums
-        return start, [
-            (peak, total + exponential(m, start, q, piece(q) * CROSS + s - peak))
-            for q, (peak, total) in enumerate(sums)
-        ]
+            tops = [exponents(0, q) for q in range(tiles)]
+            for g in range(1, 128 // GROUP):
+                tops = [jnp.maximum(top, exponents(g, q)) for q, top in enumerate(tops)]
+            state = [(jnp.max(top, axis=0, keepdims=True), jnp.zeros((GROUP, 128), jnp.float32)) for top in tops]
+        for g in range(chunk // GROUP):
+            for q, (peak, total) in enumerate(state):
+                e = jnp.exp2(exponents(g, q) - peak)
+                if e_ref is not None:
+                    at = m * chunk + g * GROUP
+                    e_ref[at:at + GROUP, lanes_of(start, q)] = e.astype(jnp.bfloat16)
+                state[q] = peak, total + e
+        return state
 
     def finish(start, state):
-        for q, (peak, total) in enumerate(state[1]):
+        for q, (peak, total) in enumerate(state):
             top_ref[...] = jnp.maximum(top_ref[...], total)
-            whole = jnp.sum(total, axis=0, keepdims=True)
-            place = pl.ds(pl.multiple_of(start + q * 128, 128), 128)
-            o_ref[:, place] = peak + jnp.log2(whole)
+            o_ref[:, lanes_of(start, q)] = peak + jnp.log2(jnp.sum(total, axis=0, keepdims=True))
             if e_ref is not None:
-                shift_ref[:, place] = peak
-
-    pipelined(chunk, width, a_ref, b_ref, sb_ref, d_ref, lambda start: (start, None), tile, finish)
+                shift_ref[:, lanes_of(start, q)] = peak
+
+    pipelined(chunk, width, a_ref, b_ref, d_ref, lambda start: None, tile, finish)
 
     @pl.when(jnp.logical_not(jnp.max(top_ref[...]) < 2.0 ** 60))
     def _():
@@ -180,18 +175,6 @@
         at = pl.multiple_of(k * width, width)
         got = lax.dot_general(w16_ref[...], e_ref[pl.ds(at, width), :], NT, preferred_element_type=jnp.float32)
         o_ref[:, pl.ds(at, width)] = jnp.sum(got, axis=0, keepdims=True)
-        return 0
-
-    lax.fori_loop(0, e_ref.shape[0] // width, block, 0)
-
-
-def row_turned_kernel(width, e_ref, w_ref, o_ref, w16_ref):
-    w16_ref[...] = stacked(w_ref)
-
-    def block(k, _):
-        at = pl.multiple_of(k * width, width)
-        got = lax.dot_general(e_ref[pl.ds(at, width), :], w16_ref[...], NT, preferred_element_type=jnp.float32)
-        o_ref[:, pl.ds(at, width)] = jnp.sum(jnp.transpose(got), axis=0, keepdims=True)
         return 0
 
     lax.fori_loop(0, e_ref.shape[0] // width, block, 0)
@@ -243,7 +226,7 @@
         scratch_shapes=[
             pltpu.VMEM((depth, 128), jnp.float32),
             pltpu.VMEM((2, chunk, width), jnp.float32),
-            pltpu.VMEM((8, 128), jnp.float32),
+            pltpu.VMEM((GROUP, 128), jnp.float32),
         ],
         compiler_params=pltpu.CompilerParams(vmem_limit_bytes=16 << 20),
         cost_estimate=pass_cost(a, b),
@@ -253,39 +236,92 @@
     return sent if is_row else (sent, out[1], out[2].reshape(lanes))
 
 
-def final_kernel(chunk, width, own_x, own_y, x_ref, y_ref, e_ref, alpha_ref, arow_ref, beta_ref, brow_ref,
-                 gi_ref, gis_ref, gc_ref, gcs_ref, ab_ref, bb_ref, yb_ref, xa_ref, b16_ref, sums_ref, rb_ref, acc_ref):
+def high_low(value):
+    high = value.astype(jnp.bfloat16)
+    return high, (value - high.astype(jnp.float32)).astype(jnp.bfloat16)
+
+
+def column_grad_kernel(width, own, xt_ref, y_ref, e_ref, alpha_ref, beta_ref, gc_ref, gcs_ref,
+                       bb_ref, cb_ref, xa_ref, sums_ref, acc_ref):
+    rows, cols = xt_ref.shape[1], y_ref.shape[0]
+    spread(beta_ref, bb_ref)
+    place = lax.broadcasted_iota(jnp.int32, (128, 512), 0)
+    for k in range(rows // 512):
+        at = k * 512
+        alpha = alpha_ref[:, at:at + 512]
+        high, low = high_low(xt_ref[:, at:at + 512].astype(jnp.float32) * alpha)
+        first, second = high_low(alpha)
+        low = jnp.where(place == 126, first.astype(jnp.float32), low.astype(jnp.float32))
+        low = jnp.where(place == 127, second.astype(jnp.float32), low)
+        xa_ref[:128, at:at + 512] = high
+        xa_ref[128:, at:at + 512] = low.astype(jnp.bfloat16)
+
+    lower = lax.broadcasted_iota(jnp.int32, (128, width), 0) < 126
+    for k in range(cols // width):
+        at = k * width
+        got = jnp.dot(xa_ref[...], e_ref[:, at:at + width], preferred_element_type=jnp.float32)
+        acc_ref[:, at:at + width] = got[:128] + jnp.where(lower, got[128:], 0.0)
+        count = got[254:255] + got[255:256]
+        for q in range(width // 128):
+            sums_ref[at // 128 + q:at // 128 + q + 1, :] = count[:, q * 128:(q + 1) * 128]
+    spread(sums_ref, cb_ref)
+    for k in range(cols // 128):
+        at = k * 128
+        pulled = jnp.transpose(acc_ref[:, at:at + 128])
+        whole = cb_ref[at:at + 128, :] * y_ref[at:at + 128, :].astype(jnp.float32)
+        grad = 2.0 * bb_ref[at:at + 128, :] * (whole - pulled)
+        if at < own:
+            gc_ref[at:at + 128, :] = grad
+        else:
+            gcs_ref[at - own:at - own + 128, :] = grad.astype(jnp.bfloat16)
+
+
+def column_grad(xt, y, e, alpha, beta, own, width=512):
+    rows, cols = xt.shape[1], y.shape[0]
+    return pl.pallas_call(
+        functools.partial(column_grad_kernel, width, own),
+        out_shape=(
+            jax.ShapeDtypeStruct((own, D), jnp.float32),
+            jax.ShapeDtypeStruct((cols - own, D), jnp.bfloat16),
+        ),
+        in_specs=[VMEM] * 5,
+        out_specs=(VMEM,) * 2,
+        scratch_shapes=[
+            pltpu.VMEM((cols, 128), jnp.float32),
+            pltpu.VMEM((cols, 128), jnp.float32),
+            pltpu.VMEM((256, rows), jnp.bfloat16),
+            pltpu.VMEM((cols // 128, 128), jnp.float32),
+            pltpu.VMEM((128, cols), jnp.float32),
+        ],
+        compiler_params=pltpu.CompilerParams(vmem_limit_bytes=16 << 20),
+        cost_estimate=pl.CostEstimate(flops=4 * e.size * D, bytes_accessed=2 * e.size, transcendentals=0),
+        name="column_grad",
+    )(xt, y, e, alpha.reshape(1, rows), beta.reshape(cols // 128, 128))
+
+
+def row_grad_kernel(chunk, own, x_ref, y_ref, e_ref, alpha_ref, beta_ref, gi_ref, gis_ref, ab_ref, bb_ref, yb_ref):
     rows, cols = x_ref.shape[0], y_ref.shape[0]
     spread(alpha_ref, ab_ref)
     spread(beta_ref, bb_ref)
-    b16_ref[...] = stacked(brow_ref)
-
-    def high_low(value):
-        high = value.astype(jnp.bfloat16)
-        return high, (value - high.astype(jnp.float32)).astype(jnp.bfloat16)
-
-    for k in range(cols // 512):
-        at = k * 512
-        yb_ref[at:at + 512, :128], yb_ref[at:at + 512, 128:] = high_low(
-            y_ref[at:at + 512, :].astype(jnp.float32) * bb_ref[at:at + 512, :])
-    for k in range(rows // 128):
-        at = k * 128
-        xa = jnp.transpose(x_ref[at:at + 128, :].astype(jnp.float32)) * arow_ref[:, at:at + 128]
-        xa_ref[:128, at:at + 128], xa_ref[128:256, at:at + 128] = high_low(xa)
-    xa_ref[256:, :] = stacked(arow_ref)
-
-    for k in range(rows // 512):
-        got = lax.dot_general(b16_ref[...], e_ref[k * 512:(k + 1) * 512, :], NT, preferred_element_type=jnp.float32)
-        got = jnp.sum(got, axis=0, keepdims=True)
-        for q in range(4):
-            sums_ref[k * 4 + q:k * 4 + q + 1, :] = got[:, q * 128:(q + 1) * 128]
-    spread(sums_ref, rb_ref)
+    place = lax.broadcasted_iota(jnp.int32, (256, 128), 1)
+    for k in range(cols // 256):
+        at = k * 256
+        beta = bb_ref[at:at + 256, :]
+        high, low = high_low(y_ref[at:at + 256, :].astype(jnp.float32) * beta)
+        first, second = high_low(beta)
+        low = jnp.where(place == 126, first.astype(jnp.float32), low.astype(jnp.float32))
+        low = jnp.where(place == 127, second.astype(jnp.float32), low)
+        yb_ref[at:at + 256, :128] = high
+        yb_ref[at:at + 256, 128:] = low.astype(jnp.bfloat16)
+
+    lower = lax.broadcasted_iota(jnp.int32, (chunk, 128), 1) < 126
 
     def block(at):
-        pulled = jnp.dot(e_ref[pl.ds(at, chunk), :], yb_ref[...], preferred_element_type=jnp.float32)
-        scale = 2.0 * ab_ref[pl.ds(at, chunk), :]
+        got = jnp.dot(e_ref[pl.ds(at, chunk), :], yb_ref[...], preferred_element_type=jnp.float32)
+        total = got[:, 254:255] + got[:, 255:256]
+        pulled = got[:, :128] + jnp.where(lower, got[:, 128:], 0.0)
         x = x_ref[pl.ds(at, chunk), :].astype(jnp.float32)
-        return scale * (rb_ref[pl.ds(at, chunk), :] * x - (pulled[:, :128] + pulled[:, 128:]))
+        return 2.0 * ab_ref[pl.ds(at, chunk), :] * (total * x - pulled)
 
     def own_block(k, _):
         at = pl.multiple_of(k * chunk, chunk)
@@ -294,56 +330,32 @@
 
     def sent_block(k, _):
         at = pl.multiple_of(k * chunk, chunk)
-        gis_ref[pl.ds(pl.multiple_of(at - own_x, chunk), chunk), :] = block(at).astype(jnp.bfloat16)
-        return 0
-
-    lax.fori_loop(0, own_x // chunk, own_block, 0)
-    lax.fori_loop(own_x // chunk, rows // chunk, sent_block, 0)
-
-    for k in range(cols // width):
-        got = jnp.dot(xa_ref[...], e_ref[:, k * width:(k + 1) * width], preferred_element_type=jnp.float32)
-        acc_ref[:, k * width:(k + 1) * width] = got[:128] + got[128:256]
-        count = jnp.sum(got[256:], axis=0, keepdims=True)
-        for q in range(width // 128):
-            at = k * width + q * 128
-            whole = jnp.transpose(jnp.broadcast_to(count[:, q * 128:(q + 1) * 128], (128, 128)))
-            pulled = jnp.transpose(acc_ref[:, at:at + 128])
-            grad = 2.0 * bb_ref[at:at + 128, :] * (whole * y_ref[at:at + 128, :].astype(jnp.float32) - pulled)
-            if at < own_y:
-                gc_ref[at:at + 128, :] = grad
-            else:
-                gcs_ref[at - own_y:at - own_y + 128, :] = grad
-
-
-def final_pass(x, y, e, alpha, beta, own_x, own_y, width=512):
+        gis_ref[pl.ds(pl.multiple_of(at - own, chunk), chunk), :] = block(at).astype(jnp.bfloat16)
+        return 0
+
+    lax.fori_loop(own // chunk, rows // chunk, sent_block, 0)
+    lax.fori_loop(0, own // chunk, own_block, 0)
+
+
+def row_grad(x, y, e, alpha, beta, own):
     rows, cols = x.shape[0], y.shape[0]
-    size = rows * cols
-    chunk = math.gcd(own_x, 512)
     return pl.pallas_call(
-        functools.partial(final_kernel, chunk, width, own_x, own_y),
+        functools.partial(row_grad_kernel, math.gcd(own, 512), own),
         out_shape=(
-            jax.ShapeDtypeStruct((own_x, D), jnp.float32),
-            jax.ShapeDtypeStruct((rows - own_x, D), jnp.bfloat16),
-            jax.ShapeDtypeStruct((own_y, D), jnp.float32),
-            jax.ShapeDtypeStruct((cols - own_y, D), jnp.float32),
+            jax.ShapeDtypeStruct((own, D), jnp.float32),
+            jax.ShapeDtypeStruct((rows - own, D), jnp.bfloat16),
         ),
-        in_specs=[VMEM] * 7,
-        out_specs=(VMEM,) * 4,
+        in_specs=[VMEM] * 5,
+        out_specs=(VMEM,) * 2,
         scratch_shapes=[
             pltpu.VMEM((rows, 128), jnp.float32),
             pltpu.VMEM((cols, 128), jnp.float32),
             pltpu.VMEM((cols, 256), jnp.bfloat16),
-            pltpu.VMEM((272, rows), jnp.bfloat16),
-            pltpu.VMEM((16, cols), jnp.bfloat16),
-            pltpu.VMEM((rows // 128, 128), jnp.float32),
-            pltpu.VMEM((rows, 128), jnp.float32),
-            pltpu.VMEM((128, cols), jnp.float32),
         ],
-        compiler_params=pltpu.CompilerParams(vmem_limit_bytes=28 << 20),
-        cost_estimate=pl.CostEstimate(flops=8 * size * D, bytes_accessed=2 * size, transcendentals=0),
-        name="final_pass",
-    )(x, y, e, alpha.reshape(rows // 128, 128), alpha.reshape(1, rows), beta.reshape(cols // 128, 128),
-      beta.reshape(1, cols))
+        compiler_params=pltpu.CompilerParams(vmem_limit_bytes=16 << 20),
+        cost_estimate=pl.CostEstimate(flops=4 * e.size * D, bytes_accessed=2 * e.size, transcendentals=0),
+        name="row_grad",
+    )(x, y, e, alpha.reshape(rows // 128, 128), beta.reshape(cols // 128, 128))
 
 
 class Groups:
@@ -415,14 +427,14 @@
 
     first_beta = beta = jnp.exp2(v + shift)
     for step in range(1, ITERS):
-        kernel = row_kernel if step == 1 else row_turned_kernel
-        alpha = mass_a / sum(row_exchange(weighted(kernel, e, beta, x.shape[0])))
+        alpha = mass_a / sum(row_exchange(weighted(row_kernel, e, beta, x.shape[0])))
         part = first_beta * weighted(col_kernel, e, alpha, y.shape[0])
         part = part + halves(swap(part, core))
         beta = first_beta * (mass_b / sum(turned(swap(part, mask), z) for z, mask in enumerate(along)))
 
-    gi, gi_send, gc, gc_send = final_pass(x, y, e, alpha, beta, share_x, nz * share_y)
-    gc = gc + swap(gc_send, core)
+    gc, gc_send = column_grad(x.T, y, e, alpha, beta, nz * share_y)
+    gc = gc + swap(gc_send, core).astype(jnp.float32)
+    gi, gi_send = row_grad(x, y, e, alpha, beta, share_x)
     for s in range(1, na):
         gi = gi + swap(gi_send[(s - 1) * share_x:s * share_x], across[s]).astype(jnp.float32)
     grad_cam = gc[:share_y]

time: 247 us -> 237 us (0.960)
  Pallas kernels: 149 us -> 143 us
    pallas_call x2, Pallas kernels: 118 us -> 114 us  [first_pass(): pl.pallas_call(functools.partial(first_kernel, chunk, width, is_row), out...]
    pallas_call x1 -> x2, Pallas kernels: 14.6 us -> 12.3 us  [the longest x1 6.85 us: row_grad(): pl.pallas_call(functools.partial(row_grad_kernel, math.gcd(own, 512), own...]
    unnamed x82 -> x68, local copies, waits for them, and re-layouts: 8.32 us -> 8.52 us
  transfers between devices with their start and end apart: 38 -> 38, of which waited for: 24 -> 24; matrix products, arithmetic and copies ran while one was open for 2% -> 2% of each run, Pallas kernels for 0% -> 3%
where the time goes in v5:
time: 237 us
  Pallas kernels  143 us (60%)
  starting transfers between devices  43.6 us (18%)
  waiting for transfers between devices  34.6 us (15%)
  local copies, waits for them, and re-layouts  11.3 us (5%)
  other arithmetic  2.68 us (1%)
    pallas_call x2, Pallas kernels, first_pass(): pl.pallas_call(functools.partial(first_kernel, chunk, width, is_row), out...  114 us
    ppermute x38, starting transfers between devices, swap(): lax.ppermute(value, ('row', 'col'), [(i, i ^ mask) for i in range(self.co...  43.6 us
    ppermute x38, waiting for transfers between devices, swap(): lax.ppermute(value, ('row', 'col'), [(i, i ^ mask) for i in range(self.co...  34.6 us
    pallas_call x4, Pallas kernels, weighted(): pl.pallas_call(functools.partial(kernel, width), out_shape=jax.ShapeDtype...  16.5 us
    unnamed x68, local copies, waits for them, and re-layouts  8.52 us
    pallas_call x1, Pallas kernels, row_grad(): pl.pallas_call(functools.partial(row_grad_kernel, math.gcd(own, 512), own...  6.85 us
    pallas_call x1, Pallas kernels, column_grad(): pl.pallas_call(functools.partial(column_grad_kernel, width, own), out_sha...  5.42 us
  transfers between devices with their start and end apart: 38, of which 24 were waited for; matrix products, arithmetic and copies ran while one was open for 2% of the time, Pallas kernels for 3%

profile of v5, /device:TPU:0, one launch (start us, length us, event | category | flops | bytes accessed | tf_op | source)
XLA Modules:
  0.0 236.6 jit_solution(14414104360053573681)
XLA Ops:
  0.6 1.0 copy.9
  1.6 4.0 %collective-permute-start.2 = (bf16[512,128]{0,1:T(8,128)(2,1)S(1)}, bf16[512,128]{0,1:T(8,128)(2,1)S(1)}, u32[]{:S(2)}, u32[]{:S(2)}) collective-permute-start(bf16[512,128]{0,1:T(8,128)(2,1)S(1)} %copy.9), channel_id=1, source_target_pairs={{0,17},{1,16},{2,19},{3,18},{4,21},{5,20},{6,23},{7,22},{8,25},{9,... | collective-permute-start | bytes 393224 | tf_op jit(solution)/shard_map/ppermute | solution.py:371
  6.2 2.0 collective-permute-start.3
  8.2 2.6 %collective-permute-start.4 = (bf16[512,128]{1,0:T(8,128)(2,1)}, bf16[512,128]{1,0:T(8,128)(2,1)S(1)}, u32[]{:S(2)}, u32[]{:S(2)}) collective-permute-start(bf16[512,128]{1,0:T(8,128)(2,1)} %bitcast.304), channel_id=1, source_target_pairs={{0,4},{1,5},{2,6},{3,7},{4,0},{5,1},{6,2},{7,3},{8,12},{9,13},{10,... | collective-permute-start | bytes 393224 | tf_op jit(solution)/shard_map/ppermute | solution.py:371
  10.8 0.9 constant_dynamic-update-slice_fusion.7
  14.2 3.8 %collective-permute-done.4 = bf16[512,128]{1,0:T(8,128)(2,1)S(1)} collective-permute-done((bf16[512,128]{1,0:T(8,128)(2,1)}, bf16[512,128]{1,0:T(8,128)(2,1)S(1)}, u32[]{:S(2)}, u32[]{:S(2)}) %collective-permute-start.4) | collective-permute-done | bytes 131104 | tf_op jit(solution)/shard_map/ppermute | solution.py:371
  18.9 1.7 collective-permute-done.5
  20.7 1.2 collective-permute-done.9
  21.9 42.1 %first_pass.2 = f32[1,3072]{1,0:T(1,128)S(1)} custom-call(bf16[4096,128]{1,0:T(8,128)(2,1)S(1)} %constant_dynamic-update-slice_fusion.a_ref.b_ref.y_ref, bf16[2048,128]{1,0:T(8,128)(2,1)S(1)} %copy.12.b_ref.a_ref.x_ref, f32[8,128]{1,0:T(8,128)S(1)} %broadcast_in_dim.6.s_ref, f32[1,1024]{1,0:T(1,128)S(1)} %bitcast.298), custom_call_target="tpu_custom_call" | custom-call | flops 2147483648 | bytes 1572864 | tf_op jit(solution)/shard_map/first_pass/pallas_call | solution.py:221
  64.2 3.4 %collective-permute-start.11 = (f32[3072]{0:T(1024)S(1)}, f32[3072]{0:T(1024)S(1)}, u32[]{:S(2)}, u32[]{:S(2)}) collective-permute-start(f32[3072]{0:T(1024)S(1)} %bitcast.297), channel_id=1, source_target_pairs={{0,1},{1,0},{2,3},{3,2},{4,5},{5,4},{6,7},{7,6},{8,9},{9,8},{10,11... | collective-permute-start | bytes 36872 | tf_op jit(solution)/shard_map/ppermute | solution.py:371
  67.6 1.0 collective-permute-done.12
  69.4 72.2 %first_pass.3 = (f32[1,5120]{1,0:T(1,128)S(1)}, bf16[2048,4096]{1,0:T(8,128)(2,1)S(1)}, f32[1,4096]{1,0:T(1,128)S(1)}) custom-call(bf16[2048,128]{1,0:T(8,128)(2,1)S(1)} %copy.12.b_ref.a_ref.x_ref, bf16[4096,128]{1,0:T(8,128)(2,1)S(1)} %constant_dynamic-update-slice_fusion.a_ref.b_ref.y_ref, f32[16,128]{1,0:T(8,128)S(1)} %add_subtract_fusion.s_ref, ...), custom_call_target="tpu_custom_call" | custom-call | flops 2147483648 | bytes 1572864 | tf_op jit(solution)/shard_map/first_pass/pallas_call | solution.py:221
  141.7 1.1 collective-permute-done.13
  142.9 2.1 collective-permute-start.14
  144.9 4.1 %collective-permute-start.16 = (f32[5120]{0:T(1024)S(1)}, f32[5120]{0:T(1024)S(1)}, u32[]{:S(2)}, u32[]{:S(2)}) collective-permute-start(f32[5120]{0:T(1024)S(1)} %pad_maximum_fusion.1), channel_id=1, source_target_pairs={{0,6},{1,7},{2,4},{3,5},{4,2},{5,3},{6,0},{7,1},{8,14},{9,15},{10,... | collective-permute-start | bytes 61448 | tf_op jit(solution)/shard_map/ppermute | solution.py:371
  149.1 4.7 %collective-permute-done.15 = f32[5120]{0:T(1024)S(1)} collective-permute-done((f32[5120]{0:T(1024)S(1)}, f32[5120]{0:T(1024)S(1)}, u32[]{:S(2)}, u32[]{:S(2)}) %collective-permute-start.15) | collective-permute-done | bytes 20512 | tf_op jit(solution)/shard_map/ppermute | solution.py:371
  154.5 5.1 %weighted_sum.4 = f32[1,2048]{1,0:T(1,128)S(1)} custom-call(bf16[2048,4096]{1,0:T(8,128)(2,1)S(1)} %get-tuple-element.9.e_ref, f32[1,4096]{1,0:T(1,128)S(1)} %multiply_exponential_fusion.1.w_ref), custom_call_target="tpu_custom_call" | custom-call | flops 16777216 | bytes 16777216 | tf_op jit(solution)/shard_map/weighted_sum/pallas_call | solution.py:196
  159.9 1.2 collective-permute-start.18
  161.1 2.0 collective-permute-start.17
  163.3 0.9 collective-permute-done.19
  164.8 3.3 %weighted_sum.5 = f32[1,4096]{1,0:T(1,128)S(1)} custom-call(bf16[2048,4096]{1,0:T(8,128)(2,1)S(1)} %get-tuple-element.9.e_ref, f32[1,2048]{1,0:T(1,128)S(1)} %fusion.23.w_ref), custom_call_target="tpu_custom_call" | custom-call | flops 16777216 | bytes 16777216 | tf_op jit(solution)/shard_map/weighted_sum/pallas_call | solution.py:196
  168.2 1.2 collective-permute-done.20
  169.4 1.3 collective-permute-start.23
  170.7 3.0 %collective-permute-start.21 = (f32[4096]{0:T(1024)S(1)}, f32[4096]{0:T(1024)S(1)}, u32[]{:S(2)}, u32[]{:S(2)}) collective-permute-start(f32[4096]{0:T(1024)S(1)} %maximum_add_fusion.1), channel_id=1, source_target_pairs={{0,2},{1,3},{2,0},{3,1},{4,6},{5,7},{6,4},{7,5},{8,10},{9,11},{10,... | collective-permute-start | bytes 49160 | tf_op jit(solution)/shard_map/ppermute | solution.py:371
  173.8 1.1 collective-permute-done.23
  176.0 4.9 %weighted_sum.6 = f32[1,2048]{1,0:T(1,128)S(1)} custom-call(bf16[2048,4096]{1,0:T(8,128)(2,1)S(1)} %get-tuple-element.9.e_ref, f32[1,4096]{1,0:T(1,128)S(1)} %divide_multiply_fusion.w_ref), custom_call_target="tpu_custom_call" | custom-call | flops 16777216 | bytes 16777216 | tf_op jit(solution)/shard_map/weighted_sum/pallas_call | solution.py:196
  181.0 2.0 collective-permute-start.24
  183.3 1.2 collective-permute-start.26
  184.7 2.0 collective-permute-done.25
  186.7 1.2 collective-permute-done.26
  187.9 3.3 %weighted_sum.7 = f32[1,4096]{1,0:T(1,128)S(1)} custom-call(bf16[2048,4096]{1,0:T(8,128)(2,1)S(1)} %get-tuple-element.9.e_ref, f32[1,2048]{1,0:T(1,128)S(1)} %fusion.22.w_ref.alpha_ref), custom_call_target="tpu_custom_call" | custom-call | flops 16777216 | bytes 16777216 | tf_op jit(solution)/shard_map/weighted_sum/pallas_call | solution.py:196
  192.5 2.1 collective-permute-start.30
  194.6 1.4 collective-permute-start.29
  196.0 1.0 collective-permute-start.28
  197.0 1.1 collective-permute-done.30
  198.1 1.2 collective-permute-done.29
  199.9 5.8 %copy-done.1 = bf16[2048,4096]{1,0:T(8,128)(2,1)S(1)} copy-done((bf16[2048,4096]{1,0:T(8,128)(2,1)S(1)}, bf16[2048,4096]{1,0:T(8,128)(2,1)}, u32[]{:S(2)}) %copy-start.1) | copy-done | bytes 16777240
  205.7 5.4 %column_grad.1 = (f32[2048,128]{1,0:T(8,128)S(1)}, bf16[2048,128]{1,0:T(8,128)(2,1)S(1)}) custom-call(bf16[128,2048]{1,0:T(8,128)(2,1)S(1)} %get-tuple-element.23.xt_ref, bf16[4096,128]{1,0:T(8,128)(2,1)S(1)} %constant_dynamic-update-slice_fusion.a_ref.b_ref.y_ref, bf16[2048,4096]{1,0:T(8,128)(2,1)S(1)} %copy-done.1, f32[1,2048]{1,0:T(1,128)S(1)} %fusion.22.w_ref.alpha_ref, ...), custom_call_target="tpu_custom_call" | custom-call | flops 4294967296 | bytes 16777216 | tf_op jit(solution)/shard_map/column_grad/pallas_call | solution.py:281
  211.4 6.8 %row_grad.1 = (f32[512,128]{1,0:T(8,128)S(1)}, bf16[1536,128]{1,0:T(8,128)(2,1)S(1)}) custom-call(bf16[2048,128]{1,0:T(8,128)(2,1)S(1)} %copy.12.b_ref.a_ref.x_ref, bf16[4096,128]{1,0:T(8,128)(2,1)S(1)} %constant_dynamic-update-slice_fusion.a_ref.b_ref.y_ref, bf16[2048,4096]{1,0:T(8,128)(2,1)S(1)} %copy-done.2, f32[16,128]{1,0:T(8,128)S(1)} %fusion.19.alpha_ref, ...), custom_call_target="tpu_custom_call" | custom-call | flops 4294967296 | bytes 16777216 | tf_op jit(solution)/shard_map/row_grad/pallas_call | solution.py:342
  218.3 1.4 collective-permute-start.33
  219.7 0.9 collective-permute-start.32
  220.6 1.3 collective-permute-start.31
  222.1 1.6 collective-permute-start.37
  223.7 1.0 collective-permute-start.36
  224.6 1.0 collective-permute-done.33
  225.6 1.0 collective-permute-start.35
  228.5 1.9 collective-permute-done.37
  230.4 5.4 %collective-permute-done.36 = bf16[512,128]{1,0:T(8,128)(2,1)S(1)} collective-permute-done((bf16[512,128]{1,0:T(8,128)(2,1)S(1)}, bf16[512,128]{1,0:T(8,128)(2,1)S(1)}, u32[]{:S(2)}, u32[]{:S(2)}) %collective-permute-start.36) | collective-permute-done | bytes 131104 | tf_op jit(solution)/shard_map/ppermute | solution.py:371
  (177 shorter events, 13.3 us)
Async XLA Ops:
  1.6 11.8 %collective-permute-start.2 = (bf16[512,128]{0,1:T(8,128)(2,1)S(1)}, bf16[512,128]{0,1:T(8,128)(2,1)S(1)}, u32[]{:S(2)}, u32[]{:S(2)}) collective-permute-start(bf16[512,128]{0,1:T(8,128)(2,1)S(1)} %copy.9), channel_id=1, source_target_pairs={{0,17},{1,16},{2,19},{3,18},{4,21},{5,20},{6,23},{7,22},{8,25},{9,... | collective-permute-start | bytes 393224 | tf_op jit(solution)/shard_map/ppermute | solution.py:371
  5.6 8.4 %collective-permute-start.1 = (bf16[512,128]{0,1:T(8,128)(2,1)S(1)}, bf16[512,128]{0,1:T(8,128)(2,1)S(1)}, u32[]{:S(2)}, u32[]{:S(2)}) collective-permute-start(bf16[512,128]{0,1:T(8,128)(2,1)S(1)} %copy.9), channel_id=1, source_target_pairs={{0,16},{1,17},{2,18},{3,19},{4,20},{5,21},{6,22},{7,23},{8,24},{9,... | collective-permute-start | bytes 393224 | tf_op jit(solution)/shard_map/ppermute | solution.py:371
  6.1 7.9 %collective-permute-start = (bf16[512,128]{0,1:T(8,128)(2,1)S(1)}, bf16[512,128]{0,1:T(8,128)(2,1)S(1)}, u32[]{:S(2)}, u32[]{:S(2)}) collective-permute-start(bf16[512,128]{0,1:T(8,128)(2,1)S(1)} %copy.9), channel_id=1, source_target_pairs={{0,1},{1,0},{2,3},{3,2},{4,5},{5,4},{6,7},{7,6},{8,9},{9,8},{10,11... | collective-permute-start | bytes 393224 | tf_op jit(solution)/shard_map/ppermute | solution.py:371
  6.2 7.9 %collective-permute-start.3 = (bf16[512,128]{1,0:T(8,128)(2,1)}, bf16[512,128]{1,0:T(8,128)(2,1)S(1)}, u32[]{:S(2)}, u32[]{:S(2)}) collective-permute-start(bf16[512,128]{1,0:T(8,128)(2,1)} %bitcast.303), channel_id=1, source_target_pairs={{0,2},{1,3},{2,0},{3,1},{4,6},{5,7},{6,4},{7,5},{8,10},{9,11},{10,... | collective-permute-start | bytes 393224 | tf_op jit(solution)/shard_map/ppermute | solution.py:371
  8.2 9.8 %collective-permute-start.4 = (bf16[512,128]{1,0:T(8,128)(2,1)}, bf16[512,128]{1,0:T(8,128)(2,1)S(1)}, u32[]{:S(2)}, u32[]{:S(2)}) collective-permute-start(bf16[512,128]{1,0:T(8,128)(2,1)} %bitcast.304), channel_id=1, source_target_pairs={{0,4},{1,5},{2,6},{3,7},{4,0},{5,1},{6,2},{7,3},{8,12},{9,13},{10,... | collective-permute-start | bytes 393224 | tf_op jit(solution)/shard_map/ppermute | solution.py:371
  13.5 7.1 %collective-permute-start.5 = (bf16[512,128]{1,0:T(8,128)(2,1)}, bf16[512,128]{1,0:T(8,128)(2,1)S(1)}, u32[]{:S(2)}, u32[]{:S(2)}) collective-permute-start(bf16[512,128]{1,0:T(8,128)(2,1)} %bitcast.305), channel_id=1, source_target_pairs={{0,6},{1,7},{2,4},{3,5},{4,2},{5,3},{6,0},{7,1},{8,14},{9,15},{10,... | collective-permute-start | bytes 393224 | tf_op jit(solution)/shard_map/ppermute | solution.py:371
  14.0 6.5 %collective-permute-start.6 = (bf16[512,128]{1,0:T(8,128)(2,1)}, bf16[512,128]{1,0:T(8,128)(2,1)S(1)}, u32[]{:S(2)}, u32[]{:S(2)}) collective-permute-start(bf16[512,128]{1,0:T(8,128)(2,1)} %bitcast.306), channel_id=1, source_target_pairs={{0,8},{1,9},{2,10},{3,11},{4,12},{5,13},{6,14},{7,15},{8,0},{9,1},... | collective-permute-start | bytes 393224 | tf_op jit(solution)/shard_map/ppermute | solution.py:371
  18.3 2.3 collective-permute-start.7
  18.4 2.3 collective-permute-start.8
  20.5 1.3 collective-permute-start.9
  64.0 4.7 %collective-permute-start.12 = (f32[3072]{0:T(1024)S(1)}, f32[3072]{0:T(1024)S(1)}, u32[]{:S(2)}, u32[]{:S(2)}) collective-permute-start(f32[3072]{0:T(1024)S(1)} %bitcast.295), channel_id=1, source_target_pairs={{0,17},{1,16},{2,19},{3,18},{4,21},{5,20},{6,23},{7,22},{8,25},{9,... | collective-permute-start | bytes 36872 | tf_op jit(solution)/shard_map/ppermute | solution.py:371
  64.1 4.5 %collective-permute-start.10 = (f32[3072]{0:T(1024)S(1)}, f32[3072]{0:T(1024)S(1)}, u32[]{:S(2)}, u32[]{:S(2)}) collective-permute-start(f32[3072]{0:T(1024)S(1)} %bitcast.296), channel_id=1, source_target_pairs={{0,16},{1,17},{2,18},{3,19},{4,20},{5,21},{6,22},{7,23},{8,24},{9,... | collective-permute-start | bytes 36872 | tf_op jit(solution)/shard_map/ppermute | solution.py:371
  64.2 5.1 %collective-permute-start.11 = (f32[3072]{0:T(1024)S(1)}, f32[3072]{0:T(1024)S(1)}, u32[]{:S(2)}, u32[]{:S(2)}) collective-permute-start(f32[3072]{0:T(1024)S(1)} %bitcast.297), channel_id=1, source_target_pairs={{0,1},{1,0},{2,3},{3,2},{4,5},{5,4},{6,7},{7,6},{8,9},{9,8},{10,11... | collective-permute-start | bytes 36872 | tf_op jit(solution)/shard_map/ppermute | solution.py:371
  141.5 46.4 %copy-start = (bf16[2048,4096]{1,0:T(8,128)(2,1)}, bf16[2048,4096]{1,0:T(8,128)(2,1)S(1)}, u32[]{:S(2)}) copy-start(bf16[2048,4096]{1,0:T(8,128)(2,1)S(1)} %get-tuple-element.9.e_ref) | copy-start | bytes 50331652
  141.6 1.2 collective-permute-start.13
  142.9 6.2 %collective-permute-start.14 = (f32[5120]{0:T(1024)S(1)}, f32[5120]{0:T(1024)S(1)}, u32[]{:S(2)}, u32[]{:S(2)}) collective-permute-start(f32[5120]{0:T(1024)S(1)} %pad_maximum_fusion.1), channel_id=1, source_target_pairs={{0,2},{1,3},{2,0},{3,1},{4,6},{5,7},{6,4},{7,5},{8,10},{9,11},{10,... | collective-permute-start | bytes 61448 | tf_op jit(solution)/shard_map/ppermute | solution.py:371
  144.9 8.8 %collective-permute-start.16 = (f32[5120]{0:T(1024)S(1)}, f32[5120]{0:T(1024)S(1)}, u32[]{:S(2)}, u32[]{:S(2)}) collective-permute-start(f32[5120]{0:T(1024)S(1)} %pad_maximum_fusion.1), channel_id=1, source_target_pairs={{0,6},{1,7},{2,4},{3,5},{4,2},{5,3},{6,0},{7,1},{8,14},{9,15},{10,... | collective-permute-start | bytes 61448 | tf_op jit(solution)/shard_map/ppermute | solution.py:371
  149.0 4.7 %collective-permute-start.15 = (f32[5120]{0:T(1024)S(1)}, f32[5120]{0:T(1024)S(1)}, u32[]{:S(2)}, u32[]{:S(2)}) collective-permute-start(f32[5120]{0:T(1024)S(1)} %pad_maximum_fusion.1), channel_id=1, source_target_pairs={{0,4},{1,5},{2,6},{3,7},{4,0},{5,1},{6,2},{7,3},{8,12},{9,13},{10,... | collective-permute-start | bytes 61448 | tf_op jit(solution)/shard_map/ppermute | solution.py:371
  159.6 4.6 %collective-permute-start.19 = (f32[2048]{0:T(1024)S(1)}, f32[2048]{0:T(1024)S(1)}, u32[]{:S(2)}, u32[]{:S(2)}) collective-permute-start(f32[2048]{0:T(1024)S(1)} %bitcast.292), channel_id=1, source_target_pairs={{0,17},{1,16},{2,19},{3,18},{4,21},{5,20},{6,23},{7,22},{8,25},{9,... | collective-permute-start | bytes 24584 | tf_op jit(solution)/shard_map/ppermute | solution.py:371
  159.9 4.3 %collective-permute-start.18 = (f32[2048]{0:T(1024)S(1)}, f32[2048]{0:T(1024)S(1)}, u32[]{:S(2)}, u32[]{:S(2)}) collective-permute-start(f32[2048]{0:T(1024)S(1)} %bitcast.293), channel_id=1, source_target_pairs={{0,16},{1,17},{2,18},{3,19},{4,20},{5,21},{6,22},{7,23},{8,24},{9,... | collective-permute-start | bytes 24584 | tf_op jit(solution)/shard_map/ppermute | solution.py:371
  161.1 3.7 %collective-permute-start.17 = (f32[2048]{0:T(1024)S(1)}, f32[2048]{0:T(1024)S(1)}, u32[]{:S(2)}, u32[]{:S(2)}) collective-permute-start(f32[2048]{0:T(1024)S(1)} %bitcast.294), channel_id=1, source_target_pairs={{0,1},{1,0},{2,3},{3,2},{4,5},{5,4},{6,7},{7,6},{8,9},{9,8},{10,11... | collective-permute-start | bytes 24584 | tf_op jit(solution)/shard_map/ppermute | solution.py:371
  168.1 1.2 collective-permute-start.20
  169.4 5.5 %collective-permute-start.23 = (f32[4096]{0:T(1024)S(1)}, f32[4096]{0:T(1024)S(1)}, u32[]{:S(2)}, u32[]{:S(2)}) collective-permute-start(f32[4096]{0:T(1024)S(1)} %maximum_add_fusion.1), channel_id=1, source_target_pairs={{0,6},{1,7},{2,4},{3,5},{4,2},{5,3},{6,0},{7,1},{8,14},{9,15},{10,... | collective-permute-start | bytes 49160 | tf_op jit(solution)/shard_map/ppermute | solution.py:371
  170.7 5.0 %collective-permute-start.22 = (f32[4096]{0:T(1024)S(1)}, f32[4096]{0:T(1024)S(1)}, u32[]{:S(2)}, u32[]{:S(2)}) collective-permute-start(f32[4096]{0:T(1024)S(1)} %maximum_add_fusion.1), channel_id=1, source_target_pairs={{0,4},{1,5},{2,6},{3,7},{4,0},{5,1},{6,2},{7,3},{8,12},{9,13},{10,... | collective-permute-start | bytes 49160 | tf_op jit(solution)/shard_map/ppermute | solution.py:371
  170.7 4.8 %collective-permute-start.21 = (f32[4096]{0:T(1024)S(1)}, f32[4096]{0:T(1024)S(1)}, u32[]{:S(2)}, u32[]{:S(2)}) collective-permute-start(f32[4096]{0:T(1024)S(1)} %maximum_add_fusion.1), channel_id=1, source_target_pairs={{0,2},{1,3},{2,0},{3,1},{4,6},{5,7},{6,4},{7,5},{8,10},{9,11},{10,... | collective-permute-start | bytes 49160 | tf_op jit(solution)/shard_map/ppermute | solution.py:371
  181.0 3.7 %collective-permute-start.24 = (f32[2048]{0:T(1024)S(1)}, f32[2048]{0:T(1024)S(1)}, u32[]{:S(2)}, u32[]{:S(2)}) collective-permute-start(f32[2048]{0:T(1024)S(1)} %bitcast.288), channel_id=1, source_target_pairs={{0,1},{1,0},{2,3},{3,2},{4,5},{5,4},{6,7},{7,6},{8,9},{9,8},{10,11... | collective-permute-start | bytes 24584 | tf_op jit(solution)/shard_map/ppermute | solution.py:371
  183.0 3.7 %collective-permute-start.25 = (f32[2048]{0:T(1024)S(1)}, f32[2048]{0:T(1024)S(1)}, u32[]{:S(2)}, u32[]{:S(2)}) collective-permute-start(f32[2048]{0:T(1024)S(1)} %bitcast.289), channel_id=1, source_target_pairs={{0,16},{1,17},{2,18},{3,19},{4,20},{5,21},{6,22},{7,23},{8,24},{9,... | collective-permute-start | bytes 24584 | tf_op jit(solution)/shard_map/ppermute | solution.py:371
  183.3 4.5 %collective-permute-start.26 = (f32[2048]{0:T(1024)S(1)}, f32[2048]{0:T(1024)S(1)}, u32[]{:S(2)}, u32[]{:S(2)}) collective-permute-start(f32[2048]{0:T(1024)S(1)} %bitcast.290), channel_id=1, source_target_pairs={{0,17},{1,16},{2,19},{3,18},{4,21},{5,20},{6,23},{7,22},{8,25},{9,... | collective-permute-start | bytes 24584 | tf_op jit(solution)/shard_map/ppermute | solution.py:371
  191.2 1.2 collective-permute-start.27
  192.5 5.6 %collective-permute-start.30 = (f32[4096]{0:T(1024)S(1)}, f32[4096]{0:T(1024)S(1)}, u32[]{:S(2)}, u32[]{:S(2)}) collective-permute-start(f32[4096]{0:T(1024)S(1)} %maximum_add_fusion.3), channel_id=1, source_target_pairs={{0,6},{1,7},{2,4},{3,5},{4,2},{5,3},{6,0},{7,1},{8,14},{9,15},{10,... | collective-permute-start | bytes 49160 | tf_op jit(solution)/shard_map/ppermute | solution.py:371
  194.6 4.7 %collective-permute-start.29 = (f32[4096]{0:T(1024)S(1)}, f32[4096]{0:T(1024)S(1)}, u32[]{:S(2)}, u32[]{:S(2)}) collective-permute-start(f32[4096]{0:T(1024)S(1)} %maximum_add_fusion.3), channel_id=1, source_target_pairs={{0,4},{1,5},{2,6},{3,7},{4,0},{5,1},{6,2},{7,3},{8,12},{9,13},{10,... | collective-permute-start | bytes 49160 | tf_op jit(solution)/shard_map/ppermute | solution.py:371
  196.0 3.7 %collective-permute-start.28 = (f32[4096]{0:T(1024)S(1)}, f32[4096]{0:T(1024)S(1)}, u32[]{:S(2)}, u32[]{:S(2)}) collective-permute-start(f32[4096]{0:T(1024)S(1)} %maximum_add_fusion.3), channel_id=1, source_target_pairs={{0,2},{1,3},{2,0},{3,1},{4,6},{5,7},{6,4},{7,5},{8,10},{9,11},{10,... | collective-permute-start | bytes 49160 | tf_op jit(solution)/shard_map/ppermute | solution.py:371
  199.9 5.8 %copy-start.1 = (bf16[2048,4096]{1,0:T(8,128)(2,1)S(1)}, bf16[2048,4096]{1,0:T(8,128)(2,1)}, u32[]{:S(2)}) copy-start(bf16[2048,4096]{1,0:T(8,128)(2,1)} %copy-done) | copy-start | bytes 50331652
  205.7 5.8 %copy-start.2 = (bf16[2048,4096]{1,0:T(8,128)(2,1)S(1)}, bf16[2048,4096]{1,0:T(8,128)(2,1)}, u32[]{:S(2)}) copy-start(bf16[2048,4096]{1,0:T(8,128)(2,1)} %copy-done) | copy-start | bytes 50331652
  211.1 10.8 %collective-permute-start.34 = (bf16[2048,128]{1,0:T(8,128)(2,1)S(1)}, bf16[2048,128]{1,0:T(8,128)(2,1)S(1)}, u32[]{:S(2)}, u32[]{:S(2)}) collective-permute-start(bf16[2048,128]{1,0:T(8,128)(2,1)S(1)} %get-tuple-element.15), channel_id=1, source_target_pairs={{0,8},{1,9},{2,10},{3,11},{4,12},{5,13},{6,14},{7,15},{8,0},{9,1},... | collective-permute-start | bytes 1572872 | tf_op jit(solution)/shard_map/ppermute | solution.py:371
  218.3 7.3 %collective-permute-start.33 = (bf16[512,128]{1,0:T(8,128)(2,1)S(1)}, bf16[512,128]{1,0:T(8,128)(2,1)S(1)}, u32[]{:S(2)}, u32[]{:S(2)}) collective-permute-start(bf16[512,128]{1,0:T(8,128)(2,1)S(1)} %get-tuple-element.26), channel_id=1, source_target_pairs={{0,17},{1,16},{2,19},{3,18},{4,21},{5,20},{6,23},{7,22},{8,25},{9,... | collective-permute-start | bytes 393224 | tf_op jit(solution)/shard_map/ppermute | solution.py:371
  219.7 7.3 %collective-permute-start.32 = (bf16[512,128]{1,0:T(8,128)(2,1)S(1)}, bf16[512,128]{1,0:T(8,128)(2,1)S(1)}, u32[]{:S(2)}, u32[]{:S(2)}) collective-permute-start(bf16[512,128]{1,0:T(8,128)(2,1)S(1)} %get-tuple-element.27), channel_id=1, source_target_pairs={{0,16},{1,17},{2,18},{3,19},{4,20},{5,21},{6,22},{7,23},{8,24},{9,... | collective-permute-start | bytes 393224 | tf_op jit(solution)/shard_map/ppermute | solution.py:371
  220.6 7.1 %collective-permute-start.31 = (bf16[512,128]{1,0:T(8,128)(2,1)S(1)}, bf16[512,128]{1,0:T(8,128)(2,1)S(1)}, u32[]{:S(2)}, u32[]{:S(2)}) collective-permute-start(bf16[512,128]{1,0:T(8,128)(2,1)S(1)} %get-tuple-element.25), channel_id=1, source_target_pairs={{0,1},{1,0},{2,3},{3,2},{4,5},{5,4},{6,7},{7,6},{8,9},{9,8},{10,11... | collective-permute-start | bytes 393224 | tf_op jit(solution)/shard_map/ppermute | solution.py:371
  222.1 8.3 %collective-permute-start.37 = (bf16[512,128]{1,0:T(8,128)(2,1)S(1)}, bf16[512,128]{1,0:T(8,128)(2,1)S(1)}, u32[]{:S(2)}, u32[]{:S(2)}) collective-permute-start(bf16[512,128]{1,0:T(8,128)(2,1)S(1)} %get-tuple-element.21), channel_id=1, source_target_pairs={{0,6},{1,7},{2,4},{3,5},{4,2},{5,3},{6,0},{7,1},{8,14},{9,15},{10,... | collective-permute-start | bytes 393224 | tf_op jit(solution)/shard_map/ppermute | solution.py:371
  223.7 12.2 %collective-permute-start.36 = (bf16[512,128]{1,0:T(8,128)(2,1)S(1)}, bf16[512,128]{1,0:T(8,128)(2,1)S(1)}, u32[]{:S(2)}, u32[]{:S(2)}) collective-permute-start(bf16[512,128]{1,0:T(8,128)(2,1)S(1)} %get-tuple-element.22), channel_id=1, source_target_pairs={{0,4},{1,5},{2,6},{3,7},{4,0},{5,1},{6,2},{7,3},{8,12},{9,13},{10,... | collective-permute-start | bytes 393224 | tf_op jit(solution)/shard_map/ppermute | solution.py:371
  225.6 10.2 %collective-permute-start.35 = (bf16[512,128]{1,0:T(8,128)(2,1)S(1)}, bf16[512,128]{1,0:T(8,128)(2,1)S(1)}, u32[]{:S(2)}, u32[]{:S(2)}) collective-permute-start(bf16[512,128]{1,0:T(8,128)(2,1)S(1)} %get-tuple-element.20), channel_id=1, source_target_pairs={{0,2},{1,3},{2,0},{3,1},{4,6},{5,7},{6,4},{7,5},{8,10},{9,11},{10,... | collective-permute-start | bytes 393224 | tf_op jit(solution)/shard_map/ppermute | solution.py:371

commit v6 on v5

--- a/solution.py
+++ b/solution.py
@@ -16,6 +16,7 @@
 NT = (((1,), (1,)), ((), ()))
 VMEM = pl.BlockSpec(memory_space=pltpu.VMEM)
 GROUP = 32
+ROOM = 8 << 20
 
 
 def spread(s_ref, sb_ref):
@@ -25,33 +26,21 @@
         sb_ref[k * 128:(k + 1) * 128, :] = jnp.broadcast_to(turned[:, k:k + 1], (128, 128))
 
 
-def norms(a_ref, sb_ref, chunk):
-    def block(k, _):
-        at = pl.multiple_of(k * chunk, chunk)
-        a = a_ref[pl.ds(at, chunk), :].astype(jnp.float32)
-        total = jnp.sum(a * a, axis=1, keepdims=True) * (-LOG2E / EPSILON)
-        sb_ref[pl.ds(at, chunk), :] = jnp.broadcast_to(total, (chunk, 128))
-        return 0
-
-    lax.fori_loop(0, a_ref.shape[0] // chunk, block, 0)
-
-
-def pipelined(chunk, width, a_ref, b_ref, d_ref, head, tile, finish):
-    depth, lanes = a_ref.shape[0], b_ref.shape[0]
-    steps, last = depth // chunk, lanes // width - 1
+def pipelined(places, chunk, width, a_ref, b_ref, d_ref, tile, finish):
+    last = b_ref.shape[0] // width - 1
 
     def product(n, m):
         b = b_ref[pl.ds(pl.multiple_of(n * width, width), width), :]
-        a = a_ref[m * chunk:(m + 1) * chunk, :]
+        a = a_ref[places[m]:places[m] + chunk, :]
         d_ref[m % 2] = lax.dot_general(a, b, NT, preferred_element_type=jnp.float32)
 
     product(0, 0)
 
     def column(n, _):
         start = pl.multiple_of(n * width, width)
-        state = head(start)
-        for m in range(steps):
-            if m + 1 < steps:
+        state = None
+        for m in range(len(places)):
+            if m + 1 < len(places):
                 product(n, m + 1)
             else:
                 product(jnp.minimum(n + 1, last), 0)
@@ -62,58 +51,40 @@
     lax.fori_loop(0, last + 1, column, 0)
 
 
-def running_max(chunk, width, a_ref, b_ref, sb_ref, o_ref, e_ref, shift_ref):
-    depth, lanes = a_ref.shape[0], b_ref.shape[0]
-
+def running_max(places, chunk, width, a_ref, b_ref, sb_ref, o_ref, e_ref, shift_ref):
     def column(n, _):
         start = pl.multiple_of(n * width, width)
         b = b_ref[pl.ds(start, width), :]
 
-        def exponents(m):
-            at = pl.multiple_of(m * chunk, chunk)
-            d = lax.dot_general(a_ref[pl.ds(at, chunk), :], b, NT, preferred_element_type=jnp.float32)
-            s = sb_ref[pl.ds(at, chunk), :]
-            return at, [d[:, q * 128:(q + 1) * 128] * CROSS + s for q in range(width // 128)]
-
-        def step(m, carry):
-            peak, total = carry
+        def exponents(at):
+            d = lax.dot_general(a_ref[at:at + chunk, :], b, NT, preferred_element_type=jnp.float32)
+            s = sb_ref[at:at + chunk, :]
+            return [d[:, q * 128:(q + 1) * 128] * CROSS + s for q in range(width // 128)]
+
+        peak, total = jnp.full((1, width), -1e30, jnp.float32), jnp.zeros((1, width), jnp.float32)
+        for at in places:
             peaks, totals = [], []
-            for q, t in enumerate(exponents(m)[1]):
+            for q, t in enumerate(exponents(at)):
                 old = peak[:, q * 128:(q + 1) * 128]
                 new = jnp.maximum(old, jnp.max(t, axis=0, keepdims=True))
                 part = jnp.sum(jnp.exp2(t - new), axis=0, keepdims=True)
                 peaks.append(new)
                 totals.append(total[:, q * 128:(q + 1) * 128] * jnp.exp2(old - new) + part)
-            return jnp.concatenate(peaks, axis=1), jnp.concatenate(totals, axis=1)
-
-        def store(m, _):
-            at, ts = exponents(m)
-            for q, t in enumerate(ts):
-                place = pl.ds(pl.multiple_of(start + q * 128, 128), 128)
-                e_ref[pl.ds(at, chunk), place] = jnp.exp2(t - shift_ref[:, place]).astype(jnp.bfloat16)
-            return 0
-
-        init = (jnp.full((1, width), -1e30, jnp.float32), jnp.zeros((1, width), jnp.float32))
-        peak, total = lax.fori_loop(0, depth // chunk, step, init)
+            peak, total = jnp.concatenate(peaks, axis=1), jnp.concatenate(totals, axis=1)
         o_ref[:, pl.ds(start, width)] = peak + jnp.log2(total)
         if e_ref is not None:
             shift_ref[:, pl.ds(start, width)] = peak
-            lax.fori_loop(0, depth // chunk, store, 0)
+            for at in places:
+                for q, t in enumerate(exponents(at)):
+                    place = pl.ds(pl.multiple_of(start + q * 128, 128), 128)
+                    e_ref[at:at + chunk, place] = jnp.exp2(t - shift_ref[:, place]).astype(jnp.bfloat16)
         return 0
 
-    lax.fori_loop(0, lanes // width, column, 0)
-
-
-def first_kernel(chunk, width, is_row, a_ref, b_ref, s_ref, mass_ref, o_ref, *rest):
-    e_ref, shift_ref = (None, None) if is_row else rest[:2]
-    sb_ref, d_ref, top_ref = rest[-3:]
-    lanes = b_ref.shape[0]
+    lax.fori_loop(0, b_ref.shape[0] // width, column, 0)
+
+
+def lse_pass(places, chunk, width, a_ref, b_ref, sb_ref, d_ref, top_ref, o_ref, e_ref=None, shift_ref=None):
     tiles = width // 128
-    if is_row:
-        norms(a_ref, sb_ref, chunk)
-    else:
-        spread(s_ref, sb_ref)
-    o_ref[:, lanes:] = mass_ref[...]
     top_ref[...] = jnp.zeros_like(top_ref)
 
     def lanes_of(start, q):
@@ -122,7 +93,7 @@
     def tile(m, start, state):
         def exponents(g, q):
             at = g * GROUP
-            s = sb_ref[m * chunk + at:m * chunk + at + GROUP, :]
+            s = sb_ref[places[m] + at:places[m] + at + GROUP, :]
             return d_ref[m % 2, at:at + GROUP, q * 128:(q + 1) * 128] * CROSS + s
 
         if m == 0:
@@ -134,7 +105,7 @@
             for q, (peak, total) in enumerate(state):
                 e = jnp.exp2(exponents(g, q) - peak)
                 if e_ref is not None:
-                    at = m * chunk + g * GROUP
+                    at = places[m] + g * GROUP
                     e_ref[at:at + GROUP, lanes_of(start, q)] = e.astype(jnp.bfloat16)
                 state[q] = peak, total + e
         return state
@@ -146,11 +117,59 @@
             if e_ref is not None:
                 shift_ref[:, lanes_of(start, q)] = peak
 
-    pipelined(chunk, width, a_ref, b_ref, d_ref, lambda start: None, tile, finish)
+    pipelined(places, chunk, width, a_ref, b_ref, d_ref, tile, finish)
 
     @pl.when(jnp.logical_not(jnp.max(top_ref[...]) < 2.0 ** 60))
     def _():
-        running_max(min(chunk, 256), min(width, 256), a_ref, b_ref, sb_ref, o_ref, e_ref, shift_ref)
+        running_max(places, chunk, min(width, 256), a_ref, b_ref, sb_ref, o_ref, e_ref, shift_ref)
+
+
+def put_pair(o_ref, at, mass_ref, axis):
+    share = mass_ref.shape[1]
+    place = lax.axis_index(axis)
+    for k in range(2):
+        o_ref[:, at + k * share:at + (k + 1) * share] = mass_ref[pl.ds(place ^ k, 1), :]
+
+
+def row_lse_kernel(width, early, nx, ny, *refs):
+    xs, ys, refs = refs[:nx], refs[nx:nx + ny], refs[nx + ny:]
+    share = ys[0].shape[0]
+    if early:
+        x_ref, xt_ref, o_ref, y_ref, sb_ref, d_ref, top_ref = refs
+        part = xs[0].shape[0]
+        for k, shard in enumerate(xs):
+            x_ref[k * part:(k + 1) * part, :] = shard[...]
+        for k in range(x_ref.shape[0] // 128):
+            at = k * 128
+            turned = jnp.transpose(x_ref[at:at + 128, :].astype(jnp.float32))
+            xt_ref[:, at:at + 128] = turned.astype(jnp.bfloat16)
+        places = [k * share for k in range(ny)]
+    else:
+        x_ref, first_ref, mass_ref, y_ref, o_ref, sb_ref, d_ref, top_ref, sum_ref = refs
+        places = [k * share for k in range(ny) if k % (ny // 2)]
+    for k, shard in enumerate(ys):
+        y_ref[k * share:(k + 1) * share, :] = shard[...]
+    for at in places:
+        y = y_ref[at:at + share, :].astype(jnp.float32)
+        total = jnp.sum(y * y, axis=1, keepdims=True) * (-LOG2E / EPSILON)
+        sb_ref[at:at + share, :] = jnp.broadcast_to(total, (share, 128))
+    if early:
+        lse_pass(places, share, width, y_ref, x_ref, sb_ref, d_ref, top_ref, o_ref)
+    else:
+        lse_pass(places, share, width, y_ref, x_ref, sb_ref, d_ref, top_ref, sum_ref)
+        rows = x_ref.shape[0]
+        one, two = first_ref[...], sum_ref[...]
+        top = jnp.maximum(one, two)
+        o_ref[:, :rows] = top + jnp.log2(jnp.exp2(one - top) + jnp.exp2(two - top))
+        put_pair(o_ref, rows, mass_ref, "col")
+
+
+def column_lse_kernel(width, chunk, x_ref, y_ref, u_ref, mass_ref, o_ref, e_ref, shift_ref,
+                      sb_ref, d_ref, top_ref, room_ref):
+    spread(u_ref, sb_ref)
+    put_pair(o_ref, y_ref.shape[0], mass_ref, "row")
+    places = list(range(0, x_ref.shape[0], chunk))
+    lse_pass(places, chunk, width, x_ref, y_ref, sb_ref, d_ref, top_ref, o_ref, e_ref, shift_ref)
 
 
 def split3(value):
@@ -206,34 +225,66 @@
     return out.reshape(lanes)
 
 
-def pass_cost(a, b):
-    size = a.shape[0] * b.shape[0]
-    return pl.CostEstimate(flops=2 * size * D, bytes_accessed=2 * (a.size + b.size), transcendentals=size)
-
-
-def first_pass(a, b, s, mass, chunk=512, width=512):
-    depth, lanes, extra = a.shape[0], b.shape[0], mass.shape[0]
-    is_row = s is None
-    s = jnp.zeros((8, 128), jnp.float32) if is_row else s.reshape(depth // 128, 128)
-    out_shape = [jax.ShapeDtypeStruct((1, lanes + extra), jnp.float32)]
-    if not is_row:
-        out_shape += [jax.ShapeDtypeStruct((depth, lanes), jnp.bfloat16), jax.ShapeDtypeStruct((1, lanes), jnp.float32)]
-    out = pl.pallas_call(
-        functools.partial(first_kernel, chunk, width, is_row),
-        out_shape=out_shape,
+def pass_cost(depth, lanes):
+    return pl.CostEstimate(flops=2 * depth * lanes * D, bytes_accessed=2 * D * (depth + lanes), transcendentals=depth * lanes)
+
+
+def shape(*dims, dtype=jnp.float32):
+    return jax.ShapeDtypeStruct(dims, dtype)
+
+
+def lse_scratch(depth, chunk, width):
+    return [
+        pltpu.VMEM((depth, 128), jnp.float32),
+        pltpu.VMEM((2, chunk, width), jnp.float32),
+        pltpu.VMEM((GROUP, 128), jnp.float32),
+    ]
+
+
+def row_lse_early(xs, ys, width=512):
+    rows, share = len(xs) * xs[0].shape[0], ys[0].shape[0]
+    depth = len(ys) * share
+    return pl.pallas_call(
+        functools.partial(row_lse_kernel, width, True, len(xs), len(ys)),
+        out_shape=(shape(rows, D, dtype=jnp.bfloat16), shape(D, rows, dtype=jnp.bfloat16), shape(1, rows)),
+        in_specs=[VMEM] * (len(xs) + len(ys)),
+        out_specs=(VMEM,) * 3,
+        scratch_shapes=[pltpu.VMEM((depth, D), jnp.bfloat16)] + lse_scratch(depth, share, width),
+        compiler_params=pltpu.CompilerParams(vmem_limit_bytes=16 << 20),
+        cost_estimate=pass_cost(depth, rows),
+        name="row_lse_early",
+    )(*xs, *ys)
+
+
+def row_lse_late(x, ys, first, mass, width=512):
+    rows, share = x.shape[0], ys[0].shape[0]
+    depth = len(ys) * share
+    tail = mass.shape[0] // lax.axis_size("col")
+    return pl.pallas_call(
+        functools.partial(row_lse_kernel, width, False, 0, len(ys)),
+        out_shape=(shape(depth, D, dtype=jnp.bfloat16), shape(1, rows + 2 * tail)),
+        in_specs=[VMEM] * (len(ys) + 3),
+        out_specs=(VMEM,) * 2,
+        scratch_shapes=lse_scratch(depth, share, width) + [pltpu.VMEM((1, rows), jnp.float32)],
+        compiler_params=pltpu.CompilerParams(vmem_limit_bytes=16 << 20),
+        cost_estimate=pass_cost(depth - 2 * share, rows),
+        name="row_lse_late",
+    )(*ys, x, first, mass.reshape(-1, tail))
+
+
+def column_lse(x, y, u, mass, width=512, chunk=512):
+    rows, cols = x.shape[0], y.shape[0]
+    tail = mass.shape[0] // lax.axis_size("row")
+    return pl.pallas_call(
+        functools.partial(column_lse_kernel, width, chunk),
+        out_shape=(shape(1, cols + 2 * tail), shape(rows, cols, dtype=jnp.bfloat16), shape(1, cols)),
         in_specs=[VMEM] * 4,
-        out_specs=[VMEM] * len(out_shape),
-        scratch_shapes=[
-            pltpu.VMEM((depth, 128), jnp.float32),
-            pltpu.VMEM((2, chunk, width), jnp.float32),
-            pltpu.VMEM((GROUP, 128), jnp.float32),
-        ],
-        compiler_params=pltpu.CompilerParams(vmem_limit_bytes=16 << 20),
-        cost_estimate=pass_cost(a, b),
-        name="first_pass",
-    )(a, b, s, mass.reshape(1, extra))
-    sent = out[0].reshape(lanes + extra)
-    return sent if is_row else (sent, out[1], out[2].reshape(lanes))
+        out_specs=(VMEM,) * 3,
+        scratch_shapes=lse_scratch(rows, chunk, width) + [pltpu.VMEM((ROOM // 512, 128), jnp.float32)],
+        compiler_params=pltpu.CompilerParams(vmem_limit_bytes=24 << 20),
+        cost_estimate=pass_cost(rows, cols),
+        name="column_lse",
+    )(x, y, u.reshape(rows // 128, 128), mass.reshape(-1, tail))
 
 
 def high_low(value):
@@ -299,8 +350,17 @@
     )(xt, y, e, alpha.reshape(1, rows), beta.reshape(cols // 128, 128))
 
 
-def row_grad_kernel(chunk, own, x_ref, y_ref, e_ref, alpha_ref, beta_ref, gi_ref, gis_ref, ab_ref, bb_ref, yb_ref):
-    rows, cols = x_ref.shape[0], y_ref.shape[0]
+def row_block(at, chunk, x_ref, e_ref, yb_ref, scale):
+    got = jnp.dot(e_ref[pl.ds(at, chunk), :], yb_ref[...], preferred_element_type=jnp.float32)
+    lower = lax.broadcasted_iota(jnp.int32, (chunk, 128), 1) < 126
+    total = got[:, 254:255] + got[:, 255:256]
+    pulled = got[:, :128] + jnp.where(lower, got[:, 128:], 0.0)
+    x = x_ref[pl.ds(at, chunk), :].astype(jnp.float32)
+    return 2.0 * scale * (total * x - pulled)
+
+
+def own_rows_kernel(x_ref, y_ref, e_ref, alpha_ref, beta_ref, gi_ref, yb_ref, ab_ref, bb_ref):
+    own, cols = gi_ref.shape[0], y_ref.shape[0]
     spread(alpha_ref, ab_ref)
     spread(beta_ref, bb_ref)
     place = lax.broadcasted_iota(jnp.int32, (256, 128), 1)
@@ -313,49 +373,48 @@
         low = jnp.where(place == 127, second.astype(jnp.float32), low)
         yb_ref[at:at + 256, :128] = high
         yb_ref[at:at + 256, 128:] = low.astype(jnp.bfloat16)
-
-    lower = lax.broadcasted_iota(jnp.int32, (chunk, 128), 1) < 126
-
-    def block(at):
-        got = jnp.dot(e_ref[pl.ds(at, chunk), :], yb_ref[...], preferred_element_type=jnp.float32)
-        total = got[:, 254:255] + got[:, 255:256]
-        pulled = got[:, :128] + jnp.where(lower, got[:, 128:], 0.0)
-        x = x_ref[pl.ds(at, chunk), :].astype(jnp.float32)
-        return 2.0 * ab_ref[pl.ds(at, chunk), :] * (total * x - pulled)
-
-    def own_block(k, _):
+    gi_ref[...] = row_block(0, own, x_ref, e_ref, yb_ref, ab_ref[:own, :])
+
+
+def sent_rows_kernel(chunk, own, x_ref, yb_ref, e_ref, alpha_ref, gis_ref, ab_ref):
+    spread(alpha_ref, ab_ref)
+
+    def block(k, _):
         at = pl.multiple_of(k * chunk, chunk)
-        gi_ref[pl.ds(at, chunk), :] = block(at)
+        grad = row_block(at, chunk, x_ref, e_ref, yb_ref, ab_ref[pl.ds(at, chunk), :])
+        gis_ref[pl.ds(pl.multiple_of(at - own, chunk), chunk), :] = grad.astype(jnp.bfloat16)
         return 0
 
-    def sent_block(k, _):
-        at = pl.multiple_of(k * chunk, chunk)
-        gis_ref[pl.ds(pl.multiple_of(at - own, chunk), chunk), :] = block(at).astype(jnp.bfloat16)
-        return 0
-
-    lax.fori_loop(own // chunk, rows // chunk, sent_block, 0)
-    lax.fori_loop(0, own // chunk, own_block, 0)
-
-
-def row_grad(x, y, e, alpha, beta, own):
+    lax.fori_loop(own // chunk, x_ref.shape[0] // chunk, block, 0)
+
+
+def own_rows(x, y, e, alpha, beta, own):
     rows, cols = x.shape[0], y.shape[0]
     return pl.pallas_call(
-        functools.partial(row_grad_kernel, math.gcd(own, 512), own),
-        out_shape=(
-            jax.ShapeDtypeStruct((own, D), jnp.float32),
-            jax.ShapeDtypeStruct((rows - own, D), jnp.bfloat16),
-        ),
+        own_rows_kernel,
+        out_shape=(shape(own, D), shape(cols, 256, dtype=jnp.bfloat16)),
         in_specs=[VMEM] * 5,
         out_specs=(VMEM,) * 2,
-        scratch_shapes=[
-            pltpu.VMEM((rows, 128), jnp.float32),
-            pltpu.VMEM((cols, 128), jnp.float32),
-            pltpu.VMEM((cols, 256), jnp.bfloat16),
-        ],
+        scratch_shapes=[pltpu.VMEM((rows, 128), jnp.float32), pltpu.VMEM((cols, 128), jnp.float32)],
         compiler_params=pltpu.CompilerParams(vmem_limit_bytes=16 << 20),
-        cost_estimate=pl.CostEstimate(flops=4 * e.size * D, bytes_accessed=2 * e.size, transcendentals=0),
-        name="row_grad",
+        cost_estimate=pl.CostEstimate(flops=4 * own * cols * D, bytes_accessed=2 * own * cols, transcendentals=0),
+        name="own_rows",
     )(x, y, e, alpha.reshape(rows // 128, 128), beta.reshape(cols // 128, 128))
+
+
+def sent_rows(x, yb, e, alpha, own):
+    rows, cols = x.shape[0], yb.shape[0]
+    rest = rows - own
+    return pl.pallas_call(
+        functools.partial(sent_rows_kernel, math.gcd(own, 512), own),
+        out_shape=shape(rest, D, dtype=jnp.bfloat16),
+        in_specs=[VMEM] * 4,
+        out_specs=VMEM,
+        scratch_shapes=[pltpu.VMEM((rows, 128), jnp.float32)],
+        compiler_params=pltpu.CompilerParams(vmem_limit_bytes=16 << 20),
+        cost_estimate=pl.CostEstimate(flops=4 * rest * cols * D, bytes_accessed=2 * rest * cols, transcendentals=0),
+        name="sent_rows",
+    )(x, yb, e, alpha.reshape(rows // 128, 128))
 
 
 class Groups:
@@ -385,18 +444,15 @@
 
 def local(imu, camera, imu_mass, cam_mass):
     nrow, ncol = lax.axis_size("row"), lax.axis_size("col")
-    row, col = lax.axis_index("row"), lax.axis_index("col")
     groups = Groups(nrow, ncol)
     swap, across, along, core = groups.swap, groups.across, groups.along, groups.core
     na, nz = len(across), len(along)
     share_x, share_y = imu.shape[0], camera.shape[1]
 
-    x = jnp.concatenate([swap(imu, mask) for mask in across])
-    near = [swap(camera[0], mask) for mask in along]
-    y = jnp.concatenate(near + [swap(part, core) for part in near])
-
-    def pair(mass, place, share):
-        return jnp.concatenate([lax.dynamic_slice_in_dim(mass, (place ^ k) * share, share, 0) for k in range(2)])
+    mine = camera[0]
+    xs = [swap(imu, mask) for mask in across]
+    near = [swap(mine, mask) for mask in along]
+    far = [swap(part, core) for part in near]
 
     def row_exchange(local_value):
         return [reordered(swap(local_value, mask), s, na) for s, mask in enumerate(across)]
@@ -404,13 +460,16 @@
     def halves(value):
         return jnp.concatenate([value[value.shape[0] // 2:], value[:value.shape[0] // 2]])
 
-    sent = first_pass(y, x, None, pair(imu_mass, col, share_x))
+    x, xt, first = row_lse_early(xs, [near[0], far[0]])
+    y, sent = row_lse_late(x, near + far, first, imu_mass)
+    sent = sent.reshape(-1)
     got = [swap(sent, mask) for mask in across]
     size = na * share_x
     mass_a = jnp.concatenate([got[2 * a][size:] for a in range(na // 2)])
     u = jnp.log2(mass_a) - lse2([reordered(got[s][:size], s, na) for s in range(na)])
 
-    sent, e, shift = first_pass(x, y, u, pair(cam_mass, row, share_y))
+    sent, e, shift = column_lse(x, y, u, cam_mass)
+    sent, shift = sent.reshape(-1), shift.reshape(-1)
     size = 2 * nz * share_y
     lse, mass = sent[:size], sent[size:]
     lse = lse2([lse, halves(swap(lse, core))])
@@ -432,15 +491,17 @@
         part = part + halves(swap(part, core))
         beta = first_beta * (mass_b / sum(turned(swap(part, mask), z) for z, mask in enumerate(along)))
 
-    gc, gc_send = column_grad(x.T, y, e, alpha, beta, nz * share_y)
+    gc, gc_send = column_grad(xt, y, e, alpha, beta, nz * share_y)
+    gi, yb = own_rows(x, y, e, alpha, beta, share_x)
     gc = gc + swap(gc_send, core).astype(jnp.float32)
-    gi, gi_send = row_grad(x, y, e, alpha, beta, share_x)
-    for s in range(1, na):
-        gi = gi + swap(gi_send[(s - 1) * share_x:s * share_x], across[s]).astype(jnp.float32)
+    gc, yb = lax.optimization_barrier((gc, yb))
     grad_cam = gc[:share_y]
     for z in range(1, nz):
         part = gc[z * share_y:(z + 1) * share_y].astype(jnp.bfloat16)
         grad_cam = grad_cam + swap(part, along[z]).astype(jnp.float32)
+    gi_send = sent_rows(x, yb, e, alpha, share_x)
+    for s in range(1, na):
+        gi = gi + swap(gi_send[(s - 1) * share_x:s * share_x], across[s]).astype(jnp.float32)
     return gi, grad_cam[None]
 
 

time: 237 us -> 174 us (0.73)
  Pallas kernels: 143 us -> 79.4 us
    pallas_call x3 -> x5, Pallas kernels: 121 us -> 57.4 us  [the longest x1 30.4 us: column_lse(): pl.pallas_call(functools.partial(column_lse_kernel, width, chunk), out_sh...]
    unnamed x68 -> x70, local copies, waits for them, and re-layouts: 8.52 us -> 9.38 us
  transfers between devices with their start and end apart: 38 -> 38, of which waited for: 24 -> 21; matrix products, arithmetic and copies ran while one was open for 2% -> 2% of each run, Pallas kernels for 3% -> 5%
where the time goes in v6:
time: 174 us
  Pallas kernels  79.4 us (46%)
  starting transfers between devices  43 us (25%)
  waiting for transfers between devices  35.6 us (20%)
  local copies, waits for them, and re-layouts  11.6 us (7%)
  other arithmetic  2.57 us (1%)
    ppermute x38, starting transfers between devices, swap(): lax.ppermute(value, ('row', 'col'), [(i, i ^ mask) for i in range(self.co...  43 us
    ppermute x38, waiting for transfers between devices, swap(): lax.ppermute(value, ('row', 'col'), [(i, i ^ mask) for i in range(self.co...  35.6 us
    pallas_call x1, Pallas kernels, column_lse(): pl.pallas_call(functools.partial(column_lse_kernel, width, chunk), out_sh...  30.4 us
    pallas_call x4, Pallas kernels, weighted(): pl.pallas_call(functools.partial(kernel, width), out_shape=jax.ShapeDtype...  16.6 us
    pallas_call x1, Pallas kernels, row_lse_late(): pl.pallas_call(functools.partial(row_lse_kernel, width, False, 0, len(ys)...  13.7 us
    unnamed x70, local copies, waits for them, and re-layouts  9.38 us
    pallas_call x1, Pallas kernels, row_lse_early(): pl.pallas_call(functools.partial(row_lse_kernel, width, True, len(xs), le...  6.66 us
    pallas_call x1, Pallas kernels, column_grad(): pl.pallas_call(functools.partial(column_grad_kernel, width, own), out_sha...  5.41 us
  transfers between devices with their start and end apart: 38, of which 21 were waited for; matrix products, arithmetic and copies ran while one was open for 2% of the time, Pallas kernels for 5%

profile of v6, /device:TPU:0, one launch (start us, length us, event | category | flops | bytes accessed | tf_op | source)
XLA Modules:
  0.0 173.6 jit_solution(1955599398806642406)
XLA Ops:
  0.6 5.1 %collective-permute-start.6 = (bf16[512,128]{1,0:T(8,128)(2,1)}, bf16[512,128]{1,0:T(8,128)(2,1)S(1)}, u32[]{:S(2)}, u32[]{:S(2)}) collective-permute-start(bf16[512,128]{1,0:T(8,128)(2,1)} %bitcast.295), channel_id=1, source_target_pairs={{0,6},{1,7},{2,4},{3,5},{4,2},{5,3},{6,0},{7,1},{8,14},{9,15},{10,... | collective-permute-start | bytes 393224 | tf_op jit(solution)/shard_map/ppermute | solution.py:430
  6.4 1.6 collective-permute-start.1
  8.0 2.4 %collective-permute-done.6.refs_3_ = bf16[512,128]{1,0:T(8,128)(2,1)S(1)} collective-permute-done((bf16[512,128]{1,0:T(8,128)(2,1)}, bf16[512,128]{1,0:T(8,128)(2,1)S(1)}, u32[]{:S(2)}, u32[]{:S(2)}) %collective-permute-start.6) | collective-permute-done | bytes 131104 | tf_op jit(solution)/shard_map/ppermute | solution.py:430
  10.4 1.7 collective-permute-start
  12.1 4.9 %collective-permute-done.5.refs_2_ = bf16[512,128]{1,0:T(8,128)(2,1)S(1)} collective-permute-done((bf16[512,128]{1,0:T(8,128)(2,1)}, bf16[512,128]{1,0:T(8,128)(2,1)S(1)}, u32[]{:S(2)}, u32[]{:S(2)}) %collective-permute-start.5) | collective-permute-done | bytes 131104 | tf_op jit(solution)/shard_map/ppermute | solution.py:430
  17.0 2.4 %collective-permute-start.2 = (bf16[512,128]{1,0:T(8,128)(2,1)}, bf16[512,128]{1,0:T(8,128)(2,1)S(1)}, u32[]{:S(2)}, u32[]{:S(2)}) collective-permute-start(bf16[512,128]{1,0:T(8,128)(2,1)} %refs_0_.1), channel_id=1, source_target_pairs={{0,17},{1,16},{2,19},{3,18},{4,21},{5,20},{6,23},{7,22},{8,25},{9,... | collective-permute-start | bytes 393224 | tf_op jit(solution)/shard_map/ppermute | solution.py:430
  20.8 2.3 %collective-permute-done.2.refs_3_ = bf16[512,128]{1,0:T(8,128)(2,1)S(1)} collective-permute-done((bf16[512,128]{1,0:T(8,128)(2,1)}, bf16[512,128]{1,0:T(8,128)(2,1)S(1)}, u32[]{:S(2)}, u32[]{:S(2)}) %collective-permute-start.2) | collective-permute-done | bytes 131104 | tf_op jit(solution)/shard_map/ppermute | solution.py:430
  23.1 0.9 copy-done.2
  24.0 0.9 copy-done.3
  24.9 6.7 %row_lse_early.1 = (bf16[2048,128]{1,0:T(8,128)(2,1)S(1)}, bf16[128,2048]{1,0:T(8,128)(2,1)S(1)}, f32[1,2048]{1,0:T(1,128)S(1)}) custom-call(bf16[512,128]{1,0:T(8,128)(2,1)S(1)} %copy-done.2, bf16[512,128]{1,0:T(8,128)(2,1)S(1)} %collective-permute-done.refs_1_, bf16[512,128]{1,0:T(8,128)(2,1)S(1)} %collective-permute-done.1.refs_2_, ...), custom_call_target="tpu_custom_call" | custom-call | flops 536870912 | bytes 786432 | tf_op jit(solution)/shard_map/row_lse_early/pallas_call | solution.py:247
  31.6 13.7 %row_lse_late.1 = (bf16[4096,128]{1,0:T(8,128)(2,1)S(1)}, f32[1,3072]{1,0:T(1,128)S(1)}) custom-call(bf16[512,128]{1,0:T(8,128)(2,1)S(1)} %bitcast.300, bf16[512,128]{1,0:T(8,128)(2,1)S(1)} %collective-permute-done.4.refs_1_, bf16[512,128]{1,0:T(8,128)(2,1)S(1)} %collective-permute-done.5.refs_2_, bf16[512,128]{1,0:T(8,128)(2,1)S(1)} %collective-permute-done.6.refs_3_, ...), custom_call_target="tpu_custom_call" | custom-call | flops 1610612736 | bytes 1310720 | tf_op jit(solution)/shard_map/row_lse_late/pallas_call | solution.py:263
  46.2 3.4 %collective-permute-start.10 = (f32[3072]{0:T(1024)S(1)}, f32[3072]{0:T(1024)S(1)}, u32[]{:S(2)}, u32[]{:S(2)}) collective-permute-start(f32[3072]{0:T(1024)S(1)} %bitcast.294), channel_id=1, source_target_pairs={{0,16},{1,17},{2,18},{3,19},{4,20},{5,21},{6,22},{7,23},{8,24},{9,... | collective-permute-start | bytes 36872 | tf_op jit(solution)/shard_map/ppermute | solution.py:430
  50.0 1.3 collective-permute-done.10
  51.3 30.4 %column_lse.1 = (f32[1,5120]{1,0:T(1,128)S(1)}, bf16[2048,4096]{1,0:T(8,128)(2,1)S(1)}, f32[1,4096]{1,0:T(1,128)S(1)}) custom-call(bf16[2048,128]{1,0:T(8,128)(2,1)S(1)} %get-tuple-element.16.refs_8_.x_ref, bf16[4096,128]{1,0:T(8,128)(2,1)S(1)} %get-tuple-element.18.y_ref, f32[16,128]{1,0:T(8,128)S(1)} %add_subtract_fusion.u_ref, ...), custom_call_target="tpu_custom_call" | custom-call | flops 2147483648 | bytes 1572864 | tf_op jit(solution)/shard_map/column_lse/pallas_call | solution.py:278
  81.9 1.1 collective-permute-done.13
  83.2 2.2 %collective-permute-start.16 = (f32[5120]{0:T(1024)S(1)}, f32[5120]{0:T(1024)S(1)}, u32[]{:S(2)}, u32[]{:S(2)}) collective-permute-start(f32[5120]{0:T(1024)S(1)} %pad_maximum_fusion), channel_id=1, source_target_pairs={{0,6},{1,7},{2,4},{3,5},{4,2},{5,3},{6,0},{7,1},{8,14},{9,15},{10,... | collective-permute-start | bytes 61448 | tf_op jit(solution)/shard_map/ppermute | solution.py:430
  85.4 1.3 collective-permute-start.15
  87.0 3.1 %collective-permute-done.15 = f32[5120]{0:T(1024)S(1)} collective-permute-done((f32[5120]{0:T(1024)S(1)}, f32[5120]{0:T(1024)S(1)}, u32[]{:S(2)}, u32[]{:S(2)}) %collective-permute-start.15) | collective-permute-done | bytes 20512 | tf_op jit(solution)/shard_map/ppermute | solution.py:430
  90.8 5.1 %weighted_sum.4 = f32[1,2048]{1,0:T(1,128)S(1)} custom-call(bf16[2048,4096]{1,0:T(8,128)(2,1)S(1)} %get-tuple-element.20.e_ref, f32[1,4096]{1,0:T(1,128)S(1)} %multiply_exponential_fusion.1.w_ref), custom_call_target="tpu_custom_call" | custom-call | flops 16777216 | bytes 16777216 | tf_op jit(solution)/shard_map/weighted_sum/pallas_call | solution.py:215
  95.9 2.9 %collective-permute-start.19 = (f32[2048]{0:T(1024)S(1)}, f32[2048]{0:T(1024)S(1)}, u32[]{:S(2)}, u32[]{:S(2)}) collective-permute-start(f32[2048]{0:T(1024)S(1)} %bitcast.289), channel_id=1, source_target_pairs={{0,17},{1,16},{2,19},{3,18},{4,21},{5,20},{6,23},{7,22},{8,25},{9,... | collective-permute-start | bytes 24584 | tf_op jit(solution)/shard_map/ppermute | solution.py:430
  100.5 2.0 %collective-permute-done.18 = f32[2048]{0:T(1024)S(1)} collective-permute-done((f32[2048]{0:T(1024)S(1)}, f32[2048]{0:T(1024)S(1)}, u32[]{:S(2)}, u32[]{:S(2)}) %collective-permute-start.18) | collective-permute-done | bytes 8224 | tf_op jit(solution)/shard_map/ppermute | solution.py:430
  102.6 3.3 %weighted_sum.5 = f32[1,4096]{1,0:T(1,128)S(1)} custom-call(bf16[2048,4096]{1,0:T(8,128)(2,1)S(1)} %get-tuple-element.20.e_ref, f32[1,2048]{1,0:T(1,128)S(1)} %fusion.20.w_ref), custom_call_target="tpu_custom_call" | custom-call | flops 16777216 | bytes 16777216 | tf_op jit(solution)/shard_map/weighted_sum/pallas_call | solution.py:215
  106.0 1.2 collective-permute-done.20
  107.1 1.1 collective-permute-start.23
  108.3 3.3 %collective-permute-start.21 = (f32[4096]{0:T(1024)S(1)}, f32[4096]{0:T(1024)S(1)}, u32[]{:S(2)}, u32[]{:S(2)}) collective-permute-start(f32[4096]{0:T(1024)S(1)} %maximum_add_fusion.1), channel_id=1, source_target_pairs={{0,2},{1,3},{2,0},{3,1},{4,6},{5,7},{6,4},{7,5},{8,10},{9,11},{10,... | collective-permute-start | bytes 49160 | tf_op jit(solution)/shard_map/ppermute | solution.py:430
  111.5 1.1 collective-permute-done.23
  113.8 4.9 %weighted_sum.6 = f32[1,2048]{1,0:T(1,128)S(1)} custom-call(bf16[2048,4096]{1,0:T(8,128)(2,1)S(1)} %get-tuple-element.20.e_ref, f32[1,4096]{1,0:T(1,128)S(1)} %divide_multiply_fusion.w_ref), custom_call_target="tpu_custom_call" | custom-call | flops 16777216 | bytes 16777216 | tf_op jit(solution)/shard_map/weighted_sum/pallas_call | solution.py:215
  118.7 2.2 %collective-permute-start.26 = (f32[2048]{0:T(1024)S(1)}, f32[2048]{0:T(1024)S(1)}, u32[]{:S(2)}, u32[]{:S(2)}) collective-permute-start(f32[2048]{0:T(1024)S(1)} %bitcast.285), channel_id=1, source_target_pairs={{0,17},{1,16},{2,19},{3,18},{4,21},{5,20},{6,23},{7,22},{8,25},{9,... | collective-permute-start | bytes 24584 | tf_op jit(solution)/shard_map/ppermute | solution.py:430
  120.9 1.4 collective-permute-start.24
  122.3 1.1 collective-permute-done.26
  123.3 1.2 collective-permute-done.25
  124.6 3.3 %weighted_sum.7 = f32[1,4096]{1,0:T(1,128)S(1)} custom-call(bf16[2048,4096]{1,0:T(8,128)(2,1)S(1)} %get-tuple-element.20.e_ref, f32[1,2048]{1,0:T(1,128)S(1)} %fusion.19.w_ref.alpha_ref), custom_call_target="tpu_custom_call" | custom-call | flops 16777216 | bytes 16777216 | tf_op jit(solution)/shard_map/weighted_sum/pallas_call | solution.py:215
  127.9 1.2 collective-permute-done.27
  129.1 2.2 %collective-permute-start.30 = (f32[4096]{0:T(1024)S(1)}, f32[4096]{0:T(1024)S(1)}, u32[]{:S(2)}, u32[]{:S(2)}) collective-permute-start(f32[4096]{0:T(1024)S(1)} %maximum_add_fusion.3), channel_id=1, source_target_pairs={{0,6},{1,7},{2,4},{3,5},{4,2},{5,3},{6,0},{7,1},{8,14},{9,15},{10,... | collective-permute-start | bytes 49160 | tf_op jit(solution)/shard_map/ppermute | solution.py:430
  131.6 1.4 collective-permute-start.29
  133.0 0.9 collective-permute-start.28
  134.7 1.7 collective-permute-done.29
  136.9 5.8 %copy-done.1 = bf16[2048,4096]{1,0:T(8,128)(2,1)S(1)} copy-done((bf16[2048,4096]{1,0:T(8,128)(2,1)S(1)}, bf16[2048,4096]{1,0:T(8,128)(2,1)}, u32[]{:S(2)}) %copy-start.1) | copy-done | bytes 16777240
  142.7 5.4 %column_grad.1 = (f32[2048,128]{1,0:T(8,128)S(1)}, bf16[2048,128]{1,0:T(8,128)(2,1)S(1)}) custom-call(bf16[128,2048]{1,0:T(8,128)(2,1)S(1)} %get-tuple-element.24.xt_ref, bf16[4096,128]{1,0:T(8,128)(2,1)S(1)} %get-tuple-element.18.y_ref, bf16[2048,4096]{1,0:T(8,128)(2,1)S(1)} %copy-done.1, f32[1,2048]{1,0:T(1,128)S(1)} %fusion.19.w_ref.alpha_ref, ...), custom_call_target="tpu_custom_call" | custom-call | flops 4294967296 | bytes 16777216 | tf_op jit(solution)/shard_map/column_grad/pallas_call | solution.py:332
  148.3 1.9 %own_rows.1 = (f32[512,128]{1,0:T(8,128)S(1)}, bf16[4096,256]{1,0:T(8,128)(2,1)S(1)}) custom-call(bf16[2048,128]{1,0:T(8,128)(2,1)S(1)} %get-tuple-element.16.refs_8_.x_ref, bf16[4096,128]{1,0:T(8,128)(2,1)S(1)} %get-tuple-element.18.y_ref, bf16[2048,4096]{1,0:T(8,128)(2,1)S(1)} %copy-done.1, f32[16,128]{1,0:T(8,128)S(1)} %fusion.16.alpha_ref, ...), custom_call_target="tpu_custom_call" | custom-call | flops 1073741824 | bytes 4194304 | tf_op jit(solution)/shard_map/own_rows/pallas_call | solution.py:393
  150.4 1.3 slice-done.3
  151.7 4.6 %sent_rows.1 = bf16[1536,128]{1,0:T(8,128)(2,1)S(1)} custom-call(bf16[2048,128]{1,0:T(8,128)(2,1)S(1)} %get-tuple-element.16.refs_8_.x_ref, bf16[4096,256]{1,0:T(8,128)(2,1)S(1)} %get-tuple-element.28.yb_ref, bf16[2048,4096]{1,0:T(8,128)(2,1)S(1)} %bitcast.279, f32[16,128]{1,0:T(8,128)S(1)} %fusion.16.alpha_ref), custom_call_target="tpu_custom_call" | custom-call | flops 3221225472 | bytes 12582912 | tf_op jit(solution)/shard_map/sent_rows/pallas_call | solution.py:408
  156.5 1.0 collective-permute-start.35
  157.5 2.1 %collective-permute-start.37 = (bf16[512,128]{1,0:T(8,128)(2,1)S(1)}, bf16[512,128]{1,0:T(8,128)(2,1)S(1)}, u32[]{:S(2)}, u32[]{:S(2)}) collective-permute-start(bf16[512,128]{1,0:T(8,128)(2,1)S(1)} %get-tuple-element.33), channel_id=1, source_target_pairs={{0,6},{1,7},{2,4},{3,5},{4,2},{5,3},{6,0},{7,1},{8,14},{9,15},{10,... | collective-permute-start | bytes 393224 | tf_op jit(solution)/shard_map/ppermute | solution.py:430
  160.0 1.5 collective-permute-start.32
  161.5 1.7 collective-permute-start.34
  164.0 2.7 %collective-permute-done.37 = bf16[512,128]{1,0:T(8,128)(2,1)S(1)} collective-permute-done((bf16[512,128]{1,0:T(8,128)(2,1)S(1)}, bf16[512,128]{1,0:T(8,128)(2,1)S(1)}, u32[]{:S(2)}, u32[]{:S(2)}) %collective-permute-start.37) | collective-permute-done | bytes 131104 | tf_op jit(solution)/shard_map/ppermute | solution.py:430
  166.8 5.3 %collective-permute-done.36 = bf16[512,128]{1,0:T(8,128)(2,1)S(1)} collective-permute-done((bf16[512,128]{1,0:T(8,128)(2,1)S(1)}, bf16[512,128]{1,0:T(8,128)(2,1)S(1)}, u32[]{:S(2)}, u32[]{:S(2)}) %collective-permute-start.36) | collective-permute-done | bytes 131104 | tf_op jit(solution)/shard_map/ppermute | solution.py:430
  (177 shorter events, 12.0 us)
Async XLA Ops:
  0.6 9.8 %collective-permute-start.6 = (bf16[512,128]{1,0:T(8,128)(2,1)}, bf16[512,128]{1,0:T(8,128)(2,1)S(1)}, u32[]{:S(2)}, u32[]{:S(2)}) collective-permute-start(bf16[512,128]{1,0:T(8,128)(2,1)} %bitcast.295), channel_id=1, source_target_pairs={{0,6},{1,7},{2,4},{3,5},{4,2},{5,3},{6,0},{7,1},{8,14},{9,15},{10,... | collective-permute-start | bytes 393224 | tf_op jit(solution)/shard_map/ppermute | solution.py:430
  5.7 11.3 %collective-permute-start.5 = (bf16[512,128]{1,0:T(8,128)(2,1)}, bf16[512,128]{1,0:T(8,128)(2,1)S(1)}, u32[]{:S(2)}, u32[]{:S(2)}) collective-permute-start(bf16[512,128]{1,0:T(8,128)(2,1)} %bitcast.296), channel_id=1, source_target_pairs={{0,4},{1,5},{2,6},{3,7},{4,0},{5,1},{6,2},{7,3},{8,12},{9,13},{10,... | collective-permute-start | bytes 393224 | tf_op jit(solution)/shard_map/ppermute | solution.py:430
  5.7 13.7 %collective-permute-start.4 = (bf16[512,128]{1,0:T(8,128)(2,1)}, bf16[512,128]{1,0:T(8,128)(2,1)S(1)}, u32[]{:S(2)}, u32[]{:S(2)}) collective-permute-start(bf16[512,128]{1,0:T(8,128)(2,1)} %bitcast.297), channel_id=1, source_target_pairs={{0,2},{1,3},{2,0},{3,1},{4,6},{5,7},{6,4},{7,5},{8,10},{9,11},{10,... | collective-permute-start | bytes 393224 | tf_op jit(solution)/shard_map/ppermute | solution.py:430
  6.4 13.1 %collective-permute-start.3 = (bf16[512,128]{1,0:T(8,128)(2,1)}, bf16[512,128]{1,0:T(8,128)(2,1)S(1)}, u32[]{:S(2)}, u32[]{:S(2)}) collective-permute-start(bf16[512,128]{1,0:T(8,128)(2,1)} %bitcast.298), channel_id=1, source_target_pairs={{0,8},{1,9},{2,10},{3,11},{4,12},{5,13},{6,14},{7,15},{8,0},{9,1},... | collective-permute-start | bytes 393224 | tf_op jit(solution)/shard_map/ppermute | solution.py:430
  6.4 13.6 %collective-permute-start.1 = (bf16[512,128]{1,0:T(8,128)(2,1)}, bf16[512,128]{1,0:T(8,128)(2,1)S(1)}, u32[]{:S(2)}, u32[]{:S(2)}) collective-permute-start(bf16[512,128]{1,0:T(8,128)(2,1)} %refs_0_.1), channel_id=1, source_target_pairs={{0,16},{1,17},{2,18},{3,19},{4,20},{5,21},{6,22},{7,23},{8,24},{9,... | collective-permute-start | bytes 393224 | tf_op jit(solution)/shard_map/ppermute | solution.py:430
  10.4 10.4 %collective-permute-start = (bf16[512,128]{1,0:T(8,128)(2,1)}, bf16[512,128]{1,0:T(8,128)(2,1)S(1)}, u32[]{:S(2)}, u32[]{:S(2)}) collective-permute-start(bf16[512,128]{1,0:T(8,128)(2,1)} %refs_0_.1), channel_id=1, source_target_pairs={{0,1},{1,0},{2,3},{3,2},{4,5},{5,4},{6,7},{7,6},{8,9},{9,8},{10,11... | collective-permute-start | bytes 393224 | tf_op jit(solution)/shard_map/ppermute | solution.py:430
  17.0 6.1 %collective-permute-start.2 = (bf16[512,128]{1,0:T(8,128)(2,1)}, bf16[512,128]{1,0:T(8,128)(2,1)S(1)}, u32[]{:S(2)}, u32[]{:S(2)}) collective-permute-start(bf16[512,128]{1,0:T(8,128)(2,1)} %refs_0_.1), channel_id=1, source_target_pairs={{0,17},{1,16},{2,19},{3,18},{4,21},{5,20},{6,23},{7,22},{8,25},{9,... | collective-permute-start | bytes 393224 | tf_op jit(solution)/shard_map/ppermute | solution.py:430
  19.5 12.1 %collective-permute-start.9 = (bf16[512,128]{1,0:T(8,128)(2,1)S(1)}, bf16[512,128]{1,0:T(8,128)(2,1)S(1)}, u32[]{:S(2)}, u32[]{:S(2)}) collective-permute-start(bf16[512,128]{1,0:T(8,128)(2,1)S(1)} %collective-permute-done.6.refs_3_), channel_id=1, source_target_pairs={{0,8},{1,9},{2,10},{3,11},{4,12},{5,13},{6,14},{7,15},{8,0},{9,1},... | collective-permute-start | bytes 393224 | tf_op jit(solution)/shard_map/ppermute | solution.py:430
  19.5 12.1 %collective-permute-start.8 = (bf16[512,128]{1,0:T(8,128)(2,1)S(1)}, bf16[512,128]{1,0:T(8,128)(2,1)S(1)}, u32[]{:S(2)}, u32[]{:S(2)}) collective-permute-start(bf16[512,128]{1,0:T(8,128)(2,1)S(1)} %collective-permute-done.5.refs_2_), channel_id=1, source_target_pairs={{0,8},{1,9},{2,10},{3,11},{4,12},{5,13},{6,14},{7,15},{8,0},{9,1},... | collective-permute-start | bytes 393224 | tf_op jit(solution)/shard_map/ppermute | solution.py:430
  20.0 11.6 %collective-permute-start.7 = (bf16[512,128]{1,0:T(8,128)(2,1)S(1)}, bf16[512,128]{1,0:T(8,128)(2,1)S(1)}, u32[]{:S(2)}, u32[]{:S(2)}) collective-permute-start(bf16[512,128]{1,0:T(8,128)(2,1)S(1)} %collective-permute-done.4.refs_1_), channel_id=1, source_target_pairs={{0,8},{1,9},{2,10},{3,11},{4,12},{5,13},{6,14},{7,15},{8,0},{9,1},... | collective-permute-start | bytes 393224 | tf_op jit(solution)/shard_map/ppermute | solution.py:430
  23.1 0.9 copy-start.2
  24.0 0.9 copy-start.3
  45.3 4.7 %collective-permute-start.12 = (f32[3072]{0:T(1024)S(1)}, f32[3072]{0:T(1024)S(1)}, u32[]{:S(2)}, u32[]{:S(2)}) collective-permute-start(f32[3072]{0:T(1024)S(1)} %bitcast.292), channel_id=1, source_target_pairs={{0,17},{1,16},{2,19},{3,18},{4,21},{5,20},{6,23},{7,22},{8,25},{9,... | collective-permute-start | bytes 36872 | tf_op jit(solution)/shard_map/ppermute | solution.py:430
  46.2 5.1 %collective-permute-start.11 = (f32[3072]{0:T(1024)S(1)}, f32[3072]{0:T(1024)S(1)}, u32[]{:S(2)}, u32[]{:S(2)}) collective-permute-start(f32[3072]{0:T(1024)S(1)} %bitcast.293), channel_id=1, source_target_pairs={{0,1},{1,0},{2,3},{3,2},{4,5},{5,4},{6,7},{7,6},{8,9},{9,8},{10,11... | collective-permute-start | bytes 36872 | tf_op jit(solution)/shard_map/ppermute | solution.py:430
  46.2 5.1 %collective-permute-start.10 = (f32[3072]{0:T(1024)S(1)}, f32[3072]{0:T(1024)S(1)}, u32[]{:S(2)}, u32[]{:S(2)}) collective-permute-start(f32[3072]{0:T(1024)S(1)} %bitcast.294), channel_id=1, source_target_pairs={{0,16},{1,17},{2,18},{3,19},{4,20},{5,21},{6,22},{7,23},{8,24},{9,... | collective-permute-start | bytes 36872 | tf_op jit(solution)/shard_map/ppermute | solution.py:430
  81.8 42.8 %copy-start = (bf16[2048,4096]{1,0:T(8,128)(2,1)}, bf16[2048,4096]{1,0:T(8,128)(2,1)S(1)}, u32[]{:S(2)}) copy-start(bf16[2048,4096]{1,0:T(8,128)(2,1)S(1)} %get-tuple-element.20.e_ref) | copy-start | bytes 50331652
  81.8 1.2 collective-permute-start.13
  83.1 3.8 %collective-permute-start.14 = (f32[5120]{0:T(1024)S(1)}, f32[5120]{0:T(1024)S(1)}, u32[]{:S(2)}, u32[]{:S(2)}) collective-permute-start(f32[5120]{0:T(1024)S(1)} %pad_maximum_fusion), channel_id=1, source_target_pairs={{0,2},{1,3},{2,0},{3,1},{4,6},{5,7},{6,4},{7,5},{8,10},{9,11},{10,... | collective-permute-start | bytes 61448 | tf_op jit(solution)/shard_map/ppermute | solution.py:430
  83.2 6.9 %collective-permute-start.16 = (f32[5120]{0:T(1024)S(1)}, f32[5120]{0:T(1024)S(1)}, u32[]{:S(2)}, u32[]{:S(2)}) collective-permute-start(f32[5120]{0:T(1024)S(1)} %pad_maximum_fusion), channel_id=1, source_target_pairs={{0,6},{1,7},{2,4},{3,5},{4,2},{5,3},{6,0},{7,1},{8,14},{9,15},{10,... | collective-permute-start | bytes 61448 | tf_op jit(solution)/shard_map/ppermute | solution.py:430
  85.4 4.7 %collective-permute-start.15 = (f32[5120]{0:T(1024)S(1)}, f32[5120]{0:T(1024)S(1)}, u32[]{:S(2)}, u32[]{:S(2)}) collective-permute-start(f32[5120]{0:T(1024)S(1)} %pad_maximum_fusion), channel_id=1, source_target_pairs={{0,4},{1,5},{2,6},{3,7},{4,0},{5,1},{6,2},{7,3},{8,12},{9,13},{10,... | collective-permute-start | bytes 61448 | tf_op jit(solution)/shard_map/ppermute | solution.py:430
  95.9 4.6 %collective-permute-start.19 = (f32[2048]{0:T(1024)S(1)}, f32[2048]{0:T(1024)S(1)}, u32[]{:S(2)}, u32[]{:S(2)}) collective-permute-start(f32[2048]{0:T(1024)S(1)} %bitcast.289), channel_id=1, source_target_pairs={{0,17},{1,16},{2,19},{3,18},{4,21},{5,20},{6,23},{7,22},{8,25},{9,... | collective-permute-start | bytes 24584 | tf_op jit(solution)/shard_map/ppermute | solution.py:430
  98.9 3.7 %collective-permute-start.18 = (f32[2048]{0:T(1024)S(1)}, f32[2048]{0:T(1024)S(1)}, u32[]{:S(2)}, u32[]{:S(2)}) collective-permute-start(f32[2048]{0:T(1024)S(1)} %bitcast.290), channel_id=1, source_target_pairs={{0,16},{1,17},{2,18},{3,19},{4,20},{5,21},{6,22},{7,23},{8,24},{9,... | collective-permute-start | bytes 24584 | tf_op jit(solution)/shard_map/ppermute | solution.py:430
  98.9 3.7 %collective-permute-start.17 = (f32[2048]{0:T(1024)S(1)}, f32[2048]{0:T(1024)S(1)}, u32[]{:S(2)}, u32[]{:S(2)}) collective-permute-start(f32[2048]{0:T(1024)S(1)} %bitcast.291), channel_id=1, source_target_pairs={{0,1},{1,0},{2,3},{3,2},{4,5},{5,4},{6,7},{7,6},{8,9},{9,8},{10,11... | collective-permute-start | bytes 24584 | tf_op jit(solution)/shard_map/ppermute | solution.py:430
  105.9 1.2 collective-permute-start.20
  107.1 5.5 %collective-permute-start.23 = (f32[4096]{0:T(1024)S(1)}, f32[4096]{0:T(1024)S(1)}, u32[]{:S(2)}, u32[]{:S(2)}) collective-permute-start(f32[4096]{0:T(1024)S(1)} %maximum_add_fusion.1), channel_id=1, source_target_pairs={{0,6},{1,7},{2,4},{3,5},{4,2},{5,3},{6,0},{7,1},{8,14},{9,15},{10,... | collective-permute-start | bytes 49160 | tf_op jit(solution)/shard_map/ppermute | solution.py:430
  108.2 5.2 %collective-permute-start.22 = (f32[4096]{0:T(1024)S(1)}, f32[4096]{0:T(1024)S(1)}, u32[]{:S(2)}, u32[]{:S(2)}) collective-permute-start(f32[4096]{0:T(1024)S(1)} %maximum_add_fusion.1), channel_id=1, source_target_pairs={{0,4},{1,5},{2,6},{3,7},{4,0},{5,1},{6,2},{7,3},{8,12},{9,13},{10,... | collective-permute-start | bytes 49160 | tf_op jit(solution)/shard_map/ppermute | solution.py:430
  108.3 5.0 %collective-permute-start.21 = (f32[4096]{0:T(1024)S(1)}, f32[4096]{0:T(1024)S(1)}, u32[]{:S(2)}, u32[]{:S(2)}) collective-permute-start(f32[4096]{0:T(1024)S(1)} %maximum_add_fusion.1), channel_id=1, source_target_pairs={{0,2},{1,3},{2,0},{3,1},{4,6},{5,7},{6,4},{7,5},{8,10},{9,11},{10,... | collective-permute-start | bytes 49160 | tf_op jit(solution)/shard_map/ppermute | solution.py:430
  118.7 4.6 %collective-permute-start.26 = (f32[2048]{0:T(1024)S(1)}, f32[2048]{0:T(1024)S(1)}, u32[]{:S(2)}, u32[]{:S(2)}) collective-permute-start(f32[2048]{0:T(1024)S(1)} %bitcast.285), channel_id=1, source_target_pairs={{0,17},{1,16},{2,19},{3,18},{4,21},{5,20},{6,23},{7,22},{8,25},{9,... | collective-permute-start | bytes 24584 | tf_op jit(solution)/shard_map/ppermute | solution.py:430
  120.9 3.7 %collective-permute-start.25 = (f32[2048]{0:T(1024)S(1)}, f32[2048]{0:T(1024)S(1)}, u32[]{:S(2)}, u32[]{:S(2)}) collective-permute-start(f32[2048]{0:T(1024)S(1)} %bitcast.286), channel_id=1, source_target_pairs={{0,16},{1,17},{2,18},{3,19},{4,20},{5,21},{6,22},{7,23},{8,24},{9,... | collective-permute-start | bytes 24584 | tf_op jit(solution)/shard_map/ppermute | solution.py:430
  120.9 3.7 %collective-permute-start.24 = (f32[2048]{0:T(1024)S(1)}, f32[2048]{0:T(1024)S(1)}, u32[]{:S(2)}, u32[]{:S(2)}) collective-permute-start(f32[2048]{0:T(1024)S(1)} %bitcast.287), channel_id=1, source_target_pairs={{0,1},{1,0},{2,3},{3,2},{4,5},{5,4},{6,7},{7,6},{8,9},{9,8},{10,11... | collective-permute-start | bytes 24584 | tf_op jit(solution)/shard_map/ppermute | solution.py:430
  127.9 1.2 collective-permute-start.27
  129.1 5.6 %collective-permute-start.30 = (f32[4096]{0:T(1024)S(1)}, f32[4096]{0:T(1024)S(1)}, u32[]{:S(2)}, u32[]{:S(2)}) collective-permute-start(f32[4096]{0:T(1024)S(1)} %maximum_add_fusion.3), channel_id=1, source_target_pairs={{0,6},{1,7},{2,4},{3,5},{4,2},{5,3},{6,0},{7,1},{8,14},{9,15},{10,... | collective-permute-start | bytes 49160 | tf_op jit(solution)/shard_map/ppermute | solution.py:430
  131.6 4.8 %collective-permute-start.29 = (f32[4096]{0:T(1024)S(1)}, f32[4096]{0:T(1024)S(1)}, u32[]{:S(2)}, u32[]{:S(2)}) collective-permute-start(f32[4096]{0:T(1024)S(1)} %maximum_add_fusion.3), channel_id=1, source_target_pairs={{0,4},{1,5},{2,6},{3,7},{4,0},{5,1},{6,2},{7,3},{8,12},{9,13},{10,... | collective-permute-start | bytes 49160 | tf_op jit(solution)/shard_map/ppermute | solution.py:430
  133.0 3.7 %collective-permute-start.28 = (f32[4096]{0:T(1024)S(1)}, f32[4096]{0:T(1024)S(1)}, u32[]{:S(2)}, u32[]{:S(2)}) collective-permute-start(f32[4096]{0:T(1024)S(1)} %maximum_add_fusion.3), channel_id=1, source_target_pairs={{0,2},{1,3},{2,0},{3,1},{4,6},{5,7},{6,4},{7,5},{8,10},{9,11},{10,... | collective-permute-start | bytes 49160 | tf_op jit(solution)/shard_map/ppermute | solution.py:430
  136.9 5.8 %copy-start.1 = (bf16[2048,4096]{1,0:T(8,128)(2,1)S(1)}, bf16[2048,4096]{1,0:T(8,128)(2,1)}, u32[]{:S(2)}) copy-start(bf16[2048,4096]{1,0:T(8,128)(2,1)} %copy-done) | copy-start | bytes 50331652
  142.7 7.6 %slice-start = ((s8[16777216]{0:T(1024)(128)(4,1)}), s8[4194304]{0:T(1024)(128)(4,1)S(1)}, s32[]{:S(2)}) async-start(s8[16777216]{0:T(1024)(128)(4,1)} %bitcast.278), calls=%async_computation | async-start | bytes 8388608
  142.7 7.6 %slice-start.1 = ((s8[16777216]{0:T(1024)(128)(4,1)}), s8[4194304]{0:T(1024)(128)(4,1)S(1)}, s32[]{:S(2)}) async-start(s8[16777216]{0:T(1024)(128)(4,1)} %bitcast.278), calls=%async_computation.1 | async-start | bytes 8388608
  148.1 2.1 %collective-permute-start.31 = (bf16[2048,128]{1,0:T(8,128)(2,1)S(1)}, bf16[2048,128]{1,0:T(8,128)(2,1)S(1)}, u32[]{:S(2)}, u32[]{:S(2)}) collective-permute-start(bf16[2048,128]{1,0:T(8,128)(2,1)S(1)} %get-tuple-element.26), channel_id=1, source_target_pairs={{0,8},{1,9},{2,10},{3,11},{4,12},{5,13},{6,14},{7,15},{8,0},{9,1},... | collective-permute-start | bytes 1572872 | tf_op jit(solution)/shard_map/ppermute | solution.py:430
  148.2 2.2 %slice-start.2 = ((s8[16777216]{0:T(1024)(128)(4,1)}), s8[4194304]{0:T(1024)(128)(4,1)S(1)}, s32[]{:S(2)}) async-start(s8[16777216]{0:T(1024)(128)(4,1)} %bitcast.278), calls=%async_computation.2 | async-start | bytes 8388608
  148.3 3.5 %slice-start.3 = ((s8[16777216]{0:T(1024)(128)(4,1)}), s8[4194304]{0:T(1024)(128)(4,1)S(1)}, s32[]{:S(2)}) async-start(s8[16777216]{0:T(1024)(128)(4,1)} %bitcast.278), calls=%async_computation.3 | async-start | bytes 8388608
  156.5 6.7 %collective-permute-start.35 = (bf16[512,128]{1,0:T(8,128)(2,1)S(1)}, bf16[512,128]{1,0:T(8,128)(2,1)S(1)}, u32[]{:S(2)}, u32[]{:S(2)}) collective-permute-start(bf16[512,128]{1,0:T(8,128)(2,1)S(1)} %get-tuple-element.32), channel_id=1, source_target_pairs={{0,2},{1,3},{2,0},{3,1},{4,6},{5,7},{6,4},{7,5},{8,10},{9,11},{10,... | collective-permute-start | bytes 393224 | tf_op jit(solution)/shard_map/ppermute | solution.py:430
  157.5 9.3 %collective-permute-start.37 = (bf16[512,128]{1,0:T(8,128)(2,1)S(1)}, bf16[512,128]{1,0:T(8,128)(2,1)S(1)}, u32[]{:S(2)}, u32[]{:S(2)}) collective-permute-start(bf16[512,128]{1,0:T(8,128)(2,1)S(1)} %get-tuple-element.33), channel_id=1, source_target_pairs={{0,6},{1,7},{2,4},{3,5},{4,2},{5,3},{6,0},{7,1},{8,14},{9,15},{10,... | collective-permute-start | bytes 393224 | tf_op jit(solution)/shard_map/ppermute | solution.py:430
  159.6 12.4 %collective-permute-start.36 = (bf16[512,128]{1,0:T(8,128)(2,1)S(1)}, bf16[512,128]{1,0:T(8,128)(2,1)S(1)}, u32[]{:S(2)}, u32[]{:S(2)}) collective-permute-start(bf16[512,128]{1,0:T(8,128)(2,1)S(1)} %get-tuple-element.34), channel_id=1, source_target_pairs={{0,4},{1,5},{2,6},{3,7},{4,0},{5,1},{6,2},{7,3},{8,12},{9,13},{10,... | collective-permute-start | bytes 393224 | tf_op jit(solution)/shard_map/ppermute | solution.py:430
  160.0 12.8 %collective-permute-start.32 = (bf16[512,128]{1,0:T(8,128)(2,1)S(1)}, bf16[512,128]{1,0:T(8,128)(2,1)S(1)}, u32[]{:S(2)}, u32[]{:S(2)}) collective-permute-start(bf16[512,128]{1,0:T(8,128)(2,1)S(1)} %get-tuple-element.35), channel_id=1, source_target_pairs={{0,1},{1,0},{2,3},{3,2},{4,5},{5,4},{6,7},{7,6},{8,9},{9,8},{10,11... | collective-permute-start | bytes 393224 | tf_op jit(solution)/shard_map/ppermute | solution.py:430
  161.5 11.3 %collective-permute-start.34 = (bf16[512,128]{1,0:T(8,128)(2,1)S(1)}, bf16[512,128]{1,0:T(8,128)(2,1)S(1)}, u32[]{:S(2)}, u32[]{:S(2)}) collective-permute-start(bf16[512,128]{1,0:T(8,128)(2,1)S(1)} %get-tuple-element.36), channel_id=1, source_target_pairs={{0,17},{1,16},{2,19},{3,18},{4,21},{5,20},{6,23},{7,22},{8,25},{9,... | collective-permute-start | bytes 393224 | tf_op jit(solution)/shard_map/ppermute | solution.py:430
  163.2 9.6 %collective-permute-start.33 = (bf16[512,128]{1,0:T(8,128)(2,1)S(1)}, bf16[512,128]{1,0:T(8,128)(2,1)S(1)}, u32[]{:S(2)}, u32[]{:S(2)}) collective-permute-start(bf16[512,128]{1,0:T(8,128)(2,1)S(1)} %get-tuple-element.37), channel_id=1, source_target_pairs={{0,16},{1,17},{2,18},{3,19},{4,20},{5,21},{6,22},{7,23},{8,24},{9,... | collective-permute-start | bytes 393224 | tf_op jit(solution)/shard_map/ppermute | solution.py:430

commit v7 on v6

--- a/solution.py
+++ b/solution.py
@@ -16,14 +16,28 @@
 NT = (((1,), (1,)), ((), ()))
 VMEM = pl.BlockSpec(memory_space=pltpu.VMEM)
 GROUP = 32
-ROOM = 8 << 20
-
-
-def spread(s_ref, sb_ref):
-    chunks = s_ref.shape[0]
+
+
+def spread(value, s_ref, sb_ref):
+    chunks = value.shape[1] // 128
+    for k in range(chunks):
+        s_ref[k:k + 1, :] = value[:, k * 128:(k + 1) * 128]
     turned = jnp.transpose(s_ref[...])
     for k in range(chunks):
         sb_ref[k * 128:(k + 1) * 128, :] = jnp.broadcast_to(turned[:, k:k + 1], (128, 128))
+
+
+def ordered(refs, size, parts):
+    share = size // parts
+    return [
+        jnp.concatenate([ref[:, (k ^ s) * share:((k ^ s) + 1) * share] for k in range(parts)], axis=1)
+        for s, ref in enumerate(refs)
+    ]
+
+
+def lse2(parts):
+    top = functools.reduce(jnp.maximum, parts)
+    return top + jnp.log2(sum(jnp.exp2(part - top) for part in parts))
 
 
 def pipelined(places, chunk, width, a_ref, b_ref, d_ref, tile, finish):
@@ -124,11 +138,11 @@
         running_max(places, chunk, min(width, 256), a_ref, b_ref, sb_ref, o_ref, e_ref, shift_ref)
 
 
-def put_pair(o_ref, at, mass_ref, axis):
-    share = mass_ref.shape[1]
+def put_pair(o_ref, at, share, mass_ref, axis):
     place = lax.axis_index(axis)
     for k in range(2):
-        o_ref[:, at + k * share:at + (k + 1) * share] = mass_ref[pl.ds(place ^ k, 1), :]
+        start = pl.multiple_of((place ^ k) * share, share)
+        o_ref[:, at + k * share:at + (k + 1) * share] = mass_ref[:, pl.ds(start, share)]
 
 
 def row_lse_kernel(width, early, nx, ny, *refs):
@@ -161,15 +175,29 @@
         one, two = first_ref[...], sum_ref[...]
         top = jnp.maximum(one, two)
         o_ref[:, :rows] = top + jnp.log2(jnp.exp2(one - top) + jnp.exp2(two - top))
-        put_pair(o_ref, rows, mass_ref, "col")
-
-
-def column_lse_kernel(width, chunk, x_ref, y_ref, u_ref, mass_ref, o_ref, e_ref, shift_ref,
-                      sb_ref, d_ref, top_ref, room_ref):
-    spread(u_ref, sb_ref)
-    put_pair(o_ref, y_ref.shape[0], mass_ref, "row")
-    places = list(range(0, x_ref.shape[0], chunk))
+        put_pair(o_ref, rows, (o_ref.shape[1] - rows) // 2, mass_ref, "col")
+
+
+def column_lse_kernel(width, chunk, na, x_ref, y_ref, mass_ref, *refs):
+    got, (o_ref, e_ref, shift_ref, a_ref, s_ref, sb_ref, d_ref, top_ref) = refs[:na], refs[na:]
+    rows, cols = x_ref.shape[0], y_ref.shape[0]
+    share = rows // na
+    for k in range(na):
+        at = rows + (k % 2) * share
+        a_ref[:, k * share:(k + 1) * share] = got[k - k % 2][:, at:at + share]
+    u = jnp.log2(a_ref[...]) - lse2(ordered(got, rows, na))
+    spread(u, s_ref, sb_ref)
+    put_pair(o_ref, cols, (o_ref.shape[1] - cols) // 2, mass_ref, "row")
+    places = list(range(0, rows, chunk))
     lse_pass(places, chunk, width, x_ref, y_ref, sb_ref, d_ref, top_ref, o_ref, e_ref, shift_ref)
+
+
+def pair_kernel(cols, combine, one_ref, two_ref, o_ref):
+    half = cols // 2
+    two = jnp.concatenate([two_ref[:, half:cols], two_ref[:, :half]], axis=1)
+    o_ref[:, :cols] = combine([one_ref[:, :cols], two])
+    if o_ref.shape[1] > cols:
+        o_ref[:, cols:] = one_ref[:, cols:]
 
 
 def split3(value):
@@ -179,17 +207,15 @@
     return high, mid, (rest - mid.astype(jnp.float32)).astype(jnp.bfloat16)
 
 
-def stacked(w_ref):
-    high, mid, low = [part.astype(jnp.float32) for part in split3(w_ref[...])]
-    shape = (16, w_ref.shape[1])
-    place = lax.broadcasted_iota(jnp.int32, shape, 0)
+def stacked(value):
+    high, mid, low = [part.astype(jnp.float32) for part in split3(value)]
+    dims = (16, value.shape[1])
+    place = lax.broadcasted_iota(jnp.int32, dims, 0)
     parts = jnp.where(place == 0, high, jnp.where(place == 1, mid, jnp.where(place == 2, low, 0.0)))
     return parts.astype(jnp.bfloat16)
 
 
-def row_kernel(width, e_ref, w_ref, o_ref, w16_ref):
-    w16_ref[...] = stacked(w_ref)
-
+def row_sums(width, e_ref, w16_ref, o_ref):
     def block(k, _):
         at = pl.multiple_of(k * width, width)
         got = lax.dot_general(w16_ref[...], e_ref[pl.ds(at, width), :], NT, preferred_element_type=jnp.float32)
@@ -199,30 +225,54 @@
     lax.fori_loop(0, e_ref.shape[0] // width, block, 0)
 
 
-def col_kernel(width, e_ref, w_ref, o_ref, w16_ref):
-    w16_ref[...] = stacked(w_ref)
+def first_row_kernel(width, nz, e_ref, shift_ref, *refs):
+    got, (o_ref, beta_ref, b_ref, w16_ref) = refs[:nz], refs[nz:]
+    cols = e_ref.shape[1]
+    share = cols // (2 * nz)
+    for k in range(2 * nz):
+        at = cols + (k // nz) * share
+        b_ref[:, k * share:(k + 1) * share] = got[k % nz][:, at:at + share]
+    beta_ref[...] = jnp.exp2(jnp.log2(b_ref[...]) - lse2(ordered(got, cols, 2 * nz)) + shift_ref[...])
+    w16_ref[...] = stacked(beta_ref[...])
+    row_sums(width, e_ref, w16_ref, o_ref)
+
+
+def new_beta(first_ref, b_ref, got):
+    return first_ref[...] * (b_ref[...] / sum(ordered(got, b_ref.shape[1], 2 * len(got))))
+
+
+def row_kernel(width, nz, e_ref, first_ref, b_ref, *refs):
+    got, (o_ref, w16_ref) = refs[:nz], refs[nz:]
+    w16_ref[...] = stacked(new_beta(first_ref, b_ref, got))
+    row_sums(width, e_ref, w16_ref, o_ref)
+
+
+def column_kernel(width, na, e_ref, a_ref, first_ref, *refs):
+    got, (o_ref, alpha_ref, w16_ref) = refs[:na], refs[na:]
+    alpha_ref[...] = a_ref[...] / sum(ordered(got, a_ref.shape[1], na))
+    w16_ref[...] = stacked(alpha_ref[...])
 
     def block(k, _):
         at = pl.multiple_of(k * width, width)
         got = jnp.dot(w16_ref[...], e_ref[:, pl.ds(at, width)], preferred_element_type=jnp.float32)
-        o_ref[:, pl.ds(at, width)] = jnp.sum(got, axis=0, keepdims=True)
+        o_ref[:, pl.ds(at, width)] = first_ref[:, pl.ds(at, width)] * jnp.sum(got, axis=0, keepdims=True)
         return 0
 
     lax.fori_loop(0, e_ref.shape[1] // width, block, 0)
 
 
-def weighted(kernel, e, w, lanes, width=512):
-    out = pl.pallas_call(
-        functools.partial(kernel, width),
-        out_shape=jax.ShapeDtypeStruct((1, lanes), jnp.float32),
-        in_specs=[VMEM] * 2,
-        out_specs=VMEM,
-        scratch_shapes=[pltpu.VMEM((16, w.shape[0]), jnp.bfloat16)],
+def weighted(kernel, outs, e, rows, got, width=512):
+    size = e.shape[0] if kernel is column_kernel else e.shape[1]
+    return pl.pallas_call(
+        functools.partial(kernel, width, len(got)),
+        out_shape=[shape(1, n) for n in outs],
+        in_specs=[VMEM] * (1 + len(rows) + len(got)),
+        out_specs=[VMEM] * len(outs),
+        scratch_shapes=[pltpu.VMEM((16, size), jnp.bfloat16)],
         compiler_params=pltpu.CompilerParams(vmem_limit_bytes=16 << 20),
         cost_estimate=pl.CostEstimate(flops=2 * e.size, bytes_accessed=2 * e.size, transcendentals=0),
         name="weighted_sum",
-    )(e, w.reshape(1, w.shape[0]))
-    return out.reshape(lanes)
+    )(e, *rows, *[part.reshape(1, -1) for part in got])
 
 
 def pass_cost(depth, lanes):
@@ -269,22 +319,34 @@
         compiler_params=pltpu.CompilerParams(vmem_limit_bytes=16 << 20),
         cost_estimate=pass_cost(depth - 2 * share, rows),
         name="row_lse_late",
-    )(*ys, x, first, mass.reshape(-1, tail))
-
-
-def column_lse(x, y, u, mass, width=512, chunk=512):
+    )(*ys, x, first, mass.reshape(1, -1))
+
+
+def column_lse(x, y, mass, got, width=512, chunk=512):
     rows, cols = x.shape[0], y.shape[0]
     tail = mass.shape[0] // lax.axis_size("row")
     return pl.pallas_call(
-        functools.partial(column_lse_kernel, width, chunk),
-        out_shape=(shape(1, cols + 2 * tail), shape(rows, cols, dtype=jnp.bfloat16), shape(1, cols)),
-        in_specs=[VMEM] * 4,
-        out_specs=(VMEM,) * 3,
-        scratch_shapes=lse_scratch(rows, chunk, width) + [pltpu.VMEM((ROOM // 512, 128), jnp.float32)],
-        compiler_params=pltpu.CompilerParams(vmem_limit_bytes=24 << 20),
+        functools.partial(column_lse_kernel, width, chunk, len(got)),
+        out_shape=(shape(1, cols + 2 * tail), shape(rows, cols, dtype=jnp.bfloat16), shape(1, cols), shape(1, rows)),
+        in_specs=[VMEM] * (3 + len(got)),
+        out_specs=(VMEM,) * 4,
+        scratch_shapes=[pltpu.VMEM((rows // 128, 128), jnp.float32)] + lse_scratch(rows, chunk, width),
+        compiler_params=pltpu.CompilerParams(vmem_limit_bytes=16 << 20),
         cost_estimate=pass_cost(rows, cols),
         name="column_lse",
-    )(x, y, u.reshape(rows // 128, 128), mass.reshape(-1, tail))
+    )(x, y, mass.reshape(1, -1), *[part.reshape(1, -1) for part in got])
+
+
+def pair_of(combine, one, two, cols):
+    size = one.shape[-1]
+    return pl.pallas_call(
+        functools.partial(pair_kernel, cols, combine),
+        out_shape=shape(1, size),
+        in_specs=[VMEM] * 2,
+        out_specs=VMEM,
+        compiler_params=pltpu.CompilerParams(vmem_limit_bytes=16 << 20),
+        name="pair",
+    )(one.reshape(1, size), two.reshape(1, size))
 
 
 def high_low(value):
@@ -292,10 +354,11 @@
     return high, (value - high.astype(jnp.float32)).astype(jnp.bfloat16)
 
 
-def column_grad_kernel(width, own, xt_ref, y_ref, e_ref, alpha_ref, beta_ref, gc_ref, gcs_ref,
-                       bb_ref, cb_ref, xa_ref, sums_ref, acc_ref):
+def column_grad_kernel(width, own, nz, xt_ref, y_ref, e_ref, alpha_ref, first_ref, b_ref, *refs):
+    got, (gc_ref, gcs_ref, beta_ref, bb_ref, cb_ref, xa_ref, s_ref, count_ref, acc_ref) = refs[:nz], refs[nz:]
     rows, cols = xt_ref.shape[1], y_ref.shape[0]
-    spread(beta_ref, bb_ref)
+    beta_ref[...] = new_beta(first_ref, b_ref, got)
+    spread(beta_ref[...], s_ref, bb_ref)
     place = lax.broadcasted_iota(jnp.int32, (128, 512), 0)
     for k in range(rows // 512):
         at = k * 512
@@ -312,10 +375,8 @@
         at = k * width
         got = jnp.dot(xa_ref[...], e_ref[:, at:at + width], preferred_element_type=jnp.float32)
         acc_ref[:, at:at + width] = got[:128] + jnp.where(lower, got[128:], 0.0)
-        count = got[254:255] + got[255:256]
-        for q in range(width // 128):
-            sums_ref[at // 128 + q:at // 128 + q + 1, :] = count[:, q * 128:(q + 1) * 128]
-    spread(sums_ref, cb_ref)
+        count_ref[:, at:at + width] = got[254:255] + got[255:256]
+    spread(count_ref[...], s_ref, cb_ref)
     for k in range(cols // 128):
         at = k * 128
         pulled = jnp.transpose(acc_ref[:, at:at + 128])
@@ -327,27 +388,25 @@
             gcs_ref[at - own:at - own + 128, :] = grad.astype(jnp.bfloat16)
 
 
-def column_grad(xt, y, e, alpha, beta, own, width=512):
+def column_grad(xt, y, e, alpha, first, mass, got, own, width=512):
     rows, cols = xt.shape[1], y.shape[0]
     return pl.pallas_call(
-        functools.partial(column_grad_kernel, width, own),
-        out_shape=(
-            jax.ShapeDtypeStruct((own, D), jnp.float32),
-            jax.ShapeDtypeStruct((cols - own, D), jnp.bfloat16),
-        ),
-        in_specs=[VMEM] * 5,
-        out_specs=(VMEM,) * 2,
+        functools.partial(column_grad_kernel, width, own, len(got)),
+        out_shape=(shape(own, D), shape(cols - own, D, dtype=jnp.bfloat16), shape(1, cols)),
+        in_specs=[VMEM] * (6 + len(got)),
+        out_specs=(VMEM,) * 3,
         scratch_shapes=[
             pltpu.VMEM((cols, 128), jnp.float32),
             pltpu.VMEM((cols, 128), jnp.float32),
             pltpu.VMEM((256, rows), jnp.bfloat16),
             pltpu.VMEM((cols // 128, 128), jnp.float32),
+            pltpu.VMEM((1, cols), jnp.float32),
             pltpu.VMEM((128, cols), jnp.float32),
         ],
         compiler_params=pltpu.CompilerParams(vmem_limit_bytes=16 << 20),
         cost_estimate=pl.CostEstimate(flops=4 * e.size * D, bytes_accessed=2 * e.size, transcendentals=0),
         name="column_grad",
-    )(xt, y, e, alpha.reshape(1, rows), beta.reshape(cols // 128, 128))
+    )(xt, y, e, alpha, first, mass, *[part.reshape(1, -1) for part in got])
 
 
 def row_block(at, chunk, x_ref, e_ref, yb_ref, scale):
@@ -359,10 +418,10 @@
     return 2.0 * scale * (total * x - pulled)
 
 
-def own_rows_kernel(x_ref, y_ref, e_ref, alpha_ref, beta_ref, gi_ref, yb_ref, ab_ref, bb_ref):
+def own_rows_kernel(x_ref, y_ref, e_ref, alpha_ref, beta_ref, gi_ref, yb_ref, sa_ref, ab_ref, sb_ref, bb_ref):
     own, cols = gi_ref.shape[0], y_ref.shape[0]
-    spread(alpha_ref, ab_ref)
-    spread(beta_ref, bb_ref)
+    spread(alpha_ref[:, :own], sa_ref, ab_ref)
+    spread(beta_ref[...], sb_ref, bb_ref)
     place = lax.broadcasted_iota(jnp.int32, (256, 128), 1)
     for k in range(cols // 256):
         at = k * 256
@@ -373,19 +432,17 @@
         low = jnp.where(place == 127, second.astype(jnp.float32), low)
         yb_ref[at:at + 256, :128] = high
         yb_ref[at:at + 256, 128:] = low.astype(jnp.bfloat16)
-    gi_ref[...] = row_block(0, own, x_ref, e_ref, yb_ref, ab_ref[:own, :])
-
-
-def sent_rows_kernel(chunk, own, x_ref, yb_ref, e_ref, alpha_ref, gis_ref, ab_ref):
-    spread(alpha_ref, ab_ref)
-
-    def block(k, _):
-        at = pl.multiple_of(k * chunk, chunk)
-        grad = row_block(at, chunk, x_ref, e_ref, yb_ref, ab_ref[pl.ds(at, chunk), :])
-        gis_ref[pl.ds(pl.multiple_of(at - own, chunk), chunk), :] = grad.astype(jnp.bfloat16)
-        return 0
-
-    lax.fori_loop(own // chunk, x_ref.shape[0] // chunk, block, 0)
+    gi_ref[...] = row_block(0, own, x_ref, e_ref, yb_ref, ab_ref[...])
+
+
+def sent_rows_kernel(chunk, own, x_ref, yb_ref, e_ref, alpha_ref, *refs):
+    outs, (sa_ref, ab_ref) = refs[:-2], refs[-2:]
+    spread(alpha_ref[...], sa_ref, ab_ref)
+    for k, out_ref in enumerate(outs):
+        for part in range(own // chunk):
+            at = (k + 1) * own + part * chunk
+            grad = row_block(at, chunk, x_ref, e_ref, yb_ref, ab_ref[at:at + chunk, :])
+            out_ref[part * chunk:(part + 1) * chunk, :] = grad.astype(jnp.bfloat16)
 
 
 def own_rows(x, y, e, alpha, beta, own):
@@ -395,11 +452,16 @@
         out_shape=(shape(own, D), shape(cols, 256, dtype=jnp.bfloat16)),
         in_specs=[VMEM] * 5,
         out_specs=(VMEM,) * 2,
-        scratch_shapes=[pltpu.VMEM((rows, 128), jnp.float32), pltpu.VMEM((cols, 128), jnp.float32)],
+        scratch_shapes=[
+            pltpu.VMEM((own // 128, 128), jnp.float32),
+            pltpu.VMEM((own, 128), jnp.float32),
+            pltpu.VMEM((cols // 128, 128), jnp.float32),
+            pltpu.VMEM((cols, 128), jnp.float32),
+        ],
         compiler_params=pltpu.CompilerParams(vmem_limit_bytes=16 << 20),
         cost_estimate=pl.CostEstimate(flops=4 * own * cols * D, bytes_accessed=2 * own * cols, transcendentals=0),
         name="own_rows",
-    )(x, y, e, alpha.reshape(rows // 128, 128), beta.reshape(cols // 128, 128))
+    )(x, y, e, alpha, beta)
 
 
 def sent_rows(x, yb, e, alpha, own):
@@ -407,14 +469,37 @@
     rest = rows - own
     return pl.pallas_call(
         functools.partial(sent_rows_kernel, math.gcd(own, 512), own),
-        out_shape=shape(rest, D, dtype=jnp.bfloat16),
+        out_shape=[shape(own, D, dtype=jnp.bfloat16)] * (rest // own),
         in_specs=[VMEM] * 4,
-        out_specs=VMEM,
-        scratch_shapes=[pltpu.VMEM((rows, 128), jnp.float32)],
+        out_specs=[VMEM] * (rest // own),
+        scratch_shapes=[pltpu.VMEM((rows // 128, 128), jnp.float32), pltpu.VMEM((rows, 128), jnp.float32)],
         compiler_params=pltpu.CompilerParams(vmem_limit_bytes=16 << 20),
         cost_estimate=pl.CostEstimate(flops=4 * rest * cols * D, bytes_accessed=2 * rest * cols, transcendentals=0),
         name="sent_rows",
-    )(x, yb, e, alpha.reshape(rows // 128, 128))
+    )(x, yb, e, alpha)
+
+
+def shares_kernel(gc_ref, other_ref, own_ref, *outs):
+    share = own_ref.shape[0]
+    for k in range(len(outs) + 1):
+        at = k * share
+        total = gc_ref[at:at + share, :] + other_ref[at:at + share, :].astype(jnp.float32)
+        if k == 0:
+            own_ref[...] = total
+        else:
+            outs[k - 1][...] = total.astype(jnp.bfloat16)
+
+
+def shares(gc, other, count):
+    share = gc.shape[0] // count
+    return pl.pallas_call(
+        shares_kernel,
+        out_shape=[shape(share, D)] + [shape(share, D, dtype=jnp.bfloat16)] * (count - 1),
+        in_specs=[VMEM] * 2,
+        out_specs=[VMEM] * count,
+        compiler_params=pltpu.CompilerParams(vmem_limit_bytes=16 << 20),
+        name="shares",
+    )(gc, other)
 
 
 class Groups:
@@ -430,78 +515,53 @@
         return lax.ppermute(value, ("row", "col"), [(i, i ^ mask) for i in range(self.count)])
 
 
-def reordered(value, shift, parts):
-    if shift == 0:
-        return value
-    blocks = value.reshape(parts, -1)
-    return jnp.concatenate([blocks[s ^ shift] for s in range(parts)])
-
-
-def lse2(parts):
-    top = functools.reduce(jnp.maximum, parts)
-    return top + jnp.log2(sum(jnp.exp2(part - top) for part in parts))
-
-
 def local(imu, camera, imu_mass, cam_mass):
     nrow, ncol = lax.axis_size("row"), lax.axis_size("col")
     groups = Groups(nrow, ncol)
     swap, across, along, core = groups.swap, groups.across, groups.along, groups.core
     na, nz = len(across), len(along)
     share_x, share_y = imu.shape[0], camera.shape[1]
-
-    mine = camera[0]
-    xs = [swap(imu, mask) for mask in across]
-    near = [swap(mine, mask) for mask in along]
-    far = [swap(part, core) for part in near]
-
-    def row_exchange(local_value):
-        return [reordered(swap(local_value, mask), s, na) for s, mask in enumerate(across)]
-
-    def halves(value):
-        return jnp.concatenate([value[value.shape[0] // 2:], value[:value.shape[0] // 2]])
+    rows, cols = na * share_x, 2 * nz * share_y
+
+    def from_rows(value):
+        return [swap(value, mask) for mask in across]
+
+    def from_columns(value):
+        return [swap(value, mask) for mask in along]
+
+    near, far = [camera[0]], [swap(camera[0], core)]
+    for z in range(1, nz):
+        near.append(swap(near[z & (z - 1)], along[z & -z]))
+    xs = from_rows(imu)
 
     x, xt, first = row_lse_early(xs, [near[0], far[0]])
-    y, sent = row_lse_late(x, near + far, first, imu_mass)
-    sent = sent.reshape(-1)
-    got = [swap(sent, mask) for mask in across]
-    size = na * share_x
-    mass_a = jnp.concatenate([got[2 * a][size:] for a in range(na // 2)])
-    u = jnp.log2(mass_a) - lse2([reordered(got[s][:size], s, na) for s in range(na)])
-
-    sent, e, shift = column_lse(x, y, u, cam_mass)
-    sent, shift = sent.reshape(-1), shift.reshape(-1)
-    size = 2 * nz * share_y
-    lse, mass = sent[:size], sent[size:]
-    lse = lse2([lse, halves(swap(lse, core))])
-    sent = jnp.concatenate([lse, mass])
-    got = [swap(sent, mask) for mask in along]
-
-    def turned(value, z):
-        half = value.shape[0] // 2
-        return jnp.concatenate([reordered(value[:half], z, nz), reordered(value[half:], z, nz)])
-
-    masses = [part[size:].reshape(2, share_y) for part in got]
-    mass_b = jnp.concatenate([part[0] for part in masses] + [part[1] for part in masses])
-    v = jnp.log2(mass_b) - lse2([turned(got[z][:size], z) for z in range(nz)])
-
-    first_beta = beta = jnp.exp2(v + shift)
+    rest = lax.optimization_barrier((first, *near[1:]))
+    far += [swap(part, core) for part in rest[1:]]
+    y, sent = row_lse_late(x, [near[0], *rest[1:], *far], rest[0], imu_mass)
+    got = from_rows(sent.reshape(-1))
+
+    sent, e, shift, mass_a = column_lse(x, y, cam_mass, got)
+    sent = pair_of(lse2, sent, swap(sent.reshape(-1), core), cols)
+    got = from_columns(sent.reshape(-1))
+
+    sums, first_beta, mass_b = weighted(first_row_kernel, [rows, cols, cols], e, [shift], got)
     for step in range(1, ITERS):
-        alpha = mass_a / sum(row_exchange(weighted(row_kernel, e, beta, x.shape[0])))
-        part = first_beta * weighted(col_kernel, e, alpha, y.shape[0])
-        part = part + halves(swap(part, core))
-        beta = first_beta * (mass_b / sum(turned(swap(part, mask), z) for z, mask in enumerate(along)))
-
-    gc, gc_send = column_grad(xt, y, e, alpha, beta, nz * share_y)
+        if step > 1:
+            sums, = weighted(row_kernel, [rows], e, [first_beta, mass_b], got)
+        part, alpha = weighted(column_kernel, [cols, rows], e, [mass_a, first_beta], from_rows(sums.reshape(-1)))
+        part = pair_of(sum, part, swap(part.reshape(-1), core), cols)
+        got = from_columns(part.reshape(-1))
+
+    gc, gc_send, beta = column_grad(xt, y, e, alpha, first_beta, mass_b, got, nz * share_y)
     gi, yb = own_rows(x, y, e, alpha, beta, share_x)
-    gc = gc + swap(gc_send, core).astype(jnp.float32)
-    gc, yb = lax.optimization_barrier((gc, yb))
-    grad_cam = gc[:share_y]
-    for z in range(1, nz):
-        part = gc[z * share_y:(z + 1) * share_y].astype(jnp.bfloat16)
-        grad_cam = grad_cam + swap(part, along[z]).astype(jnp.float32)
-    gi_send = sent_rows(x, yb, e, alpha, share_x)
-    for s in range(1, na):
-        gi = gi + swap(gi_send[(s - 1) * share_x:s * share_x], across[s]).astype(jnp.float32)
+    (grad_cam, *parts), yb = lax.optimization_barrier((shares(gc, swap(gc_send, core), nz), yb))
+    parts = [swap(part, along[z + 1]) for z, part in enumerate(parts)]
+    sent = sent_rows(x, yb, e, alpha, share_x)
+    sent, parts[0] = lax.optimization_barrier((sent, parts[0]))
+    for s, part in enumerate(sent):
+        gi = gi + swap(part, across[s + 1]).astype(jnp.float32)
+    for part in parts:
+        grad_cam = grad_cam + part.astype(jnp.float32)
     return gi, grad_cam[None]
 
 

time: 174 us -> 157 us (0.902)
  local copies, waits for them, and re-layouts: 11.6 us -> 3.22 us
  waiting for transfers between devices: 35.6 us -> 28.7 us
    ppermute x38, waiting for transfers between devices: 35.6 us -> 28.7 us  [swap(): lax.ppermute(value, ('row', 'col'), [(i, i ^ mask) for i in range(self.co...]
    unnamed x70 -> x8, local copies, waits for them, and re-layouts: 9.38 us -> 3.22 us
    pallas_call x6 -> x10, Pallas kernels: 52.4 us -> 53.5 us  [the longest x1 30.9 us: column_lse(): pl.pallas_call(functools.partial(column_lse_kernel, width, chunk, len(got...]
  transfers between devices with their start and end apart: 38 -> 38, of which waited for: 21 -> 27; matrix products, arithmetic and copies ran while one was open for 2% -> 0% of each run, Pallas kernels for 5% -> 8%
where the time goes in v7:
time: 157 us
  Pallas kernels  79.9 us (51%)
  starting transfers between devices  42.5 us (27%)
  waiting for transfers between devices  28.7 us (18%)
  local copies, waits for them, and re-layouts  3.22 us (2%)
    ppermute x38, starting transfers between devices, swap(): lax.ppermute(value, ('row', 'col'), [(i, i ^ mask) for i in range(self.co...  42.5 us
    pallas_call x1, Pallas kernels, column_lse(): pl.pallas_call(functools.partial(column_lse_kernel, width, chunk, len(got...  30.9 us
    ppermute x38, waiting for transfers between devices, swap(): lax.ppermute(value, ('row', 'col'), [(i, i ^ mask) for i in range(self.co...  28.7 us
    pallas_call x4, Pallas kernels, weighted(): pl.pallas_call(functools.partial(kernel, width, len(got)), out_shape=[sha...  17 us
    pallas_call x1, Pallas kernels, row_lse_late(): pl.pallas_call(functools.partial(row_lse_kernel, width, False, 0, len(ys)...  13.9 us
    pallas_call x1, Pallas kernels, row_lse_early(): pl.pallas_call(functools.partial(row_lse_kernel, width, True, len(xs), le...  6.69 us
    pallas_call x1, Pallas kernels, column_grad(): pl.pallas_call(functools.partial(column_grad_kernel, width, own, len(got)...  5.55 us
    pallas_call x1, Pallas kernels, sent_rows(): pl.pallas_call(functools.partial(sent_rows_kernel, math.gcd(own, 512), ow...  3.71 us
  transfers between devices with their start and end apart: 38, of which 27 were waited for; matrix products, arithmetic and copies ran while one was open for 0% of the time, Pallas kernels for 8%

profile of v7, /device:TPU:0, one launch (start us, length us, event | category | flops | bytes accessed | tf_op | source)
XLA Modules:
  0.0 156.6 jit_solution(3434805783400170765)
XLA Ops:
  0.6 4.1 %collective-permute-start.5 = (bf16[512,128]{1,0:T(8,128)(2,1)}, bf16[512,128]{1,0:T(8,128)(2,1)S(1)}, u32[]{:S(2)}, u32[]{:S(2)}) collective-permute-start(bf16[512,128]{1,0:T(8,128)(2,1)} %bitcast.71), channel_id=1, source_target_pairs={{0,4},{1,5},{2,6},{3,7},{4,0},{5,1},{6,2},{7,3},{8,12},{9,13},{10,... | collective-permute-start | bytes 393224 | tf_op jit(solution)/shard_map/ppermute | solution.py:515
  4.7 1.5 collective-permute-start.1
  6.2 1.5 collective-permute-start
  8.2 3.0 %collective-permute-done.5.refs_2_ = bf16[512,128]{1,0:T(8,128)(2,1)S(1)} collective-permute-done((bf16[512,128]{1,0:T(8,128)(2,1)}, bf16[512,128]{1,0:T(8,128)(2,1)S(1)}, u32[]{:S(2)}, u32[]{:S(2)}) %collective-permute-start.5) | collective-permute-done | bytes 131104 | tf_op jit(solution)/shard_map/ppermute | solution.py:515
  12.1 1.2 collective-permute-start.6
  13.3 1.6 %collective-permute-done.refs_1_ = bf16[512,128]{1,0:T(8,128)(2,1)S(1)} collective-permute-done((bf16[512,128]{1,0:T(8,128)(2,1)}, bf16[512,128]{1,0:T(8,128)(2,1)S(1)}, u32[]{:S(2)}, u32[]{:S(2)}) %collective-permute-start) | collective-permute-done | bytes 131104 | tf_op jit(solution)/shard_map/ppermute | solution.py:515
  16.7 6.7 %row_lse_early.1 = (bf16[2048,128]{1,0:T(8,128)(2,1)S(1)}, bf16[128,2048]{1,0:T(8,128)(2,1)S(1)}, f32[1,2048]{1,0:T(1,128)S(1)}) custom-call(bf16[512,128]{1,0:T(8,128)(2,1)S(1)} %copy-done, bf16[512,128]{1,0:T(8,128)(2,1)S(1)} %collective-permute-done.refs_1_, bf16[512,128]{1,0:T(8,128)(2,1)S(1)} %collective-permute-done.1.refs_2_, ...), custom_call_target="tpu_custom_call" | custom-call | flops 536870912 | bytes 786432 | tf_op jit(solution)/shard_map/row_lse_early/pallas_call | solution.py:297
  26.0 13.9 %row_lse_late.1 = (bf16[4096,128]{1,0:T(8,128)(2,1)S(1)}, f32[1,3072]{1,0:T(1,128)S(1)}) custom-call(bf16[512,128]{1,0:T(8,128)(2,1)S(1)} %bitcast.75, bf16[512,128]{1,0:T(8,128)(2,1)S(1)} %collective-permute-done.4.refs_1_, bf16[512,128]{1,0:T(8,128)(2,1)S(1)} %collective-permute-done.5.refs_2_, bf16[512,128]{1,0:T(8,128)(2,1)S(1)} %collective-permute-done.6.refs_3_, ...), custom_call_target="tpu_custom_call" | custom-call | flops 1610612736 | bytes 1310720 | tf_op jit(solution)/shard_map/row_lse_late/pallas_call | solution.py:313
  40.2 3.4 %collective-permute-start.10 = (f32[3072]{0:T(1024)S(1)}, f32[3072]{0:T(1024)S(1)}, u32[]{:S(2)}, u32[]{:S(2)}) collective-permute-start(f32[3072]{0:T(1024)S(1)} %bitcast.79), channel_id=1, source_target_pairs={{0,1},{1,0},{2,3},{3,2},{4,5},{5,4},{6,7},{7,6},{8,9},{9,8},{10,11... | collective-permute-start | bytes 36872 | tf_op jit(solution)/shard_map/ppermute | solution.py:515
  43.6 1.1 collective-permute-done.12
  45.9 30.9 %column_lse.1 = (f32[1,5120]{1,0:T(1,128)S(1)}, bf16[2048,4096]{1,0:T(8,128)(2,1)S(1)}, f32[1,4096]{1,0:T(1,128)S(1)}, f32[1,2048]{1,0:T(1,128)S(1)}) custom-call(bf16[2048,128]{1,0:T(8,128)(2,1)S(1)} %get-tuple-element.42.refs_8_.x_ref, bf16[4096,128]{1,0:T(8,128)(2,1)S(1)} %get-tuple-element.48.y_ref, f32[1,2048]{1,0:T(1,128)S(1)} %bitcast.83, ...), custom_call_target="tpu_custom_call" | custom-call | flops 2147483648 | bytes 1572864 | tf_op jit(solution)/shard_map/column_lse/pallas_call | solution.py:328
  76.9 1.2 collective-permute-done.13
  78.1 2.1 %collective-permute-start.16 = (f32[5120]{0:T(1024)S(1)}, f32[5120]{0:T(1024)S(1)}, u32[]{:S(2)}, u32[]{:S(2)}) collective-permute-start(f32[5120]{0:T(1024)S(1)} %bitcast.35), channel_id=1, source_target_pairs={{0,6},{1,7},{2,4},{3,5},{4,2},{5,3},{6,0},{7,1},{8,14},{9,15},{10,... | collective-permute-start | bytes 61448 | tf_op jit(solution)/shard_map/ppermute | solution.py:515
  80.5 2.1 %collective-permute-start.14 = (f32[5120]{0:T(1024)S(1)}, f32[5120]{0:T(1024)S(1)}, u32[]{:S(2)}, u32[]{:S(2)}) collective-permute-start(f32[5120]{0:T(1024)S(1)} %bitcast.37), channel_id=1, source_target_pairs={{0,2},{1,3},{2,0},{3,1},{4,6},{5,7},{6,4},{7,5},{8,10},{9,11},{10,... | collective-permute-start | bytes 61448 | tf_op jit(solution)/shard_map/ppermute | solution.py:515
  82.5 1.4 collective-permute-done.16
  83.9 1.1 collective-permute-done.15
  85.1 5.1 %weighted_sum.4 = (f32[1,2048]{1,0:T(1,128)S(1)}, f32[1,4096]{1,0:T(1,128)S(1)}, f32[1,4096]{1,0:T(1,128)S(1)}) custom-call(bf16[2048,4096]{1,0:T(8,128)(2,1)S(1)} %get-tuple-element.50.e_ref, f32[1,4096]{1,0:T(1,128)S(1)} %get-tuple-element.52.shift_ref, f32[1,5120]{1,0:T(1,128)S(1)} %pair.3.refs_0_, f32[1,5120]{1,0:T(1,128)S(1)} %bitcast.49, ...), custom_call_target="tpu_custom_call" | custom-call | flops 16777216 | bytes 16777216 | tf_op jit(solution)/shard_map/weighted_sum/pallas_call | solution.py:266
  90.2 2.1 %collective-permute-start.19 = (f32[2048]{0:T(1024)S(1)}, f32[2048]{0:T(1024)S(1)}, u32[]{:S(2)}, u32[]{:S(2)}) collective-permute-start(f32[2048]{0:T(1024)S(1)} %bitcast.62), channel_id=1, source_target_pairs={{0,17},{1,16},{2,19},{3,18},{4,21},{5,20},{6,23},{7,22},{8,25},{9,... | collective-permute-start | bytes 24584 | tf_op jit(solution)/shard_map/ppermute | solution.py:515
  93.7 1.1 collective-permute-done.19
  94.8 1.1 collective-permute-done.18
  96.6 3.5 %weighted_sum.5 = (f32[1,4096]{1,0:T(1,128)S(1)}, f32[1,2048]{1,0:T(1,128)}) custom-call(bf16[2048,4096]{1,0:T(8,128)(2,1)S(1)} %get-tuple-element.50.e_ref, f32[1,2048]{1,0:T(1,128)S(1)} %get-tuple-element.51.a_ref, f32[1,4096]{1,0:T(1,128)S(1)} %get-tuple-element.54.first_ref, f32[1,2048]{1,0:T(1,128)S(1)} %get-tuple-element.56.refs_0_, ...), custom_call_target="tpu_custom_call" | custom-call | flops 16777216 | bytes 16777216 | tf_op jit(solution)/shard_map/weighted_sum/pallas_call | solution.py:266
  100.1 1.2 collective-permute-done.20
  101.3 2.4 %collective-permute-start.23 = (f32[4096]{0:T(1024)S(1)}, f32[4096]{0:T(1024)S(1)}, u32[]{:S(2)}, u32[]{:S(2)}) collective-permute-start(f32[4096]{0:T(1024)S(1)} %bitcast.41), channel_id=1, source_target_pairs={{0,6},{1,7},{2,4},{3,5},{4,2},{5,3},{6,0},{7,1},{8,14},{9,15},{10,... | collective-permute-start | bytes 49160 | tf_op jit(solution)/shard_map/ppermute | solution.py:515
  103.7 1.1 collective-permute-start.22
  105.7 1.2 collective-permute-done.23
  106.9 1.5 collective-permute-done.22
  108.6 5.0 %weighted_sum.6.refs_0_ = f32[1,2048]{1,0:T(1,128)S(1)} custom-call(bf16[2048,4096]{1,0:T(8,128)(2,1)S(1)} %get-tuple-element.50.e_ref, f32[1,4096]{1,0:T(1,128)S(1)} %get-tuple-element.54.first_ref, f32[1,4096]{1,0:T(1,128)S(1)} %get-tuple-element.55.b_ref, f32[1,4096]{1,0:T(1,128)S(1)} %pair.4.refs_0_, f32[1,4096]{1,0:T(1,128)S(1)} %bitcast.61, ...), custom_call_target="tpu_custom_call" | custom-call | flops 16777216 | bytes 16777216 | tf_op jit(solution)/shard_map/weighted_sum/pallas_call | solution.py:266
  113.6 1.2 collective-permute-start.26
  115.2 1.9 %collective-permute-start.24 = (f32[2048]{0:T(1024)S(1)}, f32[2048]{0:T(1024)S(1)}, u32[]{:S(2)}, u32[]{:S(2)}) collective-permute-start(f32[2048]{0:T(1024)S(1)} %bitcast.46), channel_id=1, source_target_pairs={{0,1},{1,0},{2,3},{3,2},{4,5},{5,4},{6,7},{7,6},{8,9},{9,8},{10,11... | collective-permute-start | bytes 24584 | tf_op jit(solution)/shard_map/ppermute | solution.py:515
  117.1 1.1 collective-permute-done.26
  118.9 3.5 %weighted_sum.7 = (f32[1,4096]{1,0:T(1,128)S(1)}, f32[1,2048]{1,0:T(1,128)S(1)}) custom-call(bf16[2048,4096]{1,0:T(8,128)(2,1)S(1)} %get-tuple-element.50.e_ref, f32[1,2048]{1,0:T(1,128)S(1)} %get-tuple-element.51.a_ref, f32[1,4096]{1,0:T(1,128)S(1)} %get-tuple-element.54.first_ref, f32[1,2048]{1,0:T(1,128)S(1)} %weighted_sum.6.refs_0_, ...), custom_call_target="tpu_custom_call" | custom-call | flops 16777216 | bytes 16777216 | tf_op jit(solution)/shard_map/weighted_sum/pallas_call | solution.py:266
  122.4 1.2 collective-permute-done.27
  123.6 2.1 %collective-permute-start.30 = (f32[4096]{0:T(1024)S(1)}, f32[4096]{0:T(1024)S(1)}, u32[]{:S(2)}, u32[]{:S(2)}) collective-permute-start(f32[4096]{0:T(1024)S(1)} %bitcast.38), channel_id=1, source_target_pairs={{0,6},{1,7},{2,4},{3,5},{4,2},{5,3},{6,0},{7,1},{8,14},{9,15},{10,... | collective-permute-start | bytes 49160 | tf_op jit(solution)/shard_map/ppermute | solution.py:515
  125.7 1.0 collective-permute-start.29
  126.7 1.4 collective-permute-start.28
  128.1 1.2 collective-permute-done.30
  129.3 1.1 collective-permute-done.29
  130.5 5.6 %column_grad.1 = (f32[2048,128]{1,0:T(8,128)S(1)}, bf16[2048,128]{1,0:T(8,128)(2,1)S(1)}, f32[1,4096]{1,0:T(1,128)S(1)}) custom-call(bf16[128,2048]{1,0:T(8,128)(2,1)S(1)} %get-tuple-element.59.xt_ref, bf16[4096,128]{1,0:T(8,128)(2,1)S(1)} %get-tuple-element.48.y_ref, bf16[2048,4096]{1,0:T(8,128)(2,1)S(1)} %get-tuple-element.50.e_ref, ...), custom_call_target="tpu_custom_call" | custom-call | flops 4294967296 | bytes 16777216 | tf_op jit(solution)/shard_map/column_grad/pallas_call | solution.py:393
  136.2 2.0 %own_rows.1 = (f32[512,128]{1,0:T(8,128)S(1)}, bf16[4096,256]{1,0:T(8,128)(2,1)S(1)}) custom-call(bf16[2048,128]{1,0:T(8,128)(2,1)S(1)} %get-tuple-element.42.refs_8_.x_ref, bf16[4096,128]{1,0:T(8,128)(2,1)S(1)} %get-tuple-element.48.y_ref, bf16[2048,4096]{1,0:T(8,128)(2,1)S(1)} %get-tuple-element.50.e_ref, f32[1,2048]{1,0:T(1,128)S(1)} %get-tuple-element.58.alpha_ref, ...), custom_call_target="tpu_custom_call" | custom-call | flops 1073741824 | bytes 4194304 | tf_op jit(solution)/shard_map/own_rows/pallas_call | solution.py:450
  138.3 1.4 collective-permute-start.32
  139.6 1.1 collective-permute-start.36
  140.7 2.0 %collective-permute-start.37 = (bf16[512,128]{1,0:T(8,128)(2,1)S(1)}, bf16[512,128]{1,0:T(8,128)(2,1)S(1)}, u32[]{:S(2)}, u32[]{:S(2)}) collective-permute-start(bf16[512,128]{1,0:T(8,128)(2,1)S(1)} %get-tuple-element.81), channel_id=1, source_target_pairs={{0,6},{1,7},{2,4},{3,5},{4,2},{5,3},{6,0},{7,1},{8,14},{9,15},{10,... | collective-permute-start | bytes 393224 | tf_op jit(solution)/shard_map/ppermute | solution.py:515
  142.7 3.7 %sent_rows.1 = (bf16[512,128]{1,0:T(8,128)(2,1)S(1)}, bf16[512,128]{1,0:T(8,128)(2,1)S(1)}, bf16[512,128]{1,0:T(8,128)(2,1)S(1)}) custom-call(bf16[2048,128]{1,0:T(8,128)(2,1)S(1)} %get-tuple-element.42.refs_8_.x_ref, bf16[4096,256]{1,0:T(8,128)(2,1)S(1)} %get-tuple-element.70.yb_ref, bf16[2048,4096]{1,0:T(8,128)(2,1)S(1)} %get-tuple-element.50.e_ref, ...), custom_call_target="tpu_custom_call" | custom-call | flops 3221225472 | bytes 12582912 | tf_op jit(solution)/shard_map/sent_rows/pallas_call | solution.py:470
  146.4 1.3 collective-permute-start.33
  147.8 1.3 collective-permute-start.34
  149.0 1.0 collective-permute-start.35
  150.0 2.5 %collective-permute-done.36 = bf16[512,128]{1,0:T(8,128)(2,1)S(1)} collective-permute-done((bf16[512,128]{1,0:T(8,128)(2,1)S(1)}, bf16[512,128]{1,0:T(8,128)(2,1)S(1)}, u32[]{:S(2)}, u32[]{:S(2)}) %collective-permute-start.36) | collective-permute-done | bytes 131104 | tf_op jit(solution)/shard_map/ppermute | solution.py:515
  153.9 2.0 %collective-permute-done.35 = bf16[512,128]{1,0:T(8,128)(2,1)S(1)} collective-permute-done((bf16[512,128]{1,0:T(8,128)(2,1)S(1)}, bf16[512,128]{1,0:T(8,128)(2,1)S(1)}, u32[]{:S(2)}, u32[]{:S(2)}) %collective-permute-start.35) | collective-permute-done | bytes 131104 | tf_op jit(solution)/shard_map/ppermute | solution.py:515
  (52 shorter events, 14.6 us)
Async XLA Ops:
  0.6 10.6 %collective-permute-start.5 = (bf16[512,128]{1,0:T(8,128)(2,1)}, bf16[512,128]{1,0:T(8,128)(2,1)S(1)}, u32[]{:S(2)}, u32[]{:S(2)}) collective-permute-start(bf16[512,128]{1,0:T(8,128)(2,1)} %bitcast.71), channel_id=1, source_target_pairs={{0,4},{1,5},{2,6},{3,7},{4,0},{5,1},{6,2},{7,3},{8,12},{9,13},{10,... | collective-permute-start | bytes 393224 | tf_op jit(solution)/shard_map/ppermute | solution.py:515
  4.7 7.3 %collective-permute-start.3 = (bf16[512,128]{1,0:T(8,128)(2,1)}, bf16[512,128]{1,0:T(8,128)(2,1)S(1)}, u32[]{:S(2)}, u32[]{:S(2)}) collective-permute-start(bf16[512,128]{1,0:T(8,128)(2,1)} %bitcast.72), channel_id=1, source_target_pairs={{0,8},{1,9},{2,10},{3,11},{4,12},{5,13},{6,14},{7,15},{8,0},{9,1},... | collective-permute-start | bytes 393224 | tf_op jit(solution)/shard_map/ppermute | solution.py:515
  4.7 8.5 %collective-permute-start.1 = (bf16[512,128]{1,0:T(8,128)(2,1)}, bf16[512,128]{1,0:T(8,128)(2,1)S(1)}, u32[]{:S(2)}, u32[]{:S(2)}) collective-permute-start(bf16[512,128]{1,0:T(8,128)(2,1)} %refs_0_.1), channel_id=1, source_target_pairs={{0,16},{1,17},{2,18},{3,19},{4,20},{5,21},{6,22},{7,23},{8,24},{9,... | collective-permute-start | bytes 393224 | tf_op jit(solution)/shard_map/ppermute | solution.py:515
  6.2 8.6 %collective-permute-start = (bf16[512,128]{1,0:T(8,128)(2,1)}, bf16[512,128]{1,0:T(8,128)(2,1)S(1)}, u32[]{:S(2)}, u32[]{:S(2)}) collective-permute-start(bf16[512,128]{1,0:T(8,128)(2,1)} %refs_0_.1), channel_id=1, source_target_pairs={{0,1},{1,0},{2,3},{3,2},{4,5},{5,4},{6,7},{7,6},{8,9},{9,8},{10,11... | collective-permute-start | bytes 393224 | tf_op jit(solution)/shard_map/ppermute | solution.py:515
  7.7 7.1 %collective-permute-start.2 = (bf16[512,128]{1,0:T(8,128)(2,1)}, bf16[512,128]{1,0:T(8,128)(2,1)S(1)}, u32[]{:S(2)}, u32[]{:S(2)}) collective-permute-start(bf16[512,128]{1,0:T(8,128)(2,1)} %refs_0_.1), channel_id=1, source_target_pairs={{0,17},{1,16},{2,19},{3,18},{4,21},{5,20},{6,23},{7,22},{8,25},{9,... | collective-permute-start | bytes 393224 | tf_op jit(solution)/shard_map/ppermute | solution.py:515
  11.2 12.1 %collective-permute-start.4 = (bf16[512,128]{1,0:T(8,128)(2,1)}, bf16[512,128]{1,0:T(8,128)(2,1)S(1)}, u32[]{:S(2)}, u32[]{:S(2)}) collective-permute-start(bf16[512,128]{1,0:T(8,128)(2,1)} %bitcast.73), channel_id=1, source_target_pairs={{0,2},{1,3},{2,0},{3,1},{4,6},{5,7},{6,4},{7,5},{8,10},{9,11},{10,... | collective-permute-start | bytes 393224 | tf_op jit(solution)/shard_map/ppermute | solution.py:515
  12.1 11.3 %collective-permute-start.6 = (bf16[512,128]{1,0:T(8,128)(2,1)S(1)}, bf16[512,128]{1,0:T(8,128)(2,1)S(1)}, u32[]{:S(2)}, u32[]{:S(2)}) collective-permute-start(bf16[512,128]{1,0:T(8,128)(2,1)S(1)} %collective-permute-done.5.refs_2_), channel_id=1, source_target_pairs={{0,2},{1,3},{2,0},{3,1},{4,6},{5,7},{6,4},{7,5},{8,10},{9,11},{10,... | collective-permute-start | bytes 393224 | tf_op jit(solution)/shard_map/ppermute | solution.py:515
  14.9 0.9 copy-start
  15.8 0.9 copy-start.1
  23.4 1.4 collective-permute-start.7
  23.5 1.5 collective-permute-start.8
  24.0 1.3 collective-permute-start.9
  25.3 0.7 copy-start.2
  40.0 4.7 %collective-permute-start.12 = (f32[3072]{0:T(1024)S(1)}, f32[3072]{0:T(1024)S(1)}, u32[]{:S(2)}, u32[]{:S(2)}) collective-permute-start(f32[3072]{0:T(1024)S(1)} %bitcast.77), channel_id=1, source_target_pairs={{0,17},{1,16},{2,19},{3,18},{4,21},{5,20},{6,23},{7,22},{8,25},{9,... | collective-permute-start | bytes 36872 | tf_op jit(solution)/shard_map/ppermute | solution.py:515
  40.1 4.6 %collective-permute-start.11 = (f32[3072]{0:T(1024)S(1)}, f32[3072]{0:T(1024)S(1)}, u32[]{:S(2)}, u32[]{:S(2)}) collective-permute-start(f32[3072]{0:T(1024)S(1)} %bitcast.78), channel_id=1, source_target_pairs={{0,16},{1,17},{2,18},{3,19},{4,20},{5,21},{6,22},{7,23},{8,24},{9,... | collective-permute-start | bytes 36872 | tf_op jit(solution)/shard_map/ppermute | solution.py:515
  40.2 5.1 %collective-permute-start.10 = (f32[3072]{0:T(1024)S(1)}, f32[3072]{0:T(1024)S(1)}, u32[]{:S(2)}, u32[]{:S(2)}) collective-permute-start(f32[3072]{0:T(1024)S(1)} %bitcast.79), channel_id=1, source_target_pairs={{0,1},{1,0},{2,3},{3,2},{4,5},{5,4},{6,7},{7,6},{8,9},{9,8},{10,11... | collective-permute-start | bytes 36872 | tf_op jit(solution)/shard_map/ppermute | solution.py:515
  45.2 0.7 copy-start.3
  76.8 1.3 collective-permute-start.13
  78.1 5.9 %collective-permute-start.16 = (f32[5120]{0:T(1024)S(1)}, f32[5120]{0:T(1024)S(1)}, u32[]{:S(2)}, u32[]{:S(2)}) collective-permute-start(f32[5120]{0:T(1024)S(1)} %bitcast.35), channel_id=1, source_target_pairs={{0,6},{1,7},{2,4},{3,5},{4,2},{5,3},{6,0},{7,1},{8,14},{9,15},{10,... | collective-permute-start | bytes 61448 | tf_op jit(solution)/shard_map/ppermute | solution.py:515
  80.2 4.9 %collective-permute-start.15 = (f32[5120]{0:T(1024)S(1)}, f32[5120]{0:T(1024)S(1)}, u32[]{:S(2)}, u32[]{:S(2)}) collective-permute-start(f32[5120]{0:T(1024)S(1)} %bitcast.36), channel_id=1, source_target_pairs={{0,4},{1,5},{2,6},{3,7},{4,0},{5,1},{6,2},{7,3},{8,12},{9,13},{10,... | collective-permute-start | bytes 61448 | tf_op jit(solution)/shard_map/ppermute | solution.py:515
  80.5 4.6 %collective-permute-start.14 = (f32[5120]{0:T(1024)S(1)}, f32[5120]{0:T(1024)S(1)}, u32[]{:S(2)}, u32[]{:S(2)}) collective-permute-start(f32[5120]{0:T(1024)S(1)} %bitcast.37), channel_id=1, source_target_pairs={{0,2},{1,3},{2,0},{3,1},{4,6},{5,7},{6,4},{7,5},{8,10},{9,11},{10,... | collective-permute-start | bytes 61448 | tf_op jit(solution)/shard_map/ppermute | solution.py:515
  90.2 4.6 %collective-permute-start.19 = (f32[2048]{0:T(1024)S(1)}, f32[2048]{0:T(1024)S(1)}, u32[]{:S(2)}, u32[]{:S(2)}) collective-permute-start(f32[2048]{0:T(1024)S(1)} %bitcast.62), channel_id=1, source_target_pairs={{0,17},{1,16},{2,19},{3,18},{4,21},{5,20},{6,23},{7,22},{8,25},{9,... | collective-permute-start | bytes 24584 | tf_op jit(solution)/shard_map/ppermute | solution.py:515
  92.3 3.7 %collective-permute-start.18 = (f32[2048]{0:T(1024)S(1)}, f32[2048]{0:T(1024)S(1)}, u32[]{:S(2)}, u32[]{:S(2)}) collective-permute-start(f32[2048]{0:T(1024)S(1)} %bitcast.63), channel_id=1, source_target_pairs={{0,16},{1,17},{2,18},{3,19},{4,20},{5,21},{6,22},{7,23},{8,24},{9,... | collective-permute-start | bytes 24584 | tf_op jit(solution)/shard_map/ppermute | solution.py:515
  93.0 3.7 %collective-permute-start.17 = (f32[2048]{0:T(1024)S(1)}, f32[2048]{0:T(1024)S(1)}, u32[]{:S(2)}, u32[]{:S(2)}) collective-permute-start(f32[2048]{0:T(1024)S(1)} %bitcast.64), channel_id=1, source_target_pairs={{0,1},{1,0},{2,3},{3,2},{4,5},{5,4},{6,7},{7,6},{8,9},{9,8},{10,11... | collective-permute-start | bytes 24584 | tf_op jit(solution)/shard_map/ppermute | solution.py:515
  100.1 1.2 collective-permute-start.20
  101.3 5.6 %collective-permute-start.23 = (f32[4096]{0:T(1024)S(1)}, f32[4096]{0:T(1024)S(1)}, u32[]{:S(2)}, u32[]{:S(2)}) collective-permute-start(f32[4096]{0:T(1024)S(1)} %bitcast.41), channel_id=1, source_target_pairs={{0,6},{1,7},{2,4},{3,5},{4,2},{5,3},{6,0},{7,1},{8,14},{9,15},{10,... | collective-permute-start | bytes 49160 | tf_op jit(solution)/shard_map/ppermute | solution.py:515
  103.7 4.6 %collective-permute-start.22 = (f32[4096]{0:T(1024)S(1)}, f32[4096]{0:T(1024)S(1)}, u32[]{:S(2)}, u32[]{:S(2)}) collective-permute-start(f32[4096]{0:T(1024)S(1)} %bitcast.42), channel_id=1, source_target_pairs={{0,4},{1,5},{2,6},{3,7},{4,0},{5,1},{6,2},{7,3},{8,12},{9,13},{10,... | collective-permute-start | bytes 49160 | tf_op jit(solution)/shard_map/ppermute | solution.py:515
  104.8 3.7 %collective-permute-start.21 = (f32[4096]{0:T(1024)S(1)}, f32[4096]{0:T(1024)S(1)}, u32[]{:S(2)}, u32[]{:S(2)}) collective-permute-start(f32[4096]{0:T(1024)S(1)} %bitcast.43), channel_id=1, source_target_pairs={{0,2},{1,3},{2,0},{3,1},{4,6},{5,7},{6,4},{7,5},{8,10},{9,11},{10,... | collective-permute-start | bytes 49160 | tf_op jit(solution)/shard_map/ppermute | solution.py:515
  113.6 4.6 %collective-permute-start.26 = (f32[2048]{0:T(1024)S(1)}, f32[2048]{0:T(1024)S(1)}, u32[]{:S(2)}, u32[]{:S(2)}) collective-permute-start(f32[2048]{0:T(1024)S(1)} %bitcast.44), channel_id=1, source_target_pairs={{0,17},{1,16},{2,19},{3,18},{4,21},{5,20},{6,23},{7,22},{8,25},{9,... | collective-permute-start | bytes 24584 | tf_op jit(solution)/shard_map/ppermute | solution.py:515
  114.7 3.7 %collective-permute-start.25 = (f32[2048]{0:T(1024)S(1)}, f32[2048]{0:T(1024)S(1)}, u32[]{:S(2)}, u32[]{:S(2)}) collective-permute-start(f32[2048]{0:T(1024)S(1)} %bitcast.45), channel_id=1, source_target_pairs={{0,16},{1,17},{2,18},{3,19},{4,20},{5,21},{6,22},{7,23},{8,24},{9,... | collective-permute-start | bytes 24584 | tf_op jit(solution)/shard_map/ppermute | solution.py:515
  115.2 3.7 %collective-permute-start.24 = (f32[2048]{0:T(1024)S(1)}, f32[2048]{0:T(1024)S(1)}, u32[]{:S(2)}, u32[]{:S(2)}) collective-permute-start(f32[2048]{0:T(1024)S(1)} %bitcast.46), channel_id=1, source_target_pairs={{0,1},{1,0},{2,3},{3,2},{4,5},{5,4},{6,7},{7,6},{8,9},{9,8},{10,11... | collective-permute-start | bytes 24584 | tf_op jit(solution)/shard_map/ppermute | solution.py:515
  122.4 1.2 collective-permute-start.27
  123.6 5.6 %collective-permute-start.30 = (f32[4096]{0:T(1024)S(1)}, f32[4096]{0:T(1024)S(1)}, u32[]{:S(2)}, u32[]{:S(2)}) collective-permute-start(f32[4096]{0:T(1024)S(1)} %bitcast.38), channel_id=1, source_target_pairs={{0,6},{1,7},{2,4},{3,5},{4,2},{5,3},{6,0},{7,1},{8,14},{9,15},{10,... | collective-permute-start | bytes 49160 | tf_op jit(solution)/shard_map/ppermute | solution.py:515
  125.7 4.7 %collective-permute-start.29 = (f32[4096]{0:T(1024)S(1)}, f32[4096]{0:T(1024)S(1)}, u32[]{:S(2)}, u32[]{:S(2)}) collective-permute-start(f32[4096]{0:T(1024)S(1)} %bitcast.39), channel_id=1, source_target_pairs={{0,4},{1,5},{2,6},{3,7},{4,0},{5,1},{6,2},{7,3},{8,12},{9,13},{10,... | collective-permute-start | bytes 49160 | tf_op jit(solution)/shard_map/ppermute | solution.py:515
  126.7 3.9 %collective-permute-start.28 = (f32[4096]{0:T(1024)S(1)}, f32[4096]{0:T(1024)S(1)}, u32[]{:S(2)}, u32[]{:S(2)}) collective-permute-start(f32[4096]{0:T(1024)S(1)} %bitcast.40), channel_id=1, source_target_pairs={{0,2},{1,3},{2,0},{3,1},{4,6},{5,7},{6,4},{7,5},{8,10},{9,11},{10,... | collective-permute-start | bytes 49160 | tf_op jit(solution)/shard_map/ppermute | solution.py:515
  136.1 2.1 %collective-permute-start.31 = (bf16[2048,128]{1,0:T(8,128)(2,1)S(1)}, bf16[2048,128]{1,0:T(8,128)(2,1)S(1)}, u32[]{:S(2)}, u32[]{:S(2)}) collective-permute-start(bf16[2048,128]{1,0:T(8,128)(2,1)S(1)} %get-tuple-element.64), channel_id=1, source_target_pairs={{0,8},{1,9},{2,10},{3,11},{4,12},{5,13},{6,14},{7,15},{8,0},{9,1},... | collective-permute-start | bytes 1572872 | tf_op jit(solution)/shard_map/ppermute | solution.py:515
  138.3 8.2 %collective-permute-start.32 = (bf16[512,128]{1,0:T(8,128)(2,1)S(1)}, bf16[512,128]{1,0:T(8,128)(2,1)S(1)}, u32[]{:S(2)}, u32[]{:S(2)}) collective-permute-start(bf16[512,128]{1,0:T(8,128)(2,1)S(1)} %get-tuple-element.74), channel_id=1, source_target_pairs={{0,2},{1,3},{2,0},{3,1},{4,6},{5,7},{6,4},{7,5},{8,10},{9,11},{10,... | collective-permute-start | bytes 393224 | tf_op jit(solution)/shard_map/ppermute | solution.py:515
  139.6 12.9 %collective-permute-start.36 = (bf16[512,128]{1,0:T(8,128)(2,1)S(1)}, bf16[512,128]{1,0:T(8,128)(2,1)S(1)}, u32[]{:S(2)}, u32[]{:S(2)}) collective-permute-start(bf16[512,128]{1,0:T(8,128)(2,1)S(1)} %get-tuple-element.80), channel_id=1, source_target_pairs={{0,4},{1,5},{2,6},{3,7},{4,0},{5,1},{6,2},{7,3},{8,12},{9,13},{10,... | collective-permute-start | bytes 393224 | tf_op jit(solution)/shard_map/ppermute | solution.py:515
  140.7 11.8 %collective-permute-start.37 = (bf16[512,128]{1,0:T(8,128)(2,1)S(1)}, bf16[512,128]{1,0:T(8,128)(2,1)S(1)}, u32[]{:S(2)}, u32[]{:S(2)}) collective-permute-start(bf16[512,128]{1,0:T(8,128)(2,1)S(1)} %get-tuple-element.81), channel_id=1, source_target_pairs={{0,6},{1,7},{2,4},{3,5},{4,2},{5,3},{6,0},{7,1},{8,14},{9,15},{10,... | collective-permute-start | bytes 393224 | tf_op jit(solution)/shard_map/ppermute | solution.py:515
  146.4 6.8 %collective-permute-start.33 = (bf16[512,128]{1,0:T(8,128)(2,1)S(1)}, bf16[512,128]{1,0:T(8,128)(2,1)S(1)}, u32[]{:S(2)}, u32[]{:S(2)}) collective-permute-start(bf16[512,128]{1,0:T(8,128)(2,1)S(1)} %get-tuple-element.75), channel_id=1, source_target_pairs={{0,1},{1,0},{2,3},{3,2},{4,5},{5,4},{6,7},{7,6},{8,9},{9,8},{10,11... | collective-permute-start | bytes 393224 | tf_op jit(solution)/shard_map/ppermute | solution.py:515
  147.8 6.1 %collective-permute-start.34 = (bf16[512,128]{1,0:T(8,128)(2,1)S(1)}, bf16[512,128]{1,0:T(8,128)(2,1)S(1)}, u32[]{:S(2)}, u32[]{:S(2)}) collective-permute-start(bf16[512,128]{1,0:T(8,128)(2,1)S(1)} %get-tuple-element.76), channel_id=1, source_target_pairs={{0,16},{1,17},{2,18},{3,19},{4,20},{5,21},{6,22},{7,23},{8,24},{9,... | collective-permute-start | bytes 393224 | tf_op jit(solution)/shard_map/ppermute | solution.py:515
  149.0 6.8 %collective-permute-start.35 = (bf16[512,128]{1,0:T(8,128)(2,1)S(1)}, bf16[512,128]{1,0:T(8,128)(2,1)S(1)}, u32[]{:S(2)}, u32[]{:S(2)}) collective-permute-start(bf16[512,128]{1,0:T(8,128)(2,1)S(1)} %get-tuple-element.77), channel_id=1, source_target_pairs={{0,17},{1,16},{2,19},{3,18},{4,21},{5,20},{6,23},{7,22},{8,25},{9,... | collective-permute-start | bytes 393224 | tf_op jit(solution)/shard_map/ppermute | solution.py:515

commit v8 on v7

v8 whole, which is shorter than its diff:
```python
import functools
import math

import jax
import jax.numpy as jnp
from jax import lax
from jax.experimental import pallas as pl
from jax.experimental.pallas import tpu as pltpu
from jax.sharding import PartitionSpec as P

D = 128
ITERS = 3
EPSILON = D / 20.0
LOG2E = math.log2(math.e)
CROSS = 2.0 * LOG2E / EPSILON
NT = (((1,), (1,)), ((), ()))
VMEM = pl.BlockSpec(memory_space=pltpu.VMEM)
HBM = pl.BlockSpec(memory_space=pltpu.HBM)
GROUP = 32


def spread(value, s_ref, sb_ref):
    chunks = value.shape[1] // 128
    for k in range(chunks):
        s_ref[k:k + 1, :] = value[:, k * 128:(k + 1) * 128]
    turned = jnp.transpose(s_ref[...])
    for k in range(chunks):
        sb_ref[k * 128:(k + 1) * 128, :] = jnp.broadcast_to(turned[:, k:k + 1], (128, 128))


def ordered(values, shifts, parts):
    share = values[0].shape[1] // parts
    return [
        jnp.concatenate([value[:, (k ^ s) * share:((k ^ s) + 1) * share] for k in range(parts)], axis=1)
        for value, s in zip(values, shifts)
    ]


def lse2(parts):
    top = functools.reduce(jnp.maximum, parts)
    return top + jnp.log2(sum(jnp.exp2(part - top) for part in parts))


def pipelined(places, chunk, width, a_ref, b_ref, d_ref, tile, finish):
    last = b_ref.shape[0] // width - 1

    def product(n, m):
        b = b_ref[pl.ds(pl.multiple_of(n * width, width), width), :]
        a = a_ref[places[m]:places[m] + chunk, :]
        d_ref[m % 2] = lax.dot_general(a, b, NT, preferred_element_type=jnp.float32)

    product(0, 0)

    def column(n, _):
        start = pl.multiple_of(n * width, width)
        state = None
        for m in range(len(places)):
            if m + 1 < len(places):
                product(n, m + 1)
            else:
                product(jnp.minimum(n + 1, last), 0)
            state = tile(m, start, state)
        finish(start, state)
        return 0

    lax.fori_loop(0, last + 1, column, 0)


def running_max(places, chunk, width, a_ref, b_ref, sb_ref, o_ref, e_ref, shift_ref):
    def column(n, _):
        start = pl.multiple_of(n * width, width)
        b = b_ref[pl.ds(start, width), :]

        def exponents(at):
            d = lax.dot_general(a_ref[at:at + chunk, :], b, NT, preferred_element_type=jnp.float32)
            s = sb_ref[at:at + chunk, :]
            return [d[:, q * 128:(q + 1) * 128] * CROSS + s for q in range(width // 128)]

        peak, total = jnp.full((1, width), -1e30, jnp.float32), jnp.zeros((1, width), jnp.float32)
        for at in places:
            peaks, totals = [], []
            for q, t in enumerate(exponents(at)):
                old = peak[:, q * 128:(q + 1) * 128]
                new = jnp.maximum(old, jnp.max(t, axis=0, keepdims=True))
                part = jnp.sum(jnp.exp2(t - new), axis=0, keepdims=True)
                peaks.append(new)
                totals.append(total[:, q * 128:(q + 1) * 128] * jnp.exp2(old - new) + part)
            peak, total = jnp.concatenate(peaks, axis=1), jnp.concatenate(totals, axis=1)
        o_ref[:, pl.ds(start, width)] = peak + jnp.log2(total)
        if e_ref is not None:
            shift_ref[:, pl.ds(start, width)] = peak
            for at in places:
                for q, t in enumerate(exponents(at)):
                    place = pl.ds(pl.multiple_of(start + q * 128, 128), 128)
                    e_ref[at:at + chunk, place] = jnp.exp2(t - shift_ref[:, place]).astype(jnp.bfloat16)
        return 0

    lax.fori_loop(0, b_ref.shape[0] // width, column, 0)


def lse_pass(places, chunk, width, a_ref, b_ref, sb_ref, d_ref, top_ref, o_ref, e_ref=None, shift_ref=None):
    tiles = width // 128
    top_ref[...] = jnp.zeros_like(top_ref)

    def lanes_of(start, q):
        return pl.ds(pl.multiple_of(start + q * 128, 128), 128)

    def tile(m, start, state):
        def exponents(g, q):
            at = g * GROUP
            s = sb_ref[places[m] + at:places[m] + at + GROUP, :]
            return d_ref[m % 2, at:at + GROUP, q * 128:(q + 1) * 128] * CROSS + s

        if m == 0:
            tops = [exponents(0, q) for q in range(tiles)]
            for g in range(1, 128 // GROUP):
                tops = [jnp.maximum(top, exponents(g, q)) for q, top in enumerate(tops)]
            state = [(jnp.max(top, axis=0, keepdims=True), jnp.zeros((GROUP, 128), jnp.float32)) for top in tops]
        for g in range(chunk // GROUP):
            for q, (peak, total) in enumerate(state):
                e = jnp.exp2(exponents(g, q) - peak)
                if e_ref is not None:
                    at = places[m] + g * GROUP
                    e_ref[at:at + GROUP, lanes_of(start, q)] = e.astype(jnp.bfloat16)
                state[q] = peak, total + e
        return state

    def finish(start, state):
        for q, (peak, total) in enumerate(state):
            top_ref[...] = jnp.maximum(top_ref[...], total)
            o_ref[:, lanes_of(start, q)] = peak + jnp.log2(jnp.sum(total, axis=0, keepdims=True))
            if e_ref is not None:
                shift_ref[:, lanes_of(start, q)] = peak

    pipelined(places, chunk, width, a_ref, b_ref, d_ref, tile, finish)

    @pl.when(jnp.logical_not(jnp.max(top_ref[...]) < 2.0 ** 60))
    def _():
        running_max(places, chunk, min(width, 256), a_ref, b_ref, sb_ref, o_ref, e_ref, shift_ref)


def pair_copies(o_ref, at, mass_ref, axis, sem):
    share = (o_ref.shape[1] - at) // 2
    place = lax.axis_index(axis)
    copies = []
    for k in range(2):
        start = pl.multiple_of((place ^ k) * share, share)
        there = o_ref.at[:, at + k * share:at + (k + 1) * share]
        copies.append(pltpu.make_async_copy(mass_ref.at[:, pl.ds(start, share)], there, sem.at[k]))
    return copies


def fill(out_ref, own_ref, others, sem):
    share = own_ref.shape[0]
    copy = pltpu.make_async_copy(own_ref, out_ref.at[pl.ds(0, share), :], sem)
    copy.start()
    for k, shard in enumerate(others):
        out_ref[(k + 1) * share:(k + 2) * share, :] = shard[...]
    return copy


def put_norms(places, share, y_ref, sb_ref):
    for at in places:
        y = y_ref[at:at + share, :].astype(jnp.float32)
        total = jnp.sum(y * y, axis=1, keepdims=True) * (-LOG2E / EPSILON)
        sb_ref[at:at + share, :] = jnp.broadcast_to(total, (share, 128))


def row_lse_early_kernel(width, nx, x_own, y_own, *refs):
    xs, y_other, refs = refs[:nx], refs[nx], refs[nx + 1:]
    x_ref, xt_ref, o_ref, y_ref, sb_ref, d_ref, top_ref, sem = refs
    share = y_own.shape[0]
    copies = [fill(x_ref, x_own, xs, sem.at[0]), fill(y_ref, y_own, [y_other], sem.at[1])]
    for copy in copies:
        copy.wait()
    for k in range(x_ref.shape[0] // 128):
        at = k * 128
        xt_ref[:, at:at + 128] = jnp.transpose(x_ref[at:at + 128, :].astype(jnp.float32)).astype(jnp.bfloat16)
    places = [0, share]
    put_norms(places, share, y_ref, sb_ref)
    lse_pass(places, share, width, y_ref, x_ref, sb_ref, d_ref, top_ref, o_ref)


def row_lse_late_kernel(width, ny, y_own, mass_ref, x_ref, first_ref, *refs):
    ys, (y_ref, o_ref, sb_ref, d_ref, top_ref, sum_ref, sem) = refs[:ny], refs[ny:]
    share, rows = y_own.shape[0], x_ref.shape[0]
    copies = [fill(y_ref, y_own, ys, sem.at[2])]
    masses = pair_copies(o_ref, rows, mass_ref, "col", sem)
    for copy in masses:
        copy.start()
    places = [k * share for k in range(ny + 1) if k % ((ny + 1) // 2)]
    put_norms(places, share, y_ref, sb_ref)
    lse_pass(places, share, width, y_ref, x_ref, sb_ref, d_ref, top_ref, sum_ref)
    o_ref[:, :rows] = lse2([first_ref[...], sum_ref[...]])
    for copy in copies + masses:
        copy.wait()


def column_lse_kernel(width, chunk, na, x_ref, y_ref, mass_ref, *refs):
    got, (o_ref, e_ref, shift_ref, a_ref, s_ref, sb_ref, d_ref, top_ref, sem) = refs[:na], refs[na:]
    rows, cols = x_ref.shape[0], y_ref.shape[0]
    masses = pair_copies(o_ref, cols, mass_ref, "row", sem)
    for copy in masses:
        copy.start()
    share = rows // na
    for k in range(na):
        at = rows + (k % 2) * share
        a_ref[:, k * share:(k + 1) * share] = got[k - k % 2][:, at:at + share]
    u = jnp.log2(a_ref[...]) - lse2(ordered([part[:, :rows] for part in got], range(na), na))
    spread(u, s_ref, sb_ref)
    places = list(range(0, rows, chunk))
    lse_pass(places, chunk, width, x_ref, y_ref, sb_ref, d_ref, top_ref, o_ref, e_ref, shift_ref)
    for copy in masses:
        copy.wait()


def pair_kernel(size, shift, parts, combine, one_ref, two_ref, o_ref):
    two, = ordered([two_ref[:, :size]], [shift], parts)
    o_ref[:, :size] = combine([one_ref[:, :size], two])
    if o_ref.shape[1] > size:
        o_ref[:, size:] = one_ref[:, size:]


def split3(value):
    high = value.astype(jnp.bfloat16)
    rest = value - high.astype(jnp.float32)
    mid = rest.astype(jnp.bfloat16)
    return high, mid, (rest - mid.astype(jnp.float32)).astype(jnp.bfloat16)


def stacked(value):
    high, mid, low = [part.astype(jnp.float32) for part in split3(value)]
    dims = (16, value.shape[1])
    place = lax.broadcasted_iota(jnp.int32, dims, 0)
    parts = jnp.where(place == 0, high, jnp.where(place == 1, mid, jnp.where(place == 2, low, 0.0)))
    return parts.astype(jnp.bfloat16)


def row_sums(width, e_ref, w16_ref, o_ref):
    for at in range(0, e_ref.shape[0], width):
        got = lax.dot_general(w16_ref[...], e_ref[at:at + width, :], NT, preferred_element_type=jnp.float32)
        got = jnp.sum(got, axis=0, keepdims=True)
        if len(o_ref.shape) == 2:
            o_ref[:, at:at + width] = got
        else:
            for k in range(o_ref.shape[0]):
                o_ref[k, :, at:at + width] = got


def received(refs):
    if len(refs) == 1 and len(refs[0].shape) == 3:
        place = ((lax.axis_index("row") >> 1) << 1) | (lax.axis_index("col") & 1)
        return [refs[0][place ^ s] for s in range(refs[0].shape[0])]
    return [ref[...] for ref in refs]


def first_row_kernel(width, shifts, parts, e_ref, shift_ref, *refs):
    nz = len(shifts)
    got, (o_ref, beta_ref, b_ref, w16_ref) = refs[:nz], refs[nz:]
    cols = e_ref.shape[1]
    share = cols // parts
    for k in range(parts):
        at = cols + (k // nz) * share
        b_ref[:, k * share:(k + 1) * share] = got[k % nz][:, at:at + share]
    lse = lse2(ordered([part[:, :cols] for part in got], shifts, parts))
    beta_ref[...] = jnp.exp2(jnp.log2(b_ref[...]) - lse + shift_ref[...])
    w16_ref[...] = stacked(beta_ref[...])
    row_sums(width, e_ref, w16_ref, o_ref)


def new_beta(first_ref, b_ref, got, shifts, parts):
    return first_ref[...] * (b_ref[...] / sum(ordered(received(got), shifts, parts)))


def row_kernel(width, shifts, parts, e_ref, first_ref, b_ref, *refs):
    got, (o_ref, w16_ref) = refs[:-2], refs[-2:]
    w16_ref[...] = stacked(new_beta(first_ref, b_ref, got, shifts, parts))
    row_sums(width, e_ref, w16_ref, o_ref)


def column_kernel(width, shifts, parts, e_ref, a_ref, first_ref, *refs):
    got, (o_ref, alpha_ref, w16_ref) = refs[:-3], refs[-3:]
    alpha_ref[...] = a_ref[...] / sum(ordered(received(got), shifts, parts))
    w16_ref[...] = stacked(alpha_ref[...])
    for at in range(0, e_ref.shape[1], width):
        sums = jnp.dot(w16_ref[...], e_ref[:, at:at + width], preferred_element_type=jnp.float32)
        o_ref[:, at:at + width] = first_ref[:, at:at + width] * jnp.sum(sums, axis=0, keepdims=True)


def flat(value):
    return value.reshape(1, -1) if value.ndim == 1 else value


def weighted(kernel, outs, e, rows, got, parts, width=512):
    got, shifts = got
    size = e.shape[0] if kernel is column_kernel else e.shape[1]
    return pl.pallas_call(
        functools.partial(kernel, width, tuple(shifts), parts),
        out_shape=[shape(*dims) for dims in outs],
        in_specs=[VMEM] * (1 + len(rows) + len(got)),
        out_specs=[VMEM] * len(outs),
        scratch_shapes=[pltpu.VMEM((16, size), jnp.bfloat16)],
        compiler_params=pltpu.CompilerParams(vmem_limit_bytes=16 << 20),
        cost_estimate=pl.CostEstimate(flops=2 * e.size, bytes_accessed=2 * e.size, transcendentals=0),
        name="weighted_sum",
    )(e, *rows, *[flat(part) for part in got])


def pass_cost(depth, lanes):
    return pl.CostEstimate(flops=2 * depth * lanes * D, bytes_accessed=2 * D * (depth + lanes), transcendentals=depth * lanes)


def shape(*dims, dtype=jnp.float32):
    return jax.ShapeDtypeStruct(dims, dtype)


def lse_scratch(depth, chunk, width):
    return [
        pltpu.VMEM((depth, 128), jnp.float32),
        pltpu.VMEM((2, chunk, width), jnp.float32),
        pltpu.VMEM((GROUP, 128), jnp.float32),
    ]


def row_lse_early(xs, ys, width=512):
    share_x, share = xs[0].shape[0], ys[0].shape[0]
    rows, depth = len(xs) * share_x, 2 * share
    return pl.pallas_call(
        functools.partial(row_lse_early_kernel, width, len(xs) - 1),
        out_shape=(shape(rows, D, dtype=jnp.bfloat16), shape(D, rows, dtype=jnp.bfloat16), shape(1, rows)),
        in_specs=[HBM] * 2 + [VMEM] * len(xs),
        out_specs=(VMEM,) * 3,
        scratch_shapes=[
            pltpu.VMEM((depth, D), jnp.bfloat16),
            *lse_scratch(depth, share, width),
            pltpu.SemaphoreType.DMA((2,)),
        ],
        compiler_params=pltpu.CompilerParams(vmem_limit_bytes=16 << 20),
        cost_estimate=pass_cost(depth, rows),
        name="row_lse_early",
    )(xs[0], ys[0], *xs[1:], ys[1])


def row_lse_late(x, ys, first, mass, width=512):
    rows, share = x.shape[0], ys[0].shape[0]
    depth = len(ys) * share
    tail = mass.shape[0] // lax.axis_size("col")
    return pl.pallas_call(
        functools.partial(row_lse_late_kernel, width, len(ys) - 1),
        out_shape=(shape(depth, D, dtype=jnp.bfloat16), shape(1, rows + 2 * tail)),
        in_specs=[HBM] * 2 + [VMEM] * (len(ys) + 1),
        out_specs=(VMEM,) * 2,
        scratch_shapes=[
            *lse_scratch(depth, share, width),
            pltpu.VMEM((1, rows), jnp.float32),
            pltpu.SemaphoreType.DMA((3,)),
        ],
        compiler_params=pltpu.CompilerParams(vmem_limit_bytes=16 << 20),
        cost_estimate=pass_cost(depth - 2 * share, rows),
        name="row_lse_late",
    )(ys[0], mass.reshape(1, -1), x, first, *ys[1:])


def column_lse(x, y, mass, got, width=512, chunk=512):
    rows, cols = x.shape[0], y.shape[0]
    tail = mass.shape[0] // lax.axis_size("row")
    return pl.pallas_call(
        functools.partial(column_lse_kernel, width, chunk, len(got)),
        out_shape=(shape(1, cols + 2 * tail), shape(rows, cols, dtype=jnp.bfloat16), shape(1, cols), shape(1, rows)),
        in_specs=[VMEM] * 2 + [HBM] + [VMEM] * len(got),
        out_specs=(VMEM,) * 4,
        scratch_shapes=[
            pltpu.VMEM((rows // 128, 128), jnp.float32),
            *lse_scratch(rows, chunk, width),
            pltpu.SemaphoreType.DMA((2,)),
        ],
        compiler_params=pltpu.CompilerParams(vmem_limit_bytes=16 << 20),
        cost_estimate=pass_cost(rows, cols),
        name="column_lse",
    )(x, y, mass.reshape(1, -1), *[part.reshape(1, -1) for part in got])


def pair_of(combine, one, two, size, shift, parts):
    whole = one.shape[-1]
    return pl.pallas_call(
        functools.partial(pair_kernel, size, shift, parts, combine),
        out_shape=shape(1, whole),
        in_specs=[VMEM] * 2,
        out_specs=VMEM,
        compiler_params=pltpu.CompilerParams(vmem_limit_bytes=16 << 20),
        name="pair",
    )(one.reshape(1, whole), two.reshape(1, whole))


def high_low(value):
    high = value.astype(jnp.bfloat16)
    return high, (value - high.astype(jnp.float32)).astype(jnp.bfloat16)


def column_grad_kernel(width, own, shifts, parts, xt_ref, y_ref, e_ref, alpha_ref, first_ref, b_ref, *refs):
    got, (gc_ref, gcs_ref, beta_ref, bb_ref, cb_ref, xa_ref, s_ref, count_ref, acc_ref) = refs[:-9], refs[-9:]
    rows, cols = xt_ref.shape[1], y_ref.shape[0]
    beta_ref[...] = new_beta(first_ref, b_ref, got, shifts, parts)
    spread(beta_ref[...], s_ref, bb_ref)
    place = lax.broadcasted_iota(jnp.int32, (128, 512), 0)
    for k in range(rows // 512):
        at = k * 512
        alpha = alpha_ref[:, at:at + 512]
        high, low = high_low(xt_ref[:, at:at + 512].astype(jnp.float32) * alpha)
        first, second = high_low(alpha)
        low = jnp.where(place == 126, first.astype(jnp.float32), low.astype(jnp.float32))
        low = jnp.where(place == 127, second.astype(jnp.float32), low)
        xa_ref[:128, at:at + 512] = high
        xa_ref[128:, at:at + 512] = low.astype(jnp.bfloat16)

    lower = lax.broadcasted_iota(jnp.int32, (128, width), 0) < 126
    for k in range(cols // width):
        at = k * width
        got = jnp.dot(xa_ref[...], e_ref[:, at:at + width], preferred_element_type=jnp.float32)
        acc_ref[:, at:at + width] = got[:128] + jnp.where(lower, got[128:], 0.0)
        count_ref[:, at:at + width] = got[254:255] + got[255:256]
    spread(count_ref[...], s_ref, cb_ref)
    for k in range(cols // 128):
        at = k * 128
        pulled = jnp.transpose(acc_ref[:, at:at + 128])
        whole = cb_ref[at:at + 128, :] * y_ref[at:at + 128, :].astype(jnp.float32)
        grad = 2.0 * bb_ref[at:at + 128, :] * (whole - pulled)
        if at < own:
            gc_ref[at:at + 128, :] = grad
        else:
            gcs_ref[at - own:at - own + 128, :] = grad.astype(jnp.bfloat16)


def column_grad(xt, y, e, alpha, first, mass, got, parts, own, width=512):
    rows, cols = xt.shape[1], y.shape[0]
    got, shifts = got
    return pl.pallas_call(
        functools.partial(column_grad_kernel, width, own, tuple(shifts), parts),
        out_shape=(shape(own, D), shape(cols - own, D, dtype=jnp.bfloat16), shape(1, cols)),
        in_specs=[VMEM] * (6 + len(got)),
        out_specs=(VMEM,) * 3,
        scratch_shapes=[
            pltpu.VMEM((cols, 128), jnp.float32),
            pltpu.VMEM((cols, 128), jnp.float32),
            pltpu.VMEM((256, rows), jnp.bfloat16),
            pltpu.VMEM((cols // 128, 128), jnp.float32),
            pltpu.VMEM((1, cols), jnp.float32),
            pltpu.VMEM((128, cols), jnp.float32),
        ],
        compiler_params=pltpu.CompilerParams(vmem_limit_bytes=16 << 20),
        cost_estimate=pl.CostEstimate(flops=4 * e.size * D, bytes_accessed=2 * e.size, transcendentals=0),
        name="column_grad",
    )(xt, y, e, alpha, first, mass, *[flat(part) for part in got])


def row_block(at, chunk, x_ref, e_ref, yb_ref, scale):
    got = jnp.dot(e_ref[pl.ds(at, chunk), :], yb_ref[...], preferred_element_type=jnp.float32)
    lower = lax.broadcasted_iota(jnp.int32, (chunk, 128), 1) < 126
    total = got[:, 254:255] + got[:, 255:256]
    pulled = got[:, :128] + jnp.where(lower, got[:, 128:], 0.0)
    x = x_ref[pl.ds(at, chunk), :].astype(jnp.float32)
    return 2.0 * scale * (total * x - pulled)


def put_yb(y_ref, beta_ref, yb_ref, s_ref, bb_ref):
    spread(beta_ref[...], s_ref, bb_ref)
    place = lax.broadcasted_iota(jnp.int32, (256, 128), 1)
    for at in range(0, y_ref.shape[0], 256):
        beta = bb_ref[at:at + 256, :]
        high, low = high_low(y_ref[at:at + 256, :].astype(jnp.float32) * beta)
        first, second = high_low(beta)
        low = jnp.where(place == 126, first.astype(jnp.float32), low.astype(jnp.float32))
        low = jnp.where(place == 127, second.astype(jnp.float32), low)
        yb_ref[at:at + 256, :128] = high
        yb_ref[at:at + 256, 128:] = low.astype(jnp.bfloat16)


def row_parts(parts, x_ref, e_ref, alpha_ref, yb_ref, outs, sa_ref, ab_ref):
    share = outs[0].shape[0]
    chunk = math.gcd(share, 512)
    for part, out_ref in zip(parts, outs):
        spread(alpha_ref[:, part * share:(part + 1) * share], sa_ref, ab_ref)
        for k in range(0, share, chunk):
            grad = row_block(part * share + k, chunk, x_ref, e_ref, yb_ref, ab_ref[k:k + chunk, :])
            out_ref[k:k + chunk, :] = grad.astype(out_ref.dtype)


def first_rows_kernel(parts, x_ref, y_ref, e_ref, alpha_ref, beta_ref, *refs):
    yb_ref, outs, (s_ref, bb_ref, sa_ref, ab_ref) = refs[0], refs[1:-4], refs[-4:]
    put_yb(y_ref, beta_ref, yb_ref, s_ref, bb_ref)
    row_parts(parts, x_ref, e_ref, alpha_ref, yb_ref, outs, sa_ref, ab_ref)


def rows_kernel(parts, x_ref, yb_ref, e_ref, alpha_ref, *refs):
    row_parts(parts, x_ref, e_ref, alpha_ref, yb_ref, refs[:-2], *refs[-2:])


def rows_scratch(share):
    return [pltpu.VMEM((share // 128, 128), jnp.float32), pltpu.VMEM((share, 128), jnp.float32)]


def rows_cost(share, parts, cols):
    size = share * len(parts) * cols
    return pl.CostEstimate(flops=4 * size * D, bytes_accessed=2 * size, transcendentals=0)


def first_rows(parts, share, x, y, e, alpha, beta):
    cols = y.shape[0]
    return pl.pallas_call(
        functools.partial(first_rows_kernel, parts),
        out_shape=[shape(cols, 256, dtype=jnp.bfloat16)] + [shape(share, D, dtype=jnp.bfloat16)] * len(parts),
        in_specs=[VMEM] * 5,
        out_specs=[VMEM] * (1 + len(parts)),
        scratch_shapes=[
            pltpu.VMEM((cols // 128, 128), jnp.float32),
            pltpu.VMEM((cols, 128), jnp.float32),
            *rows_scratch(share),
        ],
        compiler_params=pltpu.CompilerParams(vmem_limit_bytes=16 << 20),
        cost_estimate=rows_cost(share, parts, cols),
        name="first_rows",
    )(x, y, e, alpha, beta)


def other_rows(parts, share, x, yb, e, alpha, dtype):
    return pl.pallas_call(
        functools.partial(rows_kernel, parts),
        out_shape=[shape(share, D, dtype=dtype)] * len(parts),
        in_specs=[VMEM] * 4,
        out_specs=[VMEM] * len(parts),
        scratch_shapes=rows_scratch(share),
        compiler_params=pltpu.CompilerParams(vmem_limit_bytes=16 << 20),
        cost_estimate=rows_cost(share, parts, yb.shape[0]),
        name="other_rows",
    )(x, yb, e, alpha)


def add_up_kernel(na, *refs):
    ins, outs = refs[:-2], refs[-2:]
    for out_ref, parts in zip(outs, (ins[:na], ins[na:])):
        out_ref[...] = sum(part[...].astype(jnp.float32) for part in parts)


def add_up(rows, columns):
    return pl.pallas_call(
        functools.partial(add_up_kernel, len(rows)),
        out_shape=(shape(*rows[0].shape), shape(*columns[0].shape)),
        in_specs=[VMEM] * (len(rows) + len(columns)),
        out_specs=(VMEM,) * 2,
        compiler_params=pltpu.CompilerParams(vmem_limit_bytes=16 << 20),
        name="add_up",
    )(*rows, *columns)


def shares_kernel(gc_ref, other_ref, own_ref, *outs):
    share = own_ref.shape[0]
    for k in range(len(outs) + 1):
        at = k * share
        total = gc_ref[at:at + share, :] + other_ref[at:at + share, :].astype(jnp.float32)
        if k == 0:
            own_ref[...] = total
        else:
            outs[k - 1][...] = total.astype(jnp.bfloat16)


def shares(gc, other, count):
    share = gc.shape[0] // count
    return pl.pallas_call(
        shares_kernel,
        out_shape=[shape(share, D)] + [shape(share, D, dtype=jnp.bfloat16)] * (count - 1),
        in_specs=[VMEM] * 2,
        out_specs=[VMEM] * count,
        compiler_params=pltpu.CompilerParams(vmem_limit_bytes=16 << 20),
        name="shares",
    )(gc, other)


class Groups:
    def __init__(self, nrow, ncol):
        self.count = nrow * ncol
        self.across = [(a << 1) * ncol + b for a in range(nrow // 2) for b in range(2)]
        self.along = [z << 1 for z in range(ncol // 2)]
        self.core = ncol
        self.squares = [
            [(a * 2 + core) * ncol + z * 2 + b for a in range(nrow // 2) for b in range(2)]
            for core in range(2) for z in range(ncol // 2)
        ]

    def swap(self, value, mask):
        if mask == 0:
            return value
        return lax.ppermute(value, ("row", "col"), [(i, i ^ mask) for i in range(self.count)])


def local(imu, camera, imu_mass, cam_mass):
    nrow, ncol = lax.axis_size("row"), lax.axis_size("col")
    groups = Groups(nrow, ncol)
    swap, across, along, core = groups.swap, groups.across, groups.along, groups.core
    na, nz = len(across), len(along)
    share_x, share_y = imu.shape[0], camera.shape[1]
    rows, cols = na * share_x, 2 * nz * share_y

    def direct(value, masks):
        return [swap(value, mask) for mask in masks], range(len(masks))

    def halved(value, masks, parts):
        size, bit = value.shape[-1], len(masks) // 2
        while bit > 1:
            value = pair_of(sum, value, swap(value.reshape(-1), masks[bit]), size, bit, parts).reshape(-1)
            bit //= 2
        return [value, swap(value, masks[1])], (0, 1)

    near, far = [camera[0]], [swap(camera[0], core)]
    for z in range(1, nz):
        near.append(swap(near[z & (z - 1)], along[z & -z]))
    xs, _ = direct(imu, across)

    x, xt, first = row_lse_early(xs, [near[0], far[0]])
    rest = lax.optimization_barrier((first, *near[1:]))
    far += [swap(part, core) for part in rest[1:]]
    y, sent = row_lse_late(x, [near[0], *rest[1:], *far], rest[0], imu_mass)
    got, _ = direct(sent.reshape(-1), across)

    sent, e, shift, mass_a = column_lse(x, y, cam_mass, got)
    sent = pair_of(lse2, sent, swap(sent.reshape(-1), core), cols, 1, 2)
    got = direct(sent.reshape(-1), along)

    sums, first_beta, mass_b = weighted(
        first_row_kernel, [(na, 1, rows), (1, cols), (1, cols)], e, [shift], got, 2 * nz)
    for step in range(1, ITERS):
        if step == 1:
            got = [lax.all_to_all(sums, ("row", "col"), 0, 0, axis_index_groups=groups.squares)], range(na)
        else:
            sums, = weighted(row_kernel, [(1, rows)], e, [first_beta, mass_b], got, 2 * nz)
            got = halved(sums.reshape(-1), across, na)
        part, alpha = weighted(column_kernel, [(1, cols), (1, rows)], e, [mass_a, first_beta], got, na)
        part = pair_of(sum, part, swap(part.reshape(-1), core), cols, 1, 2).reshape(-1)
        got = halved(part, along, 2 * nz) if step == 1 else direct(part, along)

    gc, gc_send, beta = column_grad(xt, y, e, alpha, first_beta, mass_b, got, 2 * nz, nz * share_y)
    yb, last = first_rows([na - 1], share_x, x, y, e, alpha, beta)
    (grad_cam, *parts), yb = lax.optimization_barrier((shares(gc, swap(gc_send, core), nz), yb))
    parts = [swap(part, along[z + 1]) for z, part in enumerate(parts)]
    sent = [*other_rows(list(range(1, na - 1)), share_x, x, yb, e, alpha, jnp.bfloat16), last]
    sent, parts[0] = lax.optimization_barrier((sent, parts[0]))
    sent = [swap(part, across[s + 1]) for s, part in enumerate(sent)]
    gi, = other_rows([0], share_x, x, yb, e, alpha, jnp.float32)
    grad_imu, grad_cam = add_up([gi, *sent], [grad_cam, *parts])
    return grad_imu, grad_cam[None]


def solution(mesh):
    in_specs = (P(("row", "col"), None), P("col", "row", None), P("row"), P("col"))
    out_specs = (P(("row", "col"), None), P("col", "row", None))
    return jax.shard_map(local, mesh=mesh, in_specs=in_specs, out_specs=out_specs, check_vma=False)
```

time: 157 us -> 159 us (1.013)
  blocking collectives: 0 us -> 7.83 us
  starting transfers between devices: 42.5 us -> 35.5 us
  waiting for transfers between devices: 28.7 us -> 31.3 us
    all_to_all x0 -> x1, blocking collectives: none -> 7.83 us  [local(): lax.all_to_all(sums, ('row', 'col'), 0, 0, axis_index_groups=groups.squares)]
    ppermute x38 -> x33, starting transfers between devices: 42.5 us -> 35.5 us  [swap(): lax.ppermute(value, ('row', 'col'), [(i, i ^ mask) for i in range(self.co...]
    ppermute x38 -> x33, waiting for transfers between devices: 28.7 us -> 31.3 us  [swap(): lax.ppermute(value, ('row', 'col'), [(i, i ^ mask) for i in range(self.co...]
    pallas_call x12 -> x16, Pallas kernels: 48.9 us -> 47.9 us  [the longest x1 14.1 us: row_lse_late(): pl.pallas_call(functools.partial(row_lse_late_kernel, width, len(ys) - 1)...]
    unnamed x8 -> x10, local copies, waits for them, and re-layouts: 3.22 us -> 4.13 us
  transfers between devices with their start and end apart: 38 -> 33, of which waited for: 27 -> 22; matrix products, arithmetic and copies ran while one was open for 0% -> 0% of each run, Pallas kernels for 8% -> 8%
where the time goes in v8:
time: 159 us; the launch traced here: 158 us
  Pallas kernels  78.9 us (50%)
  starting transfers between devices  35.5 us (22%)
  waiting for transfers between devices  31.3 us (20%)
  blocking collectives  7.83 us (5%)
  local copies, waits for them, and re-layouts  4.13 us (3%)
    ppermute x33, starting transfers between devices, swap(): lax.ppermute(value, ('row', 'col'), [(i, i ^ mask) for i in range(self.co...  35.5 us
    ppermute x33, waiting for transfers between devices, swap(): lax.ppermute(value, ('row', 'col'), [(i, i ^ mask) for i in range(self.co...  31.3 us
    pallas_call x1, Pallas kernels, column_lse(): pl.pallas_call(functools.partial(column_lse_kernel, width, chunk, len(got...  30.9 us
    pallas_call x1, Pallas kernels, row_lse_late(): pl.pallas_call(functools.partial(row_lse_late_kernel, width, len(ys) - 1)...  14.1 us
    pallas_call x4, Pallas kernels, weighted(): pl.pallas_call(functools.partial(kernel, width, tuple(shifts), parts), ou...  14 us
    all_to_all x1, blocking collectives, local(): lax.all_to_all(sums, ('row', 'col'), 0, 0, axis_index_groups=groups.squares)  7.83 us
    pallas_call x1, Pallas kernels, row_lse_early(): pl.pallas_call(functools.partial(row_lse_early_kernel, width, len(xs) - 1...  7.01 us
    pallas_call x1, Pallas kernels, column_grad(): pl.pallas_call(functools.partial(column_grad_kernel, width, own, tuple(sh...  5.52 us
  transfers between devices with their start and end apart: 33, of which 22 were waited for; matrix products, arithmetic and copies ran while one was open for 0% of the time, Pallas kernels for 8%

profile of v8, /device:TPU:0, one launch (start us, length us, event | category | flops | bytes accessed | tf_op | source)
XLA Modules:
  0.0 158.4 jit_solution(10959749186544313827)
XLA Ops:
  0.6 4.1 %collective-permute-start.5 = (bf16[512,128]{1,0:T(8,128)(2,1)}, bf16[512,128]{1,0:T(8,128)(2,1)S(1)}, u32[]{:S(2)}, u32[]{:S(2)}) collective-permute-start(bf16[512,128]{1,0:T(8,128)(2,1)} %bitcast.56), channel_id=1, source_target_pairs={{0,4},{1,5},{2,6},{3,7},{4,0},{5,1},{6,2},{7,3},{8,12},{9,13},{10,... | collective-permute-start | bytes 393224 | tf_op jit(solution)/shard_map/ppermute | solution.py:592
  4.7 1.5 collective-permute-start.1
  6.2 1.5 collective-permute-start
  8.2 3.0 %collective-permute-done.5.refs_1_ = bf16[512,128]{1,0:T(8,128)(2,1)S(1)} collective-permute-done((bf16[512,128]{1,0:T(8,128)(2,1)}, bf16[512,128]{1,0:T(8,128)(2,1)S(1)}, u32[]{:S(2)}, u32[]{:S(2)}) %collective-permute-start.5) | collective-permute-done | bytes 131104 | tf_op jit(solution)/shard_map/ppermute | solution.py:592
  11.2 0.8 collective-permute-start.4
  12.1 1.2 collective-permute-start.6
  13.3 1.6 %collective-permute-done.refs_0_ = bf16[512,128]{1,0:T(8,128)(2,1)S(1)} collective-permute-done((bf16[512,128]{1,0:T(8,128)(2,1)}, bf16[512,128]{1,0:T(8,128)(2,1)S(1)}, u32[]{:S(2)}, u32[]{:S(2)}) %collective-permute-start) | collective-permute-done | bytes 131104 | tf_op jit(solution)/shard_map/ppermute | solution.py:592
  14.9 0.9 copy-done
  15.8 0.9 copy-done.1
  16.7 7.0 %row_lse_early.1 = (bf16[2048,128]{1,0:T(8,128)(2,1)S(1)}, bf16[128,2048]{1,0:T(8,128)(2,1)S(1)}, f32[1,2048]{1,0:T(1,128)S(1)}) custom-call(bf16[512,128]{1,0:T(8,128)(2,1)S(1)} %copy-done, bf16[512,128]{1,0:T(8,128)(2,1)S(1)} %bitcast.59, bf16[512,128]{1,0:T(8,128)(2,1)S(1)} %collective-permute-done.refs_0_, ...), custom_call_target="tpu_custom_call" | custom-call | flops 536870912 | bytes 786432 | tf_op jit(solution)/shard_map/row_lse_early/pallas_call | solution.py:328
  25.7 0.9 copy-done.2
  27.3 14.1 %row_lse_late.1 = (bf16[4096,128]{1,0:T(8,128)(2,1)S(1)}, f32[1,3072]{1,0:T(1,128)S(1)}) custom-call(bf16[512,128]{1,0:T(8,128)(2,1)S(1)} %bitcast.60, f32[1,4096]{1,0:T(1,128)S(1)} %bitcast.61, bf16[2048,128]{1,0:T(8,128)(2,1)S(1)} %get-tuple-element.43.x_ref, f32[1,2048]{1,0:T(1,128)S(1)} %get-tuple-element.46.first_ref, ...), custom_call_target="tpu_custom_call" | custom-call | flops 1610612736 | bytes 1310720 | tf_op jit(solution)/shard_map/row_lse_late/pallas_call | solution.py:348
  41.5 3.4 %collective-permute-start.10 = (f32[3072]{0:T(1024)S(1)}, f32[3072]{0:T(1024)S(1)}, u32[]{:S(2)}, u32[]{:S(2)}) collective-permute-start(f32[3072]{0:T(1024)S(1)} %bitcast.64), channel_id=1, source_target_pairs={{0,1},{1,0},{2,3},{3,2},{4,5},{5,4},{6,7},{7,6},{8,9},{9,8},{10,11... | collective-permute-start | bytes 36872 | tf_op jit(solution)/shard_map/ppermute | solution.py:592
  44.9 1.1 collective-permute-done.12
  47.3 30.9 %column_lse.1 = (f32[1,5120]{1,0:T(1,128)S(1)}, bf16[2048,4096]{1,0:T(8,128)(2,1)S(1)}, f32[1,4096]{1,0:T(1,128)S(1)}, f32[1,2048]{1,0:T(1,128)S(1)}) custom-call(bf16[2048,128]{1,0:T(8,128)(2,1)S(1)} %get-tuple-element.43.x_ref, bf16[4096,128]{1,0:T(8,128)(2,1)S(1)} %get-tuple-element.50.y_ref, f32[1,2048]{1,0:T(1,128)S(1)} %bitcast.68, ...), custom_call_target="tpu_custom_call" | custom-call | flops 2147483648 | bytes 1572864 | tf_op jit(solution)/shard_map/column_lse/pallas_call | solution.py:367
  78.2 1.2 collective-permute-done.13
  79.5 2.1 %collective-permute-start.16 = (f32[5120]{0:T(1024)S(1)}, f32[5120]{0:T(1024)S(1)}, u32[]{:S(2)}, u32[]{:S(2)}) collective-permute-start(f32[5120]{0:T(1024)S(1)} %bitcast.30), channel_id=1, source_target_pairs={{0,6},{1,7},{2,4},{3,5},{4,2},{5,3},{6,0},{7,1},{8,14},{9,15},{10,... | collective-permute-start | bytes 61448 | tf_op jit(solution)/shard_map/ppermute | solution.py:592
  81.8 2.1 %collective-permute-start.14 = (f32[5120]{0:T(1024)S(1)}, f32[5120]{0:T(1024)S(1)}, u32[]{:S(2)}, u32[]{:S(2)}) collective-permute-start(f32[5120]{0:T(1024)S(1)} %bitcast.32), channel_id=1, source_target_pairs={{0,2},{1,3},{2,0},{3,1},{4,6},{5,7},{6,4},{7,5},{8,10},{9,11},{10,... | collective-permute-start | bytes 61448 | tf_op jit(solution)/shard_map/ppermute | solution.py:592
  83.9 1.4 collective-permute-done.16
  85.3 1.1 collective-permute-done.15
  86.5 4.5 %weighted_sum.4 = (f32[4,1,2048]{2,1,0:T(1,128)S(1)}, f32[1,4096]{1,0:T(1,128)S(1)}, f32[1,4096]{1,0:T(1,128)S(1)}) custom-call(bf16[2048,4096]{1,0:T(8,128)(2,1)S(1)} %get-tuple-element.52.e_ref, f32[1,4096]{1,0:T(1,128)S(1)} %get-tuple-element.54.shift_ref, f32[1,5120]{1,0:T(1,128)S(1)} %pair.5.refs_0_, f32[1,5120]{1,0:T(1,128)S(1)} %bitcast.42, ...), custom_call_target="tpu_custom_call" | custom-call | flops 16777216 | bytes 16777216 | tf_op jit(solution)/shard_map/weighted_sum/pallas_call | solution.py:297
  90.9 7.8 %all_to_all.5.refs_0_ = f32[4,1,2048]{2,1,0:T(1,128)S(1)} all-to-all(f32[4,1,2048]{2,1,0:T(1,128)S(1)} %get-tuple-element.58), channel_id=1, replica_groups={{0,1,16,17},{2,3,18,19},{4,5,20,21},{6,7,22,23},{8,9,24,25},{10,11,26,2..., dimensions={0} | all-to-all | bytes 65536 | tf_op jit(solution)/shard_map/all_to_all | solution.py:632
  98.8 2.8 %weighted_sum.5 = (f32[1,4096]{1,0:T(1,128)S(1)}, f32[1,2048]{1,0:T(1,128)}) custom-call(bf16[2048,4096]{1,0:T(8,128)(2,1)S(1)} %get-tuple-element.52.e_ref, f32[1,2048]{1,0:T(1,128)S(1)} %get-tuple-element.53.a_ref, f32[1,4096]{1,0:T(1,128)S(1)} %get-tuple-element.56.first_ref, f32[4,1,2048]{2,1,0:T(1,128)S(1)} %all_to_all.5.refs_0_), custom_call_target="tpu_custom_call" | custom-call | flops 16777216 | bytes 16777216 | tf_op jit(solution)/shard_map/weighted_sum/pallas_call | solution.py:297
  101.5 1.2 collective-permute-done.17
  102.7 1.9 %collective-permute-start.18 = (f32[4096]{0:T(1024)S(1)}, f32[4096]{0:T(1024)S(1)}, u32[]{:S(2)}, u32[]{:S(2)}) collective-permute-start(f32[4096]{0:T(1024)S(1)} %bitcast.33), channel_id=1, source_target_pairs={{0,4},{1,5},{2,6},{3,7},{4,0},{5,1},{6,2},{7,3},{8,12},{9,13},{10,... | collective-permute-start | bytes 49160 | tf_op jit(solution)/shard_map/ppermute | solution.py:592
  104.7 2.8 %collective-permute-done.18 = f32[4096]{0:T(1024)S(1)} collective-permute-done((f32[4096]{0:T(1024)S(1)}, f32[4096]{0:T(1024)S(1)}, u32[]{:S(2)}, u32[]{:S(2)}) %collective-permute-start.18) | collective-permute-done | bytes 16416 | tf_op jit(solution)/shard_map/ppermute | solution.py:592
  107.5 1.3 collective-permute-start.19
  108.8 2.5 %collective-permute-done.19 = f32[4096]{0:T(1024)S(1)} collective-permute-done((f32[4096]{0:T(1024)S(1)}, f32[4096]{0:T(1024)S(1)}, u32[]{:S(2)}, u32[]{:S(2)}) %collective-permute-start.19) | collective-permute-done | bytes 16416 | tf_op jit(solution)/shard_map/ppermute | solution.py:592
  111.3 4.4 %weighted_sum.6.one_ref = f32[1,2048]{1,0:T(1,128)S(1)} custom-call(bf16[2048,4096]{1,0:T(8,128)(2,1)S(1)} %get-tuple-element.52.e_ref, f32[1,4096]{1,0:T(1,128)S(1)} %get-tuple-element.56.first_ref, f32[1,4096]{1,0:T(1,128)S(1)} %get-tuple-element.57.b_ref, f32[1,4096]{1,0:T(1,128)S(1)} %pair.7.refs_0_, f32[1,4096]{1,0:T(1,128)S(1)} %bitcast.53), custom_call_target="tpu_custom_call" | custom-call | flops 16777216 | bytes 16777216 | tf_op jit(solution)/shard_map/weighted_sum/pallas_call | solution.py:297
  116.5 3.0 %collective-permute-done.20 = f32[2048]{0:T(1024)S(1)} collective-permute-done((f32[2048]{0:T(1024)S(1)}, f32[2048]{0:T(1024)S(1)}, u32[]{:S(2)}, u32[]{:S(2)}) %collective-permute-start.20) | collective-permute-done | bytes 8224 | tf_op jit(solution)/shard_map/ppermute | solution.py:592
  120.2 3.0 %collective-permute-done.21 = f32[2048]{0:T(1024)S(1)} collective-permute-done((f32[2048]{0:T(1024)S(1)}, f32[2048]{0:T(1024)S(1)}, u32[]{:S(2)}, u32[]{:S(2)}) %collective-permute-start.21) | collective-permute-done | bytes 8224 | tf_op jit(solution)/shard_map/ppermute | solution.py:592
  123.2 2.3 %weighted_sum.7 = (f32[1,4096]{1,0:T(1,128)S(1)}, f32[1,2048]{1,0:T(1,128)S(1)}) custom-call(bf16[2048,4096]{1,0:T(8,128)(2,1)S(1)} %get-tuple-element.52.e_ref, f32[1,2048]{1,0:T(1,128)S(1)} %get-tuple-element.53.a_ref, f32[1,4096]{1,0:T(1,128)S(1)} %get-tuple-element.56.first_ref, f32[1,2048]{1,0:T(1,128)S(1)} %pair.8.refs_0_, f32[1,2048]{1,0:T(1,128)S(1)} %bitcast.54), custom_call_target="tpu_custom_call" | custom-call | flops 16777216 | bytes 16777216 | tf_op jit(solution)/shard_map/weighted_sum/pallas_call | solution.py:297
  125.6 1.2 collective-permute-done.22
  126.8 1.6 %collective-permute-start.25 = (f32[4096]{0:T(1024)S(1)}, f32[4096]{0:T(1024)S(1)}, u32[]{:S(2)}, u32[]{:S(2)}) collective-permute-start(f32[4096]{0:T(1024)S(1)} %bitcast.34), channel_id=1, source_target_pairs={{0,6},{1,7},{2,4},{3,5},{4,2},{5,3},{6,0},{7,1},{8,14},{9,15},{10,... | collective-permute-start | bytes 49160 | tf_op jit(solution)/shard_map/ppermute | solution.py:592
  128.4 1.1 collective-permute-start.24
  129.5 1.7 %collective-permute-start.23 = (f32[4096]{0:T(1024)S(1)}, f32[4096]{0:T(1024)S(1)}, u32[]{:S(2)}, u32[]{:S(2)}) collective-permute-start(f32[4096]{0:T(1024)S(1)} %bitcast.36), channel_id=1, source_target_pairs={{0,2},{1,3},{2,0},{3,1},{4,6},{5,7},{6,4},{7,5},{8,10},{9,11},{10,... | collective-permute-start | bytes 49160 | tf_op jit(solution)/shard_map/ppermute | solution.py:592
  131.3 1.1 collective-permute-done.25
  133.3 5.5 %column_grad.1 = (f32[2048,128]{1,0:T(8,128)S(1)}, bf16[2048,128]{1,0:T(8,128)(2,1)S(1)}, f32[1,4096]{1,0:T(1,128)S(1)}) custom-call(bf16[128,2048]{1,0:T(8,128)(2,1)S(1)} %get-tuple-element.44.xt_ref, bf16[4096,128]{1,0:T(8,128)(2,1)S(1)} %get-tuple-element.50.y_ref, bf16[2048,4096]{1,0:T(8,128)(2,1)S(1)} %get-tuple-element.52.e_ref, ...), custom_call_target="tpu_custom_call" | custom-call | flops 4294967296 | bytes 16777216 | tf_op jit(solution)/shard_map/column_grad/pallas_call | solution.py:437
  138.9 2.3 %first_rows.1 = (bf16[4096,256]{1,0:T(8,128)(2,1)S(1)}, bf16[512,128]{1,0:T(8,128)(2,1)S(1)}) custom-call(bf16[2048,128]{1,0:T(8,128)(2,1)S(1)} %get-tuple-element.43.x_ref, bf16[4096,128]{1,0:T(8,128)(2,1)S(1)} %get-tuple-element.50.y_ref, bf16[2048,4096]{1,0:T(8,128)(2,1)S(1)} %get-tuple-element.52.e_ref, f32[1,2048]{1,0:T(1,128)S(1)} %get-tuple-element.60.alpha_ref, ...), custom_call_target="tpu_custom_call" | custom-call | flops 1073741824 | bytes 4194304 | tf_op jit(solution)/shard_map/first_rows/pallas_call | solution.py:509
  141.3 1.8 %collective-permute-start.27 = (bf16[512,128]{1,0:T(8,128)(2,1)S(1)}, bf16[512,128]{1,0:T(8,128)(2,1)S(1)}, u32[]{:S(2)}, u32[]{:S(2)}) collective-permute-start(bf16[512,128]{1,0:T(8,128)(2,1)S(1)} %get-tuple-element.74), channel_id=1, source_target_pairs={{0,2},{1,3},{2,0},{3,1},{4,6},{5,7},{6,4},{7,5},{8,10},{9,11},{10,... | collective-permute-start | bytes 393224 | tf_op jit(solution)/shard_map/ppermute | solution.py:592
  143.1 1.1 collective-permute-start.31
  144.2 1.6 collective-permute-start.32
  145.7 2.6 %other_rows.3 = (bf16[512,128]{1,0:T(8,128)(2,1)S(1)}, bf16[512,128]{1,0:T(8,128)(2,1)S(1)}) custom-call(bf16[2048,128]{1,0:T(8,128)(2,1)S(1)} %get-tuple-element.43.x_ref, bf16[4096,256]{1,0:T(8,128)(2,1)S(1)} %get-tuple-element.70.yb_ref, bf16[2048,4096]{1,0:T(8,128)(2,1)S(1)} %get-tuple-element.52.e_ref, f32[1,2048]{1,0:T(1,128)S(1)} %get-tuple-element.60.alpha_ref), custom_call_target="tpu_custom_call" | custom-call | flops 2147483648 | bytes 8388608 | tf_op jit(solution)/shard_map/other_rows/pallas_call | solution.py:526
  150.2 2.3 %collective-permute-start.30 = (bf16[512,128]{1,0:T(8,128)(2,1)S(1)}, bf16[512,128]{1,0:T(8,128)(2,1)S(1)}, u32[]{:S(2)}, u32[]{:S(2)}) collective-permute-start(bf16[512,128]{1,0:T(8,128)(2,1)S(1)} %get-tuple-element.77), channel_id=1, source_target_pairs={{0,17},{1,16},{2,19},{3,18},{4,21},{5,20},{6,23},{7,22},{8,25},{9,... | collective-permute-start | bytes 393224 | tf_op jit(solution)/shard_map/ppermute | solution.py:592
  152.4 1.4 other_rows.2.refs_0_
  153.9 2.1 %collective-permute-done.31.refs_6_ = bf16[512,128]{1,0:T(8,128)(2,1)S(1)} collective-permute-done((bf16[512,128]{1,0:T(8,128)(2,1)S(1)}, bf16[512,128]{1,0:T(8,128)(2,1)S(1)}, u32[]{:S(2)}, u32[]{:S(2)}) %collective-permute-start.31) | collective-permute-done | bytes 131104 | tf_op jit(solution)/shard_map/ppermute | solution.py:592
  156.0 1.6 collective-permute-done.30.refs_3_
  157.6 0.8 add_up.1
  (47 shorter events, 9.3 us)
Async XLA Ops:
  0.6 10.6 %collective-permute-start.5 = (bf16[512,128]{1,0:T(8,128)(2,1)}, bf16[512,128]{1,0:T(8,128)(2,1)S(1)}, u32[]{:S(2)}, u32[]{:S(2)}) collective-permute-start(bf16[512,128]{1,0:T(8,128)(2,1)} %bitcast.56), channel_id=1, source_target_pairs={{0,4},{1,5},{2,6},{3,7},{4,0},{5,1},{6,2},{7,3},{8,12},{9,13},{10,... | collective-permute-start | bytes 393224 | tf_op jit(solution)/shard_map/ppermute | solution.py:592
  4.7 7.3 %collective-permute-start.3 = (bf16[512,128]{1,0:T(8,128)(2,1)}, bf16[512,128]{1,0:T(8,128)(2,1)S(1)}, u32[]{:S(2)}, u32[]{:S(2)}) collective-permute-start(bf16[512,128]{1,0:T(8,128)(2,1)} %bitcast.57), channel_id=1, source_target_pairs={{0,8},{1,9},{2,10},{3,11},{4,12},{5,13},{6,14},{7,15},{8,0},{9,1},... | collective-permute-start | bytes 393224 | tf_op jit(solution)/shard_map/ppermute | solution.py:592
  4.7 8.5 %collective-permute-start.1 = (bf16[512,128]{1,0:T(8,128)(2,1)}, bf16[512,128]{1,0:T(8,128)(2,1)S(1)}, u32[]{:S(2)}, u32[]{:S(2)}) collective-permute-start(bf16[512,128]{1,0:T(8,128)(2,1)} %x_own.1), channel_id=1, source_target_pairs={{0,16},{1,17},{2,18},{3,19},{4,20},{5,21},{6,22},{7,23},{8,24},{9,... | collective-permute-start | bytes 393224 | tf_op jit(solution)/shard_map/ppermute | solution.py:592
  6.2 8.6 %collective-permute-start = (bf16[512,128]{1,0:T(8,128)(2,1)}, bf16[512,128]{1,0:T(8,128)(2,1)S(1)}, u32[]{:S(2)}, u32[]{:S(2)}) collective-permute-start(bf16[512,128]{1,0:T(8,128)(2,1)} %x_own.1), channel_id=1, source_target_pairs={{0,1},{1,0},{2,3},{3,2},{4,5},{5,4},{6,7},{7,6},{8,9},{9,8},{10,11... | collective-permute-start | bytes 393224 | tf_op jit(solution)/shard_map/ppermute | solution.py:592
  7.7 7.1 %collective-permute-start.2 = (bf16[512,128]{1,0:T(8,128)(2,1)}, bf16[512,128]{1,0:T(8,128)(2,1)S(1)}, u32[]{:S(2)}, u32[]{:S(2)}) collective-permute-start(bf16[512,128]{1,0:T(8,128)(2,1)} %x_own.1), channel_id=1, source_target_pairs={{0,17},{1,16},{2,19},{3,18},{4,21},{5,20},{6,23},{7,22},{8,25},{9,... | collective-permute-start | bytes 393224 | tf_op jit(solution)/shard_map/ppermute | solution.py:592
  11.2 12.5 %collective-permute-start.4 = (bf16[512,128]{1,0:T(8,128)(2,1)}, bf16[512,128]{1,0:T(8,128)(2,1)S(1)}, u32[]{:S(2)}, u32[]{:S(2)}) collective-permute-start(bf16[512,128]{1,0:T(8,128)(2,1)} %bitcast.58), channel_id=1, source_target_pairs={{0,2},{1,3},{2,0},{3,1},{4,6},{5,7},{6,4},{7,5},{8,10},{9,11},{10,... | collective-permute-start | bytes 393224 | tf_op jit(solution)/shard_map/ppermute | solution.py:592
  12.1 11.6 %collective-permute-start.6 = (bf16[512,128]{1,0:T(8,128)(2,1)S(1)}, bf16[512,128]{1,0:T(8,128)(2,1)S(1)}, u32[]{:S(2)}, u32[]{:S(2)}) collective-permute-start(bf16[512,128]{1,0:T(8,128)(2,1)S(1)} %collective-permute-done.5.refs_1_), channel_id=1, source_target_pairs={{0,2},{1,3},{2,0},{3,1},{4,6},{5,7},{6,4},{7,5},{8,10},{9,11},{10,... | collective-permute-start | bytes 393224 | tf_op jit(solution)/shard_map/ppermute | solution.py:592
  14.9 0.9 copy-start
  15.8 0.9 copy-start.1
  23.7 1.4 collective-permute-start.7
  23.8 1.5 collective-permute-start.8
  24.3 1.3 collective-permute-start.9
  25.7 0.9 copy-start.2
  26.6 0.7 copy-start.3
  41.3 4.7 %collective-permute-start.12 = (f32[3072]{0:T(1024)S(1)}, f32[3072]{0:T(1024)S(1)}, u32[]{:S(2)}, u32[]{:S(2)}) collective-permute-start(f32[3072]{0:T(1024)S(1)} %bitcast.62), channel_id=1, source_target_pairs={{0,17},{1,16},{2,19},{3,18},{4,21},{5,20},{6,23},{7,22},{8,25},{9,... | collective-permute-start | bytes 36872 | tf_op jit(solution)/shard_map/ppermute | solution.py:592
  41.4 4.6 %collective-permute-start.11 = (f32[3072]{0:T(1024)S(1)}, f32[3072]{0:T(1024)S(1)}, u32[]{:S(2)}, u32[]{:S(2)}) collective-permute-start(f32[3072]{0:T(1024)S(1)} %bitcast.63), channel_id=1, source_target_pairs={{0,16},{1,17},{2,18},{3,19},{4,20},{5,21},{6,22},{7,23},{8,24},{9,... | collective-permute-start | bytes 36872 | tf_op jit(solution)/shard_map/ppermute | solution.py:592
  41.5 5.1 %collective-permute-start.10 = (f32[3072]{0:T(1024)S(1)}, f32[3072]{0:T(1024)S(1)}, u32[]{:S(2)}, u32[]{:S(2)}) collective-permute-start(f32[3072]{0:T(1024)S(1)} %bitcast.64), channel_id=1, source_target_pairs={{0,1},{1,0},{2,3},{3,2},{4,5},{5,4},{6,7},{7,6},{8,9},{9,8},{10,11... | collective-permute-start | bytes 36872 | tf_op jit(solution)/shard_map/ppermute | solution.py:592
  46.6 0.7 copy-start.4
  78.2 1.3 collective-permute-start.13
  79.5 5.9 %collective-permute-start.16 = (f32[5120]{0:T(1024)S(1)}, f32[5120]{0:T(1024)S(1)}, u32[]{:S(2)}, u32[]{:S(2)}) collective-permute-start(f32[5120]{0:T(1024)S(1)} %bitcast.30), channel_id=1, source_target_pairs={{0,6},{1,7},{2,4},{3,5},{4,2},{5,3},{6,0},{7,1},{8,14},{9,15},{10,... | collective-permute-start | bytes 61448 | tf_op jit(solution)/shard_map/ppermute | solution.py:592
  81.6 4.8 %collective-permute-start.15 = (f32[5120]{0:T(1024)S(1)}, f32[5120]{0:T(1024)S(1)}, u32[]{:S(2)}, u32[]{:S(2)}) collective-permute-start(f32[5120]{0:T(1024)S(1)} %bitcast.31), channel_id=1, source_target_pairs={{0,4},{1,5},{2,6},{3,7},{4,0},{5,1},{6,2},{7,3},{8,12},{9,13},{10,... | collective-permute-start | bytes 61448 | tf_op jit(solution)/shard_map/ppermute | solution.py:592
  81.8 4.6 %collective-permute-start.14 = (f32[5120]{0:T(1024)S(1)}, f32[5120]{0:T(1024)S(1)}, u32[]{:S(2)}, u32[]{:S(2)}) collective-permute-start(f32[5120]{0:T(1024)S(1)} %bitcast.32), channel_id=1, source_target_pairs={{0,2},{1,3},{2,0},{3,1},{4,6},{5,7},{6,4},{7,5},{8,10},{9,11},{10,... | collective-permute-start | bytes 61448 | tf_op jit(solution)/shard_map/ppermute | solution.py:592
  101.5 1.2 collective-permute-start.17
  102.7 4.8 %collective-permute-start.18 = (f32[4096]{0:T(1024)S(1)}, f32[4096]{0:T(1024)S(1)}, u32[]{:S(2)}, u32[]{:S(2)}) collective-permute-start(f32[4096]{0:T(1024)S(1)} %bitcast.33), channel_id=1, source_target_pairs={{0,4},{1,5},{2,6},{3,7},{4,0},{5,1},{6,2},{7,3},{8,12},{9,13},{10,... | collective-permute-start | bytes 49160 | tf_op jit(solution)/shard_map/ppermute | solution.py:592
  107.5 3.8 %collective-permute-start.19 = (f32[4096]{0:T(1024)S(1)}, f32[4096]{0:T(1024)S(1)}, u32[]{:S(2)}, u32[]{:S(2)}) collective-permute-start(f32[4096]{0:T(1024)S(1)} %bitcast.37), channel_id=1, source_target_pairs={{0,2},{1,3},{2,0},{3,1},{4,6},{5,7},{6,4},{7,5},{8,10},{9,11},{10,... | collective-permute-start | bytes 49160 | tf_op jit(solution)/shard_map/ppermute | solution.py:592
  115.8 3.7 %collective-permute-start.20 = (f32[2048]{0:T(1024)S(1)}, f32[2048]{0:T(1024)S(1)}, u32[]{:S(2)}, u32[]{:S(2)}) collective-permute-start(f32[2048]{0:T(1024)S(1)} %bitcast.39), channel_id=1, source_target_pairs={{0,16},{1,17},{2,18},{3,19},{4,20},{5,21},{6,22},{7,23},{8,24},{9,... | collective-permute-start | bytes 24584 | tf_op jit(solution)/shard_map/ppermute | solution.py:592
  119.5 3.7 %collective-permute-start.21 = (f32[2048]{0:T(1024)S(1)}, f32[2048]{0:T(1024)S(1)}, u32[]{:S(2)}, u32[]{:S(2)}) collective-permute-start(f32[2048]{0:T(1024)S(1)} %bitcast.38), channel_id=1, source_target_pairs={{0,1},{1,0},{2,3},{3,2},{4,5},{5,4},{6,7},{7,6},{8,9},{9,8},{10,11... | collective-permute-start | bytes 24584 | tf_op jit(solution)/shard_map/ppermute | solution.py:592
  125.6 1.2 collective-permute-start.22
  126.8 5.6 %collective-permute-start.25 = (f32[4096]{0:T(1024)S(1)}, f32[4096]{0:T(1024)S(1)}, u32[]{:S(2)}, u32[]{:S(2)}) collective-permute-start(f32[4096]{0:T(1024)S(1)} %bitcast.34), channel_id=1, source_target_pairs={{0,6},{1,7},{2,4},{3,5},{4,2},{5,3},{6,0},{7,1},{8,14},{9,15},{10,... | collective-permute-start | bytes 49160 | tf_op jit(solution)/shard_map/ppermute | solution.py:592
  128.4 4.6 %collective-permute-start.24 = (f32[4096]{0:T(1024)S(1)}, f32[4096]{0:T(1024)S(1)}, u32[]{:S(2)}, u32[]{:S(2)}) collective-permute-start(f32[4096]{0:T(1024)S(1)} %bitcast.35), channel_id=1, source_target_pairs={{0,4},{1,5},{2,6},{3,7},{4,0},{5,1},{6,2},{7,3},{8,12},{9,13},{10,... | collective-permute-start | bytes 49160 | tf_op jit(solution)/shard_map/ppermute | solution.py:592
  129.5 3.7 %collective-permute-start.23 = (f32[4096]{0:T(1024)S(1)}, f32[4096]{0:T(1024)S(1)}, u32[]{:S(2)}, u32[]{:S(2)}) collective-permute-start(f32[4096]{0:T(1024)S(1)} %bitcast.36), channel_id=1, source_target_pairs={{0,2},{1,3},{2,0},{3,1},{4,6},{5,7},{6,4},{7,5},{8,10},{9,11},{10,... | collective-permute-start | bytes 49160 | tf_op jit(solution)/shard_map/ppermute | solution.py:592
  138.8 2.4 %collective-permute-start.26 = (bf16[2048,128]{1,0:T(8,128)(2,1)S(1)}, bf16[2048,128]{1,0:T(8,128)(2,1)S(1)}, u32[]{:S(2)}, u32[]{:S(2)}) collective-permute-start(bf16[2048,128]{1,0:T(8,128)(2,1)S(1)} %get-tuple-element.63), channel_id=1, source_target_pairs={{0,8},{1,9},{2,10},{3,11},{4,12},{5,13},{6,14},{7,15},{8,0},{9,1},... | collective-permute-start | bytes 1572872 | tf_op jit(solution)/shard_map/ppermute | solution.py:592
  141.3 7.7 %collective-permute-start.27 = (bf16[512,128]{1,0:T(8,128)(2,1)S(1)}, bf16[512,128]{1,0:T(8,128)(2,1)S(1)}, u32[]{:S(2)}, u32[]{:S(2)}) collective-permute-start(bf16[512,128]{1,0:T(8,128)(2,1)S(1)} %get-tuple-element.74), channel_id=1, source_target_pairs={{0,2},{1,3},{2,0},{3,1},{4,6},{5,7},{6,4},{7,5},{8,10},{9,11},{10,... | collective-permute-start | bytes 393224 | tf_op jit(solution)/shard_map/ppermute | solution.py:592
  143.1 12.9 %collective-permute-start.31 = (bf16[512,128]{1,0:T(8,128)(2,1)S(1)}, bf16[512,128]{1,0:T(8,128)(2,1)S(1)}, u32[]{:S(2)}, u32[]{:S(2)}) collective-permute-start(bf16[512,128]{1,0:T(8,128)(2,1)S(1)} %get-tuple-element.80), channel_id=1, source_target_pairs={{0,4},{1,5},{2,6},{3,7},{4,0},{5,1},{6,2},{7,3},{8,12},{9,13},{10,... | collective-permute-start | bytes 393224 | tf_op jit(solution)/shard_map/ppermute | solution.py:592
  144.2 11.8 %collective-permute-start.32 = (bf16[512,128]{1,0:T(8,128)(2,1)S(1)}, bf16[512,128]{1,0:T(8,128)(2,1)S(1)}, u32[]{:S(2)}, u32[]{:S(2)}) collective-permute-start(bf16[512,128]{1,0:T(8,128)(2,1)S(1)} %get-tuple-element.81), channel_id=1, source_target_pairs={{0,6},{1,7},{2,4},{3,5},{4,2},{5,3},{6,0},{7,1},{8,14},{9,15},{10,... | collective-permute-start | bytes 393224 | tf_op jit(solution)/shard_map/ppermute | solution.py:592
  148.9 7.0 %collective-permute-start.28 = (bf16[512,128]{1,0:T(8,128)(2,1)S(1)}, bf16[512,128]{1,0:T(8,128)(2,1)S(1)}, u32[]{:S(2)}, u32[]{:S(2)}) collective-permute-start(bf16[512,128]{1,0:T(8,128)(2,1)S(1)} %get-tuple-element.75), channel_id=1, source_target_pairs={{0,1},{1,0},{2,3},{3,2},{4,5},{5,4},{6,7},{7,6},{8,9},{9,8},{10,11... | collective-permute-start | bytes 393224 | tf_op jit(solution)/shard_map/ppermute | solution.py:592
  149.6 6.4 %collective-permute-start.29 = (bf16[512,128]{1,0:T(8,128)(2,1)S(1)}, bf16[512,128]{1,0:T(8,128)(2,1)S(1)}, u32[]{:S(2)}, u32[]{:S(2)}) collective-permute-start(bf16[512,128]{1,0:T(8,128)(2,1)S(1)} %get-tuple-element.76), channel_id=1, source_target_pairs={{0,16},{1,17},{2,18},{3,19},{4,20},{5,21},{6,22},{7,23},{8,24},{9,... | collective-permute-start | bytes 393224 | tf_op jit(solution)/shard_map/ppermute | solution.py:592
  150.2 7.4 %collective-permute-start.30 = (bf16[512,128]{1,0:T(8,128)(2,1)S(1)}, bf16[512,128]{1,0:T(8,128)(2,1)S(1)}, u32[]{:S(2)}, u32[]{:S(2)}) collective-permute-start(bf16[512,128]{1,0:T(8,128)(2,1)S(1)} %get-tuple-element.77), channel_id=1, source_target_pairs={{0,17},{1,16},{2,19},{3,18},{4,21},{5,20},{6,23},{7,22},{8,25},{9,... | collective-permute-start | bytes 393224 | tf_op jit(solution)/shard_map/ppermute | solution.py:592

commit v9 on v8

--- a/solution.py
+++ b/solution.py
@@ -15,8 +15,8 @@
 CROSS = 2.0 * LOG2E / EPSILON
 NT = (((1,), (1,)), ((), ()))
 VMEM = pl.BlockSpec(memory_space=pltpu.VMEM)
-HBM = pl.BlockSpec(memory_space=pltpu.HBM)
 GROUP = 32
+HEAVY = 32
 
 
 def spread(value, s_ref, sb_ref):
@@ -139,26 +139,6 @@
         running_max(places, chunk, min(width, 256), a_ref, b_ref, sb_ref, o_ref, e_ref, shift_ref)
 
 
-def pair_copies(o_ref, at, mass_ref, axis, sem):
-    share = (o_ref.shape[1] - at) // 2
-    place = lax.axis_index(axis)
-    copies = []
-    for k in range(2):
-        start = pl.multiple_of((place ^ k) * share, share)
-        there = o_ref.at[:, at + k * share:at + (k + 1) * share]
-        copies.append(pltpu.make_async_copy(mass_ref.at[:, pl.ds(start, share)], there, sem.at[k]))
-    return copies
-
-
-def fill(out_ref, own_ref, others, sem):
-    share = own_ref.shape[0]
-    copy = pltpu.make_async_copy(own_ref, out_ref.at[pl.ds(0, share), :], sem)
-    copy.start()
-    for k, shard in enumerate(others):
-        out_ref[(k + 1) * share:(k + 2) * share, :] = shard[...]
-    return copy
-
-
 def put_norms(places, share, y_ref, sb_ref):
     for at in places:
         y = y_ref[at:at + share, :].astype(jnp.float32)
@@ -166,13 +146,20 @@
         sb_ref[at:at + share, :] = jnp.broadcast_to(total, (share, 128))
 
 
-def row_lse_early_kernel(width, nx, x_own, y_own, *refs):
+def join(out_ref, parts):
+    at = 0
+    for part in parts:
+        out_ref[at:at + part.shape[0], :] = part[...]
+        at += part.shape[0]
+
+
+def row_lse_early_kernel(width, nx, own_ref, *refs):
     xs, y_other, refs = refs[:nx], refs[nx], refs[nx + 1:]
-    x_ref, xt_ref, o_ref, y_ref, sb_ref, d_ref, top_ref, sem = refs
-    share = y_own.shape[0]
-    copies = [fill(x_ref, x_own, xs, sem.at[0]), fill(y_ref, y_own, [y_other], sem.at[1])]
-    for copy in copies:
-        copy.wait()
+    x_ref, xt_ref, o_ref, y_ref, sb_ref, d_ref, top_ref = refs
+    share = y_other.shape[0]
+    mine = own_ref.shape[0] - share
+    join(x_ref, [own_ref.at[:mine, :], *xs])
+    join(y_ref, [own_ref.at[mine:, :], y_other])
     for k in range(x_ref.shape[0] // 128):
         at = k * 128
         xt_ref[:, at:at + 128] = jnp.transpose(x_ref[at:at + 128, :].astype(jnp.float32)).astype(jnp.bfloat16)
@@ -181,27 +168,31 @@
     lse_pass(places, share, width, y_ref, x_ref, sb_ref, d_ref, top_ref, o_ref)
 
 
-def row_lse_late_kernel(width, ny, y_own, mass_ref, x_ref, first_ref, *refs):
-    ys, (y_ref, o_ref, sb_ref, d_ref, top_ref, sum_ref, sem) = refs[:ny], refs[ny:]
-    share, rows = y_own.shape[0], x_ref.shape[0]
-    copies = [fill(y_ref, y_own, ys, sem.at[2])]
-    masses = pair_copies(o_ref, rows, mass_ref, "col", sem)
-    for copy in masses:
-        copy.start()
-    places = [k * share for k in range(ny + 1) if k % ((ny + 1) // 2)]
+def row_lse_middle_kernel(width, ny, x_ref, first_ref, *refs):
+    ys, (o_ref, y_ref, sb_ref, d_ref, top_ref, sum_ref) = refs[:ny], refs[ny:]
+    share = ys[0].shape[0]
+    join(y_ref, ys)
+    places = [k * share for k in range(ny)]
+    put_norms(places, share, y_ref, sb_ref)
+    lse_pass(places, share, width, y_ref, x_ref, sb_ref, d_ref, top_ref, sum_ref)
+    o_ref[...] = lse2([first_ref[...], sum_ref[...]])
+
+
+def row_lse_late_kernel(width, ny, own_ref, mass_ref, x_ref, first_ref, *refs):
+    ys, (y_ref, o_ref, sb_ref, d_ref, top_ref, sum_ref) = refs[:ny], refs[ny:]
+    share, rows, half = ys[0].shape[0], x_ref.shape[0], (ny + 1) // 2
+    join(y_ref, [own_ref.at[own_ref.shape[0] - share:, :], *ys])
+    places = [k * share for k in range(half - 1, 2 * half) if k != half]
     put_norms(places, share, y_ref, sb_ref)
     lse_pass(places, share, width, y_ref, x_ref, sb_ref, d_ref, top_ref, sum_ref)
     o_ref[:, :rows] = lse2([first_ref[...], sum_ref[...]])
-    for copy in copies + masses:
-        copy.wait()
+    o_ref[:, rows:] = mass_ref[:, :o_ref.shape[1] - rows]
 
 
 def column_lse_kernel(width, chunk, na, x_ref, y_ref, mass_ref, *refs):
-    got, (o_ref, e_ref, shift_ref, a_ref, s_ref, sb_ref, d_ref, top_ref, sem) = refs[:na], refs[na:]
+    got, (o_ref, e_ref, shift_ref, a_ref, s_ref, sb_ref, d_ref, top_ref) = refs[:na], refs[na:]
     rows, cols = x_ref.shape[0], y_ref.shape[0]
-    masses = pair_copies(o_ref, cols, mass_ref, "row", sem)
-    for copy in masses:
-        copy.start()
+    o_ref[:, cols:] = mass_ref[:, mass_ref.shape[1] - o_ref.shape[1] + cols:]
     share = rows // na
     for k in range(na):
         at = rows + (k % 2) * share
@@ -210,8 +201,6 @@
     spread(u, s_ref, sb_ref)
     places = list(range(0, rows, chunk))
     lse_pass(places, chunk, width, x_ref, y_ref, sb_ref, d_ref, top_ref, o_ref, e_ref, shift_ref)
-    for copy in masses:
-        copy.wait()
 
 
 def pair_kernel(size, shift, parts, combine, one_ref, two_ref, o_ref):
@@ -239,19 +228,7 @@
 def row_sums(width, e_ref, w16_ref, o_ref):
     for at in range(0, e_ref.shape[0], width):
         got = lax.dot_general(w16_ref[...], e_ref[at:at + width, :], NT, preferred_element_type=jnp.float32)
-        got = jnp.sum(got, axis=0, keepdims=True)
-        if len(o_ref.shape) == 2:
-            o_ref[:, at:at + width] = got
-        else:
-            for k in range(o_ref.shape[0]):
-                o_ref[k, :, at:at + width] = got
-
-
-def received(refs):
-    if len(refs) == 1 and len(refs[0].shape) == 3:
-        place = ((lax.axis_index("row") >> 1) << 1) | (lax.axis_index("col") & 1)
-        return [refs[0][place ^ s] for s in range(refs[0].shape[0])]
-    return [ref[...] for ref in refs]
+        o_ref[:, at:at + width] = jnp.sum(got, axis=0, keepdims=True)
 
 
 def first_row_kernel(width, shifts, parts, e_ref, shift_ref, *refs):
@@ -268,19 +245,19 @@
     row_sums(width, e_ref, w16_ref, o_ref)
 
 
-def new_beta(first_ref, b_ref, got, shifts, parts):
-    return first_ref[...] * (b_ref[...] / sum(ordered(received(got), shifts, parts)))
+def new_scale(b_ref, got, shifts, parts):
+    return b_ref[...] / sum(ordered([part[...] for part in got], shifts, parts))
 
 
 def row_kernel(width, shifts, parts, e_ref, first_ref, b_ref, *refs):
     got, (o_ref, w16_ref) = refs[:-2], refs[-2:]
-    w16_ref[...] = stacked(new_beta(first_ref, b_ref, got, shifts, parts))
+    w16_ref[...] = stacked(first_ref[...] * new_scale(b_ref, got, shifts, parts))
     row_sums(width, e_ref, w16_ref, o_ref)
 
 
 def column_kernel(width, shifts, parts, e_ref, a_ref, first_ref, *refs):
     got, (o_ref, alpha_ref, w16_ref) = refs[:-3], refs[-3:]
-    alpha_ref[...] = a_ref[...] / sum(ordered(received(got), shifts, parts))
+    alpha_ref[...] = a_ref[...] / sum(ordered([part[...] for part in got], shifts, parts))
     w16_ref[...] = stacked(alpha_ref[...])
     for at in range(0, e_ref.shape[1], width):
         sums = jnp.dot(w16_ref[...], e_ref[:, at:at + width], preferred_element_type=jnp.float32)
@@ -322,58 +299,63 @@
     ]
 
 
-def row_lse_early(xs, ys, width=512):
-    share_x, share = xs[0].shape[0], ys[0].shape[0]
-    rows, depth = len(xs) * share_x, 2 * share
-    return pl.pallas_call(
-        functools.partial(row_lse_early_kernel, width, len(xs) - 1),
+def row_lse_early(own, xs, y_other, width=512):
+    share = y_other.shape[0]
+    rows, depth = own.shape[0] - share + sum(part.shape[0] for part in xs), 2 * share
+    return pl.pallas_call(
+        functools.partial(row_lse_early_kernel, width, len(xs)),
         out_shape=(shape(rows, D, dtype=jnp.bfloat16), shape(D, rows, dtype=jnp.bfloat16), shape(1, rows)),
-        in_specs=[HBM] * 2 + [VMEM] * len(xs),
+        in_specs=[VMEM] * (len(xs) + 2),
         out_specs=(VMEM,) * 3,
+        scratch_shapes=[pltpu.VMEM((depth, D), jnp.bfloat16), *lse_scratch(depth, share, width)],
+        compiler_params=pltpu.CompilerParams(vmem_limit_bytes=16 << 20),
+        cost_estimate=pass_cost(depth, rows),
+        name="row_lse_early",
+    )(own, *xs, y_other)
+
+
+def row_lse_middle(x, ys, first, width=512):
+    rows, share = x.shape[0], ys[0].shape[0]
+    depth = len(ys) * share
+    return pl.pallas_call(
+        functools.partial(row_lse_middle_kernel, width, len(ys)),
+        out_shape=shape(1, rows),
+        in_specs=[VMEM] * (len(ys) + 2),
+        out_specs=VMEM,
         scratch_shapes=[
             pltpu.VMEM((depth, D), jnp.bfloat16),
             *lse_scratch(depth, share, width),
-            pltpu.SemaphoreType.DMA((2,)),
+            pltpu.VMEM((1, rows), jnp.float32),
         ],
         compiler_params=pltpu.CompilerParams(vmem_limit_bytes=16 << 20),
         cost_estimate=pass_cost(depth, rows),
-        name="row_lse_early",
-    )(xs[0], ys[0], *xs[1:], ys[1])
-
-
-def row_lse_late(x, ys, first, mass, width=512):
+        name="row_lse_middle",
+    )(x, first, *ys)
+
+
+def row_lse_late(own, x, ys, first, mass, tail, width=512):
     rows, share = x.shape[0], ys[0].shape[0]
-    depth = len(ys) * share
-    tail = mass.shape[0] // lax.axis_size("col")
-    return pl.pallas_call(
-        functools.partial(row_lse_late_kernel, width, len(ys) - 1),
-        out_shape=(shape(depth, D, dtype=jnp.bfloat16), shape(1, rows + 2 * tail)),
-        in_specs=[HBM] * 2 + [VMEM] * (len(ys) + 1),
+    depth = (len(ys) + 1) * share
+    return pl.pallas_call(
+        functools.partial(row_lse_late_kernel, width, len(ys)),
+        out_shape=(shape(depth, D, dtype=jnp.bfloat16), shape(1, rows + tail)),
+        in_specs=[VMEM] * (len(ys) + 4),
         out_specs=(VMEM,) * 2,
-        scratch_shapes=[
-            *lse_scratch(depth, share, width),
-            pltpu.VMEM((1, rows), jnp.float32),
-            pltpu.SemaphoreType.DMA((3,)),
-        ],
-        compiler_params=pltpu.CompilerParams(vmem_limit_bytes=16 << 20),
-        cost_estimate=pass_cost(depth - 2 * share, rows),
+        scratch_shapes=[*lse_scratch(depth, share, width), pltpu.VMEM((1, rows), jnp.float32)],
+        compiler_params=pltpu.CompilerParams(vmem_limit_bytes=16 << 20),
+        cost_estimate=pass_cost(depth // 2, rows),
         name="row_lse_late",
-    )(ys[0], mass.reshape(1, -1), x, first, *ys[1:])
-
-
-def column_lse(x, y, mass, got, width=512, chunk=512):
+    )(own, mass.reshape(1, -1), x, first, *ys)
+
+
+def column_lse(x, y, mass, tail, got, width=512, chunk=512):
     rows, cols = x.shape[0], y.shape[0]
-    tail = mass.shape[0] // lax.axis_size("row")
     return pl.pallas_call(
         functools.partial(column_lse_kernel, width, chunk, len(got)),
-        out_shape=(shape(1, cols + 2 * tail), shape(rows, cols, dtype=jnp.bfloat16), shape(1, cols), shape(1, rows)),
-        in_specs=[VMEM] * 2 + [HBM] + [VMEM] * len(got),
+        out_shape=(shape(1, cols + tail), shape(rows, cols, dtype=jnp.bfloat16), shape(1, cols), shape(1, rows)),
+        in_specs=[VMEM] * (3 + len(got)),
         out_specs=(VMEM,) * 4,
-        scratch_shapes=[
-            pltpu.VMEM((rows // 128, 128), jnp.float32),
-            *lse_scratch(rows, chunk, width),
-            pltpu.SemaphoreType.DMA((2,)),
-        ],
+        scratch_shapes=[pltpu.VMEM((rows // 128, 128), jnp.float32), *lse_scratch(rows, chunk, width)],
         compiler_params=pltpu.CompilerParams(vmem_limit_bytes=16 << 20),
         cost_estimate=pass_cost(rows, cols),
         name="column_lse",
@@ -397,14 +379,13 @@
     return high, (value - high.astype(jnp.float32)).astype(jnp.bfloat16)
 
 
-def column_grad_kernel(width, own, shifts, parts, xt_ref, y_ref, e_ref, alpha_ref, first_ref, b_ref, *refs):
-    got, (gc_ref, gcs_ref, beta_ref, bb_ref, cb_ref, xa_ref, s_ref, count_ref, acc_ref) = refs[:-9], refs[-9:]
+def column_grad_kernel(width, xt_ref, y_ref, e_ref, alpha_ref, first_ref, own_ref, sent_ref,
+                       bb_ref, cb_ref, xa_ref, s_ref, count_ref, acc_ref):
     rows, cols = xt_ref.shape[1], y_ref.shape[0]
-    beta_ref[...] = new_beta(first_ref, b_ref, got, shifts, parts)
-    spread(beta_ref[...], s_ref, bb_ref)
+    own = own_ref.shape[0]
+    spread(first_ref[...], s_ref, bb_ref)
     place = lax.broadcasted_iota(jnp.int32, (128, 512), 0)
-    for k in range(rows // 512):
-        at = k * 512
+    for at in range(0, rows, 512):
         alpha = alpha_ref[:, at:at + 512]
         high, low = high_low(xt_ref[:, at:at + 512].astype(jnp.float32) * alpha)
         first, second = high_low(alpha)
@@ -414,31 +395,28 @@
         xa_ref[128:, at:at + 512] = low.astype(jnp.bfloat16)
 
     lower = lax.broadcasted_iota(jnp.int32, (128, width), 0) < 126
-    for k in range(cols // width):
-        at = k * width
+    for at in range(0, cols, width):
         got = jnp.dot(xa_ref[...], e_ref[:, at:at + width], preferred_element_type=jnp.float32)
         acc_ref[:, at:at + width] = got[:128] + jnp.where(lower, got[128:], 0.0)
         count_ref[:, at:at + width] = got[254:255] + got[255:256]
     spread(count_ref[...], s_ref, cb_ref)
-    for k in range(cols // 128):
-        at = k * 128
+    for at in range(0, cols, 128):
         pulled = jnp.transpose(acc_ref[:, at:at + 128])
         whole = cb_ref[at:at + 128, :] * y_ref[at:at + 128, :].astype(jnp.float32)
-        grad = 2.0 * bb_ref[at:at + 128, :] * (whole - pulled)
+        grad = bb_ref[at:at + 128, :] * (whole - pulled)
         if at < own:
-            gc_ref[at:at + 128, :] = grad
+            own_ref[at:at + 128, :] = grad
         else:
-            gcs_ref[at - own:at - own + 128, :] = grad.astype(jnp.bfloat16)
-
-
-def column_grad(xt, y, e, alpha, first, mass, got, parts, own, width=512):
+            sent_ref[at - own:at - own + 128, :] = grad.astype(jnp.bfloat16)
+
+
+def column_grad(xt, y, e, alpha, first, own, width=512):
     rows, cols = xt.shape[1], y.shape[0]
-    got, shifts = got
-    return pl.pallas_call(
-        functools.partial(column_grad_kernel, width, own, tuple(shifts), parts),
-        out_shape=(shape(own, D), shape(cols - own, D, dtype=jnp.bfloat16), shape(1, cols)),
-        in_specs=[VMEM] * (6 + len(got)),
-        out_specs=(VMEM,) * 3,
+    return pl.pallas_call(
+        functools.partial(column_grad_kernel, width),
+        out_shape=(shape(own, D), shape(cols - own, D, dtype=jnp.bfloat16)),
+        in_specs=[VMEM] * 5,
+        out_specs=(VMEM,) * 2,
         scratch_shapes=[
             pltpu.VMEM((cols, 128), jnp.float32),
             pltpu.VMEM((cols, 128), jnp.float32),
@@ -450,7 +428,7 @@
         compiler_params=pltpu.CompilerParams(vmem_limit_bytes=16 << 20),
         cost_estimate=pl.CostEstimate(flops=4 * e.size * D, bytes_accessed=2 * e.size, transcendentals=0),
         name="column_grad",
-    )(xt, y, e, alpha, first, mass, *[flat(part) for part in got])
+    )(xt, y, e, alpha, first)
 
 
 def row_block(at, chunk, x_ref, e_ref, yb_ref, scale):
@@ -462,8 +440,8 @@
     return 2.0 * scale * (total * x - pulled)
 
 
-def put_yb(y_ref, beta_ref, yb_ref, s_ref, bb_ref):
-    spread(beta_ref[...], s_ref, bb_ref)
+def put_yb(y_ref, beta, yb_ref, s_ref, bb_ref):
+    spread(beta, s_ref, bb_ref)
     place = lax.broadcasted_iota(jnp.int32, (256, 128), 1)
     for at in range(0, y_ref.shape[0], 256):
         beta = bb_ref[at:at + 256, :]
@@ -485,9 +463,11 @@
             out_ref[k:k + chunk, :] = grad.astype(out_ref.dtype)
 
 
-def first_rows_kernel(parts, x_ref, y_ref, e_ref, alpha_ref, beta_ref, *refs):
-    yb_ref, outs, (s_ref, bb_ref, sa_ref, ab_ref) = refs[0], refs[1:-4], refs[-4:]
-    put_yb(y_ref, beta_ref, yb_ref, s_ref, bb_ref)
+def first_rows_kernel(parts, shifts, blocks, nz, x_ref, y_ref, e_ref, alpha_ref, first_ref, b_ref, *refs):
+    got, (yb_ref, scale_ref, *outs), (s_ref, bb_ref, sa_ref, ab_ref) = refs[:nz], refs[nz:-4], refs[-4:]
+    scale = new_scale(b_ref, got, shifts, blocks)
+    scale_ref[...] = scale[:, :scale_ref.shape[1]]
+    put_yb(y_ref, first_ref[...] * scale, yb_ref, s_ref, bb_ref)
     row_parts(parts, x_ref, e_ref, alpha_ref, yb_ref, outs, sa_ref, ab_ref)
 
 
@@ -504,22 +484,24 @@
     return pl.CostEstimate(flops=4 * size * D, bytes_accessed=2 * size, transcendentals=0)
 
 
-def first_rows(parts, share, x, y, e, alpha, beta):
+def first_rows(parts, share, x, y, e, alpha, first, mass, got, blocks):
     cols = y.shape[0]
-    return pl.pallas_call(
-        functools.partial(first_rows_kernel, parts),
-        out_shape=[shape(cols, 256, dtype=jnp.bfloat16)] + [shape(share, D, dtype=jnp.bfloat16)] * len(parts),
-        in_specs=[VMEM] * 5,
-        out_specs=[VMEM] * (1 + len(parts)),
+    got, shifts = got
+    return pl.pallas_call(
+        functools.partial(first_rows_kernel, parts, tuple(shifts), blocks, len(got)),
+        out_shape=[shape(cols, 256, dtype=jnp.bfloat16), shape(1, cols // blocks)]
+        + [shape(share, D, dtype=jnp.bfloat16)] * len(parts),
+        in_specs=[VMEM] * (6 + len(got)),
+        out_specs=[VMEM] * (2 + len(parts)),
         scratch_shapes=[
             pltpu.VMEM((cols // 128, 128), jnp.float32),
             pltpu.VMEM((cols, 128), jnp.float32),
             *rows_scratch(share),
         ],
         compiler_params=pltpu.CompilerParams(vmem_limit_bytes=16 << 20),
-        cost_estimate=rows_cost(share, parts, cols),
+        cost_estimate=rows_cost(share * HEAVY, parts, cols),
         name="first_rows",
-    )(x, y, e, alpha, beta)
+    )(x, y, e, alpha, first, mass, *[flat(part) for part in got])
 
 
 def other_rows(parts, share, x, yb, e, alpha, dtype):
@@ -535,21 +517,24 @@
     )(x, yb, e, alpha)
 
 
-def add_up_kernel(na, *refs):
-    ins, outs = refs[:-2], refs[-2:]
-    for out_ref, parts in zip(outs, (ins[:na], ins[na:])):
-        out_ref[...] = sum(part[...].astype(jnp.float32) for part in parts)
-
-
-def add_up(rows, columns):
+def add_up_kernel(na, scale_ref, *refs):
+    ins, (rows_ref, cols_ref, s_ref, sb_ref) = refs[:-4], refs[-4:]
+    rows_ref[...] = sum(part[...].astype(jnp.float32) for part in ins[:na])
+    spread(scale_ref[...], s_ref, sb_ref)
+    cols_ref[...] = 2.0 * sb_ref[...] * sum(part[...].astype(jnp.float32) for part in ins[na:])
+
+
+def add_up(rows, columns, scale):
+    share = scale.shape[1]
     return pl.pallas_call(
         functools.partial(add_up_kernel, len(rows)),
         out_shape=(shape(*rows[0].shape), shape(*columns[0].shape)),
-        in_specs=[VMEM] * (len(rows) + len(columns)),
+        in_specs=[VMEM] * (1 + len(rows) + len(columns)),
         out_specs=(VMEM,) * 2,
+        scratch_shapes=rows_scratch(share),
         compiler_params=pltpu.CompilerParams(vmem_limit_bytes=16 << 20),
         name="add_up",
-    )(*rows, *columns)
+    )(scale, *rows, *columns)
 
 
 def shares_kernel(gc_ref, other_ref, own_ref, *outs):
@@ -581,10 +566,6 @@
         self.across = [(a << 1) * ncol + b for a in range(nrow // 2) for b in range(2)]
         self.along = [z << 1 for z in range(ncol // 2)]
         self.core = ncol
-        self.squares = [
-            [(a * 2 + core) * ncol + z * 2 + b for a in range(nrow // 2) for b in range(2)]
-            for core in range(2) for z in range(ncol // 2)
-        ]
 
     def swap(self, value, mask):
         if mask == 0:
@@ -603,49 +584,51 @@
     def direct(value, masks):
         return [swap(value, mask) for mask in masks], range(len(masks))
 
-    def halved(value, masks, parts):
-        size, bit = value.shape[-1], len(masks) // 2
-        while bit > 1:
-            value = pair_of(sum, value, swap(value.reshape(-1), masks[bit]), size, bit, parts).reshape(-1)
-            bit //= 2
-        return [value, swap(value, masks[1])], (0, 1)
-
     near, far = [camera[0]], [swap(camera[0], core)]
     for z in range(1, nz):
         near.append(swap(near[z & (z - 1)], along[z & -z]))
     xs, _ = direct(imu, across)
 
-    x, xt, first = row_lse_early(xs, [near[0], far[0]])
-    rest = lax.optimization_barrier((first, *near[1:]))
-    far += [swap(part, core) for part in rest[1:]]
-    y, sent = row_lse_late(x, [near[0], *rest[1:], *far], rest[0], imu_mass)
+    def pair(mass, place, share):
+        return [lax.dynamic_slice_in_dim(mass, (place ^ k) * share, share, 0) for k in range(2)]
+
+    own = jnp.concatenate([imu, camera[0]])
+    row, col = lax.axis_index("row"), lax.axis_index("col")
+    mass = jnp.concatenate(pair(imu_mass, col, share_x) + pair(cam_mass, row, share_y))
+
+    x, xt, first = row_lse_early(own, xs[1:], far[0])
+    first, *middle = lax.optimization_barrier((first, *near[1:-1]))
+    far += [swap(part, core) for part in middle]
+    first = row_lse_middle(x, middle, first)
+    first, last = lax.optimization_barrier((first, near[-1]))
+    far.append(swap(last, core))
+    y, sent = row_lse_late(own, x, [*middle, last, *far], first, mass, 2 * share_x)
     got, _ = direct(sent.reshape(-1), across)
 
-    sent, e, shift, mass_a = column_lse(x, y, cam_mass, got)
+    sent, e, shift, mass_a = column_lse(x, y, mass, 2 * share_y, got)
     sent = pair_of(lse2, sent, swap(sent.reshape(-1), core), cols, 1, 2)
     got = direct(sent.reshape(-1), along)
 
     sums, first_beta, mass_b = weighted(
-        first_row_kernel, [(na, 1, rows), (1, cols), (1, cols)], e, [shift], got, 2 * nz)
+        first_row_kernel, [(1, rows), (1, cols), (1, cols)], e, [shift], got, 2 * nz)
     for step in range(1, ITERS):
-        if step == 1:
-            got = [lax.all_to_all(sums, ("row", "col"), 0, 0, axis_index_groups=groups.squares)], range(na)
-        else:
+        if step > 1:
             sums, = weighted(row_kernel, [(1, rows)], e, [first_beta, mass_b], got, 2 * nz)
-            got = halved(sums.reshape(-1), across, na)
+        got = direct(sums.reshape(-1), across)
         part, alpha = weighted(column_kernel, [(1, cols), (1, rows)], e, [mass_a, first_beta], got, na)
-        part = pair_of(sum, part, swap(part.reshape(-1), core), cols, 1, 2).reshape(-1)
-        got = halved(part, along, 2 * nz) if step == 1 else direct(part, along)
-
-    gc, gc_send, beta = column_grad(xt, y, e, alpha, first_beta, mass_b, got, 2 * nz, nz * share_y)
-    yb, last = first_rows([na - 1], share_x, x, y, e, alpha, beta)
+        part = pair_of(sum, part, swap(part.reshape(-1), core), cols, 1, 2)
+        part, alpha = lax.optimization_barrier((part, alpha))
+        got = direct(part.reshape(-1), along)
+
+    gc, gc_send = column_grad(xt, y, e, alpha, first_beta, nz * share_y)
+    yb, scale, last = first_rows([na - 1], share_x, x, y, e, alpha, first_beta, mass_b, got, 2 * nz)
     (grad_cam, *parts), yb = lax.optimization_barrier((shares(gc, swap(gc_send, core), nz), yb))
     parts = [swap(part, along[z + 1]) for z, part in enumerate(parts)]
     sent = [*other_rows(list(range(1, na - 1)), share_x, x, yb, e, alpha, jnp.bfloat16), last]
     sent, parts[0] = lax.optimization_barrier((sent, parts[0]))
     sent = [swap(part, across[s + 1]) for s, part in enumerate(sent)]
     gi, = other_rows([0], share_x, x, yb, e, alpha, jnp.float32)
-    grad_imu, grad_cam = add_up([gi, *sent], [grad_cam, *parts])
+    grad_imu, grad_cam = add_up([gi, *sent], [grad_cam, *parts], scale)
     return grad_imu, grad_cam[None]
 
 

time: 159 us -> 152 us (0.956)
  blocking collectives: 7.83 us -> 0 us
  starting transfers between devices: 35.5 us -> 42.5 us
  waiting for transfers between devices: 31.3 us -> 25.4 us
  local copies, waits for them, and re-layouts: 4.13 us -> 0.84 us
  Pallas kernels: 78.9 us -> 81.5 us
    all_to_all x1 -> x0, blocking collectives: 7.83 us -> none  [local(): lax.all_to_all(sums, ('row', 'col'), 0, 0, axis_index_groups=groups.squares)]
    ppermute x33 -> x38, starting transfers between devices: 35.5 us -> 42.5 us  [swap(): lax.ppermute(value, ('row', 'col'), [(i, i ^ mask) for i in range(self.co...]
    ppermute x33 -> x38, waiting for transfers between devices: 31.3 us -> 25.4 us  [swap(): lax.ppermute(value, ('row', 'col'), [(i, i ^ mask) for i in range(self.co...]
    unnamed x10 -> x0, local copies, waits for them, and re-layouts: 4.13 us -> none
    pallas_call x4 -> x5, Pallas kernels: 28.9 us -> 31.2 us  [the longest x1 10.1 us: row_lse_late(): pl.pallas_call(functools.partial(row_lse_late_kernel, width, len(ys)), ou...]
  transfers between devices with their start and end apart: 33 -> 38, of which waited for: 22 -> 23; matrix products, arithmetic and copies ran while one was open for 0% -> 1% of each run, Pallas kernels for 8% -> 17%
where the time goes in v9:
time: 152 us
  Pallas kernels  81.5 us (54%)
  starting transfers between devices  42.5 us (28%)
  waiting for transfers between devices  25.4 us (17%)
    ppermute x38, starting transfers between devices, swap(): lax.ppermute(value, ('row', 'col'), [(i, i ^ mask) for i in range(self.co...  42.5 us
    pallas_call x1, Pallas kernels, column_lse(): pl.pallas_call(functools.partial(column_lse_kernel, width, chunk, len(got...  31 us
    ppermute x38, waiting for transfers between devices, swap(): lax.ppermute(value, ('row', 'col'), [(i, i ^ mask) for i in range(self.co...  25.4 us
    pallas_call x4, Pallas kernels, weighted(): pl.pallas_call(functools.partial(kernel, width, tuple(shifts), parts), ou...  14 us
    pallas_call x1, Pallas kernels, row_lse_late(): pl.pallas_call(functools.partial(row_lse_late_kernel, width, len(ys)), ou...  10.1 us
    pallas_call x1, Pallas kernels, row_lse_early(): pl.pallas_call(functools.partial(row_lse_early_kernel, width, len(xs)), o...  6.69 us
    pallas_call x1, Pallas kernels, row_lse_middle(): pl.pallas_call(functools.partial(row_lse_middle_kernel, width, len(ys)),...  6.58 us
    pallas_call x1, Pallas kernels, column_grad(): pl.pallas_call(functools.partial(column_grad_kernel, width), out_shape=(s...  5.76 us
  transfers between devices with their start and end apart: 38, of which 23 were waited for; matrix products, arithmetic and copies ran while one was open for 1% of the time, Pallas kernels for 17%

profile of v9, /device:TPU:0, one launch (start us, length us, event | category | flops | bytes accessed | tf_op | source)
XLA Modules:
  0.0 152.1 jit_solution(17607217523709091749)
XLA Ops:
  0.6 4.1 %collective-permute-start.5 = (bf16[512,128]{1,0:T(8,128)(2,1)}, bf16[512,128]{1,0:T(8,128)(2,1)S(1)}, u32[]{:S(2)}, u32[]{:S(2)}) collective-permute-start(bf16[512,128]{1,0:T(8,128)(2,1)} %bitcast.77), channel_id=1, source_target_pairs={{0,4},{1,5},{2,6},{3,7},{4,0},{5,1},{6,2},{7,3},{8,12},{9,13},{10,... | collective-permute-start | bytes 393224 | tf_op jit(solution)/shard_map/ppermute | solution.py:573
  4.7 1.5 collective-permute-start
  6.3 1.4 collective-permute-start.2
  8.2 3.0 %collective-permute-done.5.refs_1_ = bf16[512,128]{1,0:T(8,128)(2,1)S(1)} collective-permute-done((bf16[512,128]{1,0:T(8,128)(2,1)}, bf16[512,128]{1,0:T(8,128)(2,1)S(1)}, u32[]{:S(2)}, u32[]{:S(2)}) %collective-permute-start.5) | collective-permute-done | bytes 131104 | tf_op jit(solution)/shard_map/ppermute | solution.py:573
  12.1 1.2 collective-permute-start.6
  13.3 1.0 pad_maximum_fusion.own_ref
  14.9 6.7 %row_lse_early.1 = (bf16[2048,128]{1,0:T(8,128)(2,1)S(1)}, bf16[128,2048]{1,0:T(8,128)(2,1)S(1)}, f32[1,2048]{1,0:T(1,128)S(1)}) custom-call(bf16[1024,128]{1,0:T(8,128)(2,1)S(1)} %pad_maximum_fusion.own_ref, bf16[512,128]{1,0:T(8,128)(2,1)S(1)} %collective-permute-done.refs_0_, bf16[512,128]{1,0:T(8,128)(2,1)S(1)} %collective-permute-done.1.refs_1_, ...), custom_call_target="tpu_custom_call" | custom-call | flops 536870912 | bytes 786432 | tf_op jit(solution)/shard_map/row_lse_early/pallas_call | solution.py:305
  22.2 6.6 %row_lse_middle.1.first_ref = f32[1,2048]{1,0:T(1,128)S(1)} custom-call(bf16[2048,128]{1,0:T(8,128)(2,1)S(1)} %get-tuple-element.46.x_ref, f32[1,2048]{1,0:T(1,128)S(1)} %get-tuple-element.48.first_ref, bf16[512,128]{1,0:T(8,128)(2,1)S(1)} %collective-permute-done.4.refs_0_, bf16[512,128]{1,0:T(8,128)(2,1)S(1)} %collective-permute-done.5.refs_1_), custom_call_target="tpu_custom_call" | custom-call | flops 536870912 | bytes 786432 | tf_op jit(solution)/shard_map/row_lse_middle/pallas_call | solution.py:320
  30.2 10.1 %row_lse_late.1 = (bf16[4096,128]{1,0:T(8,128)(2,1)S(1)}, f32[1,3072]{1,0:T(1,128)S(1)}) custom-call(bf16[1024,128]{1,0:T(8,128)(2,1)S(1)} %pad_maximum_fusion.own_ref, f32[1,2048]{1,0:T(1,128)S(1)} %bitcast.66, bf16[2048,128]{1,0:T(8,128)(2,1)S(1)} %get-tuple-element.46.x_ref, f32[1,2048]{1,0:T(1,128)S(1)} %row_lse_middle.1.first_ref, ...), custom_call_target="tpu_custom_call" | custom-call | flops 1073741824 | bytes 1048576 | tf_op jit(solution)/shard_map/row_lse_late/pallas_call | solution.py:339
  40.4 3.4 %collective-permute-start.10 = (f32[3072]{0:T(1024)S(1)}, f32[3072]{0:T(1024)S(1)}, u32[]{:S(2)}, u32[]{:S(2)}) collective-permute-start(f32[3072]{0:T(1024)S(1)} %bitcast.73), channel_id=1, source_target_pairs={{0,1},{1,0},{2,3},{3,2},{4,5},{5,4},{6,7},{7,6},{8,9},{9,8},{10,11... | collective-permute-start | bytes 36872 | tf_op jit(solution)/shard_map/ppermute | solution.py:573
  43.8 1.1 collective-permute-done.12
  45.5 31.0 %column_lse.1 = (f32[1,5120]{1,0:T(1,128)S(1)}, bf16[2048,4096]{1,0:T(8,128)(2,1)S(1)}, f32[1,4096]{1,0:T(1,128)S(1)}, f32[1,2048]{1,0:T(1,128)S(1)}) custom-call(bf16[2048,128]{1,0:T(8,128)(2,1)S(1)} %get-tuple-element.46.x_ref, bf16[4096,128]{1,0:T(8,128)(2,1)S(1)} %get-tuple-element.53.y_ref, f32[1,2048]{1,0:T(1,128)S(1)} %bitcast.67, ...), custom_call_target="tpu_custom_call" | custom-call | flops 2147483648 | bytes 1572864 | tf_op jit(solution)/shard_map/column_lse/pallas_call | solution.py:353
  76.6 1.2 collective-permute-done.13
  77.8 3.1 %collective-permute-start.16 = (f32[5120]{0:T(1024)S(1)}, f32[5120]{0:T(1024)S(1)}, u32[]{:S(2)}, u32[]{:S(2)}) collective-permute-start(f32[5120]{0:T(1024)S(1)} %bitcast.33), channel_id=1, source_target_pairs={{0,6},{1,7},{2,4},{3,5},{4,2},{5,3},{6,0},{7,1},{8,14},{9,15},{10,... | collective-permute-start | bytes 61448 | tf_op jit(solution)/shard_map/ppermute | solution.py:573
  81.0 1.3 collective-permute-start.14
  82.3 1.2 collective-permute-done.16
  83.5 2.4 %collective-permute-done.15 = f32[5120]{0:T(1024)S(1)} collective-permute-done((f32[5120]{0:T(1024)S(1)}, f32[5120]{0:T(1024)S(1)}, u32[]{:S(2)}, u32[]{:S(2)}) %collective-permute-start.15) | collective-permute-done | bytes 20512 | tf_op jit(solution)/shard_map/ppermute | solution.py:573
  85.9 4.5 %weighted_sum.4 = (f32[1,2048]{1,0:T(1,128)S(1)}, f32[1,4096]{1,0:T(1,128)S(1)}, f32[1,4096]{1,0:T(1,128)S(1)}) custom-call(bf16[2048,4096]{1,0:T(8,128)(2,1)S(1)} %get-tuple-element.55.e_ref, f32[1,4096]{1,0:T(1,128)S(1)} %get-tuple-element.57.shift_ref, f32[1,5120]{1,0:T(1,128)S(1)} %pair.3.refs_0_, f32[1,5120]{1,0:T(1,128)S(1)} %bitcast.44, ...), custom_call_target="tpu_custom_call" | custom-call | flops 16777216 | bytes 16777216 | tf_op jit(solution)/shard_map/weighted_sum/pallas_call | solution.py:274
  90.3 1.3 collective-permute-start.19
  92.3 1.6 %collective-permute-start.17 = (f32[2048]{0:T(1024)S(1)}, f32[2048]{0:T(1024)S(1)}, u32[]{:S(2)}, u32[]{:S(2)}) collective-permute-start(f32[2048]{0:T(1024)S(1)} %bitcast.59), channel_id=1, source_target_pairs={{0,1},{1,0},{2,3},{3,2},{4,5},{5,4},{6,7},{7,6},{8,9},{9,8},{10,11... | collective-permute-start | bytes 24584 | tf_op jit(solution)/shard_map/ppermute | solution.py:573
  93.9 1.1 collective-permute-done.19
  96.0 2.8 %weighted_sum.5 = (f32[1,4096]{1,0:T(1,128)S(1)}, f32[1,2048]{1,0:T(1,128)}) custom-call(bf16[2048,4096]{1,0:T(8,128)(2,1)S(1)} %get-tuple-element.55.e_ref, f32[1,2048]{1,0:T(1,128)S(1)} %get-tuple-element.56.a_ref, f32[1,4096]{1,0:T(1,128)S(1)} %get-tuple-element.59.first_ref, f32[1,2048]{1,0:T(1,128)S(1)} %get-tuple-element.61.refs_0_, ...), custom_call_target="tpu_custom_call" | custom-call | flops 16777216 | bytes 16777216 | tf_op jit(solution)/shard_map/weighted_sum/pallas_call | solution.py:274
  98.7 1.2 collective-permute-done.20
  99.9 2.2 %collective-permute-start.23 = (f32[4096]{0:T(1024)S(1)}, f32[4096]{0:T(1024)S(1)}, u32[]{:S(2)}, u32[]{:S(2)}) collective-permute-start(f32[4096]{0:T(1024)S(1)} %bitcast.36), channel_id=1, source_target_pairs={{0,6},{1,7},{2,4},{3,5},{4,2},{5,3},{6,0},{7,1},{8,14},{9,15},{10,... | collective-permute-start | bytes 49160 | tf_op jit(solution)/shard_map/ppermute | solution.py:573
  102.1 1.1 collective-permute-start.22
  103.3 1.1 collective-permute-start.21
  104.4 1.4 collective-permute-done.23
  105.8 1.1 collective-permute-done.22
  107.0 4.4 %weighted_sum.6.refs_0_ = f32[1,2048]{1,0:T(1,128)S(1)} custom-call(bf16[2048,4096]{1,0:T(8,128)(2,1)S(1)} %get-tuple-element.55.e_ref, f32[1,4096]{1,0:T(1,128)S(1)} %get-tuple-element.59.first_ref, f32[1,4096]{1,0:T(1,128)S(1)} %get-tuple-element.60.b_ref, f32[1,4096]{1,0:T(1,128)S(1)} %pair.4.refs_0_, f32[1,4096]{1,0:T(1,128)S(1)} %bitcast.56, ...), custom_call_target="tpu_custom_call" | custom-call | flops 16777216 | bytes 16777216 | tf_op jit(solution)/shard_map/weighted_sum/pallas_call | solution.py:274
  111.5 2.2 %collective-permute-start.26 = (f32[2048]{0:T(1024)S(1)}, f32[2048]{0:T(1024)S(1)}, u32[]{:S(2)}, u32[]{:S(2)}) collective-permute-start(f32[2048]{0:T(1024)S(1)} %bitcast.39), channel_id=1, source_target_pairs={{0,17},{1,16},{2,19},{3,18},{4,21},{5,20},{6,23},{7,22},{8,25},{9,... | collective-permute-start | bytes 24584 | tf_op jit(solution)/shard_map/ppermute | solution.py:573
  115.0 1.1 collective-permute-done.26
  116.1 1.2 collective-permute-done.25
  117.8 2.3 %weighted_sum.7 = (f32[1,4096]{1,0:T(1,128)S(1)}, f32[1,2048]{1,0:T(1,128)S(1)}) custom-call(bf16[2048,4096]{1,0:T(8,128)(2,1)S(1)} %get-tuple-element.55.e_ref, f32[1,2048]{1,0:T(1,128)S(1)} %get-tuple-element.56.a_ref, f32[1,4096]{1,0:T(1,128)S(1)} %get-tuple-element.59.first_ref, f32[1,2048]{1,0:T(1,128)S(1)} %weighted_sum.6.refs_0_, ...), custom_call_target="tpu_custom_call" | custom-call | flops 16777216 | bytes 16777216 | tf_op jit(solution)/shard_map/weighted_sum/pallas_call | solution.py:274
  120.2 1.2 collective-permute-done.27
  121.4 2.1 %collective-permute-start.30 = (f32[4096]{0:T(1024)S(1)}, f32[4096]{0:T(1024)S(1)}, u32[]{:S(2)}, u32[]{:S(2)}) collective-permute-start(f32[4096]{0:T(1024)S(1)} %bitcast.47), channel_id=1, source_target_pairs={{0,6},{1,7},{2,4},{3,5},{4,2},{5,3},{6,0},{7,1},{8,14},{9,15},{10,... | collective-permute-start | bytes 49160 | tf_op jit(solution)/shard_map/ppermute | solution.py:573
  123.5 1.0 collective-permute-start.29
  124.5 1.4 collective-permute-start.28
  125.9 5.8 %column_grad.1 = (f32[2048,128]{1,0:T(8,128)S(1)}, bf16[2048,128]{1,0:T(8,128)(2,1)S(1)}) custom-call(bf16[128,2048]{1,0:T(8,128)(2,1)S(1)} %get-tuple-element.68.xt_ref, bf16[4096,128]{1,0:T(8,128)(2,1)S(1)} %get-tuple-element.53.y_ref, bf16[2048,4096]{1,0:T(8,128)(2,1)S(1)} %get-tuple-element.55.e_ref, f32[1,2048]{1,0:T(1,128)S(1)} %get-tuple-element.65.alpha_ref, ...), custom_call_target="tpu_custom_call" | custom-call | flops 4294967296 | bytes 16777216 | tf_op jit(solution)/shard_map/column_grad/pallas_call | solution.py:415
  131.8 2.1 %first_rows.1 = (bf16[4096,256]{1,0:T(8,128)(2,1)S(1)}, f32[1,512]{1,0:T(1,128)S(1)}, bf16[512,128]{1,0:T(8,128)(2,1)S(1)}) custom-call(bf16[2048,128]{1,0:T(8,128)(2,1)S(1)} %get-tuple-element.46.x_ref, bf16[4096,128]{1,0:T(8,128)(2,1)S(1)} %get-tuple-element.53.y_ref, bf16[2048,4096]{1,0:T(8,128)(2,1)S(1)} %get-tuple-element.55.e_ref, ...), custom_call_target="tpu_custom_call" | custom-call | flops 34359738368 | bytes 134217728 | tf_op jit(solution)/shard_map/first_rows/pallas_call | solution.py:490
  134.6 2.0 %collective-permute-start.36 = (bf16[512,128]{1,0:T(8,128)(2,1)S(1)}, bf16[512,128]{1,0:T(8,128)(2,1)S(1)}, u32[]{:S(2)}, u32[]{:S(2)}) collective-permute-start(bf16[512,128]{1,0:T(8,128)(2,1)S(1)} %get-tuple-element.86), channel_id=1, source_target_pairs={{0,4},{1,5},{2,6},{3,7},{4,0},{5,1},{6,2},{7,3},{8,12},{9,13},{10,... | collective-permute-start | bytes 393224 | tf_op jit(solution)/shard_map/ppermute | solution.py:573
  136.6 1.8 %collective-permute-start.37 = (bf16[512,128]{1,0:T(8,128)(2,1)S(1)}, bf16[512,128]{1,0:T(8,128)(2,1)S(1)}, u32[]{:S(2)}, u32[]{:S(2)}) collective-permute-start(bf16[512,128]{1,0:T(8,128)(2,1)S(1)} %get-tuple-element.87), channel_id=1, source_target_pairs={{0,6},{1,7},{2,4},{3,5},{4,2},{5,3},{6,0},{7,1},{8,14},{9,15},{10,... | collective-permute-start | bytes 393224 | tf_op jit(solution)/shard_map/ppermute | solution.py:573
  138.4 2.6 %other_rows.3 = (bf16[512,128]{1,0:T(8,128)(2,1)S(1)}, bf16[512,128]{1,0:T(8,128)(2,1)S(1)}) custom-call(bf16[2048,128]{1,0:T(8,128)(2,1)S(1)} %get-tuple-element.46.x_ref, bf16[4096,256]{1,0:T(8,128)(2,1)S(1)} %get-tuple-element.76.yb_ref, bf16[2048,4096]{1,0:T(8,128)(2,1)S(1)} %get-tuple-element.55.e_ref, f32[1,2048]{1,0:T(1,128)S(1)} %get-tuple-element.65.alpha_ref), custom_call_target="tpu_custom_call" | custom-call | flops 2147483648 | bytes 8388608 | tf_op jit(solution)/shard_map/other_rows/pallas_call | solution.py:508
  141.9 1.0 collective-permute-start.33
  143.4 2.1 %collective-permute-start.35 = (bf16[512,128]{1,0:T(8,128)(2,1)S(1)}, bf16[512,128]{1,0:T(8,128)(2,1)S(1)}, u32[]{:S(2)}, u32[]{:S(2)}) collective-permute-start(bf16[512,128]{1,0:T(8,128)(2,1)S(1)} %get-tuple-element.83), channel_id=1, source_target_pairs={{0,17},{1,16},{2,19},{3,18},{4,21},{5,20},{6,23},{7,22},{8,25},{9,... | collective-permute-start | bytes 393224 | tf_op jit(solution)/shard_map/ppermute | solution.py:573
  145.4 1.4 other_rows.2.refs_0_
  147.6 1.8 %collective-permute-done.34.refs_2_ = bf16[512,128]{1,0:T(8,128)(2,1)S(1)} collective-permute-done((bf16[512,128]{1,0:T(8,128)(2,1)S(1)}, bf16[512,128]{1,0:T(8,128)(2,1)S(1)}, u32[]{:S(2)}, u32[]{:S(2)}) %collective-permute-start.34) | collective-permute-done | bytes 131104 | tf_op jit(solution)/shard_map/ppermute | solution.py:573
  149.3 1.7 %collective-permute-done.35.refs_3_ = bf16[512,128]{1,0:T(8,128)(2,1)S(1)} collective-permute-done((bf16[512,128]{1,0:T(8,128)(2,1)S(1)}, bf16[512,128]{1,0:T(8,128)(2,1)S(1)}, u32[]{:S(2)}, u32[]{:S(2)}) %collective-permute-start.35) | collective-permute-done | bytes 131104 | tf_op jit(solution)/shard_map/ppermute | solution.py:573
  151.0 1.1 add_up.1
  (48 shorter events, 11.5 us)
Async XLA Ops:
  0.6 10.6 %collective-permute-start.5 = (bf16[512,128]{1,0:T(8,128)(2,1)}, bf16[512,128]{1,0:T(8,128)(2,1)S(1)}, u32[]{:S(2)}, u32[]{:S(2)}) collective-permute-start(bf16[512,128]{1,0:T(8,128)(2,1)} %bitcast.77), channel_id=1, source_target_pairs={{0,4},{1,5},{2,6},{3,7},{4,0},{5,1},{6,2},{7,3},{8,12},{9,13},{10,... | collective-permute-start | bytes 393224 | tf_op jit(solution)/shard_map/ppermute | solution.py:573
  4.7 7.3 %collective-permute-start.3 = (bf16[512,128]{1,0:T(8,128)(2,1)}, bf16[512,128]{1,0:T(8,128)(2,1)S(1)}, u32[]{:S(2)}, u32[]{:S(2)}) collective-permute-start(bf16[512,128]{1,0:T(8,128)(2,1)} %bitcast.78), channel_id=1, source_target_pairs={{0,8},{1,9},{2,10},{3,11},{4,12},{5,13},{6,14},{7,15},{8,0},{9,1},... | collective-permute-start | bytes 393224 | tf_op jit(solution)/shard_map/ppermute | solution.py:573
  4.7 9.6 %collective-permute-start = (bf16[512,128]{1,0:T(8,128)(2,1)}, bf16[512,128]{1,0:T(8,128)(2,1)S(1)}, u32[]{:S(2)}, u32[]{:S(2)}) collective-permute-start(bf16[512,128]{1,0:T(8,128)(2,1)} %param.4), channel_id=1, source_target_pairs={{0,1},{1,0},{2,3},{3,2},{4,5},{5,4},{6,7},{7,6},{8,9},{9,8},{10,11... | collective-permute-start | bytes 393224 | tf_op jit(solution)/shard_map/ppermute | solution.py:573
  6.3 8.0 %collective-permute-start.2 = (bf16[512,128]{1,0:T(8,128)(2,1)}, bf16[512,128]{1,0:T(8,128)(2,1)S(1)}, u32[]{:S(2)}, u32[]{:S(2)}) collective-permute-start(bf16[512,128]{1,0:T(8,128)(2,1)} %param.4), channel_id=1, source_target_pairs={{0,17},{1,16},{2,19},{3,18},{4,21},{5,20},{6,23},{7,22},{8,25},{9,... | collective-permute-start | bytes 393224 | tf_op jit(solution)/shard_map/ppermute | solution.py:573
  7.7 7.2 %collective-permute-start.1 = (bf16[512,128]{1,0:T(8,128)(2,1)}, bf16[512,128]{1,0:T(8,128)(2,1)S(1)}, u32[]{:S(2)}, u32[]{:S(2)}) collective-permute-start(bf16[512,128]{1,0:T(8,128)(2,1)} %param.4), channel_id=1, source_target_pairs={{0,16},{1,17},{2,18},{3,19},{4,20},{5,21},{6,22},{7,23},{8,24},{9,... | collective-permute-start | bytes 393224 | tf_op jit(solution)/shard_map/ppermute | solution.py:573
  11.2 10.3 %collective-permute-start.4 = (bf16[512,128]{1,0:T(8,128)(2,1)}, bf16[512,128]{1,0:T(8,128)(2,1)S(1)}, u32[]{:S(2)}, u32[]{:S(2)}) collective-permute-start(bf16[512,128]{1,0:T(8,128)(2,1)} %bitcast.79), channel_id=1, source_target_pairs={{0,2},{1,3},{2,0},{3,1},{4,6},{5,7},{6,4},{7,5},{8,10},{9,11},{10,... | collective-permute-start | bytes 393224 | tf_op jit(solution)/shard_map/ppermute | solution.py:573
  12.1 16.7 %collective-permute-start.6 = (bf16[512,128]{1,0:T(8,128)(2,1)S(1)}, bf16[512,128]{1,0:T(8,128)(2,1)S(1)}, u32[]{:S(2)}, u32[]{:S(2)}) collective-permute-start(bf16[512,128]{1,0:T(8,128)(2,1)S(1)} %collective-permute-done.5.refs_1_), channel_id=1, source_target_pairs={{0,2},{1,3},{2,0},{3,1},{4,6},{5,7},{6,4},{7,5},{8,10},{9,11},{10,... | collective-permute-start | bytes 393224 | tf_op jit(solution)/shard_map/ppermute | solution.py:573
  21.6 8.2 %collective-permute-start.7 = (bf16[512,128]{1,0:T(8,128)(2,1)S(1)}, bf16[512,128]{1,0:T(8,128)(2,1)S(1)}, u32[]{:S(2)}, u32[]{:S(2)}) collective-permute-start(bf16[512,128]{1,0:T(8,128)(2,1)S(1)} %collective-permute-done.4.refs_0_), channel_id=1, source_target_pairs={{0,8},{1,9},{2,10},{3,11},{4,12},{5,13},{6,14},{7,15},{8,0},{9,1},... | collective-permute-start | bytes 393224 | tf_op jit(solution)/shard_map/ppermute | solution.py:573
  21.7 8.1 %collective-permute-start.8 = (bf16[512,128]{1,0:T(8,128)(2,1)S(1)}, bf16[512,128]{1,0:T(8,128)(2,1)S(1)}, u32[]{:S(2)}, u32[]{:S(2)}) collective-permute-start(bf16[512,128]{1,0:T(8,128)(2,1)S(1)} %collective-permute-done.5.refs_1_), channel_id=1, source_target_pairs={{0,8},{1,9},{2,10},{3,11},{4,12},{5,13},{6,14},{7,15},{8,0},{9,1},... | collective-permute-start | bytes 393224 | tf_op jit(solution)/shard_map/ppermute | solution.py:573
  28.8 1.4 collective-permute-start.9
  40.3 4.7 %collective-permute-start.12 = (f32[3072]{0:T(1024)S(1)}, f32[3072]{0:T(1024)S(1)}, u32[]{:S(2)}, u32[]{:S(2)}) collective-permute-start(f32[3072]{0:T(1024)S(1)} %bitcast.71), channel_id=1, source_target_pairs={{0,17},{1,16},{2,19},{3,18},{4,21},{5,20},{6,23},{7,22},{8,25},{9,... | collective-permute-start | bytes 36872 | tf_op jit(solution)/shard_map/ppermute | solution.py:573
  40.4 4.6 %collective-permute-start.11 = (f32[3072]{0:T(1024)S(1)}, f32[3072]{0:T(1024)S(1)}, u32[]{:S(2)}, u32[]{:S(2)}) collective-permute-start(f32[3072]{0:T(1024)S(1)} %bitcast.72), channel_id=1, source_target_pairs={{0,16},{1,17},{2,18},{3,19},{4,20},{5,21},{6,22},{7,23},{8,24},{9,... | collective-permute-start | bytes 36872 | tf_op jit(solution)/shard_map/ppermute | solution.py:573
  40.4 5.1 %collective-permute-start.10 = (f32[3072]{0:T(1024)S(1)}, f32[3072]{0:T(1024)S(1)}, u32[]{:S(2)}, u32[]{:S(2)}) collective-permute-start(f32[3072]{0:T(1024)S(1)} %bitcast.73), channel_id=1, source_target_pairs={{0,1},{1,0},{2,3},{3,2},{4,5},{5,4},{6,7},{7,6},{8,9},{9,8},{10,11... | collective-permute-start | bytes 36872 | tf_op jit(solution)/shard_map/ppermute | solution.py:573
  76.5 1.3 collective-permute-start.13
  77.8 5.6 %collective-permute-start.16 = (f32[5120]{0:T(1024)S(1)}, f32[5120]{0:T(1024)S(1)}, u32[]{:S(2)}, u32[]{:S(2)}) collective-permute-start(f32[5120]{0:T(1024)S(1)} %bitcast.33), channel_id=1, source_target_pairs={{0,6},{1,7},{2,4},{3,5},{4,2},{5,3},{6,0},{7,1},{8,14},{9,15},{10,... | collective-permute-start | bytes 61448 | tf_op jit(solution)/shard_map/ppermute | solution.py:573
  81.0 4.9 %collective-permute-start.15 = (f32[5120]{0:T(1024)S(1)}, f32[5120]{0:T(1024)S(1)}, u32[]{:S(2)}, u32[]{:S(2)}) collective-permute-start(f32[5120]{0:T(1024)S(1)} %bitcast.34), channel_id=1, source_target_pairs={{0,4},{1,5},{2,6},{3,7},{4,0},{5,1},{6,2},{7,3},{8,12},{9,13},{10,... | collective-permute-start | bytes 61448 | tf_op jit(solution)/shard_map/ppermute | solution.py:573
  81.0 4.8 %collective-permute-start.14 = (f32[5120]{0:T(1024)S(1)}, f32[5120]{0:T(1024)S(1)}, u32[]{:S(2)}, u32[]{:S(2)}) collective-permute-start(f32[5120]{0:T(1024)S(1)} %bitcast.35), channel_id=1, source_target_pairs={{0,2},{1,3},{2,0},{3,1},{4,6},{5,7},{6,4},{7,5},{8,10},{9,11},{10,... | collective-permute-start | bytes 61448 | tf_op jit(solution)/shard_map/ppermute | solution.py:573
  90.3 4.6 %collective-permute-start.19 = (f32[2048]{0:T(1024)S(1)}, f32[2048]{0:T(1024)S(1)}, u32[]{:S(2)}, u32[]{:S(2)}) collective-permute-start(f32[2048]{0:T(1024)S(1)} %bitcast.57), channel_id=1, source_target_pairs={{0,17},{1,16},{2,19},{3,18},{4,21},{5,20},{6,23},{7,22},{8,25},{9,... | collective-permute-start | bytes 24584 | tf_op jit(solution)/shard_map/ppermute | solution.py:573
  91.7 3.7 %collective-permute-start.18 = (f32[2048]{0:T(1024)S(1)}, f32[2048]{0:T(1024)S(1)}, u32[]{:S(2)}, u32[]{:S(2)}) collective-permute-start(f32[2048]{0:T(1024)S(1)} %bitcast.58), channel_id=1, source_target_pairs={{0,16},{1,17},{2,18},{3,19},{4,20},{5,21},{6,22},{7,23},{8,24},{9,... | collective-permute-start | bytes 24584 | tf_op jit(solution)/shard_map/ppermute | solution.py:573
  92.3 3.7 %collective-permute-start.17 = (f32[2048]{0:T(1024)S(1)}, f32[2048]{0:T(1024)S(1)}, u32[]{:S(2)}, u32[]{:S(2)}) collective-permute-start(f32[2048]{0:T(1024)S(1)} %bitcast.59), channel_id=1, source_target_pairs={{0,1},{1,0},{2,3},{3,2},{4,5},{5,4},{6,7},{7,6},{8,9},{9,8},{10,11... | collective-permute-start | bytes 24584 | tf_op jit(solution)/shard_map/ppermute | solution.py:573
  98.7 1.2 collective-permute-start.20
  99.9 5.8 %collective-permute-start.23 = (f32[4096]{0:T(1024)S(1)}, f32[4096]{0:T(1024)S(1)}, u32[]{:S(2)}, u32[]{:S(2)}) collective-permute-start(f32[4096]{0:T(1024)S(1)} %bitcast.36), channel_id=1, source_target_pairs={{0,6},{1,7},{2,4},{3,5},{4,2},{5,3},{6,0},{7,1},{8,14},{9,15},{10,... | collective-permute-start | bytes 49160 | tf_op jit(solution)/shard_map/ppermute | solution.py:573
  102.1 4.7 %collective-permute-start.22 = (f32[4096]{0:T(1024)S(1)}, f32[4096]{0:T(1024)S(1)}, u32[]{:S(2)}, u32[]{:S(2)}) collective-permute-start(f32[4096]{0:T(1024)S(1)} %bitcast.37), channel_id=1, source_target_pairs={{0,4},{1,5},{2,6},{3,7},{4,0},{5,1},{6,2},{7,3},{8,12},{9,13},{10,... | collective-permute-start | bytes 49160 | tf_op jit(solution)/shard_map/ppermute | solution.py:573
  103.3 3.7 %collective-permute-start.21 = (f32[4096]{0:T(1024)S(1)}, f32[4096]{0:T(1024)S(1)}, u32[]{:S(2)}, u32[]{:S(2)}) collective-permute-start(f32[4096]{0:T(1024)S(1)} %bitcast.38), channel_id=1, source_target_pairs={{0,2},{1,3},{2,0},{3,1},{4,6},{5,7},{6,4},{7,5},{8,10},{9,11},{10,... | collective-permute-start | bytes 49160 | tf_op jit(solution)/shard_map/ppermute | solution.py:573
  111.5 4.6 %collective-permute-start.26 = (f32[2048]{0:T(1024)S(1)}, f32[2048]{0:T(1024)S(1)}, u32[]{:S(2)}, u32[]{:S(2)}) collective-permute-start(f32[2048]{0:T(1024)S(1)} %bitcast.39), channel_id=1, source_target_pairs={{0,17},{1,16},{2,19},{3,18},{4,21},{5,20},{6,23},{7,22},{8,25},{9,... | collective-permute-start | bytes 24584 | tf_op jit(solution)/shard_map/ppermute | solution.py:573
  113.6 3.7 %collective-permute-start.25 = (f32[2048]{0:T(1024)S(1)}, f32[2048]{0:T(1024)S(1)}, u32[]{:S(2)}, u32[]{:S(2)}) collective-permute-start(f32[2048]{0:T(1024)S(1)} %bitcast.40), channel_id=1, source_target_pairs={{0,16},{1,17},{2,18},{3,19},{4,20},{5,21},{6,22},{7,23},{8,24},{9,... | collective-permute-start | bytes 24584 | tf_op jit(solution)/shard_map/ppermute | solution.py:573
  114.2 3.7 %collective-permute-start.24 = (f32[2048]{0:T(1024)S(1)}, f32[2048]{0:T(1024)S(1)}, u32[]{:S(2)}, u32[]{:S(2)}) collective-permute-start(f32[2048]{0:T(1024)S(1)} %bitcast.41), channel_id=1, source_target_pairs={{0,1},{1,0},{2,3},{3,2},{4,5},{5,4},{6,7},{7,6},{8,9},{9,8},{10,11... | collective-permute-start | bytes 24584 | tf_op jit(solution)/shard_map/ppermute | solution.py:573
  120.2 1.2 collective-permute-start.27
  121.4 10.3 %collective-permute-start.30 = (f32[4096]{0:T(1024)S(1)}, f32[4096]{0:T(1024)S(1)}, u32[]{:S(2)}, u32[]{:S(2)}) collective-permute-start(f32[4096]{0:T(1024)S(1)} %bitcast.47), channel_id=1, source_target_pairs={{0,6},{1,7},{2,4},{3,5},{4,2},{5,3},{6,0},{7,1},{8,14},{9,15},{10,... | collective-permute-start | bytes 49160 | tf_op jit(solution)/shard_map/ppermute | solution.py:573
  123.5 8.2 %collective-permute-start.29 = (f32[4096]{0:T(1024)S(1)}, f32[4096]{0:T(1024)S(1)}, u32[]{:S(2)}, u32[]{:S(2)}) collective-permute-start(f32[4096]{0:T(1024)S(1)} %bitcast.48), channel_id=1, source_target_pairs={{0,4},{1,5},{2,6},{3,7},{4,0},{5,1},{6,2},{7,3},{8,12},{9,13},{10,... | collective-permute-start | bytes 49160 | tf_op jit(solution)/shard_map/ppermute | solution.py:573
  124.5 7.3 %collective-permute-start.28 = (f32[4096]{0:T(1024)S(1)}, f32[4096]{0:T(1024)S(1)}, u32[]{:S(2)}, u32[]{:S(2)}) collective-permute-start(f32[4096]{0:T(1024)S(1)} %bitcast.49), channel_id=1, source_target_pairs={{0,2},{1,3},{2,0},{3,1},{4,6},{5,7},{6,4},{7,5},{8,10},{9,11},{10,... | collective-permute-start | bytes 49160 | tf_op jit(solution)/shard_map/ppermute | solution.py:573
  131.6 2.2 %collective-permute-start.31 = (bf16[2048,128]{1,0:T(8,128)(2,1)S(1)}, bf16[2048,128]{1,0:T(8,128)(2,1)S(1)}, u32[]{:S(2)}, u32[]{:S(2)}) collective-permute-start(bf16[2048,128]{1,0:T(8,128)(2,1)S(1)} %get-tuple-element.70), channel_id=1, source_target_pairs={{0,8},{1,9},{2,10},{3,11},{4,12},{5,13},{6,14},{7,15},{8,0},{9,1},... | collective-permute-start | bytes 1572872 | tf_op jit(solution)/shard_map/ppermute | solution.py:573
  134.0 8.0 %collective-permute-start.32 = (bf16[512,128]{1,0:T(8,128)(2,1)S(1)}, bf16[512,128]{1,0:T(8,128)(2,1)S(1)}, u32[]{:S(2)}, u32[]{:S(2)}) collective-permute-start(bf16[512,128]{1,0:T(8,128)(2,1)S(1)} %get-tuple-element.80), channel_id=1, source_target_pairs={{0,2},{1,3},{2,0},{3,1},{4,6},{5,7},{6,4},{7,5},{8,10},{9,11},{10,... | collective-permute-start | bytes 393224 | tf_op jit(solution)/shard_map/ppermute | solution.py:573
  134.6 12.9 %collective-permute-start.36 = (bf16[512,128]{1,0:T(8,128)(2,1)S(1)}, bf16[512,128]{1,0:T(8,128)(2,1)S(1)}, u32[]{:S(2)}, u32[]{:S(2)}) collective-permute-start(bf16[512,128]{1,0:T(8,128)(2,1)S(1)} %get-tuple-element.86), channel_id=1, source_target_pairs={{0,4},{1,5},{2,6},{3,7},{4,0},{5,1},{6,2},{7,3},{8,12},{9,13},{10,... | collective-permute-start | bytes 393224 | tf_op jit(solution)/shard_map/ppermute | solution.py:573
  136.6 10.9 %collective-permute-start.37 = (bf16[512,128]{1,0:T(8,128)(2,1)S(1)}, bf16[512,128]{1,0:T(8,128)(2,1)S(1)}, u32[]{:S(2)}, u32[]{:S(2)}) collective-permute-start(bf16[512,128]{1,0:T(8,128)(2,1)S(1)} %get-tuple-element.87), channel_id=1, source_target_pairs={{0,6},{1,7},{2,4},{3,5},{4,2},{5,3},{6,0},{7,1},{8,14},{9,15},{10,... | collective-permute-start | bytes 393224 | tf_op jit(solution)/shard_map/ppermute | solution.py:573
  141.9 5.6 %collective-permute-start.33 = (bf16[512,128]{1,0:T(8,128)(2,1)S(1)}, bf16[512,128]{1,0:T(8,128)(2,1)S(1)}, u32[]{:S(2)}, u32[]{:S(2)}) collective-permute-start(bf16[512,128]{1,0:T(8,128)(2,1)S(1)} %get-tuple-element.81), channel_id=1, source_target_pairs={{0,1},{1,0},{2,3},{3,2},{4,5},{5,4},{6,7},{7,6},{8,9},{9,8},{10,11... | collective-permute-start | bytes 393224 | tf_op jit(solution)/shard_map/ppermute | solution.py:573
  143.0 6.4 %collective-permute-start.34 = (bf16[512,128]{1,0:T(8,128)(2,1)S(1)}, bf16[512,128]{1,0:T(8,128)(2,1)S(1)}, u32[]{:S(2)}, u32[]{:S(2)}) collective-permute-start(bf16[512,128]{1,0:T(8,128)(2,1)S(1)} %get-tuple-element.82), channel_id=1, source_target_pairs={{0,16},{1,17},{2,18},{3,19},{4,20},{5,21},{6,22},{7,23},{8,24},{9,... | collective-permute-start | bytes 393224 | tf_op jit(solution)/shard_map/ppermute | solution.py:573
  143.4 7.7 %collective-permute-start.35 = (bf16[512,128]{1,0:T(8,128)(2,1)S(1)}, bf16[512,128]{1,0:T(8,128)(2,1)S(1)}, u32[]{:S(2)}, u32[]{:S(2)}) collective-permute-start(bf16[512,128]{1,0:T(8,128)(2,1)S(1)} %get-tuple-element.83), channel_id=1, source_target_pairs={{0,17},{1,16},{2,19},{3,18},{4,21},{5,20},{6,23},{7,22},{8,25},{9,... | collective-permute-start | bytes 393224 | tf_op jit(solution)/shard_map/ppermute | solution.py:573

commit v10 on v9

--- a/solution.py
+++ b/solution.py
@@ -299,7 +299,7 @@
     ]
 
 
-def row_lse_early(own, xs, y_other, width=512):
+def row_lse_early(own, xs, y_other, width=1024):
     share = y_other.shape[0]
     rows, depth = own.shape[0] - share + sum(part.shape[0] for part in xs), 2 * share
     return pl.pallas_call(
@@ -333,7 +333,7 @@
     )(x, first, *ys)
 
 
-def row_lse_late(own, x, ys, first, mass, tail, width=512):
+def row_lse_late(own, x, ys, first, mass, tail, width=256):
     rows, share = x.shape[0], ys[0].shape[0]
     depth = (len(ys) + 1) * share
     return pl.pallas_call(
@@ -348,7 +348,7 @@
     )(own, mass.reshape(1, -1), x, first, *ys)
 
 
-def column_lse(x, y, mass, tail, got, width=512, chunk=512):
+def column_lse(x, y, mass, tail, got, width=1024, chunk=256):
     rows, cols = x.shape[0], y.shape[0]
     return pl.pallas_call(
         functools.partial(column_lse_kernel, width, chunk, len(got)),
@@ -584,10 +584,13 @@
     def direct(value, masks):
         return [swap(value, mask) for mask in masks], range(len(masks))
 
+    xs, _ = direct(imu, across)
     near, far = [camera[0]], [swap(camera[0], core)]
     for z in range(1, nz):
-        near.append(swap(near[z & (z - 1)], along[z & -z]))
-    xs, _ = direct(imu, across)
+        part = near[z & (z - 1)]
+        if z & (z - 1):
+            part, near[z & -z], xs = lax.optimization_barrier((part, near[z & -z], xs))
+        near.append(swap(part, along[z & -z]))
 
     def pair(mass, place, share):
         return [lax.dynamic_slice_in_dim(mass, (place ^ k) * share, share, 0) for k in range(2)]
@@ -624,9 +627,10 @@
     yb, scale, last = first_rows([na - 1], share_x, x, y, e, alpha, first_beta, mass_b, got, 2 * nz)
     (grad_cam, *parts), yb = lax.optimization_barrier((shares(gc, swap(gc_send, core), nz), yb))
     parts = [swap(part, along[z + 1]) for z, part in enumerate(parts)]
-    sent = [*other_rows(list(range(1, na - 1)), share_x, x, yb, e, alpha, jnp.bfloat16), last]
-    sent, parts[0] = lax.optimization_barrier((sent, parts[0]))
-    sent = [swap(part, across[s + 1]) for s, part in enumerate(sent)]
+    last = swap(last, across[na - 1])
+    sent = other_rows(list(range(1, na - 1)), share_x, x, yb, e, alpha, jnp.bfloat16)
+    sent, parts[0], last = lax.optimization_barrier((sent, parts[0], last))
+    sent = [swap(part, across[s + 1]) for s, part in enumerate(sent)] + [last]
     gi, = other_rows([0], share_x, x, yb, e, alpha, jnp.float32)
     grad_imu, grad_cam = add_up([gi, *sent], [grad_cam, *parts], scale)
     return grad_imu, grad_cam[None]

time: 152 us -> 152 us (level)
  transfers between devices with their start and end apart: 38 -> 38, of which waited for: 23 -> 21; matrix products, arithmetic and copies ran while one was open for 1% -> 1% of each run, Pallas kernels for 17% -> 16%
where the time goes in v10:
time: 152 us
  Pallas kernels  82.3 us (54%)
  starting transfers between devices  42.5 us (28%)
  waiting for transfers between devices  24.7 us (16%)
    ppermute x38, starting transfers between devices, swap(): lax.ppermute(value, ('row', 'col'), [(i, i ^ mask) for i in range(self.co...  42.5 us
    pallas_call x1, Pallas kernels, column_lse(): pl.pallas_call(functools.partial(column_lse_kernel, width, chunk, len(got...  31.1 us
    ppermute x38, waiting for transfers between devices, swap(): lax.ppermute(value, ('row', 'col'), [(i, i ^ mask) for i in range(self.co...  24.7 us
    pallas_call x4, Pallas kernels, weighted(): pl.pallas_call(functools.partial(kernel, width, tuple(shifts), parts), ou...  14 us
    pallas_call x1, Pallas kernels, row_lse_late(): pl.pallas_call(functools.partial(row_lse_late_kernel, width, len(ys)), ou...  11 us
    pallas_call x1, Pallas kernels, row_lse_middle(): pl.pallas_call(functools.partial(row_lse_middle_kernel, width, len(ys)),...  6.58 us
    pallas_call x1, Pallas kernels, row_lse_early(): pl.pallas_call(functools.partial(row_lse_early_kernel, width, len(xs)), o...  6.5 us
    pallas_call x1, Pallas kernels, column_grad(): pl.pallas_call(functools.partial(column_grad_kernel, width), out_shape=(s...  5.76 us
  transfers between devices with their start and end apart: 38, of which 21 were waited for; matrix products, arithmetic and copies ran while one was open for 1% of the time, Pallas kernels for 16%

profile of v10, /device:TPU:0, one launch (start us, length us, event | category | flops | bytes accessed | tf_op | source)
XLA Modules:
  0.0 152.2 jit_solution(18209002530964826141)
XLA Ops:
  0.6 3.1 %collective-permute-start.1 = (bf16[512,128]{1,0:T(8,128)(2,1)}, bf16[512,128]{1,0:T(8,128)(2,1)S(1)}, u32[]{:S(2)}, u32[]{:S(2)}) collective-permute-start(bf16[512,128]{1,0:T(8,128)(2,1)} %bitcast.77), channel_id=1, source_target_pairs={{0,2},{1,3},{2,0},{3,1},{4,6},{5,7},{6,4},{7,5},{8,10},{9,11},{10,... | collective-permute-start | bytes 393224 | tf_op jit(solution)/shard_map/ppermute | solution.py:573
  3.7 2.6 %collective-permute-start = (bf16[512,128]{1,0:T(8,128)(2,1)}, bf16[512,128]{1,0:T(8,128)(2,1)S(1)}, u32[]{:S(2)}, u32[]{:S(2)}) collective-permute-start(bf16[512,128]{1,0:T(8,128)(2,1)} %bitcast.78), channel_id=1, source_target_pairs={{0,4},{1,5},{2,6},{3,7},{4,0},{5,1},{6,2},{7,3},{8,12},{9,13},{10,... | collective-permute-start | bytes 393224 | tf_op jit(solution)/shard_map/ppermute | solution.py:573
  6.3 1.5 collective-permute-start.3
  7.8 1.5 collective-permute-start.2
  9.8 2.9 %collective-permute-done.refs_1_ = bf16[512,128]{1,0:T(8,128)(2,1)S(1)} collective-permute-done((bf16[512,128]{1,0:T(8,128)(2,1)}, bf16[512,128]{1,0:T(8,128)(2,1)S(1)}, u32[]{:S(2)}, u32[]{:S(2)}) %collective-permute-start) | collective-permute-done | bytes 131104 | tf_op jit(solution)/shard_map/ppermute | solution.py:573
  12.7 3.1 %collective-permute-done.2.refs_0_ = bf16[512,128]{1,0:T(8,128)(2,1)S(1)} collective-permute-done((bf16[512,128]{1,0:T(8,128)(2,1)}, bf16[512,128]{1,0:T(8,128)(2,1)S(1)}, u32[]{:S(2)}, u32[]{:S(2)}) %collective-permute-start.2) | collective-permute-done | bytes 131104 | tf_op jit(solution)/shard_map/ppermute | solution.py:573
  16.2 1.0 pad_maximum_fusion.own_ref
  17.3 6.5 %row_lse_early.1 = (bf16[2048,128]{1,0:T(8,128)(2,1)S(1)}, bf16[128,2048]{1,0:T(8,128)(2,1)S(1)}, f32[1,2048]{1,0:T(1,128)S(1)}) custom-call(bf16[1024,128]{1,0:T(8,128)(2,1)S(1)} %pad_maximum_fusion.own_ref, bf16[512,128]{1,0:T(8,128)(2,1)S(1)} %collective-permute-done.2.refs_0_, bf16[512,128]{1,0:T(8,128)(2,1)S(1)} %collective-permute-done.3.refs_1_, ...), custom_call_target="tpu_custom_call" | custom-call | flops 536870912 | bytes 786432 | tf_op jit(solution)/shard_map/row_lse_early/pallas_call | solution.py:305
  24.3 6.6 %row_lse_middle.1.first_ref = f32[1,2048]{1,0:T(1,128)S(1)} custom-call(bf16[2048,128]{1,0:T(8,128)(2,1)S(1)} %get-tuple-element.54.x_ref, f32[1,2048]{1,0:T(1,128)S(1)} %get-tuple-element.57.first_ref, bf16[512,128]{1,0:T(8,128)(2,1)S(1)} %collective-permute-done.1.refs_0_, bf16[512,128]{1,0:T(8,128)(2,1)S(1)} %collective-permute-done.refs_1_), custom_call_target="tpu_custom_call" | custom-call | flops 536870912 | bytes 786432 | tf_op jit(solution)/shard_map/row_lse_middle/pallas_call | solution.py:320
  32.3 11.0 %row_lse_late.1 = (bf16[4096,128]{1,0:T(8,128)(2,1)S(1)}, f32[1,3072]{1,0:T(1,128)S(1)}) custom-call(bf16[1024,128]{1,0:T(8,128)(2,1)S(1)} %pad_maximum_fusion.own_ref, f32[1,2048]{1,0:T(1,128)S(1)} %bitcast.66, bf16[2048,128]{1,0:T(8,128)(2,1)S(1)} %get-tuple-element.54.x_ref, f32[1,2048]{1,0:T(1,128)S(1)} %row_lse_middle.1.first_ref, ...), custom_call_target="tpu_custom_call" | custom-call | flops 1073741824 | bytes 1048576 | tf_op jit(solution)/shard_map/row_lse_late/pallas_call | solution.py:339
  43.5 3.4 %collective-permute-start.10 = (f32[3072]{0:T(1024)S(1)}, f32[3072]{0:T(1024)S(1)}, u32[]{:S(2)}, u32[]{:S(2)}) collective-permute-start(f32[3072]{0:T(1024)S(1)} %bitcast.73), channel_id=1, source_target_pairs={{0,1},{1,0},{2,3},{3,2},{4,5},{5,4},{6,7},{7,6},{8,9},{9,8},{10,11... | collective-permute-start | bytes 36872 | tf_op jit(solution)/shard_map/ppermute | solution.py:573
  46.9 1.1 collective-permute-done.12
  48.6 31.1 %column_lse.1 = (f32[1,5120]{1,0:T(1,128)S(1)}, bf16[2048,4096]{1,0:T(8,128)(2,1)S(1)}, f32[1,4096]{1,0:T(1,128)S(1)}, f32[1,2048]{1,0:T(1,128)S(1)}) custom-call(bf16[2048,128]{1,0:T(8,128)(2,1)S(1)} %get-tuple-element.54.x_ref, bf16[4096,128]{1,0:T(8,128)(2,1)S(1)} %get-tuple-element.63.y_ref, f32[1,2048]{1,0:T(1,128)S(1)} %bitcast.67, ...), custom_call_target="tpu_custom_call" | custom-call | flops 2147483648 | bytes 1572864 | tf_op jit(solution)/shard_map/column_lse/pallas_call | solution.py:353
  79.8 1.2 collective-permute-done.13
  81.1 1.4 collective-permute-start.15
  82.5 2.9 %collective-permute-start.14 = (f32[5120]{0:T(1024)S(1)}, f32[5120]{0:T(1024)S(1)}, u32[]{:S(2)}, u32[]{:S(2)}) collective-permute-start(f32[5120]{0:T(1024)S(1)} %bitcast.35), channel_id=1, source_target_pairs={{0,2},{1,3},{2,0},{3,1},{4,6},{5,7},{6,4},{7,5},{8,10},{9,11},{10,... | collective-permute-start | bytes 61448 | tf_op jit(solution)/shard_map/ppermute | solution.py:573
  85.4 1.2 collective-permute-done.16
  87.2 4.5 %weighted_sum.4 = (f32[1,2048]{1,0:T(1,128)S(1)}, f32[1,4096]{1,0:T(1,128)S(1)}, f32[1,4096]{1,0:T(1,128)S(1)}) custom-call(bf16[2048,4096]{1,0:T(8,128)(2,1)S(1)} %get-tuple-element.65.e_ref, f32[1,4096]{1,0:T(1,128)S(1)} %get-tuple-element.67.shift_ref, f32[1,5120]{1,0:T(1,128)S(1)} %pair.3.refs_0_, f32[1,5120]{1,0:T(1,128)S(1)} %bitcast.44, ...), custom_call_target="tpu_custom_call" | custom-call | flops 16777216 | bytes 16777216 | tf_op jit(solution)/shard_map/weighted_sum/pallas_call | solution.py:274
  91.7 1.5 %collective-permute-start.19 = (f32[2048]{0:T(1024)S(1)}, f32[2048]{0:T(1024)S(1)}, u32[]{:S(2)}, u32[]{:S(2)}) collective-permute-start(f32[2048]{0:T(1024)S(1)} %bitcast.57), channel_id=1, source_target_pairs={{0,17},{1,16},{2,19},{3,18},{4,21},{5,20},{6,23},{7,22},{8,25},{9,... | collective-permute-start | bytes 24584 | tf_op jit(solution)/shard_map/ppermute | solution.py:573
  93.2 2.0 %collective-permute-start.18 = (f32[2048]{0:T(1024)S(1)}, f32[2048]{0:T(1024)S(1)}, u32[]{:S(2)}, u32[]{:S(2)}) collective-permute-start(f32[2048]{0:T(1024)S(1)} %bitcast.58), channel_id=1, source_target_pairs={{0,16},{1,17},{2,18},{3,19},{4,20},{5,21},{6,22},{7,23},{8,24},{9,... | collective-permute-start | bytes 24584 | tf_op jit(solution)/shard_map/ppermute | solution.py:573
  95.2 1.1 collective-permute-done.19
  96.9 1.9 %collective-permute-done.17 = f32[2048]{0:T(1024)S(1)} collective-permute-done((f32[2048]{0:T(1024)S(1)}, f32[2048]{0:T(1024)S(1)}, u32[]{:S(2)}, u32[]{:S(2)}) %collective-permute-start.17) | collective-permute-done | bytes 8224 | tf_op jit(solution)/shard_map/ppermute | solution.py:573
  98.9 2.8 %weighted_sum.5 = (f32[1,4096]{1,0:T(1,128)S(1)}, f32[1,2048]{1,0:T(1,128)}) custom-call(bf16[2048,4096]{1,0:T(8,128)(2,1)S(1)} %get-tuple-element.65.e_ref, f32[1,2048]{1,0:T(1,128)S(1)} %get-tuple-element.66.a_ref, f32[1,4096]{1,0:T(1,128)S(1)} %get-tuple-element.69.first_ref, f32[1,2048]{1,0:T(1,128)S(1)} %get-tuple-element.71.refs_0_, ...), custom_call_target="tpu_custom_call" | custom-call | flops 16777216 | bytes 16777216 | tf_op jit(solution)/shard_map/weighted_sum/pallas_call | solution.py:274
  101.6 1.2 collective-permute-done.20
  102.8 2.4 %collective-permute-start.23 = (f32[4096]{0:T(1024)S(1)}, f32[4096]{0:T(1024)S(1)}, u32[]{:S(2)}, u32[]{:S(2)}) collective-permute-start(f32[4096]{0:T(1024)S(1)} %bitcast.36), channel_id=1, source_target_pairs={{0,6},{1,7},{2,4},{3,5},{4,2},{5,3},{6,0},{7,1},{8,14},{9,15},{10,... | collective-permute-start | bytes 49160 | tf_op jit(solution)/shard_map/ppermute | solution.py:573
  105.3 1.1 collective-permute-start.22
  107.3 1.2 collective-permute-done.23
  108.5 1.5 collective-permute-done.22
  110.1 4.4 %weighted_sum.6.refs_0_ = f32[1,2048]{1,0:T(1,128)S(1)} custom-call(bf16[2048,4096]{1,0:T(8,128)(2,1)S(1)} %get-tuple-element.65.e_ref, f32[1,4096]{1,0:T(1,128)S(1)} %get-tuple-element.69.first_ref, f32[1,4096]{1,0:T(1,128)S(1)} %get-tuple-element.70.b_ref, f32[1,4096]{1,0:T(1,128)S(1)} %pair.4.refs_0_, f32[1,4096]{1,0:T(1,128)S(1)} %bitcast.56, ...), custom_call_target="tpu_custom_call" | custom-call | flops 16777216 | bytes 16777216 | tf_op jit(solution)/shard_map/weighted_sum/pallas_call | solution.py:274
  114.7 1.4 collective-permute-start.25
  116.1 2.0 %collective-permute-start.24 = (f32[2048]{0:T(1024)S(1)}, f32[2048]{0:T(1024)S(1)}, u32[]{:S(2)}, u32[]{:S(2)}) collective-permute-start(f32[2048]{0:T(1024)S(1)} %bitcast.41), channel_id=1, source_target_pairs={{0,1},{1,0},{2,3},{3,2},{4,5},{5,4},{6,7},{7,6},{8,9},{9,8},{10,11... | collective-permute-start | bytes 24584 | tf_op jit(solution)/shard_map/ppermute | solution.py:573
  118.1 1.1 collective-permute-done.26
  119.8 2.3 %weighted_sum.7 = (f32[1,4096]{1,0:T(1,128)S(1)}, f32[1,2048]{1,0:T(1,128)S(1)}) custom-call(bf16[2048,4096]{1,0:T(8,128)(2,1)S(1)} %get-tuple-element.65.e_ref, f32[1,2048]{1,0:T(1,128)S(1)} %get-tuple-element.66.a_ref, f32[1,4096]{1,0:T(1,128)S(1)} %get-tuple-element.69.first_ref, f32[1,2048]{1,0:T(1,128)S(1)} %weighted_sum.6.refs_0_, ...), custom_call_target="tpu_custom_call" | custom-call | flops 16777216 | bytes 16777216 | tf_op jit(solution)/shard_map/weighted_sum/pallas_call | solution.py:274
  122.2 1.2 collective-permute-done.27
  123.4 1.5 collective-permute-start.30
  124.8 1.0 collective-permute-start.29
  125.8 2.0 %collective-permute-start.28 = (f32[4096]{0:T(1024)S(1)}, f32[4096]{0:T(1024)S(1)}, u32[]{:S(2)}, u32[]{:S(2)}) collective-permute-start(f32[4096]{0:T(1024)S(1)} %bitcast.49), channel_id=1, source_target_pairs={{0,2},{1,3},{2,0},{3,1},{4,6},{5,7},{6,4},{7,5},{8,10},{9,11},{10,... | collective-permute-start | bytes 49160 | tf_op jit(solution)/shard_map/ppermute | solution.py:573
  127.8 5.8 %column_grad.1 = (f32[2048,128]{1,0:T(8,128)S(1)}, bf16[2048,128]{1,0:T(8,128)(2,1)S(1)}) custom-call(bf16[128,2048]{1,0:T(8,128)(2,1)S(1)} %get-tuple-element.78.xt_ref, bf16[4096,128]{1,0:T(8,128)(2,1)S(1)} %get-tuple-element.63.y_ref, bf16[2048,4096]{1,0:T(8,128)(2,1)S(1)} %get-tuple-element.65.e_ref, f32[1,2048]{1,0:T(1,128)S(1)} %get-tuple-element.75.alpha_ref, ...), custom_call_target="tpu_custom_call" | custom-call | flops 4294967296 | bytes 16777216 | tf_op jit(solution)/shard_map/column_grad/pallas_call | solution.py:415
  133.7 2.1 %first_rows.1 = (bf16[4096,256]{1,0:T(8,128)(2,1)S(1)}, f32[1,512]{1,0:T(1,128)S(1)}, bf16[512,128]{1,0:T(8,128)(2,1)S(1)}) custom-call(bf16[2048,128]{1,0:T(8,128)(2,1)S(1)} %get-tuple-element.54.x_ref, bf16[4096,128]{1,0:T(8,128)(2,1)S(1)} %get-tuple-element.63.y_ref, bf16[2048,4096]{1,0:T(8,128)(2,1)S(1)} %get-tuple-element.65.e_ref, ...), custom_call_target="tpu_custom_call" | custom-call | flops 34359738368 | bytes 134217728 | tf_op jit(solution)/shard_map/first_rows/pallas_call | solution.py:490
  135.8 1.5 %collective-permute-start.33 = (bf16[512,128]{1,0:T(8,128)(2,1)S(1)}, bf16[512,128]{1,0:T(8,128)(2,1)S(1)}, u32[]{:S(2)}, u32[]{:S(2)}) collective-permute-start(bf16[512,128]{1,0:T(8,128)(2,1)S(1)} %get-tuple-element.90), channel_id=1, source_target_pairs={{0,17},{1,16},{2,19},{3,18},{4,21},{5,20},{6,23},{7,22},{8,25},{9,... | collective-permute-start | bytes 393224 | tf_op jit(solution)/shard_map/ppermute | solution.py:573
  137.5 2.0 %collective-permute-start.36 = (bf16[512,128]{1,0:T(8,128)(2,1)S(1)}, bf16[512,128]{1,0:T(8,128)(2,1)S(1)}, u32[]{:S(2)}, u32[]{:S(2)}) collective-permute-start(bf16[512,128]{1,0:T(8,128)(2,1)S(1)} %get-tuple-element.96), channel_id=1, source_target_pairs={{0,4},{1,5},{2,6},{3,7},{4,0},{5,1},{6,2},{7,3},{8,12},{9,13},{10,... | collective-permute-start | bytes 393224 | tf_op jit(solution)/shard_map/ppermute | solution.py:573
  139.5 2.4 %collective-permute-start.37 = (bf16[512,128]{1,0:T(8,128)(2,1)S(1)}, bf16[512,128]{1,0:T(8,128)(2,1)S(1)}, u32[]{:S(2)}, u32[]{:S(2)}) collective-permute-start(bf16[512,128]{1,0:T(8,128)(2,1)S(1)} %get-tuple-element.97), channel_id=1, source_target_pairs={{0,6},{1,7},{2,4},{3,5},{4,2},{5,3},{6,0},{7,1},{8,14},{9,15},{10,... | collective-permute-start | bytes 393224 | tf_op jit(solution)/shard_map/ppermute | solution.py:573
  141.9 2.6 %other_rows.3 = (bf16[512,128]{1,0:T(8,128)(2,1)S(1)}, bf16[512,128]{1,0:T(8,128)(2,1)S(1)}) custom-call(bf16[2048,128]{1,0:T(8,128)(2,1)S(1)} %get-tuple-element.54.x_ref, bf16[4096,256]{1,0:T(8,128)(2,1)S(1)} %get-tuple-element.86.yb_ref, bf16[2048,4096]{1,0:T(8,128)(2,1)S(1)} %get-tuple-element.65.e_ref, f32[1,2048]{1,0:T(1,128)S(1)} %get-tuple-element.75.alpha_ref), custom_call_target="tpu_custom_call" | custom-call | flops 2147483648 | bytes 8388608 | tf_op jit(solution)/shard_map/other_rows/pallas_call | solution.py:508
  145.2 0.9 collective-permute-start.34
  146.2 1.1 collective-permute-start.35
  147.3 1.4 other_rows.2.refs_0_
  148.7 1.8 %collective-permute-done.36.refs_6_ = bf16[512,128]{1,0:T(8,128)(2,1)S(1)} collective-permute-done((bf16[512,128]{1,0:T(8,128)(2,1)S(1)}, bf16[512,128]{1,0:T(8,128)(2,1)S(1)}, u32[]{:S(2)}, u32[]{:S(2)}) %collective-permute-start.36) | collective-permute-done | bytes 131104 | tf_op jit(solution)/shard_map/ppermute | solution.py:573
  151.2 1.1 add_up.1
  (48 shorter events, 8.6 us)
Async XLA Ops:
  0.6 9.2 %collective-permute-start.1 = (bf16[512,128]{1,0:T(8,128)(2,1)}, bf16[512,128]{1,0:T(8,128)(2,1)S(1)}, u32[]{:S(2)}, u32[]{:S(2)}) collective-permute-start(bf16[512,128]{1,0:T(8,128)(2,1)} %bitcast.77), channel_id=1, source_target_pairs={{0,2},{1,3},{2,0},{3,1},{4,6},{5,7},{6,4},{7,5},{8,10},{9,11},{10,... | collective-permute-start | bytes 393224 | tf_op jit(solution)/shard_map/ppermute | solution.py:573
  3.7 8.9 %collective-permute-start = (bf16[512,128]{1,0:T(8,128)(2,1)}, bf16[512,128]{1,0:T(8,128)(2,1)S(1)}, u32[]{:S(2)}, u32[]{:S(2)}) collective-permute-start(bf16[512,128]{1,0:T(8,128)(2,1)} %bitcast.78), channel_id=1, source_target_pairs={{0,4},{1,5},{2,6},{3,7},{4,0},{5,1},{6,2},{7,3},{8,12},{9,13},{10,... | collective-permute-start | bytes 393224 | tf_op jit(solution)/shard_map/ppermute | solution.py:573
  6.3 6.4 %collective-permute-start.3 = (bf16[512,128]{1,0:T(8,128)(2,1)}, bf16[512,128]{1,0:T(8,128)(2,1)S(1)}, u32[]{:S(2)}, u32[]{:S(2)}) collective-permute-start(bf16[512,128]{1,0:T(8,128)(2,1)} %param.4), channel_id=1, source_target_pairs={{0,16},{1,17},{2,18},{3,19},{4,20},{5,21},{6,22},{7,23},{8,24},{9,... | collective-permute-start | bytes 393224 | tf_op jit(solution)/shard_map/ppermute | solution.py:573
  7.8 8.0 %collective-permute-start.2 = (bf16[512,128]{1,0:T(8,128)(2,1)}, bf16[512,128]{1,0:T(8,128)(2,1)S(1)}, u32[]{:S(2)}, u32[]{:S(2)}) collective-permute-start(bf16[512,128]{1,0:T(8,128)(2,1)} %param.4), channel_id=1, source_target_pairs={{0,1},{1,0},{2,3},{3,2},{4,5},{5,4},{6,7},{7,6},{8,9},{9,8},{10,11... | collective-permute-start | bytes 393224 | tf_op jit(solution)/shard_map/ppermute | solution.py:573
  9.3 6.5 %collective-permute-start.4 = (bf16[512,128]{1,0:T(8,128)(2,1)}, bf16[512,128]{1,0:T(8,128)(2,1)S(1)}, u32[]{:S(2)}, u32[]{:S(2)}) collective-permute-start(bf16[512,128]{1,0:T(8,128)(2,1)} %param.4), channel_id=1, source_target_pairs={{0,17},{1,16},{2,19},{3,18},{4,21},{5,20},{6,23},{7,22},{8,25},{9,... | collective-permute-start | bytes 393224 | tf_op jit(solution)/shard_map/ppermute | solution.py:573
  9.8 7.5 %collective-permute-start.5 = (bf16[512,128]{1,0:T(8,128)(2,1)}, bf16[512,128]{1,0:T(8,128)(2,1)S(1)}, u32[]{:S(2)}, u32[]{:S(2)}) collective-permute-start(bf16[512,128]{1,0:T(8,128)(2,1)} %bitcast.79), channel_id=1, source_target_pairs={{0,8},{1,9},{2,10},{3,11},{4,12},{5,13},{6,14},{7,15},{8,0},{9,1},... | collective-permute-start | bytes 393224 | tf_op jit(solution)/shard_map/ppermute | solution.py:573
  15.8 15.1 %collective-permute-start.6 = (bf16[512,128]{1,0:T(8,128)(2,1)S(1)}, bf16[512,128]{1,0:T(8,128)(2,1)S(1)}, u32[]{:S(2)}, u32[]{:S(2)}) collective-permute-start(bf16[512,128]{1,0:T(8,128)(2,1)S(1)} %collective-permute-done.refs_1_), channel_id=1, source_target_pairs={{0,2},{1,3},{2,0},{3,1},{4,6},{5,7},{6,4},{7,5},{8,10},{9,11},{10,... | collective-permute-start | bytes 393224 | tf_op jit(solution)/shard_map/ppermute | solution.py:573
  23.8 8.2 %collective-permute-start.7 = (bf16[512,128]{1,0:T(8,128)(2,1)S(1)}, bf16[512,128]{1,0:T(8,128)(2,1)S(1)}, u32[]{:S(2)}, u32[]{:S(2)}) collective-permute-start(bf16[512,128]{1,0:T(8,128)(2,1)S(1)} %collective-permute-done.1.refs_0_), channel_id=1, source_target_pairs={{0,8},{1,9},{2,10},{3,11},{4,12},{5,13},{6,14},{7,15},{8,0},{9,1},... | collective-permute-start | bytes 393224 | tf_op jit(solution)/shard_map/ppermute | solution.py:573
  23.8 8.1 %collective-permute-start.8 = (bf16[512,128]{1,0:T(8,128)(2,1)S(1)}, bf16[512,128]{1,0:T(8,128)(2,1)S(1)}, u32[]{:S(2)}, u32[]{:S(2)}) collective-permute-start(bf16[512,128]{1,0:T(8,128)(2,1)S(1)} %collective-permute-done.refs_1_), channel_id=1, source_target_pairs={{0,8},{1,9},{2,10},{3,11},{4,12},{5,13},{6,14},{7,15},{8,0},{9,1},... | collective-permute-start | bytes 393224 | tf_op jit(solution)/shard_map/ppermute | solution.py:573
  30.9 1.4 collective-permute-start.9
  43.4 4.7 %collective-permute-start.12 = (f32[3072]{0:T(1024)S(1)}, f32[3072]{0:T(1024)S(1)}, u32[]{:S(2)}, u32[]{:S(2)}) collective-permute-start(f32[3072]{0:T(1024)S(1)} %bitcast.71), channel_id=1, source_target_pairs={{0,17},{1,16},{2,19},{3,18},{4,21},{5,20},{6,23},{7,22},{8,25},{9,... | collective-permute-start | bytes 36872 | tf_op jit(solution)/shard_map/ppermute | solution.py:573
  43.4 4.6 %collective-permute-start.11 = (f32[3072]{0:T(1024)S(1)}, f32[3072]{0:T(1024)S(1)}, u32[]{:S(2)}, u32[]{:S(2)}) collective-permute-start(f32[3072]{0:T(1024)S(1)} %bitcast.72), channel_id=1, source_target_pairs={{0,16},{1,17},{2,18},{3,19},{4,20},{5,21},{6,22},{7,23},{8,24},{9,... | collective-permute-start | bytes 36872 | tf_op jit(solution)/shard_map/ppermute | solution.py:573
  43.5 5.1 %collective-permute-start.10 = (f32[3072]{0:T(1024)S(1)}, f32[3072]{0:T(1024)S(1)}, u32[]{:S(2)}, u32[]{:S(2)}) collective-permute-start(f32[3072]{0:T(1024)S(1)} %bitcast.73), channel_id=1, source_target_pairs={{0,1},{1,0},{2,3},{3,2},{4,5},{5,4},{6,7},{7,6},{8,9},{9,8},{10,11... | collective-permute-start | bytes 36872 | tf_op jit(solution)/shard_map/ppermute | solution.py:573
  79.7 1.3 collective-permute-start.13
  81.0 5.6 %collective-permute-start.16 = (f32[5120]{0:T(1024)S(1)}, f32[5120]{0:T(1024)S(1)}, u32[]{:S(2)}, u32[]{:S(2)}) collective-permute-start(f32[5120]{0:T(1024)S(1)} %bitcast.33), channel_id=1, source_target_pairs={{0,6},{1,7},{2,4},{3,5},{4,2},{5,3},{6,0},{7,1},{8,14},{9,15},{10,... | collective-permute-start | bytes 61448 | tf_op jit(solution)/shard_map/ppermute | solution.py:573
  81.1 5.6 %collective-permute-start.15 = (f32[5120]{0:T(1024)S(1)}, f32[5120]{0:T(1024)S(1)}, u32[]{:S(2)}, u32[]{:S(2)}) collective-permute-start(f32[5120]{0:T(1024)S(1)} %bitcast.34), channel_id=1, source_target_pairs={{0,4},{1,5},{2,6},{3,7},{4,0},{5,1},{6,2},{7,3},{8,12},{9,13},{10,... | collective-permute-start | bytes 61448 | tf_op jit(solution)/shard_map/ppermute | solution.py:573
  82.5 4.7 %collective-permute-start.14 = (f32[5120]{0:T(1024)S(1)}, f32[5120]{0:T(1024)S(1)}, u32[]{:S(2)}, u32[]{:S(2)}) collective-permute-start(f32[5120]{0:T(1024)S(1)} %bitcast.35), channel_id=1, source_target_pairs={{0,2},{1,3},{2,0},{3,1},{4,6},{5,7},{6,4},{7,5},{8,10},{9,11},{10,... | collective-permute-start | bytes 61448 | tf_op jit(solution)/shard_map/ppermute | solution.py:573
  91.7 4.6 %collective-permute-start.19 = (f32[2048]{0:T(1024)S(1)}, f32[2048]{0:T(1024)S(1)}, u32[]{:S(2)}, u32[]{:S(2)}) collective-permute-start(f32[2048]{0:T(1024)S(1)} %bitcast.57), channel_id=1, source_target_pairs={{0,17},{1,16},{2,19},{3,18},{4,21},{5,20},{6,23},{7,22},{8,25},{9,... | collective-permute-start | bytes 24584 | tf_op jit(solution)/shard_map/ppermute | solution.py:573
  93.2 3.7 %collective-permute-start.18 = (f32[2048]{0:T(1024)S(1)}, f32[2048]{0:T(1024)S(1)}, u32[]{:S(2)}, u32[]{:S(2)}) collective-permute-start(f32[2048]{0:T(1024)S(1)} %bitcast.58), channel_id=1, source_target_pairs={{0,16},{1,17},{2,18},{3,19},{4,20},{5,21},{6,22},{7,23},{8,24},{9,... | collective-permute-start | bytes 24584 | tf_op jit(solution)/shard_map/ppermute | solution.py:573
  95.2 3.7 %collective-permute-start.17 = (f32[2048]{0:T(1024)S(1)}, f32[2048]{0:T(1024)S(1)}, u32[]{:S(2)}, u32[]{:S(2)}) collective-permute-start(f32[2048]{0:T(1024)S(1)} %bitcast.59), channel_id=1, source_target_pairs={{0,1},{1,0},{2,3},{3,2},{4,5},{5,4},{6,7},{7,6},{8,9},{9,8},{10,11... | collective-permute-start | bytes 24584 | tf_op jit(solution)/shard_map/ppermute | solution.py:573
  101.6 1.2 collective-permute-start.20
  102.8 5.6 %collective-permute-start.23 = (f32[4096]{0:T(1024)S(1)}, f32[4096]{0:T(1024)S(1)}, u32[]{:S(2)}, u32[]{:S(2)}) collective-permute-start(f32[4096]{0:T(1024)S(1)} %bitcast.36), channel_id=1, source_target_pairs={{0,6},{1,7},{2,4},{3,5},{4,2},{5,3},{6,0},{7,1},{8,14},{9,15},{10,... | collective-permute-start | bytes 49160 | tf_op jit(solution)/shard_map/ppermute | solution.py:573
  105.3 4.6 %collective-permute-start.22 = (f32[4096]{0:T(1024)S(1)}, f32[4096]{0:T(1024)S(1)}, u32[]{:S(2)}, u32[]{:S(2)}) collective-permute-start(f32[4096]{0:T(1024)S(1)} %bitcast.37), channel_id=1, source_target_pairs={{0,4},{1,5},{2,6},{3,7},{4,0},{5,1},{6,2},{7,3},{8,12},{9,13},{10,... | collective-permute-start | bytes 49160 | tf_op jit(solution)/shard_map/ppermute | solution.py:573
  106.4 3.7 %collective-permute-start.21 = (f32[4096]{0:T(1024)S(1)}, f32[4096]{0:T(1024)S(1)}, u32[]{:S(2)}, u32[]{:S(2)}) collective-permute-start(f32[4096]{0:T(1024)S(1)} %bitcast.38), channel_id=1, source_target_pairs={{0,2},{1,3},{2,0},{3,1},{4,6},{5,7},{6,4},{7,5},{8,10},{9,11},{10,... | collective-permute-start | bytes 49160 | tf_op jit(solution)/shard_map/ppermute | solution.py:573
  114.6 4.6 %collective-permute-start.26 = (f32[2048]{0:T(1024)S(1)}, f32[2048]{0:T(1024)S(1)}, u32[]{:S(2)}, u32[]{:S(2)}) collective-permute-start(f32[2048]{0:T(1024)S(1)} %bitcast.39), channel_id=1, source_target_pairs={{0,17},{1,16},{2,19},{3,18},{4,21},{5,20},{6,23},{7,22},{8,25},{9,... | collective-permute-start | bytes 24584 | tf_op jit(solution)/shard_map/ppermute | solution.py:573
  114.7 4.5 %collective-permute-start.25 = (f32[2048]{0:T(1024)S(1)}, f32[2048]{0:T(1024)S(1)}, u32[]{:S(2)}, u32[]{:S(2)}) collective-permute-start(f32[2048]{0:T(1024)S(1)} %bitcast.40), channel_id=1, source_target_pairs={{0,16},{1,17},{2,18},{3,19},{4,20},{5,21},{6,22},{7,23},{8,24},{9,... | collective-permute-start | bytes 24584 | tf_op jit(solution)/shard_map/ppermute | solution.py:573
  116.1 3.7 %collective-permute-start.24 = (f32[2048]{0:T(1024)S(1)}, f32[2048]{0:T(1024)S(1)}, u32[]{:S(2)}, u32[]{:S(2)}) collective-permute-start(f32[2048]{0:T(1024)S(1)} %bitcast.41), channel_id=1, source_target_pairs={{0,1},{1,0},{2,3},{3,2},{4,5},{5,4},{6,7},{7,6},{8,9},{9,8},{10,11... | collective-permute-start | bytes 24584 | tf_op jit(solution)/shard_map/ppermute | solution.py:573
  122.1 1.2 collective-permute-start.27
  123.4 10.3 %collective-permute-start.30 = (f32[4096]{0:T(1024)S(1)}, f32[4096]{0:T(1024)S(1)}, u32[]{:S(2)}, u32[]{:S(2)}) collective-permute-start(f32[4096]{0:T(1024)S(1)} %bitcast.47), channel_id=1, source_target_pairs={{0,6},{1,7},{2,4},{3,5},{4,2},{5,3},{6,0},{7,1},{8,14},{9,15},{10,... | collective-permute-start | bytes 49160 | tf_op jit(solution)/shard_map/ppermute | solution.py:573
  124.8 8.8 %collective-permute-start.29 = (f32[4096]{0:T(1024)S(1)}, f32[4096]{0:T(1024)S(1)}, u32[]{:S(2)}, u32[]{:S(2)}) collective-permute-start(f32[4096]{0:T(1024)S(1)} %bitcast.48), channel_id=1, source_target_pairs={{0,4},{1,5},{2,6},{3,7},{4,0},{5,1},{6,2},{7,3},{8,12},{9,13},{10,... | collective-permute-start | bytes 49160 | tf_op jit(solution)/shard_map/ppermute | solution.py:573
  125.8 7.9 %collective-permute-start.28 = (f32[4096]{0:T(1024)S(1)}, f32[4096]{0:T(1024)S(1)}, u32[]{:S(2)}, u32[]{:S(2)}) collective-permute-start(f32[4096]{0:T(1024)S(1)} %bitcast.49), channel_id=1, source_target_pairs={{0,2},{1,3},{2,0},{3,1},{4,6},{5,7},{6,4},{7,5},{8,10},{9,11},{10,... | collective-permute-start | bytes 49160 | tf_op jit(solution)/shard_map/ppermute | solution.py:573
  133.6 3.8 %collective-permute-start.31 = (bf16[2048,128]{1,0:T(8,128)(2,1)S(1)}, bf16[2048,128]{1,0:T(8,128)(2,1)S(1)}, u32[]{:S(2)}, u32[]{:S(2)}) collective-permute-start(bf16[2048,128]{1,0:T(8,128)(2,1)S(1)} %get-tuple-element.80), channel_id=1, source_target_pairs={{0,8},{1,9},{2,10},{3,11},{4,12},{5,13},{6,14},{7,15},{8,0},{9,1},... | collective-permute-start | bytes 1572872 | tf_op jit(solution)/shard_map/ppermute | solution.py:573
  135.8 8.7 %collective-permute-start.33 = (bf16[512,128]{1,0:T(8,128)(2,1)S(1)}, bf16[512,128]{1,0:T(8,128)(2,1)S(1)}, u32[]{:S(2)}, u32[]{:S(2)}) collective-permute-start(bf16[512,128]{1,0:T(8,128)(2,1)S(1)} %get-tuple-element.90), channel_id=1, source_target_pairs={{0,17},{1,16},{2,19},{3,18},{4,21},{5,20},{6,23},{7,22},{8,25},{9,... | collective-permute-start | bytes 393224 | tf_op jit(solution)/shard_map/ppermute | solution.py:573
  137.4 7.8 %collective-permute-start.32 = (bf16[512,128]{1,0:T(8,128)(2,1)S(1)}, bf16[512,128]{1,0:T(8,128)(2,1)S(1)}, u32[]{:S(2)}, u32[]{:S(2)}) collective-permute-start(bf16[512,128]{1,0:T(8,128)(2,1)S(1)} %get-tuple-element.89), channel_id=1, source_target_pairs={{0,2},{1,3},{2,0},{3,1},{4,6},{5,7},{6,4},{7,5},{8,10},{9,11},{10,... | collective-permute-start | bytes 393224 | tf_op jit(solution)/shard_map/ppermute | solution.py:573
  137.5 13.0 %collective-permute-start.36 = (bf16[512,128]{1,0:T(8,128)(2,1)S(1)}, bf16[512,128]{1,0:T(8,128)(2,1)S(1)}, u32[]{:S(2)}, u32[]{:S(2)}) collective-permute-start(bf16[512,128]{1,0:T(8,128)(2,1)S(1)} %get-tuple-element.96), channel_id=1, source_target_pairs={{0,4},{1,5},{2,6},{3,7},{4,0},{5,1},{6,2},{7,3},{8,12},{9,13},{10,... | collective-permute-start | bytes 393224 | tf_op jit(solution)/shard_map/ppermute | solution.py:573
  139.5 11.0 %collective-permute-start.37 = (bf16[512,128]{1,0:T(8,128)(2,1)S(1)}, bf16[512,128]{1,0:T(8,128)(2,1)S(1)}, u32[]{:S(2)}, u32[]{:S(2)}) collective-permute-start(bf16[512,128]{1,0:T(8,128)(2,1)S(1)} %get-tuple-element.97), channel_id=1, source_target_pairs={{0,6},{1,7},{2,4},{3,5},{4,2},{5,3},{6,0},{7,1},{8,14},{9,15},{10,... | collective-permute-start | bytes 393224 | tf_op jit(solution)/shard_map/ppermute | solution.py:573
  145.2 5.2 %collective-permute-start.34 = (bf16[512,128]{1,0:T(8,128)(2,1)S(1)}, bf16[512,128]{1,0:T(8,128)(2,1)S(1)}, u32[]{:S(2)}, u32[]{:S(2)}) collective-permute-start(bf16[512,128]{1,0:T(8,128)(2,1)S(1)} %get-tuple-element.91), channel_id=1, source_target_pairs={{0,1},{1,0},{2,3},{3,2},{4,5},{5,4},{6,7},{7,6},{8,9},{9,8},{10,11... | collective-permute-start | bytes 393224 | tf_op jit(solution)/shard_map/ppermute | solution.py:573
  146.2 5.0 %collective-permute-start.35 = (bf16[512,128]{1,0:T(8,128)(2,1)S(1)}, bf16[512,128]{1,0:T(8,128)(2,1)S(1)}, u32[]{:S(2)}, u32[]{:S(2)}) collective-permute-start(bf16[512,128]{1,0:T(8,128)(2,1)S(1)} %get-tuple-element.92), channel_id=1, source_target_pairs={{0,16},{1,17},{2,18},{3,19},{4,20},{5,21},{6,22},{7,23},{8,24},{9,... | collective-permute-start | bytes 393224 | tf_op jit(solution)/shard_map/ppermute | solution.py:573

commit v11 on v10

--- a/solution.py
+++ b/solution.py
@@ -314,7 +314,7 @@
     )(own, *xs, y_other)
 
 
-def row_lse_middle(x, ys, first, width=512):
+def row_lse_middle(x, ys, first, width=1024):
     rows, share = x.shape[0], ys[0].shape[0]
     depth = len(ys) * share
     return pl.pallas_call(
@@ -333,7 +333,7 @@
     )(x, first, *ys)
 
 
-def row_lse_late(own, x, ys, first, mass, tail, width=256):
+def row_lse_late(own, x, ys, first, mass, tail, width=1024):
     rows, share = x.shape[0], ys[0].shape[0]
     depth = (len(ys) + 1) * share
     return pl.pallas_call(
@@ -348,7 +348,7 @@
     )(own, mass.reshape(1, -1), x, first, *ys)
 
 
-def column_lse(x, y, mass, tail, got, width=1024, chunk=256):
+def column_lse(x, y, mass, tail, got, width=1024, chunk=512):
     rows, cols = x.shape[0], y.shape[0]
     return pl.pallas_call(
         functools.partial(column_lse_kernel, width, chunk, len(got)),
@@ -585,22 +585,22 @@
         return [swap(value, mask) for mask in masks], range(len(masks))
 
     xs, _ = direct(imu, across)
-    near, far = [camera[0]], [swap(camera[0], core)]
-    for z in range(1, nz):
-        part = near[z & (z - 1)]
-        if z & (z - 1):
-            part, near[z & -z], xs = lax.optimization_barrier((part, near[z & -z], xs))
-        near.append(swap(part, along[z & -z]))
+    own, mine = lax.optimization_barrier((jnp.concatenate([imu, camera[0]]), camera[0]))
+    far = [swap(mine, core)]
+    near = [mine if z == 0 else None if z & (z - 1) else swap(mine, along[z]) for z in range(nz)]
 
     def pair(mass, place, share):
         return [lax.dynamic_slice_in_dim(mass, (place ^ k) * share, share, 0) for k in range(2)]
 
-    own = jnp.concatenate([imu, camera[0]])
     row, col = lax.axis_index("row"), lax.axis_index("col")
     mass = jnp.concatenate(pair(imu_mass, col, share_x) + pair(cam_mass, row, share_y))
 
     x, xt, first = row_lse_early(own, xs[1:], far[0])
-    first, *middle = lax.optimization_barrier((first, *near[1:-1]))
+    first, near, mass = lax.optimization_barrier((first, near, mass))
+    for z in range(1, nz):
+        if z & (z - 1):
+            near[z] = swap(near[z & (z - 1)], along[z & -z])
+    middle = near[1:-1]
     far += [swap(part, core) for part in middle]
     first = row_lse_middle(x, middle, first)
     first, last = lax.optimization_barrier((first, near[-1]))

time: 152 us -> 148 us (0.974)
  waiting for transfers between devices: 24.7 us -> 20.6 us
    ppermute x38, waiting for transfers between devices: 24.7 us -> 20.6 us  [swap(): lax.ppermute(value, ('row', 'col'), [(i, i ^ mask) for i in range(self.co...]
  transfers between devices with their start and end apart: 38 -> 38, of which waited for: 21 -> 20; matrix products, arithmetic and copies ran while one was open for 1% -> 1% of each run, Pallas kernels for 16% -> 17%
where the time goes in v11:
time: 148 us
  Pallas kernels  81.9 us (55%)
  starting transfers between devices  42.7 us (29%)
  waiting for transfers between devices  20.6 us (14%)
    ppermute x38, starting transfers between devices, swap(): lax.ppermute(value, ('row', 'col'), [(i, i ^ mask) for i in range(self.co...  42.7 us
    pallas_call x1, Pallas kernels, column_lse(): pl.pallas_call(functools.partial(column_lse_kernel, width, chunk, len(got...  31.5 us
    ppermute x38, waiting for transfers between devices, swap(): lax.ppermute(value, ('row', 'col'), [(i, i ^ mask) for i in range(self.co...  20.6 us
    pallas_call x4, Pallas kernels, weighted(): pl.pallas_call(functools.partial(kernel, width, tuple(shifts), parts), ou...  14 us
    pallas_call x1, Pallas kernels, row_lse_late(): pl.pallas_call(functools.partial(row_lse_late_kernel, width, len(ys)), ou...  10.2 us
    pallas_call x1, Pallas kernels, row_lse_middle(): pl.pallas_call(functools.partial(row_lse_middle_kernel, width, len(ys)),...  6.53 us
    pallas_call x1, Pallas kernels, row_lse_early(): pl.pallas_call(functools.partial(row_lse_early_kernel, width, len(xs)), o...  6.49 us
    pallas_call x1, Pallas kernels, column_grad(): pl.pallas_call(functools.partial(column_grad_kernel, width), out_shape=(s...  5.76 us
  transfers between devices with their start and end apart: 38, of which 20 were waited for; matrix products, arithmetic and copies ran while one was open for 1% of the time, Pallas kernels for 17%

profile of v11, /device:TPU:0, one launch (start us, length us, event | category | flops | bytes accessed | tf_op | source)
XLA Modules:
  0.0 147.9 jit_solution(17752676510637681305)
XLA Ops:
  0.6 3.0 %collective-permute-start = (bf16[512,128]{1,0:T(8,128)(2,1)}, bf16[512,128]{1,0:T(8,128)(2,1)S(1)}, u32[]{:S(2)}, u32[]{:S(2)}) collective-permute-start(bf16[512,128]{1,0:T(8,128)(2,1)} %param.4), channel_id=1, source_target_pairs={{0,1},{1,0},{2,3},{3,2},{4,5},{5,4},{6,7},{7,6},{8,9},{9,8},{10,11... | collective-permute-start | bytes 393224 | tf_op jit(solution)/shard_map/ppermute | solution.py:573
  3.7 1.4 collective-permute-start.2
  5.2 1.0 pad_maximum_fusion.own_ref
  6.2 3.1 %collective-permute-start.5 = (bf16[512,128]{1,0:T(8,128)(2,1)}, bf16[512,128]{1,0:T(8,128)(2,1)S(1)}, u32[]{:S(2)}, u32[]{:S(2)}) collective-permute-start(bf16[512,128]{1,0:T(8,128)(2,1)} %bitcast.78), channel_id=1, source_target_pairs={{0,4},{1,5},{2,6},{3,7},{4,0},{5,1},{6,2},{7,3},{8,12},{9,13},{10,... | collective-permute-start | bytes 393224 | tf_op jit(solution)/shard_map/ppermute | solution.py:573
  9.3 0.8 fusion
  10.1 1.6 %collective-permute-start.4 = (bf16[512,128]{1,0:T(8,128)(2,1)}, bf16[512,128]{1,0:T(8,128)(2,1)S(1)}, u32[]{:S(2)}, u32[]{:S(2)}) collective-permute-start(bf16[512,128]{1,0:T(8,128)(2,1)} %bitcast.80), channel_id=1, source_target_pairs={{0,2},{1,3},{2,0},{3,1},{4,6},{5,7},{6,4},{7,5},{8,10},{9,11},{10,... | collective-permute-start | bytes 393224 | tf_op jit(solution)/shard_map/ppermute | solution.py:573
  11.8 6.5 %row_lse_early.1 = (bf16[2048,128]{1,0:T(8,128)(2,1)S(1)}, bf16[128,2048]{1,0:T(8,128)(2,1)S(1)}, f32[1,2048]{1,0:T(1,128)S(1)}) custom-call(bf16[1024,128]{1,0:T(8,128)(2,1)S(1)} %pad_maximum_fusion.own_ref, bf16[512,128]{1,0:T(8,128)(2,1)S(1)} %collective-permute-done.refs_0_, bf16[512,128]{1,0:T(8,128)(2,1)S(1)} %collective-permute-done.1.refs_1_, ...), custom_call_target="tpu_custom_call" | custom-call | flops 536870912 | bytes 786432 | tf_op jit(solution)/shard_map/row_lse_early/pallas_call | solution.py:305
  18.9 6.5 %row_lse_middle.1.first_ref = f32[1,2048]{1,0:T(1,128)S(1)} custom-call(bf16[2048,128]{1,0:T(8,128)(2,1)S(1)} %get-tuple-element.51.x_ref, f32[1,2048]{1,0:T(1,128)S(1)} %get-tuple-element.54.first_ref, bf16[512,128]{1,0:T(8,128)(2,1)S(1)} %collective-permute-done.4.refs_0_, bf16[512,128]{1,0:T(8,128)(2,1)S(1)} %collective-permute-done.5.refs_1_), custom_call_target="tpu_custom_call" | custom-call | flops 536870912 | bytes 786432 | tf_op jit(solution)/shard_map/row_lse_middle/pallas_call | solution.py:320
  25.6 1.3 collective-permute-done.9.refs_6_
  26.9 10.2 %row_lse_late.1 = (bf16[4096,128]{1,0:T(8,128)(2,1)S(1)}, f32[1,3072]{1,0:T(1,128)S(1)}) custom-call(bf16[1024,128]{1,0:T(8,128)(2,1)S(1)} %pad_maximum_fusion.own_ref, f32[1,2048]{1,0:T(1,128)S(1)} %bitcast.66, bf16[2048,128]{1,0:T(8,128)(2,1)S(1)} %get-tuple-element.51.x_ref, f32[1,2048]{1,0:T(1,128)S(1)} %row_lse_middle.1.first_ref, ...), custom_call_target="tpu_custom_call" | custom-call | flops 1073741824 | bytes 1048576 | tf_op jit(solution)/shard_map/row_lse_late/pallas_call | solution.py:339
  37.2 3.4 %collective-permute-start.10 = (f32[3072]{0:T(1024)S(1)}, f32[3072]{0:T(1024)S(1)}, u32[]{:S(2)}, u32[]{:S(2)}) collective-permute-start(f32[3072]{0:T(1024)S(1)} %bitcast.73), channel_id=1, source_target_pairs={{0,1},{1,0},{2,3},{3,2},{4,5},{5,4},{6,7},{7,6},{8,9},{9,8},{10,11... | collective-permute-start | bytes 36872 | tf_op jit(solution)/shard_map/ppermute | solution.py:573
  40.6 1.1 collective-permute-done.12
  42.3 31.5 %column_lse.1 = (f32[1,5120]{1,0:T(1,128)S(1)}, bf16[2048,4096]{1,0:T(8,128)(2,1)S(1)}, f32[1,4096]{1,0:T(1,128)S(1)}, f32[1,2048]{1,0:T(1,128)S(1)}) custom-call(bf16[2048,128]{1,0:T(8,128)(2,1)S(1)} %get-tuple-element.51.x_ref, bf16[4096,128]{1,0:T(8,128)(2,1)S(1)} %get-tuple-element.59.y_ref, f32[1,2048]{1,0:T(1,128)S(1)} %bitcast.67, ...), custom_call_target="tpu_custom_call" | custom-call | flops 2147483648 | bytes 1572864 | tf_op jit(solution)/shard_map/column_lse/pallas_call | solution.py:353
  73.9 1.2 collective-permute-done.13
  75.1 2.9 %collective-permute-start.16 = (f32[5120]{0:T(1024)S(1)}, f32[5120]{0:T(1024)S(1)}, u32[]{:S(2)}, u32[]{:S(2)}) collective-permute-start(f32[5120]{0:T(1024)S(1)} %bitcast.33), channel_id=1, source_target_pairs={{0,6},{1,7},{2,4},{3,5},{4,2},{5,3},{6,0},{7,1},{8,14},{9,15},{10,... | collective-permute-start | bytes 61448 | tf_op jit(solution)/shard_map/ppermute | solution.py:573
  78.0 1.6 %collective-permute-start.15 = (f32[5120]{0:T(1024)S(1)}, f32[5120]{0:T(1024)S(1)}, u32[]{:S(2)}, u32[]{:S(2)}) collective-permute-start(f32[5120]{0:T(1024)S(1)} %bitcast.34), channel_id=1, source_target_pairs={{0,4},{1,5},{2,6},{3,7},{4,0},{5,1},{6,2},{7,3},{8,12},{9,13},{10,... | collective-permute-start | bytes 61448 | tf_op jit(solution)/shard_map/ppermute | solution.py:573
  80.8 1.9 %collective-permute-done.15 = f32[5120]{0:T(1024)S(1)} collective-permute-done((f32[5120]{0:T(1024)S(1)}, f32[5120]{0:T(1024)S(1)}, u32[]{:S(2)}, u32[]{:S(2)}) %collective-permute-start.15) | collective-permute-done | bytes 20512 | tf_op jit(solution)/shard_map/ppermute | solution.py:573
  82.7 0.7 collective-permute-done.14
  83.4 4.5 %weighted_sum.4 = (f32[1,2048]{1,0:T(1,128)S(1)}, f32[1,4096]{1,0:T(1,128)S(1)}, f32[1,4096]{1,0:T(1,128)S(1)}) custom-call(bf16[2048,4096]{1,0:T(8,128)(2,1)S(1)} %get-tuple-element.61.e_ref, f32[1,4096]{1,0:T(1,128)S(1)} %get-tuple-element.63.shift_ref, f32[1,5120]{1,0:T(1,128)S(1)} %pair.3.refs_0_, f32[1,5120]{1,0:T(1,128)S(1)} %bitcast.44, ...), custom_call_target="tpu_custom_call" | custom-call | flops 16777216 | bytes 16777216 | tf_op jit(solution)/shard_map/weighted_sum/pallas_call | solution.py:274
  87.9 1.0 collective-permute-start.19
  89.6 1.9 %collective-permute-start.17 = (f32[2048]{0:T(1024)S(1)}, f32[2048]{0:T(1024)S(1)}, u32[]{:S(2)}, u32[]{:S(2)}) collective-permute-start(f32[2048]{0:T(1024)S(1)} %bitcast.59), channel_id=1, source_target_pairs={{0,1},{1,0},{2,3},{3,2},{4,5},{5,4},{6,7},{7,6},{8,9},{9,8},{10,11... | collective-permute-start | bytes 24584 | tf_op jit(solution)/shard_map/ppermute | solution.py:573
  91.4 1.1 collective-permute-done.19
  93.2 2.8 %weighted_sum.5 = (f32[1,4096]{1,0:T(1,128)S(1)}, f32[1,2048]{1,0:T(1,128)}) custom-call(bf16[2048,4096]{1,0:T(8,128)(2,1)S(1)} %get-tuple-element.61.e_ref, f32[1,2048]{1,0:T(1,128)S(1)} %get-tuple-element.62.a_ref, f32[1,4096]{1,0:T(1,128)S(1)} %get-tuple-element.65.first_ref, f32[1,2048]{1,0:T(1,128)S(1)} %get-tuple-element.67.refs_0_, ...), custom_call_target="tpu_custom_call" | custom-call | flops 16777216 | bytes 16777216 | tf_op jit(solution)/shard_map/weighted_sum/pallas_call | solution.py:274
  96.0 1.2 collective-permute-done.20
  97.2 2.7 %collective-permute-start.23 = (f32[4096]{0:T(1024)S(1)}, f32[4096]{0:T(1024)S(1)}, u32[]{:S(2)}, u32[]{:S(2)}) collective-permute-start(f32[4096]{0:T(1024)S(1)} %bitcast.36), channel_id=1, source_target_pairs={{0,6},{1,7},{2,4},{3,5},{4,2},{5,3},{6,0},{7,1},{8,14},{9,15},{10,... | collective-permute-start | bytes 49160 | tf_op jit(solution)/shard_map/ppermute | solution.py:573
  100.5 1.1 collective-permute-start.21
  101.7 1.2 collective-permute-done.23
  102.8 1.8 %collective-permute-done.22 = f32[4096]{0:T(1024)S(1)} collective-permute-done((f32[4096]{0:T(1024)S(1)}, f32[4096]{0:T(1024)S(1)}, u32[]{:S(2)}, u32[]{:S(2)}) %collective-permute-start.22) | collective-permute-done | bytes 16416 | tf_op jit(solution)/shard_map/ppermute | solution.py:573
  104.6 4.4 %weighted_sum.6.refs_0_ = f32[1,2048]{1,0:T(1,128)S(1)} custom-call(bf16[2048,4096]{1,0:T(8,128)(2,1)S(1)} %get-tuple-element.61.e_ref, f32[1,4096]{1,0:T(1,128)S(1)} %get-tuple-element.65.first_ref, f32[1,4096]{1,0:T(1,128)S(1)} %get-tuple-element.66.b_ref, f32[1,4096]{1,0:T(1,128)S(1)} %pair.4.refs_0_, f32[1,4096]{1,0:T(1,128)S(1)} %bitcast.56, ...), custom_call_target="tpu_custom_call" | custom-call | flops 16777216 | bytes 16777216 | tf_op jit(solution)/shard_map/weighted_sum/pallas_call | solution.py:274
  109.0 1.6 %collective-permute-start.26 = (f32[2048]{0:T(1024)S(1)}, f32[2048]{0:T(1024)S(1)}, u32[]{:S(2)}, u32[]{:S(2)}) collective-permute-start(f32[2048]{0:T(1024)S(1)} %bitcast.39), channel_id=1, source_target_pairs={{0,17},{1,16},{2,19},{3,18},{4,21},{5,20},{6,23},{7,22},{8,25},{9,... | collective-permute-start | bytes 24584 | tf_op jit(solution)/shard_map/ppermute | solution.py:573
  110.7 1.9 %collective-permute-start.25 = (f32[2048]{0:T(1024)S(1)}, f32[2048]{0:T(1024)S(1)}, u32[]{:S(2)}, u32[]{:S(2)}) collective-permute-start(f32[2048]{0:T(1024)S(1)} %bitcast.40), channel_id=1, source_target_pairs={{0,16},{1,17},{2,18},{3,19},{4,20},{5,21},{6,22},{7,23},{8,24},{9,... | collective-permute-start | bytes 24584 | tf_op jit(solution)/shard_map/ppermute | solution.py:573
  112.6 1.1 collective-permute-done.26
  114.3 1.9 %collective-permute-done.24 = f32[2048]{0:T(1024)S(1)} collective-permute-done((f32[2048]{0:T(1024)S(1)}, f32[2048]{0:T(1024)S(1)}, u32[]{:S(2)}, u32[]{:S(2)}) %collective-permute-start.24) | collective-permute-done | bytes 8224 | tf_op jit(solution)/shard_map/ppermute | solution.py:573
  116.2 2.3 %weighted_sum.7 = (f32[1,4096]{1,0:T(1,128)S(1)}, f32[1,2048]{1,0:T(1,128)S(1)}) custom-call(bf16[2048,4096]{1,0:T(8,128)(2,1)S(1)} %get-tuple-element.61.e_ref, f32[1,2048]{1,0:T(1,128)S(1)} %get-tuple-element.62.a_ref, f32[1,4096]{1,0:T(1,128)S(1)} %get-tuple-element.65.first_ref, f32[1,2048]{1,0:T(1,128)S(1)} %weighted_sum.6.refs_0_, ...), custom_call_target="tpu_custom_call" | custom-call | flops 16777216 | bytes 16777216 | tf_op jit(solution)/shard_map/weighted_sum/pallas_call | solution.py:274
  118.7 1.2 collective-permute-done.27
  119.8 1.5 %collective-permute-start.30 = (f32[4096]{0:T(1024)S(1)}, f32[4096]{0:T(1024)S(1)}, u32[]{:S(2)}, u32[]{:S(2)}) collective-permute-start(f32[4096]{0:T(1024)S(1)} %bitcast.47), channel_id=1, source_target_pairs={{0,6},{1,7},{2,4},{3,5},{4,2},{5,3},{6,0},{7,1},{8,14},{9,15},{10,... | collective-permute-start | bytes 49160 | tf_op jit(solution)/shard_map/ppermute | solution.py:573
  122.0 2.3 %collective-permute-start.28 = (f32[4096]{0:T(1024)S(1)}, f32[4096]{0:T(1024)S(1)}, u32[]{:S(2)}, u32[]{:S(2)}) collective-permute-start(f32[4096]{0:T(1024)S(1)} %bitcast.49), channel_id=1, source_target_pairs={{0,2},{1,3},{2,0},{3,1},{4,6},{5,7},{6,4},{7,5},{8,10},{9,11},{10,... | collective-permute-start | bytes 49160 | tf_op jit(solution)/shard_map/ppermute | solution.py:573
  124.3 5.8 %column_grad.1 = (f32[2048,128]{1,0:T(8,128)S(1)}, bf16[2048,128]{1,0:T(8,128)(2,1)S(1)}) custom-call(bf16[128,2048]{1,0:T(8,128)(2,1)S(1)} %get-tuple-element.74.xt_ref, bf16[4096,128]{1,0:T(8,128)(2,1)S(1)} %get-tuple-element.59.y_ref, bf16[2048,4096]{1,0:T(8,128)(2,1)S(1)} %get-tuple-element.61.e_ref, f32[1,2048]{1,0:T(1,128)S(1)} %get-tuple-element.71.alpha_ref, ...), custom_call_target="tpu_custom_call" | custom-call | flops 4294967296 | bytes 16777216 | tf_op jit(solution)/shard_map/column_grad/pallas_call | solution.py:415
  130.2 2.1 %first_rows.1 = (bf16[4096,256]{1,0:T(8,128)(2,1)S(1)}, f32[1,512]{1,0:T(1,128)S(1)}, bf16[512,128]{1,0:T(8,128)(2,1)S(1)}) custom-call(bf16[2048,128]{1,0:T(8,128)(2,1)S(1)} %get-tuple-element.51.x_ref, bf16[4096,128]{1,0:T(8,128)(2,1)S(1)} %get-tuple-element.59.y_ref, bf16[2048,4096]{1,0:T(8,128)(2,1)S(1)} %get-tuple-element.61.e_ref, ...), custom_call_target="tpu_custom_call" | custom-call | flops 34359738368 | bytes 134217728 | tf_op jit(solution)/shard_map/first_rows/pallas_call | solution.py:490
  133.2 2.0 %collective-permute-start.36 = (bf16[512,128]{1,0:T(8,128)(2,1)S(1)}, bf16[512,128]{1,0:T(8,128)(2,1)S(1)}, u32[]{:S(2)}, u32[]{:S(2)}) collective-permute-start(bf16[512,128]{1,0:T(8,128)(2,1)S(1)} %get-tuple-element.92), channel_id=1, source_target_pairs={{0,4},{1,5},{2,6},{3,7},{4,0},{5,1},{6,2},{7,3},{8,12},{9,13},{10,... | collective-permute-start | bytes 393224 | tf_op jit(solution)/shard_map/ppermute | solution.py:573
  135.2 1.8 %collective-permute-start.37 = (bf16[512,128]{1,0:T(8,128)(2,1)S(1)}, bf16[512,128]{1,0:T(8,128)(2,1)S(1)}, u32[]{:S(2)}, u32[]{:S(2)}) collective-permute-start(bf16[512,128]{1,0:T(8,128)(2,1)S(1)} %get-tuple-element.93), channel_id=1, source_target_pairs={{0,6},{1,7},{2,4},{3,5},{4,2},{5,3},{6,0},{7,1},{8,14},{9,15},{10,... | collective-permute-start | bytes 393224 | tf_op jit(solution)/shard_map/ppermute | solution.py:573
  137.0 2.6 %other_rows.3 = (bf16[512,128]{1,0:T(8,128)(2,1)S(1)}, bf16[512,128]{1,0:T(8,128)(2,1)S(1)}) custom-call(bf16[2048,128]{1,0:T(8,128)(2,1)S(1)} %get-tuple-element.51.x_ref, bf16[4096,256]{1,0:T(8,128)(2,1)S(1)} %get-tuple-element.82.yb_ref, bf16[2048,4096]{1,0:T(8,128)(2,1)S(1)} %get-tuple-element.61.e_ref, f32[1,2048]{1,0:T(1,128)S(1)} %get-tuple-element.71.alpha_ref), custom_call_target="tpu_custom_call" | custom-call | flops 2147483648 | bytes 8388608 | tf_op jit(solution)/shard_map/other_rows/pallas_call | solution.py:508
  139.6 0.9 collective-permute-done.32.refs_5_
  140.5 1.0 collective-permute-start.34
  141.5 2.3 %collective-permute-start.35 = (bf16[512,128]{1,0:T(8,128)(2,1)S(1)}, bf16[512,128]{1,0:T(8,128)(2,1)S(1)}, u32[]{:S(2)}, u32[]{:S(2)}) collective-permute-start(bf16[512,128]{1,0:T(8,128)(2,1)S(1)} %get-tuple-element.88), channel_id=1, source_target_pairs={{0,16},{1,17},{2,18},{3,19},{4,20},{5,21},{6,22},{7,23},{8,24},{9,... | collective-permute-start | bytes 393224 | tf_op jit(solution)/shard_map/ppermute | solution.py:573
  143.9 1.4 other_rows.2.refs_0_
  145.3 0.9 collective-permute-done.36.refs_6_
  146.8 1.1 add_up.1
  (48 shorter events, 8.0 us)
Async XLA Ops:
  0.6 9.5 %collective-permute-start = (bf16[512,128]{1,0:T(8,128)(2,1)}, bf16[512,128]{1,0:T(8,128)(2,1)S(1)}, u32[]{:S(2)}, u32[]{:S(2)}) collective-permute-start(bf16[512,128]{1,0:T(8,128)(2,1)} %param.4), channel_id=1, source_target_pairs={{0,1},{1,0},{2,3},{3,2},{4,5},{5,4},{6,7},{7,6},{8,9},{9,8},{10,11... | collective-permute-start | bytes 393224 | tf_op jit(solution)/shard_map/ppermute | solution.py:573
  3.7 8.1 %collective-permute-start.2 = (bf16[512,128]{1,0:T(8,128)(2,1)}, bf16[512,128]{1,0:T(8,128)(2,1)S(1)}, u32[]{:S(2)}, u32[]{:S(2)}) collective-permute-start(bf16[512,128]{1,0:T(8,128)(2,1)} %param.4), channel_id=1, source_target_pairs={{0,17},{1,16},{2,19},{3,18},{4,21},{5,20},{6,23},{7,22},{8,25},{9,... | collective-permute-start | bytes 393224 | tf_op jit(solution)/shard_map/ppermute | solution.py:573
  5.1 6.7 %collective-permute-start.1 = (bf16[512,128]{1,0:T(8,128)(2,1)}, bf16[512,128]{1,0:T(8,128)(2,1)S(1)}, u32[]{:S(2)}, u32[]{:S(2)}) collective-permute-start(bf16[512,128]{1,0:T(8,128)(2,1)} %param.4), channel_id=1, source_target_pairs={{0,16},{1,17},{2,18},{3,19},{4,20},{5,21},{6,22},{7,23},{8,24},{9,... | collective-permute-start | bytes 393224 | tf_op jit(solution)/shard_map/ppermute | solution.py:573
  6.2 12.1 %collective-permute-start.5 = (bf16[512,128]{1,0:T(8,128)(2,1)}, bf16[512,128]{1,0:T(8,128)(2,1)S(1)}, u32[]{:S(2)}, u32[]{:S(2)}) collective-permute-start(bf16[512,128]{1,0:T(8,128)(2,1)} %bitcast.78), channel_id=1, source_target_pairs={{0,4},{1,5},{2,6},{3,7},{4,0},{5,1},{6,2},{7,3},{8,12},{9,13},{10,... | collective-permute-start | bytes 393224 | tf_op jit(solution)/shard_map/ppermute | solution.py:573
  9.3 2.5 %collective-permute-start.3 = (bf16[512,128]{1,0:T(8,128)(2,1)}, bf16[512,128]{1,0:T(8,128)(2,1)S(1)}, u32[]{:S(2)}, u32[]{:S(2)}) collective-permute-start(bf16[512,128]{1,0:T(8,128)(2,1)} %bitcast.79), channel_id=1, source_target_pairs={{0,8},{1,9},{2,10},{3,11},{4,12},{5,13},{6,14},{7,15},{8,0},{9,1},... | collective-permute-start | bytes 393224 | tf_op jit(solution)/shard_map/ppermute | solution.py:573
  10.1 8.1 %collective-permute-start.4 = (bf16[512,128]{1,0:T(8,128)(2,1)}, bf16[512,128]{1,0:T(8,128)(2,1)S(1)}, u32[]{:S(2)}, u32[]{:S(2)}) collective-permute-start(bf16[512,128]{1,0:T(8,128)(2,1)} %bitcast.80), channel_id=1, source_target_pairs={{0,2},{1,3},{2,0},{3,1},{4,6},{5,7},{6,4},{7,5},{8,10},{9,11},{10,... | collective-permute-start | bytes 393224 | tf_op jit(solution)/shard_map/ppermute | solution.py:573
  18.3 7.2 %collective-permute-start.6 = (bf16[512,128]{1,0:T(8,128)(2,1)S(1)}, bf16[512,128]{1,0:T(8,128)(2,1)S(1)}, u32[]{:S(2)}, u32[]{:S(2)}) collective-permute-start(bf16[512,128]{1,0:T(8,128)(2,1)S(1)} %collective-permute-done.5.refs_1_), channel_id=1, source_target_pairs={{0,2},{1,3},{2,0},{3,1},{4,6},{5,7},{6,4},{7,5},{8,10},{9,11},{10,... | collective-permute-start | bytes 393224 | tf_op jit(solution)/shard_map/ppermute | solution.py:573
  18.4 7.3 %collective-permute-start.8 = (bf16[512,128]{1,0:T(8,128)(2,1)S(1)}, bf16[512,128]{1,0:T(8,128)(2,1)S(1)}, u32[]{:S(2)}, u32[]{:S(2)}) collective-permute-start(bf16[512,128]{1,0:T(8,128)(2,1)S(1)} %collective-permute-done.5.refs_1_), channel_id=1, source_target_pairs={{0,8},{1,9},{2,10},{3,11},{4,12},{5,13},{6,14},{7,15},{8,0},{9,1},... | collective-permute-start | bytes 393224 | tf_op jit(solution)/shard_map/ppermute | solution.py:573
  18.4 7.2 %collective-permute-start.7 = (bf16[512,128]{1,0:T(8,128)(2,1)S(1)}, bf16[512,128]{1,0:T(8,128)(2,1)S(1)}, u32[]{:S(2)}, u32[]{:S(2)}) collective-permute-start(bf16[512,128]{1,0:T(8,128)(2,1)S(1)} %collective-permute-done.4.refs_0_), channel_id=1, source_target_pairs={{0,8},{1,9},{2,10},{3,11},{4,12},{5,13},{6,14},{7,15},{8,0},{9,1},... | collective-permute-start | bytes 393224 | tf_op jit(solution)/shard_map/ppermute | solution.py:573
  25.5 1.4 collective-permute-start.9
  37.1 4.7 %collective-permute-start.12 = (f32[3072]{0:T(1024)S(1)}, f32[3072]{0:T(1024)S(1)}, u32[]{:S(2)}, u32[]{:S(2)}) collective-permute-start(f32[3072]{0:T(1024)S(1)} %bitcast.71), channel_id=1, source_target_pairs={{0,17},{1,16},{2,19},{3,18},{4,21},{5,20},{6,23},{7,22},{8,25},{9,... | collective-permute-start | bytes 36872 | tf_op jit(solution)/shard_map/ppermute | solution.py:573
  37.2 4.6 %collective-permute-start.11 = (f32[3072]{0:T(1024)S(1)}, f32[3072]{0:T(1024)S(1)}, u32[]{:S(2)}, u32[]{:S(2)}) collective-permute-start(f32[3072]{0:T(1024)S(1)} %bitcast.72), channel_id=1, source_target_pairs={{0,16},{1,17},{2,18},{3,19},{4,20},{5,21},{6,22},{7,23},{8,24},{9,... | collective-permute-start | bytes 36872 | tf_op jit(solution)/shard_map/ppermute | solution.py:573
  37.2 5.1 %collective-permute-start.10 = (f32[3072]{0:T(1024)S(1)}, f32[3072]{0:T(1024)S(1)}, u32[]{:S(2)}, u32[]{:S(2)}) collective-permute-start(f32[3072]{0:T(1024)S(1)} %bitcast.73), channel_id=1, source_target_pairs={{0,1},{1,0},{2,3},{3,2},{4,5},{5,4},{6,7},{7,6},{8,9},{9,8},{10,11... | collective-permute-start | bytes 36872 | tf_op jit(solution)/shard_map/ppermute | solution.py:573
  73.8 1.3 collective-permute-start.13
  75.1 5.7 %collective-permute-start.16 = (f32[5120]{0:T(1024)S(1)}, f32[5120]{0:T(1024)S(1)}, u32[]{:S(2)}, u32[]{:S(2)}) collective-permute-start(f32[5120]{0:T(1024)S(1)} %bitcast.33), channel_id=1, source_target_pairs={{0,6},{1,7},{2,4},{3,5},{4,2},{5,3},{6,0},{7,1},{8,14},{9,15},{10,... | collective-permute-start | bytes 61448 | tf_op jit(solution)/shard_map/ppermute | solution.py:573
  78.0 4.7 %collective-permute-start.15 = (f32[5120]{0:T(1024)S(1)}, f32[5120]{0:T(1024)S(1)}, u32[]{:S(2)}, u32[]{:S(2)}) collective-permute-start(f32[5120]{0:T(1024)S(1)} %bitcast.34), channel_id=1, source_target_pairs={{0,4},{1,5},{2,6},{3,7},{4,0},{5,1},{6,2},{7,3},{8,12},{9,13},{10,... | collective-permute-start | bytes 61448 | tf_op jit(solution)/shard_map/ppermute | solution.py:573
  79.6 3.8 %collective-permute-start.14 = (f32[5120]{0:T(1024)S(1)}, f32[5120]{0:T(1024)S(1)}, u32[]{:S(2)}, u32[]{:S(2)}) collective-permute-start(f32[5120]{0:T(1024)S(1)} %bitcast.35), channel_id=1, source_target_pairs={{0,2},{1,3},{2,0},{3,1},{4,6},{5,7},{6,4},{7,5},{8,10},{9,11},{10,... | collective-permute-start | bytes 61448 | tf_op jit(solution)/shard_map/ppermute | solution.py:573
  87.9 4.6 %collective-permute-start.19 = (f32[2048]{0:T(1024)S(1)}, f32[2048]{0:T(1024)S(1)}, u32[]{:S(2)}, u32[]{:S(2)}) collective-permute-start(f32[2048]{0:T(1024)S(1)} %bitcast.57), channel_id=1, source_target_pairs={{0,17},{1,16},{2,19},{3,18},{4,21},{5,20},{6,23},{7,22},{8,25},{9,... | collective-permute-start | bytes 24584 | tf_op jit(solution)/shard_map/ppermute | solution.py:573
  88.9 3.7 %collective-permute-start.18 = (f32[2048]{0:T(1024)S(1)}, f32[2048]{0:T(1024)S(1)}, u32[]{:S(2)}, u32[]{:S(2)}) collective-permute-start(f32[2048]{0:T(1024)S(1)} %bitcast.58), channel_id=1, source_target_pairs={{0,16},{1,17},{2,18},{3,19},{4,20},{5,21},{6,22},{7,23},{8,24},{9,... | collective-permute-start | bytes 24584 | tf_op jit(solution)/shard_map/ppermute | solution.py:573
  89.6 3.7 %collective-permute-start.17 = (f32[2048]{0:T(1024)S(1)}, f32[2048]{0:T(1024)S(1)}, u32[]{:S(2)}, u32[]{:S(2)}) collective-permute-start(f32[2048]{0:T(1024)S(1)} %bitcast.59), channel_id=1, source_target_pairs={{0,1},{1,0},{2,3},{3,2},{4,5},{5,4},{6,7},{7,6},{8,9},{9,8},{10,11... | collective-permute-start | bytes 24584 | tf_op jit(solution)/shard_map/ppermute | solution.py:573
  96.0 1.2 collective-permute-start.20
  97.2 5.6 %collective-permute-start.23 = (f32[4096]{0:T(1024)S(1)}, f32[4096]{0:T(1024)S(1)}, u32[]{:S(2)}, u32[]{:S(2)}) collective-permute-start(f32[4096]{0:T(1024)S(1)} %bitcast.36), channel_id=1, source_target_pairs={{0,6},{1,7},{2,4},{3,5},{4,2},{5,3},{6,0},{7,1},{8,14},{9,15},{10,... | collective-permute-start | bytes 49160 | tf_op jit(solution)/shard_map/ppermute | solution.py:573
  100.0 4.6 %collective-permute-start.22 = (f32[4096]{0:T(1024)S(1)}, f32[4096]{0:T(1024)S(1)}, u32[]{:S(2)}, u32[]{:S(2)}) collective-permute-start(f32[4096]{0:T(1024)S(1)} %bitcast.37), channel_id=1, source_target_pairs={{0,4},{1,5},{2,6},{3,7},{4,0},{5,1},{6,2},{7,3},{8,12},{9,13},{10,... | collective-permute-start | bytes 49160 | tf_op jit(solution)/shard_map/ppermute | solution.py:573
  100.5 4.0 %collective-permute-start.21 = (f32[4096]{0:T(1024)S(1)}, f32[4096]{0:T(1024)S(1)}, u32[]{:S(2)}, u32[]{:S(2)}) collective-permute-start(f32[4096]{0:T(1024)S(1)} %bitcast.38), channel_id=1, source_target_pairs={{0,2},{1,3},{2,0},{3,1},{4,6},{5,7},{6,4},{7,5},{8,10},{9,11},{10,... | collective-permute-start | bytes 49160 | tf_op jit(solution)/shard_map/ppermute | solution.py:573
  109.0 4.6 %collective-permute-start.26 = (f32[2048]{0:T(1024)S(1)}, f32[2048]{0:T(1024)S(1)}, u32[]{:S(2)}, u32[]{:S(2)}) collective-permute-start(f32[2048]{0:T(1024)S(1)} %bitcast.39), channel_id=1, source_target_pairs={{0,17},{1,16},{2,19},{3,18},{4,21},{5,20},{6,23},{7,22},{8,25},{9,... | collective-permute-start | bytes 24584 | tf_op jit(solution)/shard_map/ppermute | solution.py:573
  110.7 3.7 %collective-permute-start.25 = (f32[2048]{0:T(1024)S(1)}, f32[2048]{0:T(1024)S(1)}, u32[]{:S(2)}, u32[]{:S(2)}) collective-permute-start(f32[2048]{0:T(1024)S(1)} %bitcast.40), channel_id=1, source_target_pairs={{0,16},{1,17},{2,18},{3,19},{4,20},{5,21},{6,22},{7,23},{8,24},{9,... | collective-permute-start | bytes 24584 | tf_op jit(solution)/shard_map/ppermute | solution.py:573
  112.6 3.7 %collective-permute-start.24 = (f32[2048]{0:T(1024)S(1)}, f32[2048]{0:T(1024)S(1)}, u32[]{:S(2)}, u32[]{:S(2)}) collective-permute-start(f32[2048]{0:T(1024)S(1)} %bitcast.41), channel_id=1, source_target_pairs={{0,1},{1,0},{2,3},{3,2},{4,5},{5,4},{6,7},{7,6},{8,9},{9,8},{10,11... | collective-permute-start | bytes 24584 | tf_op jit(solution)/shard_map/ppermute | solution.py:573
  118.6 1.2 collective-permute-start.27
  119.8 10.3 %collective-permute-start.30 = (f32[4096]{0:T(1024)S(1)}, f32[4096]{0:T(1024)S(1)}, u32[]{:S(2)}, u32[]{:S(2)}) collective-permute-start(f32[4096]{0:T(1024)S(1)} %bitcast.47), channel_id=1, source_target_pairs={{0,6},{1,7},{2,4},{3,5},{4,2},{5,3},{6,0},{7,1},{8,14},{9,15},{10,... | collective-permute-start | bytes 49160 | tf_op jit(solution)/shard_map/ppermute | solution.py:573
  121.4 8.8 %collective-permute-start.29 = (f32[4096]{0:T(1024)S(1)}, f32[4096]{0:T(1024)S(1)}, u32[]{:S(2)}, u32[]{:S(2)}) collective-permute-start(f32[4096]{0:T(1024)S(1)} %bitcast.48), channel_id=1, source_target_pairs={{0,4},{1,5},{2,6},{3,7},{4,0},{5,1},{6,2},{7,3},{8,12},{9,13},{10,... | collective-permute-start | bytes 49160 | tf_op jit(solution)/shard_map/ppermute | solution.py:573
  122.0 8.2 %collective-permute-start.28 = (f32[4096]{0:T(1024)S(1)}, f32[4096]{0:T(1024)S(1)}, u32[]{:S(2)}, u32[]{:S(2)}) collective-permute-start(f32[4096]{0:T(1024)S(1)} %bitcast.49), channel_id=1, source_target_pairs={{0,2},{1,3},{2,0},{3,1},{4,6},{5,7},{6,4},{7,5},{8,10},{9,11},{10,... | collective-permute-start | bytes 49160 | tf_op jit(solution)/shard_map/ppermute | solution.py:573
  130.1 2.4 %collective-permute-start.31 = (bf16[2048,128]{1,0:T(8,128)(2,1)S(1)}, bf16[2048,128]{1,0:T(8,128)(2,1)S(1)}, u32[]{:S(2)}, u32[]{:S(2)}) collective-permute-start(bf16[2048,128]{1,0:T(8,128)(2,1)S(1)} %get-tuple-element.76), channel_id=1, source_target_pairs={{0,8},{1,9},{2,10},{3,11},{4,12},{5,13},{6,14},{7,15},{8,0},{9,1},... | collective-permute-start | bytes 1572872 | tf_op jit(solution)/shard_map/ppermute | solution.py:573
  132.3 7.3 %collective-permute-start.33 = (bf16[512,128]{1,0:T(8,128)(2,1)S(1)}, bf16[512,128]{1,0:T(8,128)(2,1)S(1)}, u32[]{:S(2)}, u32[]{:S(2)}) collective-permute-start(bf16[512,128]{1,0:T(8,128)(2,1)S(1)} %get-tuple-element.86), channel_id=1, source_target_pairs={{0,17},{1,16},{2,19},{3,18},{4,21},{5,20},{6,23},{7,22},{8,25},{9,... | collective-permute-start | bytes 393224 | tf_op jit(solution)/shard_map/ppermute | solution.py:573
  132.5 8.0 %collective-permute-start.32 = (bf16[512,128]{1,0:T(8,128)(2,1)S(1)}, bf16[512,128]{1,0:T(8,128)(2,1)S(1)}, u32[]{:S(2)}, u32[]{:S(2)}) collective-permute-start(bf16[512,128]{1,0:T(8,128)(2,1)S(1)} %get-tuple-element.85), channel_id=1, source_target_pairs={{0,2},{1,3},{2,0},{3,1},{4,6},{5,7},{6,4},{7,5},{8,10},{9,11},{10,... | collective-permute-start | bytes 393224 | tf_op jit(solution)/shard_map/ppermute | solution.py:573
  133.2 12.9 %collective-permute-start.36 = (bf16[512,128]{1,0:T(8,128)(2,1)S(1)}, bf16[512,128]{1,0:T(8,128)(2,1)S(1)}, u32[]{:S(2)}, u32[]{:S(2)}) collective-permute-start(bf16[512,128]{1,0:T(8,128)(2,1)S(1)} %get-tuple-element.92), channel_id=1, source_target_pairs={{0,4},{1,5},{2,6},{3,7},{4,0},{5,1},{6,2},{7,3},{8,12},{9,13},{10,... | collective-permute-start | bytes 393224 | tf_op jit(solution)/shard_map/ppermute | solution.py:573
  135.2 10.9 %collective-permute-start.37 = (bf16[512,128]{1,0:T(8,128)(2,1)S(1)}, bf16[512,128]{1,0:T(8,128)(2,1)S(1)}, u32[]{:S(2)}, u32[]{:S(2)}) collective-permute-start(bf16[512,128]{1,0:T(8,128)(2,1)S(1)} %get-tuple-element.93), channel_id=1, source_target_pairs={{0,6},{1,7},{2,4},{3,5},{4,2},{5,3},{6,0},{7,1},{8,14},{9,15},{10,... | collective-permute-start | bytes 393224 | tf_op jit(solution)/shard_map/ppermute | solution.py:573
  140.5 5.6 %collective-permute-start.34 = (bf16[512,128]{1,0:T(8,128)(2,1)S(1)}, bf16[512,128]{1,0:T(8,128)(2,1)S(1)}, u32[]{:S(2)}, u32[]{:S(2)}) collective-permute-start(bf16[512,128]{1,0:T(8,128)(2,1)S(1)} %get-tuple-element.87), channel_id=1, source_target_pairs={{0,1},{1,0},{2,3},{3,2},{4,5},{5,4},{6,7},{7,6},{8,9},{9,8},{10,11... | collective-permute-start | bytes 393224 | tf_op jit(solution)/shard_map/ppermute | solution.py:573
  141.5 5.3 %collective-permute-start.35 = (bf16[512,128]{1,0:T(8,128)(2,1)S(1)}, bf16[512,128]{1,0:T(8,128)(2,1)S(1)}, u32[]{:S(2)}, u32[]{:S(2)}) collective-permute-start(bf16[512,128]{1,0:T(8,128)(2,1)S(1)} %get-tuple-element.88), channel_id=1, source_target_pairs={{0,16},{1,17},{2,18},{3,19},{4,20},{5,21},{6,22},{7,23},{8,24},{9,... | collective-permute-start | bytes 393224 | tf_op jit(solution)/shard_map/ppermute | solution.py:573

commit v12 on v11

--- a/solution.py
+++ b/solution.py
@@ -15,7 +15,7 @@
 CROSS = 2.0 * LOG2E / EPSILON
 NT = (((1,), (1,)), ((), ()))
 VMEM = pl.BlockSpec(memory_space=pltpu.VMEM)
-GROUP = 32
+GROUP = 64
 HEAVY = 32
 
 
@@ -225,15 +225,26 @@
     return parts.astype(jnp.bfloat16)
 
 
-def row_sums(width, e_ref, w16_ref, o_ref):
-    for at in range(0, e_ref.shape[0], width):
+def row_sums(width, e_ref, w_ref, w16_ref, acc_ref, o_ref):
+    rows, cols = e_ref.shape
+    half = rows - acc_ref.shape[0]
+    for at in range(0, half, width):
         got = lax.dot_general(w16_ref[...], e_ref[at:at + width, :], NT, preferred_element_type=jnp.float32)
+        for k in range(at, at + width, 64):
+            total = jnp.zeros((64, 128), jnp.float32)
+            for q in range(0, cols, 128):
+                e = e_ref[half + k:half + k + 64, q:q + 128].astype(jnp.float32)
+                total = total + e * w_ref[:, q:q + 128]
+            acc_ref[k:k + 64, :] = total
         o_ref[:, at:at + width] = jnp.sum(got, axis=0, keepdims=True)
+    for at in range(0, rows - half, 128):
+        total = jnp.sum(jnp.transpose(acc_ref[at:at + 128, :]), axis=0, keepdims=True)
+        o_ref[:, half + at:half + at + 128] = total
 
 
 def first_row_kernel(width, shifts, parts, e_ref, shift_ref, *refs):
     nz = len(shifts)
-    got, (o_ref, beta_ref, b_ref, w16_ref) = refs[:nz], refs[nz:]
+    got, (o_ref, beta_ref, b_ref, w16_ref, acc_ref) = refs[:nz], refs[nz:]
     cols = e_ref.shape[1]
     share = cols // parts
     for k in range(parts):
@@ -242,7 +253,7 @@
     lse = lse2(ordered([part[:, :cols] for part in got], shifts, parts))
     beta_ref[...] = jnp.exp2(jnp.log2(b_ref[...]) - lse + shift_ref[...])
     w16_ref[...] = stacked(beta_ref[...])
-    row_sums(width, e_ref, w16_ref, o_ref)
+    row_sums(width, e_ref, beta_ref, w16_ref, acc_ref, o_ref)
 
 
 def new_scale(b_ref, got, shifts, parts):
@@ -250,9 +261,10 @@
 
 
 def row_kernel(width, shifts, parts, e_ref, first_ref, b_ref, *refs):
-    got, (o_ref, w16_ref) = refs[:-2], refs[-2:]
-    w16_ref[...] = stacked(first_ref[...] * new_scale(b_ref, got, shifts, parts))
-    row_sums(width, e_ref, w16_ref, o_ref)
+    got, (o_ref, w16_ref, acc_ref, w_ref) = refs[:-4], refs[-4:]
+    w_ref[...] = first_ref[...] * new_scale(b_ref, got, shifts, parts)
+    w16_ref[...] = stacked(w_ref[...])
+    row_sums(width, e_ref, w_ref, w16_ref, acc_ref, o_ref)
 
 
 def column_kernel(width, shifts, parts, e_ref, a_ref, first_ref, *refs):
@@ -268,15 +280,21 @@
     return value.reshape(1, -1) if value.ndim == 1 else value
 
 
-def weighted(kernel, outs, e, rows, got, parts, width=512):
+def weighted(kernel, outs, e, rows, got, parts):
     got, shifts = got
     size = e.shape[0] if kernel is column_kernel else e.shape[1]
+    width = 512 if kernel is column_kernel else 256
+    scratch = [pltpu.VMEM((16, size), jnp.bfloat16)]
+    if kernel is not column_kernel:
+        scratch.append(pltpu.VMEM((e.shape[0] // 2, 128), jnp.float32))
+    if kernel is row_kernel:
+        scratch.append(pltpu.VMEM((1, size), jnp.float32))
     return pl.pallas_call(
         functools.partial(kernel, width, tuple(shifts), parts),
         out_shape=[shape(*dims) for dims in outs],
         in_specs=[VMEM] * (1 + len(rows) + len(got)),
         out_specs=[VMEM] * len(outs),
-        scratch_shapes=[pltpu.VMEM((16, size), jnp.bfloat16)],
+        scratch_shapes=scratch,
         compiler_params=pltpu.CompilerParams(vmem_limit_bytes=16 << 20),
         cost_estimate=pl.CostEstimate(flops=2 * e.size, bytes_accessed=2 * e.size, transcendentals=0),
         name="weighted_sum",
@@ -348,7 +366,7 @@
     )(own, mass.reshape(1, -1), x, first, *ys)
 
 
-def column_lse(x, y, mass, tail, got, width=1024, chunk=512):
+def column_lse(x, y, mass, tail, got, width=512, chunk=512):
     rows, cols = x.shape[0], y.shape[0]
     return pl.pallas_call(
         functools.partial(column_lse_kernel, width, chunk, len(got)),
@@ -586,8 +604,11 @@
 
     xs, _ = direct(imu, across)
     own, mine = lax.optimization_barrier((jnp.concatenate([imu, camera[0]]), camera[0]))
+    near = [mine] + [None] * (nz - 1)
+    for z in range(1, nz):
+        if not z & (z - 1):
+            near[z] = swap(mine if z == 1 else camera[0], along[z])
     far = [swap(mine, core)]
-    near = [mine if z == 0 else None if z & (z - 1) else swap(mine, along[z]) for z in range(nz)]
 
     def pair(mass, place, share):
         return [lax.dynamic_slice_in_dim(mass, (place ^ k) * share, share, 0) for k in range(2)]
@@ -596,7 +617,10 @@
     mass = jnp.concatenate(pair(imu_mass, col, share_x) + pair(cam_mass, row, share_y))
 
     x, xt, first = row_lse_early(own, xs[1:], far[0])
-    first, near, mass = lax.optimization_barrier((first, near, mass))
+    relays = [z for z in range(2, nz) if not z & (z - 1)]
+    first, mass, got = lax.optimization_barrier((first, mass, [near[z] for z in relays]))
+    for z, part in zip(relays, got):
+        near[z] = part
     for z in range(1, nz):
         if z & (z - 1):
             near[z] = swap(near[z & (z - 1)], along[z & -z])

time: 148 us -> 148 us (level)
  transfers between devices with their start and end apart: 38 -> 38, of which waited for: 20 -> 19; matrix products, arithmetic and copies ran while one was open for 1% -> 1% of each run, Pallas kernels for 17% -> 17%
where the time goes in v12:
time: 148 us
  Pallas kernels  81.6 us (55%)
  starting transfers between devices  42.7 us (29%)
  waiting for transfers between devices  20.6 us (14%)
    ppermute x38, starting transfers between devices, swap(): lax.ppermute(value, ('row', 'col'), [(i, i ^ mask) for i in range(self.co...  42.7 us
    pallas_call x1, Pallas kernels, column_lse(): pl.pallas_call(functools.partial(column_lse_kernel, width, chunk, len(got...  32.5 us
    ppermute x38, waiting for transfers between devices, swap(): lax.ppermute(value, ('row', 'col'), [(i, i ^ mask) for i in range(self.co...  20.6 us
    pallas_call x4, Pallas kernels, weighted(): pl.pallas_call(functools.partial(kernel, width, tuple(shifts), parts), ou...  12.7 us
    pallas_call x1, Pallas kernels, row_lse_late(): pl.pallas_call(functools.partial(row_lse_late_kernel, width, len(ys)), ou...  10.2 us
    pallas_call x1, Pallas kernels, row_lse_early(): pl.pallas_call(functools.partial(row_lse_early_kernel, width, len(xs)), o...  6.52 us
    pallas_call x1, Pallas kernels, row_lse_middle(): pl.pallas_call(functools.partial(row_lse_middle_kernel, width, len(ys)),...  6.5 us
    pallas_call x1, Pallas kernels, column_grad(): pl.pallas_call(functools.partial(column_grad_kernel, width), out_shape=(s...  5.76 us
  transfers between devices with their start and end apart: 38, of which 19 were waited for; matrix products, arithmetic and copies ran while one was open for 1% of the time, Pallas kernels for 17%

profile of v12, /device:TPU:0, one launch (start us, length us, event | category | flops | bytes accessed | tf_op | source)
XLA Modules:
  0.0 147.6 jit_solution(7989861139934724478)
XLA Ops:
  0.6 3.0 %collective-permute-start = (bf16[512,128]{1,0:T(8,128)(2,1)}, bf16[512,128]{1,0:T(8,128)(2,1)S(1)}, u32[]{:S(2)}, u32[]{:S(2)}) collective-permute-start(bf16[512,128]{1,0:T(8,128)(2,1)} %param.4), channel_id=1, source_target_pairs={{0,1},{1,0},{2,3},{3,2},{4,5},{5,4},{6,7},{7,6},{8,9},{9,8},{10,11... | collective-permute-start | bytes 393224 | tf_op jit(solution)/shard_map/ppermute | solution.py:591
  3.7 1.4 collective-permute-start.2
  5.2 3.0 %collective-permute-start.4 = (bf16[512,128]{1,0:T(8,128)(2,1)}, bf16[512,128]{1,0:T(8,128)(2,1)S(1)}, u32[]{:S(2)}, u32[]{:S(2)}) collective-permute-start(bf16[512,128]{1,0:T(8,128)(2,1)} %bitcast.77), channel_id=1, source_target_pairs={{0,4},{1,5},{2,6},{3,7},{4,0},{5,1},{6,2},{7,3},{8,12},{9,13},{10,... | collective-permute-start | bytes 393224 | tf_op jit(solution)/shard_map/ppermute | solution.py:591
  8.2 1.0 pad_maximum_fusion.own_ref
  9.3 0.9 fusion
  10.2 1.6 %collective-permute-start.5 = (bf16[512,128]{1,0:T(8,128)(2,1)}, bf16[512,128]{1,0:T(8,128)(2,1)S(1)}, u32[]{:S(2)}, u32[]{:S(2)}) collective-permute-start(bf16[512,128]{1,0:T(8,128)(2,1)} %bitcast.80), channel_id=1, source_target_pairs={{0,2},{1,3},{2,0},{3,1},{4,6},{5,7},{6,4},{7,5},{8,10},{9,11},{10,... | collective-permute-start | bytes 393224 | tf_op jit(solution)/shard_map/ppermute | solution.py:591
  11.8 6.5 %row_lse_early.1 = (bf16[2048,128]{1,0:T(8,128)(2,1)S(1)}, bf16[128,2048]{1,0:T(8,128)(2,1)S(1)}, f32[1,2048]{1,0:T(1,128)S(1)}) custom-call(bf16[1024,128]{1,0:T(8,128)(2,1)S(1)} %pad_maximum_fusion.own_ref, bf16[512,128]{1,0:T(8,128)(2,1)S(1)} %collective-permute-done.refs_0_, bf16[512,128]{1,0:T(8,128)(2,1)S(1)} %collective-permute-done.1.refs_1_, ...), custom_call_target="tpu_custom_call" | custom-call | flops 536870912 | bytes 786432 | tf_op jit(solution)/shard_map/row_lse_early/pallas_call | solution.py:323
  19.0 6.5 %row_lse_middle.1.first_ref = f32[1,2048]{1,0:T(1,128)S(1)} custom-call(bf16[2048,128]{1,0:T(8,128)(2,1)S(1)} %get-tuple-element.50.x_ref, f32[1,2048]{1,0:T(1,128)S(1)} %get-tuple-element.53.first_ref, bf16[512,128]{1,0:T(8,128)(2,1)S(1)} %collective-permute-done.5.refs_0_, bf16[512,128]{1,0:T(8,128)(2,1)S(1)} %collective-permute-done.4.refs_1_), custom_call_target="tpu_custom_call" | custom-call | flops 536870912 | bytes 786432 | tf_op jit(solution)/shard_map/row_lse_middle/pallas_call | solution.py:338
  25.7 1.2 collective-permute-done.9.refs_6_
  27.0 10.2 %row_lse_late.1 = (bf16[4096,128]{1,0:T(8,128)(2,1)S(1)}, f32[1,3072]{1,0:T(1,128)S(1)}) custom-call(bf16[1024,128]{1,0:T(8,128)(2,1)S(1)} %pad_maximum_fusion.own_ref, f32[1,2048]{1,0:T(1,128)S(1)} %bitcast.66, bf16[2048,128]{1,0:T(8,128)(2,1)S(1)} %get-tuple-element.50.x_ref, f32[1,2048]{1,0:T(1,128)S(1)} %row_lse_middle.1.first_ref, ...), custom_call_target="tpu_custom_call" | custom-call | flops 1073741824 | bytes 1048576 | tf_op jit(solution)/shard_map/row_lse_late/pallas_call | solution.py:357
  37.3 3.4 %collective-permute-start.10 = (f32[3072]{0:T(1024)S(1)}, f32[3072]{0:T(1024)S(1)}, u32[]{:S(2)}, u32[]{:S(2)}) collective-permute-start(f32[3072]{0:T(1024)S(1)} %bitcast.73), channel_id=1, source_target_pairs={{0,1},{1,0},{2,3},{3,2},{4,5},{5,4},{6,7},{7,6},{8,9},{9,8},{10,11... | collective-permute-start | bytes 36872 | tf_op jit(solution)/shard_map/ppermute | solution.py:591
  40.7 1.1 collective-permute-done.12
  42.4 32.5 %column_lse.1 = (f32[1,5120]{1,0:T(1,128)S(1)}, bf16[2048,4096]{1,0:T(8,128)(2,1)S(1)}, f32[1,4096]{1,0:T(1,128)S(1)}, f32[1,2048]{1,0:T(1,128)S(1)}) custom-call(bf16[2048,128]{1,0:T(8,128)(2,1)S(1)} %get-tuple-element.50.x_ref, bf16[4096,128]{1,0:T(8,128)(2,1)S(1)} %get-tuple-element.57.y_ref, f32[1,2048]{1,0:T(1,128)S(1)} %bitcast.67, ...), custom_call_target="tpu_custom_call" | custom-call | flops 2147483648 | bytes 1572864 | tf_op jit(solution)/shard_map/column_lse/pallas_call | solution.py:371
  75.0 1.2 collective-permute-done.13
  76.2 2.8 %collective-permute-start.16 = (f32[5120]{0:T(1024)S(1)}, f32[5120]{0:T(1024)S(1)}, u32[]{:S(2)}, u32[]{:S(2)}) collective-permute-start(f32[5120]{0:T(1024)S(1)} %bitcast.33), channel_id=1, source_target_pairs={{0,6},{1,7},{2,4},{3,5},{4,2},{5,3},{6,0},{7,1},{8,14},{9,15},{10,... | collective-permute-start | bytes 61448 | tf_op jit(solution)/shard_map/ppermute | solution.py:591
  79.0 1.6 %collective-permute-start.15 = (f32[5120]{0:T(1024)S(1)}, f32[5120]{0:T(1024)S(1)}, u32[]{:S(2)}, u32[]{:S(2)}) collective-permute-start(f32[5120]{0:T(1024)S(1)} %bitcast.34), channel_id=1, source_target_pairs={{0,4},{1,5},{2,6},{3,7},{4,0},{5,1},{6,2},{7,3},{8,12},{9,13},{10,... | collective-permute-start | bytes 61448 | tf_op jit(solution)/shard_map/ppermute | solution.py:591
  81.1 0.9 collective-permute-done.16
  82.0 1.7 %collective-permute-done.15 = f32[5120]{0:T(1024)S(1)} collective-permute-done((f32[5120]{0:T(1024)S(1)}, f32[5120]{0:T(1024)S(1)}, u32[]{:S(2)}, u32[]{:S(2)}) %collective-permute-start.15) | collective-permute-done | bytes 20512 | tf_op jit(solution)/shard_map/ppermute | solution.py:591
  84.4 3.8 %weighted_sum.4 = (f32[1,2048]{1,0:T(1,128)S(1)}, f32[1,4096]{1,0:T(1,128)S(1)}, f32[1,4096]{1,0:T(1,128)S(1)}) custom-call(bf16[2048,4096]{1,0:T(8,128)(2,1)S(1)} %get-tuple-element.59.e_ref, f32[1,4096]{1,0:T(1,128)S(1)} %get-tuple-element.61.shift_ref, f32[1,5120]{1,0:T(1,128)S(1)} %pair.3.refs_0_, f32[1,5120]{1,0:T(1,128)S(1)} %bitcast.44, ...), custom_call_target="tpu_custom_call" | custom-call | flops 16777216 | bytes 16777216 | tf_op jit(solution)/shard_map/weighted_sum/pallas_call | solution.py:292
  88.2 0.9 collective-permute-start.19
  89.1 0.8 collective-permute-start.18
  89.9 1.9 %collective-permute-start.17 = (f32[2048]{0:T(1024)S(1)}, f32[2048]{0:T(1024)S(1)}, u32[]{:S(2)}, u32[]{:S(2)}) collective-permute-start(f32[2048]{0:T(1024)S(1)} %bitcast.59), channel_id=1, source_target_pairs={{0,1},{1,0},{2,3},{3,2},{4,5},{5,4},{6,7},{7,6},{8,9},{9,8},{10,11... | collective-permute-start | bytes 24584 | tf_op jit(solution)/shard_map/ppermute | solution.py:591
  91.8 1.1 collective-permute-done.19
  93.6 2.8 %weighted_sum.5 = (f32[1,4096]{1,0:T(1,128)S(1)}, f32[1,2048]{1,0:T(1,128)}) custom-call(bf16[2048,4096]{1,0:T(8,128)(2,1)S(1)} %get-tuple-element.59.e_ref, f32[1,2048]{1,0:T(1,128)S(1)} %get-tuple-element.60.a_ref, f32[1,4096]{1,0:T(1,128)S(1)} %get-tuple-element.63.first_ref, f32[1,2048]{1,0:T(1,128)S(1)} %get-tuple-element.65.refs_0_, ...), custom_call_target="tpu_custom_call" | custom-call | flops 16777216 | bytes 16777216 | tf_op jit(solution)/shard_map/weighted_sum/pallas_call | solution.py:292
  96.4 1.2 collective-permute-done.20
  97.6 2.7 %collective-permute-start.23 = (f32[4096]{0:T(1024)S(1)}, f32[4096]{0:T(1024)S(1)}, u32[]{:S(2)}, u32[]{:S(2)}) collective-permute-start(f32[4096]{0:T(1024)S(1)} %bitcast.36), channel_id=1, source_target_pairs={{0,6},{1,7},{2,4},{3,5},{4,2},{5,3},{6,0},{7,1},{8,14},{9,15},{10,... | collective-permute-start | bytes 49160 | tf_op jit(solution)/shard_map/ppermute | solution.py:591
  101.0 1.0 collective-permute-start.21
  102.0 1.1 collective-permute-done.23
  103.2 1.8 %collective-permute-done.22 = f32[4096]{0:T(1024)S(1)} collective-permute-done((f32[4096]{0:T(1024)S(1)}, f32[4096]{0:T(1024)S(1)}, u32[]{:S(2)}, u32[]{:S(2)}) %collective-permute-start.22) | collective-permute-done | bytes 16416 | tf_op jit(solution)/shard_map/ppermute | solution.py:591
  104.9 3.8 %weighted_sum.6.refs_0_ = f32[1,2048]{1,0:T(1,128)S(1)} custom-call(bf16[2048,4096]{1,0:T(8,128)(2,1)S(1)} %get-tuple-element.59.e_ref, f32[1,4096]{1,0:T(1,128)S(1)} %get-tuple-element.63.first_ref, f32[1,4096]{1,0:T(1,128)S(1)} %get-tuple-element.64.b_ref, f32[1,4096]{1,0:T(1,128)S(1)} %pair.4.refs_0_, f32[1,4096]{1,0:T(1,128)S(1)} %bitcast.56, ...), custom_call_target="tpu_custom_call" | custom-call | flops 16777216 | bytes 16777216 | tf_op jit(solution)/shard_map/weighted_sum/pallas_call | solution.py:292
  108.8 1.6 %collective-permute-start.26 = (f32[2048]{0:T(1024)S(1)}, f32[2048]{0:T(1024)S(1)}, u32[]{:S(2)}, u32[]{:S(2)}) collective-permute-start(f32[2048]{0:T(1024)S(1)} %bitcast.39), channel_id=1, source_target_pairs={{0,17},{1,16},{2,19},{3,18},{4,21},{5,20},{6,23},{7,22},{8,25},{9,... | collective-permute-start | bytes 24584 | tf_op jit(solution)/shard_map/ppermute | solution.py:591
  110.4 1.9 %collective-permute-start.25 = (f32[2048]{0:T(1024)S(1)}, f32[2048]{0:T(1024)S(1)}, u32[]{:S(2)}, u32[]{:S(2)}) collective-permute-start(f32[2048]{0:T(1024)S(1)} %bitcast.40), channel_id=1, source_target_pairs={{0,16},{1,17},{2,18},{3,19},{4,20},{5,21},{6,22},{7,23},{8,24},{9,... | collective-permute-start | bytes 24584 | tf_op jit(solution)/shard_map/ppermute | solution.py:591
  112.3 1.1 collective-permute-done.26
  114.1 1.9 %collective-permute-done.24 = f32[2048]{0:T(1024)S(1)} collective-permute-done((f32[2048]{0:T(1024)S(1)}, f32[2048]{0:T(1024)S(1)}, u32[]{:S(2)}, u32[]{:S(2)}) %collective-permute-start.24) | collective-permute-done | bytes 8224 | tf_op jit(solution)/shard_map/ppermute | solution.py:591
  116.0 2.3 %weighted_sum.7 = (f32[1,4096]{1,0:T(1,128)S(1)}, f32[1,2048]{1,0:T(1,128)S(1)}) custom-call(bf16[2048,4096]{1,0:T(8,128)(2,1)S(1)} %get-tuple-element.59.e_ref, f32[1,2048]{1,0:T(1,128)S(1)} %get-tuple-element.60.a_ref, f32[1,4096]{1,0:T(1,128)S(1)} %get-tuple-element.63.first_ref, f32[1,2048]{1,0:T(1,128)S(1)} %weighted_sum.6.refs_0_, ...), custom_call_target="tpu_custom_call" | custom-call | flops 16777216 | bytes 16777216 | tf_op jit(solution)/shard_map/weighted_sum/pallas_call | solution.py:292
  118.4 1.2 collective-permute-done.27
  119.6 1.5 %collective-permute-start.30 = (f32[4096]{0:T(1024)S(1)}, f32[4096]{0:T(1024)S(1)}, u32[]{:S(2)}, u32[]{:S(2)}) collective-permute-start(f32[4096]{0:T(1024)S(1)} %bitcast.47), channel_id=1, source_target_pairs={{0,6},{1,7},{2,4},{3,5},{4,2},{5,3},{6,0},{7,1},{8,14},{9,15},{10,... | collective-permute-start | bytes 49160 | tf_op jit(solution)/shard_map/ppermute | solution.py:591
  121.7 2.3 %collective-permute-start.28 = (f32[4096]{0:T(1024)S(1)}, f32[4096]{0:T(1024)S(1)}, u32[]{:S(2)}, u32[]{:S(2)}) collective-permute-start(f32[4096]{0:T(1024)S(1)} %bitcast.49), channel_id=1, source_target_pairs={{0,2},{1,3},{2,0},{3,1},{4,6},{5,7},{6,4},{7,5},{8,10},{9,11},{10,... | collective-permute-start | bytes 49160 | tf_op jit(solution)/shard_map/ppermute | solution.py:591
  124.0 5.8 %column_grad.1 = (f32[2048,128]{1,0:T(8,128)S(1)}, bf16[2048,128]{1,0:T(8,128)(2,1)S(1)}) custom-call(bf16[128,2048]{1,0:T(8,128)(2,1)S(1)} %get-tuple-element.72.xt_ref, bf16[4096,128]{1,0:T(8,128)(2,1)S(1)} %get-tuple-element.57.y_ref, bf16[2048,4096]{1,0:T(8,128)(2,1)S(1)} %get-tuple-element.59.e_ref, f32[1,2048]{1,0:T(1,128)S(1)} %get-tuple-element.69.alpha_ref, ...), custom_call_target="tpu_custom_call" | custom-call | flops 4294967296 | bytes 16777216 | tf_op jit(solution)/shard_map/column_grad/pallas_call | solution.py:433
  129.9 2.1 %first_rows.1 = (bf16[4096,256]{1,0:T(8,128)(2,1)S(1)}, f32[1,512]{1,0:T(1,128)S(1)}, bf16[512,128]{1,0:T(8,128)(2,1)S(1)}) custom-call(bf16[2048,128]{1,0:T(8,128)(2,1)S(1)} %get-tuple-element.50.x_ref, bf16[4096,128]{1,0:T(8,128)(2,1)S(1)} %get-tuple-element.57.y_ref, bf16[2048,4096]{1,0:T(8,128)(2,1)S(1)} %get-tuple-element.59.e_ref, ...), custom_call_target="tpu_custom_call" | custom-call | flops 34359738368 | bytes 134217728 | tf_op jit(solution)/shard_map/first_rows/pallas_call | solution.py:508
  132.8 2.0 %collective-permute-start.36 = (bf16[512,128]{1,0:T(8,128)(2,1)S(1)}, bf16[512,128]{1,0:T(8,128)(2,1)S(1)}, u32[]{:S(2)}, u32[]{:S(2)}) collective-permute-start(bf16[512,128]{1,0:T(8,128)(2,1)S(1)} %get-tuple-element.90), channel_id=1, source_target_pairs={{0,4},{1,5},{2,6},{3,7},{4,0},{5,1},{6,2},{7,3},{8,12},{9,13},{10,... | collective-permute-start | bytes 393224 | tf_op jit(solution)/shard_map/ppermute | solution.py:591
  134.8 2.0 %collective-permute-start.37 = (bf16[512,128]{1,0:T(8,128)(2,1)S(1)}, bf16[512,128]{1,0:T(8,128)(2,1)S(1)}, u32[]{:S(2)}, u32[]{:S(2)}) collective-permute-start(bf16[512,128]{1,0:T(8,128)(2,1)S(1)} %get-tuple-element.91), channel_id=1, source_target_pairs={{0,6},{1,7},{2,4},{3,5},{4,2},{5,3},{6,0},{7,1},{8,14},{9,15},{10,... | collective-permute-start | bytes 393224 | tf_op jit(solution)/shard_map/ppermute | solution.py:591
  136.8 2.6 %other_rows.3 = (bf16[512,128]{1,0:T(8,128)(2,1)S(1)}, bf16[512,128]{1,0:T(8,128)(2,1)S(1)}) custom-call(bf16[2048,128]{1,0:T(8,128)(2,1)S(1)} %get-tuple-element.50.x_ref, bf16[4096,256]{1,0:T(8,128)(2,1)S(1)} %get-tuple-element.80.yb_ref, bf16[2048,4096]{1,0:T(8,128)(2,1)S(1)} %get-tuple-element.59.e_ref, f32[1,2048]{1,0:T(1,128)S(1)} %get-tuple-element.69.alpha_ref), custom_call_target="tpu_custom_call" | custom-call | flops 2147483648 | bytes 8388608 | tf_op jit(solution)/shard_map/other_rows/pallas_call | solution.py:526
  139.4 0.9 collective-permute-done.32.refs_5_
  140.3 1.0 collective-permute-start.34
  141.3 2.3 %collective-permute-start.35 = (bf16[512,128]{1,0:T(8,128)(2,1)S(1)}, bf16[512,128]{1,0:T(8,128)(2,1)S(1)}, u32[]{:S(2)}, u32[]{:S(2)}) collective-permute-start(bf16[512,128]{1,0:T(8,128)(2,1)S(1)} %get-tuple-element.86), channel_id=1, source_target_pairs={{0,16},{1,17},{2,18},{3,19},{4,20},{5,21},{6,22},{7,23},{8,24},{9,... | collective-permute-start | bytes 393224 | tf_op jit(solution)/shard_map/ppermute | solution.py:591
  143.6 1.4 other_rows.2.refs_0_
  146.5 1.1 add_up.1
  (48 shorter events, 8.3 us)
Async XLA Ops:
  0.6 9.5 %collective-permute-start = (bf16[512,128]{1,0:T(8,128)(2,1)}, bf16[512,128]{1,0:T(8,128)(2,1)S(1)}, u32[]{:S(2)}, u32[]{:S(2)}) collective-permute-start(bf16[512,128]{1,0:T(8,128)(2,1)} %param.4), channel_id=1, source_target_pairs={{0,1},{1,0},{2,3},{3,2},{4,5},{5,4},{6,7},{7,6},{8,9},{9,8},{10,11... | collective-permute-start | bytes 393224 | tf_op jit(solution)/shard_map/ppermute | solution.py:591
  3.7 8.2 %collective-permute-start.2 = (bf16[512,128]{1,0:T(8,128)(2,1)}, bf16[512,128]{1,0:T(8,128)(2,1)S(1)}, u32[]{:S(2)}, u32[]{:S(2)}) collective-permute-start(bf16[512,128]{1,0:T(8,128)(2,1)} %param.4), channel_id=1, source_target_pairs={{0,17},{1,16},{2,19},{3,18},{4,21},{5,20},{6,23},{7,22},{8,25},{9,... | collective-permute-start | bytes 393224 | tf_op jit(solution)/shard_map/ppermute | solution.py:591
  5.1 6.7 %collective-permute-start.1 = (bf16[512,128]{1,0:T(8,128)(2,1)}, bf16[512,128]{1,0:T(8,128)(2,1)S(1)}, u32[]{:S(2)}, u32[]{:S(2)}) collective-permute-start(bf16[512,128]{1,0:T(8,128)(2,1)} %param.4), channel_id=1, source_target_pairs={{0,16},{1,17},{2,18},{3,19},{4,20},{5,21},{6,22},{7,23},{8,24},{9,... | collective-permute-start | bytes 393224 | tf_op jit(solution)/shard_map/ppermute | solution.py:591
  5.2 13.2 %collective-permute-start.4 = (bf16[512,128]{1,0:T(8,128)(2,1)}, bf16[512,128]{1,0:T(8,128)(2,1)S(1)}, u32[]{:S(2)}, u32[]{:S(2)}) collective-permute-start(bf16[512,128]{1,0:T(8,128)(2,1)} %bitcast.77), channel_id=1, source_target_pairs={{0,4},{1,5},{2,6},{3,7},{4,0},{5,1},{6,2},{7,3},{8,12},{9,13},{10,... | collective-permute-start | bytes 393224 | tf_op jit(solution)/shard_map/ppermute | solution.py:591
  9.2 2.6 %collective-permute-start.3 = (bf16[512,128]{1,0:T(8,128)(2,1)}, bf16[512,128]{1,0:T(8,128)(2,1)S(1)}, u32[]{:S(2)}, u32[]{:S(2)}) collective-permute-start(bf16[512,128]{1,0:T(8,128)(2,1)} %bitcast.79), channel_id=1, source_target_pairs={{0,8},{1,9},{2,10},{3,11},{4,12},{5,13},{6,14},{7,15},{8,0},{9,1},... | collective-permute-start | bytes 393224 | tf_op jit(solution)/shard_map/ppermute | solution.py:591
  10.2 8.3 %collective-permute-start.5 = (bf16[512,128]{1,0:T(8,128)(2,1)}, bf16[512,128]{1,0:T(8,128)(2,1)S(1)}, u32[]{:S(2)}, u32[]{:S(2)}) collective-permute-start(bf16[512,128]{1,0:T(8,128)(2,1)} %bitcast.80), channel_id=1, source_target_pairs={{0,2},{1,3},{2,0},{3,1},{4,6},{5,7},{6,4},{7,5},{8,10},{9,11},{10,... | collective-permute-start | bytes 393224 | tf_op jit(solution)/shard_map/ppermute | solution.py:591
  18.4 7.2 %collective-permute-start.6 = (bf16[512,128]{1,0:T(8,128)(2,1)S(1)}, bf16[512,128]{1,0:T(8,128)(2,1)S(1)}, u32[]{:S(2)}, u32[]{:S(2)}) collective-permute-start(bf16[512,128]{1,0:T(8,128)(2,1)S(1)} %collective-permute-done.4.refs_1_), channel_id=1, source_target_pairs={{0,2},{1,3},{2,0},{3,1},{4,6},{5,7},{6,4},{7,5},{8,10},{9,11},{10,... | collective-permute-start | bytes 393224 | tf_op jit(solution)/shard_map/ppermute | solution.py:591
  18.4 7.3 %collective-permute-start.8 = (bf16[512,128]{1,0:T(8,128)(2,1)S(1)}, bf16[512,128]{1,0:T(8,128)(2,1)S(1)}, u32[]{:S(2)}, u32[]{:S(2)}) collective-permute-start(bf16[512,128]{1,0:T(8,128)(2,1)S(1)} %collective-permute-done.4.refs_1_), channel_id=1, source_target_pairs={{0,8},{1,9},{2,10},{3,11},{4,12},{5,13},{6,14},{7,15},{8,0},{9,1},... | collective-permute-start | bytes 393224 | tf_op jit(solution)/shard_map/ppermute | solution.py:591
  18.5 7.2 %collective-permute-start.7 = (bf16[512,128]{1,0:T(8,128)(2,1)S(1)}, bf16[512,128]{1,0:T(8,128)(2,1)S(1)}, u32[]{:S(2)}, u32[]{:S(2)}) collective-permute-start(bf16[512,128]{1,0:T(8,128)(2,1)S(1)} %collective-permute-done.5.refs_0_), channel_id=1, source_target_pairs={{0,8},{1,9},{2,10},{3,11},{4,12},{5,13},{6,14},{7,15},{8,0},{9,1},... | collective-permute-start | bytes 393224 | tf_op jit(solution)/shard_map/ppermute | solution.py:591
  25.5 1.4 collective-permute-start.9
  37.2 4.7 %collective-permute-start.12 = (f32[3072]{0:T(1024)S(1)}, f32[3072]{0:T(1024)S(1)}, u32[]{:S(2)}, u32[]{:S(2)}) collective-permute-start(f32[3072]{0:T(1024)S(1)} %bitcast.71), channel_id=1, source_target_pairs={{0,17},{1,16},{2,19},{3,18},{4,21},{5,20},{6,23},{7,22},{8,25},{9,... | collective-permute-start | bytes 36872 | tf_op jit(solution)/shard_map/ppermute | solution.py:591
  37.3 4.6 %collective-permute-start.11 = (f32[3072]{0:T(1024)S(1)}, f32[3072]{0:T(1024)S(1)}, u32[]{:S(2)}, u32[]{:S(2)}) collective-permute-start(f32[3072]{0:T(1024)S(1)} %bitcast.72), channel_id=1, source_target_pairs={{0,16},{1,17},{2,18},{3,19},{4,20},{5,21},{6,22},{7,23},{8,24},{9,... | collective-permute-start | bytes 36872 | tf_op jit(solution)/shard_map/ppermute | solution.py:591
  37.3 5.1 %collective-permute-start.10 = (f32[3072]{0:T(1024)S(1)}, f32[3072]{0:T(1024)S(1)}, u32[]{:S(2)}, u32[]{:S(2)}) collective-permute-start(f32[3072]{0:T(1024)S(1)} %bitcast.73), channel_id=1, source_target_pairs={{0,1},{1,0},{2,3},{3,2},{4,5},{5,4},{6,7},{7,6},{8,9},{9,8},{10,11... | collective-permute-start | bytes 36872 | tf_op jit(solution)/shard_map/ppermute | solution.py:591
  74.9 1.3 collective-permute-start.13
  76.2 5.8 %collective-permute-start.16 = (f32[5120]{0:T(1024)S(1)}, f32[5120]{0:T(1024)S(1)}, u32[]{:S(2)}, u32[]{:S(2)}) collective-permute-start(f32[5120]{0:T(1024)S(1)} %bitcast.33), channel_id=1, source_target_pairs={{0,6},{1,7},{2,4},{3,5},{4,2},{5,3},{6,0},{7,1},{8,14},{9,15},{10,... | collective-permute-start | bytes 61448 | tf_op jit(solution)/shard_map/ppermute | solution.py:591
  79.0 4.7 %collective-permute-start.15 = (f32[5120]{0:T(1024)S(1)}, f32[5120]{0:T(1024)S(1)}, u32[]{:S(2)}, u32[]{:S(2)}) collective-permute-start(f32[5120]{0:T(1024)S(1)} %bitcast.34), channel_id=1, source_target_pairs={{0,4},{1,5},{2,6},{3,7},{4,0},{5,1},{6,2},{7,3},{8,12},{9,13},{10,... | collective-permute-start | bytes 61448 | tf_op jit(solution)/shard_map/ppermute | solution.py:591
  80.6 3.8 %collective-permute-start.14 = (f32[5120]{0:T(1024)S(1)}, f32[5120]{0:T(1024)S(1)}, u32[]{:S(2)}, u32[]{:S(2)}) collective-permute-start(f32[5120]{0:T(1024)S(1)} %bitcast.35), channel_id=1, source_target_pairs={{0,2},{1,3},{2,0},{3,1},{4,6},{5,7},{6,4},{7,5},{8,10},{9,11},{10,... | collective-permute-start | bytes 61448 | tf_op jit(solution)/shard_map/ppermute | solution.py:591
  88.2 4.6 %collective-permute-start.19 = (f32[2048]{0:T(1024)S(1)}, f32[2048]{0:T(1024)S(1)}, u32[]{:S(2)}, u32[]{:S(2)}) collective-permute-start(f32[2048]{0:T(1024)S(1)} %bitcast.57), channel_id=1, source_target_pairs={{0,17},{1,16},{2,19},{3,18},{4,21},{5,20},{6,23},{7,22},{8,25},{9,... | collective-permute-start | bytes 24584 | tf_op jit(solution)/shard_map/ppermute | solution.py:591
  89.1 3.7 %collective-permute-start.18 = (f32[2048]{0:T(1024)S(1)}, f32[2048]{0:T(1024)S(1)}, u32[]{:S(2)}, u32[]{:S(2)}) collective-permute-start(f32[2048]{0:T(1024)S(1)} %bitcast.58), channel_id=1, source_target_pairs={{0,16},{1,17},{2,18},{3,19},{4,20},{5,21},{6,22},{7,23},{8,24},{9,... | collective-permute-start | bytes 24584 | tf_op jit(solution)/shard_map/ppermute | solution.py:591
  89.9 3.7 %collective-permute-start.17 = (f32[2048]{0:T(1024)S(1)}, f32[2048]{0:T(1024)S(1)}, u32[]{:S(2)}, u32[]{:S(2)}) collective-permute-start(f32[2048]{0:T(1024)S(1)} %bitcast.59), channel_id=1, source_target_pairs={{0,1},{1,0},{2,3},{3,2},{4,5},{5,4},{6,7},{7,6},{8,9},{9,8},{10,11... | collective-permute-start | bytes 24584 | tf_op jit(solution)/shard_map/ppermute | solution.py:591
  96.4 1.2 collective-permute-start.20
  97.6 5.6 %collective-permute-start.23 = (f32[4096]{0:T(1024)S(1)}, f32[4096]{0:T(1024)S(1)}, u32[]{:S(2)}, u32[]{:S(2)}) collective-permute-start(f32[4096]{0:T(1024)S(1)} %bitcast.36), channel_id=1, source_target_pairs={{0,6},{1,7},{2,4},{3,5},{4,2},{5,3},{6,0},{7,1},{8,14},{9,15},{10,... | collective-permute-start | bytes 49160 | tf_op jit(solution)/shard_map/ppermute | solution.py:591
  100.3 4.6 %collective-permute-start.22 = (f32[4096]{0:T(1024)S(1)}, f32[4096]{0:T(1024)S(1)}, u32[]{:S(2)}, u32[]{:S(2)}) collective-permute-start(f32[4096]{0:T(1024)S(1)} %bitcast.37), channel_id=1, source_target_pairs={{0,4},{1,5},{2,6},{3,7},{4,0},{5,1},{6,2},{7,3},{8,12},{9,13},{10,... | collective-permute-start | bytes 49160 | tf_op jit(solution)/shard_map/ppermute | solution.py:591
  101.0 4.0 %collective-permute-start.21 = (f32[4096]{0:T(1024)S(1)}, f32[4096]{0:T(1024)S(1)}, u32[]{:S(2)}, u32[]{:S(2)}) collective-permute-start(f32[4096]{0:T(1024)S(1)} %bitcast.38), channel_id=1, source_target_pairs={{0,2},{1,3},{2,0},{3,1},{4,6},{5,7},{6,4},{7,5},{8,10},{9,11},{10,... | collective-permute-start | bytes 49160 | tf_op jit(solution)/shard_map/ppermute | solution.py:591
  108.8 4.6 %collective-permute-start.26 = (f32[2048]{0:T(1024)S(1)}, f32[2048]{0:T(1024)S(1)}, u32[]{:S(2)}, u32[]{:S(2)}) collective-permute-start(f32[2048]{0:T(1024)S(1)} %bitcast.39), channel_id=1, source_target_pairs={{0,17},{1,16},{2,19},{3,18},{4,21},{5,20},{6,23},{7,22},{8,25},{9,... | collective-permute-start | bytes 24584 | tf_op jit(solution)/shard_map/ppermute | solution.py:591
  110.4 3.7 %collective-permute-start.25 = (f32[2048]{0:T(1024)S(1)}, f32[2048]{0:T(1024)S(1)}, u32[]{:S(2)}, u32[]{:S(2)}) collective-permute-start(f32[2048]{0:T(1024)S(1)} %bitcast.40), channel_id=1, source_target_pairs={{0,16},{1,17},{2,18},{3,19},{4,20},{5,21},{6,22},{7,23},{8,24},{9,... | collective-permute-start | bytes 24584 | tf_op jit(solution)/shard_map/ppermute | solution.py:591
  112.3 3.7 %collective-permute-start.24 = (f32[2048]{0:T(1024)S(1)}, f32[2048]{0:T(1024)S(1)}, u32[]{:S(2)}, u32[]{:S(2)}) collective-permute-start(f32[2048]{0:T(1024)S(1)} %bitcast.41), channel_id=1, source_target_pairs={{0,1},{1,0},{2,3},{3,2},{4,5},{5,4},{6,7},{7,6},{8,9},{9,8},{10,11... | collective-permute-start | bytes 24584 | tf_op jit(solution)/shard_map/ppermute | solution.py:591
  118.3 1.2 collective-permute-start.27
  119.6 10.3 %collective-permute-start.30 = (f32[4096]{0:T(1024)S(1)}, f32[4096]{0:T(1024)S(1)}, u32[]{:S(2)}, u32[]{:S(2)}) collective-permute-start(f32[4096]{0:T(1024)S(1)} %bitcast.47), channel_id=1, source_target_pairs={{0,6},{1,7},{2,4},{3,5},{4,2},{5,3},{6,0},{7,1},{8,14},{9,15},{10,... | collective-permute-start | bytes 49160 | tf_op jit(solution)/shard_map/ppermute | solution.py:591
  121.1 8.8 %collective-permute-start.29 = (f32[4096]{0:T(1024)S(1)}, f32[4096]{0:T(1024)S(1)}, u32[]{:S(2)}, u32[]{:S(2)}) collective-permute-start(f32[4096]{0:T(1024)S(1)} %bitcast.48), channel_id=1, source_target_pairs={{0,4},{1,5},{2,6},{3,7},{4,0},{5,1},{6,2},{7,3},{8,12},{9,13},{10,... | collective-permute-start | bytes 49160 | tf_op jit(solution)/shard_map/ppermute | solution.py:591
  121.7 8.2 %collective-permute-start.28 = (f32[4096]{0:T(1024)S(1)}, f32[4096]{0:T(1024)S(1)}, u32[]{:S(2)}, u32[]{:S(2)}) collective-permute-start(f32[4096]{0:T(1024)S(1)} %bitcast.49), channel_id=1, source_target_pairs={{0,2},{1,3},{2,0},{3,1},{4,6},{5,7},{6,4},{7,5},{8,10},{9,11},{10,... | collective-permute-start | bytes 49160 | tf_op jit(solution)/shard_map/ppermute | solution.py:591
  129.8 2.4 %collective-permute-start.31 = (bf16[2048,128]{1,0:T(8,128)(2,1)S(1)}, bf16[2048,128]{1,0:T(8,128)(2,1)S(1)}, u32[]{:S(2)}, u32[]{:S(2)}) collective-permute-start(bf16[2048,128]{1,0:T(8,128)(2,1)S(1)} %get-tuple-element.74), channel_id=1, source_target_pairs={{0,8},{1,9},{2,10},{3,11},{4,12},{5,13},{6,14},{7,15},{8,0},{9,1},... | collective-permute-start | bytes 1572872 | tf_op jit(solution)/shard_map/ppermute | solution.py:591
  132.0 7.4 %collective-permute-start.33 = (bf16[512,128]{1,0:T(8,128)(2,1)S(1)}, bf16[512,128]{1,0:T(8,128)(2,1)S(1)}, u32[]{:S(2)}, u32[]{:S(2)}) collective-permute-start(bf16[512,128]{1,0:T(8,128)(2,1)S(1)} %get-tuple-element.84), channel_id=1, source_target_pairs={{0,17},{1,16},{2,19},{3,18},{4,21},{5,20},{6,23},{7,22},{8,25},{9,... | collective-permute-start | bytes 393224 | tf_op jit(solution)/shard_map/ppermute | solution.py:591
  132.3 8.0 %collective-permute-start.32 = (bf16[512,128]{1,0:T(8,128)(2,1)S(1)}, bf16[512,128]{1,0:T(8,128)(2,1)S(1)}, u32[]{:S(2)}, u32[]{:S(2)}) collective-permute-start(bf16[512,128]{1,0:T(8,128)(2,1)S(1)} %get-tuple-element.83), channel_id=1, source_target_pairs={{0,2},{1,3},{2,0},{3,1},{4,6},{5,7},{6,4},{7,5},{8,10},{9,11},{10,... | collective-permute-start | bytes 393224 | tf_op jit(solution)/shard_map/ppermute | solution.py:591
  132.8 12.9 %collective-permute-start.36 = (bf16[512,128]{1,0:T(8,128)(2,1)S(1)}, bf16[512,128]{1,0:T(8,128)(2,1)S(1)}, u32[]{:S(2)}, u32[]{:S(2)}) collective-permute-start(bf16[512,128]{1,0:T(8,128)(2,1)S(1)} %get-tuple-element.90), channel_id=1, source_target_pairs={{0,4},{1,5},{2,6},{3,7},{4,0},{5,1},{6,2},{7,3},{8,12},{9,13},{10,... | collective-permute-start | bytes 393224 | tf_op jit(solution)/shard_map/ppermute | solution.py:591
  134.8 10.9 %collective-permute-start.37 = (bf16[512,128]{1,0:T(8,128)(2,1)S(1)}, bf16[512,128]{1,0:T(8,128)(2,1)S(1)}, u32[]{:S(2)}, u32[]{:S(2)}) collective-permute-start(bf16[512,128]{1,0:T(8,128)(2,1)S(1)} %get-tuple-element.91), channel_id=1, source_target_pairs={{0,6},{1,7},{2,4},{3,5},{4,2},{5,3},{6,0},{7,1},{8,14},{9,15},{10,... | collective-permute-start | bytes 393224 | tf_op jit(solution)/shard_map/ppermute | solution.py:591
  140.3 5.4 %collective-permute-start.34 = (bf16[512,128]{1,0:T(8,128)(2,1)S(1)}, bf16[512,128]{1,0:T(8,128)(2,1)S(1)}, u32[]{:S(2)}, u32[]{:S(2)}) collective-permute-start(bf16[512,128]{1,0:T(8,128)(2,1)S(1)} %get-tuple-element.85), channel_id=1, source_target_pairs={{0,1},{1,0},{2,3},{3,2},{4,5},{5,4},{6,7},{7,6},{8,9},{9,8},{10,11... | collective-permute-start | bytes 393224 | tf_op jit(solution)/shard_map/ppermute | solution.py:591
  141.3 5.2 %collective-permute-start.35 = (bf16[512,128]{1,0:T(8,128)(2,1)S(1)}, bf16[512,128]{1,0:T(8,128)(2,1)S(1)}, u32[]{:S(2)}, u32[]{:S(2)}) collective-permute-start(bf16[512,128]{1,0:T(8,128)(2,1)S(1)} %get-tuple-element.86), channel_id=1, source_target_pairs={{0,16},{1,17},{2,18},{3,19},{4,20},{5,21},{6,22},{7,23},{8,24},{9,... | collective-permute-start | bytes 393224 | tf_op jit(solution)/shard_map/ppermute | solution.py:591

commit v13 on v12

--- a/solution.py
+++ b/solution.py
@@ -15,7 +15,7 @@
 CROSS = 2.0 * LOG2E / EPSILON
 NT = (((1,), (1,)), ((), ()))
 VMEM = pl.BlockSpec(memory_space=pltpu.VMEM)
-GROUP = 64
+GROUP = 16
 HEAVY = 32
 
 
@@ -397,13 +397,9 @@
     return high, (value - high.astype(jnp.float32)).astype(jnp.bfloat16)
 
 
-def column_grad_kernel(width, xt_ref, y_ref, e_ref, alpha_ref, first_ref, own_ref, sent_ref,
-                       bb_ref, cb_ref, xa_ref, s_ref, count_ref, acc_ref):
-    rows, cols = xt_ref.shape[1], y_ref.shape[0]
-    own = own_ref.shape[0]
-    spread(first_ref[...], s_ref, bb_ref)
+def put_xa(xt_ref, alpha_ref, xa_ref):
     place = lax.broadcasted_iota(jnp.int32, (128, 512), 0)
-    for at in range(0, rows, 512):
+    for at in range(0, xt_ref.shape[1], 512):
         alpha = alpha_ref[:, at:at + 512]
         high, low = high_low(xt_ref[:, at:at + 512].astype(jnp.float32) * alpha)
         first, second = high_low(alpha)
@@ -412,41 +408,64 @@
         xa_ref[:128, at:at + 512] = high
         xa_ref[128:, at:at + 512] = low.astype(jnp.bfloat16)
 
-    lower = lax.broadcasted_iota(jnp.int32, (128, width), 0) < 126
-    for at in range(0, cols, width):
-        got = jnp.dot(xa_ref[...], e_ref[:, at:at + width], preferred_element_type=jnp.float32)
-        acc_ref[:, at:at + width] = got[:128] + jnp.where(lower, got[128:], 0.0)
-        count_ref[:, at:at + width] = got[254:255] + got[255:256]
+
+def column_parts(blocks, share, xa_ref, y_ref, e_ref, first_ref, own_ref, sent_ref,
+                 bb_ref, cb_ref, s_ref, count_ref, acc_ref):
+    spread(jnp.concatenate([first_ref[:, at:at + share] for at in blocks], axis=1), s_ref, bb_ref)
+    lower = lax.broadcasted_iota(jnp.int32, (128, share), 0) < 126
+    for k, at in enumerate(blocks):
+        to = k * share
+        got = jnp.dot(xa_ref[...], e_ref[:, at:at + share], preferred_element_type=jnp.float32)
+        acc_ref[:, to:to + share] = got[:128] + jnp.where(lower, got[128:], 0.0)
+        count_ref[:, to:to + share] = got[254:255] + got[255:256]
     spread(count_ref[...], s_ref, cb_ref)
-    for at in range(0, cols, 128):
-        pulled = jnp.transpose(acc_ref[:, at:at + 128])
-        whole = cb_ref[at:at + 128, :] * y_ref[at:at + 128, :].astype(jnp.float32)
-        grad = bb_ref[at:at + 128, :] * (whole - pulled)
-        if at < own:
-            own_ref[at:at + 128, :] = grad
-        else:
-            sent_ref[at - own:at - own + 128, :] = grad.astype(jnp.bfloat16)
-
-
-def column_grad(xt, y, e, alpha, first, own, width=512):
-    rows, cols = xt.shape[1], y.shape[0]
-    return pl.pallas_call(
-        functools.partial(column_grad_kernel, width),
-        out_shape=(shape(own, D), shape(cols - own, D, dtype=jnp.bfloat16)),
-        in_specs=[VMEM] * 5,
-        out_specs=(VMEM,) * 2,
+    own = own_ref.shape[0]
+    for k, at in enumerate(blocks):
+        for q in range(0, share, 128):
+            to = k * share + q
+            pulled = jnp.transpose(acc_ref[:, to:to + 128])
+            whole = cb_ref[to:to + 128, :] * y_ref[at + q:at + q + 128, :].astype(jnp.float32)
+            grad = bb_ref[to:to + 128, :] * (whole - pulled)
+            if to < own:
+                own_ref[to:to + 128, :] = grad
+            else:
+                sent_ref[to - own:to - own + 128, :] = grad.astype(jnp.bfloat16)
+
+
+def first_columns_kernel(blocks, share, xt_ref, y_ref, e_ref, alpha_ref, first_ref, own_ref, sent_ref, xa_ref, *rest):
+    put_xa(xt_ref, alpha_ref, xa_ref)
+    column_parts(blocks, share, xa_ref, y_ref, e_ref, first_ref, own_ref, sent_ref, *rest)
+
+
+def columns_kernel(blocks, share, xa_ref, y_ref, e_ref, first_ref, own_ref, sent_ref, *rest):
+    column_parts(blocks, share, xa_ref, y_ref, e_ref, first_ref, own_ref, sent_ref, *rest)
+
+
+def column_grad(zs, nz, share, y, e, first, xt=None, alpha=None, xa=None):
+    rows, size = e.shape[0], 2 * len(zs) * share
+    blocks = [z * share for z in zs] + [(nz + z) * share for z in zs]
+    out_shape = [shape(size // 2, D), shape(size // 2, D, dtype=jnp.bfloat16)]
+    if xa is None:
+        kernel, args = first_columns_kernel, (xt, y, e, alpha, first)
+        out_shape.append(shape(256, rows, dtype=jnp.bfloat16))
+    else:
+        kernel, args = columns_kernel, (xa, y, e, first)
+    return pl.pallas_call(
+        functools.partial(kernel, blocks, share),
+        out_shape=out_shape,
+        in_specs=[VMEM] * len(args),
+        out_specs=[VMEM] * len(out_shape),
         scratch_shapes=[
-            pltpu.VMEM((cols, 128), jnp.float32),
-            pltpu.VMEM((cols, 128), jnp.float32),
-            pltpu.VMEM((256, rows), jnp.bfloat16),
-            pltpu.VMEM((cols // 128, 128), jnp.float32),
-            pltpu.VMEM((1, cols), jnp.float32),
-            pltpu.VMEM((128, cols), jnp.float32),
+            pltpu.VMEM((size, 128), jnp.float32),
+            pltpu.VMEM((size, 128), jnp.float32),
+            pltpu.VMEM((size // 128, 128), jnp.float32),
+            pltpu.VMEM((1, size), jnp.float32),
+            pltpu.VMEM((128, size), jnp.float32),
         ],
         compiler_params=pltpu.CompilerParams(vmem_limit_bytes=16 << 20),
-        cost_estimate=pl.CostEstimate(flops=4 * e.size * D, bytes_accessed=2 * e.size, transcendentals=0),
+        cost_estimate=pl.CostEstimate(flops=4 * rows * size * D, bytes_accessed=2 * rows * size, transcendentals=0),
         name="column_grad",
-    )(xt, y, e, alpha, first)
+    )(*args)
 
 
 def row_block(at, chunk, x_ref, e_ref, yb_ref, scale):
@@ -555,24 +574,21 @@
     )(scale, *rows, *columns)
 
 
-def shares_kernel(gc_ref, other_ref, own_ref, *outs):
-    share = own_ref.shape[0]
-    for k in range(len(outs) + 1):
+def shares_kernel(gc_ref, other_ref, *outs):
+    share = outs[0].shape[0]
+    for k, out_ref in enumerate(outs):
         at = k * share
         total = gc_ref[at:at + share, :] + other_ref[at:at + share, :].astype(jnp.float32)
-        if k == 0:
-            own_ref[...] = total
-        else:
-            outs[k - 1][...] = total.astype(jnp.bfloat16)
-
-
-def shares(gc, other, count):
-    share = gc.shape[0] // count
+        out_ref[...] = total.astype(out_ref.dtype)
+
+
+def shares(gc, other, dtypes):
+    share = gc.shape[0] // len(dtypes)
     return pl.pallas_call(
         shares_kernel,
-        out_shape=[shape(share, D)] + [shape(share, D, dtype=jnp.bfloat16)] * (count - 1),
+        out_shape=[shape(share, D, dtype=dtype) for dtype in dtypes],
         in_specs=[VMEM] * 2,
-        out_specs=[VMEM] * count,
+        out_specs=[VMEM] * len(dtypes),
         compiler_params=pltpu.CompilerParams(vmem_limit_bytes=16 << 20),
         name="shares",
     )(gc, other)
@@ -647,16 +663,22 @@
         part, alpha = lax.optimization_barrier((part, alpha))
         got = direct(part.reshape(-1), along)
 
-    gc, gc_send = column_grad(xt, y, e, alpha, first_beta, nz * share_y)
+    half = nz // 2
+    gc, gc_send, xa = column_grad(range(half, nz), nz, share_y, y, e, first_beta, xt=xt, alpha=alpha)
+    far_gc = shares(gc, swap(gc_send, core), [jnp.bfloat16] * (nz - half))
+    gc, gc_send = column_grad(range(half), nz, share_y, y, e, first_beta, xa=xa)
+    far_gc, alpha = lax.optimization_barrier((far_gc, alpha))
+    far_gc = [swap(part, along[half + z]) for z, part in enumerate(far_gc)]
     yb, scale, last = first_rows([na - 1], share_x, x, y, e, alpha, first_beta, mass_b, got, 2 * nz)
-    (grad_cam, *parts), yb = lax.optimization_barrier((shares(gc, swap(gc_send, core), nz), yb))
+    near_gc = shares(gc, swap(gc_send, core), [jnp.float32] + [jnp.bfloat16] * (half - 1))
+    (grad_cam, *parts), yb = lax.optimization_barrier((near_gc, yb))
     parts = [swap(part, along[z + 1]) for z, part in enumerate(parts)]
     last = swap(last, across[na - 1])
     sent = other_rows(list(range(1, na - 1)), share_x, x, yb, e, alpha, jnp.bfloat16)
     sent, parts[0], last = lax.optimization_barrier((sent, parts[0], last))
     sent = [swap(part, across[s + 1]) for s, part in enumerate(sent)] + [last]
     gi, = other_rows([0], share_x, x, yb, e, alpha, jnp.float32)
-    grad_imu, grad_cam = add_up([gi, *sent], [grad_cam, *parts], scale)
+    grad_imu, grad_cam = add_up([gi, *sent], [grad_cam, *parts, *far_gc], scale)
     return grad_imu, grad_cam[None]
 
 

time: 148 us -> 150 us (1.014)
  waiting for transfers between devices: 20.6 us -> 27.4 us
  starting transfers between devices: 42.7 us -> 39.6 us
  Pallas kernels: 81.6 us -> 79.9 us
    ppermute x38 -> x39, waiting for transfers between devices: 20.6 us -> 27.4 us  [swap(): lax.ppermute(value, ('row', 'col'), [(i, i ^ mask) for i in range(self.co...]
    ppermute x38 -> x39, starting transfers between devices: 42.7 us -> 39.6 us  [swap(): lax.ppermute(value, ('row', 'col'), [(i, i ^ mask) for i in range(self.co...]
    pallas_call x1, Pallas kernels: 32.5 us -> 30.3 us  [column_lse(): pl.pallas_call(functools.partial(column_lse_kernel, width, chunk, len(got...]
    pallas_call x2 -> x4, Pallas kernels: 5.85 us -> 6.27 us  [the longest x2 6.18 us: column_grad(): pl.pallas_call(functools.partial(kernel, blocks, share), out_shape=out_sh...]
  transfers between devices with their start and end apart: 38 -> 39, of which waited for: 19 -> 18; matrix products, arithmetic and copies ran while one was open for 1% -> 1% of each run, Pallas kernels for 17% -> 15%
where the time goes in v13:
time: 150 us
  Pallas kernels  79.9 us (53%)
  starting transfers between devices  39.6 us (26%)
  waiting for transfers between devices  27.4 us (18%)
    ppermute x39, starting transfers between devices, swap(): lax.ppermute(value, ('row', 'col'), [(i, i ^ mask) for i in range(self.co...  39.6 us
    pallas_call x1, Pallas kernels, column_lse(): pl.pallas_call(functools.partial(column_lse_kernel, width, chunk, len(got...  30.3 us
    ppermute x39, waiting for transfers between devices, swap(): lax.ppermute(value, ('row', 'col'), [(i, i ^ mask) for i in range(self.co...  27.4 us
    pallas_call x4, Pallas kernels, weighted(): pl.pallas_call(functools.partial(kernel, width, tuple(shifts), parts), ou...  12.7 us
    pallas_call x1, Pallas kernels, row_lse_late(): pl.pallas_call(functools.partial(row_lse_late_kernel, width, len(ys)), ou...  9.98 us
    pallas_call x1, Pallas kernels, row_lse_middle(): pl.pallas_call(functools.partial(row_lse_middle_kernel, width, len(ys)),...  6.7 us
    pallas_call x1, Pallas kernels, row_lse_early(): pl.pallas_call(functools.partial(row_lse_early_kernel, width, len(xs)), o...  6.69 us
    pallas_call x2, Pallas kernels, column_grad(): pl.pallas_call(functools.partial(kernel, blocks, share), out_shape=out_sh...  6.18 us
  transfers between devices with their start and end apart: 39, of which 18 were waited for; matrix products, arithmetic and copies ran while one was open for 1% of the time, Pallas kernels for 15%

profile of v13, /device:TPU:0, one launch (start us, length us, event | category | flops | bytes accessed | tf_op | source)
XLA Modules:
  0.0 149.7 jit_solution(4594182078192847489)
XLA Ops:
  0.6 3.0 %collective-permute-start = (bf16[512,128]{1,0:T(8,128)(2,1)}, bf16[512,128]{1,0:T(8,128)(2,1)S(1)}, u32[]{:S(2)}, u32[]{:S(2)}) collective-permute-start(bf16[512,128]{1,0:T(8,128)(2,1)} %param.4), channel_id=1, source_target_pairs={{0,1},{1,0},{2,3},{3,2},{4,5},{5,4},{6,7},{7,6},{8,9},{9,8},{10,11... | collective-permute-start | bytes 393224 | tf_op jit(solution)/shard_map/ppermute | solution.py:607
  3.7 1.4 collective-permute-start.2
  5.2 3.0 %collective-permute-start.4 = (bf16[512,128]{1,0:T(8,128)(2,1)}, bf16[512,128]{1,0:T(8,128)(2,1)S(1)}, u32[]{:S(2)}, u32[]{:S(2)}) collective-permute-start(bf16[512,128]{1,0:T(8,128)(2,1)} %bitcast.77), channel_id=1, source_target_pairs={{0,4},{1,5},{2,6},{3,7},{4,0},{5,1},{6,2},{7,3},{8,12},{9,13},{10,... | collective-permute-start | bytes 393224 | tf_op jit(solution)/shard_map/ppermute | solution.py:607
  8.2 1.0 pad_maximum_fusion.own_ref
  10.2 1.6 %collective-permute-start.5 = (bf16[512,128]{1,0:T(8,128)(2,1)}, bf16[512,128]{1,0:T(8,128)(2,1)S(1)}, u32[]{:S(2)}, u32[]{:S(2)}) collective-permute-start(bf16[512,128]{1,0:T(8,128)(2,1)} %bitcast.80), channel_id=1, source_target_pairs={{0,2},{1,3},{2,0},{3,1},{4,6},{5,7},{6,4},{7,5},{8,10},{9,11},{10,... | collective-permute-start | bytes 393224 | tf_op jit(solution)/shard_map/ppermute | solution.py:607
  11.8 6.7 %row_lse_early.1 = (bf16[2048,128]{1,0:T(8,128)(2,1)S(1)}, bf16[128,2048]{1,0:T(8,128)(2,1)S(1)}, f32[1,2048]{1,0:T(1,128)S(1)}) custom-call(bf16[1024,128]{1,0:T(8,128)(2,1)S(1)} %pad_maximum_fusion.own_ref, bf16[512,128]{1,0:T(8,128)(2,1)S(1)} %collective-permute-done.refs_0_, bf16[512,128]{1,0:T(8,128)(2,1)S(1)} %collective-permute-done.1.refs_1_, ...), custom_call_target="tpu_custom_call" | custom-call | flops 536870912 | bytes 786432 | tf_op jit(solution)/shard_map/row_lse_early/pallas_call | solution.py:323
  19.2 6.7 %row_lse_middle.1.first_ref = f32[1,2048]{1,0:T(1,128)S(1)} custom-call(bf16[2048,128]{1,0:T(8,128)(2,1)S(1)} %get-tuple-element.54.x_ref, f32[1,2048]{1,0:T(1,128)S(1)} %get-tuple-element.57.first_ref, bf16[512,128]{1,0:T(8,128)(2,1)S(1)} %collective-permute-done.5.refs_0_, bf16[512,128]{1,0:T(8,128)(2,1)S(1)} %collective-permute-done.4.refs_1_), custom_call_target="tpu_custom_call" | custom-call | flops 536870912 | bytes 786432 | tf_op jit(solution)/shard_map/row_lse_middle/pallas_call | solution.py:338
  26.1 1.3 collective-permute-done.9.refs_6_
  27.3 10.0 %row_lse_late.1 = (bf16[4096,128]{1,0:T(8,128)(2,1)S(1)}, f32[1,3072]{1,0:T(1,128)S(1)}) custom-call(bf16[1024,128]{1,0:T(8,128)(2,1)S(1)} %pad_maximum_fusion.own_ref, f32[1,2048]{1,0:T(1,128)S(1)} %bitcast.66, bf16[2048,128]{1,0:T(8,128)(2,1)S(1)} %get-tuple-element.54.x_ref, f32[1,2048]{1,0:T(1,128)S(1)} %row_lse_middle.1.first_ref, ...), custom_call_target="tpu_custom_call" | custom-call | flops 1073741824 | bytes 1048576 | tf_op jit(solution)/shard_map/row_lse_late/pallas_call | solution.py:357
  37.5 3.4 %collective-permute-start.10 = (f32[3072]{0:T(1024)S(1)}, f32[3072]{0:T(1024)S(1)}, u32[]{:S(2)}, u32[]{:S(2)}) collective-permute-start(f32[3072]{0:T(1024)S(1)} %bitcast.73), channel_id=1, source_target_pairs={{0,1},{1,0},{2,3},{3,2},{4,5},{5,4},{6,7},{7,6},{8,9},{9,8},{10,11... | collective-permute-start | bytes 36872 | tf_op jit(solution)/shard_map/ppermute | solution.py:607
  40.9 1.1 collective-permute-done.12
  42.5 30.3 %column_lse.1 = (f32[1,5120]{1,0:T(1,128)S(1)}, bf16[2048,4096]{1,0:T(8,128)(2,1)S(1)}, f32[1,4096]{1,0:T(1,128)S(1)}, f32[1,2048]{1,0:T(1,128)S(1)}) custom-call(bf16[2048,128]{1,0:T(8,128)(2,1)S(1)} %get-tuple-element.54.x_ref, bf16[4096,128]{1,0:T(8,128)(2,1)S(1)} %get-tuple-element.61.y_ref, f32[1,2048]{1,0:T(1,128)S(1)} %bitcast.67, ...), custom_call_target="tpu_custom_call" | custom-call | flops 2147483648 | bytes 1572864 | tf_op jit(solution)/shard_map/column_lse/pallas_call | solution.py:371
  73.0 1.2 collective-permute-done.13
  74.2 2.7 %collective-permute-start.16 = (f32[5120]{0:T(1024)S(1)}, f32[5120]{0:T(1024)S(1)}, u32[]{:S(2)}, u32[]{:S(2)}) collective-permute-start(f32[5120]{0:T(1024)S(1)} %bitcast.33), channel_id=1, source_target_pairs={{0,6},{1,7},{2,4},{3,5},{4,2},{5,3},{6,0},{7,1},{8,14},{9,15},{10,... | collective-permute-start | bytes 61448 | tf_op jit(solution)/shard_map/ppermute | solution.py:607
  76.9 1.6 %collective-permute-start.15 = (f32[5120]{0:T(1024)S(1)}, f32[5120]{0:T(1024)S(1)}, u32[]{:S(2)}, u32[]{:S(2)}) collective-permute-start(f32[5120]{0:T(1024)S(1)} %bitcast.34), channel_id=1, source_target_pairs={{0,4},{1,5},{2,6},{3,7},{4,0},{5,1},{6,2},{7,3},{8,12},{9,13},{10,... | collective-permute-start | bytes 61448 | tf_op jit(solution)/shard_map/ppermute | solution.py:607
  79.1 0.9 collective-permute-done.16
  79.9 1.7 %collective-permute-done.15 = f32[5120]{0:T(1024)S(1)} collective-permute-done((f32[5120]{0:T(1024)S(1)}, f32[5120]{0:T(1024)S(1)}, u32[]{:S(2)}, u32[]{:S(2)}) %collective-permute-start.15) | collective-permute-done | bytes 20512 | tf_op jit(solution)/shard_map/ppermute | solution.py:607
  82.4 3.8 %weighted_sum.4 = (f32[1,2048]{1,0:T(1,128)S(1)}, f32[1,4096]{1,0:T(1,128)S(1)}, f32[1,4096]{1,0:T(1,128)S(1)}) custom-call(bf16[2048,4096]{1,0:T(8,128)(2,1)S(1)} %get-tuple-element.63.e_ref, f32[1,4096]{1,0:T(1,128)S(1)} %get-tuple-element.66.shift_ref, f32[1,5120]{1,0:T(1,128)S(1)} %pair.3.refs_0_, f32[1,5120]{1,0:T(1,128)S(1)} %bitcast.44, ...), custom_call_target="tpu_custom_call" | custom-call | flops 16777216 | bytes 16777216 | tf_op jit(solution)/shard_map/weighted_sum/pallas_call | solution.py:292
  87.0 0.9 collective-permute-start.18
  87.9 1.9 %collective-permute-start.17 = (f32[2048]{0:T(1024)S(1)}, f32[2048]{0:T(1024)S(1)}, u32[]{:S(2)}, u32[]{:S(2)}) collective-permute-start(f32[2048]{0:T(1024)S(1)} %bitcast.59), channel_id=1, source_target_pairs={{0,1},{1,0},{2,3},{3,2},{4,5},{5,4},{6,7},{7,6},{8,9},{9,8},{10,11... | collective-permute-start | bytes 24584 | tf_op jit(solution)/shard_map/ppermute | solution.py:607
  89.7 1.1 collective-permute-done.19
  91.5 2.8 %weighted_sum.5 = (f32[1,4096]{1,0:T(1,128)S(1)}, f32[1,2048]{1,0:T(1,128)}) custom-call(bf16[2048,4096]{1,0:T(8,128)(2,1)S(1)} %get-tuple-element.63.e_ref, f32[1,2048]{1,0:T(1,128)S(1)} %get-tuple-element.65.a_ref, f32[1,4096]{1,0:T(1,128)S(1)} %get-tuple-element.68.first_ref, f32[1,2048]{1,0:T(1,128)S(1)} %get-tuple-element.70.refs_0_, ...), custom_call_target="tpu_custom_call" | custom-call | flops 16777216 | bytes 16777216 | tf_op jit(solution)/shard_map/weighted_sum/pallas_call | solution.py:292
  94.3 1.2 collective-permute-done.20
  95.5 2.7 %collective-permute-start.23 = (f32[4096]{0:T(1024)S(1)}, f32[4096]{0:T(1024)S(1)}, u32[]{:S(2)}, u32[]{:S(2)}) collective-permute-start(f32[4096]{0:T(1024)S(1)} %bitcast.36), channel_id=1, source_target_pairs={{0,6},{1,7},{2,4},{3,5},{4,2},{5,3},{6,0},{7,1},{8,14},{9,15},{10,... | collective-permute-start | bytes 49160 | tf_op jit(solution)/shard_map/ppermute | solution.py:607
  98.9 1.0 collective-permute-start.21
  100.0 1.1 collective-permute-done.23
  101.1 1.8 %collective-permute-done.22 = f32[4096]{0:T(1024)S(1)} collective-permute-done((f32[4096]{0:T(1024)S(1)}, f32[4096]{0:T(1024)S(1)}, u32[]{:S(2)}, u32[]{:S(2)}) %collective-permute-start.22) | collective-permute-done | bytes 16416 | tf_op jit(solution)/shard_map/ppermute | solution.py:607
  102.9 3.8 %weighted_sum.6.refs_0_ = f32[1,2048]{1,0:T(1,128)S(1)} custom-call(bf16[2048,4096]{1,0:T(8,128)(2,1)S(1)} %get-tuple-element.63.e_ref, f32[1,4096]{1,0:T(1,128)S(1)} %get-tuple-element.68.first_ref, f32[1,4096]{1,0:T(1,128)S(1)} %get-tuple-element.69.b_ref, f32[1,4096]{1,0:T(1,128)S(1)} %pair.4.refs_0_, f32[1,4096]{1,0:T(1,128)S(1)} %bitcast.56, ...), custom_call_target="tpu_custom_call" | custom-call | flops 16777216 | bytes 16777216 | tf_op jit(solution)/shard_map/weighted_sum/pallas_call | solution.py:292
  106.7 1.6 %collective-permute-start.26 = (f32[2048]{0:T(1024)S(1)}, f32[2048]{0:T(1024)S(1)}, u32[]{:S(2)}, u32[]{:S(2)}) collective-permute-start(f32[2048]{0:T(1024)S(1)} %bitcast.39), channel_id=1, source_target_pairs={{0,17},{1,16},{2,19},{3,18},{4,21},{5,20},{6,23},{7,22},{8,25},{9,... | collective-permute-start | bytes 24584 | tf_op jit(solution)/shard_map/ppermute | solution.py:607
  108.3 2.0 %collective-permute-start.25 = (f32[2048]{0:T(1024)S(1)}, f32[2048]{0:T(1024)S(1)}, u32[]{:S(2)}, u32[]{:S(2)}) collective-permute-start(f32[2048]{0:T(1024)S(1)} %bitcast.40), channel_id=1, source_target_pairs={{0,16},{1,17},{2,18},{3,19},{4,20},{5,21},{6,22},{7,23},{8,24},{9,... | collective-permute-start | bytes 24584 | tf_op jit(solution)/shard_map/ppermute | solution.py:607
  110.3 1.1 collective-permute-done.26
  112.0 1.9 %collective-permute-done.24 = f32[2048]{0:T(1024)S(1)} collective-permute-done((f32[2048]{0:T(1024)S(1)}, f32[2048]{0:T(1024)S(1)}, u32[]{:S(2)}, u32[]{:S(2)}) %collective-permute-start.24) | collective-permute-done | bytes 8224 | tf_op jit(solution)/shard_map/ppermute | solution.py:607
  113.9 2.3 %weighted_sum.7 = (f32[1,4096]{1,0:T(1,128)S(1)}, f32[1,2048]{1,0:T(1,128)S(1)}) custom-call(bf16[2048,4096]{1,0:T(8,128)(2,1)S(1)} %get-tuple-element.63.e_ref, f32[1,2048]{1,0:T(1,128)S(1)} %get-tuple-element.65.a_ref, f32[1,4096]{1,0:T(1,128)S(1)} %get-tuple-element.68.first_ref, f32[1,2048]{1,0:T(1,128)S(1)} %weighted_sum.6.refs_0_, ...), custom_call_target="tpu_custom_call" | custom-call | flops 16777216 | bytes 16777216 | tf_op jit(solution)/shard_map/weighted_sum/pallas_call | solution.py:292
  116.3 1.2 collective-permute-done.27
  117.5 3.2 %column_grad.2 = (f32[1024,128]{1,0:T(8,128)S(1)}, bf16[1024,128]{1,0:T(8,128)(2,1)S(1)}, bf16[256,2048]{1,0:T(8,128)(2,1)S(1)}) custom-call(bf16[128,2048]{1,0:T(8,128)(2,1)S(1)} %get-tuple-element.64.xt_ref, bf16[4096,128]{1,0:T(8,128)(2,1)S(1)} %get-tuple-element.61.y_ref, bf16[2048,4096]{1,0:T(8,128)(2,1)S(1)} %get-tuple-element.63.e_ref, ...), custom_call_target="tpu_custom_call" | custom-call | flops 2147483648 | bytes 8388608 | tf_op jit(solution)/shard_map/column_grad/pallas_call | solution.py:453
  121.0 1.5 collective-permute-start.31
  123.1 2.3 %collective-permute-start.29 = (f32[4096]{0:T(1024)S(1)}, f32[4096]{0:T(1024)S(1)}, u32[]{:S(2)}, u32[]{:S(2)}) collective-permute-start(f32[4096]{0:T(1024)S(1)} %bitcast.49), channel_id=1, source_target_pairs={{0,2},{1,3},{2,0},{3,1},{4,6},{5,7},{6,4},{7,5},{8,10},{9,11},{10,... | collective-permute-start | bytes 49160 | tf_op jit(solution)/shard_map/ppermute | solution.py:607
  125.4 3.0 %column_grad.3 = (f32[1024,128]{1,0:T(8,128)S(1)}, bf16[1024,128]{1,0:T(8,128)(2,1)S(1)}) custom-call(bf16[256,2048]{1,0:T(8,128)(2,1)S(1)} %get-tuple-element.82.xa_ref, bf16[4096,128]{1,0:T(8,128)(2,1)S(1)} %get-tuple-element.61.y_ref, bf16[2048,4096]{1,0:T(8,128)(2,1)S(1)} %get-tuple-element.63.e_ref, f32[1,4096]{1,0:T(1,128)S(1)} %get-tuple-element.68.first_ref), custom_call_target="tpu_custom_call" | custom-call | flops 2147483648 | bytes 8388608 | tf_op jit(solution)/shard_map/column_grad/pallas_call | solution.py:453
  128.5 1.2 collective-permute-start.37
  129.7 1.2 collective-permute-start.38
  130.9 2.0 %first_rows.1 = (bf16[4096,256]{1,0:T(8,128)(2,1)S(1)}, f32[1,512]{1,0:T(1,128)S(1)}, bf16[512,128]{1,0:T(8,128)(2,1)S(1)}) custom-call(bf16[2048,128]{1,0:T(8,128)(2,1)S(1)} %get-tuple-element.54.x_ref, bf16[4096,128]{1,0:T(8,128)(2,1)S(1)} %get-tuple-element.61.y_ref, bf16[2048,4096]{1,0:T(8,128)(2,1)S(1)} %get-tuple-element.63.e_ref, ...), custom_call_target="tpu_custom_call" | custom-call | flops 34359738368 | bytes 134217728 | tf_op jit(solution)/shard_map/first_rows/pallas_call | solution.py:527
  133.0 1.2 collective-permute-start.33
  134.3 2.6 %other_rows.3 = (bf16[512,128]{1,0:T(8,128)(2,1)S(1)}, bf16[512,128]{1,0:T(8,128)(2,1)S(1)}) custom-call(bf16[2048,128]{1,0:T(8,128)(2,1)S(1)} %get-tuple-element.54.x_ref, bf16[4096,256]{1,0:T(8,128)(2,1)S(1)} %get-tuple-element.88.yb_ref, bf16[2048,4096]{1,0:T(8,128)(2,1)S(1)} %get-tuple-element.63.e_ref, f32[1,2048]{1,0:T(1,128)S(1)} %get-tuple-element.79.alpha_ref), custom_call_target="tpu_custom_call" | custom-call | flops 2147483648 | bytes 8388608 | tf_op jit(solution)/shard_map/other_rows/pallas_call | solution.py:545
  136.9 6.3 %collective-permute-done.33.refs_5_ = bf16[512,128]{1,0:T(8,128)(2,1)S(1)} collective-permute-done((bf16[512,128]{1,0:T(8,128)(2,1)S(1)}, bf16[512,128]{1,0:T(8,128)(2,1)S(1)}, u32[]{:S(2)}, u32[]{:S(2)}) %collective-permute-start.33) | collective-permute-done | bytes 131104 | tf_op jit(solution)/shard_map/ppermute | solution.py:607
  143.2 1.0 collective-permute-start.36
  144.2 1.4 other_rows.2.refs_0_
  145.7 2.9 %collective-permute-done.35.refs_1_ = bf16[512,128]{1,0:T(8,128)(2,1)S(1)} collective-permute-done((bf16[512,128]{1,0:T(8,128)(2,1)S(1)}, bf16[512,128]{1,0:T(8,128)(2,1)S(1)}, u32[]{:S(2)}, u32[]{:S(2)}) %collective-permute-start.35) | collective-permute-done | bytes 131104 | tf_op jit(solution)/shard_map/ppermute | solution.py:607
  148.6 1.1 add_up.1
  (52 shorter events, 8.1 us)
Async XLA Ops:
  0.6 9.5 %collective-permute-start = (bf16[512,128]{1,0:T(8,128)(2,1)}, bf16[512,128]{1,0:T(8,128)(2,1)S(1)}, u32[]{:S(2)}, u32[]{:S(2)}) collective-permute-start(bf16[512,128]{1,0:T(8,128)(2,1)} %param.4), channel_id=1, source_target_pairs={{0,1},{1,0},{2,3},{3,2},{4,5},{5,4},{6,7},{7,6},{8,9},{9,8},{10,11... | collective-permute-start | bytes 393224 | tf_op jit(solution)/shard_map/ppermute | solution.py:607
  3.7 8.2 %collective-permute-start.2 = (bf16[512,128]{1,0:T(8,128)(2,1)}, bf16[512,128]{1,0:T(8,128)(2,1)S(1)}, u32[]{:S(2)}, u32[]{:S(2)}) collective-permute-start(bf16[512,128]{1,0:T(8,128)(2,1)} %param.4), channel_id=1, source_target_pairs={{0,17},{1,16},{2,19},{3,18},{4,21},{5,20},{6,23},{7,22},{8,25},{9,... | collective-permute-start | bytes 393224 | tf_op jit(solution)/shard_map/ppermute | solution.py:607
  5.1 6.7 %collective-permute-start.1 = (bf16[512,128]{1,0:T(8,128)(2,1)}, bf16[512,128]{1,0:T(8,128)(2,1)S(1)}, u32[]{:S(2)}, u32[]{:S(2)}) collective-permute-start(bf16[512,128]{1,0:T(8,128)(2,1)} %param.4), channel_id=1, source_target_pairs={{0,16},{1,17},{2,18},{3,19},{4,20},{5,21},{6,22},{7,23},{8,24},{9,... | collective-permute-start | bytes 393224 | tf_op jit(solution)/shard_map/ppermute | solution.py:607
  5.2 13.3 %collective-permute-start.4 = (bf16[512,128]{1,0:T(8,128)(2,1)}, bf16[512,128]{1,0:T(8,128)(2,1)S(1)}, u32[]{:S(2)}, u32[]{:S(2)}) collective-permute-start(bf16[512,128]{1,0:T(8,128)(2,1)} %bitcast.77), channel_id=1, source_target_pairs={{0,4},{1,5},{2,6},{3,7},{4,0},{5,1},{6,2},{7,3},{8,12},{9,13},{10,... | collective-permute-start | bytes 393224 | tf_op jit(solution)/shard_map/ppermute | solution.py:607
  9.2 2.6 %collective-permute-start.3 = (bf16[512,128]{1,0:T(8,128)(2,1)}, bf16[512,128]{1,0:T(8,128)(2,1)S(1)}, u32[]{:S(2)}, u32[]{:S(2)}) collective-permute-start(bf16[512,128]{1,0:T(8,128)(2,1)} %bitcast.79), channel_id=1, source_target_pairs={{0,8},{1,9},{2,10},{3,11},{4,12},{5,13},{6,14},{7,15},{8,0},{9,1},... | collective-permute-start | bytes 393224 | tf_op jit(solution)/shard_map/ppermute | solution.py:607
  10.2 8.5 %collective-permute-start.5 = (bf16[512,128]{1,0:T(8,128)(2,1)}, bf16[512,128]{1,0:T(8,128)(2,1)S(1)}, u32[]{:S(2)}, u32[]{:S(2)}) collective-permute-start(bf16[512,128]{1,0:T(8,128)(2,1)} %bitcast.80), channel_id=1, source_target_pairs={{0,2},{1,3},{2,0},{3,1},{4,6},{5,7},{6,4},{7,5},{8,10},{9,11},{10,... | collective-permute-start | bytes 393224 | tf_op jit(solution)/shard_map/ppermute | solution.py:607
  18.5 7.4 %collective-permute-start.6 = (bf16[512,128]{1,0:T(8,128)(2,1)S(1)}, bf16[512,128]{1,0:T(8,128)(2,1)S(1)}, u32[]{:S(2)}, u32[]{:S(2)}) collective-permute-start(bf16[512,128]{1,0:T(8,128)(2,1)S(1)} %collective-permute-done.4.refs_1_), channel_id=1, source_target_pairs={{0,2},{1,3},{2,0},{3,1},{4,6},{5,7},{6,4},{7,5},{8,10},{9,11},{10,... | collective-permute-start | bytes 393224 | tf_op jit(solution)/shard_map/ppermute | solution.py:607
  18.6 7.4 %collective-permute-start.8 = (bf16[512,128]{1,0:T(8,128)(2,1)S(1)}, bf16[512,128]{1,0:T(8,128)(2,1)S(1)}, u32[]{:S(2)}, u32[]{:S(2)}) collective-permute-start(bf16[512,128]{1,0:T(8,128)(2,1)S(1)} %collective-permute-done.4.refs_1_), channel_id=1, source_target_pairs={{0,8},{1,9},{2,10},{3,11},{4,12},{5,13},{6,14},{7,15},{8,0},{9,1},... | collective-permute-start | bytes 393224 | tf_op jit(solution)/shard_map/ppermute | solution.py:607
  18.7 7.4 %collective-permute-start.7 = (bf16[512,128]{1,0:T(8,128)(2,1)S(1)}, bf16[512,128]{1,0:T(8,128)(2,1)S(1)}, u32[]{:S(2)}, u32[]{:S(2)}) collective-permute-start(bf16[512,128]{1,0:T(8,128)(2,1)S(1)} %collective-permute-done.5.refs_0_), channel_id=1, source_target_pairs={{0,8},{1,9},{2,10},{3,11},{4,12},{5,13},{6,14},{7,15},{8,0},{9,1},... | collective-permute-start | bytes 393224 | tf_op jit(solution)/shard_map/ppermute | solution.py:607
  25.9 1.4 collective-permute-start.9
  37.3 4.7 %collective-permute-start.12 = (f32[3072]{0:T(1024)S(1)}, f32[3072]{0:T(1024)S(1)}, u32[]{:S(2)}, u32[]{:S(2)}) collective-permute-start(f32[3072]{0:T(1024)S(1)} %bitcast.71), channel_id=1, source_target_pairs={{0,17},{1,16},{2,19},{3,18},{4,21},{5,20},{6,23},{7,22},{8,25},{9,... | collective-permute-start | bytes 36872 | tf_op jit(solution)/shard_map/ppermute | solution.py:607
  37.4 4.6 %collective-permute-start.11 = (f32[3072]{0:T(1024)S(1)}, f32[3072]{0:T(1024)S(1)}, u32[]{:S(2)}, u32[]{:S(2)}) collective-permute-start(f32[3072]{0:T(1024)S(1)} %bitcast.72), channel_id=1, source_target_pairs={{0,16},{1,17},{2,18},{3,19},{4,20},{5,21},{6,22},{7,23},{8,24},{9,... | collective-permute-start | bytes 36872 | tf_op jit(solution)/shard_map/ppermute | solution.py:607
  37.5 5.1 %collective-permute-start.10 = (f32[3072]{0:T(1024)S(1)}, f32[3072]{0:T(1024)S(1)}, u32[]{:S(2)}, u32[]{:S(2)}) collective-permute-start(f32[3072]{0:T(1024)S(1)} %bitcast.73), channel_id=1, source_target_pairs={{0,1},{1,0},{2,3},{3,2},{4,5},{5,4},{6,7},{7,6},{8,9},{9,8},{10,11... | collective-permute-start | bytes 36872 | tf_op jit(solution)/shard_map/ppermute | solution.py:607
  72.9 1.3 collective-permute-start.13
  74.2 5.8 %collective-permute-start.16 = (f32[5120]{0:T(1024)S(1)}, f32[5120]{0:T(1024)S(1)}, u32[]{:S(2)}, u32[]{:S(2)}) collective-permute-start(f32[5120]{0:T(1024)S(1)} %bitcast.33), channel_id=1, source_target_pairs={{0,6},{1,7},{2,4},{3,5},{4,2},{5,3},{6,0},{7,1},{8,14},{9,15},{10,... | collective-permute-start | bytes 61448 | tf_op jit(solution)/shard_map/ppermute | solution.py:607
  76.9 4.7 %collective-permute-start.15 = (f32[5120]{0:T(1024)S(1)}, f32[5120]{0:T(1024)S(1)}, u32[]{:S(2)}, u32[]{:S(2)}) collective-permute-start(f32[5120]{0:T(1024)S(1)} %bitcast.34), channel_id=1, source_target_pairs={{0,4},{1,5},{2,6},{3,7},{4,0},{5,1},{6,2},{7,3},{8,12},{9,13},{10,... | collective-permute-start | bytes 61448 | tf_op jit(solution)/shard_map/ppermute | solution.py:607
  78.6 3.8 %collective-permute-start.14 = (f32[5120]{0:T(1024)S(1)}, f32[5120]{0:T(1024)S(1)}, u32[]{:S(2)}, u32[]{:S(2)}) collective-permute-start(f32[5120]{0:T(1024)S(1)} %bitcast.35), channel_id=1, source_target_pairs={{0,2},{1,3},{2,0},{3,1},{4,6},{5,7},{6,4},{7,5},{8,10},{9,11},{10,... | collective-permute-start | bytes 61448 | tf_op jit(solution)/shard_map/ppermute | solution.py:607
  86.2 4.6 %collective-permute-start.19 = (f32[2048]{0:T(1024)S(1)}, f32[2048]{0:T(1024)S(1)}, u32[]{:S(2)}, u32[]{:S(2)}) collective-permute-start(f32[2048]{0:T(1024)S(1)} %bitcast.57), channel_id=1, source_target_pairs={{0,17},{1,16},{2,19},{3,18},{4,21},{5,20},{6,23},{7,22},{8,25},{9,... | collective-permute-start | bytes 24584 | tf_op jit(solution)/shard_map/ppermute | solution.py:607
  87.0 3.8 %collective-permute-start.18 = (f32[2048]{0:T(1024)S(1)}, f32[2048]{0:T(1024)S(1)}, u32[]{:S(2)}, u32[]{:S(2)}) collective-permute-start(f32[2048]{0:T(1024)S(1)} %bitcast.58), channel_id=1, source_target_pairs={{0,16},{1,17},{2,18},{3,19},{4,20},{5,21},{6,22},{7,23},{8,24},{9,... | collective-permute-start | bytes 24584 | tf_op jit(solution)/shard_map/ppermute | solution.py:607
  87.9 3.7 %collective-permute-start.17 = (f32[2048]{0:T(1024)S(1)}, f32[2048]{0:T(1024)S(1)}, u32[]{:S(2)}, u32[]{:S(2)}) collective-permute-start(f32[2048]{0:T(1024)S(1)} %bitcast.59), channel_id=1, source_target_pairs={{0,1},{1,0},{2,3},{3,2},{4,5},{5,4},{6,7},{7,6},{8,9},{9,8},{10,11... | collective-permute-start | bytes 24584 | tf_op jit(solution)/shard_map/ppermute | solution.py:607
  94.3 1.2 collective-permute-start.20
  95.5 5.6 %collective-permute-start.23 = (f32[4096]{0:T(1024)S(1)}, f32[4096]{0:T(1024)S(1)}, u32[]{:S(2)}, u32[]{:S(2)}) collective-permute-start(f32[4096]{0:T(1024)S(1)} %bitcast.36), channel_id=1, source_target_pairs={{0,6},{1,7},{2,4},{3,5},{4,2},{5,3},{6,0},{7,1},{8,14},{9,15},{10,... | collective-permute-start | bytes 49160 | tf_op jit(solution)/shard_map/ppermute | solution.py:607
  98.2 4.6 %collective-permute-start.22 = (f32[4096]{0:T(1024)S(1)}, f32[4096]{0:T(1024)S(1)}, u32[]{:S(2)}, u32[]{:S(2)}) collective-permute-start(f32[4096]{0:T(1024)S(1)} %bitcast.37), channel_id=1, source_target_pairs={{0,4},{1,5},{2,6},{3,7},{4,0},{5,1},{6,2},{7,3},{8,12},{9,13},{10,... | collective-permute-start | bytes 49160 | tf_op jit(solution)/shard_map/ppermute | solution.py:607
  98.9 3.9 %collective-permute-start.21 = (f32[4096]{0:T(1024)S(1)}, f32[4096]{0:T(1024)S(1)}, u32[]{:S(2)}, u32[]{:S(2)}) collective-permute-start(f32[4096]{0:T(1024)S(1)} %bitcast.38), channel_id=1, source_target_pairs={{0,2},{1,3},{2,0},{3,1},{4,6},{5,7},{6,4},{7,5},{8,10},{9,11},{10,... | collective-permute-start | bytes 49160 | tf_op jit(solution)/shard_map/ppermute | solution.py:607
  106.7 4.6 %collective-permute-start.26 = (f32[2048]{0:T(1024)S(1)}, f32[2048]{0:T(1024)S(1)}, u32[]{:S(2)}, u32[]{:S(2)}) collective-permute-start(f32[2048]{0:T(1024)S(1)} %bitcast.39), channel_id=1, source_target_pairs={{0,17},{1,16},{2,19},{3,18},{4,21},{5,20},{6,23},{7,22},{8,25},{9,... | collective-permute-start | bytes 24584 | tf_op jit(solution)/shard_map/ppermute | solution.py:607
  108.3 3.7 %collective-permute-start.25 = (f32[2048]{0:T(1024)S(1)}, f32[2048]{0:T(1024)S(1)}, u32[]{:S(2)}, u32[]{:S(2)}) collective-permute-start(f32[2048]{0:T(1024)S(1)} %bitcast.40), channel_id=1, source_target_pairs={{0,16},{1,17},{2,18},{3,19},{4,20},{5,21},{6,22},{7,23},{8,24},{9,... | collective-permute-start | bytes 24584 | tf_op jit(solution)/shard_map/ppermute | solution.py:607
  110.3 3.7 %collective-permute-start.24 = (f32[2048]{0:T(1024)S(1)}, f32[2048]{0:T(1024)S(1)}, u32[]{:S(2)}, u32[]{:S(2)}) collective-permute-start(f32[2048]{0:T(1024)S(1)} %bitcast.41), channel_id=1, source_target_pairs={{0,1},{1,0},{2,3},{3,2},{4,5},{5,4},{6,7},{7,6},{8,9},{9,8},{10,11... | collective-permute-start | bytes 24584 | tf_op jit(solution)/shard_map/ppermute | solution.py:607
  116.3 1.2 collective-permute-start.27
  120.7 7.7 %collective-permute-start.28 = (bf16[1024,128]{1,0:T(8,128)(2,1)S(1)}, bf16[1024,128]{1,0:T(8,128)(2,1)S(1)}, u32[]{:S(2)}, u32[]{:S(2)}) collective-permute-start(bf16[1024,128]{1,0:T(8,128)(2,1)S(1)} %get-tuple-element.76), channel_id=1, source_target_pairs={{0,8},{1,9},{2,10},{3,11},{4,12},{5,13},{6,14},{7,15},{8,0},{9,1},... | collective-permute-start | bytes 786440 | tf_op jit(solution)/shard_map/ppermute | solution.py:607
  121.0 8.7 %collective-permute-start.31 = (f32[4096]{0:T(1024)S(1)}, f32[4096]{0:T(1024)S(1)}, u32[]{:S(2)}, u32[]{:S(2)}) collective-permute-start(f32[4096]{0:T(1024)S(1)} %bitcast.47), channel_id=1, source_target_pairs={{0,6},{1,7},{2,4},{3,5},{4,2},{5,3},{6,0},{7,1},{8,14},{9,15},{10,... | collective-permute-start | bytes 49160 | tf_op jit(solution)/shard_map/ppermute | solution.py:607
  122.4 8.5 %collective-permute-start.30 = (f32[4096]{0:T(1024)S(1)}, f32[4096]{0:T(1024)S(1)}, u32[]{:S(2)}, u32[]{:S(2)}) collective-permute-start(f32[4096]{0:T(1024)S(1)} %bitcast.48), channel_id=1, source_target_pairs={{0,4},{1,5},{2,6},{3,7},{4,0},{5,1},{6,2},{7,3},{8,12},{9,13},{10,... | collective-permute-start | bytes 49160 | tf_op jit(solution)/shard_map/ppermute | solution.py:607
  123.1 7.8 %collective-permute-start.29 = (f32[4096]{0:T(1024)S(1)}, f32[4096]{0:T(1024)S(1)}, u32[]{:S(2)}, u32[]{:S(2)}) collective-permute-start(f32[4096]{0:T(1024)S(1)} %bitcast.49), channel_id=1, source_target_pairs={{0,2},{1,3},{2,0},{3,1},{4,6},{5,7},{6,4},{7,5},{8,10},{9,11},{10,... | collective-permute-start | bytes 49160 | tf_op jit(solution)/shard_map/ppermute | solution.py:607
  128.3 4.6 %collective-permute-start.32 = (bf16[1024,128]{1,0:T(8,128)(2,1)S(1)}, bf16[1024,128]{1,0:T(8,128)(2,1)S(1)}, u32[]{:S(2)}, u32[]{:S(2)}) collective-permute-start(bf16[1024,128]{1,0:T(8,128)(2,1)S(1)} %get-tuple-element.84), channel_id=1, source_target_pairs={{0,8},{1,9},{2,10},{3,11},{4,12},{5,13},{6,14},{7,15},{8,0},{9,1},... | collective-permute-start | bytes 786440 | tf_op jit(solution)/shard_map/ppermute | solution.py:607
  128.5 17.2 %collective-permute-start.37 = (bf16[512,128]{1,0:T(8,128)(2,1)S(1)}, bf16[512,128]{1,0:T(8,128)(2,1)S(1)}, u32[]{:S(2)}, u32[]{:S(2)}) collective-permute-start(bf16[512,128]{1,0:T(8,128)(2,1)S(1)} %get-tuple-element.98), channel_id=1, source_target_pairs={{0,4},{1,5},{2,6},{3,7},{4,0},{5,1},{6,2},{7,3},{8,12},{9,13},{10,... | collective-permute-start | bytes 393224 | tf_op jit(solution)/shard_map/ppermute | solution.py:607
  129.7 16.0 %collective-permute-start.38 = (bf16[512,128]{1,0:T(8,128)(2,1)S(1)}, bf16[512,128]{1,0:T(8,128)(2,1)S(1)}, u32[]{:S(2)}, u32[]{:S(2)}) collective-permute-start(bf16[512,128]{1,0:T(8,128)(2,1)S(1)} %get-tuple-element.99), channel_id=1, source_target_pairs={{0,6},{1,7},{2,4},{3,5},{4,2},{5,3},{6,0},{7,1},{8,14},{9,15},{10,... | collective-permute-start | bytes 393224 | tf_op jit(solution)/shard_map/ppermute | solution.py:607
  133.0 10.2 %collective-permute-start.33 = (bf16[512,128]{1,0:T(8,128)(2,1)S(1)}, bf16[512,128]{1,0:T(8,128)(2,1)S(1)}, u32[]{:S(2)}, u32[]{:S(2)}) collective-permute-start(bf16[512,128]{1,0:T(8,128)(2,1)S(1)} %get-tuple-element.91), channel_id=1, source_target_pairs={{0,2},{1,3},{2,0},{3,1},{4,6},{5,7},{6,4},{7,5},{8,10},{9,11},{10,... | collective-permute-start | bytes 393224 | tf_op jit(solution)/shard_map/ppermute | solution.py:607
  134.2 9.0 %collective-permute-start.34 = (bf16[512,128]{1,0:T(8,128)(2,1)S(1)}, bf16[512,128]{1,0:T(8,128)(2,1)S(1)}, u32[]{:S(2)}, u32[]{:S(2)}) collective-permute-start(bf16[512,128]{1,0:T(8,128)(2,1)S(1)} %get-tuple-element.92), channel_id=1, source_target_pairs={{0,17},{1,16},{2,19},{3,18},{4,21},{5,20},{6,23},{7,22},{8,25},{9,... | collective-permute-start | bytes 393224 | tf_op jit(solution)/shard_map/ppermute | solution.py:607
  143.2 5.4 %collective-permute-start.35 = (bf16[512,128]{1,0:T(8,128)(2,1)S(1)}, bf16[512,128]{1,0:T(8,128)(2,1)S(1)}, u32[]{:S(2)}, u32[]{:S(2)}) collective-permute-start(bf16[512,128]{1,0:T(8,128)(2,1)S(1)} %get-tuple-element.93), channel_id=1, source_target_pairs={{0,1},{1,0},{2,3},{3,2},{4,5},{5,4},{6,7},{7,6},{8,9},{9,8},{10,11... | collective-permute-start | bytes 393224 | tf_op jit(solution)/shard_map/ppermute | solution.py:607
  143.2 5.4 %collective-permute-start.36 = (bf16[512,128]{1,0:T(8,128)(2,1)S(1)}, bf16[512,128]{1,0:T(8,128)(2,1)S(1)}, u32[]{:S(2)}, u32[]{:S(2)}) collective-permute-start(bf16[512,128]{1,0:T(8,128)(2,1)S(1)} %get-tuple-element.94), channel_id=1, source_target_pairs={{0,16},{1,17},{2,18},{3,19},{4,20},{5,21},{6,22},{7,23},{8,24},{9,... | collective-permute-start | bytes 393224 | tf_op jit(solution)/shard_map/ppermute | solution.py:607

commit v14 on v13

--- a/solution.py
+++ b/solution.py
@@ -15,7 +15,6 @@
 CROSS = 2.0 * LOG2E / EPSILON
 NT = (((1,), (1,)), ((), ()))
 VMEM = pl.BlockSpec(memory_space=pltpu.VMEM)
-GROUP = 16
 HEAVY = 32
 
 
@@ -99,7 +98,7 @@
 
 
 def lse_pass(places, chunk, width, a_ref, b_ref, sb_ref, d_ref, top_ref, o_ref, e_ref=None, shift_ref=None):
-    tiles = width // 128
+    tiles, group = width // 128, top_ref.shape[0]
     top_ref[...] = jnp.zeros_like(top_ref)
 
     def lanes_of(start, q):
@@ -107,21 +106,21 @@
 
     def tile(m, start, state):
         def exponents(g, q):
-            at = g * GROUP
-            s = sb_ref[places[m] + at:places[m] + at + GROUP, :]
-            return d_ref[m % 2, at:at + GROUP, q * 128:(q + 1) * 128] * CROSS + s
+            at = g * group
+            s = sb_ref[places[m] + at:places[m] + at + group, :]
+            return d_ref[m % 2, at:at + group, q * 128:(q + 1) * 128] * CROSS + s
 
         if m == 0:
             tops = [exponents(0, q) for q in range(tiles)]
-            for g in range(1, 128 // GROUP):
+            for g in range(1, 128 // group):
                 tops = [jnp.maximum(top, exponents(g, q)) for q, top in enumerate(tops)]
-            state = [(jnp.max(top, axis=0, keepdims=True), jnp.zeros((GROUP, 128), jnp.float32)) for top in tops]
-        for g in range(chunk // GROUP):
+            state = [(jnp.max(top, axis=0, keepdims=True), jnp.zeros((group, 128), jnp.float32)) for top in tops]
+        for g in range(chunk // group):
             for q, (peak, total) in enumerate(state):
                 e = jnp.exp2(exponents(g, q) - peak)
                 if e_ref is not None:
-                    at = places[m] + g * GROUP
-                    e_ref[at:at + GROUP, lanes_of(start, q)] = e.astype(jnp.bfloat16)
+                    at = places[m] + g * group
+                    e_ref[at:at + group, lanes_of(start, q)] = e.astype(jnp.bfloat16)
                 state[q] = peak, total + e
         return state
 
@@ -309,11 +308,11 @@
     return jax.ShapeDtypeStruct(dims, dtype)
 
 
-def lse_scratch(depth, chunk, width):
+def lse_scratch(depth, chunk, width, group=32):
     return [
         pltpu.VMEM((depth, 128), jnp.float32),
         pltpu.VMEM((2, chunk, width), jnp.float32),
-        pltpu.VMEM((GROUP, 128), jnp.float32),
+        pltpu.VMEM((group, 128), jnp.float32),
     ]
 
 
@@ -373,7 +372,7 @@
         out_shape=(shape(1, cols + tail), shape(rows, cols, dtype=jnp.bfloat16), shape(1, cols), shape(1, rows)),
         in_specs=[VMEM] * (3 + len(got)),
         out_specs=(VMEM,) * 4,
-        scratch_shapes=[pltpu.VMEM((rows // 128, 128), jnp.float32), *lse_scratch(rows, chunk, width)],
+        scratch_shapes=[pltpu.VMEM((rows // 128, 128), jnp.float32), *lse_scratch(rows, chunk, width, 16)],
         compiler_params=pltpu.CompilerParams(vmem_limit_bytes=16 << 20),
         cost_estimate=pass_cost(rows, cols),
         name="column_lse",
@@ -675,7 +674,7 @@
     parts = [swap(part, along[z + 1]) for z, part in enumerate(parts)]
     last = swap(last, across[na - 1])
     sent = other_rows(list(range(1, na - 1)), share_x, x, yb, e, alpha, jnp.bfloat16)
-    sent, parts[0], last = lax.optimization_barrier((sent, parts[0], last))
+    sent, last = lax.optimization_barrier((sent, last))
     sent = [swap(part, across[s + 1]) for s, part in enumerate(sent)] + [last]
     gi, = other_rows([0], share_x, x, yb, e, alpha, jnp.float32)
     grad_imu, grad_cam = add_up([gi, *sent], [grad_cam, *parts, *far_gc], scale)

time: 150 us -> 146 us (0.973)
  waiting for transfers between devices: 27.4 us -> 24.1 us
    ppermute x39, waiting for transfers between devices: 27.4 us -> 24.1 us  [swap(): lax.ppermute(value, ('row', 'col'), [(i, i ^ mask) for i in range(self.co...]
  transfers between devices with their start and end apart: 39 -> 39, of which waited for: 18 -> 19; matrix products, arithmetic and copies ran while one was open for 1% -> 1% of each run, Pallas kernels for 15% -> 15%
where the time goes in v14:
time: 146 us
  Pallas kernels  79.6 us (55%)
  starting transfers between devices  39.5 us (27%)
  waiting for transfers between devices  24.1 us (17%)
    ppermute x39, starting transfers between devices, swap(): lax.ppermute(value, ('row', 'col'), [(i, i ^ mask) for i in range(self.co...  39.5 us
    pallas_call x1, Pallas kernels, column_lse(): pl.pallas_call(functools.partial(column_lse_kernel, width, chunk, len(got...  30.3 us
    ppermute x39, waiting for transfers between devices, swap(): lax.ppermute(value, ('row', 'col'), [(i, i ^ mask) for i in range(self.co...  24.1 us
    pallas_call x4, Pallas kernels, weighted(): pl.pallas_call(functools.partial(kernel, width, tuple(shifts), parts), ou...  12.7 us
    pallas_call x1, Pallas kernels, row_lse_late(): pl.pallas_call(functools.partial(row_lse_late_kernel, width, len(ys)), ou...  10.1 us
    pallas_call x1, Pallas kernels, row_lse_middle(): pl.pallas_call(functools.partial(row_lse_middle_kernel, width, len(ys)),...  6.5 us
    pallas_call x1, Pallas kernels, row_lse_early(): pl.pallas_call(functools.partial(row_lse_early_kernel, width, len(xs)), o...  6.48 us
    pallas_call x2, Pallas kernels, column_grad(): pl.pallas_call(functools.partial(kernel, blocks, share), out_shape=out_sh...  6.18 us
  transfers between devices with their start and end apart: 39, of which 19 were waited for; matrix products, arithmetic and copies ran while one was open for 1% of the time, Pallas kernels for 15%

profile of v14, /device:TPU:0, one launch (start us, length us, event | category | flops | bytes accessed | tf_op | source)
XLA Modules:
  0.0 145.9 jit_solution(4413607934990074570)
XLA Ops:
  0.6 3.0 %collective-permute-start = (bf16[512,128]{1,0:T(8,128)(2,1)}, bf16[512,128]{1,0:T(8,128)(2,1)S(1)}, u32[]{:S(2)}, u32[]{:S(2)}) collective-permute-start(bf16[512,128]{1,0:T(8,128)(2,1)} %param.4), channel_id=1, source_target_pairs={{0,1},{1,0},{2,3},{3,2},{4,5},{5,4},{6,7},{7,6},{8,9},{9,8},{10,11... | collective-permute-start | bytes 393224 | tf_op jit(solution)/shard_map/ppermute | solution.py:606
  3.7 1.4 collective-permute-start.2
  5.2 3.0 %collective-permute-start.4 = (bf16[512,128]{1,0:T(8,128)(2,1)}, bf16[512,128]{1,0:T(8,128)(2,1)S(1)}, u32[]{:S(2)}, u32[]{:S(2)}) collective-permute-start(bf16[512,128]{1,0:T(8,128)(2,1)} %bitcast.77), channel_id=1, source_target_pairs={{0,4},{1,5},{2,6},{3,7},{4,0},{5,1},{6,2},{7,3},{8,12},{9,13},{10,... | collective-permute-start | bytes 393224 | tf_op jit(solution)/shard_map/ppermute | solution.py:606
  8.2 1.0 pad_maximum_fusion.own_ref
  9.3 0.9 fusion
  10.2 1.6 %collective-permute-start.5 = (bf16[512,128]{1,0:T(8,128)(2,1)}, bf16[512,128]{1,0:T(8,128)(2,1)S(1)}, u32[]{:S(2)}, u32[]{:S(2)}) collective-permute-start(bf16[512,128]{1,0:T(8,128)(2,1)} %bitcast.80), channel_id=1, source_target_pairs={{0,2},{1,3},{2,0},{3,1},{4,6},{5,7},{6,4},{7,5},{8,10},{9,11},{10,... | collective-permute-start | bytes 393224 | tf_op jit(solution)/shard_map/ppermute | solution.py:606
  11.8 6.5 %row_lse_early.1 = (bf16[2048,128]{1,0:T(8,128)(2,1)S(1)}, bf16[128,2048]{1,0:T(8,128)(2,1)S(1)}, f32[1,2048]{1,0:T(1,128)S(1)}) custom-call(bf16[1024,128]{1,0:T(8,128)(2,1)S(1)} %pad_maximum_fusion.own_ref, bf16[512,128]{1,0:T(8,128)(2,1)S(1)} %collective-permute-done.refs_0_, bf16[512,128]{1,0:T(8,128)(2,1)S(1)} %collective-permute-done.1.refs_1_, ...), custom_call_target="tpu_custom_call" | custom-call | flops 536870912 | bytes 786432 | tf_op jit(solution)/shard_map/row_lse_early/pallas_call | solution.py:322
  19.0 6.5 %row_lse_middle.1.first_ref = f32[1,2048]{1,0:T(1,128)S(1)} custom-call(bf16[2048,128]{1,0:T(8,128)(2,1)S(1)} %get-tuple-element.53.x_ref, f32[1,2048]{1,0:T(1,128)S(1)} %get-tuple-element.56.first_ref, bf16[512,128]{1,0:T(8,128)(2,1)S(1)} %collective-permute-done.5.refs_0_, bf16[512,128]{1,0:T(8,128)(2,1)S(1)} %collective-permute-done.4.refs_1_), custom_call_target="tpu_custom_call" | custom-call | flops 536870912 | bytes 786432 | tf_op jit(solution)/shard_map/row_lse_middle/pallas_call | solution.py:337
  25.7 1.3 collective-permute-done.9.refs_6_
  26.9 10.1 %row_lse_late.1 = (bf16[4096,128]{1,0:T(8,128)(2,1)S(1)}, f32[1,3072]{1,0:T(1,128)S(1)}) custom-call(bf16[1024,128]{1,0:T(8,128)(2,1)S(1)} %pad_maximum_fusion.own_ref, f32[1,2048]{1,0:T(1,128)S(1)} %bitcast.66, bf16[2048,128]{1,0:T(8,128)(2,1)S(1)} %get-tuple-element.53.x_ref, f32[1,2048]{1,0:T(1,128)S(1)} %row_lse_middle.1.first_ref, ...), custom_call_target="tpu_custom_call" | custom-call | flops 1073741824 | bytes 1048576 | tf_op jit(solution)/shard_map/row_lse_late/pallas_call | solution.py:356
  37.1 3.4 %collective-permute-start.10 = (f32[3072]{0:T(1024)S(1)}, f32[3072]{0:T(1024)S(1)}, u32[]{:S(2)}, u32[]{:S(2)}) collective-permute-start(f32[3072]{0:T(1024)S(1)} %bitcast.73), channel_id=1, source_target_pairs={{0,1},{1,0},{2,3},{3,2},{4,5},{5,4},{6,7},{7,6},{8,9},{9,8},{10,11... | collective-permute-start | bytes 36872 | tf_op jit(solution)/shard_map/ppermute | solution.py:606
  40.5 1.1 collective-permute-done.12
  42.2 30.3 %column_lse.1 = (f32[1,5120]{1,0:T(1,128)S(1)}, bf16[2048,4096]{1,0:T(8,128)(2,1)S(1)}, f32[1,4096]{1,0:T(1,128)S(1)}, f32[1,2048]{1,0:T(1,128)S(1)}) custom-call(bf16[2048,128]{1,0:T(8,128)(2,1)S(1)} %get-tuple-element.53.x_ref, bf16[4096,128]{1,0:T(8,128)(2,1)S(1)} %get-tuple-element.60.y_ref, f32[1,2048]{1,0:T(1,128)S(1)} %bitcast.67, ...), custom_call_target="tpu_custom_call" | custom-call | flops 2147483648 | bytes 1572864 | tf_op jit(solution)/shard_map/column_lse/pallas_call | solution.py:370
  72.7 1.2 collective-permute-done.13
  73.9 2.8 %collective-permute-start.16 = (f32[5120]{0:T(1024)S(1)}, f32[5120]{0:T(1024)S(1)}, u32[]{:S(2)}, u32[]{:S(2)}) collective-permute-start(f32[5120]{0:T(1024)S(1)} %bitcast.33), channel_id=1, source_target_pairs={{0,6},{1,7},{2,4},{3,5},{4,2},{5,3},{6,0},{7,1},{8,14},{9,15},{10,... | collective-permute-start | bytes 61448 | tf_op jit(solution)/shard_map/ppermute | solution.py:606
  76.7 1.6 %collective-permute-start.15 = (f32[5120]{0:T(1024)S(1)}, f32[5120]{0:T(1024)S(1)}, u32[]{:S(2)}, u32[]{:S(2)}) collective-permute-start(f32[5120]{0:T(1024)S(1)} %bitcast.34), channel_id=1, source_target_pairs={{0,4},{1,5},{2,6},{3,7},{4,0},{5,1},{6,2},{7,3},{8,12},{9,13},{10,... | collective-permute-start | bytes 61448 | tf_op jit(solution)/shard_map/ppermute | solution.py:606
  78.8 0.9 collective-permute-done.16
  79.6 1.7 %collective-permute-done.15 = f32[5120]{0:T(1024)S(1)} collective-permute-done((f32[5120]{0:T(1024)S(1)}, f32[5120]{0:T(1024)S(1)}, u32[]{:S(2)}, u32[]{:S(2)}) %collective-permute-start.15) | collective-permute-done | bytes 20512 | tf_op jit(solution)/shard_map/ppermute | solution.py:606
  82.1 3.8 %weighted_sum.4 = (f32[1,2048]{1,0:T(1,128)S(1)}, f32[1,4096]{1,0:T(1,128)S(1)}, f32[1,4096]{1,0:T(1,128)S(1)}) custom-call(bf16[2048,4096]{1,0:T(8,128)(2,1)S(1)} %get-tuple-element.62.e_ref, f32[1,4096]{1,0:T(1,128)S(1)} %get-tuple-element.65.shift_ref, f32[1,5120]{1,0:T(1,128)S(1)} %pair.3.refs_0_, f32[1,5120]{1,0:T(1,128)S(1)} %bitcast.44, ...), custom_call_target="tpu_custom_call" | custom-call | flops 16777216 | bytes 16777216 | tf_op jit(solution)/shard_map/weighted_sum/pallas_call | solution.py:291
  85.9 0.9 collective-permute-start.19
  87.6 1.9 %collective-permute-start.17 = (f32[2048]{0:T(1024)S(1)}, f32[2048]{0:T(1024)S(1)}, u32[]{:S(2)}, u32[]{:S(2)}) collective-permute-start(f32[2048]{0:T(1024)S(1)} %bitcast.59), channel_id=1, source_target_pairs={{0,1},{1,0},{2,3},{3,2},{4,5},{5,4},{6,7},{7,6},{8,9},{9,8},{10,11... | collective-permute-start | bytes 24584 | tf_op jit(solution)/shard_map/ppermute | solution.py:606
  89.4 1.1 collective-permute-done.19
  91.2 2.8 %weighted_sum.5 = (f32[1,4096]{1,0:T(1,128)S(1)}, f32[1,2048]{1,0:T(1,128)}) custom-call(bf16[2048,4096]{1,0:T(8,128)(2,1)S(1)} %get-tuple-element.62.e_ref, f32[1,2048]{1,0:T(1,128)S(1)} %get-tuple-element.64.a_ref, f32[1,4096]{1,0:T(1,128)S(1)} %get-tuple-element.67.first_ref, f32[1,2048]{1,0:T(1,128)S(1)} %get-tuple-element.69.refs_0_, ...), custom_call_target="tpu_custom_call" | custom-call | flops 16777216 | bytes 16777216 | tf_op jit(solution)/shard_map/weighted_sum/pallas_call | solution.py:291
  94.0 1.2 collective-permute-done.20
  95.2 2.7 %collective-permute-start.23 = (f32[4096]{0:T(1024)S(1)}, f32[4096]{0:T(1024)S(1)}, u32[]{:S(2)}, u32[]{:S(2)}) collective-permute-start(f32[4096]{0:T(1024)S(1)} %bitcast.36), channel_id=1, source_target_pairs={{0,6},{1,7},{2,4},{3,5},{4,2},{5,3},{6,0},{7,1},{8,14},{9,15},{10,... | collective-permute-start | bytes 49160 | tf_op jit(solution)/shard_map/ppermute | solution.py:606
  98.6 1.0 collective-permute-start.21
  99.7 1.1 collective-permute-done.23
  100.8 1.8 %collective-permute-done.22 = f32[4096]{0:T(1024)S(1)} collective-permute-done((f32[4096]{0:T(1024)S(1)}, f32[4096]{0:T(1024)S(1)}, u32[]{:S(2)}, u32[]{:S(2)}) %collective-permute-start.22) | collective-permute-done | bytes 16416 | tf_op jit(solution)/shard_map/ppermute | solution.py:606
  102.6 3.8 %weighted_sum.6.refs_0_ = f32[1,2048]{1,0:T(1,128)S(1)} custom-call(bf16[2048,4096]{1,0:T(8,128)(2,1)S(1)} %get-tuple-element.62.e_ref, f32[1,4096]{1,0:T(1,128)S(1)} %get-tuple-element.67.first_ref, f32[1,4096]{1,0:T(1,128)S(1)} %get-tuple-element.68.b_ref, f32[1,4096]{1,0:T(1,128)S(1)} %pair.4.refs_0_, f32[1,4096]{1,0:T(1,128)S(1)} %bitcast.56, ...), custom_call_target="tpu_custom_call" | custom-call | flops 16777216 | bytes 16777216 | tf_op jit(solution)/shard_map/weighted_sum/pallas_call | solution.py:291
  106.4 1.6 %collective-permute-start.26 = (f32[2048]{0:T(1024)S(1)}, f32[2048]{0:T(1024)S(1)}, u32[]{:S(2)}, u32[]{:S(2)}) collective-permute-start(f32[2048]{0:T(1024)S(1)} %bitcast.39), channel_id=1, source_target_pairs={{0,17},{1,16},{2,19},{3,18},{4,21},{5,20},{6,23},{7,22},{8,25},{9,... | collective-permute-start | bytes 24584 | tf_op jit(solution)/shard_map/ppermute | solution.py:606
  108.0 1.9 %collective-permute-start.25 = (f32[2048]{0:T(1024)S(1)}, f32[2048]{0:T(1024)S(1)}, u32[]{:S(2)}, u32[]{:S(2)}) collective-permute-start(f32[2048]{0:T(1024)S(1)} %bitcast.40), channel_id=1, source_target_pairs={{0,16},{1,17},{2,18},{3,19},{4,20},{5,21},{6,22},{7,23},{8,24},{9,... | collective-permute-start | bytes 24584 | tf_op jit(solution)/shard_map/ppermute | solution.py:606
  110.0 1.1 collective-permute-done.26
  111.7 1.9 %collective-permute-done.24 = f32[2048]{0:T(1024)S(1)} collective-permute-done((f32[2048]{0:T(1024)S(1)}, f32[2048]{0:T(1024)S(1)}, u32[]{:S(2)}, u32[]{:S(2)}) %collective-permute-start.24) | collective-permute-done | bytes 8224 | tf_op jit(solution)/shard_map/ppermute | solution.py:606
  113.6 2.3 %weighted_sum.7 = (f32[1,4096]{1,0:T(1,128)S(1)}, f32[1,2048]{1,0:T(1,128)S(1)}) custom-call(bf16[2048,4096]{1,0:T(8,128)(2,1)S(1)} %get-tuple-element.62.e_ref, f32[1,2048]{1,0:T(1,128)S(1)} %get-tuple-element.64.a_ref, f32[1,4096]{1,0:T(1,128)S(1)} %get-tuple-element.67.first_ref, f32[1,2048]{1,0:T(1,128)S(1)} %weighted_sum.6.refs_0_, ...), custom_call_target="tpu_custom_call" | custom-call | flops 16777216 | bytes 16777216 | tf_op jit(solution)/shard_map/weighted_sum/pallas_call | solution.py:291
  116.0 1.2 collective-permute-done.27
  117.2 3.2 %column_grad.2 = (f32[1024,128]{1,0:T(8,128)S(1)}, bf16[1024,128]{1,0:T(8,128)(2,1)S(1)}, bf16[256,2048]{1,0:T(8,128)(2,1)S(1)}) custom-call(bf16[128,2048]{1,0:T(8,128)(2,1)S(1)} %get-tuple-element.63.xt_ref, bf16[4096,128]{1,0:T(8,128)(2,1)S(1)} %get-tuple-element.60.y_ref, bf16[2048,4096]{1,0:T(8,128)(2,1)S(1)} %get-tuple-element.62.e_ref, ...), custom_call_target="tpu_custom_call" | custom-call | flops 2147483648 | bytes 8388608 | tf_op jit(solution)/shard_map/column_grad/pallas_call | solution.py:452
  120.7 1.5 collective-permute-start.31
  122.8 2.3 %collective-permute-start.29 = (f32[4096]{0:T(1024)S(1)}, f32[4096]{0:T(1024)S(1)}, u32[]{:S(2)}, u32[]{:S(2)}) collective-permute-start(f32[4096]{0:T(1024)S(1)} %bitcast.49), channel_id=1, source_target_pairs={{0,2},{1,3},{2,0},{3,1},{4,6},{5,7},{6,4},{7,5},{8,10},{9,11},{10,... | collective-permute-start | bytes 49160 | tf_op jit(solution)/shard_map/ppermute | solution.py:606
  125.1 3.0 %column_grad.3 = (f32[1024,128]{1,0:T(8,128)S(1)}, bf16[1024,128]{1,0:T(8,128)(2,1)S(1)}) custom-call(bf16[256,2048]{1,0:T(8,128)(2,1)S(1)} %get-tuple-element.81.xa_ref, bf16[4096,128]{1,0:T(8,128)(2,1)S(1)} %get-tuple-element.60.y_ref, bf16[2048,4096]{1,0:T(8,128)(2,1)S(1)} %get-tuple-element.62.e_ref, f32[1,4096]{1,0:T(1,128)S(1)} %get-tuple-element.67.first_ref), custom_call_target="tpu_custom_call" | custom-call | flops 2147483648 | bytes 8388608 | tf_op jit(solution)/shard_map/column_grad/pallas_call | solution.py:452
  128.2 1.2 collective-permute-start.37
  129.4 1.2 collective-permute-start.38
  130.6 2.0 %first_rows.1 = (bf16[4096,256]{1,0:T(8,128)(2,1)S(1)}, f32[1,512]{1,0:T(1,128)S(1)}, bf16[512,128]{1,0:T(8,128)(2,1)S(1)}) custom-call(bf16[2048,128]{1,0:T(8,128)(2,1)S(1)} %get-tuple-element.53.x_ref, bf16[4096,128]{1,0:T(8,128)(2,1)S(1)} %get-tuple-element.60.y_ref, bf16[2048,4096]{1,0:T(8,128)(2,1)S(1)} %get-tuple-element.62.e_ref, ...), custom_call_target="tpu_custom_call" | custom-call | flops 34359738368 | bytes 134217728 | tf_op jit(solution)/shard_map/first_rows/pallas_call | solution.py:526
  132.7 1.2 collective-permute-start.36
  134.0 2.6 %other_rows.3 = (bf16[512,128]{1,0:T(8,128)(2,1)S(1)}, bf16[512,128]{1,0:T(8,128)(2,1)S(1)}) custom-call(bf16[2048,128]{1,0:T(8,128)(2,1)S(1)} %get-tuple-element.53.x_ref, bf16[4096,256]{1,0:T(8,128)(2,1)S(1)} %get-tuple-element.87.yb_ref, bf16[2048,4096]{1,0:T(8,128)(2,1)S(1)} %get-tuple-element.62.e_ref, f32[1,2048]{1,0:T(1,128)S(1)} %get-tuple-element.78.alpha_ref), custom_call_target="tpu_custom_call" | custom-call | flops 2147483648 | bytes 8388608 | tf_op jit(solution)/shard_map/other_rows/pallas_call | solution.py:544
  136.6 3.2 %collective-permute-done.33.refs_3_ = bf16[512,128]{1,0:T(8,128)(2,1)S(1)} collective-permute-done((bf16[512,128]{1,0:T(8,128)(2,1)S(1)}, bf16[512,128]{1,0:T(8,128)(2,1)S(1)}, u32[]{:S(2)}, u32[]{:S(2)}) %collective-permute-start.33) | collective-permute-done | bytes 131104 | tf_op jit(solution)/shard_map/ppermute | solution.py:606
  140.7 1.4 other_rows.2.refs_0_
  142.9 1.9 %collective-permute-done.34.refs_1_ = bf16[512,128]{1,0:T(8,128)(2,1)S(1)} collective-permute-done((bf16[512,128]{1,0:T(8,128)(2,1)S(1)}, bf16[512,128]{1,0:T(8,128)(2,1)S(1)}, u32[]{:S(2)}, u32[]{:S(2)}) %collective-permute-start.34) | collective-permute-done | bytes 131104 | tf_op jit(solution)/shard_map/ppermute | solution.py:606
  144.8 1.1 add_up.1
  (52 shorter events, 8.8 us)
Async XLA Ops:
  0.6 9.5 %collective-permute-start = (bf16[512,128]{1,0:T(8,128)(2,1)}, bf16[512,128]{1,0:T(8,128)(2,1)S(1)}, u32[]{:S(2)}, u32[]{:S(2)}) collective-permute-start(bf16[512,128]{1,0:T(8,128)(2,1)} %param.4), channel_id=1, source_target_pairs={{0,1},{1,0},{2,3},{3,2},{4,5},{5,4},{6,7},{7,6},{8,9},{9,8},{10,11... | collective-permute-start | bytes 393224 | tf_op jit(solution)/shard_map/ppermute | solution.py:606
  3.7 8.2 %collective-permute-start.2 = (bf16[512,128]{1,0:T(8,128)(2,1)}, bf16[512,128]{1,0:T(8,128)(2,1)S(1)}, u32[]{:S(2)}, u32[]{:S(2)}) collective-permute-start(bf16[512,128]{1,0:T(8,128)(2,1)} %param.4), channel_id=1, source_target_pairs={{0,17},{1,16},{2,19},{3,18},{4,21},{5,20},{6,23},{7,22},{8,25},{9,... | collective-permute-start | bytes 393224 | tf_op jit(solution)/shard_map/ppermute | solution.py:606
  5.1 6.7 %collective-permute-start.1 = (bf16[512,128]{1,0:T(8,128)(2,1)}, bf16[512,128]{1,0:T(8,128)(2,1)S(1)}, u32[]{:S(2)}, u32[]{:S(2)}) collective-permute-start(bf16[512,128]{1,0:T(8,128)(2,1)} %param.4), channel_id=1, source_target_pairs={{0,16},{1,17},{2,18},{3,19},{4,20},{5,21},{6,22},{7,23},{8,24},{9,... | collective-permute-start | bytes 393224 | tf_op jit(solution)/shard_map/ppermute | solution.py:606
  5.2 13.1 %collective-permute-start.4 = (bf16[512,128]{1,0:T(8,128)(2,1)}, bf16[512,128]{1,0:T(8,128)(2,1)S(1)}, u32[]{:S(2)}, u32[]{:S(2)}) collective-permute-start(bf16[512,128]{1,0:T(8,128)(2,1)} %bitcast.77), channel_id=1, source_target_pairs={{0,4},{1,5},{2,6},{3,7},{4,0},{5,1},{6,2},{7,3},{8,12},{9,13},{10,... | collective-permute-start | bytes 393224 | tf_op jit(solution)/shard_map/ppermute | solution.py:606
  9.2 2.6 %collective-permute-start.3 = (bf16[512,128]{1,0:T(8,128)(2,1)}, bf16[512,128]{1,0:T(8,128)(2,1)S(1)}, u32[]{:S(2)}, u32[]{:S(2)}) collective-permute-start(bf16[512,128]{1,0:T(8,128)(2,1)} %bitcast.79), channel_id=1, source_target_pairs={{0,8},{1,9},{2,10},{3,11},{4,12},{5,13},{6,14},{7,15},{8,0},{9,1},... | collective-permute-start | bytes 393224 | tf_op jit(solution)/shard_map/ppermute | solution.py:606
  10.2 8.3 %collective-permute-start.5 = (bf16[512,128]{1,0:T(8,128)(2,1)}, bf16[512,128]{1,0:T(8,128)(2,1)S(1)}, u32[]{:S(2)}, u32[]{:S(2)}) collective-permute-start(bf16[512,128]{1,0:T(8,128)(2,1)} %bitcast.80), channel_id=1, source_target_pairs={{0,2},{1,3},{2,0},{3,1},{4,6},{5,7},{6,4},{7,5},{8,10},{9,11},{10,... | collective-permute-start | bytes 393224 | tf_op jit(solution)/shard_map/ppermute | solution.py:606
  18.3 7.2 %collective-permute-start.6 = (bf16[512,128]{1,0:T(8,128)(2,1)S(1)}, bf16[512,128]{1,0:T(8,128)(2,1)S(1)}, u32[]{:S(2)}, u32[]{:S(2)}) collective-permute-start(bf16[512,128]{1,0:T(8,128)(2,1)S(1)} %collective-permute-done.4.refs_1_), channel_id=1, source_target_pairs={{0,2},{1,3},{2,0},{3,1},{4,6},{5,7},{6,4},{7,5},{8,10},{9,11},{10,... | collective-permute-start | bytes 393224 | tf_op jit(solution)/shard_map/ppermute | solution.py:606
  18.4 7.3 %collective-permute-start.8 = (bf16[512,128]{1,0:T(8,128)(2,1)S(1)}, bf16[512,128]{1,0:T(8,128)(2,1)S(1)}, u32[]{:S(2)}, u32[]{:S(2)}) collective-permute-start(bf16[512,128]{1,0:T(8,128)(2,1)S(1)} %collective-permute-done.4.refs_1_), channel_id=1, source_target_pairs={{0,8},{1,9},{2,10},{3,11},{4,12},{5,13},{6,14},{7,15},{8,0},{9,1},... | collective-permute-start | bytes 393224 | tf_op jit(solution)/shard_map/ppermute | solution.py:606
  18.5 7.2 %collective-permute-start.7 = (bf16[512,128]{1,0:T(8,128)(2,1)S(1)}, bf16[512,128]{1,0:T(8,128)(2,1)S(1)}, u32[]{:S(2)}, u32[]{:S(2)}) collective-permute-start(bf16[512,128]{1,0:T(8,128)(2,1)S(1)} %collective-permute-done.5.refs_0_), channel_id=1, source_target_pairs={{0,8},{1,9},{2,10},{3,11},{4,12},{5,13},{6,14},{7,15},{8,0},{9,1},... | collective-permute-start | bytes 393224 | tf_op jit(solution)/shard_map/ppermute | solution.py:606
  25.5 1.4 collective-permute-start.9
  37.0 4.7 %collective-permute-start.12 = (f32[3072]{0:T(1024)S(1)}, f32[3072]{0:T(1024)S(1)}, u32[]{:S(2)}, u32[]{:S(2)}) collective-permute-start(f32[3072]{0:T(1024)S(1)} %bitcast.71), channel_id=1, source_target_pairs={{0,17},{1,16},{2,19},{3,18},{4,21},{5,20},{6,23},{7,22},{8,25},{9,... | collective-permute-start | bytes 36872 | tf_op jit(solution)/shard_map/ppermute | solution.py:606
  37.1 4.6 %collective-permute-start.11 = (f32[3072]{0:T(1024)S(1)}, f32[3072]{0:T(1024)S(1)}, u32[]{:S(2)}, u32[]{:S(2)}) collective-permute-start(f32[3072]{0:T(1024)S(1)} %bitcast.72), channel_id=1, source_target_pairs={{0,16},{1,17},{2,18},{3,19},{4,20},{5,21},{6,22},{7,23},{8,24},{9,... | collective-permute-start | bytes 36872 | tf_op jit(solution)/shard_map/ppermute | solution.py:606
  37.1 5.1 %collective-permute-start.10 = (f32[3072]{0:T(1024)S(1)}, f32[3072]{0:T(1024)S(1)}, u32[]{:S(2)}, u32[]{:S(2)}) collective-permute-start(f32[3072]{0:T(1024)S(1)} %bitcast.73), channel_id=1, source_target_pairs={{0,1},{1,0},{2,3},{3,2},{4,5},{5,4},{6,7},{7,6},{8,9},{9,8},{10,11... | collective-permute-start | bytes 36872 | tf_op jit(solution)/shard_map/ppermute | solution.py:606
  72.6 1.3 collective-permute-start.13
  73.9 5.8 %collective-permute-start.16 = (f32[5120]{0:T(1024)S(1)}, f32[5120]{0:T(1024)S(1)}, u32[]{:S(2)}, u32[]{:S(2)}) collective-permute-start(f32[5120]{0:T(1024)S(1)} %bitcast.33), channel_id=1, source_target_pairs={{0,6},{1,7},{2,4},{3,5},{4,2},{5,3},{6,0},{7,1},{8,14},{9,15},{10,... | collective-permute-start | bytes 61448 | tf_op jit(solution)/shard_map/ppermute | solution.py:606
  76.7 4.7 %collective-permute-start.15 = (f32[5120]{0:T(1024)S(1)}, f32[5120]{0:T(1024)S(1)}, u32[]{:S(2)}, u32[]{:S(2)}) collective-permute-start(f32[5120]{0:T(1024)S(1)} %bitcast.34), channel_id=1, source_target_pairs={{0,4},{1,5},{2,6},{3,7},{4,0},{5,1},{6,2},{7,3},{8,12},{9,13},{10,... | collective-permute-start | bytes 61448 | tf_op jit(solution)/shard_map/ppermute | solution.py:606
  78.3 3.8 %collective-permute-start.14 = (f32[5120]{0:T(1024)S(1)}, f32[5120]{0:T(1024)S(1)}, u32[]{:S(2)}, u32[]{:S(2)}) collective-permute-start(f32[5120]{0:T(1024)S(1)} %bitcast.35), channel_id=1, source_target_pairs={{0,2},{1,3},{2,0},{3,1},{4,6},{5,7},{6,4},{7,5},{8,10},{9,11},{10,... | collective-permute-start | bytes 61448 | tf_op jit(solution)/shard_map/ppermute | solution.py:606
  85.9 4.6 %collective-permute-start.19 = (f32[2048]{0:T(1024)S(1)}, f32[2048]{0:T(1024)S(1)}, u32[]{:S(2)}, u32[]{:S(2)}) collective-permute-start(f32[2048]{0:T(1024)S(1)} %bitcast.57), channel_id=1, source_target_pairs={{0,17},{1,16},{2,19},{3,18},{4,21},{5,20},{6,23},{7,22},{8,25},{9,... | collective-permute-start | bytes 24584 | tf_op jit(solution)/shard_map/ppermute | solution.py:606
  86.7 3.7 %collective-permute-start.18 = (f32[2048]{0:T(1024)S(1)}, f32[2048]{0:T(1024)S(1)}, u32[]{:S(2)}, u32[]{:S(2)}) collective-permute-start(f32[2048]{0:T(1024)S(1)} %bitcast.58), channel_id=1, source_target_pairs={{0,16},{1,17},{2,18},{3,19},{4,20},{5,21},{6,22},{7,23},{8,24},{9,... | collective-permute-start | bytes 24584 | tf_op jit(solution)/shard_map/ppermute | solution.py:606
  87.6 3.7 %collective-permute-start.17 = (f32[2048]{0:T(1024)S(1)}, f32[2048]{0:T(1024)S(1)}, u32[]{:S(2)}, u32[]{:S(2)}) collective-permute-start(f32[2048]{0:T(1024)S(1)} %bitcast.59), channel_id=1, source_target_pairs={{0,1},{1,0},{2,3},{3,2},{4,5},{5,4},{6,7},{7,6},{8,9},{9,8},{10,11... | collective-permute-start | bytes 24584 | tf_op jit(solution)/shard_map/ppermute | solution.py:606
  94.0 1.2 collective-permute-start.20
  95.2 5.6 %collective-permute-start.23 = (f32[4096]{0:T(1024)S(1)}, f32[4096]{0:T(1024)S(1)}, u32[]{:S(2)}, u32[]{:S(2)}) collective-permute-start(f32[4096]{0:T(1024)S(1)} %bitcast.36), channel_id=1, source_target_pairs={{0,6},{1,7},{2,4},{3,5},{4,2},{5,3},{6,0},{7,1},{8,14},{9,15},{10,... | collective-permute-start | bytes 49160 | tf_op jit(solution)/shard_map/ppermute | solution.py:606
  97.9 4.6 %collective-permute-start.22 = (f32[4096]{0:T(1024)S(1)}, f32[4096]{0:T(1024)S(1)}, u32[]{:S(2)}, u32[]{:S(2)}) collective-permute-start(f32[4096]{0:T(1024)S(1)} %bitcast.37), channel_id=1, source_target_pairs={{0,4},{1,5},{2,6},{3,7},{4,0},{5,1},{6,2},{7,3},{8,12},{9,13},{10,... | collective-permute-start | bytes 49160 | tf_op jit(solution)/shard_map/ppermute | solution.py:606
  98.6 4.0 %collective-permute-start.21 = (f32[4096]{0:T(1024)S(1)}, f32[4096]{0:T(1024)S(1)}, u32[]{:S(2)}, u32[]{:S(2)}) collective-permute-start(f32[4096]{0:T(1024)S(1)} %bitcast.38), channel_id=1, source_target_pairs={{0,2},{1,3},{2,0},{3,1},{4,6},{5,7},{6,4},{7,5},{8,10},{9,11},{10,... | collective-permute-start | bytes 49160 | tf_op jit(solution)/shard_map/ppermute | solution.py:606
  106.4 4.6 %collective-permute-start.26 = (f32[2048]{0:T(1024)S(1)}, f32[2048]{0:T(1024)S(1)}, u32[]{:S(2)}, u32[]{:S(2)}) collective-permute-start(f32[2048]{0:T(1024)S(1)} %bitcast.39), channel_id=1, source_target_pairs={{0,17},{1,16},{2,19},{3,18},{4,21},{5,20},{6,23},{7,22},{8,25},{9,... | collective-permute-start | bytes 24584 | tf_op jit(solution)/shard_map/ppermute | solution.py:606
  108.0 3.7 %collective-permute-start.25 = (f32[2048]{0:T(1024)S(1)}, f32[2048]{0:T(1024)S(1)}, u32[]{:S(2)}, u32[]{:S(2)}) collective-permute-start(f32[2048]{0:T(1024)S(1)} %bitcast.40), channel_id=1, source_target_pairs={{0,16},{1,17},{2,18},{3,19},{4,20},{5,21},{6,22},{7,23},{8,24},{9,... | collective-permute-start | bytes 24584 | tf_op jit(solution)/shard_map/ppermute | solution.py:606
  110.0 3.7 %collective-permute-start.24 = (f32[2048]{0:T(1024)S(1)}, f32[2048]{0:T(1024)S(1)}, u32[]{:S(2)}, u32[]{:S(2)}) collective-permute-start(f32[2048]{0:T(1024)S(1)} %bitcast.41), channel_id=1, source_target_pairs={{0,1},{1,0},{2,3},{3,2},{4,5},{5,4},{6,7},{7,6},{8,9},{9,8},{10,11... | collective-permute-start | bytes 24584 | tf_op jit(solution)/shard_map/ppermute | solution.py:606
  116.0 1.2 collective-permute-start.27
  120.4 7.7 %collective-permute-start.28 = (bf16[1024,128]{1,0:T(8,128)(2,1)S(1)}, bf16[1024,128]{1,0:T(8,128)(2,1)S(1)}, u32[]{:S(2)}, u32[]{:S(2)}) collective-permute-start(bf16[1024,128]{1,0:T(8,128)(2,1)S(1)} %get-tuple-element.75), channel_id=1, source_target_pairs={{0,8},{1,9},{2,10},{3,11},{4,12},{5,13},{6,14},{7,15},{8,0},{9,1},... | collective-permute-start | bytes 786440 | tf_op jit(solution)/shard_map/ppermute | solution.py:606
  120.7 8.7 %collective-permute-start.31 = (f32[4096]{0:T(1024)S(1)}, f32[4096]{0:T(1024)S(1)}, u32[]{:S(2)}, u32[]{:S(2)}) collective-permute-start(f32[4096]{0:T(1024)S(1)} %bitcast.47), channel_id=1, source_target_pairs={{0,6},{1,7},{2,4},{3,5},{4,2},{5,3},{6,0},{7,1},{8,14},{9,15},{10,... | collective-permute-start | bytes 49160 | tf_op jit(solution)/shard_map/ppermute | solution.py:606
  122.1 8.5 %collective-permute-start.30 = (f32[4096]{0:T(1024)S(1)}, f32[4096]{0:T(1024)S(1)}, u32[]{:S(2)}, u32[]{:S(2)}) collective-permute-start(f32[4096]{0:T(1024)S(1)} %bitcast.48), channel_id=1, source_target_pairs={{0,4},{1,5},{2,6},{3,7},{4,0},{5,1},{6,2},{7,3},{8,12},{9,13},{10,... | collective-permute-start | bytes 49160 | tf_op jit(solution)/shard_map/ppermute | solution.py:606
  122.8 7.8 %collective-permute-start.29 = (f32[4096]{0:T(1024)S(1)}, f32[4096]{0:T(1024)S(1)}, u32[]{:S(2)}, u32[]{:S(2)}) collective-permute-start(f32[4096]{0:T(1024)S(1)} %bitcast.49), channel_id=1, source_target_pairs={{0,2},{1,3},{2,0},{3,1},{4,6},{5,7},{6,4},{7,5},{8,10},{9,11},{10,... | collective-permute-start | bytes 49160 | tf_op jit(solution)/shard_map/ppermute | solution.py:606
  128.0 4.6 %collective-permute-start.32 = (bf16[1024,128]{1,0:T(8,128)(2,1)S(1)}, bf16[1024,128]{1,0:T(8,128)(2,1)S(1)}, u32[]{:S(2)}, u32[]{:S(2)}) collective-permute-start(bf16[1024,128]{1,0:T(8,128)(2,1)S(1)} %get-tuple-element.83), channel_id=1, source_target_pairs={{0,8},{1,9},{2,10},{3,11},{4,12},{5,13},{6,14},{7,15},{8,0},{9,1},... | collective-permute-start | bytes 786440 | tf_op jit(solution)/shard_map/ppermute | solution.py:606
  128.2 14.0 %collective-permute-start.37 = (bf16[512,128]{1,0:T(8,128)(2,1)S(1)}, bf16[512,128]{1,0:T(8,128)(2,1)S(1)}, u32[]{:S(2)}, u32[]{:S(2)}) collective-permute-start(bf16[512,128]{1,0:T(8,128)(2,1)S(1)} %get-tuple-element.96), channel_id=1, source_target_pairs={{0,4},{1,5},{2,6},{3,7},{4,0},{5,1},{6,2},{7,3},{8,12},{9,13},{10,... | collective-permute-start | bytes 393224 | tf_op jit(solution)/shard_map/ppermute | solution.py:606
  129.4 12.8 %collective-permute-start.38 = (bf16[512,128]{1,0:T(8,128)(2,1)S(1)}, bf16[512,128]{1,0:T(8,128)(2,1)S(1)}, u32[]{:S(2)}, u32[]{:S(2)}) collective-permute-start(bf16[512,128]{1,0:T(8,128)(2,1)S(1)} %get-tuple-element.97), channel_id=1, source_target_pairs={{0,6},{1,7},{2,4},{3,5},{4,2},{5,3},{6,0},{7,1},{8,14},{9,15},{10,... | collective-permute-start | bytes 393224 | tf_op jit(solution)/shard_map/ppermute | solution.py:606
  132.7 10.2 %collective-permute-start.36 = (bf16[512,128]{1,0:T(8,128)(2,1)S(1)}, bf16[512,128]{1,0:T(8,128)(2,1)S(1)}, u32[]{:S(2)}, u32[]{:S(2)}) collective-permute-start(bf16[512,128]{1,0:T(8,128)(2,1)S(1)} %get-tuple-element.95), channel_id=1, source_target_pairs={{0,2},{1,3},{2,0},{3,1},{4,6},{5,7},{6,4},{7,5},{8,10},{9,11},{10,... | collective-permute-start | bytes 393224 | tf_op jit(solution)/shard_map/ppermute | solution.py:606
  133.9 5.9 %collective-permute-start.33 = (bf16[512,128]{1,0:T(8,128)(2,1)S(1)}, bf16[512,128]{1,0:T(8,128)(2,1)S(1)}, u32[]{:S(2)}, u32[]{:S(2)}) collective-permute-start(bf16[512,128]{1,0:T(8,128)(2,1)S(1)} %get-tuple-element.90), channel_id=1, source_target_pairs={{0,17},{1,16},{2,19},{3,18},{4,21},{5,20},{6,23},{7,22},{8,25},{9,... | collective-permute-start | bytes 393224 | tf_op jit(solution)/shard_map/ppermute | solution.py:606
  139.9 5.0 %collective-permute-start.34 = (bf16[512,128]{1,0:T(8,128)(2,1)S(1)}, bf16[512,128]{1,0:T(8,128)(2,1)S(1)}, u32[]{:S(2)}, u32[]{:S(2)}) collective-permute-start(bf16[512,128]{1,0:T(8,128)(2,1)S(1)} %get-tuple-element.91), channel_id=1, source_target_pairs={{0,1},{1,0},{2,3},{3,2},{4,5},{5,4},{6,7},{7,6},{8,9},{9,8},{10,11... | collective-permute-start | bytes 393224 | tf_op jit(solution)/shard_map/ppermute | solution.py:606
  139.9 5.0 %collective-permute-start.35 = (bf16[512,128]{1,0:T(8,128)(2,1)S(1)}, bf16[512,128]{1,0:T(8,128)(2,1)S(1)}, u32[]{:S(2)}, u32[]{:S(2)}) collective-permute-start(bf16[512,128]{1,0:T(8,128)(2,1)S(1)} %get-tuple-element.92), channel_id=1, source_target_pairs={{0,16},{1,17},{2,18},{3,19},{4,20},{5,21},{6,22},{7,23},{8,24},{9,... | collective-permute-start | bytes 393224 | tf_op jit(solution)/shard_map/ppermute | solution.py:606

commit v15 on v14

--- a/solution.py
+++ b/solution.py
@@ -112,7 +112,7 @@
 
         if m == 0:
             tops = [exponents(0, q) for q in range(tiles)]
-            for g in range(1, 128 // group):
+            for g in range(1, 32 // group):
                 tops = [jnp.maximum(top, exponents(g, q)) for q, top in enumerate(tops)]
             state = [(jnp.max(top, axis=0, keepdims=True), jnp.zeros((group, 128), jnp.float32)) for top in tops]
         for g in range(chunk // group):
@@ -226,19 +226,21 @@
 
 def row_sums(width, e_ref, w_ref, w16_ref, acc_ref, o_ref):
     rows, cols = e_ref.shape
-    half = rows - acc_ref.shape[0]
-    for at in range(0, half, width):
+    split = rows - acc_ref.shape[0]
+    blocks = list(range(0, rows - split, 64))
+    dots = list(range(0, split, width))
+    for n, at in enumerate(dots):
         got = lax.dot_general(w16_ref[...], e_ref[at:at + width, :], NT, preferred_element_type=jnp.float32)
-        for k in range(at, at + width, 64):
+        for k in blocks[n * len(blocks) // len(dots):(n + 1) * len(blocks) // len(dots)]:
             total = jnp.zeros((64, 128), jnp.float32)
             for q in range(0, cols, 128):
-                e = e_ref[half + k:half + k + 64, q:q + 128].astype(jnp.float32)
+                e = e_ref[split + k:split + k + 64, q:q + 128].astype(jnp.float32)
                 total = total + e * w_ref[:, q:q + 128]
             acc_ref[k:k + 64, :] = total
         o_ref[:, at:at + width] = jnp.sum(got, axis=0, keepdims=True)
-    for at in range(0, rows - half, 128):
+    for at in range(0, rows - split, 128):
         total = jnp.sum(jnp.transpose(acc_ref[at:at + 128, :]), axis=0, keepdims=True)
-        o_ref[:, half + at:half + at + 128] = total
+        o_ref[:, split + at:split + at + 128] = total
 
 
 def first_row_kernel(width, shifts, parts, e_ref, shift_ref, *refs):
@@ -285,7 +287,8 @@
     width = 512 if kernel is column_kernel else 256
     scratch = [pltpu.VMEM((16, size), jnp.bfloat16)]
     if kernel is not column_kernel:
-        scratch.append(pltpu.VMEM((e.shape[0] // 2, 128), jnp.float32))
+        part = 3 if kernel is row_kernel else 1
+        scratch.append(pltpu.VMEM((e.shape[0] * part // 4, 128), jnp.float32))
     if kernel is row_kernel:
         scratch.append(pltpu.VMEM((1, size), jnp.float32))
     return pl.pallas_call(
@@ -674,7 +677,6 @@
     parts = [swap(part, along[z + 1]) for z, part in enumerate(parts)]
     last = swap(last, across[na - 1])
     sent = other_rows(list(range(1, na - 1)), share_x, x, yb, e, alpha, jnp.bfloat16)
-    sent, last = lax.optimization_barrier((sent, last))
     sent = [swap(part, across[s + 1]) for s, part in enumerate(sent)] + [last]
     gi, = other_rows([0], share_x, x, yb, e, alpha, jnp.float32)
     grad_imu, grad_cam = add_up([gi, *sent], [grad_cam, *parts, *far_gc], scale)

time: 146 us -> 147 us (level)
  starting transfers between devices: 39.5 us -> 42.1 us
  waiting for transfers between devices: 24.1 us -> 22.2 us
    ppermute x39, starting transfers between devices: 39.5 us -> 42.1 us  [swap(): lax.ppermute(value, ('row', 'col'), [(i, i ^ mask) for i in range(self.co...]
    ppermute x39, waiting for transfers between devices: 24.1 us -> 22.2 us  [swap(): lax.ppermute(value, ('row', 'col'), [(i, i ^ mask) for i in range(self.co...]
  transfers between devices with their start and end apart: 39 -> 39, of which waited for: 19 -> 20; matrix products, arithmetic and copies ran while one was open for 1% -> 1% of each run, Pallas kernels for 15% -> 15%
where the time goes in v15:
time: 147 us; the launch traced here: 146 us
  Pallas kernels  79.2 us (54%)
  starting transfers between devices  42.1 us (29%)
  waiting for transfers between devices  22.2 us (15%)
    ppermute x39, starting transfers between devices, swap(): lax.ppermute(value, ('row', 'col'), [(i, i ^ mask) for i in range(self.co...  42.1 us
    pallas_call x1, Pallas kernels, column_lse(): pl.pallas_call(functools.partial(column_lse_kernel, width, chunk, len(got...  30 us
    ppermute x39, waiting for transfers between devices, swap(): lax.ppermute(value, ('row', 'col'), [(i, i ^ mask) for i in range(self.co...  22.2 us
    pallas_call x4, Pallas kernels, weighted(): pl.pallas_call(functools.partial(kernel, width, tuple(shifts), parts), ou...  12.8 us
    pallas_call x1, Pallas kernels, row_lse_late(): pl.pallas_call(functools.partial(row_lse_late_kernel, width, len(ys)), ou...  9.94 us
    pallas_call x1, Pallas kernels, row_lse_middle(): pl.pallas_call(functools.partial(row_lse_middle_kernel, width, len(ys)),...  6.45 us
    pallas_call x1, Pallas kernels, row_lse_early(): pl.pallas_call(functools.partial(row_lse_early_kernel, width, len(xs)), o...  6.45 us
    pallas_call x2, Pallas kernels, column_grad(): pl.pallas_call(functools.partial(kernel, blocks, share), out_shape=out_sh...  6.19 us
  transfers between devices with their start and end apart: 39, of which 20 were waited for; matrix products, arithmetic and copies ran while one was open for 1% of the time, Pallas kernels for 15%

profile of v15, /device:TPU:0, one launch (start us, length us, event | category | flops | bytes accessed | tf_op | source)
XLA Modules:
  0.0 146.2 jit_solution(12582513806555104450)
XLA Ops:
  0.6 3.0 %collective-permute-start = (bf16[512,128]{1,0:T(8,128)(2,1)}, bf16[512,128]{1,0:T(8,128)(2,1)S(1)}, u32[]{:S(2)}, u32[]{:S(2)}) collective-permute-start(bf16[512,128]{1,0:T(8,128)(2,1)} %param.4), channel_id=1, source_target_pairs={{0,1},{1,0},{2,3},{3,2},{4,5},{5,4},{6,7},{7,6},{8,9},{9,8},{10,11... | collective-permute-start | bytes 393224 | tf_op jit(solution)/shard_map/ppermute | solution.py:609
  3.7 1.4 collective-permute-start.2
  5.2 3.0 %collective-permute-start.4 = (bf16[512,128]{1,0:T(8,128)(2,1)}, bf16[512,128]{1,0:T(8,128)(2,1)S(1)}, u32[]{:S(2)}, u32[]{:S(2)}) collective-permute-start(bf16[512,128]{1,0:T(8,128)(2,1)} %bitcast.77), channel_id=1, source_target_pairs={{0,4},{1,5},{2,6},{3,7},{4,0},{5,1},{6,2},{7,3},{8,12},{9,13},{10,... | collective-permute-start | bytes 393224 | tf_op jit(solution)/shard_map/ppermute | solution.py:609
  10.2 1.6 %collective-permute-start.5 = (bf16[512,128]{1,0:T(8,128)(2,1)}, bf16[512,128]{1,0:T(8,128)(2,1)S(1)}, u32[]{:S(2)}, u32[]{:S(2)}) collective-permute-start(bf16[512,128]{1,0:T(8,128)(2,1)} %bitcast.80), channel_id=1, source_target_pairs={{0,2},{1,3},{2,0},{3,1},{4,6},{5,7},{6,4},{7,5},{8,10},{9,11},{10,... | collective-permute-start | bytes 393224 | tf_op jit(solution)/shard_map/ppermute | solution.py:609
  11.8 6.4 %row_lse_early.1 = (bf16[2048,128]{1,0:T(8,128)(2,1)S(1)}, bf16[128,2048]{1,0:T(8,128)(2,1)S(1)}, f32[1,2048]{1,0:T(1,128)S(1)}) custom-call(bf16[1024,128]{1,0:T(8,128)(2,1)S(1)} %pad_maximum_fusion.own_ref, bf16[512,128]{1,0:T(8,128)(2,1)S(1)} %collective-permute-done.refs_0_, bf16[512,128]{1,0:T(8,128)(2,1)S(1)} %collective-permute-done.1.refs_1_, ...), custom_call_target="tpu_custom_call" | custom-call | flops 536870912 | bytes 786432 | tf_op jit(solution)/shard_map/row_lse_early/pallas_call | solution.py:325
  18.3 1.4 collective-permute-start.6
  20.2 6.5 %row_lse_middle.1.first_ref = f32[1,2048]{1,0:T(1,128)S(1)} custom-call(bf16[2048,128]{1,0:T(8,128)(2,1)S(1)} %get-tuple-element.50.x_ref, f32[1,2048]{1,0:T(1,128)S(1)} %get-tuple-element.53.first_ref, bf16[512,128]{1,0:T(8,128)(2,1)S(1)} %collective-permute-done.5.refs_0_, bf16[512,128]{1,0:T(8,128)(2,1)S(1)} %collective-permute-done.4.refs_1_), custom_call_target="tpu_custom_call" | custom-call | flops 536870912 | bytes 786432 | tf_op jit(solution)/shard_map/row_lse_middle/pallas_call | solution.py:340
  26.8 1.3 collective-permute-done.9.refs_6_
  28.1 9.9 %row_lse_late.1 = (bf16[4096,128]{1,0:T(8,128)(2,1)S(1)}, f32[1,3072]{1,0:T(1,128)S(1)}) custom-call(bf16[1024,128]{1,0:T(8,128)(2,1)S(1)} %pad_maximum_fusion.own_ref, f32[1,2048]{1,0:T(1,128)S(1)} %bitcast.66, bf16[2048,128]{1,0:T(8,128)(2,1)S(1)} %get-tuple-element.50.x_ref, f32[1,2048]{1,0:T(1,128)S(1)} %row_lse_middle.1.first_ref, ...), custom_call_target="tpu_custom_call" | custom-call | flops 1073741824 | bytes 1048576 | tf_op jit(solution)/shard_map/row_lse_late/pallas_call | solution.py:359
  38.2 3.4 %collective-permute-start.10 = (f32[3072]{0:T(1024)S(1)}, f32[3072]{0:T(1024)S(1)}, u32[]{:S(2)}, u32[]{:S(2)}) collective-permute-start(f32[3072]{0:T(1024)S(1)} %bitcast.73), channel_id=1, source_target_pairs={{0,1},{1,0},{2,3},{3,2},{4,5},{5,4},{6,7},{7,6},{8,9},{9,8},{10,11... | collective-permute-start | bytes 36872 | tf_op jit(solution)/shard_map/ppermute | solution.py:609
  41.6 1.1 collective-permute-done.12
  43.3 30.0 %column_lse.1 = (f32[1,5120]{1,0:T(1,128)S(1)}, bf16[2048,4096]{1,0:T(8,128)(2,1)S(1)}, f32[1,4096]{1,0:T(1,128)S(1)}, f32[1,2048]{1,0:T(1,128)S(1)}) custom-call(bf16[2048,128]{1,0:T(8,128)(2,1)S(1)} %get-tuple-element.50.x_ref, bf16[4096,128]{1,0:T(8,128)(2,1)S(1)} %get-tuple-element.57.y_ref, f32[1,2048]{1,0:T(1,128)S(1)} %bitcast.67, ...), custom_call_target="tpu_custom_call" | custom-call | flops 2147483648 | bytes 1572864 | tf_op jit(solution)/shard_map/column_lse/pallas_call | solution.py:373
  73.4 1.2 collective-permute-done.13
  74.7 1.5 %collective-permute-start.16 = (f32[5120]{0:T(1024)S(1)}, f32[5120]{0:T(1024)S(1)}, u32[]{:S(2)}, u32[]{:S(2)}) collective-permute-start(f32[5120]{0:T(1024)S(1)} %bitcast.33), channel_id=1, source_target_pairs={{0,6},{1,7},{2,4},{3,5},{4,2},{5,3},{6,0},{7,1},{8,14},{9,15},{10,... | collective-permute-start | bytes 61448 | tf_op jit(solution)/shard_map/ppermute | solution.py:609
  76.2 1.5 %collective-permute-start.15 = (f32[5120]{0:T(1024)S(1)}, f32[5120]{0:T(1024)S(1)}, u32[]{:S(2)}, u32[]{:S(2)}) collective-permute-start(f32[5120]{0:T(1024)S(1)} %bitcast.34), channel_id=1, source_target_pairs={{0,4},{1,5},{2,6},{3,7},{4,0},{5,1},{6,2},{7,3},{8,12},{9,13},{10,... | collective-permute-start | bytes 61448 | tf_op jit(solution)/shard_map/ppermute | solution.py:609
  77.8 1.4 collective-permute-start.14
  79.1 1.2 collective-permute-done.16
  81.5 4.1 %weighted_sum.4 = (f32[1,2048]{1,0:T(1,128)S(1)}, f32[1,4096]{1,0:T(1,128)S(1)}, f32[1,4096]{1,0:T(1,128)S(1)}) custom-call(bf16[2048,4096]{1,0:T(8,128)(2,1)S(1)} %get-tuple-element.59.e_ref, f32[1,4096]{1,0:T(1,128)S(1)} %get-tuple-element.62.shift_ref, f32[1,5120]{1,0:T(1,128)S(1)} %pair.3.refs_0_, f32[1,5120]{1,0:T(1,128)S(1)} %bitcast.44, ...), custom_call_target="tpu_custom_call" | custom-call | flops 16777216 | bytes 16777216 | tf_op jit(solution)/shard_map/weighted_sum/pallas_call | solution.py:294
  85.6 2.2 %collective-permute-start.19 = (f32[2048]{0:T(1024)S(1)}, f32[2048]{0:T(1024)S(1)}, u32[]{:S(2)}, u32[]{:S(2)}) collective-permute-start(f32[2048]{0:T(1024)S(1)} %bitcast.57), channel_id=1, source_target_pairs={{0,17},{1,16},{2,19},{3,18},{4,21},{5,20},{6,23},{7,22},{8,25},{9,... | collective-permute-start | bytes 24584 | tf_op jit(solution)/shard_map/ppermute | solution.py:609
  89.2 1.1 collective-permute-done.19
  90.2 1.2 collective-permute-done.18
  92.2 2.8 %weighted_sum.5 = (f32[1,4096]{1,0:T(1,128)S(1)}, f32[1,2048]{1,0:T(1,128)}) custom-call(bf16[2048,4096]{1,0:T(8,128)(2,1)S(1)} %get-tuple-element.59.e_ref, f32[1,2048]{1,0:T(1,128)S(1)} %get-tuple-element.61.a_ref, f32[1,4096]{1,0:T(1,128)S(1)} %get-tuple-element.64.first_ref, f32[1,2048]{1,0:T(1,128)S(1)} %get-tuple-element.66.refs_0_, ...), custom_call_target="tpu_custom_call" | custom-call | flops 16777216 | bytes 16777216 | tf_op jit(solution)/shard_map/weighted_sum/pallas_call | solution.py:294
  94.9 1.2 collective-permute-done.20
  96.1 2.4 %collective-permute-start.23 = (f32[4096]{0:T(1024)S(1)}, f32[4096]{0:T(1024)S(1)}, u32[]{:S(2)}, u32[]{:S(2)}) collective-permute-start(f32[4096]{0:T(1024)S(1)} %bitcast.36), channel_id=1, source_target_pairs={{0,6},{1,7},{2,4},{3,5},{4,2},{5,3},{6,0},{7,1},{8,14},{9,15},{10,... | collective-permute-start | bytes 49160 | tf_op jit(solution)/shard_map/ppermute | solution.py:609
  98.6 1.1 collective-permute-start.22
  100.6 1.2 collective-permute-done.23
  101.7 1.5 collective-permute-done.22
  103.4 3.6 %weighted_sum.6.refs_0_ = f32[1,2048]{1,0:T(1,128)S(1)} custom-call(bf16[2048,4096]{1,0:T(8,128)(2,1)S(1)} %get-tuple-element.59.e_ref, f32[1,4096]{1,0:T(1,128)S(1)} %get-tuple-element.64.first_ref, f32[1,4096]{1,0:T(1,128)S(1)} %get-tuple-element.65.b_ref, f32[1,4096]{1,0:T(1,128)S(1)} %pair.4.refs_0_, f32[1,4096]{1,0:T(1,128)S(1)} %bitcast.56, ...), custom_call_target="tpu_custom_call" | custom-call | flops 16777216 | bytes 16777216 | tf_op jit(solution)/shard_map/weighted_sum/pallas_call | solution.py:294
  107.6 1.9 %collective-permute-start.25 = (f32[2048]{0:T(1024)S(1)}, f32[2048]{0:T(1024)S(1)}, u32[]{:S(2)}, u32[]{:S(2)}) collective-permute-start(f32[2048]{0:T(1024)S(1)} %bitcast.40), channel_id=1, source_target_pairs={{0,16},{1,17},{2,18},{3,19},{4,20},{5,21},{6,22},{7,23},{8,24},{9,... | collective-permute-start | bytes 24584 | tf_op jit(solution)/shard_map/ppermute | solution.py:609
  109.5 1.1 collective-permute-start.24
  110.6 1.1 collective-permute-done.26
  111.7 1.5 %collective-permute-done.24 = f32[2048]{0:T(1024)S(1)} collective-permute-done((f32[2048]{0:T(1024)S(1)}, f32[2048]{0:T(1024)S(1)}, u32[]{:S(2)}, u32[]{:S(2)}) %collective-permute-start.24) | collective-permute-done | bytes 8224 | tf_op jit(solution)/shard_map/ppermute | solution.py:609
  113.2 2.3 %weighted_sum.7 = (f32[1,4096]{1,0:T(1,128)S(1)}, f32[1,2048]{1,0:T(1,128)S(1)}) custom-call(bf16[2048,4096]{1,0:T(8,128)(2,1)S(1)} %get-tuple-element.59.e_ref, f32[1,2048]{1,0:T(1,128)S(1)} %get-tuple-element.61.a_ref, f32[1,4096]{1,0:T(1,128)S(1)} %get-tuple-element.64.first_ref, f32[1,2048]{1,0:T(1,128)S(1)} %weighted_sum.6.refs_0_, ...), custom_call_target="tpu_custom_call" | custom-call | flops 16777216 | bytes 16777216 | tf_op jit(solution)/shard_map/weighted_sum/pallas_call | solution.py:294
  115.6 1.2 collective-permute-done.27
  116.7 3.2 %column_grad.2 = (f32[1024,128]{1,0:T(8,128)S(1)}, bf16[1024,128]{1,0:T(8,128)(2,1)S(1)}, bf16[256,2048]{1,0:T(8,128)(2,1)S(1)}) custom-call(bf16[128,2048]{1,0:T(8,128)(2,1)S(1)} %get-tuple-element.60.xt_ref, bf16[4096,128]{1,0:T(8,128)(2,1)S(1)} %get-tuple-element.57.y_ref, bf16[2048,4096]{1,0:T(8,128)(2,1)S(1)} %get-tuple-element.59.e_ref, ...), custom_call_target="tpu_custom_call" | custom-call | flops 2147483648 | bytes 8388608 | tf_op jit(solution)/shard_map/column_grad/pallas_call | solution.py:455
  120.2 1.5 %collective-permute-start.31 = (f32[4096]{0:T(1024)S(1)}, f32[4096]{0:T(1024)S(1)}, u32[]{:S(2)}, u32[]{:S(2)}) collective-permute-start(f32[4096]{0:T(1024)S(1)} %bitcast.47), channel_id=1, source_target_pairs={{0,6},{1,7},{2,4},{3,5},{4,2},{5,3},{6,0},{7,1},{8,14},{9,15},{10,... | collective-permute-start | bytes 49160 | tf_op jit(solution)/shard_map/ppermute | solution.py:609
  122.3 2.3 %collective-permute-start.29 = (f32[4096]{0:T(1024)S(1)}, f32[4096]{0:T(1024)S(1)}, u32[]{:S(2)}, u32[]{:S(2)}) collective-permute-start(f32[4096]{0:T(1024)S(1)} %bitcast.49), channel_id=1, source_target_pairs={{0,2},{1,3},{2,0},{3,1},{4,6},{5,7},{6,4},{7,5},{8,10},{9,11},{10,... | collective-permute-start | bytes 49160 | tf_op jit(solution)/shard_map/ppermute | solution.py:609
  124.6 3.0 %column_grad.3 = (f32[1024,128]{1,0:T(8,128)S(1)}, bf16[1024,128]{1,0:T(8,128)(2,1)S(1)}) custom-call(bf16[256,2048]{1,0:T(8,128)(2,1)S(1)} %get-tuple-element.78.xa_ref, bf16[4096,128]{1,0:T(8,128)(2,1)S(1)} %get-tuple-element.57.y_ref, bf16[2048,4096]{1,0:T(8,128)(2,1)S(1)} %get-tuple-element.59.e_ref, f32[1,4096]{1,0:T(1,128)S(1)} %get-tuple-element.64.first_ref), custom_call_target="tpu_custom_call" | custom-call | flops 2147483648 | bytes 8388608 | tf_op jit(solution)/shard_map/column_grad/pallas_call | solution.py:455
  127.7 1.2 collective-permute-start.37
  128.9 1.2 collective-permute-start.38
  130.1 2.1 %first_rows.1 = (bf16[4096,256]{1,0:T(8,128)(2,1)S(1)}, f32[1,512]{1,0:T(1,128)S(1)}, bf16[512,128]{1,0:T(8,128)(2,1)S(1)}) custom-call(bf16[2048,128]{1,0:T(8,128)(2,1)S(1)} %get-tuple-element.50.x_ref, bf16[4096,128]{1,0:T(8,128)(2,1)S(1)} %get-tuple-element.57.y_ref, bf16[2048,4096]{1,0:T(8,128)(2,1)S(1)} %get-tuple-element.59.e_ref, ...), custom_call_target="tpu_custom_call" | custom-call | flops 34359738368 | bytes 134217728 | tf_op jit(solution)/shard_map/first_rows/pallas_call | solution.py:529
  132.3 1.2 collective-permute-start.36
  134.2 2.6 %other_rows.3 = (bf16[512,128]{1,0:T(8,128)(2,1)S(1)}, bf16[512,128]{1,0:T(8,128)(2,1)S(1)}) custom-call(bf16[2048,128]{1,0:T(8,128)(2,1)S(1)} %get-tuple-element.50.x_ref, bf16[4096,256]{1,0:T(8,128)(2,1)S(1)} %get-tuple-element.84.yb_ref, bf16[2048,4096]{1,0:T(8,128)(2,1)S(1)} %get-tuple-element.59.e_ref, f32[1,2048]{1,0:T(1,128)S(1)} %get-tuple-element.75.alpha_ref), custom_call_target="tpu_custom_call" | custom-call | flops 2147483648 | bytes 8388608 | tf_op jit(solution)/shard_map/other_rows/pallas_call | solution.py:547
  137.8 2.0 %collective-permute-done.37.refs_6_ = bf16[512,128]{1,0:T(8,128)(2,1)S(1)} collective-permute-done((bf16[512,128]{1,0:T(8,128)(2,1)S(1)}, bf16[512,128]{1,0:T(8,128)(2,1)S(1)}, u32[]{:S(2)}, u32[]{:S(2)}) %collective-permute-start.37) | collective-permute-done | bytes 131104 | tf_op jit(solution)/shard_map/ppermute | solution.py:609
  139.7 1.1 collective-permute-start.34
  140.8 1.4 other_rows.2.refs_0_
  142.4 2.7 %collective-permute-done.34.refs_2_ = bf16[512,128]{1,0:T(8,128)(2,1)S(1)} collective-permute-done((bf16[512,128]{1,0:T(8,128)(2,1)S(1)}, bf16[512,128]{1,0:T(8,128)(2,1)S(1)}, u32[]{:S(2)}, u32[]{:S(2)}) %collective-permute-start.34) | collective-permute-done | bytes 131104 | tf_op jit(solution)/shard_map/ppermute | solution.py:609
  145.1 1.1 add_up.1
  (52 shorter events, 11.6 us)
Async XLA Ops:
  0.6 9.5 %collective-permute-start = (bf16[512,128]{1,0:T(8,128)(2,1)}, bf16[512,128]{1,0:T(8,128)(2,1)S(1)}, u32[]{:S(2)}, u32[]{:S(2)}) collective-permute-start(bf16[512,128]{1,0:T(8,128)(2,1)} %param.4), channel_id=1, source_target_pairs={{0,1},{1,0},{2,3},{3,2},{4,5},{5,4},{6,7},{7,6},{8,9},{9,8},{10,11... | collective-permute-start | bytes 393224 | tf_op jit(solution)/shard_map/ppermute | solution.py:609
  3.7 8.2 %collective-permute-start.2 = (bf16[512,128]{1,0:T(8,128)(2,1)}, bf16[512,128]{1,0:T(8,128)(2,1)S(1)}, u32[]{:S(2)}, u32[]{:S(2)}) collective-permute-start(bf16[512,128]{1,0:T(8,128)(2,1)} %param.4), channel_id=1, source_target_pairs={{0,17},{1,16},{2,19},{3,18},{4,21},{5,20},{6,23},{7,22},{8,25},{9,... | collective-permute-start | bytes 393224 | tf_op jit(solution)/shard_map/ppermute | solution.py:609
  5.1 6.7 %collective-permute-start.1 = (bf16[512,128]{1,0:T(8,128)(2,1)}, bf16[512,128]{1,0:T(8,128)(2,1)S(1)}, u32[]{:S(2)}, u32[]{:S(2)}) collective-permute-start(bf16[512,128]{1,0:T(8,128)(2,1)} %param.4), channel_id=1, source_target_pairs={{0,16},{1,17},{2,18},{3,19},{4,20},{5,21},{6,22},{7,23},{8,24},{9,... | collective-permute-start | bytes 393224 | tf_op jit(solution)/shard_map/ppermute | solution.py:609
  5.2 13.1 %collective-permute-start.4 = (bf16[512,128]{1,0:T(8,128)(2,1)}, bf16[512,128]{1,0:T(8,128)(2,1)S(1)}, u32[]{:S(2)}, u32[]{:S(2)}) collective-permute-start(bf16[512,128]{1,0:T(8,128)(2,1)} %bitcast.77), channel_id=1, source_target_pairs={{0,4},{1,5},{2,6},{3,7},{4,0},{5,1},{6,2},{7,3},{8,12},{9,13},{10,... | collective-permute-start | bytes 393224 | tf_op jit(solution)/shard_map/ppermute | solution.py:609
  9.2 2.6 %collective-permute-start.3 = (bf16[512,128]{1,0:T(8,128)(2,1)}, bf16[512,128]{1,0:T(8,128)(2,1)S(1)}, u32[]{:S(2)}, u32[]{:S(2)}) collective-permute-start(bf16[512,128]{1,0:T(8,128)(2,1)} %bitcast.79), channel_id=1, source_target_pairs={{0,8},{1,9},{2,10},{3,11},{4,12},{5,13},{6,14},{7,15},{8,0},{9,1},... | collective-permute-start | bytes 393224 | tf_op jit(solution)/shard_map/ppermute | solution.py:609
  10.2 9.6 %collective-permute-start.5 = (bf16[512,128]{1,0:T(8,128)(2,1)}, bf16[512,128]{1,0:T(8,128)(2,1)S(1)}, u32[]{:S(2)}, u32[]{:S(2)}) collective-permute-start(bf16[512,128]{1,0:T(8,128)(2,1)} %bitcast.80), channel_id=1, source_target_pairs={{0,2},{1,3},{2,0},{3,1},{4,6},{5,7},{6,4},{7,5},{8,10},{9,11},{10,... | collective-permute-start | bytes 393224 | tf_op jit(solution)/shard_map/ppermute | solution.py:609
  18.3 8.4 %collective-permute-start.6 = (bf16[512,128]{1,0:T(8,128)(2,1)S(1)}, bf16[512,128]{1,0:T(8,128)(2,1)S(1)}, u32[]{:S(2)}, u32[]{:S(2)}) collective-permute-start(bf16[512,128]{1,0:T(8,128)(2,1)S(1)} %collective-permute-done.4.refs_1_), channel_id=1, source_target_pairs={{0,2},{1,3},{2,0},{3,1},{4,6},{5,7},{6,4},{7,5},{8,10},{9,11},{10,... | collective-permute-start | bytes 393224 | tf_op jit(solution)/shard_map/ppermute | solution.py:609
  19.7 7.1 %collective-permute-start.8 = (bf16[512,128]{1,0:T(8,128)(2,1)S(1)}, bf16[512,128]{1,0:T(8,128)(2,1)S(1)}, u32[]{:S(2)}, u32[]{:S(2)}) collective-permute-start(bf16[512,128]{1,0:T(8,128)(2,1)S(1)} %collective-permute-done.4.refs_1_), channel_id=1, source_target_pairs={{0,8},{1,9},{2,10},{3,11},{4,12},{5,13},{6,14},{7,15},{8,0},{9,1},... | collective-permute-start | bytes 393224 | tf_op jit(solution)/shard_map/ppermute | solution.py:609
  19.7 7.1 %collective-permute-start.7 = (bf16[512,128]{1,0:T(8,128)(2,1)S(1)}, bf16[512,128]{1,0:T(8,128)(2,1)S(1)}, u32[]{:S(2)}, u32[]{:S(2)}) collective-permute-start(bf16[512,128]{1,0:T(8,128)(2,1)S(1)} %collective-permute-done.5.refs_0_), channel_id=1, source_target_pairs={{0,8},{1,9},{2,10},{3,11},{4,12},{5,13},{6,14},{7,15},{8,0},{9,1},... | collective-permute-start | bytes 393224 | tf_op jit(solution)/shard_map/ppermute | solution.py:609
  26.7 1.4 collective-permute-start.9
  38.1 4.7 %collective-permute-start.12 = (f32[3072]{0:T(1024)S(1)}, f32[3072]{0:T(1024)S(1)}, u32[]{:S(2)}, u32[]{:S(2)}) collective-permute-start(f32[3072]{0:T(1024)S(1)} %bitcast.71), channel_id=1, source_target_pairs={{0,17},{1,16},{2,19},{3,18},{4,21},{5,20},{6,23},{7,22},{8,25},{9,... | collective-permute-start | bytes 36872 | tf_op jit(solution)/shard_map/ppermute | solution.py:609
  38.2 4.6 %collective-permute-start.11 = (f32[3072]{0:T(1024)S(1)}, f32[3072]{0:T(1024)S(1)}, u32[]{:S(2)}, u32[]{:S(2)}) collective-permute-start(f32[3072]{0:T(1024)S(1)} %bitcast.72), channel_id=1, source_target_pairs={{0,16},{1,17},{2,18},{3,19},{4,20},{5,21},{6,22},{7,23},{8,24},{9,... | collective-permute-start | bytes 36872 | tf_op jit(solution)/shard_map/ppermute | solution.py:609
  38.2 5.1 %collective-permute-start.10 = (f32[3072]{0:T(1024)S(1)}, f32[3072]{0:T(1024)S(1)}, u32[]{:S(2)}, u32[]{:S(2)}) collective-permute-start(f32[3072]{0:T(1024)S(1)} %bitcast.73), channel_id=1, source_target_pairs={{0,1},{1,0},{2,3},{3,2},{4,5},{5,4},{6,7},{7,6},{8,9},{9,8},{10,11... | collective-permute-start | bytes 36872 | tf_op jit(solution)/shard_map/ppermute | solution.py:609
  73.4 1.3 collective-permute-start.13
  74.7 5.7 %collective-permute-start.16 = (f32[5120]{0:T(1024)S(1)}, f32[5120]{0:T(1024)S(1)}, u32[]{:S(2)}, u32[]{:S(2)}) collective-permute-start(f32[5120]{0:T(1024)S(1)} %bitcast.33), channel_id=1, source_target_pairs={{0,6},{1,7},{2,4},{3,5},{4,2},{5,3},{6,0},{7,1},{8,14},{9,15},{10,... | collective-permute-start | bytes 61448 | tf_op jit(solution)/shard_map/ppermute | solution.py:609
  76.2 4.7 %collective-permute-start.15 = (f32[5120]{0:T(1024)S(1)}, f32[5120]{0:T(1024)S(1)}, u32[]{:S(2)}, u32[]{:S(2)}) collective-permute-start(f32[5120]{0:T(1024)S(1)} %bitcast.34), channel_id=1, source_target_pairs={{0,4},{1,5},{2,6},{3,7},{4,0},{5,1},{6,2},{7,3},{8,12},{9,13},{10,... | collective-permute-start | bytes 61448 | tf_op jit(solution)/shard_map/ppermute | solution.py:609
  77.8 3.8 %collective-permute-start.14 = (f32[5120]{0:T(1024)S(1)}, f32[5120]{0:T(1024)S(1)}, u32[]{:S(2)}, u32[]{:S(2)}) collective-permute-start(f32[5120]{0:T(1024)S(1)} %bitcast.35), channel_id=1, source_target_pairs={{0,2},{1,3},{2,0},{3,1},{4,6},{5,7},{6,4},{7,5},{8,10},{9,11},{10,... | collective-permute-start | bytes 61448 | tf_op jit(solution)/shard_map/ppermute | solution.py:609
  85.6 4.6 %collective-permute-start.19 = (f32[2048]{0:T(1024)S(1)}, f32[2048]{0:T(1024)S(1)}, u32[]{:S(2)}, u32[]{:S(2)}) collective-permute-start(f32[2048]{0:T(1024)S(1)} %bitcast.57), channel_id=1, source_target_pairs={{0,17},{1,16},{2,19},{3,18},{4,21},{5,20},{6,23},{7,22},{8,25},{9,... | collective-permute-start | bytes 24584 | tf_op jit(solution)/shard_map/ppermute | solution.py:609
  87.8 3.7 %collective-permute-start.18 = (f32[2048]{0:T(1024)S(1)}, f32[2048]{0:T(1024)S(1)}, u32[]{:S(2)}, u32[]{:S(2)}) collective-permute-start(f32[2048]{0:T(1024)S(1)} %bitcast.58), channel_id=1, source_target_pairs={{0,16},{1,17},{2,18},{3,19},{4,20},{5,21},{6,22},{7,23},{8,24},{9,... | collective-permute-start | bytes 24584 | tf_op jit(solution)/shard_map/ppermute | solution.py:609
  88.5 3.7 %collective-permute-start.17 = (f32[2048]{0:T(1024)S(1)}, f32[2048]{0:T(1024)S(1)}, u32[]{:S(2)}, u32[]{:S(2)}) collective-permute-start(f32[2048]{0:T(1024)S(1)} %bitcast.59), channel_id=1, source_target_pairs={{0,1},{1,0},{2,3},{3,2},{4,5},{5,4},{6,7},{7,6},{8,9},{9,8},{10,11... | collective-permute-start | bytes 24584 | tf_op jit(solution)/shard_map/ppermute | solution.py:609
  94.9 1.2 collective-permute-start.20
  96.1 5.6 %collective-permute-start.23 = (f32[4096]{0:T(1024)S(1)}, f32[4096]{0:T(1024)S(1)}, u32[]{:S(2)}, u32[]{:S(2)}) collective-permute-start(f32[4096]{0:T(1024)S(1)} %bitcast.36), channel_id=1, source_target_pairs={{0,6},{1,7},{2,4},{3,5},{4,2},{5,3},{6,0},{7,1},{8,14},{9,15},{10,... | collective-permute-start | bytes 49160 | tf_op jit(solution)/shard_map/ppermute | solution.py:609
  98.6 4.6 %collective-permute-start.22 = (f32[4096]{0:T(1024)S(1)}, f32[4096]{0:T(1024)S(1)}, u32[]{:S(2)}, u32[]{:S(2)}) collective-permute-start(f32[4096]{0:T(1024)S(1)} %bitcast.37), channel_id=1, source_target_pairs={{0,4},{1,5},{2,6},{3,7},{4,0},{5,1},{6,2},{7,3},{8,12},{9,13},{10,... | collective-permute-start | bytes 49160 | tf_op jit(solution)/shard_map/ppermute | solution.py:609
  99.7 3.7 %collective-permute-start.21 = (f32[4096]{0:T(1024)S(1)}, f32[4096]{0:T(1024)S(1)}, u32[]{:S(2)}, u32[]{:S(2)}) collective-permute-start(f32[4096]{0:T(1024)S(1)} %bitcast.38), channel_id=1, source_target_pairs={{0,2},{1,3},{2,0},{3,1},{4,6},{5,7},{6,4},{7,5},{8,10},{9,11},{10,... | collective-permute-start | bytes 49160 | tf_op jit(solution)/shard_map/ppermute | solution.py:609
  107.0 4.6 %collective-permute-start.26 = (f32[2048]{0:T(1024)S(1)}, f32[2048]{0:T(1024)S(1)}, u32[]{:S(2)}, u32[]{:S(2)}) collective-permute-start(f32[2048]{0:T(1024)S(1)} %bitcast.39), channel_id=1, source_target_pairs={{0,17},{1,16},{2,19},{3,18},{4,21},{5,20},{6,23},{7,22},{8,25},{9,... | collective-permute-start | bytes 24584 | tf_op jit(solution)/shard_map/ppermute | solution.py:609
  107.6 4.0 %collective-permute-start.25 = (f32[2048]{0:T(1024)S(1)}, f32[2048]{0:T(1024)S(1)}, u32[]{:S(2)}, u32[]{:S(2)}) collective-permute-start(f32[2048]{0:T(1024)S(1)} %bitcast.40), channel_id=1, source_target_pairs={{0,16},{1,17},{2,18},{3,19},{4,20},{5,21},{6,22},{7,23},{8,24},{9,... | collective-permute-start | bytes 24584 | tf_op jit(solution)/shard_map/ppermute | solution.py:609
  109.5 3.7 %collective-permute-start.24 = (f32[2048]{0:T(1024)S(1)}, f32[2048]{0:T(1024)S(1)}, u32[]{:S(2)}, u32[]{:S(2)}) collective-permute-start(f32[2048]{0:T(1024)S(1)} %bitcast.41), channel_id=1, source_target_pairs={{0,1},{1,0},{2,3},{3,2},{4,5},{5,4},{6,7},{7,6},{8,9},{9,8},{10,11... | collective-permute-start | bytes 24584 | tf_op jit(solution)/shard_map/ppermute | solution.py:609
  115.5 1.2 collective-permute-start.27
  120.0 7.7 %collective-permute-start.28 = (bf16[1024,128]{1,0:T(8,128)(2,1)S(1)}, bf16[1024,128]{1,0:T(8,128)(2,1)S(1)}, u32[]{:S(2)}, u32[]{:S(2)}) collective-permute-start(bf16[1024,128]{1,0:T(8,128)(2,1)S(1)} %get-tuple-element.72), channel_id=1, source_target_pairs={{0,8},{1,9},{2,10},{3,11},{4,12},{5,13},{6,14},{7,15},{8,0},{9,1},... | collective-permute-start | bytes 786440 | tf_op jit(solution)/shard_map/ppermute | solution.py:609
  120.2 8.7 %collective-permute-start.31 = (f32[4096]{0:T(1024)S(1)}, f32[4096]{0:T(1024)S(1)}, u32[]{:S(2)}, u32[]{:S(2)}) collective-permute-start(f32[4096]{0:T(1024)S(1)} %bitcast.47), channel_id=1, source_target_pairs={{0,6},{1,7},{2,4},{3,5},{4,2},{5,3},{6,0},{7,1},{8,14},{9,15},{10,... | collective-permute-start | bytes 49160 | tf_op jit(solution)/shard_map/ppermute | solution.py:609
  121.7 8.5 %collective-permute-start.30 = (f32[4096]{0:T(1024)S(1)}, f32[4096]{0:T(1024)S(1)}, u32[]{:S(2)}, u32[]{:S(2)}) collective-permute-start(f32[4096]{0:T(1024)S(1)} %bitcast.48), channel_id=1, source_target_pairs={{0,4},{1,5},{2,6},{3,7},{4,0},{5,1},{6,2},{7,3},{8,12},{9,13},{10,... | collective-permute-start | bytes 49160 | tf_op jit(solution)/shard_map/ppermute | solution.py:609
  122.3 7.8 %collective-permute-start.29 = (f32[4096]{0:T(1024)S(1)}, f32[4096]{0:T(1024)S(1)}, u32[]{:S(2)}, u32[]{:S(2)}) collective-permute-start(f32[4096]{0:T(1024)S(1)} %bitcast.49), channel_id=1, source_target_pairs={{0,2},{1,3},{2,0},{3,1},{4,6},{5,7},{6,4},{7,5},{8,10},{9,11},{10,... | collective-permute-start | bytes 49160 | tf_op jit(solution)/shard_map/ppermute | solution.py:609
  127.6 4.6 %collective-permute-start.32 = (bf16[1024,128]{1,0:T(8,128)(2,1)S(1)}, bf16[1024,128]{1,0:T(8,128)(2,1)S(1)}, u32[]{:S(2)}, u32[]{:S(2)}) collective-permute-start(bf16[1024,128]{1,0:T(8,128)(2,1)S(1)} %get-tuple-element.80), channel_id=1, source_target_pairs={{0,8},{1,9},{2,10},{3,11},{4,12},{5,13},{6,14},{7,15},{8,0},{9,1},... | collective-permute-start | bytes 786440 | tf_op jit(solution)/shard_map/ppermute | solution.py:609
  127.7 12.0 %collective-permute-start.37 = (bf16[512,128]{1,0:T(8,128)(2,1)S(1)}, bf16[512,128]{1,0:T(8,128)(2,1)S(1)}, u32[]{:S(2)}, u32[]{:S(2)}) collective-permute-start(bf16[512,128]{1,0:T(8,128)(2,1)S(1)} %get-tuple-element.90), channel_id=1, source_target_pairs={{0,4},{1,5},{2,6},{3,7},{4,0},{5,1},{6,2},{7,3},{8,12},{9,13},{10,... | collective-permute-start | bytes 393224 | tf_op jit(solution)/shard_map/ppermute | solution.py:609
  128.9 13.3 %collective-permute-start.38 = (bf16[512,128]{1,0:T(8,128)(2,1)S(1)}, bf16[512,128]{1,0:T(8,128)(2,1)S(1)}, u32[]{:S(2)}, u32[]{:S(2)}) collective-permute-start(bf16[512,128]{1,0:T(8,128)(2,1)S(1)} %get-tuple-element.91), channel_id=1, source_target_pairs={{0,6},{1,7},{2,4},{3,5},{4,2},{5,3},{6,0},{7,1},{8,14},{9,15},{10,... | collective-permute-start | bytes 393224 | tf_op jit(solution)/shard_map/ppermute | solution.py:609
  132.3 10.2 %collective-permute-start.36 = (bf16[512,128]{1,0:T(8,128)(2,1)S(1)}, bf16[512,128]{1,0:T(8,128)(2,1)S(1)}, u32[]{:S(2)}, u32[]{:S(2)}) collective-permute-start(bf16[512,128]{1,0:T(8,128)(2,1)S(1)} %get-tuple-element.89), channel_id=1, source_target_pairs={{0,2},{1,3},{2,0},{3,1},{4,6},{5,7},{6,4},{7,5},{8,10},{9,11},{10,... | collective-permute-start | bytes 393224 | tf_op jit(solution)/shard_map/ppermute | solution.py:609
  133.5 9.0 %collective-permute-start.35 = (bf16[512,128]{1,0:T(8,128)(2,1)S(1)}, bf16[512,128]{1,0:T(8,128)(2,1)S(1)}, u32[]{:S(2)}, u32[]{:S(2)}) collective-permute-start(bf16[512,128]{1,0:T(8,128)(2,1)S(1)} %get-tuple-element.87), channel_id=1, source_target_pairs={{0,17},{1,16},{2,19},{3,18},{4,21},{5,20},{6,23},{7,22},{8,25},{9,... | collective-permute-start | bytes 393224 | tf_op jit(solution)/shard_map/ppermute | solution.py:609
  136.8 5.6 %collective-permute-start.33 = (bf16[512,128]{1,0:T(8,128)(2,1)S(1)}, bf16[512,128]{1,0:T(8,128)(2,1)S(1)}, u32[]{:S(2)}, u32[]{:S(2)}) collective-permute-start(bf16[512,128]{1,0:T(8,128)(2,1)S(1)} %get-tuple-element.85), channel_id=1, source_target_pairs={{0,1},{1,0},{2,3},{3,2},{4,5},{5,4},{6,7},{7,6},{8,9},{9,8},{10,11... | collective-permute-start | bytes 393224 | tf_op jit(solution)/shard_map/ppermute | solution.py:609
  139.7 5.4 %collective-permute-start.34 = (bf16[512,128]{1,0:T(8,128)(2,1)S(1)}, bf16[512,128]{1,0:T(8,128)(2,1)S(1)}, u32[]{:S(2)}, u32[]{:S(2)}) collective-permute-start(bf16[512,128]{1,0:T(8,128)(2,1)S(1)} %get-tuple-element.86), channel_id=1, source_target_pairs={{0,16},{1,17},{2,18},{3,19},{4,20},{5,21},{6,22},{7,23},{8,24},{9,... | collective-permute-start | bytes 393224 | tf_op jit(solution)/shard_map/ppermute | solution.py:609

commit v16 on v15

--- a/solution.py
+++ b/solution.py
@@ -224,28 +224,27 @@
     return parts.astype(jnp.bfloat16)
 
 
-def row_sums(width, e_ref, w_ref, w16_ref, acc_ref, o_ref):
+def row_sums(e_ref, w_ref, o_ref):
     rows, cols = e_ref.shape
-    split = rows - acc_ref.shape[0]
-    blocks = list(range(0, rows - split, 64))
-    dots = list(range(0, split, width))
-    for n, at in enumerate(dots):
-        got = lax.dot_general(w16_ref[...], e_ref[at:at + width, :], NT, preferred_element_type=jnp.float32)
-        for k in blocks[n * len(blocks) // len(dots):(n + 1) * len(blocks) // len(dots)]:
+
+    def block(n, _):
+        totals = []
+        for k in range(0, 128, 64):
+            at = pl.multiple_of(n * 128 + k, 64)
             total = jnp.zeros((64, 128), jnp.float32)
             for q in range(0, cols, 128):
-                e = e_ref[split + k:split + k + 64, q:q + 128].astype(jnp.float32)
-                total = total + e * w_ref[:, q:q + 128]
-            acc_ref[k:k + 64, :] = total
-        o_ref[:, at:at + width] = jnp.sum(got, axis=0, keepdims=True)
-    for at in range(0, rows - split, 128):
-        total = jnp.sum(jnp.transpose(acc_ref[at:at + 128, :]), axis=0, keepdims=True)
-        o_ref[:, split + at:split + at + 128] = total
-
-
-def first_row_kernel(width, shifts, parts, e_ref, shift_ref, *refs):
+                total = total + e_ref[pl.ds(at, 64), q:q + 128].astype(jnp.float32) * w_ref[:, q:q + 128]
+            totals.append(total)
+        whole = jnp.transpose(jnp.concatenate(totals, axis=0))
+        o_ref[:, pl.ds(pl.multiple_of(n * 128, 128), 128)] = jnp.sum(whole, axis=0, keepdims=True)
+        return 0
+
+    lax.fori_loop(0, rows // 128, block, 0)
+
+
+def first_row_kernel(shifts, parts, e_ref, shift_ref, *refs):
     nz = len(shifts)
-    got, (o_ref, beta_ref, b_ref, w16_ref, acc_ref) = refs[:nz], refs[nz:]
+    got, (o_ref, beta_ref, b_ref) = refs[:nz], refs[nz:]
     cols = e_ref.shape[1]
     share = cols // parts
     for k in range(parts):
@@ -253,25 +252,24 @@
         b_ref[:, k * share:(k + 1) * share] = got[k % nz][:, at:at + share]
     lse = lse2(ordered([part[:, :cols] for part in got], shifts, parts))
     beta_ref[...] = jnp.exp2(jnp.log2(b_ref[...]) - lse + shift_ref[...])
-    w16_ref[...] = stacked(beta_ref[...])
-    row_sums(width, e_ref, beta_ref, w16_ref, acc_ref, o_ref)
+    row_sums(e_ref, beta_ref, o_ref)
 
 
 def new_scale(b_ref, got, shifts, parts):
     return b_ref[...] / sum(ordered([part[...] for part in got], shifts, parts))
 
 
-def row_kernel(width, shifts, parts, e_ref, first_ref, b_ref, *refs):
-    got, (o_ref, w16_ref, acc_ref, w_ref) = refs[:-4], refs[-4:]
+def row_kernel(shifts, parts, e_ref, first_ref, b_ref, *refs):
+    got, (o_ref, w_ref) = refs[:-2], refs[-2:]
     w_ref[...] = first_ref[...] * new_scale(b_ref, got, shifts, parts)
-    w16_ref[...] = stacked(w_ref[...])
-    row_sums(width, e_ref, w_ref, w16_ref, acc_ref, o_ref)
-
-
-def column_kernel(width, shifts, parts, e_ref, a_ref, first_ref, *refs):
+    row_sums(e_ref, w_ref, o_ref)
+
+
+def column_kernel(shifts, parts, e_ref, a_ref, first_ref, *refs):
     got, (o_ref, alpha_ref, w16_ref) = refs[:-3], refs[-3:]
     alpha_ref[...] = a_ref[...] / sum(ordered([part[...] for part in got], shifts, parts))
     w16_ref[...] = stacked(alpha_ref[...])
+    width = 512
     for at in range(0, e_ref.shape[1], width):
         sums = jnp.dot(w16_ref[...], e_ref[:, at:at + width], preferred_element_type=jnp.float32)
         o_ref[:, at:at + width] = first_ref[:, at:at + width] * jnp.sum(sums, axis=0, keepdims=True)
@@ -283,16 +281,13 @@
 
 def weighted(kernel, outs, e, rows, got, parts):
     got, shifts = got
-    size = e.shape[0] if kernel is column_kernel else e.shape[1]
-    width = 512 if kernel is column_kernel else 256
-    scratch = [pltpu.VMEM((16, size), jnp.bfloat16)]
-    if kernel is not column_kernel:
-        part = 3 if kernel is row_kernel else 1
-        scratch.append(pltpu.VMEM((e.shape[0] * part // 4, 128), jnp.float32))
+    scratch = []
+    if kernel is column_kernel:
+        scratch = [pltpu.VMEM((16, e.shape[0]), jnp.bfloat16)]
     if kernel is row_kernel:
-        scratch.append(pltpu.VMEM((1, size), jnp.float32))
-    return pl.pallas_call(
-        functools.partial(kernel, width, tuple(shifts), parts),
+        scratch = [pltpu.VMEM((1, e.shape[1]), jnp.float32)]
+    return pl.pallas_call(
+        functools.partial(kernel, tuple(shifts), parts),
         out_shape=[shape(*dims) for dims in outs],
         in_specs=[VMEM] * (1 + len(rows) + len(got)),
         out_specs=[VMEM] * len(outs),
@@ -368,7 +363,7 @@
     )(own, mass.reshape(1, -1), x, first, *ys)
 
 
-def column_lse(x, y, mass, tail, got, width=512, chunk=512):
+def column_lse(x, y, mass, tail, got, width=1024, chunk=512):
     rows, cols = x.shape[0], y.shape[0]
     return pl.pallas_call(
         functools.partial(column_lse_kernel, width, chunk, len(got)),

time: 147 us -> 148 us (level)
  Pallas kernels: 79.2 us -> 81.2 us
    pallas_call x4, Pallas kernels: 12.8 us -> 14.6 us  [weighted(): pl.pallas_call(functools.partial(kernel, tuple(shifts), parts), out_shape...]
  transfers between devices with their start and end apart: 39 -> 39, of which waited for: 20 -> 19; matrix products, arithmetic and copies ran while one was open for 1% -> 1% of each run, Pallas kernels for 15% -> 15%
where the time goes in v16:
time: 148 us
  Pallas kernels  81.2 us (55%)
  starting transfers between devices  42.7 us (29%)
  waiting for transfers between devices  21.6 us (15%)
    ppermute x39, starting transfers between devices, swap(): lax.ppermute(value, ('row', 'col'), [(i, i ^ mask) for i in range(self.co...  42.7 us
    pallas_call x1, Pallas kernels, column_lse(): pl.pallas_call(functools.partial(column_lse_kernel, width, chunk, len(got...  30.5 us
    ppermute x39, waiting for transfers between devices, swap(): lax.ppermute(value, ('row', 'col'), [(i, i ^ mask) for i in range(self.co...  21.6 us
    pallas_call x4, Pallas kernels, weighted(): pl.pallas_call(functools.partial(kernel, tuple(shifts), parts), out_shape...  14.6 us
    pallas_call x1, Pallas kernels, row_lse_late(): pl.pallas_call(functools.partial(row_lse_late_kernel, width, len(ys)), ou...  9.94 us
    pallas_call x1, Pallas kernels, row_lse_middle(): pl.pallas_call(functools.partial(row_lse_middle_kernel, width, len(ys)),...  6.45 us
    pallas_call x1, Pallas kernels, row_lse_early(): pl.pallas_call(functools.partial(row_lse_early_kernel, width, len(xs)), o...  6.45 us
    pallas_call x2, Pallas kernels, column_grad(): pl.pallas_call(functools.partial(kernel, blocks, share), out_shape=out_sh...  5.95 us
  transfers between devices with their start and end apart: 39, of which 19 were waited for; matrix products, arithmetic and copies ran while one was open for 1% of the time, Pallas kernels for 15%

profile of v16, /device:TPU:0, one launch (start us, length us, event | category | flops | bytes accessed | tf_op | source)
XLA Modules:
  0.0 148.3 jit_solution(15558466797735725763)
XLA Ops:
  0.6 3.0 %collective-permute-start = (bf16[512,128]{1,0:T(8,128)(2,1)}, bf16[512,128]{1,0:T(8,128)(2,1)S(1)}, u32[]{:S(2)}, u32[]{:S(2)}) collective-permute-start(bf16[512,128]{1,0:T(8,128)(2,1)} %param.4), channel_id=1, source_target_pairs={{0,1},{1,0},{2,3},{3,2},{4,5},{5,4},{6,7},{7,6},{8,9},{9,8},{10,11... | collective-permute-start | bytes 393224 | tf_op jit(solution)/shard_map/ppermute | solution.py:604
  3.7 1.4 collective-permute-start.2
  5.2 3.0 %collective-permute-start.4 = (bf16[512,128]{1,0:T(8,128)(2,1)}, bf16[512,128]{1,0:T(8,128)(2,1)S(1)}, u32[]{:S(2)}, u32[]{:S(2)}) collective-permute-start(bf16[512,128]{1,0:T(8,128)(2,1)} %bitcast.77), channel_id=1, source_target_pairs={{0,4},{1,5},{2,6},{3,7},{4,0},{5,1},{6,2},{7,3},{8,12},{9,13},{10,... | collective-permute-start | bytes 393224 | tf_op jit(solution)/shard_map/ppermute | solution.py:604
  8.2 1.0 pad_maximum_fusion.own_ref
  10.2 1.6 %collective-permute-start.5 = (bf16[512,128]{1,0:T(8,128)(2,1)}, bf16[512,128]{1,0:T(8,128)(2,1)S(1)}, u32[]{:S(2)}, u32[]{:S(2)}) collective-permute-start(bf16[512,128]{1,0:T(8,128)(2,1)} %bitcast.80), channel_id=1, source_target_pairs={{0,2},{1,3},{2,0},{3,1},{4,6},{5,7},{6,4},{7,5},{8,10},{9,11},{10,... | collective-permute-start | bytes 393224 | tf_op jit(solution)/shard_map/ppermute | solution.py:604
  11.8 6.4 %row_lse_early.1 = (bf16[2048,128]{1,0:T(8,128)(2,1)S(1)}, bf16[128,2048]{1,0:T(8,128)(2,1)S(1)}, f32[1,2048]{1,0:T(1,128)S(1)}) custom-call(bf16[1024,128]{1,0:T(8,128)(2,1)S(1)} %pad_maximum_fusion.own_ref, bf16[512,128]{1,0:T(8,128)(2,1)S(1)} %collective-permute-done.refs_0_, bf16[512,128]{1,0:T(8,128)(2,1)S(1)} %collective-permute-done.1.refs_1_, ...), custom_call_target="tpu_custom_call" | custom-call | flops 536870912 | bytes 786432 | tf_op jit(solution)/shard_map/row_lse_early/pallas_call | solution.py:320
  19.0 6.5 %row_lse_middle.1.first_ref = f32[1,2048]{1,0:T(1,128)S(1)} custom-call(bf16[2048,128]{1,0:T(8,128)(2,1)S(1)} %get-tuple-element.50.x_ref, f32[1,2048]{1,0:T(1,128)S(1)} %get-tuple-element.53.first_ref, bf16[512,128]{1,0:T(8,128)(2,1)S(1)} %collective-permute-done.5.refs_0_, bf16[512,128]{1,0:T(8,128)(2,1)S(1)} %collective-permute-done.4.refs_1_), custom_call_target="tpu_custom_call" | custom-call | flops 536870912 | bytes 786432 | tf_op jit(solution)/shard_map/row_lse_middle/pallas_call | solution.py:335
  25.6 1.3 collective-permute-done.9.refs_6_
  26.8 9.9 %row_lse_late.1 = (bf16[4096,128]{1,0:T(8,128)(2,1)S(1)}, f32[1,3072]{1,0:T(1,128)S(1)}) custom-call(bf16[1024,128]{1,0:T(8,128)(2,1)S(1)} %pad_maximum_fusion.own_ref, f32[1,2048]{1,0:T(1,128)S(1)} %bitcast.66, bf16[2048,128]{1,0:T(8,128)(2,1)S(1)} %get-tuple-element.50.x_ref, f32[1,2048]{1,0:T(1,128)S(1)} %row_lse_middle.1.first_ref, ...), custom_call_target="tpu_custom_call" | custom-call | flops 1073741824 | bytes 1048576 | tf_op jit(solution)/shard_map/row_lse_late/pallas_call | solution.py:354
  37.3 3.0 %collective-permute-start.10 = (f32[3072]{0:T(1024)S(1)}, f32[3072]{0:T(1024)S(1)}, u32[]{:S(2)}, u32[]{:S(2)}) collective-permute-start(f32[3072]{0:T(1024)S(1)} %bitcast.73), channel_id=1, source_target_pairs={{0,1},{1,0},{2,3},{3,2},{4,5},{5,4},{6,7},{7,6},{8,9},{9,8},{10,11... | collective-permute-start | bytes 36872 | tf_op jit(solution)/shard_map/ppermute | solution.py:604
  40.3 1.1 collective-permute-done.12
  42.0 30.5 %column_lse.1 = (f32[1,5120]{1,0:T(1,128)S(1)}, bf16[2048,4096]{1,0:T(8,128)(2,1)S(1)}, f32[1,4096]{1,0:T(1,128)S(1)}, f32[1,2048]{1,0:T(1,128)S(1)}) custom-call(bf16[2048,128]{1,0:T(8,128)(2,1)S(1)} %get-tuple-element.50.x_ref, bf16[4096,128]{1,0:T(8,128)(2,1)S(1)} %get-tuple-element.57.y_ref, f32[1,2048]{1,0:T(1,128)S(1)} %bitcast.67, ...), custom_call_target="tpu_custom_call" | custom-call | flops 2147483648 | bytes 1572864 | tf_op jit(solution)/shard_map/column_lse/pallas_call | solution.py:368
  72.6 1.2 collective-permute-done.13
  73.9 2.9 %collective-permute-start.16 = (f32[5120]{0:T(1024)S(1)}, f32[5120]{0:T(1024)S(1)}, u32[]{:S(2)}, u32[]{:S(2)}) collective-permute-start(f32[5120]{0:T(1024)S(1)} %bitcast.33), channel_id=1, source_target_pairs={{0,6},{1,7},{2,4},{3,5},{4,2},{5,3},{6,0},{7,1},{8,14},{9,15},{10,... | collective-permute-start | bytes 61448 | tf_op jit(solution)/shard_map/ppermute | solution.py:604
  76.7 1.7 %collective-permute-start.15 = (f32[5120]{0:T(1024)S(1)}, f32[5120]{0:T(1024)S(1)}, u32[]{:S(2)}, u32[]{:S(2)}) collective-permute-start(f32[5120]{0:T(1024)S(1)} %bitcast.34), channel_id=1, source_target_pairs={{0,4},{1,5},{2,6},{3,7},{4,0},{5,1},{6,2},{7,3},{8,12},{9,13},{10,... | collective-permute-start | bytes 61448 | tf_op jit(solution)/shard_map/ppermute | solution.py:604
  79.6 1.8 %collective-permute-done.15 = f32[5120]{0:T(1024)S(1)} collective-permute-done((f32[5120]{0:T(1024)S(1)}, f32[5120]{0:T(1024)S(1)}, u32[]{:S(2)}, u32[]{:S(2)}) %collective-permute-start.15) | collective-permute-done | bytes 20512 | tf_op jit(solution)/shard_map/ppermute | solution.py:604
  82.3 4.8 %weighted_sum.4 = (f32[1,2048]{1,0:T(1,128)S(1)}, f32[1,4096]{1,0:T(1,128)S(1)}, f32[1,4096]{1,0:T(1,128)S(1)}) custom-call(bf16[2048,4096]{1,0:T(8,128)(2,1)S(1)} %get-tuple-element.59.e_ref, f32[1,4096]{1,0:T(1,128)S(1)} %get-tuple-element.62.shift_ref, f32[1,5120]{1,0:T(1,128)S(1)} %pair.3.refs_0_, f32[1,5120]{1,0:T(1,128)S(1)} %bitcast.44, ...), custom_call_target="tpu_custom_call" | custom-call | flops 16777216 | bytes 16777216 | tf_op jit(solution)/shard_map/weighted_sum/pallas_call | solution.py:289
  87.0 1.5 %collective-permute-start.19 = (f32[2048]{0:T(1024)S(1)}, f32[2048]{0:T(1024)S(1)}, u32[]{:S(2)}, u32[]{:S(2)}) collective-permute-start(f32[2048]{0:T(1024)S(1)} %bitcast.57), channel_id=1, source_target_pairs={{0,17},{1,16},{2,19},{3,18},{4,21},{5,20},{6,23},{7,22},{8,25},{9,... | collective-permute-start | bytes 24584 | tf_op jit(solution)/shard_map/ppermute | solution.py:604
  89.5 1.1 collective-permute-start.17
  90.6 1.1 collective-permute-done.19
  93.1 2.8 %weighted_sum.5 = (f32[1,4096]{1,0:T(1,128)S(1)}, f32[1,2048]{1,0:T(1,128)}) custom-call(bf16[2048,4096]{1,0:T(8,128)(2,1)S(1)} %get-tuple-element.59.e_ref, f32[1,2048]{1,0:T(1,128)S(1)} %get-tuple-element.61.a_ref, f32[1,4096]{1,0:T(1,128)S(1)} %get-tuple-element.64.first_ref, f32[1,2048]{1,0:T(1,128)S(1)} %get-tuple-element.66.refs_0_, ...), custom_call_target="tpu_custom_call" | custom-call | flops 16777216 | bytes 16777216 | tf_op jit(solution)/shard_map/weighted_sum/pallas_call | solution.py:289
  95.9 1.2 collective-permute-done.20
  97.1 1.8 %collective-permute-start.23 = (f32[4096]{0:T(1024)S(1)}, f32[4096]{0:T(1024)S(1)}, u32[]{:S(2)}, u32[]{:S(2)}) collective-permute-start(f32[4096]{0:T(1024)S(1)} %bitcast.36), channel_id=1, source_target_pairs={{0,6},{1,7},{2,4},{3,5},{4,2},{5,3},{6,0},{7,1},{8,14},{9,15},{10,... | collective-permute-start | bytes 49160 | tf_op jit(solution)/shard_map/ppermute | solution.py:604
  99.6 1.9 %collective-permute-start.21 = (f32[4096]{0:T(1024)S(1)}, f32[4096]{0:T(1024)S(1)}, u32[]{:S(2)}, u32[]{:S(2)}) collective-permute-start(f32[4096]{0:T(1024)S(1)} %bitcast.38), channel_id=1, source_target_pairs={{0,2},{1,3},{2,0},{3,1},{4,6},{5,7},{6,4},{7,5},{8,10},{9,11},{10,... | collective-permute-start | bytes 49160 | tf_op jit(solution)/shard_map/ppermute | solution.py:604
  101.5 1.1 collective-permute-done.23
  103.5 4.7 %weighted_sum.6.refs_0_ = f32[1,2048]{1,0:T(1,128)S(1)} custom-call(bf16[2048,4096]{1,0:T(8,128)(2,1)S(1)} %get-tuple-element.59.e_ref, f32[1,4096]{1,0:T(1,128)S(1)} %get-tuple-element.64.first_ref, f32[1,4096]{1,0:T(1,128)S(1)} %get-tuple-element.65.b_ref, f32[1,4096]{1,0:T(1,128)S(1)} %pair.4.refs_0_, f32[1,4096]{1,0:T(1,128)S(1)} %bitcast.56, ...), custom_call_target="tpu_custom_call" | custom-call | flops 16777216 | bytes 16777216 | tf_op jit(solution)/shard_map/weighted_sum/pallas_call | solution.py:289
  108.2 2.4 %collective-permute-start.26 = (f32[2048]{0:T(1024)S(1)}, f32[2048]{0:T(1024)S(1)}, u32[]{:S(2)}, u32[]{:S(2)}) collective-permute-start(f32[2048]{0:T(1024)S(1)} %bitcast.39), channel_id=1, source_target_pairs={{0,17},{1,16},{2,19},{3,18},{4,21},{5,20},{6,23},{7,22},{8,25},{9,... | collective-permute-start | bytes 24584 | tf_op jit(solution)/shard_map/ppermute | solution.py:604
  110.6 1.2 collective-permute-start.25
  111.8 1.1 collective-permute-done.26
  112.8 1.4 collective-permute-done.25
  114.3 1.2 collective-permute-done.24
  115.4 2.3 %weighted_sum.7 = (f32[1,4096]{1,0:T(1,128)S(1)}, f32[1,2048]{1,0:T(1,128)S(1)}) custom-call(bf16[2048,4096]{1,0:T(8,128)(2,1)S(1)} %get-tuple-element.59.e_ref, f32[1,2048]{1,0:T(1,128)S(1)} %get-tuple-element.61.a_ref, f32[1,4096]{1,0:T(1,128)S(1)} %get-tuple-element.64.first_ref, f32[1,2048]{1,0:T(1,128)S(1)} %weighted_sum.6.refs_0_, ...), custom_call_target="tpu_custom_call" | custom-call | flops 16777216 | bytes 16777216 | tf_op jit(solution)/shard_map/weighted_sum/pallas_call | solution.py:289
  117.8 1.2 collective-permute-done.27
  119.0 3.0 %column_grad.2 = (f32[1024,128]{1,0:T(8,128)S(1)}, bf16[1024,128]{1,0:T(8,128)(2,1)S(1)}, bf16[256,2048]{1,0:T(8,128)(2,1)S(1)}) custom-call(bf16[128,2048]{1,0:T(8,128)(2,1)S(1)} %get-tuple-element.60.xt_ref, bf16[4096,128]{1,0:T(8,128)(2,1)S(1)} %get-tuple-element.57.y_ref, bf16[2048,4096]{1,0:T(8,128)(2,1)S(1)} %get-tuple-element.59.e_ref, ...), custom_call_target="tpu_custom_call" | custom-call | flops 2147483648 | bytes 8388608 | tf_op jit(solution)/shard_map/column_grad/pallas_call | solution.py:450
  122.2 1.5 collective-permute-start.31
  124.6 2.1 %collective-permute-start.29 = (f32[4096]{0:T(1024)S(1)}, f32[4096]{0:T(1024)S(1)}, u32[]{:S(2)}, u32[]{:S(2)}) collective-permute-start(f32[4096]{0:T(1024)S(1)} %bitcast.49), channel_id=1, source_target_pairs={{0,2},{1,3},{2,0},{3,1},{4,6},{5,7},{6,4},{7,5},{8,10},{9,11},{10,... | collective-permute-start | bytes 49160 | tf_op jit(solution)/shard_map/ppermute | solution.py:604
  126.6 3.0 %column_grad.3 = (f32[1024,128]{1,0:T(8,128)S(1)}, bf16[1024,128]{1,0:T(8,128)(2,1)S(1)}) custom-call(bf16[256,2048]{1,0:T(8,128)(2,1)S(1)} %get-tuple-element.78.xa_ref, bf16[4096,128]{1,0:T(8,128)(2,1)S(1)} %get-tuple-element.57.y_ref, bf16[2048,4096]{1,0:T(8,128)(2,1)S(1)} %get-tuple-element.59.e_ref, f32[1,4096]{1,0:T(1,128)S(1)} %get-tuple-element.64.first_ref), custom_call_target="tpu_custom_call" | custom-call | flops 2147483648 | bytes 8388608 | tf_op jit(solution)/shard_map/column_grad/pallas_call | solution.py:450
  129.8 1.2 collective-permute-start.37
  130.9 1.2 collective-permute-start.38
  132.2 2.1 %first_rows.1 = (bf16[4096,256]{1,0:T(8,128)(2,1)S(1)}, f32[1,512]{1,0:T(1,128)S(1)}, bf16[512,128]{1,0:T(8,128)(2,1)S(1)}) custom-call(bf16[2048,128]{1,0:T(8,128)(2,1)S(1)} %get-tuple-element.50.x_ref, bf16[4096,128]{1,0:T(8,128)(2,1)S(1)} %get-tuple-element.57.y_ref, bf16[2048,4096]{1,0:T(8,128)(2,1)S(1)} %get-tuple-element.59.e_ref, ...), custom_call_target="tpu_custom_call" | custom-call | flops 34359738368 | bytes 134217728 | tf_op jit(solution)/shard_map/first_rows/pallas_call | solution.py:524
  134.3 1.2 collective-permute-start.36
  135.9 2.6 %other_rows.3 = (bf16[512,128]{1,0:T(8,128)(2,1)S(1)}, bf16[512,128]{1,0:T(8,128)(2,1)S(1)}) custom-call(bf16[2048,128]{1,0:T(8,128)(2,1)S(1)} %get-tuple-element.50.x_ref, bf16[4096,256]{1,0:T(8,128)(2,1)S(1)} %get-tuple-element.84.yb_ref, bf16[2048,4096]{1,0:T(8,128)(2,1)S(1)} %get-tuple-element.59.e_ref, f32[1,2048]{1,0:T(1,128)S(1)} %get-tuple-element.75.alpha_ref), custom_call_target="tpu_custom_call" | custom-call | flops 2147483648 | bytes 8388608 | tf_op jit(solution)/shard_map/other_rows/pallas_call | solution.py:542
  138.5 2.1 %collective-permute-start.33 = (bf16[512,128]{1,0:T(8,128)(2,1)S(1)}, bf16[512,128]{1,0:T(8,128)(2,1)S(1)}, u32[]{:S(2)}, u32[]{:S(2)}) collective-permute-start(bf16[512,128]{1,0:T(8,128)(2,1)S(1)} %get-tuple-element.85), channel_id=1, source_target_pairs={{0,1},{1,0},{2,3},{3,2},{4,5},{5,4},{6,7},{7,6},{8,9},{9,8},{10,11... | collective-permute-start | bytes 393224 | tf_op jit(solution)/shard_map/ppermute | solution.py:604
  140.6 1.2 collective-permute-done.37.refs_6_
  141.8 1.8 %collective-permute-start.34 = (bf16[512,128]{1,0:T(8,128)(2,1)S(1)}, bf16[512,128]{1,0:T(8,128)(2,1)S(1)}, u32[]{:S(2)}, u32[]{:S(2)}) collective-permute-start(bf16[512,128]{1,0:T(8,128)(2,1)S(1)} %get-tuple-element.86), channel_id=1, source_target_pairs={{0,16},{1,17},{2,18},{3,19},{4,20},{5,21},{6,22},{7,23},{8,24},{9,... | collective-permute-start | bytes 393224 | tf_op jit(solution)/shard_map/ppermute | solution.py:604
  143.5 1.4 other_rows.2.refs_0_
  145.0 2.2 %collective-permute-done.34.refs_2_ = bf16[512,128]{1,0:T(8,128)(2,1)S(1)} collective-permute-done((bf16[512,128]{1,0:T(8,128)(2,1)S(1)}, bf16[512,128]{1,0:T(8,128)(2,1)S(1)}, u32[]{:S(2)}, u32[]{:S(2)}) %collective-permute-start.34) | collective-permute-done | bytes 131104 | tf_op jit(solution)/shard_map/ppermute | solution.py:604
  147.2 1.1 add_up.1
  (52 shorter events, 10.6 us)
Async XLA Ops:
  0.6 9.5 %collective-permute-start = (bf16[512,128]{1,0:T(8,128)(2,1)}, bf16[512,128]{1,0:T(8,128)(2,1)S(1)}, u32[]{:S(2)}, u32[]{:S(2)}) collective-permute-start(bf16[512,128]{1,0:T(8,128)(2,1)} %param.4), channel_id=1, source_target_pairs={{0,1},{1,0},{2,3},{3,2},{4,5},{5,4},{6,7},{7,6},{8,9},{9,8},{10,11... | collective-permute-start | bytes 393224 | tf_op jit(solution)/shard_map/ppermute | solution.py:604
  3.7 8.2 %collective-permute-start.2 = (bf16[512,128]{1,0:T(8,128)(2,1)}, bf16[512,128]{1,0:T(8,128)(2,1)S(1)}, u32[]{:S(2)}, u32[]{:S(2)}) collective-permute-start(bf16[512,128]{1,0:T(8,128)(2,1)} %param.4), channel_id=1, source_target_pairs={{0,17},{1,16},{2,19},{3,18},{4,21},{5,20},{6,23},{7,22},{8,25},{9,... | collective-permute-start | bytes 393224 | tf_op jit(solution)/shard_map/ppermute | solution.py:604
  5.1 6.7 %collective-permute-start.1 = (bf16[512,128]{1,0:T(8,128)(2,1)}, bf16[512,128]{1,0:T(8,128)(2,1)S(1)}, u32[]{:S(2)}, u32[]{:S(2)}) collective-permute-start(bf16[512,128]{1,0:T(8,128)(2,1)} %param.4), channel_id=1, source_target_pairs={{0,16},{1,17},{2,18},{3,19},{4,20},{5,21},{6,22},{7,23},{8,24},{9,... | collective-permute-start | bytes 393224 | tf_op jit(solution)/shard_map/ppermute | solution.py:604
  5.2 13.1 %collective-permute-start.4 = (bf16[512,128]{1,0:T(8,128)(2,1)}, bf16[512,128]{1,0:T(8,128)(2,1)S(1)}, u32[]{:S(2)}, u32[]{:S(2)}) collective-permute-start(bf16[512,128]{1,0:T(8,128)(2,1)} %bitcast.77), channel_id=1, source_target_pairs={{0,4},{1,5},{2,6},{3,7},{4,0},{5,1},{6,2},{7,3},{8,12},{9,13},{10,... | collective-permute-start | bytes 393224 | tf_op jit(solution)/shard_map/ppermute | solution.py:604
  9.2 2.6 %collective-permute-start.3 = (bf16[512,128]{1,0:T(8,128)(2,1)}, bf16[512,128]{1,0:T(8,128)(2,1)S(1)}, u32[]{:S(2)}, u32[]{:S(2)}) collective-permute-start(bf16[512,128]{1,0:T(8,128)(2,1)} %bitcast.79), channel_id=1, source_target_pairs={{0,8},{1,9},{2,10},{3,11},{4,12},{5,13},{6,14},{7,15},{8,0},{9,1},... | collective-permute-start | bytes 393224 | tf_op jit(solution)/shard_map/ppermute | solution.py:604
  10.2 8.3 %collective-permute-start.5 = (bf16[512,128]{1,0:T(8,128)(2,1)}, bf16[512,128]{1,0:T(8,128)(2,1)S(1)}, u32[]{:S(2)}, u32[]{:S(2)}) collective-permute-start(bf16[512,128]{1,0:T(8,128)(2,1)} %bitcast.80), channel_id=1, source_target_pairs={{0,2},{1,3},{2,0},{3,1},{4,6},{5,7},{6,4},{7,5},{8,10},{9,11},{10,... | collective-permute-start | bytes 393224 | tf_op jit(solution)/shard_map/ppermute | solution.py:604
  18.3 7.1 %collective-permute-start.6 = (bf16[512,128]{1,0:T(8,128)(2,1)S(1)}, bf16[512,128]{1,0:T(8,128)(2,1)S(1)}, u32[]{:S(2)}, u32[]{:S(2)}) collective-permute-start(bf16[512,128]{1,0:T(8,128)(2,1)S(1)} %collective-permute-done.4.refs_1_), channel_id=1, source_target_pairs={{0,2},{1,3},{2,0},{3,1},{4,6},{5,7},{6,4},{7,5},{8,10},{9,11},{10,... | collective-permute-start | bytes 393224 | tf_op jit(solution)/shard_map/ppermute | solution.py:604
  18.4 7.2 %collective-permute-start.8 = (bf16[512,128]{1,0:T(8,128)(2,1)S(1)}, bf16[512,128]{1,0:T(8,128)(2,1)S(1)}, u32[]{:S(2)}, u32[]{:S(2)}) collective-permute-start(bf16[512,128]{1,0:T(8,128)(2,1)S(1)} %collective-permute-done.4.refs_1_), channel_id=1, source_target_pairs={{0,8},{1,9},{2,10},{3,11},{4,12},{5,13},{6,14},{7,15},{8,0},{9,1},... | collective-permute-start | bytes 393224 | tf_op jit(solution)/shard_map/ppermute | solution.py:604
  18.5 7.1 %collective-permute-start.7 = (bf16[512,128]{1,0:T(8,128)(2,1)S(1)}, bf16[512,128]{1,0:T(8,128)(2,1)S(1)}, u32[]{:S(2)}, u32[]{:S(2)}) collective-permute-start(bf16[512,128]{1,0:T(8,128)(2,1)S(1)} %collective-permute-done.5.refs_0_), channel_id=1, source_target_pairs={{0,8},{1,9},{2,10},{3,11},{4,12},{5,13},{6,14},{7,15},{8,0},{9,1},... | collective-permute-start | bytes 393224 | tf_op jit(solution)/shard_map/ppermute | solution.py:604
  25.4 1.4 collective-permute-start.9
  36.8 4.7 %collective-permute-start.12 = (f32[3072]{0:T(1024)S(1)}, f32[3072]{0:T(1024)S(1)}, u32[]{:S(2)}, u32[]{:S(2)}) collective-permute-start(f32[3072]{0:T(1024)S(1)} %bitcast.71), channel_id=1, source_target_pairs={{0,17},{1,16},{2,19},{3,18},{4,21},{5,20},{6,23},{7,22},{8,25},{9,... | collective-permute-start | bytes 36872 | tf_op jit(solution)/shard_map/ppermute | solution.py:604
  37.3 4.2 %collective-permute-start.11 = (f32[3072]{0:T(1024)S(1)}, f32[3072]{0:T(1024)S(1)}, u32[]{:S(2)}, u32[]{:S(2)}) collective-permute-start(f32[3072]{0:T(1024)S(1)} %bitcast.72), channel_id=1, source_target_pairs={{0,16},{1,17},{2,18},{3,19},{4,20},{5,21},{6,22},{7,23},{8,24},{9,... | collective-permute-start | bytes 36872 | tf_op jit(solution)/shard_map/ppermute | solution.py:604
  37.3 4.7 %collective-permute-start.10 = (f32[3072]{0:T(1024)S(1)}, f32[3072]{0:T(1024)S(1)}, u32[]{:S(2)}, u32[]{:S(2)}) collective-permute-start(f32[3072]{0:T(1024)S(1)} %bitcast.73), channel_id=1, source_target_pairs={{0,1},{1,0},{2,3},{3,2},{4,5},{5,4},{6,7},{7,6},{8,9},{9,8},{10,11... | collective-permute-start | bytes 36872 | tf_op jit(solution)/shard_map/ppermute | solution.py:604
  72.6 1.3 collective-permute-start.13
  73.9 5.8 %collective-permute-start.16 = (f32[5120]{0:T(1024)S(1)}, f32[5120]{0:T(1024)S(1)}, u32[]{:S(2)}, u32[]{:S(2)}) collective-permute-start(f32[5120]{0:T(1024)S(1)} %bitcast.33), channel_id=1, source_target_pairs={{0,6},{1,7},{2,4},{3,5},{4,2},{5,3},{6,0},{7,1},{8,14},{9,15},{10,... | collective-permute-start | bytes 61448 | tf_op jit(solution)/shard_map/ppermute | solution.py:604
  76.7 4.7 %collective-permute-start.15 = (f32[5120]{0:T(1024)S(1)}, f32[5120]{0:T(1024)S(1)}, u32[]{:S(2)}, u32[]{:S(2)}) collective-permute-start(f32[5120]{0:T(1024)S(1)} %bitcast.34), channel_id=1, source_target_pairs={{0,4},{1,5},{2,6},{3,7},{4,0},{5,1},{6,2},{7,3},{8,12},{9,13},{10,... | collective-permute-start | bytes 61448 | tf_op jit(solution)/shard_map/ppermute | solution.py:604
  78.5 3.8 %collective-permute-start.14 = (f32[5120]{0:T(1024)S(1)}, f32[5120]{0:T(1024)S(1)}, u32[]{:S(2)}, u32[]{:S(2)}) collective-permute-start(f32[5120]{0:T(1024)S(1)} %bitcast.35), channel_id=1, source_target_pairs={{0,2},{1,3},{2,0},{3,1},{4,6},{5,7},{6,4},{7,5},{8,10},{9,11},{10,... | collective-permute-start | bytes 61448 | tf_op jit(solution)/shard_map/ppermute | solution.py:604
  87.0 4.6 %collective-permute-start.19 = (f32[2048]{0:T(1024)S(1)}, f32[2048]{0:T(1024)S(1)}, u32[]{:S(2)}, u32[]{:S(2)}) collective-permute-start(f32[2048]{0:T(1024)S(1)} %bitcast.57), channel_id=1, source_target_pairs={{0,17},{1,16},{2,19},{3,18},{4,21},{5,20},{6,23},{7,22},{8,25},{9,... | collective-permute-start | bytes 24584 | tf_op jit(solution)/shard_map/ppermute | solution.py:604
  88.6 3.7 %collective-permute-start.18 = (f32[2048]{0:T(1024)S(1)}, f32[2048]{0:T(1024)S(1)}, u32[]{:S(2)}, u32[]{:S(2)}) collective-permute-start(f32[2048]{0:T(1024)S(1)} %bitcast.58), channel_id=1, source_target_pairs={{0,16},{1,17},{2,18},{3,19},{4,20},{5,21},{6,22},{7,23},{8,24},{9,... | collective-permute-start | bytes 24584 | tf_op jit(solution)/shard_map/ppermute | solution.py:604
  89.5 3.7 %collective-permute-start.17 = (f32[2048]{0:T(1024)S(1)}, f32[2048]{0:T(1024)S(1)}, u32[]{:S(2)}, u32[]{:S(2)}) collective-permute-start(f32[2048]{0:T(1024)S(1)} %bitcast.59), channel_id=1, source_target_pairs={{0,1},{1,0},{2,3},{3,2},{4,5},{5,4},{6,7},{7,6},{8,9},{9,8},{10,11... | collective-permute-start | bytes 24584 | tf_op jit(solution)/shard_map/ppermute | solution.py:604
  95.9 1.2 collective-permute-start.20
  97.1 5.6 %collective-permute-start.23 = (f32[4096]{0:T(1024)S(1)}, f32[4096]{0:T(1024)S(1)}, u32[]{:S(2)}, u32[]{:S(2)}) collective-permute-start(f32[4096]{0:T(1024)S(1)} %bitcast.36), channel_id=1, source_target_pairs={{0,6},{1,7},{2,4},{3,5},{4,2},{5,3},{6,0},{7,1},{8,14},{9,15},{10,... | collective-permute-start | bytes 49160 | tf_op jit(solution)/shard_map/ppermute | solution.py:604
  98.9 4.6 %collective-permute-start.22 = (f32[4096]{0:T(1024)S(1)}, f32[4096]{0:T(1024)S(1)}, u32[]{:S(2)}, u32[]{:S(2)}) collective-permute-start(f32[4096]{0:T(1024)S(1)} %bitcast.37), channel_id=1, source_target_pairs={{0,4},{1,5},{2,6},{3,7},{4,0},{5,1},{6,2},{7,3},{8,12},{9,13},{10,... | collective-permute-start | bytes 49160 | tf_op jit(solution)/shard_map/ppermute | solution.py:604
  99.6 3.9 %collective-permute-start.21 = (f32[4096]{0:T(1024)S(1)}, f32[4096]{0:T(1024)S(1)}, u32[]{:S(2)}, u32[]{:S(2)}) collective-permute-start(f32[4096]{0:T(1024)S(1)} %bitcast.38), channel_id=1, source_target_pairs={{0,2},{1,3},{2,0},{3,1},{4,6},{5,7},{6,4},{7,5},{8,10},{9,11},{10,... | collective-permute-start | bytes 49160 | tf_op jit(solution)/shard_map/ppermute | solution.py:604
  108.2 4.6 %collective-permute-start.26 = (f32[2048]{0:T(1024)S(1)}, f32[2048]{0:T(1024)S(1)}, u32[]{:S(2)}, u32[]{:S(2)}) collective-permute-start(f32[2048]{0:T(1024)S(1)} %bitcast.39), channel_id=1, source_target_pairs={{0,17},{1,16},{2,19},{3,18},{4,21},{5,20},{6,23},{7,22},{8,25},{9,... | collective-permute-start | bytes 24584 | tf_op jit(solution)/shard_map/ppermute | solution.py:604
  110.6 3.7 %collective-permute-start.25 = (f32[2048]{0:T(1024)S(1)}, f32[2048]{0:T(1024)S(1)}, u32[]{:S(2)}, u32[]{:S(2)}) collective-permute-start(f32[2048]{0:T(1024)S(1)} %bitcast.40), channel_id=1, source_target_pairs={{0,16},{1,17},{2,18},{3,19},{4,20},{5,21},{6,22},{7,23},{8,24},{9,... | collective-permute-start | bytes 24584 | tf_op jit(solution)/shard_map/ppermute | solution.py:604
  111.8 3.7 %collective-permute-start.24 = (f32[2048]{0:T(1024)S(1)}, f32[2048]{0:T(1024)S(1)}, u32[]{:S(2)}, u32[]{:S(2)}) collective-permute-start(f32[2048]{0:T(1024)S(1)} %bitcast.41), channel_id=1, source_target_pairs={{0,1},{1,0},{2,3},{3,2},{4,5},{5,4},{6,7},{7,6},{8,9},{9,8},{10,11... | collective-permute-start | bytes 24584 | tf_op jit(solution)/shard_map/ppermute | solution.py:604
  117.8 1.2 collective-permute-start.27
  122.0 7.7 %collective-permute-start.28 = (bf16[1024,128]{1,0:T(8,128)(2,1)S(1)}, bf16[1024,128]{1,0:T(8,128)(2,1)S(1)}, u32[]{:S(2)}, u32[]{:S(2)}) collective-permute-start(bf16[1024,128]{1,0:T(8,128)(2,1)S(1)} %get-tuple-element.72), channel_id=1, source_target_pairs={{0,8},{1,9},{2,10},{3,11},{4,12},{5,13},{6,14},{7,15},{8,0},{9,1},... | collective-permute-start | bytes 786440 | tf_op jit(solution)/shard_map/ppermute | solution.py:604
  122.2 8.7 %collective-permute-start.31 = (f32[4096]{0:T(1024)S(1)}, f32[4096]{0:T(1024)S(1)}, u32[]{:S(2)}, u32[]{:S(2)}) collective-permute-start(f32[4096]{0:T(1024)S(1)} %bitcast.47), channel_id=1, source_target_pairs={{0,6},{1,7},{2,4},{3,5},{4,2},{5,3},{6,0},{7,1},{8,14},{9,15},{10,... | collective-permute-start | bytes 49160 | tf_op jit(solution)/shard_map/ppermute | solution.py:604
  123.7 8.5 %collective-permute-start.30 = (f32[4096]{0:T(1024)S(1)}, f32[4096]{0:T(1024)S(1)}, u32[]{:S(2)}, u32[]{:S(2)}) collective-permute-start(f32[4096]{0:T(1024)S(1)} %bitcast.48), channel_id=1, source_target_pairs={{0,4},{1,5},{2,6},{3,7},{4,0},{5,1},{6,2},{7,3},{8,12},{9,13},{10,... | collective-permute-start | bytes 49160 | tf_op jit(solution)/shard_map/ppermute | solution.py:604
  124.6 7.6 %collective-permute-start.29 = (f32[4096]{0:T(1024)S(1)}, f32[4096]{0:T(1024)S(1)}, u32[]{:S(2)}, u32[]{:S(2)}) collective-permute-start(f32[4096]{0:T(1024)S(1)} %bitcast.49), channel_id=1, source_target_pairs={{0,2},{1,3},{2,0},{3,1},{4,6},{5,7},{6,4},{7,5},{8,10},{9,11},{10,... | collective-permute-start | bytes 49160 | tf_op jit(solution)/shard_map/ppermute | solution.py:604
  129.6 4.6 %collective-permute-start.32 = (bf16[1024,128]{1,0:T(8,128)(2,1)S(1)}, bf16[1024,128]{1,0:T(8,128)(2,1)S(1)}, u32[]{:S(2)}, u32[]{:S(2)}) collective-permute-start(bf16[1024,128]{1,0:T(8,128)(2,1)S(1)} %get-tuple-element.80), channel_id=1, source_target_pairs={{0,8},{1,9},{2,10},{3,11},{4,12},{5,13},{6,14},{7,15},{8,0},{9,1},... | collective-permute-start | bytes 786440 | tf_op jit(solution)/shard_map/ppermute | solution.py:604
  129.8 12.0 %collective-permute-start.37 = (bf16[512,128]{1,0:T(8,128)(2,1)S(1)}, bf16[512,128]{1,0:T(8,128)(2,1)S(1)}, u32[]{:S(2)}, u32[]{:S(2)}) collective-permute-start(bf16[512,128]{1,0:T(8,128)(2,1)S(1)} %get-tuple-element.90), channel_id=1, source_target_pairs={{0,4},{1,5},{2,6},{3,7},{4,0},{5,1},{6,2},{7,3},{8,12},{9,13},{10,... | collective-permute-start | bytes 393224 | tf_op jit(solution)/shard_map/ppermute | solution.py:604
  130.9 14.0 %collective-permute-start.38 = (bf16[512,128]{1,0:T(8,128)(2,1)S(1)}, bf16[512,128]{1,0:T(8,128)(2,1)S(1)}, u32[]{:S(2)}, u32[]{:S(2)}) collective-permute-start(bf16[512,128]{1,0:T(8,128)(2,1)S(1)} %get-tuple-element.91), channel_id=1, source_target_pairs={{0,6},{1,7},{2,4},{3,5},{4,2},{5,3},{6,0},{7,1},{8,14},{9,15},{10,... | collective-permute-start | bytes 393224 | tf_op jit(solution)/shard_map/ppermute | solution.py:604
  134.3 10.6 %collective-permute-start.36 = (bf16[512,128]{1,0:T(8,128)(2,1)S(1)}, bf16[512,128]{1,0:T(8,128)(2,1)S(1)}, u32[]{:S(2)}, u32[]{:S(2)}) collective-permute-start(bf16[512,128]{1,0:T(8,128)(2,1)S(1)} %get-tuple-element.89), channel_id=1, source_target_pairs={{0,2},{1,3},{2,0},{3,1},{4,6},{5,7},{6,4},{7,5},{8,10},{9,11},{10,... | collective-permute-start | bytes 393224 | tf_op jit(solution)/shard_map/ppermute | solution.py:604
  135.5 9.5 %collective-permute-start.35 = (bf16[512,128]{1,0:T(8,128)(2,1)S(1)}, bf16[512,128]{1,0:T(8,128)(2,1)S(1)}, u32[]{:S(2)}, u32[]{:S(2)}) collective-permute-start(bf16[512,128]{1,0:T(8,128)(2,1)S(1)} %get-tuple-element.87), channel_id=1, source_target_pairs={{0,17},{1,16},{2,19},{3,18},{4,21},{5,20},{6,23},{7,22},{8,25},{9,... | collective-permute-start | bytes 393224 | tf_op jit(solution)/shard_map/ppermute | solution.py:604
  138.5 6.5 %collective-permute-start.33 = (bf16[512,128]{1,0:T(8,128)(2,1)S(1)}, bf16[512,128]{1,0:T(8,128)(2,1)S(1)}, u32[]{:S(2)}, u32[]{:S(2)}) collective-permute-start(bf16[512,128]{1,0:T(8,128)(2,1)S(1)} %get-tuple-element.85), channel_id=1, source_target_pairs={{0,1},{1,0},{2,3},{3,2},{4,5},{5,4},{6,7},{7,6},{8,9},{9,8},{10,11... | collective-permute-start | bytes 393224 | tf_op jit(solution)/shard_map/ppermute | solution.py:604
  141.8 5.4 %collective-permute-start.34 = (bf16[512,128]{1,0:T(8,128)(2,1)S(1)}, bf16[512,128]{1,0:T(8,128)(2,1)S(1)}, u32[]{:S(2)}, u32[]{:S(2)}) collective-permute-start(bf16[512,128]{1,0:T(8,128)(2,1)S(1)} %get-tuple-element.86), channel_id=1, source_target_pairs={{0,16},{1,17},{2,18},{3,19},{4,20},{5,21},{6,22},{7,23},{8,24},{9,... | collective-permute-start | bytes 393224 | tf_op jit(solution)/shard_map/ppermute | solution.py:604

commit v17 on v15

--- a/solution.py
+++ b/solution.py
@@ -287,8 +287,8 @@
     width = 512 if kernel is column_kernel else 256
     scratch = [pltpu.VMEM((16, size), jnp.bfloat16)]
     if kernel is not column_kernel:
-        part = 3 if kernel is row_kernel else 1
-        scratch.append(pltpu.VMEM((e.shape[0] * part // 4, 128), jnp.float32))
+        part = 7 if kernel is row_kernel else 6
+        scratch.append(pltpu.VMEM((e.shape[0] * part // 8, 128), jnp.float32))
     if kernel is row_kernel:
         scratch.append(pltpu.VMEM((1, size), jnp.float32))
     return pl.pallas_call(
@@ -677,9 +677,10 @@
     parts = [swap(part, along[z + 1]) for z, part in enumerate(parts)]
     last = swap(last, across[na - 1])
     sent = other_rows(list(range(1, na - 1)), share_x, x, yb, e, alpha, jnp.bfloat16)
-    sent = [swap(part, across[s + 1]) for s, part in enumerate(sent)] + [last]
+    sent = [swap(part, across[s + 1]) for s, part in enumerate(sent)]
+    last, yb = lax.optimization_barrier((last, yb))
     gi, = other_rows([0], share_x, x, yb, e, alpha, jnp.float32)
-    grad_imu, grad_cam = add_up([gi, *sent], [grad_cam, *parts, *far_gc], scale)
+    grad_imu, grad_cam = add_up([gi, *sent, last], [grad_cam, *parts, *far_gc], scale)
     return grad_imu, grad_cam[None]
 
 

time: 147 us -> 145 us (0.986)
  starting transfers between devices: 42.1 us -> 40 us
    ppermute x39, starting transfers between devices: 42.1 us -> 40 us  [swap(): lax.ppermute(value, ('row', 'col'), [(i, i ^ mask) for i in range(self.co...]
where the time goes in v17:
time: 145 us
  Pallas kernels  78.6 us (54%)
  starting transfers between devices  40 us (28%)
  waiting for transfers between devices  23.6 us (16%)
    ppermute x39, starting transfers between devices, swap(): lax.ppermute(value, ('row', 'col'), [(i, i ^ mask) for i in range(self.co...  40 us
    pallas_call x1, Pallas kernels, column_lse(): pl.pallas_call(functools.partial(column_lse_kernel, width, chunk, len(got...  30 us
    ppermute x39, waiting for transfers between devices, swap(): lax.ppermute(value, ('row', 'col'), [(i, i ^ mask) for i in range(self.co...  23.6 us
    pallas_call x4, Pallas kernels, weighted(): pl.pallas_call(functools.partial(kernel, width, tuple(shifts), parts), ou...  12.3 us
    pallas_call x1, Pallas kernels, row_lse_late(): pl.pallas_call(functools.partial(row_lse_late_kernel, width, len(ys)), ou...  9.94 us
    pallas_call x1, Pallas kernels, row_lse_middle(): pl.pallas_call(functools.partial(row_lse_middle_kernel, width, len(ys)),...  6.45 us
    pallas_call x1, Pallas kernels, row_lse_early(): pl.pallas_call(functools.partial(row_lse_early_kernel, width, len(xs)), o...  6.45 us
    pallas_call x2, Pallas kernels, column_grad(): pl.pallas_call(functools.partial(kernel, blocks, share), out_shape=out_sh...  6.18 us
  transfers between devices with their start and end apart: 39, of which 20 were waited for; matrix products, arithmetic and copies ran while one was open for 1% of the time, Pallas kernels for 15%

profile of v17, /device:TPU:0, one launch (start us, length us, event | category | flops | bytes accessed | tf_op | source)
XLA Modules:
  0.0 145.0 jit_solution(11457568931652069524)
XLA Ops:
  0.6 3.0 %collective-permute-start = (bf16[512,128]{1,0:T(8,128)(2,1)}, bf16[512,128]{1,0:T(8,128)(2,1)S(1)}, u32[]{:S(2)}, u32[]{:S(2)}) collective-permute-start(bf16[512,128]{1,0:T(8,128)(2,1)} %param.4), channel_id=1, source_target_pairs={{0,1},{1,0},{2,3},{3,2},{4,5},{5,4},{6,7},{7,6},{8,9},{9,8},{10,11... | collective-permute-start | bytes 393224 | tf_op jit(solution)/shard_map/ppermute | solution.py:609
  3.7 1.4 collective-permute-start.2
  5.2 3.0 %collective-permute-start.4 = (bf16[512,128]{1,0:T(8,128)(2,1)}, bf16[512,128]{1,0:T(8,128)(2,1)S(1)}, u32[]{:S(2)}, u32[]{:S(2)}) collective-permute-start(bf16[512,128]{1,0:T(8,128)(2,1)} %bitcast.77), channel_id=1, source_target_pairs={{0,4},{1,5},{2,6},{3,7},{4,0},{5,1},{6,2},{7,3},{8,12},{9,13},{10,... | collective-permute-start | bytes 393224 | tf_op jit(solution)/shard_map/ppermute | solution.py:609
  10.2 1.6 %collective-permute-start.5 = (bf16[512,128]{1,0:T(8,128)(2,1)}, bf16[512,128]{1,0:T(8,128)(2,1)S(1)}, u32[]{:S(2)}, u32[]{:S(2)}) collective-permute-start(bf16[512,128]{1,0:T(8,128)(2,1)} %bitcast.80), channel_id=1, source_target_pairs={{0,2},{1,3},{2,0},{3,1},{4,6},{5,7},{6,4},{7,5},{8,10},{9,11},{10,... | collective-permute-start | bytes 393224 | tf_op jit(solution)/shard_map/ppermute | solution.py:609
  11.8 6.4 %row_lse_early.1 = (bf16[2048,128]{1,0:T(8,128)(2,1)S(1)}, bf16[128,2048]{1,0:T(8,128)(2,1)S(1)}, f32[1,2048]{1,0:T(1,128)S(1)}) custom-call(bf16[1024,128]{1,0:T(8,128)(2,1)S(1)} %pad_maximum_fusion.own_ref, bf16[512,128]{1,0:T(8,128)(2,1)S(1)} %collective-permute-done.refs_0_, bf16[512,128]{1,0:T(8,128)(2,1)S(1)} %collective-permute-done.1.refs_1_, ...), custom_call_target="tpu_custom_call" | custom-call | flops 536870912 | bytes 786432 | tf_op jit(solution)/shard_map/row_lse_early/pallas_call | solution.py:325
  19.0 6.5 %row_lse_middle.1.first_ref = f32[1,2048]{1,0:T(1,128)S(1)} custom-call(bf16[2048,128]{1,0:T(8,128)(2,1)S(1)} %get-tuple-element.52.x_ref, f32[1,2048]{1,0:T(1,128)S(1)} %get-tuple-element.55.first_ref, bf16[512,128]{1,0:T(8,128)(2,1)S(1)} %collective-permute-done.5.refs_0_, bf16[512,128]{1,0:T(8,128)(2,1)S(1)} %collective-permute-done.4.refs_1_), custom_call_target="tpu_custom_call" | custom-call | flops 536870912 | bytes 786432 | tf_op jit(solution)/shard_map/row_lse_middle/pallas_call | solution.py:340
  25.6 1.3 collective-permute-done.9.refs_6_
  26.8 9.9 %row_lse_late.1 = (bf16[4096,128]{1,0:T(8,128)(2,1)S(1)}, f32[1,3072]{1,0:T(1,128)S(1)}) custom-call(bf16[1024,128]{1,0:T(8,128)(2,1)S(1)} %pad_maximum_fusion.own_ref, f32[1,2048]{1,0:T(1,128)S(1)} %bitcast.66, bf16[2048,128]{1,0:T(8,128)(2,1)S(1)} %get-tuple-element.52.x_ref, f32[1,2048]{1,0:T(1,128)S(1)} %row_lse_middle.1.first_ref, ...), custom_call_target="tpu_custom_call" | custom-call | flops 1073741824 | bytes 1048576 | tf_op jit(solution)/shard_map/row_lse_late/pallas_call | solution.py:359
  37.3 2.5 %collective-permute-start.11 = (f32[3072]{0:T(1024)S(1)}, f32[3072]{0:T(1024)S(1)}, u32[]{:S(2)}, u32[]{:S(2)}) collective-permute-start(f32[3072]{0:T(1024)S(1)} %bitcast.72), channel_id=1, source_target_pairs={{0,16},{1,17},{2,18},{3,19},{4,20},{5,21},{6,22},{7,23},{8,24},{9,... | collective-permute-start | bytes 36872 | tf_op jit(solution)/shard_map/ppermute | solution.py:609
  40.3 1.1 collective-permute-done.12
  41.6 1.9 %collective-permute-done.10 = f32[3072]{0:T(1024)S(1)} collective-permute-done((f32[3072]{0:T(1024)S(1)}, f32[3072]{0:T(1024)S(1)}, u32[]{:S(2)}, u32[]{:S(2)}) %collective-permute-start.10) | collective-permute-done | bytes 12320 | tf_op jit(solution)/shard_map/ppermute | solution.py:609
  43.5 30.0 %column_lse.1 = (f32[1,5120]{1,0:T(1,128)S(1)}, bf16[2048,4096]{1,0:T(8,128)(2,1)S(1)}, f32[1,4096]{1,0:T(1,128)S(1)}, f32[1,2048]{1,0:T(1,128)S(1)}) custom-call(bf16[2048,128]{1,0:T(8,128)(2,1)S(1)} %get-tuple-element.52.x_ref, bf16[4096,128]{1,0:T(8,128)(2,1)S(1)} %get-tuple-element.59.y_ref, f32[1,2048]{1,0:T(1,128)S(1)} %bitcast.67, ...), custom_call_target="tpu_custom_call" | custom-call | flops 2147483648 | bytes 1572864 | tf_op jit(solution)/shard_map/column_lse/pallas_call | solution.py:373
  73.7 1.2 collective-permute-done.13
  74.9 1.3 collective-permute-start.16
  76.2 1.5 %collective-permute-start.15 = (f32[5120]{0:T(1024)S(1)}, f32[5120]{0:T(1024)S(1)}, u32[]{:S(2)}, u32[]{:S(2)}) collective-permute-start(f32[5120]{0:T(1024)S(1)} %bitcast.34), channel_id=1, source_target_pairs={{0,4},{1,5},{2,6},{3,7},{4,0},{5,1},{6,2},{7,3},{8,12},{9,13},{10,... | collective-permute-start | bytes 61448 | tf_op jit(solution)/shard_map/ppermute | solution.py:609
  77.8 1.6 %collective-permute-start.14 = (f32[5120]{0:T(1024)S(1)}, f32[5120]{0:T(1024)S(1)}, u32[]{:S(2)}, u32[]{:S(2)}) collective-permute-start(f32[5120]{0:T(1024)S(1)} %bitcast.35), channel_id=1, source_target_pairs={{0,2},{1,3},{2,0},{3,1},{4,6},{5,7},{6,4},{7,5},{8,10},{9,11},{10,... | collective-permute-start | bytes 61448 | tf_op jit(solution)/shard_map/ppermute | solution.py:609
  79.3 1.3 collective-permute-done.16
  81.5 3.6 %weighted_sum.4 = (f32[1,2048]{1,0:T(1,128)S(1)}, f32[1,4096]{1,0:T(1,128)S(1)}, f32[1,4096]{1,0:T(1,128)S(1)}) custom-call(bf16[2048,4096]{1,0:T(8,128)(2,1)S(1)} %get-tuple-element.61.e_ref, f32[1,4096]{1,0:T(1,128)S(1)} %get-tuple-element.64.shift_ref, f32[1,5120]{1,0:T(1,128)S(1)} %pair.3.refs_0_, f32[1,5120]{1,0:T(1,128)S(1)} %bitcast.44, ...), custom_call_target="tpu_custom_call" | custom-call | flops 16777216 | bytes 16777216 | tf_op jit(solution)/shard_map/weighted_sum/pallas_call | solution.py:294
  86.8 1.8 %collective-permute-start.17 = (f32[2048]{0:T(1024)S(1)}, f32[2048]{0:T(1024)S(1)}, u32[]{:S(2)}, u32[]{:S(2)}) collective-permute-start(f32[2048]{0:T(1024)S(1)} %bitcast.59), channel_id=1, source_target_pairs={{0,1},{1,0},{2,3},{3,2},{4,5},{5,4},{6,7},{7,6},{8,9},{9,8},{10,11... | collective-permute-start | bytes 24584 | tf_op jit(solution)/shard_map/ppermute | solution.py:609
  88.7 1.1 collective-permute-done.19
  90.5 2.8 %weighted_sum.5 = (f32[1,4096]{1,0:T(1,128)S(1)}, f32[1,2048]{1,0:T(1,128)}) custom-call(bf16[2048,4096]{1,0:T(8,128)(2,1)S(1)} %get-tuple-element.61.e_ref, f32[1,2048]{1,0:T(1,128)S(1)} %get-tuple-element.63.a_ref, f32[1,4096]{1,0:T(1,128)S(1)} %get-tuple-element.66.first_ref, f32[1,2048]{1,0:T(1,128)S(1)} %get-tuple-element.68.refs_0_, ...), custom_call_target="tpu_custom_call" | custom-call | flops 16777216 | bytes 16777216 | tf_op jit(solution)/shard_map/weighted_sum/pallas_call | solution.py:294
  93.3 1.2 collective-permute-done.20
  94.5 2.7 %collective-permute-start.23 = (f32[4096]{0:T(1024)S(1)}, f32[4096]{0:T(1024)S(1)}, u32[]{:S(2)}, u32[]{:S(2)}) collective-permute-start(f32[4096]{0:T(1024)S(1)} %bitcast.36), channel_id=1, source_target_pairs={{0,6},{1,7},{2,4},{3,5},{4,2},{5,3},{6,0},{7,1},{8,14},{9,15},{10,... | collective-permute-start | bytes 49160 | tf_op jit(solution)/shard_map/ppermute | solution.py:609
  97.9 1.0 collective-permute-start.21
  98.9 1.2 collective-permute-done.23
  100.1 1.7 %collective-permute-done.22 = f32[4096]{0:T(1024)S(1)} collective-permute-done((f32[4096]{0:T(1024)S(1)}, f32[4096]{0:T(1024)S(1)}, u32[]{:S(2)}, u32[]{:S(2)}) %collective-permute-start.22) | collective-permute-done | bytes 16416 | tf_op jit(solution)/shard_map/ppermute | solution.py:609
  101.8 3.6 %weighted_sum.6.refs_0_ = f32[1,2048]{1,0:T(1,128)S(1)} custom-call(bf16[2048,4096]{1,0:T(8,128)(2,1)S(1)} %get-tuple-element.61.e_ref, f32[1,4096]{1,0:T(1,128)S(1)} %get-tuple-element.66.first_ref, f32[1,4096]{1,0:T(1,128)S(1)} %get-tuple-element.67.b_ref, f32[1,4096]{1,0:T(1,128)S(1)} %pair.4.refs_0_, f32[1,4096]{1,0:T(1,128)S(1)} %bitcast.56, ...), custom_call_target="tpu_custom_call" | custom-call | flops 16777216 | bytes 16777216 | tf_op jit(solution)/shard_map/weighted_sum/pallas_call | solution.py:294
  105.4 1.7 %collective-permute-start.26 = (f32[2048]{0:T(1024)S(1)}, f32[2048]{0:T(1024)S(1)}, u32[]{:S(2)}, u32[]{:S(2)}) collective-permute-start(f32[2048]{0:T(1024)S(1)} %bitcast.39), channel_id=1, source_target_pairs={{0,17},{1,16},{2,19},{3,18},{4,21},{5,20},{6,23},{7,22},{8,25},{9,... | collective-permute-start | bytes 24584 | tf_op jit(solution)/shard_map/ppermute | solution.py:609
  107.1 1.9 %collective-permute-start.25 = (f32[2048]{0:T(1024)S(1)}, f32[2048]{0:T(1024)S(1)}, u32[]{:S(2)}, u32[]{:S(2)}) collective-permute-start(f32[2048]{0:T(1024)S(1)} %bitcast.40), channel_id=1, source_target_pairs={{0,16},{1,17},{2,18},{3,19},{4,20},{5,21},{6,22},{7,23},{8,24},{9,... | collective-permute-start | bytes 24584 | tf_op jit(solution)/shard_map/ppermute | solution.py:609
  109.0 1.1 collective-permute-done.26
  110.8 1.9 %collective-permute-done.24 = f32[2048]{0:T(1024)S(1)} collective-permute-done((f32[2048]{0:T(1024)S(1)}, f32[2048]{0:T(1024)S(1)}, u32[]{:S(2)}, u32[]{:S(2)}) %collective-permute-start.24) | collective-permute-done | bytes 8224 | tf_op jit(solution)/shard_map/ppermute | solution.py:609
  112.6 2.3 %weighted_sum.7 = (f32[1,4096]{1,0:T(1,128)S(1)}, f32[1,2048]{1,0:T(1,128)S(1)}) custom-call(bf16[2048,4096]{1,0:T(8,128)(2,1)S(1)} %get-tuple-element.61.e_ref, f32[1,2048]{1,0:T(1,128)S(1)} %get-tuple-element.63.a_ref, f32[1,4096]{1,0:T(1,128)S(1)} %get-tuple-element.66.first_ref, f32[1,2048]{1,0:T(1,128)S(1)} %weighted_sum.6.refs_0_, ...), custom_call_target="tpu_custom_call" | custom-call | flops 16777216 | bytes 16777216 | tf_op jit(solution)/shard_map/weighted_sum/pallas_call | solution.py:294
  115.0 1.2 collective-permute-done.27
  116.2 3.2 %column_grad.2 = (f32[1024,128]{1,0:T(8,128)S(1)}, bf16[1024,128]{1,0:T(8,128)(2,1)S(1)}, bf16[256,2048]{1,0:T(8,128)(2,1)S(1)}) custom-call(bf16[128,2048]{1,0:T(8,128)(2,1)S(1)} %get-tuple-element.62.xt_ref, bf16[4096,128]{1,0:T(8,128)(2,1)S(1)} %get-tuple-element.59.y_ref, bf16[2048,4096]{1,0:T(8,128)(2,1)S(1)} %get-tuple-element.61.e_ref, ...), custom_call_target="tpu_custom_call" | custom-call | flops 2147483648 | bytes 8388608 | tf_op jit(solution)/shard_map/column_grad/pallas_call | solution.py:455
  119.7 1.5 %collective-permute-start.31 = (f32[4096]{0:T(1024)S(1)}, f32[4096]{0:T(1024)S(1)}, u32[]{:S(2)}, u32[]{:S(2)}) collective-permute-start(f32[4096]{0:T(1024)S(1)} %bitcast.47), channel_id=1, source_target_pairs={{0,6},{1,7},{2,4},{3,5},{4,2},{5,3},{6,0},{7,1},{8,14},{9,15},{10,... | collective-permute-start | bytes 49160 | tf_op jit(solution)/shard_map/ppermute | solution.py:609
  121.8 2.3 %collective-permute-start.29 = (f32[4096]{0:T(1024)S(1)}, f32[4096]{0:T(1024)S(1)}, u32[]{:S(2)}, u32[]{:S(2)}) collective-permute-start(f32[4096]{0:T(1024)S(1)} %bitcast.49), channel_id=1, source_target_pairs={{0,2},{1,3},{2,0},{3,1},{4,6},{5,7},{6,4},{7,5},{8,10},{9,11},{10,... | collective-permute-start | bytes 49160 | tf_op jit(solution)/shard_map/ppermute | solution.py:609
  124.1 3.0 %column_grad.3 = (f32[1024,128]{1,0:T(8,128)S(1)}, bf16[1024,128]{1,0:T(8,128)(2,1)S(1)}) custom-call(bf16[256,2048]{1,0:T(8,128)(2,1)S(1)} %get-tuple-element.81.xa_ref, bf16[4096,128]{1,0:T(8,128)(2,1)S(1)} %get-tuple-element.59.y_ref, bf16[2048,4096]{1,0:T(8,128)(2,1)S(1)} %get-tuple-element.61.e_ref, f32[1,4096]{1,0:T(1,128)S(1)} %get-tuple-element.66.first_ref), custom_call_target="tpu_custom_call" | custom-call | flops 2147483648 | bytes 8388608 | tf_op jit(solution)/shard_map/column_grad/pallas_call | solution.py:455
  127.2 1.2 collective-permute-start.37
  128.4 1.2 collective-permute-start.38
  129.6 2.1 %first_rows.1 = (bf16[4096,256]{1,0:T(8,128)(2,1)S(1)}, f32[1,512]{1,0:T(1,128)S(1)}, bf16[512,128]{1,0:T(8,128)(2,1)S(1)}) custom-call(bf16[2048,128]{1,0:T(8,128)(2,1)S(1)} %get-tuple-element.52.x_ref, bf16[4096,128]{1,0:T(8,128)(2,1)S(1)} %get-tuple-element.59.y_ref, bf16[2048,4096]{1,0:T(8,128)(2,1)S(1)} %get-tuple-element.61.e_ref, ...), custom_call_target="tpu_custom_call" | custom-call | flops 34359738368 | bytes 134217728 | tf_op jit(solution)/shard_map/first_rows/pallas_call | solution.py:529
  131.8 1.2 collective-permute-start.36
  133.1 2.6 %other_rows.3 = (bf16[512,128]{1,0:T(8,128)(2,1)S(1)}, bf16[512,128]{1,0:T(8,128)(2,1)S(1)}) custom-call(bf16[2048,128]{1,0:T(8,128)(2,1)S(1)} %get-tuple-element.52.x_ref, bf16[4096,256]{1,0:T(8,128)(2,1)S(1)} %get-tuple-element.88.yb_ref, bf16[2048,4096]{1,0:T(8,128)(2,1)S(1)} %get-tuple-element.61.e_ref, f32[1,2048]{1,0:T(1,128)S(1)} %get-tuple-element.77.alpha_ref), custom_call_target="tpu_custom_call" | custom-call | flops 2147483648 | bytes 8388608 | tf_op jit(solution)/shard_map/other_rows/pallas_call | solution.py:547
  135.7 1.5 %collective-permute-start.34 = (bf16[512,128]{1,0:T(8,128)(2,1)S(1)}, bf16[512,128]{1,0:T(8,128)(2,1)S(1)}, u32[]{:S(2)}, u32[]{:S(2)}) collective-permute-start(bf16[512,128]{1,0:T(8,128)(2,1)S(1)} %get-tuple-element.89), channel_id=1, source_target_pairs={{0,1},{1,0},{2,3},{3,2},{4,5},{5,4},{6,7},{7,6},{8,9},{9,8},{10,11... | collective-permute-start | bytes 393224 | tf_op jit(solution)/shard_map/ppermute | solution.py:609
  137.3 1.7 %collective-permute-done.32.refs_3_ = bf16[512,128]{1,0:T(8,128)(2,1)S(1)} collective-permute-done((bf16[512,128]{1,0:T(8,128)(2,1)S(1)}, bf16[512,128]{1,0:T(8,128)(2,1)S(1)}, u32[]{:S(2)}, u32[]{:S(2)}) %collective-permute-start.32) | collective-permute-done | bytes 131104 | tf_op jit(solution)/shard_map/ppermute | solution.py:609
  139.2 1.4 other_rows.2.refs_0_
  140.7 1.2 collective-permute-done.36.refs_5_
  141.9 2.0 %collective-permute-done.35.refs_2_ = bf16[512,128]{1,0:T(8,128)(2,1)S(1)} collective-permute-done((bf16[512,128]{1,0:T(8,128)(2,1)S(1)}, bf16[512,128]{1,0:T(8,128)(2,1)S(1)}, u32[]{:S(2)}, u32[]{:S(2)}) %collective-permute-start.35) | collective-permute-done | bytes 131104 | tf_op jit(solution)/shard_map/ppermute | solution.py:609
  144.0 1.1 add_up.1
  (52 shorter events, 10.5 us)
Async XLA Ops:
  0.6 9.5 %collective-permute-start = (bf16[512,128]{1,0:T(8,128)(2,1)}, bf16[512,128]{1,0:T(8,128)(2,1)S(1)}, u32[]{:S(2)}, u32[]{:S(2)}) collective-permute-start(bf16[512,128]{1,0:T(8,128)(2,1)} %param.4), channel_id=1, source_target_pairs={{0,1},{1,0},{2,3},{3,2},{4,5},{5,4},{6,7},{7,6},{8,9},{9,8},{10,11... | collective-permute-start | bytes 393224 | tf_op jit(solution)/shard_map/ppermute | solution.py:609
  3.7 8.2 %collective-permute-start.2 = (bf16[512,128]{1,0:T(8,128)(2,1)}, bf16[512,128]{1,0:T(8,128)(2,1)S(1)}, u32[]{:S(2)}, u32[]{:S(2)}) collective-permute-start(bf16[512,128]{1,0:T(8,128)(2,1)} %param.4), channel_id=1, source_target_pairs={{0,17},{1,16},{2,19},{3,18},{4,21},{5,20},{6,23},{7,22},{8,25},{9,... | collective-permute-start | bytes 393224 | tf_op jit(solution)/shard_map/ppermute | solution.py:609
  5.1 6.7 %collective-permute-start.1 = (bf16[512,128]{1,0:T(8,128)(2,1)}, bf16[512,128]{1,0:T(8,128)(2,1)S(1)}, u32[]{:S(2)}, u32[]{:S(2)}) collective-permute-start(bf16[512,128]{1,0:T(8,128)(2,1)} %param.4), channel_id=1, source_target_pairs={{0,16},{1,17},{2,18},{3,19},{4,20},{5,21},{6,22},{7,23},{8,24},{9,... | collective-permute-start | bytes 393224 | tf_op jit(solution)/shard_map/ppermute | solution.py:609
  5.2 13.1 %collective-permute-start.4 = (bf16[512,128]{1,0:T(8,128)(2,1)}, bf16[512,128]{1,0:T(8,128)(2,1)S(1)}, u32[]{:S(2)}, u32[]{:S(2)}) collective-permute-start(bf16[512,128]{1,0:T(8,128)(2,1)} %bitcast.77), channel_id=1, source_target_pairs={{0,4},{1,5},{2,6},{3,7},{4,0},{5,1},{6,2},{7,3},{8,12},{9,13},{10,... | collective-permute-start | bytes 393224 | tf_op jit(solution)/shard_map/ppermute | solution.py:609
  9.2 2.6 %collective-permute-start.3 = (bf16[512,128]{1,0:T(8,128)(2,1)}, bf16[512,128]{1,0:T(8,128)(2,1)S(1)}, u32[]{:S(2)}, u32[]{:S(2)}) collective-permute-start(bf16[512,128]{1,0:T(8,128)(2,1)} %bitcast.79), channel_id=1, source_target_pairs={{0,8},{1,9},{2,10},{3,11},{4,12},{5,13},{6,14},{7,15},{8,0},{9,1},... | collective-permute-start | bytes 393224 | tf_op jit(solution)/shard_map/ppermute | solution.py:609
  10.2 8.3 %collective-permute-start.5 = (bf16[512,128]{1,0:T(8,128)(2,1)}, bf16[512,128]{1,0:T(8,128)(2,1)S(1)}, u32[]{:S(2)}, u32[]{:S(2)}) collective-permute-start(bf16[512,128]{1,0:T(8,128)(2,1)} %bitcast.80), channel_id=1, source_target_pairs={{0,2},{1,3},{2,0},{3,1},{4,6},{5,7},{6,4},{7,5},{8,10},{9,11},{10,... | collective-permute-start | bytes 393224 | tf_op jit(solution)/shard_map/ppermute | solution.py:609
  18.3 7.1 %collective-permute-start.6 = (bf16[512,128]{1,0:T(8,128)(2,1)S(1)}, bf16[512,128]{1,0:T(8,128)(2,1)S(1)}, u32[]{:S(2)}, u32[]{:S(2)}) collective-permute-start(bf16[512,128]{1,0:T(8,128)(2,1)S(1)} %collective-permute-done.4.refs_1_), channel_id=1, source_target_pairs={{0,2},{1,3},{2,0},{3,1},{4,6},{5,7},{6,4},{7,5},{8,10},{9,11},{10,... | collective-permute-start | bytes 393224 | tf_op jit(solution)/shard_map/ppermute | solution.py:609
  18.4 7.2 %collective-permute-start.8 = (bf16[512,128]{1,0:T(8,128)(2,1)S(1)}, bf16[512,128]{1,0:T(8,128)(2,1)S(1)}, u32[]{:S(2)}, u32[]{:S(2)}) collective-permute-start(bf16[512,128]{1,0:T(8,128)(2,1)S(1)} %collective-permute-done.4.refs_1_), channel_id=1, source_target_pairs={{0,8},{1,9},{2,10},{3,11},{4,12},{5,13},{6,14},{7,15},{8,0},{9,1},... | collective-permute-start | bytes 393224 | tf_op jit(solution)/shard_map/ppermute | solution.py:609
  18.5 7.1 %collective-permute-start.7 = (bf16[512,128]{1,0:T(8,128)(2,1)S(1)}, bf16[512,128]{1,0:T(8,128)(2,1)S(1)}, u32[]{:S(2)}, u32[]{:S(2)}) collective-permute-start(bf16[512,128]{1,0:T(8,128)(2,1)S(1)} %collective-permute-done.5.refs_0_), channel_id=1, source_target_pairs={{0,8},{1,9},{2,10},{3,11},{4,12},{5,13},{6,14},{7,15},{8,0},{9,1},... | collective-permute-start | bytes 393224 | tf_op jit(solution)/shard_map/ppermute | solution.py:609
  25.4 1.4 collective-permute-start.9
  36.8 4.7 %collective-permute-start.12 = (f32[3072]{0:T(1024)S(1)}, f32[3072]{0:T(1024)S(1)}, u32[]{:S(2)}, u32[]{:S(2)}) collective-permute-start(f32[3072]{0:T(1024)S(1)} %bitcast.71), channel_id=1, source_target_pairs={{0,17},{1,16},{2,19},{3,18},{4,21},{5,20},{6,23},{7,22},{8,25},{9,... | collective-permute-start | bytes 36872 | tf_op jit(solution)/shard_map/ppermute | solution.py:609
  37.3 4.3 %collective-permute-start.11 = (f32[3072]{0:T(1024)S(1)}, f32[3072]{0:T(1024)S(1)}, u32[]{:S(2)}, u32[]{:S(2)}) collective-permute-start(f32[3072]{0:T(1024)S(1)} %bitcast.72), channel_id=1, source_target_pairs={{0,16},{1,17},{2,18},{3,19},{4,20},{5,21},{6,22},{7,23},{8,24},{9,... | collective-permute-start | bytes 36872 | tf_op jit(solution)/shard_map/ppermute | solution.py:609
  39.8 3.7 %collective-permute-start.10 = (f32[3072]{0:T(1024)S(1)}, f32[3072]{0:T(1024)S(1)}, u32[]{:S(2)}, u32[]{:S(2)}) collective-permute-start(f32[3072]{0:T(1024)S(1)} %bitcast.73), channel_id=1, source_target_pairs={{0,1},{1,0},{2,3},{3,2},{4,5},{5,4},{6,7},{7,6},{8,9},{9,8},{10,11... | collective-permute-start | bytes 36872 | tf_op jit(solution)/shard_map/ppermute | solution.py:609
  73.6 1.3 collective-permute-start.13
  74.9 5.8 %collective-permute-start.16 = (f32[5120]{0:T(1024)S(1)}, f32[5120]{0:T(1024)S(1)}, u32[]{:S(2)}, u32[]{:S(2)}) collective-permute-start(f32[5120]{0:T(1024)S(1)} %bitcast.33), channel_id=1, source_target_pairs={{0,6},{1,7},{2,4},{3,5},{4,2},{5,3},{6,0},{7,1},{8,14},{9,15},{10,... | collective-permute-start | bytes 61448 | tf_op jit(solution)/shard_map/ppermute | solution.py:609
  76.2 4.7 %collective-permute-start.15 = (f32[5120]{0:T(1024)S(1)}, f32[5120]{0:T(1024)S(1)}, u32[]{:S(2)}, u32[]{:S(2)}) collective-permute-start(f32[5120]{0:T(1024)S(1)} %bitcast.34), channel_id=1, source_target_pairs={{0,4},{1,5},{2,6},{3,7},{4,0},{5,1},{6,2},{7,3},{8,12},{9,13},{10,... | collective-permute-start | bytes 61448 | tf_op jit(solution)/shard_map/ppermute | solution.py:609
  77.8 3.8 %collective-permute-start.14 = (f32[5120]{0:T(1024)S(1)}, f32[5120]{0:T(1024)S(1)}, u32[]{:S(2)}, u32[]{:S(2)}) collective-permute-start(f32[5120]{0:T(1024)S(1)} %bitcast.35), channel_id=1, source_target_pairs={{0,2},{1,3},{2,0},{3,1},{4,6},{5,7},{6,4},{7,5},{8,10},{9,11},{10,... | collective-permute-start | bytes 61448 | tf_op jit(solution)/shard_map/ppermute | solution.py:609
  85.1 4.6 %collective-permute-start.19 = (f32[2048]{0:T(1024)S(1)}, f32[2048]{0:T(1024)S(1)}, u32[]{:S(2)}, u32[]{:S(2)}) collective-permute-start(f32[2048]{0:T(1024)S(1)} %bitcast.57), channel_id=1, source_target_pairs={{0,17},{1,16},{2,19},{3,18},{4,21},{5,20},{6,23},{7,22},{8,25},{9,... | collective-permute-start | bytes 24584 | tf_op jit(solution)/shard_map/ppermute | solution.py:609
  86.1 3.7 %collective-permute-start.18 = (f32[2048]{0:T(1024)S(1)}, f32[2048]{0:T(1024)S(1)}, u32[]{:S(2)}, u32[]{:S(2)}) collective-permute-start(f32[2048]{0:T(1024)S(1)} %bitcast.58), channel_id=1, source_target_pairs={{0,16},{1,17},{2,18},{3,19},{4,20},{5,21},{6,22},{7,23},{8,24},{9,... | collective-permute-start | bytes 24584 | tf_op jit(solution)/shard_map/ppermute | solution.py:609
  86.8 3.7 %collective-permute-start.17 = (f32[2048]{0:T(1024)S(1)}, f32[2048]{0:T(1024)S(1)}, u32[]{:S(2)}, u32[]{:S(2)}) collective-permute-start(f32[2048]{0:T(1024)S(1)} %bitcast.59), channel_id=1, source_target_pairs={{0,1},{1,0},{2,3},{3,2},{4,5},{5,4},{6,7},{7,6},{8,9},{9,8},{10,11... | collective-permute-start | bytes 24584 | tf_op jit(solution)/shard_map/ppermute | solution.py:609
  93.3 1.2 collective-permute-start.20
  94.5 5.6 %collective-permute-start.23 = (f32[4096]{0:T(1024)S(1)}, f32[4096]{0:T(1024)S(1)}, u32[]{:S(2)}, u32[]{:S(2)}) collective-permute-start(f32[4096]{0:T(1024)S(1)} %bitcast.36), channel_id=1, source_target_pairs={{0,6},{1,7},{2,4},{3,5},{4,2},{5,3},{6,0},{7,1},{8,14},{9,15},{10,... | collective-permute-start | bytes 49160 | tf_op jit(solution)/shard_map/ppermute | solution.py:609
  97.2 4.6 %collective-permute-start.22 = (f32[4096]{0:T(1024)S(1)}, f32[4096]{0:T(1024)S(1)}, u32[]{:S(2)}, u32[]{:S(2)}) collective-permute-start(f32[4096]{0:T(1024)S(1)} %bitcast.37), channel_id=1, source_target_pairs={{0,4},{1,5},{2,6},{3,7},{4,0},{5,1},{6,2},{7,3},{8,12},{9,13},{10,... | collective-permute-start | bytes 49160 | tf_op jit(solution)/shard_map/ppermute | solution.py:609
  97.9 3.9 %collective-permute-start.21 = (f32[4096]{0:T(1024)S(1)}, f32[4096]{0:T(1024)S(1)}, u32[]{:S(2)}, u32[]{:S(2)}) collective-permute-start(f32[4096]{0:T(1024)S(1)} %bitcast.38), channel_id=1, source_target_pairs={{0,2},{1,3},{2,0},{3,1},{4,6},{5,7},{6,4},{7,5},{8,10},{9,11},{10,... | collective-permute-start | bytes 49160 | tf_op jit(solution)/shard_map/ppermute | solution.py:609
  105.4 4.6 %collective-permute-start.26 = (f32[2048]{0:T(1024)S(1)}, f32[2048]{0:T(1024)S(1)}, u32[]{:S(2)}, u32[]{:S(2)}) collective-permute-start(f32[2048]{0:T(1024)S(1)} %bitcast.39), channel_id=1, source_target_pairs={{0,17},{1,16},{2,19},{3,18},{4,21},{5,20},{6,23},{7,22},{8,25},{9,... | collective-permute-start | bytes 24584 | tf_op jit(solution)/shard_map/ppermute | solution.py:609
  107.1 3.7 %collective-permute-start.25 = (f32[2048]{0:T(1024)S(1)}, f32[2048]{0:T(1024)S(1)}, u32[]{:S(2)}, u32[]{:S(2)}) collective-permute-start(f32[2048]{0:T(1024)S(1)} %bitcast.40), channel_id=1, source_target_pairs={{0,16},{1,17},{2,18},{3,19},{4,20},{5,21},{6,22},{7,23},{8,24},{9,... | collective-permute-start | bytes 24584 | tf_op jit(solution)/shard_map/ppermute | solution.py:609
  109.0 3.7 %collective-permute-start.24 = (f32[2048]{0:T(1024)S(1)}, f32[2048]{0:T(1024)S(1)}, u32[]{:S(2)}, u32[]{:S(2)}) collective-permute-start(f32[2048]{0:T(1024)S(1)} %bitcast.41), channel_id=1, source_target_pairs={{0,1},{1,0},{2,3},{3,2},{4,5},{5,4},{6,7},{7,6},{8,9},{9,8},{10,11... | collective-permute-start | bytes 24584 | tf_op jit(solution)/shard_map/ppermute | solution.py:609
  115.0 1.2 collective-permute-start.27
  119.5 7.7 %collective-permute-start.28 = (bf16[1024,128]{1,0:T(8,128)(2,1)S(1)}, bf16[1024,128]{1,0:T(8,128)(2,1)S(1)}, u32[]{:S(2)}, u32[]{:S(2)}) collective-permute-start(bf16[1024,128]{1,0:T(8,128)(2,1)S(1)} %get-tuple-element.74), channel_id=1, source_target_pairs={{0,8},{1,9},{2,10},{3,11},{4,12},{5,13},{6,14},{7,15},{8,0},{9,1},... | collective-permute-start | bytes 786440 | tf_op jit(solution)/shard_map/ppermute | solution.py:609
  119.7 8.7 %collective-permute-start.31 = (f32[4096]{0:T(1024)S(1)}, f32[4096]{0:T(1024)S(1)}, u32[]{:S(2)}, u32[]{:S(2)}) collective-permute-start(f32[4096]{0:T(1024)S(1)} %bitcast.47), channel_id=1, source_target_pairs={{0,6},{1,7},{2,4},{3,5},{4,2},{5,3},{6,0},{7,1},{8,14},{9,15},{10,... | collective-permute-start | bytes 49160 | tf_op jit(solution)/shard_map/ppermute | solution.py:609
  121.2 8.5 %collective-permute-start.30 = (f32[4096]{0:T(1024)S(1)}, f32[4096]{0:T(1024)S(1)}, u32[]{:S(2)}, u32[]{:S(2)}) collective-permute-start(f32[4096]{0:T(1024)S(1)} %bitcast.48), channel_id=1, source_target_pairs={{0,4},{1,5},{2,6},{3,7},{4,0},{5,1},{6,2},{7,3},{8,12},{9,13},{10,... | collective-permute-start | bytes 49160 | tf_op jit(solution)/shard_map/ppermute | solution.py:609
  121.8 7.8 %collective-permute-start.29 = (f32[4096]{0:T(1024)S(1)}, f32[4096]{0:T(1024)S(1)}, u32[]{:S(2)}, u32[]{:S(2)}) collective-permute-start(f32[4096]{0:T(1024)S(1)} %bitcast.49), channel_id=1, source_target_pairs={{0,2},{1,3},{2,0},{3,1},{4,6},{5,7},{6,4},{7,5},{8,10},{9,11},{10,... | collective-permute-start | bytes 49160 | tf_op jit(solution)/shard_map/ppermute | solution.py:609
  127.0 4.6 %collective-permute-start.33 = (bf16[1024,128]{1,0:T(8,128)(2,1)S(1)}, bf16[1024,128]{1,0:T(8,128)(2,1)S(1)}, u32[]{:S(2)}, u32[]{:S(2)}) collective-permute-start(bf16[1024,128]{1,0:T(8,128)(2,1)S(1)} %get-tuple-element.83), channel_id=1, source_target_pairs={{0,8},{1,9},{2,10},{3,11},{4,12},{5,13},{6,14},{7,15},{8,0},{9,1},... | collective-permute-start | bytes 786440 | tf_op jit(solution)/shard_map/ppermute | solution.py:609
  127.2 13.5 %collective-permute-start.37 = (bf16[512,128]{1,0:T(8,128)(2,1)S(1)}, bf16[512,128]{1,0:T(8,128)(2,1)S(1)}, u32[]{:S(2)}, u32[]{:S(2)}) collective-permute-start(bf16[512,128]{1,0:T(8,128)(2,1)S(1)} %get-tuple-element.94), channel_id=1, source_target_pairs={{0,4},{1,5},{2,6},{3,7},{4,0},{5,1},{6,2},{7,3},{8,12},{9,13},{10,... | collective-permute-start | bytes 393224 | tf_op jit(solution)/shard_map/ppermute | solution.py:609
  128.4 12.3 %collective-permute-start.38 = (bf16[512,128]{1,0:T(8,128)(2,1)S(1)}, bf16[512,128]{1,0:T(8,128)(2,1)S(1)}, u32[]{:S(2)}, u32[]{:S(2)}) collective-permute-start(bf16[512,128]{1,0:T(8,128)(2,1)S(1)} %get-tuple-element.95), channel_id=1, source_target_pairs={{0,6},{1,7},{2,4},{3,5},{4,2},{5,3},{6,0},{7,1},{8,14},{9,15},{10,... | collective-permute-start | bytes 393224 | tf_op jit(solution)/shard_map/ppermute | solution.py:609
  131.8 10.2 %collective-permute-start.36 = (bf16[512,128]{1,0:T(8,128)(2,1)S(1)}, bf16[512,128]{1,0:T(8,128)(2,1)S(1)}, u32[]{:S(2)}, u32[]{:S(2)}) collective-permute-start(bf16[512,128]{1,0:T(8,128)(2,1)S(1)} %get-tuple-element.93), channel_id=1, source_target_pairs={{0,2},{1,3},{2,0},{3,1},{4,6},{5,7},{6,4},{7,5},{8,10},{9,11},{10,... | collective-permute-start | bytes 393224 | tf_op jit(solution)/shard_map/ppermute | solution.py:609
  132.9 6.0 %collective-permute-start.32 = (bf16[512,128]{1,0:T(8,128)(2,1)S(1)}, bf16[512,128]{1,0:T(8,128)(2,1)S(1)}, u32[]{:S(2)}, u32[]{:S(2)}) collective-permute-start(bf16[512,128]{1,0:T(8,128)(2,1)S(1)} %get-tuple-element.80), channel_id=1, source_target_pairs={{0,17},{1,16},{2,19},{3,18},{4,21},{5,20},{6,23},{7,22},{8,25},{9,... | collective-permute-start | bytes 393224 | tf_op jit(solution)/shard_map/ppermute | solution.py:609
  135.7 6.2 %collective-permute-start.34 = (bf16[512,128]{1,0:T(8,128)(2,1)S(1)}, bf16[512,128]{1,0:T(8,128)(2,1)S(1)}, u32[]{:S(2)}, u32[]{:S(2)}) collective-permute-start(bf16[512,128]{1,0:T(8,128)(2,1)S(1)} %get-tuple-element.89), channel_id=1, source_target_pairs={{0,1},{1,0},{2,3},{3,2},{4,5},{5,4},{6,7},{7,6},{8,9},{9,8},{10,11... | collective-permute-start | bytes 393224 | tf_op jit(solution)/shard_map/ppermute | solution.py:609
  139.0 5.0 %collective-permute-start.35 = (bf16[512,128]{1,0:T(8,128)(2,1)S(1)}, bf16[512,128]{1,0:T(8,128)(2,1)S(1)}, u32[]{:S(2)}, u32[]{:S(2)}) collective-permute-start(bf16[512,128]{1,0:T(8,128)(2,1)S(1)} %get-tuple-element.90), channel_id=1, source_target_pairs={{0,16},{1,17},{2,18},{3,19},{4,20},{5,21},{6,22},{7,23},{8,24},{9,... | collective-permute-start | bytes 393224 | tf_op jit(solution)/shard_map/ppermute | solution.py:609

commit v18 on v17

--- a/solution.py
+++ b/solution.py
@@ -181,7 +181,7 @@
     ys, (y_ref, o_ref, sb_ref, d_ref, top_ref, sum_ref) = refs[:ny], refs[ny:]
     share, rows, half = ys[0].shape[0], x_ref.shape[0], (ny + 1) // 2
     join(y_ref, [own_ref.at[own_ref.shape[0] - share:, :], *ys])
-    places = [k * share for k in range(half - 1, 2 * half) if k != half]
+    places = [(half - 1) * share, (2 * half - 1) * share]
     put_norms(places, share, y_ref, sb_ref)
     lse_pass(places, share, width, y_ref, x_ref, sb_ref, d_ref, top_ref, sum_ref)
     o_ref[:, :rows] = lse2([first_ref[...], sum_ref[...]])
@@ -363,7 +363,7 @@
         out_specs=(VMEM,) * 2,
         scratch_shapes=[*lse_scratch(depth, share, width), pltpu.VMEM((1, rows), jnp.float32)],
         compiler_params=pltpu.CompilerParams(vmem_limit_bytes=16 << 20),
-        cost_estimate=pass_cost(depth // 2, rows),
+        cost_estimate=pass_cost(2 * share, rows),
         name="row_lse_late",
     )(own, mass.reshape(1, -1), x, first, *ys)
 
@@ -646,6 +646,7 @@
     far += [swap(part, core) for part in middle]
     first = row_lse_middle(x, middle, first)
     first, last = lax.optimization_barrier((first, near[-1]))
+    first = row_lse_middle(x, far[1:], first)
     far.append(swap(last, core))
     y, sent = row_lse_late(own, x, [*middle, last, *far], first, mass, 2 * share_x)
     got, _ = direct(sent.reshape(-1), across)

time: 145 us -> 148 us (1.021)
  starting transfers between devices: 40 us -> 45.3 us
  waiting for transfers between devices: 23.6 us -> 21.2 us
    pallas_call x1, Pallas kernels: 9.94 us -> 2.46 us  [row_lse_late(): pl.pallas_call(functools.partial(row_lse_late_kernel, width, len(ys)), ou...]
    pallas_call x1 -> x2, Pallas kernels: 6.45 us -> 12.9 us  [row_lse_middle(): pl.pallas_call(functools.partial(row_lse_middle_kernel, width, len(ys)),...]
    ppermute x39, starting transfers between devices: 40 us -> 45.3 us  [swap(): lax.ppermute(value, ('row', 'col'), [(i, i ^ mask) for i in range(self.co...]
    ppermute x39, waiting for transfers between devices: 23.6 us -> 21.2 us  [swap(): lax.ppermute(value, ('row', 'col'), [(i, i ^ mask) for i in range(self.co...]
  transfers between devices with their start and end apart: 39 -> 39, of which waited for: 20 -> 19; matrix products, arithmetic and copies ran while one was open for 1% -> 1% of each run, Pallas kernels for 15% -> 19%
where the time goes in v18:
time: 148 us; the launch traced here: 147 us
  Pallas kernels  77.6 us (52%)
  starting transfers between devices  45.3 us (31%)
  waiting for transfers between devices  21.2 us (14%)
    ppermute x39, starting transfers between devices, swap(): lax.ppermute(value, ('row', 'col'), [(i, i ^ mask) for i in range(self.co...  45.3 us
    pallas_call x1, Pallas kernels, column_lse(): pl.pallas_call(functools.partial(column_lse_kernel, width, chunk, len(got...  30 us
    ppermute x39, waiting for transfers between devices, swap(): lax.ppermute(value, ('row', 'col'), [(i, i ^ mask) for i in range(self.co...  21.2 us
    pallas_call x2, Pallas kernels, row_lse_middle(): pl.pallas_call(functools.partial(row_lse_middle_kernel, width, len(ys)),...  12.9 us
    pallas_call x4, Pallas kernels, weighted(): pl.pallas_call(functools.partial(kernel, width, tuple(shifts), parts), ou...  12.3 us
    pallas_call x1, Pallas kernels, row_lse_early(): pl.pallas_call(functools.partial(row_lse_early_kernel, width, len(xs)), o...  6.45 us
    pallas_call x2, Pallas kernels, column_grad(): pl.pallas_call(functools.partial(kernel, blocks, share), out_shape=out_sh...  6.18 us
    pallas_call x2, Pallas kernels, other_rows(): pl.pallas_call(functools.partial(rows_kernel, parts), out_shape=[shape(sh...  4.01 us
  transfers between devices with their start and end apart: 39, of which 19 were waited for; matrix products, arithmetic and copies ran while one was open for 1% of the time, Pallas kernels for 19%

profile of v18, /device:TPU:0, one launch (start us, length us, event | category | flops | bytes accessed | tf_op | source)
XLA Modules:
  0.0 146.8 jit_solution(4214757831621497307)
XLA Ops:
  0.6 3.0 %collective-permute-start = (bf16[512,128]{1,0:T(8,128)(2,1)}, bf16[512,128]{1,0:T(8,128)(2,1)S(1)}, u32[]{:S(2)}, u32[]{:S(2)}) collective-permute-start(bf16[512,128]{1,0:T(8,128)(2,1)} %param.4), channel_id=1, source_target_pairs={{0,1},{1,0},{2,3},{3,2},{4,5},{5,4},{6,7},{7,6},{8,9},{9,8},{10,11... | collective-permute-start | bytes 393224 | tf_op jit(solution)/shard_map/ppermute | solution.py:609
  3.7 1.4 collective-permute-start.2
  5.2 3.0 %collective-permute-start.4 = (bf16[512,128]{1,0:T(8,128)(2,1)}, bf16[512,128]{1,0:T(8,128)(2,1)S(1)}, u32[]{:S(2)}, u32[]{:S(2)}) collective-permute-start(bf16[512,128]{1,0:T(8,128)(2,1)} %bitcast.77), channel_id=1, source_target_pairs={{0,4},{1,5},{2,6},{3,7},{4,0},{5,1},{6,2},{7,3},{8,12},{9,13},{10,... | collective-permute-start | bytes 393224 | tf_op jit(solution)/shard_map/ppermute | solution.py:609
  10.2 1.6 %collective-permute-start.5 = (bf16[512,128]{1,0:T(8,128)(2,1)}, bf16[512,128]{1,0:T(8,128)(2,1)S(1)}, u32[]{:S(2)}, u32[]{:S(2)}) collective-permute-start(bf16[512,128]{1,0:T(8,128)(2,1)} %bitcast.80), channel_id=1, source_target_pairs={{0,2},{1,3},{2,0},{3,1},{4,6},{5,7},{6,4},{7,5},{8,10},{9,11},{10,... | collective-permute-start | bytes 393224 | tf_op jit(solution)/shard_map/ppermute | solution.py:609
  11.8 6.4 %row_lse_early.1 = (bf16[2048,128]{1,0:T(8,128)(2,1)S(1)}, bf16[128,2048]{1,0:T(8,128)(2,1)S(1)}, f32[1,2048]{1,0:T(1,128)S(1)}) custom-call(bf16[1024,128]{1,0:T(8,128)(2,1)S(1)} %pad_maximum_fusion.own_ref, bf16[512,128]{1,0:T(8,128)(2,1)S(1)} %collective-permute-done.refs_0_, bf16[512,128]{1,0:T(8,128)(2,1)S(1)} %collective-permute-done.1.refs_1_, ...), custom_call_target="tpu_custom_call" | custom-call | flops 536870912 | bytes 786432 | tf_op jit(solution)/shard_map/row_lse_early/pallas_call | solution.py:325
  18.3 1.4 collective-permute-start.6
  20.2 6.4 %row_lse_middle.2.first_ref = f32[1,2048]{1,0:T(1,128)S(1)} custom-call(bf16[2048,128]{1,0:T(8,128)(2,1)S(1)} %get-tuple-element.52.x_ref, f32[1,2048]{1,0:T(1,128)S(1)} %get-tuple-element.55.first_ref, bf16[512,128]{1,0:T(8,128)(2,1)S(1)} %collective-permute-done.5.refs_0_, bf16[512,128]{1,0:T(8,128)(2,1)S(1)} %collective-permute-done.4.refs_1_), custom_call_target="tpu_custom_call" | custom-call | flops 536870912 | bytes 786432 | tf_op jit(solution)/shard_map/row_lse_middle/pallas_call | solution.py:340
  26.8 6.4 %row_lse_middle.3.first_ref = f32[1,2048]{1,0:T(1,128)S(1)} custom-call(bf16[2048,128]{1,0:T(8,128)(2,1)S(1)} %get-tuple-element.52.x_ref, f32[1,2048]{1,0:T(1,128)S(1)} %row_lse_middle.2.first_ref, bf16[512,128]{1,0:T(8,128)(2,1)S(1)} %collective-permute-done.7.refs_0_.refs_4_, bf16[512,128]{1,0:T(8,128)(2,1)S(1)} %collective-permute-done.8.refs_1_.refs_5_), custom_call_target="tpu_custom_call" | custom-call | flops 536870912 | bytes 786432 | tf_op jit(solution)/shard_map/row_lse_middle/pallas_call | solution.py:340
  33.3 2.5 %row_lse_late.1 = (bf16[4096,128]{1,0:T(8,128)(2,1)S(1)}, f32[1,3072]{1,0:T(1,128)S(1)}) custom-call(bf16[1024,128]{1,0:T(8,128)(2,1)S(1)} %pad_maximum_fusion.own_ref, f32[1,2048]{1,0:T(1,128)S(1)} %bitcast.66, bf16[2048,128]{1,0:T(8,128)(2,1)S(1)} %get-tuple-element.52.x_ref, f32[1,2048]{1,0:T(1,128)S(1)} %row_lse_middle.3.first_ref, ...), custom_call_target="tpu_custom_call" | custom-call | flops 536870912 | bytes 786432 | tf_op jit(solution)/shard_map/row_lse_late/pallas_call | solution.py:359
  36.4 2.9 %collective-permute-start.10 = (f32[3072]{0:T(1024)S(1)}, f32[3072]{0:T(1024)S(1)}, u32[]{:S(2)}, u32[]{:S(2)}) collective-permute-start(f32[3072]{0:T(1024)S(1)} %bitcast.73), channel_id=1, source_target_pairs={{0,1},{1,0},{2,3},{3,2},{4,5},{5,4},{6,7},{7,6},{8,9},{9,8},{10,11... | collective-permute-start | bytes 36872 | tf_op jit(solution)/shard_map/ppermute | solution.py:609
  39.3 1.1 collective-permute-done.12
  41.0 30.0 %column_lse.1 = (f32[1,5120]{1,0:T(1,128)S(1)}, bf16[2048,4096]{1,0:T(8,128)(2,1)S(1)}, f32[1,4096]{1,0:T(1,128)S(1)}, f32[1,2048]{1,0:T(1,128)S(1)}) custom-call(bf16[2048,128]{1,0:T(8,128)(2,1)S(1)} %get-tuple-element.52.x_ref, bf16[4096,128]{1,0:T(8,128)(2,1)S(1)} %get-tuple-element.59.y_ref, f32[1,2048]{1,0:T(1,128)S(1)} %bitcast.67, ...), custom_call_target="tpu_custom_call" | custom-call | flops 2147483648 | bytes 1572864 | tf_op jit(solution)/shard_map/column_lse/pallas_call | solution.py:373
  71.0 3.2 %collective-permute-start.13 = (f32[5120]{0:T(1024)S(1)}, f32[5120]{0:T(1024)S(1)}, u32[]{:S(2)}, u32[]{:S(2)}) collective-permute-start(f32[5120]{0:T(1024)S(1)} %bitcast.45), channel_id=1, source_target_pairs={{0,8},{1,9},{2,10},{3,11},{4,12},{5,13},{6,14},{7,15},{8,0},{9,1},... | collective-permute-start | bytes 61448 | tf_op jit(solution)/shard_map/ppermute | solution.py:609
  75.1 3.1 %collective-permute-start.16 = (f32[5120]{0:T(1024)S(1)}, f32[5120]{0:T(1024)S(1)}, u32[]{:S(2)}, u32[]{:S(2)}) collective-permute-start(f32[5120]{0:T(1024)S(1)} %bitcast.33), channel_id=1, source_target_pairs={{0,6},{1,7},{2,4},{3,5},{4,2},{5,3},{6,0},{7,1},{8,14},{9,15},{10,... | collective-permute-start | bytes 61448 | tf_op jit(solution)/shard_map/ppermute | solution.py:609
  78.2 1.4 collective-permute-start.15
  80.9 2.0 %collective-permute-done.15 = f32[5120]{0:T(1024)S(1)} collective-permute-done((f32[5120]{0:T(1024)S(1)}, f32[5120]{0:T(1024)S(1)}, u32[]{:S(2)}, u32[]{:S(2)}) %collective-permute-start.15) | collective-permute-done | bytes 20512 | tf_op jit(solution)/shard_map/ppermute | solution.py:609
  83.3 3.6 %weighted_sum.4 = (f32[1,2048]{1,0:T(1,128)S(1)}, f32[1,4096]{1,0:T(1,128)S(1)}, f32[1,4096]{1,0:T(1,128)S(1)}) custom-call(bf16[2048,4096]{1,0:T(8,128)(2,1)S(1)} %get-tuple-element.61.e_ref, f32[1,4096]{1,0:T(1,128)S(1)} %get-tuple-element.64.shift_ref, f32[1,5120]{1,0:T(1,128)S(1)} %pair.3.refs_0_, f32[1,5120]{1,0:T(1,128)S(1)} %bitcast.44, ...), custom_call_target="tpu_custom_call" | custom-call | flops 16777216 | bytes 16777216 | tf_op jit(solution)/shard_map/weighted_sum/pallas_call | solution.py:294
  86.9 1.2 collective-permute-start.19
  88.7 1.8 %collective-permute-start.17 = (f32[2048]{0:T(1024)S(1)}, f32[2048]{0:T(1024)S(1)}, u32[]{:S(2)}, u32[]{:S(2)}) collective-permute-start(f32[2048]{0:T(1024)S(1)} %bitcast.59), channel_id=1, source_target_pairs={{0,1},{1,0},{2,3},{3,2},{4,5},{5,4},{6,7},{7,6},{8,9},{9,8},{10,11... | collective-permute-start | bytes 24584 | tf_op jit(solution)/shard_map/ppermute | solution.py:609
  90.5 1.1 collective-permute-done.19
  92.3 2.8 %weighted_sum.5 = (f32[1,4096]{1,0:T(1,128)S(1)}, f32[1,2048]{1,0:T(1,128)}) custom-call(bf16[2048,4096]{1,0:T(8,128)(2,1)S(1)} %get-tuple-element.61.e_ref, f32[1,2048]{1,0:T(1,128)S(1)} %get-tuple-element.63.a_ref, f32[1,4096]{1,0:T(1,128)S(1)} %get-tuple-element.66.first_ref, f32[1,2048]{1,0:T(1,128)S(1)} %get-tuple-element.68.refs_0_, ...), custom_call_target="tpu_custom_call" | custom-call | flops 16777216 | bytes 16777216 | tf_op jit(solution)/shard_map/weighted_sum/pallas_call | solution.py:294
  95.1 1.2 collective-permute-done.20
  96.3 2.7 %collective-permute-start.23 = (f32[4096]{0:T(1024)S(1)}, f32[4096]{0:T(1024)S(1)}, u32[]{:S(2)}, u32[]{:S(2)}) collective-permute-start(f32[4096]{0:T(1024)S(1)} %bitcast.36), channel_id=1, source_target_pairs={{0,6},{1,7},{2,4},{3,5},{4,2},{5,3},{6,0},{7,1},{8,14},{9,15},{10,... | collective-permute-start | bytes 49160 | tf_op jit(solution)/shard_map/ppermute | solution.py:609
  99.4 1.4 collective-permute-start.21
  100.8 1.3 collective-permute-done.23
  102.1 1.6 %collective-permute-done.22 = f32[4096]{0:T(1024)S(1)} collective-permute-done((f32[4096]{0:T(1024)S(1)}, f32[4096]{0:T(1024)S(1)}, u32[]{:S(2)}, u32[]{:S(2)}) %collective-permute-start.22) | collective-permute-done | bytes 16416 | tf_op jit(solution)/shard_map/ppermute | solution.py:609
  103.6 3.6 %weighted_sum.6.refs_0_ = f32[1,2048]{1,0:T(1,128)S(1)} custom-call(bf16[2048,4096]{1,0:T(8,128)(2,1)S(1)} %get-tuple-element.61.e_ref, f32[1,4096]{1,0:T(1,128)S(1)} %get-tuple-element.66.first_ref, f32[1,4096]{1,0:T(1,128)S(1)} %get-tuple-element.67.b_ref, f32[1,4096]{1,0:T(1,128)S(1)} %pair.4.refs_0_, f32[1,4096]{1,0:T(1,128)S(1)} %bitcast.56, ...), custom_call_target="tpu_custom_call" | custom-call | flops 16777216 | bytes 16777216 | tf_op jit(solution)/shard_map/weighted_sum/pallas_call | solution.py:294
  107.2 1.9 %collective-permute-start.26 = (f32[2048]{0:T(1024)S(1)}, f32[2048]{0:T(1024)S(1)}, u32[]{:S(2)}, u32[]{:S(2)}) collective-permute-start(f32[2048]{0:T(1024)S(1)} %bitcast.39), channel_id=1, source_target_pairs={{0,17},{1,16},{2,19},{3,18},{4,21},{5,20},{6,23},{7,22},{8,25},{9,... | collective-permute-start | bytes 24584 | tf_op jit(solution)/shard_map/ppermute | solution.py:609
  109.1 1.7 %collective-permute-start.25 = (f32[2048]{0:T(1024)S(1)}, f32[2048]{0:T(1024)S(1)}, u32[]{:S(2)}, u32[]{:S(2)}) collective-permute-start(f32[2048]{0:T(1024)S(1)} %bitcast.40), channel_id=1, source_target_pairs={{0,16},{1,17},{2,18},{3,19},{4,20},{5,21},{6,22},{7,23},{8,24},{9,... | collective-permute-start | bytes 24584 | tf_op jit(solution)/shard_map/ppermute | solution.py:609
  110.8 1.1 collective-permute-done.26
  112.8 1.7 %collective-permute-done.24 = f32[2048]{0:T(1024)S(1)} collective-permute-done((f32[2048]{0:T(1024)S(1)}, f32[2048]{0:T(1024)S(1)}, u32[]{:S(2)}, u32[]{:S(2)}) %collective-permute-start.24) | collective-permute-done | bytes 8224 | tf_op jit(solution)/shard_map/ppermute | solution.py:609
  114.4 2.3 %weighted_sum.7 = (f32[1,4096]{1,0:T(1,128)S(1)}, f32[1,2048]{1,0:T(1,128)S(1)}) custom-call(bf16[2048,4096]{1,0:T(8,128)(2,1)S(1)} %get-tuple-element.61.e_ref, f32[1,2048]{1,0:T(1,128)S(1)} %get-tuple-element.63.a_ref, f32[1,4096]{1,0:T(1,128)S(1)} %get-tuple-element.66.first_ref, f32[1,2048]{1,0:T(1,128)S(1)} %weighted_sum.6.refs_0_, ...), custom_call_target="tpu_custom_call" | custom-call | flops 16777216 | bytes 16777216 | tf_op jit(solution)/shard_map/weighted_sum/pallas_call | solution.py:294
  116.9 1.2 collective-permute-done.27
  118.0 3.2 %column_grad.2 = (f32[1024,128]{1,0:T(8,128)S(1)}, bf16[1024,128]{1,0:T(8,128)(2,1)S(1)}, bf16[256,2048]{1,0:T(8,128)(2,1)S(1)}) custom-call(bf16[128,2048]{1,0:T(8,128)(2,1)S(1)} %get-tuple-element.62.xt_ref, bf16[4096,128]{1,0:T(8,128)(2,1)S(1)} %get-tuple-element.59.y_ref, bf16[2048,4096]{1,0:T(8,128)(2,1)S(1)} %get-tuple-element.61.e_ref, ...), custom_call_target="tpu_custom_call" | custom-call | flops 2147483648 | bytes 8388608 | tf_op jit(solution)/shard_map/column_grad/pallas_call | solution.py:455
  121.5 1.5 collective-permute-start.31
  123.6 2.3 %collective-permute-start.29 = (f32[4096]{0:T(1024)S(1)}, f32[4096]{0:T(1024)S(1)}, u32[]{:S(2)}, u32[]{:S(2)}) collective-permute-start(f32[4096]{0:T(1024)S(1)} %bitcast.49), channel_id=1, source_target_pairs={{0,2},{1,3},{2,0},{3,1},{4,6},{5,7},{6,4},{7,5},{8,10},{9,11},{10,... | collective-permute-start | bytes 49160 | tf_op jit(solution)/shard_map/ppermute | solution.py:609
  125.9 3.0 %column_grad.3 = (f32[1024,128]{1,0:T(8,128)S(1)}, bf16[1024,128]{1,0:T(8,128)(2,1)S(1)}) custom-call(bf16[256,2048]{1,0:T(8,128)(2,1)S(1)} %get-tuple-element.81.xa_ref, bf16[4096,128]{1,0:T(8,128)(2,1)S(1)} %get-tuple-element.59.y_ref, bf16[2048,4096]{1,0:T(8,128)(2,1)S(1)} %get-tuple-element.61.e_ref, f32[1,4096]{1,0:T(1,128)S(1)} %get-tuple-element.66.first_ref), custom_call_target="tpu_custom_call" | custom-call | flops 2147483648 | bytes 8388608 | tf_op jit(solution)/shard_map/column_grad/pallas_call | solution.py:455
  129.0 1.2 collective-permute-start.37
  130.2 1.2 collective-permute-start.38
  131.4 2.1 %first_rows.1 = (bf16[4096,256]{1,0:T(8,128)(2,1)S(1)}, f32[1,512]{1,0:T(1,128)S(1)}, bf16[512,128]{1,0:T(8,128)(2,1)S(1)}) custom-call(bf16[2048,128]{1,0:T(8,128)(2,1)S(1)} %get-tuple-element.52.x_ref, bf16[4096,128]{1,0:T(8,128)(2,1)S(1)} %get-tuple-element.59.y_ref, bf16[2048,4096]{1,0:T(8,128)(2,1)S(1)} %get-tuple-element.61.e_ref, ...), custom_call_target="tpu_custom_call" | custom-call | flops 34359738368 | bytes 134217728 | tf_op jit(solution)/shard_map/first_rows/pallas_call | solution.py:529
  133.6 1.2 collective-permute-start.36
  134.8 2.6 %other_rows.3 = (bf16[512,128]{1,0:T(8,128)(2,1)S(1)}, bf16[512,128]{1,0:T(8,128)(2,1)S(1)}) custom-call(bf16[2048,128]{1,0:T(8,128)(2,1)S(1)} %get-tuple-element.52.x_ref, bf16[4096,256]{1,0:T(8,128)(2,1)S(1)} %get-tuple-element.88.yb_ref, bf16[2048,4096]{1,0:T(8,128)(2,1)S(1)} %get-tuple-element.61.e_ref, f32[1,2048]{1,0:T(1,128)S(1)} %get-tuple-element.77.alpha_ref), custom_call_target="tpu_custom_call" | custom-call | flops 2147483648 | bytes 8388608 | tf_op jit(solution)/shard_map/other_rows/pallas_call | solution.py:547
  137.5 1.8 %collective-permute-start.34 = (bf16[512,128]{1,0:T(8,128)(2,1)S(1)}, bf16[512,128]{1,0:T(8,128)(2,1)S(1)}, u32[]{:S(2)}, u32[]{:S(2)}) collective-permute-start(bf16[512,128]{1,0:T(8,128)(2,1)S(1)} %get-tuple-element.89), channel_id=1, source_target_pairs={{0,1},{1,0},{2,3},{3,2},{4,5},{5,4},{6,7},{7,6},{8,9},{9,8},{10,11... | collective-permute-start | bytes 393224 | tf_op jit(solution)/shard_map/ppermute | solution.py:609
  139.2 1.6 %collective-permute-done.32.refs_3_ = bf16[512,128]{1,0:T(8,128)(2,1)S(1)} collective-permute-done((bf16[512,128]{1,0:T(8,128)(2,1)S(1)}, bf16[512,128]{1,0:T(8,128)(2,1)S(1)}, u32[]{:S(2)}, u32[]{:S(2)}) %collective-permute-start.32) | collective-permute-done | bytes 131104 | tf_op jit(solution)/shard_map/ppermute | solution.py:609
  141.2 1.4 other_rows.2.refs_0_
  142.7 1.1 collective-permute-done.36.refs_5_
  143.7 2.0 %collective-permute-done.35.refs_2_ = bf16[512,128]{1,0:T(8,128)(2,1)S(1)} collective-permute-done((bf16[512,128]{1,0:T(8,128)(2,1)S(1)}, bf16[512,128]{1,0:T(8,128)(2,1)S(1)}, u32[]{:S(2)}, u32[]{:S(2)}) %collective-permute-start.35) | collective-permute-done | bytes 131104 | tf_op jit(solution)/shard_map/ppermute | solution.py:609
  145.8 1.1 add_up.1
  (53 shorter events, 10.8 us)
Async XLA Ops:
  0.6 9.5 %collective-permute-start = (bf16[512,128]{1,0:T(8,128)(2,1)}, bf16[512,128]{1,0:T(8,128)(2,1)S(1)}, u32[]{:S(2)}, u32[]{:S(2)}) collective-permute-start(bf16[512,128]{1,0:T(8,128)(2,1)} %param.4), channel_id=1, source_target_pairs={{0,1},{1,0},{2,3},{3,2},{4,5},{5,4},{6,7},{7,6},{8,9},{9,8},{10,11... | collective-permute-start | bytes 393224 | tf_op jit(solution)/shard_map/ppermute | solution.py:609
  3.7 8.2 %collective-permute-start.2 = (bf16[512,128]{1,0:T(8,128)(2,1)}, bf16[512,128]{1,0:T(8,128)(2,1)S(1)}, u32[]{:S(2)}, u32[]{:S(2)}) collective-permute-start(bf16[512,128]{1,0:T(8,128)(2,1)} %param.4), channel_id=1, source_target_pairs={{0,17},{1,16},{2,19},{3,18},{4,21},{5,20},{6,23},{7,22},{8,25},{9,... | collective-permute-start | bytes 393224 | tf_op jit(solution)/shard_map/ppermute | solution.py:609
  5.1 6.7 %collective-permute-start.1 = (bf16[512,128]{1,0:T(8,128)(2,1)}, bf16[512,128]{1,0:T(8,128)(2,1)S(1)}, u32[]{:S(2)}, u32[]{:S(2)}) collective-permute-start(bf16[512,128]{1,0:T(8,128)(2,1)} %param.4), channel_id=1, source_target_pairs={{0,16},{1,17},{2,18},{3,19},{4,20},{5,21},{6,22},{7,23},{8,24},{9,... | collective-permute-start | bytes 393224 | tf_op jit(solution)/shard_map/ppermute | solution.py:609
  5.2 13.1 %collective-permute-start.4 = (bf16[512,128]{1,0:T(8,128)(2,1)}, bf16[512,128]{1,0:T(8,128)(2,1)S(1)}, u32[]{:S(2)}, u32[]{:S(2)}) collective-permute-start(bf16[512,128]{1,0:T(8,128)(2,1)} %bitcast.77), channel_id=1, source_target_pairs={{0,4},{1,5},{2,6},{3,7},{4,0},{5,1},{6,2},{7,3},{8,12},{9,13},{10,... | collective-permute-start | bytes 393224 | tf_op jit(solution)/shard_map/ppermute | solution.py:609
  9.2 2.6 %collective-permute-start.3 = (bf16[512,128]{1,0:T(8,128)(2,1)}, bf16[512,128]{1,0:T(8,128)(2,1)S(1)}, u32[]{:S(2)}, u32[]{:S(2)}) collective-permute-start(bf16[512,128]{1,0:T(8,128)(2,1)} %bitcast.79), channel_id=1, source_target_pairs={{0,8},{1,9},{2,10},{3,11},{4,12},{5,13},{6,14},{7,15},{8,0},{9,1},... | collective-permute-start | bytes 393224 | tf_op jit(solution)/shard_map/ppermute | solution.py:609
  10.2 9.6 %collective-permute-start.5 = (bf16[512,128]{1,0:T(8,128)(2,1)}, bf16[512,128]{1,0:T(8,128)(2,1)S(1)}, u32[]{:S(2)}, u32[]{:S(2)}) collective-permute-start(bf16[512,128]{1,0:T(8,128)(2,1)} %bitcast.80), channel_id=1, source_target_pairs={{0,2},{1,3},{2,0},{3,1},{4,6},{5,7},{6,4},{7,5},{8,10},{9,11},{10,... | collective-permute-start | bytes 393224 | tf_op jit(solution)/shard_map/ppermute | solution.py:609
  18.3 8.4 %collective-permute-start.6 = (bf16[512,128]{1,0:T(8,128)(2,1)S(1)}, bf16[512,128]{1,0:T(8,128)(2,1)S(1)}, u32[]{:S(2)}, u32[]{:S(2)}) collective-permute-start(bf16[512,128]{1,0:T(8,128)(2,1)S(1)} %collective-permute-done.4.refs_1_), channel_id=1, source_target_pairs={{0,2},{1,3},{2,0},{3,1},{4,6},{5,7},{6,4},{7,5},{8,10},{9,11},{10,... | collective-permute-start | bytes 393224 | tf_op jit(solution)/shard_map/ppermute | solution.py:609
  19.7 7.1 %collective-permute-start.8 = (bf16[512,128]{1,0:T(8,128)(2,1)S(1)}, bf16[512,128]{1,0:T(8,128)(2,1)S(1)}, u32[]{:S(2)}, u32[]{:S(2)}) collective-permute-start(bf16[512,128]{1,0:T(8,128)(2,1)S(1)} %collective-permute-done.4.refs_1_), channel_id=1, source_target_pairs={{0,8},{1,9},{2,10},{3,11},{4,12},{5,13},{6,14},{7,15},{8,0},{9,1},... | collective-permute-start | bytes 393224 | tf_op jit(solution)/shard_map/ppermute | solution.py:609
  19.7 7.0 %collective-permute-start.7 = (bf16[512,128]{1,0:T(8,128)(2,1)S(1)}, bf16[512,128]{1,0:T(8,128)(2,1)S(1)}, u32[]{:S(2)}, u32[]{:S(2)}) collective-permute-start(bf16[512,128]{1,0:T(8,128)(2,1)S(1)} %collective-permute-done.5.refs_0_), channel_id=1, source_target_pairs={{0,8},{1,9},{2,10},{3,11},{4,12},{5,13},{6,14},{7,15},{8,0},{9,1},... | collective-permute-start | bytes 393224 | tf_op jit(solution)/shard_map/ppermute | solution.py:609
  26.7 6.6 %collective-permute-start.9 = (bf16[512,128]{1,0:T(8,128)(2,1)S(1)}, bf16[512,128]{1,0:T(8,128)(2,1)S(1)}, u32[]{:S(2)}, u32[]{:S(2)}) collective-permute-start(bf16[512,128]{1,0:T(8,128)(2,1)S(1)} %collective-permute-done.6.refs_2_), channel_id=1, source_target_pairs={{0,8},{1,9},{2,10},{3,11},{4,12},{5,13},{6,14},{7,15},{8,0},{9,1},... | collective-permute-start | bytes 393224 | tf_op jit(solution)/shard_map/ppermute | solution.py:609
  35.7 4.7 %collective-permute-start.12 = (f32[3072]{0:T(1024)S(1)}, f32[3072]{0:T(1024)S(1)}, u32[]{:S(2)}, u32[]{:S(2)}) collective-permute-start(f32[3072]{0:T(1024)S(1)} %bitcast.71), channel_id=1, source_target_pairs={{0,17},{1,16},{2,19},{3,18},{4,21},{5,20},{6,23},{7,22},{8,25},{9,... | collective-permute-start | bytes 36872 | tf_op jit(solution)/shard_map/ppermute | solution.py:609
  35.8 4.6 %collective-permute-start.11 = (f32[3072]{0:T(1024)S(1)}, f32[3072]{0:T(1024)S(1)}, u32[]{:S(2)}, u32[]{:S(2)}) collective-permute-start(f32[3072]{0:T(1024)S(1)} %bitcast.72), channel_id=1, source_target_pairs={{0,16},{1,17},{2,18},{3,19},{4,20},{5,21},{6,22},{7,23},{8,24},{9,... | collective-permute-start | bytes 36872 | tf_op jit(solution)/shard_map/ppermute | solution.py:609
  36.4 4.5 %collective-permute-start.10 = (f32[3072]{0:T(1024)S(1)}, f32[3072]{0:T(1024)S(1)}, u32[]{:S(2)}, u32[]{:S(2)}) collective-permute-start(f32[3072]{0:T(1024)S(1)} %bitcast.73), channel_id=1, source_target_pairs={{0,1},{1,0},{2,3},{3,2},{4,5},{5,4},{6,7},{7,6},{8,9},{9,8},{10,11... | collective-permute-start | bytes 36872 | tf_op jit(solution)/shard_map/ppermute | solution.py:609
  71.0 4.1 %collective-permute-start.13 = (f32[5120]{0:T(1024)S(1)}, f32[5120]{0:T(1024)S(1)}, u32[]{:S(2)}, u32[]{:S(2)}) collective-permute-start(f32[5120]{0:T(1024)S(1)} %bitcast.45), channel_id=1, source_target_pairs={{0,8},{1,9},{2,10},{3,11},{4,12},{5,13},{6,14},{7,15},{8,0},{9,1},... | collective-permute-start | bytes 61448 | tf_op jit(solution)/shard_map/ppermute | solution.py:609
  75.1 5.8 %collective-permute-start.16 = (f32[5120]{0:T(1024)S(1)}, f32[5120]{0:T(1024)S(1)}, u32[]{:S(2)}, u32[]{:S(2)}) collective-permute-start(f32[5120]{0:T(1024)S(1)} %bitcast.33), channel_id=1, source_target_pairs={{0,6},{1,7},{2,4},{3,5},{4,2},{5,3},{6,0},{7,1},{8,14},{9,15},{10,... | collective-permute-start | bytes 61448 | tf_op jit(solution)/shard_map/ppermute | solution.py:609
  78.2 4.7 %collective-permute-start.15 = (f32[5120]{0:T(1024)S(1)}, f32[5120]{0:T(1024)S(1)}, u32[]{:S(2)}, u32[]{:S(2)}) collective-permute-start(f32[5120]{0:T(1024)S(1)} %bitcast.34), channel_id=1, source_target_pairs={{0,4},{1,5},{2,6},{3,7},{4,0},{5,1},{6,2},{7,3},{8,12},{9,13},{10,... | collective-permute-start | bytes 61448 | tf_op jit(solution)/shard_map/ppermute | solution.py:609
  79.6 3.8 %collective-permute-start.14 = (f32[5120]{0:T(1024)S(1)}, f32[5120]{0:T(1024)S(1)}, u32[]{:S(2)}, u32[]{:S(2)}) collective-permute-start(f32[5120]{0:T(1024)S(1)} %bitcast.35), channel_id=1, source_target_pairs={{0,2},{1,3},{2,0},{3,1},{4,6},{5,7},{6,4},{7,5},{8,10},{9,11},{10,... | collective-permute-start | bytes 61448 | tf_op jit(solution)/shard_map/ppermute | solution.py:609
  86.9 4.6 %collective-permute-start.19 = (f32[2048]{0:T(1024)S(1)}, f32[2048]{0:T(1024)S(1)}, u32[]{:S(2)}, u32[]{:S(2)}) collective-permute-start(f32[2048]{0:T(1024)S(1)} %bitcast.57), channel_id=1, source_target_pairs={{0,17},{1,16},{2,19},{3,18},{4,21},{5,20},{6,23},{7,22},{8,25},{9,... | collective-permute-start | bytes 24584 | tf_op jit(solution)/shard_map/ppermute | solution.py:609
  88.1 3.7 %collective-permute-start.18 = (f32[2048]{0:T(1024)S(1)}, f32[2048]{0:T(1024)S(1)}, u32[]{:S(2)}, u32[]{:S(2)}) collective-permute-start(f32[2048]{0:T(1024)S(1)} %bitcast.58), channel_id=1, source_target_pairs={{0,16},{1,17},{2,18},{3,19},{4,20},{5,21},{6,22},{7,23},{8,24},{9,... | collective-permute-start | bytes 24584 | tf_op jit(solution)/shard_map/ppermute | solution.py:609
  88.7 3.7 %collective-permute-start.17 = (f32[2048]{0:T(1024)S(1)}, f32[2048]{0:T(1024)S(1)}, u32[]{:S(2)}, u32[]{:S(2)}) collective-permute-start(f32[2048]{0:T(1024)S(1)} %bitcast.59), channel_id=1, source_target_pairs={{0,1},{1,0},{2,3},{3,2},{4,5},{5,4},{6,7},{7,6},{8,9},{9,8},{10,11... | collective-permute-start | bytes 24584 | tf_op jit(solution)/shard_map/ppermute | solution.py:609
  95.1 1.2 collective-permute-start.20
  96.3 5.8 %collective-permute-start.23 = (f32[4096]{0:T(1024)S(1)}, f32[4096]{0:T(1024)S(1)}, u32[]{:S(2)}, u32[]{:S(2)}) collective-permute-start(f32[4096]{0:T(1024)S(1)} %bitcast.36), channel_id=1, source_target_pairs={{0,6},{1,7},{2,4},{3,5},{4,2},{5,3},{6,0},{7,1},{8,14},{9,15},{10,... | collective-permute-start | bytes 49160 | tf_op jit(solution)/shard_map/ppermute | solution.py:609
  99.0 4.6 %collective-permute-start.22 = (f32[4096]{0:T(1024)S(1)}, f32[4096]{0:T(1024)S(1)}, u32[]{:S(2)}, u32[]{:S(2)}) collective-permute-start(f32[4096]{0:T(1024)S(1)} %bitcast.37), channel_id=1, source_target_pairs={{0,4},{1,5},{2,6},{3,7},{4,0},{5,1},{6,2},{7,3},{8,12},{9,13},{10,... | collective-permute-start | bytes 49160 | tf_op jit(solution)/shard_map/ppermute | solution.py:609
  99.4 4.3 %collective-permute-start.21 = (f32[4096]{0:T(1024)S(1)}, f32[4096]{0:T(1024)S(1)}, u32[]{:S(2)}, u32[]{:S(2)}) collective-permute-start(f32[4096]{0:T(1024)S(1)} %bitcast.38), channel_id=1, source_target_pairs={{0,2},{1,3},{2,0},{3,1},{4,6},{5,7},{6,4},{7,5},{8,10},{9,11},{10,... | collective-permute-start | bytes 49160 | tf_op jit(solution)/shard_map/ppermute | solution.py:609
  107.2 4.6 %collective-permute-start.26 = (f32[2048]{0:T(1024)S(1)}, f32[2048]{0:T(1024)S(1)}, u32[]{:S(2)}, u32[]{:S(2)}) collective-permute-start(f32[2048]{0:T(1024)S(1)} %bitcast.39), channel_id=1, source_target_pairs={{0,17},{1,16},{2,19},{3,18},{4,21},{5,20},{6,23},{7,22},{8,25},{9,... | collective-permute-start | bytes 24584 | tf_op jit(solution)/shard_map/ppermute | solution.py:609
  109.1 3.7 %collective-permute-start.25 = (f32[2048]{0:T(1024)S(1)}, f32[2048]{0:T(1024)S(1)}, u32[]{:S(2)}, u32[]{:S(2)}) collective-permute-start(f32[2048]{0:T(1024)S(1)} %bitcast.40), channel_id=1, source_target_pairs={{0,16},{1,17},{2,18},{3,19},{4,20},{5,21},{6,22},{7,23},{8,24},{9,... | collective-permute-start | bytes 24584 | tf_op jit(solution)/shard_map/ppermute | solution.py:609
  110.8 3.7 %collective-permute-start.24 = (f32[2048]{0:T(1024)S(1)}, f32[2048]{0:T(1024)S(1)}, u32[]{:S(2)}, u32[]{:S(2)}) collective-permute-start(f32[2048]{0:T(1024)S(1)} %bitcast.41), channel_id=1, source_target_pairs={{0,1},{1,0},{2,3},{3,2},{4,5},{5,4},{6,7},{7,6},{8,9},{9,8},{10,11... | collective-permute-start | bytes 24584 | tf_op jit(solution)/shard_map/ppermute | solution.py:609
  116.8 1.2 collective-permute-start.27
  121.3 7.7 %collective-permute-start.28 = (bf16[1024,128]{1,0:T(8,128)(2,1)S(1)}, bf16[1024,128]{1,0:T(8,128)(2,1)S(1)}, u32[]{:S(2)}, u32[]{:S(2)}) collective-permute-start(bf16[1024,128]{1,0:T(8,128)(2,1)S(1)} %get-tuple-element.74), channel_id=1, source_target_pairs={{0,8},{1,9},{2,10},{3,11},{4,12},{5,13},{6,14},{7,15},{8,0},{9,1},... | collective-permute-start | bytes 786440 | tf_op jit(solution)/shard_map/ppermute | solution.py:609
  121.5 8.7 %collective-permute-start.31 = (f32[4096]{0:T(1024)S(1)}, f32[4096]{0:T(1024)S(1)}, u32[]{:S(2)}, u32[]{:S(2)}) collective-permute-start(f32[4096]{0:T(1024)S(1)} %bitcast.47), channel_id=1, source_target_pairs={{0,6},{1,7},{2,4},{3,5},{4,2},{5,3},{6,0},{7,1},{8,14},{9,15},{10,... | collective-permute-start | bytes 49160 | tf_op jit(solution)/shard_map/ppermute | solution.py:609
  123.0 8.5 %collective-permute-start.30 = (f32[4096]{0:T(1024)S(1)}, f32[4096]{0:T(1024)S(1)}, u32[]{:S(2)}, u32[]{:S(2)}) collective-permute-start(f32[4096]{0:T(1024)S(1)} %bitcast.48), channel_id=1, source_target_pairs={{0,4},{1,5},{2,6},{3,7},{4,0},{5,1},{6,2},{7,3},{8,12},{9,13},{10,... | collective-permute-start | bytes 49160 | tf_op jit(solution)/shard_map/ppermute | solution.py:609
  123.6 7.8 %collective-permute-start.29 = (f32[4096]{0:T(1024)S(1)}, f32[4096]{0:T(1024)S(1)}, u32[]{:S(2)}, u32[]{:S(2)}) collective-permute-start(f32[4096]{0:T(1024)S(1)} %bitcast.49), channel_id=1, source_target_pairs={{0,2},{1,3},{2,0},{3,1},{4,6},{5,7},{6,4},{7,5},{8,10},{9,11},{10,... | collective-permute-start | bytes 49160 | tf_op jit(solution)/shard_map/ppermute | solution.py:609
  128.8 4.6 %collective-permute-start.33 = (bf16[1024,128]{1,0:T(8,128)(2,1)S(1)}, bf16[1024,128]{1,0:T(8,128)(2,1)S(1)}, u32[]{:S(2)}, u32[]{:S(2)}) collective-permute-start(bf16[1024,128]{1,0:T(8,128)(2,1)S(1)} %get-tuple-element.83), channel_id=1, source_target_pairs={{0,8},{1,9},{2,10},{3,11},{4,12},{5,13},{6,14},{7,15},{8,0},{9,1},... | collective-permute-start | bytes 786440 | tf_op jit(solution)/shard_map/ppermute | solution.py:609
  129.0 13.6 %collective-permute-start.37 = (bf16[512,128]{1,0:T(8,128)(2,1)S(1)}, bf16[512,128]{1,0:T(8,128)(2,1)S(1)}, u32[]{:S(2)}, u32[]{:S(2)}) collective-permute-start(bf16[512,128]{1,0:T(8,128)(2,1)S(1)} %get-tuple-element.94), channel_id=1, source_target_pairs={{0,4},{1,5},{2,6},{3,7},{4,0},{5,1},{6,2},{7,3},{8,12},{9,13},{10,... | collective-permute-start | bytes 393224 | tf_op jit(solution)/shard_map/ppermute | solution.py:609
  130.2 12.5 %collective-permute-start.38 = (bf16[512,128]{1,0:T(8,128)(2,1)S(1)}, bf16[512,128]{1,0:T(8,128)(2,1)S(1)}, u32[]{:S(2)}, u32[]{:S(2)}) collective-permute-start(bf16[512,128]{1,0:T(8,128)(2,1)S(1)} %get-tuple-element.95), channel_id=1, source_target_pairs={{0,6},{1,7},{2,4},{3,5},{4,2},{5,3},{6,0},{7,1},{8,14},{9,15},{10,... | collective-permute-start | bytes 393224 | tf_op jit(solution)/shard_map/ppermute | solution.py:609
  133.6 10.2 %collective-permute-start.36 = (bf16[512,128]{1,0:T(8,128)(2,1)S(1)}, bf16[512,128]{1,0:T(8,128)(2,1)S(1)}, u32[]{:S(2)}, u32[]{:S(2)}) collective-permute-start(bf16[512,128]{1,0:T(8,128)(2,1)S(1)} %get-tuple-element.93), channel_id=1, source_target_pairs={{0,2},{1,3},{2,0},{3,1},{4,6},{5,7},{6,4},{7,5},{8,10},{9,11},{10,... | collective-permute-start | bytes 393224 | tf_op jit(solution)/shard_map/ppermute | solution.py:609
  134.7 6.0 %collective-permute-start.32 = (bf16[512,128]{1,0:T(8,128)(2,1)S(1)}, bf16[512,128]{1,0:T(8,128)(2,1)S(1)}, u32[]{:S(2)}, u32[]{:S(2)}) collective-permute-start(bf16[512,128]{1,0:T(8,128)(2,1)S(1)} %get-tuple-element.80), channel_id=1, source_target_pairs={{0,17},{1,16},{2,19},{3,18},{4,21},{5,20},{6,23},{7,22},{8,25},{9,... | collective-permute-start | bytes 393224 | tf_op jit(solution)/shard_map/ppermute | solution.py:609
  137.5 6.3 %collective-permute-start.34 = (bf16[512,128]{1,0:T(8,128)(2,1)S(1)}, bf16[512,128]{1,0:T(8,128)(2,1)S(1)}, u32[]{:S(2)}, u32[]{:S(2)}) collective-permute-start(bf16[512,128]{1,0:T(8,128)(2,1)S(1)} %get-tuple-element.89), channel_id=1, source_target_pairs={{0,1},{1,0},{2,3},{3,2},{4,5},{5,4},{6,7},{7,6},{8,9},{9,8},{10,11... | collective-permute-start | bytes 393224 | tf_op jit(solution)/shard_map/ppermute | solution.py:609
  140.8 5.0 %collective-permute-start.35 = (bf16[512,128]{1,0:T(8,128)(2,1)S(1)}, bf16[512,128]{1,0:T(8,128)(2,1)S(1)}, u32[]{:S(2)}, u32[]{:S(2)}) collective-permute-start(bf16[512,128]{1,0:T(8,128)(2,1)S(1)} %get-tuple-element.90), channel_id=1, source_target_pairs={{0,16},{1,17},{2,18},{3,19},{4,20},{5,21},{6,22},{7,23},{8,24},{9,... | collective-permute-start | bytes 393224 | tf_op jit(solution)/shard_map/ppermute | solution.py:609

commit v19 on v17

--- a/solution.py
+++ b/solution.py
@@ -636,7 +636,7 @@
 
     x, xt, first = row_lse_early(own, xs[1:], far[0])
     relays = [z for z in range(2, nz) if not z & (z - 1)]
-    first, mass, got = lax.optimization_barrier((first, mass, [near[z] for z in relays]))
+    first, got = lax.optimization_barrier((first, [near[z] for z in relays]))
     for z, part in zip(relays, got):
         near[z] = part
     for z in range(1, nz):
@@ -645,7 +645,7 @@
     middle = near[1:-1]
     far += [swap(part, core) for part in middle]
     first = row_lse_middle(x, middle, first)
-    first, last = lax.optimization_barrier((first, near[-1]))
+    first, last, mass = lax.optimization_barrier((first, near[-1], mass))
     far.append(swap(last, core))
     y, sent = row_lse_late(own, x, [*middle, last, *far], first, mass, 2 * share_x)
     got, _ = direct(sent.reshape(-1), across)

time: 145 us -> 146 us (level)
  starting transfers between devices: 40 us -> 44.6 us
  waiting for transfers between devices: 23.6 us -> 20.1 us
    ppermute x39, starting transfers between devices: 40 us -> 44.6 us  [swap(): lax.ppermute(value, ('row', 'col'), [(i, i ^ mask) for i in range(self.co...]
    ppermute x39, waiting for transfers between devices: 23.6 us -> 20.1 us  [swap(): lax.ppermute(value, ('row', 'col'), [(i, i ^ mask) for i in range(self.co...]
  transfers between devices with their start and end apart: 39 -> 39, of which waited for: 20 -> 19; matrix products, arithmetic and copies ran while one was open for 1% -> 1% of each run, Pallas kernels for 15% -> 15%
where the time goes in v19:
time: 146 us
  Pallas kernels  78.7 us (54%)
  starting transfers between devices  44.6 us (31%)
  waiting for transfers between devices  20.1 us (14%)
    ppermute x39, starting transfers between devices, swap(): lax.ppermute(value, ('row', 'col'), [(i, i ^ mask) for i in range(self.co...  44.6 us
    pallas_call x1, Pallas kernels, column_lse(): pl.pallas_call(functools.partial(column_lse_kernel, width, chunk, len(got...  30 us
    ppermute x39, waiting for transfers between devices, swap(): lax.ppermute(value, ('row', 'col'), [(i, i ^ mask) for i in range(self.co...  20.1 us
    pallas_call x4, Pallas kernels, weighted(): pl.pallas_call(functools.partial(kernel, width, tuple(shifts), parts), ou...  12.3 us
    pallas_call x1, Pallas kernels, row_lse_late(): pl.pallas_call(functools.partial(row_lse_late_kernel, width, len(ys)), ou...  9.94 us
    pallas_call x1, Pallas kernels, row_lse_middle(): pl.pallas_call(functools.partial(row_lse_middle_kernel, width, len(ys)),...  6.45 us
    pallas_call x1, Pallas kernels, row_lse_early(): pl.pallas_call(functools.partial(row_lse_early_kernel, width, len(xs)), o...  6.45 us
    pallas_call x2, Pallas kernels, column_grad(): pl.pallas_call(functools.partial(kernel, blocks, share), out_shape=out_sh...  6.18 us
  transfers between devices with their start and end apart: 39, of which 19 were waited for; matrix products, arithmetic and copies ran while one was open for 1% of the time, Pallas kernels for 15%

profile of v19, /device:TPU:0, one launch (start us, length us, event | category | flops | bytes accessed | tf_op | source)
XLA Modules:
  0.0 146.1 jit_solution(13394810029334100637)
XLA Ops:
  0.6 3.0 %collective-permute-start = (bf16[512,128]{1,0:T(8,128)(2,1)}, bf16[512,128]{1,0:T(8,128)(2,1)S(1)}, u32[]{:S(2)}, u32[]{:S(2)}) collective-permute-start(bf16[512,128]{1,0:T(8,128)(2,1)} %param.4), channel_id=1, source_target_pairs={{0,1},{1,0},{2,3},{3,2},{4,5},{5,4},{6,7},{7,6},{8,9},{9,8},{10,11... | collective-permute-start | bytes 393224 | tf_op jit(solution)/shard_map/ppermute | solution.py:609
  3.7 1.4 collective-permute-start.2
  5.2 1.0 pad_maximum_fusion.own_ref
  6.3 3.1 %collective-permute-start.4 = (bf16[512,128]{1,0:T(8,128)(2,1)}, bf16[512,128]{1,0:T(8,128)(2,1)S(1)}, u32[]{:S(2)}, u32[]{:S(2)}) collective-permute-start(bf16[512,128]{1,0:T(8,128)(2,1)} %bitcast.79), channel_id=1, source_target_pairs={{0,4},{1,5},{2,6},{3,7},{4,0},{5,1},{6,2},{7,3},{8,12},{9,13},{10,... | collective-permute-start | bytes 393224 | tf_op jit(solution)/shard_map/ppermute | solution.py:609
  9.4 0.8 fusion
  10.2 1.6 %collective-permute-start.5 = (bf16[512,128]{1,0:T(8,128)(2,1)}, bf16[512,128]{1,0:T(8,128)(2,1)S(1)}, u32[]{:S(2)}, u32[]{:S(2)}) collective-permute-start(bf16[512,128]{1,0:T(8,128)(2,1)} %bitcast.80), channel_id=1, source_target_pairs={{0,2},{1,3},{2,0},{3,1},{4,6},{5,7},{6,4},{7,5},{8,10},{9,11},{10,... | collective-permute-start | bytes 393224 | tf_op jit(solution)/shard_map/ppermute | solution.py:609
  11.8 6.5 %row_lse_early.1 = (bf16[2048,128]{1,0:T(8,128)(2,1)S(1)}, bf16[128,2048]{1,0:T(8,128)(2,1)S(1)}, f32[1,2048]{1,0:T(1,128)S(1)}) custom-call(bf16[1024,128]{1,0:T(8,128)(2,1)S(1)} %pad_maximum_fusion.own_ref, bf16[512,128]{1,0:T(8,128)(2,1)S(1)} %collective-permute-done.refs_0_, bf16[512,128]{1,0:T(8,128)(2,1)S(1)} %collective-permute-done.1.refs_1_, ...), custom_call_target="tpu_custom_call" | custom-call | flops 536870912 | bytes 786432 | tf_op jit(solution)/shard_map/row_lse_early/pallas_call | solution.py:325
  19.0 6.5 %row_lse_middle.1.first_ref = f32[1,2048]{1,0:T(1,128)S(1)} custom-call(bf16[2048,128]{1,0:T(8,128)(2,1)S(1)} %get-tuple-element.52.x_ref, f32[1,2048]{1,0:T(1,128)S(1)} %get-tuple-element.54.first_ref, bf16[512,128]{1,0:T(8,128)(2,1)S(1)} %collective-permute-done.5.refs_0_, bf16[512,128]{1,0:T(8,128)(2,1)S(1)} %collective-permute-done.4.refs_1_), custom_call_target="tpu_custom_call" | custom-call | flops 536870912 | bytes 786432 | tf_op jit(solution)/shard_map/row_lse_middle/pallas_call | solution.py:340
  25.6 1.3 collective-permute-done.9.refs_6_
  26.8 9.9 %row_lse_late.1 = (bf16[4096,128]{1,0:T(8,128)(2,1)S(1)}, f32[1,3072]{1,0:T(1,128)S(1)}) custom-call(bf16[1024,128]{1,0:T(8,128)(2,1)S(1)} %pad_maximum_fusion.own_ref, f32[1,2048]{1,0:T(1,128)S(1)} %bitcast.66, bf16[2048,128]{1,0:T(8,128)(2,1)S(1)} %get-tuple-element.52.x_ref, f32[1,2048]{1,0:T(1,128)S(1)} %row_lse_middle.1.first_ref, ...), custom_call_target="tpu_custom_call" | custom-call | flops 1073741824 | bytes 1048576 | tf_op jit(solution)/shard_map/row_lse_late/pallas_call | solution.py:359
  36.9 1.1 collective-permute-start.11
  38.0 2.4 %collective-permute-start.10 = (f32[3072]{0:T(1024)S(1)}, f32[3072]{0:T(1024)S(1)}, u32[]{:S(2)}, u32[]{:S(2)}) collective-permute-start(f32[3072]{0:T(1024)S(1)} %bitcast.73), channel_id=1, source_target_pairs={{0,1},{1,0},{2,3},{3,2},{4,5},{5,4},{6,7},{7,6},{8,9},{9,8},{10,11... | collective-permute-start | bytes 36872 | tf_op jit(solution)/shard_map/ppermute | solution.py:609
  40.3 1.1 collective-permute-done.12
  42.0 30.0 %column_lse.1 = (f32[1,5120]{1,0:T(1,128)S(1)}, bf16[2048,4096]{1,0:T(8,128)(2,1)S(1)}, f32[1,4096]{1,0:T(1,128)S(1)}, f32[1,2048]{1,0:T(1,128)S(1)}) custom-call(bf16[2048,128]{1,0:T(8,128)(2,1)S(1)} %get-tuple-element.52.x_ref, bf16[4096,128]{1,0:T(8,128)(2,1)S(1)} %get-tuple-element.59.y_ref, f32[1,2048]{1,0:T(1,128)S(1)} %bitcast.67, ...), custom_call_target="tpu_custom_call" | custom-call | flops 2147483648 | bytes 1572864 | tf_op jit(solution)/shard_map/column_lse/pallas_call | solution.py:373
  72.1 1.2 collective-permute-done.13
  73.4 5.7 %collective-permute-start.16 = (f32[5120]{0:T(1024)S(1)}, f32[5120]{0:T(1024)S(1)}, u32[]{:S(2)}, u32[]{:S(2)}) collective-permute-start(f32[5120]{0:T(1024)S(1)} %bitcast.33), channel_id=1, source_target_pairs={{0,6},{1,7},{2,4},{3,5},{4,2},{5,3},{6,0},{7,1},{8,14},{9,15},{10,... | collective-permute-start | bytes 61448 | tf_op jit(solution)/shard_map/ppermute | solution.py:609
  79.7 1.1 collective-permute-done.16
  80.8 2.9 %collective-permute-done.15 = f32[5120]{0:T(1024)S(1)} collective-permute-done((f32[5120]{0:T(1024)S(1)}, f32[5120]{0:T(1024)S(1)}, u32[]{:S(2)}, u32[]{:S(2)}) %collective-permute-start.15) | collective-permute-done | bytes 20512 | tf_op jit(solution)/shard_map/ppermute | solution.py:609
  83.8 3.6 %weighted_sum.4 = (f32[1,2048]{1,0:T(1,128)S(1)}, f32[1,4096]{1,0:T(1,128)S(1)}, f32[1,4096]{1,0:T(1,128)S(1)}) custom-call(bf16[2048,4096]{1,0:T(8,128)(2,1)S(1)} %get-tuple-element.61.e_ref, f32[1,4096]{1,0:T(1,128)S(1)} %get-tuple-element.64.shift_ref, f32[1,5120]{1,0:T(1,128)S(1)} %pair.3.refs_0_, f32[1,5120]{1,0:T(1,128)S(1)} %bitcast.44, ...), custom_call_target="tpu_custom_call" | custom-call | flops 16777216 | bytes 16777216 | tf_op jit(solution)/shard_map/weighted_sum/pallas_call | solution.py:294
  87.3 1.0 collective-permute-start.19
  89.0 1.9 %collective-permute-start.17 = (f32[2048]{0:T(1024)S(1)}, f32[2048]{0:T(1024)S(1)}, u32[]{:S(2)}, u32[]{:S(2)}) collective-permute-start(f32[2048]{0:T(1024)S(1)} %bitcast.59), channel_id=1, source_target_pairs={{0,1},{1,0},{2,3},{3,2},{4,5},{5,4},{6,7},{7,6},{8,9},{9,8},{10,11... | collective-permute-start | bytes 24584 | tf_op jit(solution)/shard_map/ppermute | solution.py:609
  90.9 1.1 collective-permute-done.19
  92.7 2.8 %weighted_sum.5 = (f32[1,4096]{1,0:T(1,128)S(1)}, f32[1,2048]{1,0:T(1,128)}) custom-call(bf16[2048,4096]{1,0:T(8,128)(2,1)S(1)} %get-tuple-element.61.e_ref, f32[1,2048]{1,0:T(1,128)S(1)} %get-tuple-element.63.a_ref, f32[1,4096]{1,0:T(1,128)S(1)} %get-tuple-element.66.first_ref, f32[1,2048]{1,0:T(1,128)S(1)} %get-tuple-element.68.refs_0_, ...), custom_call_target="tpu_custom_call" | custom-call | flops 16777216 | bytes 16777216 | tf_op jit(solution)/shard_map/weighted_sum/pallas_call | solution.py:294
  95.5 1.2 collective-permute-done.20
  96.7 1.5 %collective-permute-start.23 = (f32[4096]{0:T(1024)S(1)}, f32[4096]{0:T(1024)S(1)}, u32[]{:S(2)}, u32[]{:S(2)}) collective-permute-start(f32[4096]{0:T(1024)S(1)} %bitcast.36), channel_id=1, source_target_pairs={{0,6},{1,7},{2,4},{3,5},{4,2},{5,3},{6,0},{7,1},{8,14},{9,15},{10,... | collective-permute-start | bytes 49160 | tf_op jit(solution)/shard_map/ppermute | solution.py:609
  98.8 2.3 %collective-permute-start.21 = (f32[4096]{0:T(1024)S(1)}, f32[4096]{0:T(1024)S(1)}, u32[]{:S(2)}, u32[]{:S(2)}) collective-permute-start(f32[4096]{0:T(1024)S(1)} %bitcast.38), channel_id=1, source_target_pairs={{0,2},{1,3},{2,0},{3,1},{4,6},{5,7},{6,4},{7,5},{8,10},{9,11},{10,... | collective-permute-start | bytes 49160 | tf_op jit(solution)/shard_map/ppermute | solution.py:609
  101.1 1.3 collective-permute-done.23
  103.0 3.6 %weighted_sum.6.refs_0_ = f32[1,2048]{1,0:T(1,128)S(1)} custom-call(bf16[2048,4096]{1,0:T(8,128)(2,1)S(1)} %get-tuple-element.61.e_ref, f32[1,4096]{1,0:T(1,128)S(1)} %get-tuple-element.66.first_ref, f32[1,4096]{1,0:T(1,128)S(1)} %get-tuple-element.67.b_ref, f32[1,4096]{1,0:T(1,128)S(1)} %pair.4.refs_0_, f32[1,4096]{1,0:T(1,128)S(1)} %bitcast.56, ...), custom_call_target="tpu_custom_call" | custom-call | flops 16777216 | bytes 16777216 | tf_op jit(solution)/shard_map/weighted_sum/pallas_call | solution.py:294
  106.6 2.9 %collective-permute-start.26 = (f32[2048]{0:T(1024)S(1)}, f32[2048]{0:T(1024)S(1)}, u32[]{:S(2)}, u32[]{:S(2)}) collective-permute-start(f32[2048]{0:T(1024)S(1)} %bitcast.39), channel_id=1, source_target_pairs={{0,17},{1,16},{2,19},{3,18},{4,21},{5,20},{6,23},{7,22},{8,25},{9,... | collective-permute-start | bytes 24584 | tf_op jit(solution)/shard_map/ppermute | solution.py:609
  110.1 1.1 collective-permute-done.26
  111.2 1.9 %collective-permute-done.25 = f32[2048]{0:T(1024)S(1)} collective-permute-done((f32[2048]{0:T(1024)S(1)}, f32[2048]{0:T(1024)S(1)}, u32[]{:S(2)}, u32[]{:S(2)}) %collective-permute-start.25) | collective-permute-done | bytes 8224 | tf_op jit(solution)/shard_map/ppermute | solution.py:609
  113.6 2.3 %weighted_sum.7 = (f32[1,4096]{1,0:T(1,128)S(1)}, f32[1,2048]{1,0:T(1,128)S(1)}) custom-call(bf16[2048,4096]{1,0:T(8,128)(2,1)S(1)} %get-tuple-element.61.e_ref, f32[1,2048]{1,0:T(1,128)S(1)} %get-tuple-element.63.a_ref, f32[1,4096]{1,0:T(1,128)S(1)} %get-tuple-element.66.first_ref, f32[1,2048]{1,0:T(1,128)S(1)} %weighted_sum.6.refs_0_, ...), custom_call_target="tpu_custom_call" | custom-call | flops 16777216 | bytes 16777216 | tf_op jit(solution)/shard_map/weighted_sum/pallas_call | solution.py:294
  116.1 1.2 collective-permute-done.27
  117.2 3.2 %column_grad.2 = (f32[1024,128]{1,0:T(8,128)S(1)}, bf16[1024,128]{1,0:T(8,128)(2,1)S(1)}, bf16[256,2048]{1,0:T(8,128)(2,1)S(1)}) custom-call(bf16[128,2048]{1,0:T(8,128)(2,1)S(1)} %get-tuple-element.62.xt_ref, bf16[4096,128]{1,0:T(8,128)(2,1)S(1)} %get-tuple-element.59.y_ref, bf16[2048,4096]{1,0:T(8,128)(2,1)S(1)} %get-tuple-element.61.e_ref, ...), custom_call_target="tpu_custom_call" | custom-call | flops 2147483648 | bytes 8388608 | tf_op jit(solution)/shard_map/column_grad/pallas_call | solution.py:455
  120.7 2.4 %collective-permute-start.31 = (f32[4096]{0:T(1024)S(1)}, f32[4096]{0:T(1024)S(1)}, u32[]{:S(2)}, u32[]{:S(2)}) collective-permute-start(f32[4096]{0:T(1024)S(1)} %bitcast.47), channel_id=1, source_target_pairs={{0,6},{1,7},{2,4},{3,5},{4,2},{5,3},{6,0},{7,1},{8,14},{9,15},{10,... | collective-permute-start | bytes 49160 | tf_op jit(solution)/shard_map/ppermute | solution.py:609
  123.1 0.9 collective-permute-start.30
  124.0 1.1 collective-permute-start.29
  125.1 3.0 %column_grad.3 = (f32[1024,128]{1,0:T(8,128)S(1)}, bf16[1024,128]{1,0:T(8,128)(2,1)S(1)}) custom-call(bf16[256,2048]{1,0:T(8,128)(2,1)S(1)} %get-tuple-element.81.xa_ref, bf16[4096,128]{1,0:T(8,128)(2,1)S(1)} %get-tuple-element.59.y_ref, bf16[2048,4096]{1,0:T(8,128)(2,1)S(1)} %get-tuple-element.61.e_ref, f32[1,4096]{1,0:T(1,128)S(1)} %get-tuple-element.66.first_ref), custom_call_target="tpu_custom_call" | custom-call | flops 2147483648 | bytes 8388608 | tf_op jit(solution)/shard_map/column_grad/pallas_call | solution.py:455
  128.2 1.0 collective-permute-start.37
  129.2 2.4 %collective-permute-start.38 = (bf16[512,128]{1,0:T(8,128)(2,1)S(1)}, bf16[512,128]{1,0:T(8,128)(2,1)S(1)}, u32[]{:S(2)}, u32[]{:S(2)}) collective-permute-start(bf16[512,128]{1,0:T(8,128)(2,1)S(1)} %get-tuple-element.95), channel_id=1, source_target_pairs={{0,6},{1,7},{2,4},{3,5},{4,2},{5,3},{6,0},{7,1},{8,14},{9,15},{10,... | collective-permute-start | bytes 393224 | tf_op jit(solution)/shard_map/ppermute | solution.py:609
  131.6 2.1 %first_rows.1 = (bf16[4096,256]{1,0:T(8,128)(2,1)S(1)}, f32[1,512]{1,0:T(1,128)S(1)}, bf16[512,128]{1,0:T(8,128)(2,1)S(1)}) custom-call(bf16[2048,128]{1,0:T(8,128)(2,1)S(1)} %get-tuple-element.52.x_ref, bf16[4096,128]{1,0:T(8,128)(2,1)S(1)} %get-tuple-element.59.y_ref, bf16[2048,4096]{1,0:T(8,128)(2,1)S(1)} %get-tuple-element.61.e_ref, ...), custom_call_target="tpu_custom_call" | custom-call | flops 34359738368 | bytes 134217728 | tf_op jit(solution)/shard_map/first_rows/pallas_call | solution.py:529
  133.9 0.9 collective-permute-start.32
  134.9 2.6 %other_rows.3 = (bf16[512,128]{1,0:T(8,128)(2,1)S(1)}, bf16[512,128]{1,0:T(8,128)(2,1)S(1)}) custom-call(bf16[2048,128]{1,0:T(8,128)(2,1)S(1)} %get-tuple-element.52.x_ref, bf16[4096,256]{1,0:T(8,128)(2,1)S(1)} %get-tuple-element.88.yb_ref, bf16[2048,4096]{1,0:T(8,128)(2,1)S(1)} %get-tuple-element.61.e_ref, f32[1,2048]{1,0:T(1,128)S(1)} %get-tuple-element.77.alpha_ref), custom_call_target="tpu_custom_call" | custom-call | flops 2147483648 | bytes 8388608 | tf_op jit(solution)/shard_map/other_rows/pallas_call | solution.py:547
  137.5 2.1 %collective-permute-start.34 = (bf16[512,128]{1,0:T(8,128)(2,1)S(1)}, bf16[512,128]{1,0:T(8,128)(2,1)S(1)}, u32[]{:S(2)}, u32[]{:S(2)}) collective-permute-start(bf16[512,128]{1,0:T(8,128)(2,1)S(1)} %get-tuple-element.89), channel_id=1, source_target_pairs={{0,1},{1,0},{2,3},{3,2},{4,5},{5,4},{6,7},{7,6},{8,9},{9,8},{10,11... | collective-permute-start | bytes 393224 | tf_op jit(solution)/shard_map/ppermute | solution.py:609
  140.1 1.6 %collective-permute-start.35 = (bf16[512,128]{1,0:T(8,128)(2,1)S(1)}, bf16[512,128]{1,0:T(8,128)(2,1)S(1)}, u32[]{:S(2)}, u32[]{:S(2)}) collective-permute-start(bf16[512,128]{1,0:T(8,128)(2,1)S(1)} %get-tuple-element.90), channel_id=1, source_target_pairs={{0,16},{1,17},{2,18},{3,19},{4,20},{5,21},{6,22},{7,23},{8,24},{9,... | collective-permute-start | bytes 393224 | tf_op jit(solution)/shard_map/ppermute | solution.py:609
  141.7 1.4 other_rows.2.refs_0_
  143.5 1.6 %collective-permute-done.35.refs_2_ = bf16[512,128]{1,0:T(8,128)(2,1)S(1)} collective-permute-done((bf16[512,128]{1,0:T(8,128)(2,1)S(1)}, bf16[512,128]{1,0:T(8,128)(2,1)S(1)}, u32[]{:S(2)}, u32[]{:S(2)}) %collective-permute-start.35) | collective-permute-done | bytes 131104 | tf_op jit(solution)/shard_map/ppermute | solution.py:609
  145.1 1.1 add_up.1
  (52 shorter events, 7.8 us)
Async XLA Ops:
  0.6 9.6 %collective-permute-start = (bf16[512,128]{1,0:T(8,128)(2,1)}, bf16[512,128]{1,0:T(8,128)(2,1)S(1)}, u32[]{:S(2)}, u32[]{:S(2)}) collective-permute-start(bf16[512,128]{1,0:T(8,128)(2,1)} %param.4), channel_id=1, source_target_pairs={{0,1},{1,0},{2,3},{3,2},{4,5},{5,4},{6,7},{7,6},{8,9},{9,8},{10,11... | collective-permute-start | bytes 393224 | tf_op jit(solution)/shard_map/ppermute | solution.py:609
  3.7 8.2 %collective-permute-start.2 = (bf16[512,128]{1,0:T(8,128)(2,1)}, bf16[512,128]{1,0:T(8,128)(2,1)S(1)}, u32[]{:S(2)}, u32[]{:S(2)}) collective-permute-start(bf16[512,128]{1,0:T(8,128)(2,1)} %param.4), channel_id=1, source_target_pairs={{0,17},{1,16},{2,19},{3,18},{4,21},{5,20},{6,23},{7,22},{8,25},{9,... | collective-permute-start | bytes 393224 | tf_op jit(solution)/shard_map/ppermute | solution.py:609
  5.1 6.7 %collective-permute-start.1 = (bf16[512,128]{1,0:T(8,128)(2,1)}, bf16[512,128]{1,0:T(8,128)(2,1)S(1)}, u32[]{:S(2)}, u32[]{:S(2)}) collective-permute-start(bf16[512,128]{1,0:T(8,128)(2,1)} %param.4), channel_id=1, source_target_pairs={{0,16},{1,17},{2,18},{3,19},{4,20},{5,21},{6,22},{7,23},{8,24},{9,... | collective-permute-start | bytes 393224 | tf_op jit(solution)/shard_map/ppermute | solution.py:609
  6.2 5.6 %collective-permute-start.3 = (bf16[512,128]{1,0:T(8,128)(2,1)}, bf16[512,128]{1,0:T(8,128)(2,1)S(1)}, u32[]{:S(2)}, u32[]{:S(2)}) collective-permute-start(bf16[512,128]{1,0:T(8,128)(2,1)} %bitcast.78), channel_id=1, source_target_pairs={{0,8},{1,9},{2,10},{3,11},{4,12},{5,13},{6,14},{7,15},{8,0},{9,1},... | collective-permute-start | bytes 393224 | tf_op jit(solution)/shard_map/ppermute | solution.py:609
  6.3 12.0 %collective-permute-start.4 = (bf16[512,128]{1,0:T(8,128)(2,1)}, bf16[512,128]{1,0:T(8,128)(2,1)S(1)}, u32[]{:S(2)}, u32[]{:S(2)}) collective-permute-start(bf16[512,128]{1,0:T(8,128)(2,1)} %bitcast.79), channel_id=1, source_target_pairs={{0,4},{1,5},{2,6},{3,7},{4,0},{5,1},{6,2},{7,3},{8,12},{9,13},{10,... | collective-permute-start | bytes 393224 | tf_op jit(solution)/shard_map/ppermute | solution.py:609
  10.2 8.3 %collective-permute-start.5 = (bf16[512,128]{1,0:T(8,128)(2,1)}, bf16[512,128]{1,0:T(8,128)(2,1)S(1)}, u32[]{:S(2)}, u32[]{:S(2)}) collective-permute-start(bf16[512,128]{1,0:T(8,128)(2,1)} %bitcast.80), channel_id=1, source_target_pairs={{0,2},{1,3},{2,0},{3,1},{4,6},{5,7},{6,4},{7,5},{8,10},{9,11},{10,... | collective-permute-start | bytes 393224 | tf_op jit(solution)/shard_map/ppermute | solution.py:609
  18.3 7.1 %collective-permute-start.6 = (bf16[512,128]{1,0:T(8,128)(2,1)S(1)}, bf16[512,128]{1,0:T(8,128)(2,1)S(1)}, u32[]{:S(2)}, u32[]{:S(2)}) collective-permute-start(bf16[512,128]{1,0:T(8,128)(2,1)S(1)} %collective-permute-done.4.refs_1_), channel_id=1, source_target_pairs={{0,2},{1,3},{2,0},{3,1},{4,6},{5,7},{6,4},{7,5},{8,10},{9,11},{10,... | collective-permute-start | bytes 393224 | tf_op jit(solution)/shard_map/ppermute | solution.py:609
  18.4 7.2 %collective-permute-start.8 = (bf16[512,128]{1,0:T(8,128)(2,1)S(1)}, bf16[512,128]{1,0:T(8,128)(2,1)S(1)}, u32[]{:S(2)}, u32[]{:S(2)}) collective-permute-start(bf16[512,128]{1,0:T(8,128)(2,1)S(1)} %collective-permute-done.4.refs_1_), channel_id=1, source_target_pairs={{0,8},{1,9},{2,10},{3,11},{4,12},{5,13},{6,14},{7,15},{8,0},{9,1},... | collective-permute-start | bytes 393224 | tf_op jit(solution)/shard_map/ppermute | solution.py:609
  18.5 7.1 %collective-permute-start.7 = (bf16[512,128]{1,0:T(8,128)(2,1)S(1)}, bf16[512,128]{1,0:T(8,128)(2,1)S(1)}, u32[]{:S(2)}, u32[]{:S(2)}) collective-permute-start(bf16[512,128]{1,0:T(8,128)(2,1)S(1)} %collective-permute-done.5.refs_0_), channel_id=1, source_target_pairs={{0,8},{1,9},{2,10},{3,11},{4,12},{5,13},{6,14},{7,15},{8,0},{9,1},... | collective-permute-start | bytes 393224 | tf_op jit(solution)/shard_map/ppermute | solution.py:609
  25.4 1.4 collective-permute-start.9
  36.8 4.7 %collective-permute-start.12 = (f32[3072]{0:T(1024)S(1)}, f32[3072]{0:T(1024)S(1)}, u32[]{:S(2)}, u32[]{:S(2)}) collective-permute-start(f32[3072]{0:T(1024)S(1)} %bitcast.71), channel_id=1, source_target_pairs={{0,17},{1,16},{2,19},{3,18},{4,21},{5,20},{6,23},{7,22},{8,25},{9,... | collective-permute-start | bytes 36872 | tf_op jit(solution)/shard_map/ppermute | solution.py:609
  36.9 4.6 %collective-permute-start.11 = (f32[3072]{0:T(1024)S(1)}, f32[3072]{0:T(1024)S(1)}, u32[]{:S(2)}, u32[]{:S(2)}) collective-permute-start(f32[3072]{0:T(1024)S(1)} %bitcast.72), channel_id=1, source_target_pairs={{0,16},{1,17},{2,18},{3,19},{4,20},{5,21},{6,22},{7,23},{8,24},{9,... | collective-permute-start | bytes 36872 | tf_op jit(solution)/shard_map/ppermute | solution.py:609
  38.0 4.0 %collective-permute-start.10 = (f32[3072]{0:T(1024)S(1)}, f32[3072]{0:T(1024)S(1)}, u32[]{:S(2)}, u32[]{:S(2)}) collective-permute-start(f32[3072]{0:T(1024)S(1)} %bitcast.73), channel_id=1, source_target_pairs={{0,1},{1,0},{2,3},{3,2},{4,5},{5,4},{6,7},{7,6},{8,9},{9,8},{10,11... | collective-permute-start | bytes 36872 | tf_op jit(solution)/shard_map/ppermute | solution.py:609
  72.1 1.3 collective-permute-start.13
  73.4 7.5 %collective-permute-start.16 = (f32[5120]{0:T(1024)S(1)}, f32[5120]{0:T(1024)S(1)}, u32[]{:S(2)}, u32[]{:S(2)}) collective-permute-start(f32[5120]{0:T(1024)S(1)} %bitcast.33), channel_id=1, source_target_pairs={{0,6},{1,7},{2,4},{3,5},{4,2},{5,3},{6,0},{7,1},{8,14},{9,15},{10,... | collective-permute-start | bytes 61448 | tf_op jit(solution)/shard_map/ppermute | solution.py:609
  79.1 4.7 %collective-permute-start.15 = (f32[5120]{0:T(1024)S(1)}, f32[5120]{0:T(1024)S(1)}, u32[]{:S(2)}, u32[]{:S(2)}) collective-permute-start(f32[5120]{0:T(1024)S(1)} %bitcast.34), channel_id=1, source_target_pairs={{0,4},{1,5},{2,6},{3,7},{4,0},{5,1},{6,2},{7,3},{8,12},{9,13},{10,... | collective-permute-start | bytes 61448 | tf_op jit(solution)/shard_map/ppermute | solution.py:609
  79.1 4.7 %collective-permute-start.14 = (f32[5120]{0:T(1024)S(1)}, f32[5120]{0:T(1024)S(1)}, u32[]{:S(2)}, u32[]{:S(2)}) collective-permute-start(f32[5120]{0:T(1024)S(1)} %bitcast.35), channel_id=1, source_target_pairs={{0,2},{1,3},{2,0},{3,1},{4,6},{5,7},{6,4},{7,5},{8,10},{9,11},{10,... | collective-permute-start | bytes 61448 | tf_op jit(solution)/shard_map/ppermute | solution.py:609
  87.3 4.6 %collective-permute-start.19 = (f32[2048]{0:T(1024)S(1)}, f32[2048]{0:T(1024)S(1)}, u32[]{:S(2)}, u32[]{:S(2)}) collective-permute-start(f32[2048]{0:T(1024)S(1)} %bitcast.57), channel_id=1, source_target_pairs={{0,17},{1,16},{2,19},{3,18},{4,21},{5,20},{6,23},{7,22},{8,25},{9,... | collective-permute-start | bytes 24584 | tf_op jit(solution)/shard_map/ppermute | solution.py:609
  88.4 3.7 %collective-permute-start.18 = (f32[2048]{0:T(1024)S(1)}, f32[2048]{0:T(1024)S(1)}, u32[]{:S(2)}, u32[]{:S(2)}) collective-permute-start(f32[2048]{0:T(1024)S(1)} %bitcast.58), channel_id=1, source_target_pairs={{0,16},{1,17},{2,18},{3,19},{4,20},{5,21},{6,22},{7,23},{8,24},{9,... | collective-permute-start | bytes 24584 | tf_op jit(solution)/shard_map/ppermute | solution.py:609
  89.0 3.7 %collective-permute-start.17 = (f32[2048]{0:T(1024)S(1)}, f32[2048]{0:T(1024)S(1)}, u32[]{:S(2)}, u32[]{:S(2)}) collective-permute-start(f32[2048]{0:T(1024)S(1)} %bitcast.59), channel_id=1, source_target_pairs={{0,1},{1,0},{2,3},{3,2},{4,5},{5,4},{6,7},{7,6},{8,9},{9,8},{10,11... | collective-permute-start | bytes 24584 | tf_op jit(solution)/shard_map/ppermute | solution.py:609
  95.5 1.2 collective-permute-start.20
  96.7 5.7 %collective-permute-start.23 = (f32[4096]{0:T(1024)S(1)}, f32[4096]{0:T(1024)S(1)}, u32[]{:S(2)}, u32[]{:S(2)}) collective-permute-start(f32[4096]{0:T(1024)S(1)} %bitcast.36), channel_id=1, source_target_pairs={{0,6},{1,7},{2,4},{3,5},{4,2},{5,3},{6,0},{7,1},{8,14},{9,15},{10,... | collective-permute-start | bytes 49160 | tf_op jit(solution)/shard_map/ppermute | solution.py:609
  98.2 4.7 %collective-permute-start.22 = (f32[4096]{0:T(1024)S(1)}, f32[4096]{0:T(1024)S(1)}, u32[]{:S(2)}, u32[]{:S(2)}) collective-permute-start(f32[4096]{0:T(1024)S(1)} %bitcast.37), channel_id=1, source_target_pairs={{0,4},{1,5},{2,6},{3,7},{4,0},{5,1},{6,2},{7,3},{8,12},{9,13},{10,... | collective-permute-start | bytes 49160 | tf_op jit(solution)/shard_map/ppermute | solution.py:609
  98.8 4.2 %collective-permute-start.21 = (f32[4096]{0:T(1024)S(1)}, f32[4096]{0:T(1024)S(1)}, u32[]{:S(2)}, u32[]{:S(2)}) collective-permute-start(f32[4096]{0:T(1024)S(1)} %bitcast.38), channel_id=1, source_target_pairs={{0,2},{1,3},{2,0},{3,1},{4,6},{5,7},{6,4},{7,5},{8,10},{9,11},{10,... | collective-permute-start | bytes 49160 | tf_op jit(solution)/shard_map/ppermute | solution.py:609
  106.6 4.6 %collective-permute-start.26 = (f32[2048]{0:T(1024)S(1)}, f32[2048]{0:T(1024)S(1)}, u32[]{:S(2)}, u32[]{:S(2)}) collective-permute-start(f32[2048]{0:T(1024)S(1)} %bitcast.39), channel_id=1, source_target_pairs={{0,17},{1,16},{2,19},{3,18},{4,21},{5,20},{6,23},{7,22},{8,25},{9,... | collective-permute-start | bytes 24584 | tf_op jit(solution)/shard_map/ppermute | solution.py:609
  109.5 3.7 %collective-permute-start.25 = (f32[2048]{0:T(1024)S(1)}, f32[2048]{0:T(1024)S(1)}, u32[]{:S(2)}, u32[]{:S(2)}) collective-permute-start(f32[2048]{0:T(1024)S(1)} %bitcast.40), channel_id=1, source_target_pairs={{0,16},{1,17},{2,18},{3,19},{4,20},{5,21},{6,22},{7,23},{8,24},{9,... | collective-permute-start | bytes 24584 | tf_op jit(solution)/shard_map/ppermute | solution.py:609
  110.0 3.7 %collective-permute-start.24 = (f32[2048]{0:T(1024)S(1)}, f32[2048]{0:T(1024)S(1)}, u32[]{:S(2)}, u32[]{:S(2)}) collective-permute-start(f32[2048]{0:T(1024)S(1)} %bitcast.41), channel_id=1, source_target_pairs={{0,1},{1,0},{2,3},{3,2},{4,5},{5,4},{6,7},{7,6},{8,9},{9,8},{10,11... | collective-permute-start | bytes 24584 | tf_op jit(solution)/shard_map/ppermute | solution.py:609
  116.0 1.2 collective-permute-start.27
  120.5 7.7 %collective-permute-start.28 = (bf16[1024,128]{1,0:T(8,128)(2,1)S(1)}, bf16[1024,128]{1,0:T(8,128)(2,1)S(1)}, u32[]{:S(2)}, u32[]{:S(2)}) collective-permute-start(bf16[1024,128]{1,0:T(8,128)(2,1)S(1)} %get-tuple-element.74), channel_id=1, source_target_pairs={{0,8},{1,9},{2,10},{3,11},{4,12},{5,13},{6,14},{7,15},{8,0},{9,1},... | collective-permute-start | bytes 786440 | tf_op jit(solution)/shard_map/ppermute | solution.py:609
  120.7 8.5 %collective-permute-start.31 = (f32[4096]{0:T(1024)S(1)}, f32[4096]{0:T(1024)S(1)}, u32[]{:S(2)}, u32[]{:S(2)}) collective-permute-start(f32[4096]{0:T(1024)S(1)} %bitcast.47), channel_id=1, source_target_pairs={{0,6},{1,7},{2,4},{3,5},{4,2},{5,3},{6,0},{7,1},{8,14},{9,15},{10,... | collective-permute-start | bytes 49160 | tf_op jit(solution)/shard_map/ppermute | solution.py:609
  123.1 8.5 %collective-permute-start.30 = (f32[4096]{0:T(1024)S(1)}, f32[4096]{0:T(1024)S(1)}, u32[]{:S(2)}, u32[]{:S(2)}) collective-permute-start(f32[4096]{0:T(1024)S(1)} %bitcast.48), channel_id=1, source_target_pairs={{0,4},{1,5},{2,6},{3,7},{4,0},{5,1},{6,2},{7,3},{8,12},{9,13},{10,... | collective-permute-start | bytes 49160 | tf_op jit(solution)/shard_map/ppermute | solution.py:609
  124.0 7.6 %collective-permute-start.29 = (f32[4096]{0:T(1024)S(1)}, f32[4096]{0:T(1024)S(1)}, u32[]{:S(2)}, u32[]{:S(2)}) collective-permute-start(f32[4096]{0:T(1024)S(1)} %bitcast.49), channel_id=1, source_target_pairs={{0,2},{1,3},{2,0},{3,1},{4,6},{5,7},{6,4},{7,5},{8,10},{9,11},{10,... | collective-permute-start | bytes 49160 | tf_op jit(solution)/shard_map/ppermute | solution.py:609
  128.0 5.6 %collective-permute-start.33 = (bf16[1024,128]{1,0:T(8,128)(2,1)S(1)}, bf16[1024,128]{1,0:T(8,128)(2,1)S(1)}, u32[]{:S(2)}, u32[]{:S(2)}) collective-permute-start(bf16[1024,128]{1,0:T(8,128)(2,1)S(1)} %get-tuple-element.83), channel_id=1, source_target_pairs={{0,8},{1,9},{2,10},{3,11},{4,12},{5,13},{6,14},{7,15},{8,0},{9,1},... | collective-permute-start | bytes 786440 | tf_op jit(solution)/shard_map/ppermute | solution.py:609
  128.2 14.9 %collective-permute-start.37 = (bf16[512,128]{1,0:T(8,128)(2,1)S(1)}, bf16[512,128]{1,0:T(8,128)(2,1)S(1)}, u32[]{:S(2)}, u32[]{:S(2)}) collective-permute-start(bf16[512,128]{1,0:T(8,128)(2,1)S(1)} %get-tuple-element.94), channel_id=1, source_target_pairs={{0,4},{1,5},{2,6},{3,7},{4,0},{5,1},{6,2},{7,3},{8,12},{9,13},{10,... | collective-permute-start | bytes 393224 | tf_op jit(solution)/shard_map/ppermute | solution.py:609
  129.2 13.9 %collective-permute-start.38 = (bf16[512,128]{1,0:T(8,128)(2,1)S(1)}, bf16[512,128]{1,0:T(8,128)(2,1)S(1)}, u32[]{:S(2)}, u32[]{:S(2)}) collective-permute-start(bf16[512,128]{1,0:T(8,128)(2,1)S(1)} %get-tuple-element.95), channel_id=1, source_target_pairs={{0,6},{1,7},{2,4},{3,5},{4,2},{5,3},{6,0},{7,1},{8,14},{9,15},{10,... | collective-permute-start | bytes 393224 | tf_op jit(solution)/shard_map/ppermute | solution.py:609
  133.7 9.8 %collective-permute-start.36 = (bf16[512,128]{1,0:T(8,128)(2,1)S(1)}, bf16[512,128]{1,0:T(8,128)(2,1)S(1)}, u32[]{:S(2)}, u32[]{:S(2)}) collective-permute-start(bf16[512,128]{1,0:T(8,128)(2,1)S(1)} %get-tuple-element.93), channel_id=1, source_target_pairs={{0,2},{1,3},{2,0},{3,1},{4,6},{5,7},{6,4},{7,5},{8,10},{9,11},{10,... | collective-permute-start | bytes 393224 | tf_op jit(solution)/shard_map/ppermute | solution.py:609
  133.9 6.1 %collective-permute-start.32 = (bf16[512,128]{1,0:T(8,128)(2,1)S(1)}, bf16[512,128]{1,0:T(8,128)(2,1)S(1)}, u32[]{:S(2)}, u32[]{:S(2)}) collective-permute-start(bf16[512,128]{1,0:T(8,128)(2,1)S(1)} %get-tuple-element.80), channel_id=1, source_target_pairs={{0,17},{1,16},{2,19},{3,18},{4,21},{5,20},{6,23},{7,22},{8,25},{9,... | collective-permute-start | bytes 393224 | tf_op jit(solution)/shard_map/ppermute | solution.py:609
  137.5 6.0 %collective-permute-start.34 = (bf16[512,128]{1,0:T(8,128)(2,1)S(1)}, bf16[512,128]{1,0:T(8,128)(2,1)S(1)}, u32[]{:S(2)}, u32[]{:S(2)}) collective-permute-start(bf16[512,128]{1,0:T(8,128)(2,1)S(1)} %get-tuple-element.89), channel_id=1, source_target_pairs={{0,1},{1,0},{2,3},{3,2},{4,5},{5,4},{6,7},{7,6},{8,9},{9,8},{10,11... | collective-permute-start | bytes 393224 | tf_op jit(solution)/shard_map/ppermute | solution.py:609
  140.1 5.0 %collective-permute-start.35 = (bf16[512,128]{1,0:T(8,128)(2,1)S(1)}, bf16[512,128]{1,0:T(8,128)(2,1)S(1)}, u32[]{:S(2)}, u32[]{:S(2)}) collective-permute-start(bf16[512,128]{1,0:T(8,128)(2,1)S(1)} %get-tuple-element.90), channel_id=1, source_target_pairs={{0,16},{1,17},{2,18},{3,19},{4,20},{5,21},{6,22},{7,23},{8,24},{9,... | collective-permute-start | bytes 393224 | tf_op jit(solution)/shard_map/ppermute | solution.py:609
